TPU v7x, 32 devices: a whole 2x2x4 slice. The times are simulated.
32 devices in a mesh: dom: 16 (over z, y, core), depth: 2 (over x).
Axes of the slice: x: 2, y: 2, z: 4, core: 2. Of those that a mesh axis runs over, the one named last changes fastest.
Arguments:
- adjoint_now: float32 [3, 64, 34, 128], P(None, 'dom', 'depth'), may hold values from -6 to 6
- adjoint_next: float32 [3, 64, 34, 128], P(None, 'dom', 'depth'), may hold values from -6 to 6
- lame_first: float32 [16, 8, 32], P('dom', 'depth'), may hold values from 1 to 3
- shear_modulus: float32 [16, 8, 32], P('dom', 'depth'), may hold values from 1 to 3
- density: float32 [64, 34, 128], P('dom', 'depth'), may hold values from 1 to 3
- branch_flags: int32 [4, 2, 64, 128], P(None, 'depth', 'dom'), may hold values from 0 to 2
- weak_slope: float32 [2, 64, 128], P('depth', 'dom'), may hold values from 0.1 to 0.5
- normal_stress: float32 [2, 64, 128], P('depth', 'dom'), may hold values from 1 to 10
- patch_owner: int32 [2, 64], P('depth', 'dom'), may hold values from 0 to 31, as said below
Outputs:
- earlier_state: float32 [3, 64, 34, 128], P(None, 'dom', 'depth')
- later_state: float32 [3, 64, 34, 128], P(None, 'dom', 'depth')
- patch_gradient: float32 [2, 32, 128], P('depth', 'dom')
Inputs may be any that keep to these rules, and one draw needn't show every extreme that they name: `patch_owner`: patch p is owned by dom index p // 2; a column held by dom index d belongs to a patch whose owner is at most 2 indices of dom from d.
All inputs are finite; a program needn't handle non-finite values.
Results may differ from a plain program's by a relative error of at most 0.0001.
Values sent between devices are 32-bit elements; how exact they have to be, the bound alone decides.
No kernel may reach another device: no remote copies, remote signals or barrier semaphores. Data moves between devices by JAX's collectives and lax.ppermute only.
A program may use at most 64 MiB of HBM per device.

v0:
```python
import functools
import math

import jax
import jax.numpy as jnp
import ml_dtypes
import numpy as np
from jax import lax
from jax.experimental import pallas as pl
from jax.experimental.pallas import tpu as pltpu
from jax.sharding import PartitionSpec as P

PATCH_DEV = 2
REACH = 2

time_step = 0.01
lock_stiffness = 0.5

BLOCK = 16
PLANE = 5 * BLOCK


def basis_tables():
    points = [-1.0, -math.sqrt(3.0 / 7.0), 0.0, math.sqrt(3.0 / 7.0), 1.0]
    quad_weights = np.array([0.1, 49.0 / 90.0, 32.0 / 45.0, 49.0 / 90.0, 0.1])
    products = []
    for first in range(5):
        value = 1.0
        for other in range(5):
            if other != first:
                value = value * (points[first] - points[other])
        products.append(value)
    derivative = np.zeros((5, 5))
    for row in range(5):
        for column in range(5):
            if row == column:
                total = 0.0
                for other in range(5):
                    if other != row:
                        total = total + 1.0 / (points[row] - points[other])
                derivative[row, column] = total
            else:
                derivative[row, column] = (
                    products[row] / products[column] / (points[row] - points[column])
                )
    return (quad_weights, derivative)


def two_parts(table):
    high = table.astype(ml_dtypes.bfloat16)
    low = (table - high.astype(np.float64)).astype(ml_dtypes.bfloat16)
    return np.stack([high, low])


def element_stiffness():
    weights, derivative = basis_tables()
    eye = np.eye(5)
    slope = 2.0 * derivative
    grads = [
        np.kron(slope, np.kron(eye, eye)),
        np.kron(eye, np.kron(eye, slope)),
        np.kron(eye, np.kron(slope, eye)),
    ]
    quad = np.kron(weights, np.kron(weights, weights)) / 8.0
    first = np.zeros((125, 3, 125, 3))
    second = np.zeros((125, 3, 125, 3))
    lap = sum(g.T @ (quad[:, None] * g) for g in grads)
    for c in range(3):
        second[:, c, :, c] += lap
        for d in range(3):
            first[:, c, :, d] += grads[c].T @ (quad[:, None] * grads[d])
            second[:, c, :, d] += grads[d].T @ (quad[:, None] * grads[c])
    where = [
        node // 5 * BLOCK + node % 5 * 3 + c for node in range(125) for c in range(3)
    ]
    wide = []
    for small in (first, second):
        big = np.zeros((5 * PLANE, 5 * PLANE))
        big[np.ix_(where, where)] = small.reshape(375, 375)
        wide.append(big)
    return wide


OWN_COLS = 384
FAR_COLS = 128


@functools.cache
def stiffness_tables():
    wide = element_stiffness()
    own = 4 * PLANE
    parts = []
    for rows in (slice(0, own), slice(own, own + PLANE)):
        both = np.concatenate([w[rows] for w in wide])
        table = np.zeros((both.shape[0], OWN_COLS + FAR_COLS))
        table[:, :own] = both[:, :own]
        table[:, OWN_COLS : OWN_COLS + PLANE] = both[:, own:]
        parts.append(two_parts(table))
    return parts


@functools.cache
def back_table(y_elems, z_elems):
    lanes = y_elems * z_elems
    depth = 4 * z_elems
    back = np.zeros((4 * lanes, y_elems * depth), ml_dtypes.bfloat16)
    for yel in range(y_elems):
        for k in range(z_elems):
            for zl in range(4):
                back[zl * lanes + yel * z_elems + k, yel * depth + 4 * k + zl] = 1
    return back


@functools.cache
def mass_table(y_elems, z_elems):
    weights, _ = basis_tables()
    table = np.zeros((4, 5, BLOCK, y_elems, z_elems))
    for x in range(4):
        mx = 0.2 if x == 0 else weights[x]
        for zl in range(5):
            for yl in range(5):
                for yel in range(y_elems):
                    my = weights[yl]
                    if (yl == 0 and yel > 0) or (yl == 4 and yel < y_elems - 1):
                        my = 0.2
                    mz = np.full(z_elems, weights[zl])
                    if zl == 0:
                        mz[1:] = 0.2
                    if zl == 4:
                        mz[:] = 0.2
                    value = time_step * time_step * 8.0 / (mx * my * mz)
                    if zl == 4:
                        value[-1] = 0.0
                    table[x, zl, 3 * yl : 3 * yl + 3, yel] = value
    return table.reshape(4 * PLANE, y_elems * z_elems).astype(np.float32)


def pieces(value, count):
    out = []
    for _ in range(count):
        piece = value.astype(jnp.bfloat16)
        out.append(piece)
        value = value - piece.astype(jnp.float32)
    return out


def dot(a, b):
    return jnp.dot(a, b, preferred_element_type=jnp.float32)


def exact_dot(value, table, count=3):
    rows = value.shape[0]
    result = dot(jnp.concatenate(pieces(value, count), axis=0), table)
    total = result[:rows]
    for i in range(1, count):
        total = total + result[i * rows : (i + 1) * rows]
    return total


def split_dot(table_high, table_low, value):
    lanes = value.shape[1]
    high, low = pieces(value, 2)
    wide = dot(table_high, jnp.concatenate([high, low], axis=1))
    return wide[:, :lanes] + (wide[:, lanes:] + dot(table_low, high))


def ones_where(rule, shape):
    row = lax.broadcasted_iota(jnp.int32, shape, 0)
    column = lax.broadcasted_iota(jnp.int32, shape, 1)
    return jnp.where(rule(row, column), 1.0, 0.0).astype(jnp.bfloat16)


def gather_table(lanes, z_elems):
    return ones_where(lambda z, c: z == 4 * (c % z_elems) + c // lanes, (lanes, 5 * lanes))


def fault_table(lanes, z_elems):
    return ones_where(lambda z, c: z == 4 * (c % z_elems) + c // z_elems, (lanes, lanes))


def fault_table_back(lanes, z_elems):
    return ones_where(lambda c, z: z == 4 * (c % z_elems) + c // z_elems, (lanes, lanes))


def to_elements(native, scratch, table, y_elems):
    group = 4 * BLOCK
    scratch[...] = jnp.zeros_like(scratch)
    for c in range(3):
        for y in range(4 * y_elems + 1):
            rows = native(c, y)
            if y < 4 * y_elems:
                scratch[y // 4, pl.ds(y % 4 * 3 + c, 4, stride=BLOCK), :] = rows
            if y % 4 == 0 and y > 0:
                scratch[y // 4 - 1, pl.ds(12 + c, 4, stride=BLOCK), :] = rows
    high, middle, low = pieces(
        jnp.concatenate([scratch[i] for i in range(y_elems)], axis=0), 3
    )
    result = dot(
        jnp.concatenate([high, middle], axis=1), jnp.concatenate([table, table], axis=0)
    ) + dot(low, table)
    lanes = result.shape[1] // 5
    across = lax.broadcasted_iota(jnp.int32, (group, result.shape[1]), 1) % lanes // (
        lanes // y_elems
    )
    total = result[:group]
    for yel in range(1, y_elems):
        total = jnp.where(across == yel, result[yel * group : (yel + 1) * group], total)
    blocks = []
    for x in range(4):
        for zl in range(5):
            blocks.append(total[x * BLOCK : (x + 1) * BLOCK, zl * lanes : (zl + 1) * lanes])
    return jnp.concatenate(blocks, axis=0)


def from_elements(field, scratch, back_ref, out_ref, y_elems):
    rows = []
    for x in range(4):
        rows.append(
            jnp.concatenate(
                [field[x * PLANE + zl * BLOCK : x * PLANE + (zl + 1) * BLOCK] for zl in range(4)],
                axis=1,
            )
        )
    result = exact_dot(jnp.concatenate(rows, axis=0), back_ref[...])
    depth = result.shape[1] // y_elems
    for yel in range(y_elems):
        scratch[yel] = result[:, yel * depth : (yel + 1) * depth]
    for c in range(3):
        for y in range(4 * y_elems + 1):
            yel, yl = (y // 4, y % 4) if y < 4 * y_elems else (y_elems - 1, 4)
            out_ref[c, y] = scratch[yel, pl.ds(yl * 3 + c, 4, stride=BLOCK), :]


def block_iotas(lanes):
    return (
        lax.broadcasted_iota(jnp.int32, (8, lanes), 0),
        lax.broadcasted_iota(jnp.int32, (8, lanes), 1),
    )


def fault_message(field, z_elems):
    lanes = field.shape[1]
    row, lane = block_iotas(lanes)
    out = []
    for x in range(4):
        total = jnp.zeros((8, lanes), jnp.float32)
        for zl in range(4):
            at = x * PLANE + zl * BLOCK
            first = pltpu.roll(pltpu.roll(field[at : at + 8], 4, 0), zl * z_elems, 1)
            last = pltpu.roll(
                pltpu.roll(field[at + 8 : at + 16], 4, 0), (zl + 1) * z_elems % lanes, 1
            )
            here = lane // z_elems == zl
            total = jnp.where(here, jnp.where(row < 4, last, first), total)
        out.append(total)
    return jnp.concatenate(out, axis=0)


def swap_rows(message):
    parts = [pltpu.roll(message[i : i + 8], 4, 0) for i in range(0, message.shape[0], 8)]
    return jnp.concatenate(parts, axis=0)


def select_messages(parity, left, right):
    even = parity == 0
    return jnp.where(even, right, left), jnp.where(even, left, right)


def material_rows(lame_ref, shear_ref):
    y_elems, z_elems = lame_ref.shape
    both = jnp.concatenate([lame_ref[...], shear_ref[...]], axis=0)
    spread = ones_where(lambda k, c: c % z_elems == k, (z_elems, y_elems * z_elems))
    tiled = exact_dot(both, spread)
    row = lax.broadcasted_iota(jnp.int32, tiled.shape, 0)
    lane = lax.broadcasted_iota(jnp.int32, tiled.shape, 1)
    kept = jnp.where(row % y_elems == lane // z_elems, tiled, 0.0)
    return (
        jnp.sum(kept[:y_elems], axis=0, keepdims=True),
        jnp.sum(kept[y_elems:], axis=0, keepdims=True),
    )


def above_lanes(lanes, z_elems):
    return lax.broadcasted_iota(jnp.int32, (BLOCK, lanes), 1) % z_elems != 0


def edge_force(edge_ref, own, lame_row, shear_row, z_elems):
    lanes = own.shape[1]
    padded = jnp.concatenate(
        [own, jnp.zeros((OWN_COLS - own.shape[0], lanes), jnp.float32)], axis=0
    )
    result = split_dot(edge_ref[0, :, :OWN_COLS], edge_ref[1, :, :OWN_COLS], padded)
    force = lame_row * result[:PLANE] + shear_row * result[PLANE:]
    top = force[:BLOCK] + jnp.where(
        above_lanes(lanes, z_elems), pltpu.roll(force[4 * BLOCK :], 1, 1), 0.0
    )
    row = lax.broadcasted_iota(jnp.int32, top.shape, 0)
    top = jnp.where(row == BLOCK - 1, lame_row, top)
    second = jnp.where(row == BLOCK - 1, shear_row, force[BLOCK : 2 * BLOCK])
    return jnp.concatenate([top, second, force[2 * BLOCK : 4 * BLOCK]], axis=0)


def start_copies(pairs, sems):
    copies = [
        pltpu.make_async_copy(source, target, sems.at[i])
        for i, (source, target) in enumerate(pairs)
    ]
    for copy in copies:
        copy.start()
    return copies


def first_kernel(
    where_ref,
    now_hbm,
    flags_hbm,
    weak_hbm,
    lame_hbm,
    shear_hbm,
    edge_hbm,
    cur_ref,
    even_ref,
    odd_ref,
    fault_out_ref,
    material_ref,
    edge_ref,
    scratch,
    now_ref,
    flags_ref,
    weak_ref,
    lame_ref,
    shear_ref,
    sems,
):
    copies = start_copies(
        [
            (now_hbm, now_ref),
            (flags_hbm, flags_ref),
            (weak_hbm, weak_ref),
            (lame_hbm, lame_ref),
            (shear_hbm, shear_ref),
            (edge_hbm, edge_ref),
        ],
        sems,
    )
    y_elems, z_elems = lame_ref.shape
    lanes = y_elems * z_elems
    parity = where_ref[0] % 2
    gather = gather_table(lanes, z_elems)
    fault = fault_table(lanes, z_elems)
    copies[0].wait()
    cur = to_elements(lambda c, y: now_ref[c, y], scratch, gather, y_elems)
    cur_ref[...] = cur
    steps = flags_ref.shape[0]
    copies[1].wait()
    copies[2].wait()
    weak = weak_ref[...]
    tangent = []
    for i in range(steps):
        flag = flags_ref[i]
        tangent.append(
            jnp.where(flag == 0, lock_stiffness, jnp.where(flag == 1, -weak, 0.0))
        )
    tangent = exact_dot(jnp.concatenate(tangent, axis=0), fault)
    fault_out_ref[...] = jnp.concatenate([fault_message(cur, z_elems), tangent], axis=0)
    copies[3].wait()
    copies[4].wait()
    lame_row, shear_row = material_rows(lame_ref, shear_ref)
    material_ref[...] = jnp.concatenate(
        [lame_row, shear_row, jnp.zeros((6, lanes), jnp.float32)], axis=0
    )
    copies[5].wait()
    right = edge_force(edge_ref, cur, lame_row, shear_row, z_elems)
    even_ref[...], odd_ref[...] = select_messages(parity, cur[: 4 * BLOCK], right)


def setup_kernel(
    where_ref,
    next_hbm,
    density_hbm,
    flags_hbm,
    stress_hbm,
    mass_hbm,
    main_hbm,
    back_hbm,
    fol_ref,
    minv_ref,
    weight_ref,
    main_ref,
    back_ref,
    scratch,
    next_ref,
    density_ref,
    flags_ref,
    stress_ref,
    mass_ref,
    sems,
    *,
    y_elems,
    z_elems,
):
    copies = start_copies(
        [
            (next_hbm, next_ref),
            (density_hbm, density_ref),
            (flags_hbm, flags_ref),
            (stress_hbm, stress_ref),
            (mass_hbm, mass_ref),
            (main_hbm, main_ref),
            (back_hbm, back_ref),
        ],
        sems,
    )
    gather = gather_table(y_elems * z_elems, z_elems)
    fault = fault_table(y_elems * z_elems, z_elems)
    for copy in copies[:5]:
        copy.wait()
    fol_ref[...] = to_elements(lambda c, y: next_ref[c, y], scratch, gather, y_elems)
    density = to_elements(lambda c, y: density_ref[y], scratch, gather, y_elems)
    table = mass_ref[...]
    first = where_ref[0] == 0
    plane = lax.broadcasted_iota(jnp.int32, table.shape, 0) < PLANE
    table = jnp.where(jnp.logical_and(first, plane), 2.0 * table, table)
    minv_ref[...] = jnp.where(table > 0.0, table / jnp.where(table > 0.0, density, 1.0), 0.0)
    stress = stress_ref[...]
    weights = []
    for i in range(flags_ref.shape[0]):
        flag = flags_ref[i]
        weights.append(
            stress * jnp.where(flag == 1, 0.5, jnp.where(flag == 2, 1.0, 0.0))
        )
    weight_ref[...] = exact_dot(jnp.concatenate(weights, axis=0), fault)
    copies[5].wait()
    copies[6].wait()


def advance(
    step, place, last_place, cur, fol, minv, material, even_in, odd_in, fault_in, tangents, main_ref, edge_ref,
    own_fault, y_elems, z_elems,
):
    lanes = cur.shape[1]
    even = place % 2 == 0
    far = jnp.where(place == last_place, 0.0, jnp.where(even, even_in, odd_in))
    left = jnp.where(place == 0, 0.0, jnp.where(even, odd_in, even_in))
    lane_wide = lax.broadcasted_iota(jnp.int32, (BLOCK, lanes), 1)
    below = jnp.where(
        lane_wide % z_elems != z_elems - 1, pltpu.roll(far[:BLOCK], lanes - 1, 1), 0.0
    )
    far = jnp.concatenate([far, below], axis=0)
    lame_row, shear_row = material[0:1], material[1:2]
    zeros = jnp.zeros((FAR_COLS - PLANE, lanes), jnp.float32)
    gap = jnp.zeros((OWN_COLS - 4 * PLANE, lanes), jnp.float32)
    result = split_dot(
        main_ref[0], main_ref[1], jnp.concatenate([cur, gap, far, zeros], axis=0)
    )
    force = lame_row * result[: 4 * PLANE] + shear_row * result[4 * PLANE :]
    touch = split_dot(
        edge_ref[0, :, OWN_COLS:],
        edge_ref[1, :, OWN_COLS:],
        jnp.concatenate([cur[:PLANE], zeros], axis=0),
    )
    left_lame = left[BLOCK - 1 : BLOCK]
    left_shear = left[2 * BLOCK - 1 : 2 * BLOCK]
    from_left = left_lame * touch[:PLANE] + left_shear * touch[PLANE:]
    from_left = jnp.concatenate([from_left[: 4 * BLOCK] + left, from_left[4 * BLOCK :]], axis=0)
    row, lane = block_iotas(lanes)
    across = lane // z_elems
    rows_first = row < 3
    rows_last = jnp.logical_and(row >= 4, row < 7)
    add_first = jnp.logical_and(rows_first, across > 0)
    take_last = jnp.logical_and(rows_last, across < y_elems - 1)
    pull_first = jnp.logical_and(rows_first, across == 0)
    pull_last = jnp.logical_and(rows_last, across == y_elems - 1)
    above = above_lanes(lanes, z_elems)
    below_t, own_t = tangents
    planes = []
    for x in range(4):
        blocks = []
        for zl in range(5):
            at = x * PLANE + zl * BLOCK
            block = force[at : at + BLOCK]
            if x == 0:
                block = block + from_left[zl * BLOCK : (zl + 1) * BLOCK]
            blocks.append(block)
        blocks[0] = blocks[0] + jnp.where(above, pltpu.roll(blocks[4], 1, 1), 0.0)
        stiff = jnp.where(
            jnp.logical_or(row == 1, row == 5),
            lock_stiffness,
            jnp.where(row < 4, below_t[4 * step + x : 4 * step + x + 1], own_t[4 * step + x : 4 * step + x + 1]),
        )
        pulled = stiff * (fault_in[8 * x : 8 * x + 8] - own_fault[8 * x : 8 * x + 8])
        for zl in range(4):
            low, high = blocks[zl][:8], blocks[zl][8:]
            low = low + jnp.where(
                add_first, pltpu.roll(pltpu.roll(high, 4, 0), z_elems, 1), 0.0
            )
            high = jnp.where(
                take_last, pltpu.roll(pltpu.roll(low, 4, 0), lanes - z_elems, 1), high
            )
            low = low - jnp.where(
                pull_first, pltpu.roll(pulled, (lanes - zl * z_elems) % lanes, 1), 0.0
            )
            high = high - jnp.where(
                pull_last,
                pltpu.roll(pulled, (lanes - (zl + 1) * z_elems) % lanes, 1),
                0.0,
            )
            blocks[zl] = jnp.concatenate([low, high], axis=0)
        blocks[4] = pltpu.roll(blocks[0], lanes - 1, 1)
        planes.extend(blocks)
    return (2.0 * cur - fol) - minv * jnp.concatenate(planes, axis=0)


def fault_input(up_ref, down_ref, count):
    if down_ref is None:
        return up_ref[:count]
    up, down = up_ref[:count], down_ref[:count]
    row = lax.broadcasted_iota(jnp.int32, up.shape, 0)
    return jnp.where(row % 8 < 4, up, down)


def step_kernel(*refs, step, last, last_place, pair, y_elems, z_elems):
    refs = list(refs)
    where_ref, cur_ref, fol_ref, minv_ref, material_ref, even_ref, odd_ref = refs[:7]
    refs = refs[7:]
    up_ref = refs.pop(0)
    down_ref = None if pair else refs.pop(0)
    first_up_ref, own_ref, first_own_ref, main_ref, edge_ref = refs[:5]
    refs = refs[5:]
    place = where_ref[0]
    cur = cur_ref[...]
    tangents = (first_up_ref[32:], first_own_ref[32:])
    new = advance(
        step, place, last_place, cur, fol_ref[...], minv_ref[...], material_ref[...], even_ref[...], odd_ref[...],
        fault_input(up_ref, down_ref, 32), tangents, main_ref, edge_ref, swap_rows(own_ref[:32]),
        y_elems, z_elems,
    )
    if last:
        _, back_ref, out_ref, scratch = refs
        from_elements(new, scratch, back_ref, out_ref, y_elems)
    else:
        new_ref, even_out, odd_out, fault_out = refs
        new_ref[...] = new
        fault_out[...] = fault_message(new, z_elems)
        right = edge_force(edge_ref, new, material_ref[0:1], material_ref[1:2], z_elems)
        even_out[...], odd_out[...] = select_messages(place % 2, new[: 4 * BLOCK], right)


def output_kernel(field_ref, back_ref, out_ref, mark_ref, scratch, *, y_elems):
    mark_ref[...] = jnp.zeros_like(mark_ref)
    from_elements(field_ref[...], scratch, back_ref, out_ref, y_elems)


def patch_kernel(*refs, pair, steps, z_elems):
    where_ref, owner_ref, weight_ref = refs[:3]
    messages = refs[6:-5]
    home_out, out_a, out_b, out_c, out_d = refs[-5:]
    place = where_ref[0]
    lanes = weight_ref.shape[1]
    count = 2 if pair else 3
    grads = [jnp.zeros((8, lanes), jnp.float32) for _ in range(4)]
    for i in range(steps):
        group = messages[count * i : count * (i + 1)]
        slip = fault_input(group[1], None if pair else group[2], 32) - swap_rows(group[0][:32])
        for x in range(4):
            grads[x] = grads[x] + slip[8 * x : 8 * x + 8] * weight_ref[4 * i + x : 4 * i + x + 1]
    wide = 16
    number = lax.broadcasted_iota(jnp.int32, (wide, lanes), 0) + (place - REACH) * PATCH_DEV
    total = jnp.zeros((wide, lanes), jnp.float32)
    for x in range(4):
        total = total + jnp.where(number == owner_ref[0, x], grads[x][4:5], 0.0)
    total = exact_dot(total, fault_table_back(lanes, z_elems))
    rows = [total[2 * i : 2 * i + 2] for i in range(5)]
    home_out[...] = rows[2]
    even = place % 2 == 0
    out_a[...] = jnp.where(even, rows[3], rows[1])
    out_b[...] = jnp.where(even, rows[1], rows[3])
    low = place % 4 < 2
    out_c[...] = jnp.where(low, rows[4], rows[0])
    out_d[...] = jnp.where(low, rows[0], rows[4])


VMEM = pl.BlockSpec(memory_space=pltpu.VMEM)
HBM = pl.BlockSpec(memory_space=pltpu.HBM)
SMEM = pl.BlockSpec(memory_space=pltpu.SMEM)
ANY = pl.BlockSpec(memory_space=pl.ANY)


def kernel_call(body, outs, args, in_smem, scratch=(), in_hbm=(), kept=(), unread=(), **static):
    shapes = []
    for out in outs:
        shape, dtype = out if isinstance(out[0], tuple) else (out, jnp.float32)
        shapes.append((pltpu.VMEM if in_hbm else jax.ShapeDtypeStruct)(shape, dtype))
    specs = [VMEM] * len(args)
    for places, spec in ((in_smem, SMEM), (in_hbm, HBM), (unread, ANY)):
        for i in places:
            specs[i] = spec
    copied = [pltpu.VMEM(args[i].shape, args[i].dtype) for i in in_hbm if i not in kept]
    if in_hbm:
        copied.append(pltpu.SemaphoreType.DMA((len(in_hbm),)))
    return pl.pallas_call(
        functools.partial(body, **static) if static else body,
        out_shape=shapes,
        in_specs=specs,
        out_specs=[VMEM] * len(shapes),
        scratch_shapes=list(scratch) + copied,
        compiler_params=pltpu.CompilerParams(
            vmem_limit_bytes=(56 if in_hbm else 24) * 2**20
        ),
    )(*args)


def swapped(block, distance, group):
    size, across = lax.axis_size("dom"), lax.axis_size("depth")
    partner = {}
    for left in range(size - distance):
        if left // distance % 2 == group:
            partner[left], partner[left + distance] = left + distance, left
    route = []
    for i in range(size):
        for j in range(across):
            side = j if i in partner else min(j ^ 1, across - 1)
            route.append((i * across + j, partner.get(i, i) * across + side))
    return lax.ppermute(block, ("dom", "depth"), route)


def from_behind(block, axis, distance):
    size = lax.axis_size(axis)
    return lax.ppermute(block, axis, [((i - distance) % size, i) for i in range(size)])


def on_device(
    adjoint_now,
    adjoint_next,
    lame_first,
    shear_modulus,
    density,
    branch_flags,
    weak_slope,
    normal_stress,
    patch_owner,
):
    x_elems, y_elems, z_elems = lame_first.shape
    lanes = y_elems * z_elems
    assert x_elems == 1 and lanes == adjoint_now.shape[3]
    steps = branch_flags.shape[0]
    pair = lax.axis_size("depth") == 2
    place = lax.axis_index("dom").astype(jnp.int32).reshape(1)
    main_table, edge_table = (jnp.asarray(t) for t in stiffness_tables())
    back = jnp.asarray(back_table(y_elems, z_elems))
    mass = jnp.asarray(mass_table(y_elems, z_elems))
    now = jnp.transpose(adjoint_now, (0, 2, 1, 3))
    following = jnp.transpose(adjoint_next, (0, 2, 1, 3))
    rho = jnp.transpose(density, (1, 0, 2))
    flags = branch_flags[:, 0]
    native = pltpu.VMEM((y_elems, 4 * BLOCK, lanes), jnp.float32)
    field = (4 * PLANE, lanes)
    plane = (4 * BLOCK, lanes)

    def exchange(even, odd, fault_rows):
        if pair:
            faults = [from_behind(fault_rows, "depth", 1)]
        else:
            faults = [from_behind(fault_rows, "depth", 1), from_behind(fault_rows, "depth", -1)]
        return swapped(even, 1, 0), swapped(odd, 1, 1), faults

    cur, even, odd, fault_rows, material, edge_table = kernel_call(
        first_kernel,
        [
            field, plane, plane, (32 + 4 * steps, lanes), (8, lanes),
            (edge_table.shape, edge_table.dtype),
        ],
        (
            place, now, flags, weak_slope[0], lame_first[0], shear_modulus[0], edge_table,
        ),
        (0,),
        [native],
        range(1, 7),
        (6,),
    )
    first_fault = fault_rows
    even_in, odd_in, fault_in = exchange(even, odd, fault_rows)
    first_in = fault_in
    fol, minv, weight, main_table, back = kernel_call(
        setup_kernel,
        [
            field, field, (4 * steps, lanes), (main_table.shape, main_table.dtype),
            (back.shape, back.dtype),
        ],
        (place, following, rho, flags, normal_stress[0], mass, main_table, back),
        (0,),
        [native],
        range(1, 8),
        (6, 7),
        y_elems=y_elems,
        z_elems=z_elems,
    )
    seen = []
    for step in range(steps):
        last = step == steps - 1
        seen += [fault_rows] + fault_in
        args = [place, cur, fol, minv, material, even_in, odd_in] + fault_in
        args += [first_in[0], fault_rows, first_fault, main_table, edge_table]
        static = dict(
            step=step, last=last, last_place=lax.axis_size("dom") - 1, pair=pair, y_elems=y_elems,
            z_elems=z_elems,
        )
        if not last:
            new, even, odd, new_fault = kernel_call(
                step_kernel, [field, plane, plane, (32, lanes)], args, (0,), **static
            )
            fol, cur, fault_rows = cur, new, new_fault
            even_in, odd_in, fault_in = exchange(even, odd, fault_rows)
        else:
            whole = (3, 4 * y_elems + 1, 4, lanes)
            later, mark = kernel_call(
                output_kernel, [whole, (8, lanes)], [cur, back], (), [native], y_elems=y_elems
            )
            sums = kernel_call(
                patch_kernel,
                [(PATCH_DEV, lanes)] * 5,
                [place, patch_owner, weight, even_in, odd_in, mark] + seen,
                (0, 1),
                unread=(3, 4, 5),
                pair=pair,
                steps=steps,
                z_elems=z_elems,
            )
            patch_sums = sums[0]
            for out, distance, group in zip(sums[1:], (1, 1, 2, 2), (0, 1, 0, 1)):
                patch_sums = patch_sums + swapped(out, distance, group)
            earlier = kernel_call(
                step_kernel,
                [whole],
                args + [sums[0], back],
                (0,),
                [native],
                unread=(len(args),),
                **static,
            )[0]
    return (
        jnp.transpose(earlier, (0, 2, 1, 3)),
        jnp.transpose(later, (0, 2, 1, 3)),
        patch_sums[None],
    )


def solution(mesh):
    return jax.shard_map(
        on_device,
        mesh=mesh,
        in_specs=(
            P(None, "dom", "depth", None),
            P(None, "dom", "depth", None),
            P("dom", "depth", None),
            P("dom", "depth", None),
            P("dom", "depth", None),
            P(None, "depth", "dom", None),
            P("depth", "dom", None),
            P("depth", "dom", None),
            P("depth", "dom"),
        ),
        out_specs=(
            P(None, "dom", "depth", None),
            P(None, "dom", "depth", None),
            P("depth", "dom", None),
        ),
        check_vma=False,
    )
```

profile of v0, /device:TPU:0, one launch (start us, length us, event | category | flops | bytes accessed | tf_op | source)
XLA Modules:
  0.0 34.3 jit_solution(14916362783757111853)
XLA Ops:
  0.6 1.9 %shard_map.148 = (f32[320,128]{1,0:T(8,128)S(1)}, f32[64,128]{1,0:T(8,128)S(1)}, f32[64,128]{1,0:T(8,128)S(1)}, f32[48,128]{1,0:T(8,128)S(1)}, f32[8,128]{1,0:T(8,128)S(1)}, /*index=5*/bf16[2,160,512]{2,1,0:T(8,128)(2,1)S(1)}) custom-call(s32[1]{0:T(128)} %bitcast.where_ref.refs_0_, f32[3,17,4,128]{3,2,1,0:T(4,128)} %bitcast.14, s32[4,4,128]{2,1,0:T(4,128)} %bitcast.17, ...), custom_call_target="tpu_custom_call" | custom-call | tf_op jit(solution)/shard_map/pallas_call | solution.py:601
  2.6 0.5 %collective-permute-start = (f32[64,128]{1,0:T(8,128)S(1)}, f32[64,128]{1,0:T(8,128)S(1)}, u32[]{:S(2)}, u32[]{:S(2)}) collective-permute-start(f32[64,128]{1,0:T(8,128)S(1)} %get-tuple-element.37), channel_id=1, source_target_pairs={{0,2},{1,3},{2,0},{3,1},{4,6},{5,7},{6,4},{7,5},{8,10},{9,11},{10,... | collective-permute-start | bytes 98312 | tf_op jit(solution)/shard_map/ppermute | solution.py:624
  3.1 2.6 %collective-permute-start.1 = (f32[64,128]{1,0:T(8,128)S(1)}, f32[64,128]{1,0:T(8,128)S(1)}, u32[]{:S(2)}, u32[]{:S(2)}) collective-permute-start(f32[64,128]{1,0:T(8,128)S(1)} %get-tuple-element.38), channel_id=1, source_target_pairs={{0,1},{1,0},{2,4},{3,5},{4,2},{5,3},{6,8},{7,9},{8,6},{9,7},{10,12... | collective-permute-start | bytes 98312 | tf_op jit(solution)/shard_map/ppermute | solution.py:624
  5.7 1.7 %shard_map.149 = (f32[320,128]{1,0:T(8,128)S(1)}, f32[320,128]{1,0:T(8,128)S(1)}, f32[16,128]{1,0:T(8,128)S(1)}, bf16[2,640,512]{2,1,0:T(8,128)(2,1)S(1)}, bf16[512,512]{1,0:T(8,128)(2,1)S(1)}) custom-call(s32[1]{0:T(128)} %bitcast.where_ref.refs_0_, f32[3,17,4,128]{3,2,1,0:T(4,128)} %bitcast.15, f32[17,4,128]{2,1,0:T(4,128)} %bitcast.16, ...), custom_call_target="tpu_custom_call" | custom-call | tf_op jit(solution)/shard_map/pallas_call | solution.py:601
  7.4 2.1 %collective-permute-done.2.refs_7_.refs_8_ = f32[48,128]{1,0:T(8,128)S(1)} collective-permute-done((f32[48,128]{1,0:T(8,128)S(1)}, f32[48,128]{1,0:T(8,128)S(1)}, u32[]{:S(2)}, u32[]{:S(2)}) %collective-permute-start.2) | collective-permute-done | bytes 24608 | tf_op jit(solution)/shard_map/ppermute | solution.py:629
  9.5 1.2 %shard_map.150 = (f32[320,128]{1,0:T(8,128)S(1)}, f32[64,128]{1,0:T(8,128)S(1)}, f32[64,128]{1,0:T(8,128)S(1)}, f32[32,128]{1,0:T(8,128)S(1)}) custom-call(s32[1]{0:T(128)} %bitcast.where_ref.refs_0_, f32[320,128]{1,0:T(8,128)S(1)} %get-tuple-element.33.refs_1_.refs_2_, f32[320,128]{1,0:T(8,128)S(1)} %get-tuple-element.34.refs_2_, ...), custom_call_target="tpu_custom_call" | custom-call | tf_op jit(solution)/shard_map/pallas_call | solution.py:601
  10.7 0.5 %collective-permute-start.4 = (f32[64,128]{1,0:T(8,128)S(1)}, f32[64,128]{1,0:T(8,128)S(1)}, u32[]{:S(2)}, u32[]{:S(2)}) collective-permute-start(f32[64,128]{1,0:T(8,128)S(1)} %get-tuple-element.44), channel_id=1, source_target_pairs={{0,1},{1,0},{2,4},{3,5},{4,2},{5,3},{6,8},{7,9},{8,6},{9,7},{10,12... | collective-permute-start | bytes 98312 | tf_op jit(solution)/shard_map/ppermute | solution.py:624
  11.2 1.6 %collective-permute-start.5 = (f32[32,128]{1,0:T(8,128)S(1)}, f32[32,128]{1,0:T(8,128)S(1)}, u32[]{:S(2)}, u32[]{:S(2)}) collective-permute-start(f32[32,128]{1,0:T(8,128)S(1)} %get-tuple-element.45.refs_9_.refs_8_), channel_id=1, source_target_pairs={{1,0},{0,1},{3,2},{2,3},{5,4},{4,5},{7,6},{6,7},{9,8},{8,9},{11,10... | collective-permute-start | bytes 49160 | tf_op jit(solution)/shard_map/ppermute | solution.py:629
  12.8 2.2 %collective-permute-done.5.refs_7_.refs_9_ = f32[32,128]{1,0:T(8,128)S(1)} collective-permute-done((f32[32,128]{1,0:T(8,128)S(1)}, f32[32,128]{1,0:T(8,128)S(1)}, u32[]{:S(2)}, u32[]{:S(2)}) %collective-permute-start.5) | collective-permute-done | bytes 16416 | tf_op jit(solution)/shard_map/ppermute | solution.py:629
  15.0 1.2 %shard_map.151 = (f32[320,128]{1,0:T(8,128)S(1)}, f32[64,128]{1,0:T(8,128)S(1)}, f32[64,128]{1,0:T(8,128)S(1)}, f32[32,128]{1,0:T(8,128)S(1)}) custom-call(s32[1]{0:T(128)} %bitcast.where_ref.refs_0_, f32[320,128]{1,0:T(8,128)S(1)} %get-tuple-element.42.refs_1_.refs_2_, f32[320,128]{1,0:T(8,128)S(1)} %get-tuple-element.33.refs_1_.refs_2_, ...), custom_call_target="tpu_custom_call" | custom-call | tf_op jit(solution)/shard_map/pallas_call | solution.py:601
  16.2 1.6 %collective-permute-start.7 = (f32[64,128]{1,0:T(8,128)S(1)}, f32[64,128]{1,0:T(8,128)S(1)}, u32[]{:S(2)}, u32[]{:S(2)}) collective-permute-start(f32[64,128]{1,0:T(8,128)S(1)} %get-tuple-element.48), channel_id=1, source_target_pairs={{0,1},{1,0},{2,4},{3,5},{4,2},{5,3},{6,8},{7,9},{8,6},{9,7},{10,12... | collective-permute-start | bytes 98312 | tf_op jit(solution)/shard_map/ppermute | solution.py:624
  17.8 0.4 %collective-permute-start.8 = (f32[32,128]{1,0:T(8,128)S(1)}, f32[32,128]{1,0:T(8,128)S(1)}, u32[]{:S(2)}, u32[]{:S(2)}) collective-permute-start(f32[32,128]{1,0:T(8,128)S(1)} %get-tuple-element.49.refs_9_.refs_10_), channel_id=1, source_target_pairs={{1,0},{0,1},{3,2},{2,3},{5,4},{4,5},{7,6},{6,7},{9,8},{8,9},{11,10... | collective-permute-start | bytes 49160 | tf_op jit(solution)/shard_map/ppermute | solution.py:629
  18.3 3.3 %collective-permute-done.8.refs_7_.refs_11_ = f32[32,128]{1,0:T(8,128)S(1)} collective-permute-done((f32[32,128]{1,0:T(8,128)S(1)}, f32[32,128]{1,0:T(8,128)S(1)}, u32[]{:S(2)}, u32[]{:S(2)}) %collective-permute-start.8) | collective-permute-done | bytes 16416 | tf_op jit(solution)/shard_map/ppermute | solution.py:629
  21.6 1.2 %shard_map.152 = (f32[320,128]{1,0:T(8,128)S(1)}, f32[64,128]{1,0:T(8,128)S(1)}, f32[64,128]{1,0:T(8,128)S(1)}, f32[32,128]{1,0:T(8,128)S(1)}) custom-call(s32[1]{0:T(128)} %bitcast.where_ref.refs_0_, f32[320,128]{1,0:T(8,128)S(1)} %get-tuple-element.46.refs_1_.refs_2_, f32[320,128]{1,0:T(8,128)S(1)} %get-tuple-element.42.refs_1_.refs_2_, ...), custom_call_target="tpu_custom_call" | custom-call | tf_op jit(solution)/shard_map/pallas_call | solution.py:601
  22.8 0.7 %collective-permute-start.10 = (f32[64,128]{1,0:T(8,128)S(1)}, f32[64,128]{1,0:T(8,128)S(1)}, u32[]{:S(2)}, u32[]{:S(2)}) collective-permute-start(f32[64,128]{1,0:T(8,128)S(1)} %get-tuple-element.52), channel_id=1, source_target_pairs={{0,1},{1,0},{2,4},{3,5},{4,2},{5,3},{6,8},{7,9},{8,6},{9,7},{10,12... | collective-permute-start | bytes 98312 | tf_op jit(solution)/shard_map/ppermute | solution.py:624
  23.5 1.4 %collective-permute-start.11 = (f32[32,128]{1,0:T(8,128)S(1)}, f32[32,128]{1,0:T(8,128)S(1)}, u32[]{:S(2)}, u32[]{:S(2)}) collective-permute-start(f32[32,128]{1,0:T(8,128)S(1)} %get-tuple-element.53.refs_12_.refs_9_), channel_id=1, source_target_pairs={{1,0},{0,1},{3,2},{2,3},{5,4},{4,5},{7,6},{6,7},{9,8},{8,9},{11,10... | collective-permute-start | bytes 49160 | tf_op jit(solution)/shard_map/ppermute | solution.py:629
  24.9 0.9 %shard_map.153 = (f32[3,17,4,128]{3,2,1,0:T(4,128)}, f32[8,128]{1,0:T(8,128)S(1)}) custom-call(f32[320,128]{1,0:T(8,128)S(1)} %get-tuple-element.50.field_ref.refs_1_, bf16[512,512]{1,0:T(8,128)(2,1)S(1)} %get-tuple-element.55.back_ref.refs_14_), custom_call_target="tpu_custom_call" | custom-call | tf_op jit(solution)/shard_map/pallas_call | solution.py:601
  25.9 1.4 %collective-permute-done.11.refs_13_.refs_7_ = f32[32,128]{1,0:T(8,128)S(1)} collective-permute-done((f32[32,128]{1,0:T(8,128)S(1)}, f32[32,128]{1,0:T(8,128)S(1)}, u32[]{:S(2)}, u32[]{:S(2)}) %collective-permute-start.11) | collective-permute-done | bytes 16416 | tf_op jit(solution)/shard_map/ppermute | solution.py:629
  27.3 0.7 %shard_map.154 = (f32[2,128]{1,0:T(2,128)S(1)}, f32[2,128]{1,0:T(2,128)S(1)}, f32[2,128]{1,0:T(2,128)S(1)}, f32[2,128]{1,0:T(2,128)S(1)}, f32[2,128]{1,0:T(2,128)S(1)}) custom-call(s32[1]{0:T(128)} %bitcast.where_ref.refs_0_, s32[1,4]{1,0:T(1,128)S(1)} %copy-done, f32[16,128]{1,0:T(8,128)S(1)} %get-tuple-element.54.refs_2_, ...), custom_call_target="tpu_custom_call" | custom-call | tf_op jit(solution)/shard_map/pallas_call | solution.py:601
  28.0 1.5 %collective-permute-start.13 = (f32[2,128]{1,0:T(2,128)S(1)}, f32[2,128]{1,0:T(2,128)S(1)}, u32[]{:S(2)}, u32[]{:S(2)}) collective-permute-start(f32[2,128]{1,0:T(2,128)S(1)} %get-tuple-element.60), channel_id=1, source_target_pairs={{0,1},{1,0},{2,4},{3,5},{4,2},{5,3},{6,8},{7,9},{8,6},{9,7},{10,12... | collective-permute-start | bytes 3080 | tf_op jit(solution)/shard_map/ppermute | solution.py:624
  29.4 0.7 %collective-permute-start.14 = (f32[2,128]{1,0:T(2,128)S(1)}, f32[2,128]{1,0:T(2,128)S(1)}, u32[]{:S(2)}, u32[]{:S(2)}) collective-permute-start(f32[2,128]{1,0:T(2,128)S(1)} %get-tuple-element.61), channel_id=1, source_target_pairs={{0,4},{1,5},{2,6},{3,7},{4,0},{5,1},{6,2},{7,3},{8,12},{9,13},{10,... | collective-permute-start | bytes 3080 | tf_op jit(solution)/shard_map/ppermute | solution.py:624
  30.1 1.4 %collective-permute-start.15 = (f32[2,128]{1,0:T(2,128)S(1)}, f32[2,128]{1,0:T(2,128)S(1)}, u32[]{:S(2)}, u32[]{:S(2)}) collective-permute-start(f32[2,128]{1,0:T(2,128)S(1)} %get-tuple-element.62), channel_id=1, source_target_pairs={{0,1},{1,0},{2,3},{3,2},{4,8},{5,9},{6,10},{7,11},{8,4},{9,5},{10,... | collective-permute-start | bytes 3080 | tf_op jit(solution)/shard_map/ppermute | solution.py:624
  31.5 1.7 %shard_map.155 = f32[3,17,4,128]{3,2,1,0:T(4,128)} custom-call(s32[1]{0:T(128)} %bitcast.where_ref.refs_0_, f32[320,128]{1,0:T(8,128)S(1)} %get-tuple-element.50.field_ref.refs_1_, f32[320,128]{1,0:T(8,128)S(1)} %get-tuple-element.46.refs_1_.refs_2_, f32[320,128]{1,0:T(8,128)S(1)} %get-tuple-element.35.refs_3_, f32[8,128]{1,0:T(8,128)S(1)} %get-tuple-element.36.refs_4_, ...), custom_call_target="tpu_custom_call" | custom-call | tf_op jit(solution)/shard_map/pallas_call | solution.py:601
  33.7 0.6 %add_bitcast_fusion = f32[1,2,128]{2,1,0:T(2,128)} fusion(f32[2,128]{1,0:T(2,128)S(1)} %collective-permute-done.15, f32[2,128]{1,0:T(2,128)S(1)} %collective-permute-done.14, f32[2,128]{1,0:T(2,128)S(1)} %collective-permute-done.13, f32[2,128]{1,0:T(2,128)S(1)} %get-tuple-element.57.refs_13_, f32[2,128]{1,0:T(2,128)S(1)} %collective-permute-done.12), kind=kLoop, calls=%fused_computation | loop fusion | flops 1024 | bytes 6144 | tf_op jit(solution)/shard_map/broadcast_in_dim | solution.py:744
  (19 shorter events, 0.6 us)
Async XLA Ops:
  2.6 6.9 %collective-permute-start = (f32[64,128]{1,0:T(8,128)S(1)}, f32[64,128]{1,0:T(8,128)S(1)}, u32[]{:S(2)}, u32[]{:S(2)}) collective-permute-start(f32[64,128]{1,0:T(8,128)S(1)} %get-tuple-element.37), channel_id=1, source_target_pairs={{0,2},{1,3},{2,0},{3,1},{4,6},{5,7},{6,4},{7,5},{8,10},{9,11},{10,... | collective-permute-start | bytes 98312 | tf_op jit(solution)/shard_map/ppermute | solution.py:624
  3.1 6.4 %collective-permute-start.1 = (f32[64,128]{1,0:T(8,128)S(1)}, f32[64,128]{1,0:T(8,128)S(1)}, u32[]{:S(2)}, u32[]{:S(2)}) collective-permute-start(f32[64,128]{1,0:T(8,128)S(1)} %get-tuple-element.38), channel_id=1, source_target_pairs={{0,1},{1,0},{2,4},{3,5},{4,2},{5,3},{6,8},{7,9},{8,6},{9,7},{10,12... | collective-permute-start | bytes 98312 | tf_op jit(solution)/shard_map/ppermute | solution.py:624
  5.7 3.8 %collective-permute-start.2 = (f32[48,128]{1,0:T(8,128)S(1)}, f32[48,128]{1,0:T(8,128)S(1)}, u32[]{:S(2)}, u32[]{:S(2)}) collective-permute-start(f32[48,128]{1,0:T(8,128)S(1)} %get-tuple-element.39.refs_9_.refs_10_.refs_6_), channel_id=1, source_target_pairs={{1,0},{0,1},{3,2},{2,3},{5,4},{4,5},{7,6},{6,7},{9,8},{8,9},{11,10... | collective-permute-start | bytes 73736 | tf_op jit(solution)/shard_map/ppermute | solution.py:629
  10.7 4.3 %collective-permute-start.3 = (f32[64,128]{1,0:T(8,128)S(1)}, f32[64,128]{1,0:T(8,128)S(1)}, u32[]{:S(2)}, u32[]{:S(2)}) collective-permute-start(f32[64,128]{1,0:T(8,128)S(1)} %get-tuple-element.43), channel_id=1, source_target_pairs={{0,2},{1,3},{2,0},{3,1},{4,6},{5,7},{6,4},{7,5},{8,10},{9,11},{10,... | collective-permute-start | bytes 98312 | tf_op jit(solution)/shard_map/ppermute | solution.py:624
  10.7 4.3 %collective-permute-start.4 = (f32[64,128]{1,0:T(8,128)S(1)}, f32[64,128]{1,0:T(8,128)S(1)}, u32[]{:S(2)}, u32[]{:S(2)}) collective-permute-start(f32[64,128]{1,0:T(8,128)S(1)} %get-tuple-element.44), channel_id=1, source_target_pairs={{0,1},{1,0},{2,4},{3,5},{4,2},{5,3},{6,8},{7,9},{8,6},{9,7},{10,12... | collective-permute-start | bytes 98312 | tf_op jit(solution)/shard_map/ppermute | solution.py:624
  11.2 3.8 %collective-permute-start.5 = (f32[32,128]{1,0:T(8,128)S(1)}, f32[32,128]{1,0:T(8,128)S(1)}, u32[]{:S(2)}, u32[]{:S(2)}) collective-permute-start(f32[32,128]{1,0:T(8,128)S(1)} %get-tuple-element.45.refs_9_.refs_8_), channel_id=1, source_target_pairs={{1,0},{0,1},{3,2},{2,3},{5,4},{4,5},{7,6},{6,7},{9,8},{8,9},{11,10... | collective-permute-start | bytes 49160 | tf_op jit(solution)/shard_map/ppermute | solution.py:629
  16.2 5.4 %collective-permute-start.6 = (f32[64,128]{1,0:T(8,128)S(1)}, f32[64,128]{1,0:T(8,128)S(1)}, u32[]{:S(2)}, u32[]{:S(2)}) collective-permute-start(f32[64,128]{1,0:T(8,128)S(1)} %get-tuple-element.47), channel_id=1, source_target_pairs={{0,2},{1,3},{2,0},{3,1},{4,6},{5,7},{6,4},{7,5},{8,10},{9,11},{10,... | collective-permute-start | bytes 98312 | tf_op jit(solution)/shard_map/ppermute | solution.py:624
  16.2 5.4 %collective-permute-start.7 = (f32[64,128]{1,0:T(8,128)S(1)}, f32[64,128]{1,0:T(8,128)S(1)}, u32[]{:S(2)}, u32[]{:S(2)}) collective-permute-start(f32[64,128]{1,0:T(8,128)S(1)} %get-tuple-element.48), channel_id=1, source_target_pairs={{0,1},{1,0},{2,4},{3,5},{4,2},{5,3},{6,8},{7,9},{8,6},{9,7},{10,12... | collective-permute-start | bytes 98312 | tf_op jit(solution)/shard_map/ppermute | solution.py:624
  17.8 3.7 %collective-permute-start.8 = (f32[32,128]{1,0:T(8,128)S(1)}, f32[32,128]{1,0:T(8,128)S(1)}, u32[]{:S(2)}, u32[]{:S(2)}) collective-permute-start(f32[32,128]{1,0:T(8,128)S(1)} %get-tuple-element.49.refs_9_.refs_10_), channel_id=1, source_target_pairs={{1,0},{0,1},{3,2},{2,3},{5,4},{4,5},{7,6},{6,7},{9,8},{8,9},{11,10... | collective-permute-start | bytes 49160 | tf_op jit(solution)/shard_map/ppermute | solution.py:629
  21.6 5.7 %copy-start = (s32[1,4]{1,0:T(1,128)S(1)}, s32[1,4]{1,0:T(1,128)}, u32[]{:S(2)}) copy-start(s32[1,4]{1,0:T(1,128)} %refs_1_.1) | copy-start | bytes 52
  22.8 4.5 %collective-permute-start.9 = (f32[64,128]{1,0:T(8,128)S(1)}, f32[64,128]{1,0:T(8,128)S(1)}, u32[]{:S(2)}, u32[]{:S(2)}) collective-permute-start(f32[64,128]{1,0:T(8,128)S(1)} %get-tuple-element.51), channel_id=1, source_target_pairs={{0,2},{1,3},{2,0},{3,1},{4,6},{5,7},{6,4},{7,5},{8,10},{9,11},{10,... | collective-permute-start | bytes 98312 | tf_op jit(solution)/shard_map/ppermute | solution.py:624
  22.8 4.4 %collective-permute-start.10 = (f32[64,128]{1,0:T(8,128)S(1)}, f32[64,128]{1,0:T(8,128)S(1)}, u32[]{:S(2)}, u32[]{:S(2)}) collective-permute-start(f32[64,128]{1,0:T(8,128)S(1)} %get-tuple-element.52), channel_id=1, source_target_pairs={{0,1},{1,0},{2,4},{3,5},{4,2},{5,3},{6,8},{7,9},{8,6},{9,7},{10,12... | collective-permute-start | bytes 98312 | tf_op jit(solution)/shard_map/ppermute | solution.py:624
  23.5 3.7 %collective-permute-start.11 = (f32[32,128]{1,0:T(8,128)S(1)}, f32[32,128]{1,0:T(8,128)S(1)}, u32[]{:S(2)}, u32[]{:S(2)}) collective-permute-start(f32[32,128]{1,0:T(8,128)S(1)} %get-tuple-element.53.refs_12_.refs_9_), channel_id=1, source_target_pairs={{1,0},{0,1},{3,2},{2,3},{5,4},{4,5},{7,6},{6,7},{9,8},{8,9},{11,10... | collective-permute-start | bytes 49160 | tf_op jit(solution)/shard_map/ppermute | solution.py:629
  28.0 5.3 %collective-permute-start.12 = (f32[2,128]{1,0:T(2,128)S(1)}, f32[2,128]{1,0:T(2,128)S(1)}, u32[]{:S(2)}, u32[]{:S(2)}) collective-permute-start(f32[2,128]{1,0:T(2,128)S(1)} %get-tuple-element.59), channel_id=1, source_target_pairs={{0,2},{1,3},{2,0},{3,1},{4,6},{5,7},{6,4},{7,5},{8,10},{9,11},{10,... | collective-permute-start | bytes 3080 | tf_op jit(solution)/shard_map/ppermute | solution.py:624
  28.0 5.3 %collective-permute-start.13 = (f32[2,128]{1,0:T(2,128)S(1)}, f32[2,128]{1,0:T(2,128)S(1)}, u32[]{:S(2)}, u32[]{:S(2)}) collective-permute-start(f32[2,128]{1,0:T(2,128)S(1)} %get-tuple-element.60), channel_id=1, source_target_pairs={{0,1},{1,0},{2,4},{3,5},{4,2},{5,3},{6,8},{7,9},{8,6},{9,7},{10,12... | collective-permute-start | bytes 3080 | tf_op jit(solution)/shard_map/ppermute | solution.py:624
  29.4 3.8 %collective-permute-start.14 = (f32[2,128]{1,0:T(2,128)S(1)}, f32[2,128]{1,0:T(2,128)S(1)}, u32[]{:S(2)}, u32[]{:S(2)}) collective-permute-start(f32[2,128]{1,0:T(2,128)S(1)} %get-tuple-element.61), channel_id=1, source_target_pairs={{0,4},{1,5},{2,6},{3,7},{4,0},{5,1},{6,2},{7,3},{8,12},{9,13},{10,... | collective-permute-start | bytes 3080 | tf_op jit(solution)/shard_map/ppermute | solution.py:624
  30.1 3.6 %collective-permute-start.15 = (f32[2,128]{1,0:T(2,128)S(1)}, f32[2,128]{1,0:T(2,128)S(1)}, u32[]{:S(2)}, u32[]{:S(2)}) collective-permute-start(f32[2,128]{1,0:T(2,128)S(1)} %get-tuple-element.62), channel_id=1, source_target_pairs={{0,1},{1,0},{2,3},{3,2},{4,8},{5,9},{6,10},{7,11},{8,4},{9,5},{10,... | collective-permute-start | bytes 3080 | tf_op jit(solution)/shard_map/ppermute | solution.py:624
where the time goes:
time: 34.4 us; the launch traced here: 34.3 us
  starting transfers between devices  13 us (38%)
  Pallas kernels  10.6 us (31%)
  waiting for transfers between devices  9.35 us (27%)
  between operations  0.7 us (2%)
  other arithmetic  0.57 us (2%)
    pallas_call x8, Pallas kernels, kernel_call(): pl.pallas_call(functools.partial(body, **static) if static else body, out...  10.6 us
    ppermute x12, starting transfers between devices, swapped(): return lax.ppermute(block, ('dom', 'depth'), route)  9.49 us
    ppermute x4, waiting for transfers between devices, from_behind(): lax.ppermute(block, axis, [((i - distance) % size, i) for i in range(size)])  8.9 us
    ppermute x4, starting transfers between devices, from_behind(): lax.ppermute(block, axis, [((i - distance) % size, i) for i in range(size)])  3.55 us
  transfers between devices with their start and end apart: 16, of which 5 were waited for; matrix products, arithmetic and copies ran while one was open for 0% of the time, Pallas kernels for 13%

commit v1 on v0

--- a/solution.py
+++ b/solution.py
@@ -82,21 +82,29 @@
 
 
 OWN_COLS = 384
-FAR_COLS = 128
+
+
+def padded_table(table, columns):
+    return np.pad(table, ((0, 0), (0, columns - table.shape[1])))
 
 
 @functools.cache
 def stiffness_tables():
     wide = element_stiffness()
     own = 4 * PLANE
-    parts = []
-    for rows in (slice(0, own), slice(own, own + PLANE)):
-        both = np.concatenate([w[rows] for w in wide])
-        table = np.zeros((both.shape[0], OWN_COLS + FAR_COLS))
-        table[:, :own] = both[:, :own]
-        table[:, OWN_COLS : OWN_COLS + PLANE] = both[:, own:]
-        parts.append(two_parts(table))
-    return parts
+    inner = np.concatenate([w[:own] for w in wide])
+    outer = np.concatenate([w[own:] for w in wide])
+
+    def three(table):
+        high, low = two_parts(table)
+        return padded_table(np.concatenate([high, low, high], axis=1), 256)
+
+    return (
+        two_parts(padded_table(inner[:, :own], OWN_COLS)),
+        three(inner[:, own:]),
+        two_parts(padded_table(outer[:, :own], OWN_COLS)),
+        three(outer[:, own:]),
+    )
 
 
 @functools.cache
@@ -182,6 +190,12 @@
     return ones_where(lambda c, z: z == 4 * (c % z_elems) + c // z_elems, (lanes, lanes))
 
 
+def stacked_dot(table, value):
+    high, low = pieces(value, 2)
+    gap = jnp.zeros((table.shape[1] - 3 * value.shape[0], value.shape[1]), jnp.bfloat16)
+    return dot(table, jnp.concatenate([high, high, low, gap], axis=0))
+
+
 def to_elements(native, scratch, table, y_elems):
     group = 4 * BLOCK
     scratch[...] = jnp.zeros_like(scratch)
@@ -289,7 +303,7 @@
     padded = jnp.concatenate(
         [own, jnp.zeros((OWN_COLS - own.shape[0], lanes), jnp.float32)], axis=0
     )
-    result = split_dot(edge_ref[0, :, :OWN_COLS], edge_ref[1, :, :OWN_COLS], padded)
+    result = split_dot(edge_ref[0], edge_ref[1], padded)
     force = lame_row * result[:PLANE] + shear_row * result[PLANE:]
     top = force[:BLOCK] + jnp.where(
         above_lanes(lanes, z_elems), pltpu.roll(force[4 * BLOCK :], 1, 1), 0.0
@@ -298,6 +312,13 @@
     top = jnp.where(row == BLOCK - 1, lame_row, top)
     second = jnp.where(row == BLOCK - 1, shear_row, force[BLOCK : 2 * BLOCK])
     return jnp.concatenate([top, second, force[2 * BLOCK : 4 * BLOCK]], axis=0)
+
+
+def own_force(own_ref, cur, lame_row, shear_row):
+    rows, lanes = cur.shape
+    padded = jnp.concatenate([cur, jnp.zeros((OWN_COLS - rows, lanes), jnp.float32)], axis=0)
+    result = split_dot(own_ref[0], own_ref[1], padded)
+    return lame_row * result[:rows] + shear_row * result[rows:]
 
 
 def start_copies(pairs, sems):
@@ -348,30 +369,35 @@
     parity = where_ref[0] % 2
     gather = gather_table(lanes, z_elems)
     fault = fault_table(lanes, z_elems)
-    copies[0].wait()
-    cur = to_elements(lambda c, y: now_ref[c, y], scratch, gather, y_elems)
-    cur_ref[...] = cur
-    steps = flags_ref.shape[0]
     copies[1].wait()
     copies[2].wait()
     weak = weak_ref[...]
     tangent = []
-    for i in range(steps):
+    for i in range(flags_ref.shape[0]):
         flag = flags_ref[i]
         tangent.append(
             jnp.where(flag == 0, lock_stiffness, jnp.where(flag == 1, -weak, 0.0))
         )
-    tangent = exact_dot(jnp.concatenate(tangent, axis=0), fault)
-    fault_out_ref[...] = jnp.concatenate([fault_message(cur, z_elems), tangent], axis=0)
+    fault_out_ref[32:] = exact_dot(jnp.concatenate(tangent, axis=0), fault)
     copies[3].wait()
     copies[4].wait()
     lame_row, shear_row = material_rows(lame_ref, shear_ref)
     material_ref[...] = jnp.concatenate(
         [lame_row, shear_row, jnp.zeros((6, lanes), jnp.float32)], axis=0
     )
+    copies[0].wait()
+    cur = to_elements(lambda c, y: now_ref[c, y], scratch, gather, y_elems)
     copies[5].wait()
     right = edge_force(edge_ref, cur, lame_row, shear_row, z_elems)
     even_ref[...], odd_ref[...] = select_messages(parity, cur[: 4 * BLOCK], right)
+    cur_ref[...] = cur
+    fault_out_ref[:32] = fault_message(cur, z_elems)
+
+
+def prepare_kernel(cur_ref, material_ref, own_ref, touch_ref, base_ref, edge_part_ref):
+    cur = cur_ref[...]
+    base_ref[...] = own_force(own_ref, cur, material_ref[0:1], material_ref[1:2])
+    edge_part_ref[...] = stacked_dot(touch_ref[...], cur[:PLANE])
 
 
 def setup_kernel(
@@ -381,12 +407,16 @@
     flags_hbm,
     stress_hbm,
     mass_hbm,
-    main_hbm,
+    own_hbm,
+    far_hbm,
+    touch_hbm,
     back_hbm,
     fol_ref,
     minv_ref,
     weight_ref,
-    main_ref,
+    own_ref,
+    far_ref,
+    touch_ref,
     back_ref,
     scratch,
     next_ref,
@@ -406,7 +436,9 @@
             (flags_hbm, flags_ref),
             (stress_hbm, stress_ref),
             (mass_hbm, mass_ref),
-            (main_hbm, main_ref),
+            (own_hbm, own_ref),
+            (far_hbm, far_ref),
+            (touch_hbm, touch_ref),
             (back_hbm, back_ref),
         ],
         sems,
@@ -430,13 +462,13 @@
             stress * jnp.where(flag == 1, 0.5, jnp.where(flag == 2, 1.0, 0.0))
         )
     weight_ref[...] = exact_dot(jnp.concatenate(weights, axis=0), fault)
-    copies[5].wait()
-    copies[6].wait()
+    for copy in copies[5:]:
+        copy.wait()
 
 
 def advance(
-    step, place, last_place, cur, fol, minv, material, even_in, odd_in, fault_in, tangents, main_ref, edge_ref,
-    own_fault, y_elems, z_elems,
+    step, place, last_place, cur, fol, minv, base, touch, material, even_in, odd_in, fault_in, tangents, far_table, own_fault,
+    y_elems, z_elems,
 ):
     lanes = cur.shape[1]
     even = place % 2 == 0
@@ -448,17 +480,8 @@
     )
     far = jnp.concatenate([far, below], axis=0)
     lame_row, shear_row = material[0:1], material[1:2]
-    zeros = jnp.zeros((FAR_COLS - PLANE, lanes), jnp.float32)
-    gap = jnp.zeros((OWN_COLS - 4 * PLANE, lanes), jnp.float32)
-    result = split_dot(
-        main_ref[0], main_ref[1], jnp.concatenate([cur, gap, far, zeros], axis=0)
-    )
-    force = lame_row * result[: 4 * PLANE] + shear_row * result[4 * PLANE :]
-    touch = split_dot(
-        edge_ref[0, :, OWN_COLS:],
-        edge_ref[1, :, OWN_COLS:],
-        jnp.concatenate([cur[:PLANE], zeros], axis=0),
-    )
+    result = stacked_dot(far_table, far)
+    force = base + (lame_row * result[: 4 * PLANE] + shear_row * result[4 * PLANE :])
     left_lame = left[BLOCK - 1 : BLOCK]
     left_shear = left[2 * BLOCK - 1 : 2 * BLOCK]
     from_left = left_lame * touch[:PLANE] + left_shear * touch[PLANE:]
@@ -521,19 +544,20 @@
 
 def step_kernel(*refs, step, last, last_place, pair, y_elems, z_elems):
     refs = list(refs)
-    where_ref, cur_ref, fol_ref, minv_ref, material_ref, even_ref, odd_ref = refs[:7]
-    refs = refs[7:]
+    where_ref, cur_ref, fol_ref, minv_ref, base_ref, touch_ref, material_ref = refs[:7]
+    even_ref, odd_ref = refs[7:9]
+    refs = refs[9:]
     up_ref = refs.pop(0)
     down_ref = None if pair else refs.pop(0)
-    first_up_ref, own_ref, first_own_ref, main_ref, edge_ref = refs[:5]
+    first_up_ref, own_ref, first_own_ref, far_ref, edge_ref = refs[:5]
     refs = refs[5:]
     place = where_ref[0]
     cur = cur_ref[...]
     tangents = (first_up_ref[32:], first_own_ref[32:])
     new = advance(
-        step, place, last_place, cur, fol_ref[...], minv_ref[...], material_ref[...], even_ref[...], odd_ref[...],
-        fault_input(up_ref, down_ref, 32), tangents, main_ref, edge_ref, swap_rows(own_ref[:32]),
-        y_elems, z_elems,
+        step, place, last_place, cur, fol_ref[...], minv_ref[...], base_ref[...], touch_ref[...],
+        material_ref[...], even_ref[...], odd_ref[...], fault_input(up_ref, down_ref, 32), tangents,
+        far_ref[...], swap_rows(own_ref[:32]), y_elems, z_elems,
     )
     if last:
         _, back_ref, out_ref, scratch = refs
@@ -546,30 +570,39 @@
         even_out[...], odd_out[...] = select_messages(place % 2, new[: 4 * BLOCK], right)
 
 
-def output_kernel(field_ref, back_ref, out_ref, mark_ref, scratch, *, y_elems):
-    mark_ref[...] = jnp.zeros_like(mark_ref)
+def output_kernel(*refs, pair, steps, y_elems, z_elems):
+    field_ref, back_ref, weight_ref = refs[:3]
+    out_ref, grad_ref, table_ref, scratch = refs[-4:]
+    messages = refs[3:-4]
+    count = 2 if pair else 3
+    grads = [jnp.zeros((8, weight_ref.shape[1]), jnp.float32) for _ in range(4)]
+    for i in range(steps):
+        group = messages[count * i : count * (i + 1)]
+        slip = -swap_rows(group[0][:32])
+        if i < steps - 1:
+            slip = slip + fault_input(group[1], None if pair else group[2], 32)
+        for x in range(4):
+            grads[x] = grads[x] + slip[8 * x : 8 * x + 8] * weight_ref[4 * i + x : 4 * i + x + 1]
+    grad_ref[...] = jnp.concatenate(grads, axis=0)
+    table_ref[...] = fault_table_back(weight_ref.shape[1], z_elems)
     from_elements(field_ref[...], scratch, back_ref, out_ref, y_elems)
 
 
-def patch_kernel(*refs, pair, steps, z_elems):
-    where_ref, owner_ref, weight_ref = refs[:3]
-    messages = refs[6:-5]
+def patch_kernel(*refs, pair, steps):
+    where_ref, owner_ref, weight_ref, grad_ref, table_ref, _, _, _, up_ref = refs[:9]
+    down_ref = None if pair else refs[9]
     home_out, out_a, out_b, out_c, out_d = refs[-5:]
     place = where_ref[0]
     lanes = weight_ref.shape[1]
-    count = 2 if pair else 3
-    grads = [jnp.zeros((8, lanes), jnp.float32) for _ in range(4)]
-    for i in range(steps):
-        group = messages[count * i : count * (i + 1)]
-        slip = fault_input(group[1], None if pair else group[2], 32) - swap_rows(group[0][:32])
-        for x in range(4):
-            grads[x] = grads[x] + slip[8 * x : 8 * x + 8] * weight_ref[4 * i + x : 4 * i + x + 1]
+    slip = fault_input(up_ref, down_ref, 32)
     wide = 16
     number = lax.broadcasted_iota(jnp.int32, (wide, lanes), 0) + (place - REACH) * PATCH_DEV
     total = jnp.zeros((wide, lanes), jnp.float32)
     for x in range(4):
-        total = total + jnp.where(number == owner_ref[0, x], grads[x][4:5], 0.0)
-    total = exact_dot(total, fault_table_back(lanes, z_elems))
+        at, k = 8 * x + 4, 4 * (steps - 1) + x
+        grad = grad_ref[at : at + 1] + slip[at : at + 1] * weight_ref[k : k + 1]
+        total = total + jnp.where(number == owner_ref[0, x], grad, 0.0)
+    total = exact_dot(total, table_ref[...])
     rows = [total[2 * i : 2 * i + 2] for i in range(5)]
     home_out[...] = rows[2]
     even = place % 2 == 0
@@ -646,7 +679,7 @@
     steps = branch_flags.shape[0]
     pair = lax.axis_size("depth") == 2
     place = lax.axis_index("dom").astype(jnp.int32).reshape(1)
-    main_table, edge_table = (jnp.asarray(t) for t in stiffness_tables())
+    own_table, far_table, edge_table, touch_table = (jnp.asarray(t) for t in stiffness_tables())
     back = jnp.asarray(back_table(y_elems, z_elems))
     mass = jnp.asarray(mass_table(y_elems, z_elems))
     now = jnp.transpose(adjoint_now, (0, 2, 1, 3))
@@ -662,7 +695,8 @@
             faults = [from_behind(fault_rows, "depth", 1)]
         else:
             faults = [from_behind(fault_rows, "depth", 1), from_behind(fault_rows, "depth", -1)]
-        return swapped(even, 1, 0), swapped(odd, 1, 1), faults
+        odd_in = swapped(odd, 1, 1)
+        return swapped(even, 1, 0), odd_in, faults
 
     cur, even, odd, fault_rows, material, edge_table = kernel_call(
         first_kernel,
@@ -681,17 +715,15 @@
     first_fault = fault_rows
     even_in, odd_in, fault_in = exchange(even, odd, fault_rows)
     first_in = fault_in
-    fol, minv, weight, main_table, back = kernel_call(
+    tables = (own_table, far_table, touch_table, back)
+    fol, minv, weight, own_table, far_table, touch_table, back = kernel_call(
         setup_kernel,
-        [
-            field, field, (4 * steps, lanes), (main_table.shape, main_table.dtype),
-            (back.shape, back.dtype),
-        ],
-        (place, following, rho, flags, normal_stress[0], mass, main_table, back),
+        [field, field, (4 * steps, lanes)] + [(t.shape, t.dtype) for t in tables],
+        (place, following, rho, flags, normal_stress[0], mass) + tables,
         (0,),
         [native],
-        range(1, 8),
-        (6, 7),
+        range(1, 10),
+        range(6, 10),
         y_elems=y_elems,
         z_elems=z_elems,
     )
@@ -699,8 +731,14 @@
     for step in range(steps):
         last = step == steps - 1
         seen += [fault_rows] + fault_in
-        args = [place, cur, fol, minv, material, even_in, odd_in] + fault_in
-        args += [first_in[0], fault_rows, first_fault, main_table, edge_table]
+        base, touch = kernel_call(
+            prepare_kernel,
+            [field, (2 * PLANE, lanes)],
+            [cur, material, own_table, touch_table],
+            (),
+        )
+        args = [place, cur, fol, minv, base, touch, material, even_in, odd_in] + fault_in
+        args += [first_in[0], fault_rows, first_fault, far_table, edge_table]
         static = dict(
             step=step, last=last, last_place=lax.axis_size("dom") - 1, pair=pair, y_elems=y_elems,
             z_elems=z_elems,
@@ -713,22 +751,30 @@
             even_in, odd_in, fault_in = exchange(even, odd, fault_rows)
         else:
             whole = (3, 4 * y_elems + 1, 4, lanes)
-            later, mark = kernel_call(
-                output_kernel, [whole, (8, lanes)], [cur, back], (), [native], y_elems=y_elems
+            known = seen[: len(seen) - len(fault_in)]
+            later, grad, table = kernel_call(
+                output_kernel,
+                [whole, (32, lanes), ((lanes, lanes), jnp.bfloat16)],
+                [cur, back, weight] + known,
+                (),
+                [native],
+                pair=pair,
+                steps=steps,
+                y_elems=y_elems,
+                z_elems=z_elems,
             )
             sums = kernel_call(
                 patch_kernel,
                 [(PATCH_DEV, lanes)] * 5,
-                [place, patch_owner, weight, even_in, odd_in, mark] + seen,
+                [place, patch_owner, weight, grad, table, even_in, odd_in, touch] + fault_in,
                 (0, 1),
-                unread=(3, 4, 5),
+                unread=(5, 6, 7),
                 pair=pair,
                 steps=steps,
-                z_elems=z_elems,
             )
             patch_sums = sums[0]
-            for out, distance, group in zip(sums[1:], (1, 1, 2, 2), (0, 1, 0, 1)):
-                patch_sums = patch_sums + swapped(out, distance, group)
+            for i, distance, group in ((2, 1, 1), (4, 2, 1), (3, 2, 0), (1, 1, 0)):
+                patch_sums = patch_sums + swapped(sums[i], distance, group)
             earlier = kernel_call(
                 step_kernel,
                 [whole],

time: 34.4 us -> 34.5 us (level)
  waiting for transfers between devices: 9.35 us -> 6.83 us
  Pallas kernels: 10.6 us -> 11.9 us
  starting transfers between devices: 13 us -> 13.7 us
  local copies, waits for them, and re-layouts: 0.01 us -> 0.65 us
    ppermute x4, waiting for transfers between devices: 8.9 us -> 6.79 us  [from_behind(): lax.ppermute(block, axis, [((i - distance) % size, i) for i in range(size)])]
    pallas_call x8 -> x12, Pallas kernels: 10.6 us -> 11.9 us  [kernel_call(): pl.pallas_call(functools.partial(body, **static) if static else body, out...]
    ppermute x12, starting transfers between devices: 9.49 us -> 10.2 us  [swapped(): return lax.ppermute(block, ('dom', 'depth'), route)]
    unnamed x2, local copies, waits for them, and re-layouts: 0.01 us -> 0.65 us
    ppermute x12, waiting for transfers between devices: 0.46 us -> 0.03 us  [swapped(): return lax.ppermute(block, ('dom', 'depth'), route)]
  transfers between devices with their start and end apart: 16 -> 16, of which waited for: 5 -> 4; matrix products, arithmetic and copies ran while one was open for 0% -> 0% of each run, Pallas kernels for 13% -> 18%
where the time goes in v1:
time: 34.5 us; the launch traced here: 34.4 us
  starting transfers between devices  13.7 us (40%)
  Pallas kernels  11.9 us (34%)
  waiting for transfers between devices  6.83 us (20%)
  between operations  0.71 us (2%)
  local copies, waits for them, and re-layouts  0.65 us (2%)
  other arithmetic  0.57 us (2%)
    pallas_call x12, Pallas kernels, kernel_call(): pl.pallas_call(functools.partial(body, **static) if static else body, out...  11.9 us
    ppermute x12, starting transfers between devices, swapped(): return lax.ppermute(block, ('dom', 'depth'), route)  10.2 us
    ppermute x4, waiting for transfers between devices, from_behind(): lax.ppermute(block, axis, [((i - distance) % size, i) for i in range(size)])  6.79 us
    ppermute x4, starting transfers between devices, from_behind(): lax.ppermute(block, axis, [((i - distance) % size, i) for i in range(size)])  3.56 us
  transfers between devices with their start and end apart: 16, of which 4 were waited for; matrix products, arithmetic and copies ran while one was open for 0% of the time, Pallas kernels for 18%

profile of v1, /device:TPU:0, one launch (start us, length us, event | category | flops | bytes accessed | tf_op | source)
XLA Modules:
  0.0 34.4 jit_solution(12790648092030137827)
XLA Ops:
  0.6 1.8 %shard_map.166 = (f32[320,128]{1,0:T(8,128)S(1)}, f32[64,128]{1,0:T(8,128)S(1)}, f32[64,128]{1,0:T(8,128)S(1)}, f32[48,128]{1,0:T(8,128)S(1)}, f32[8,128]{1,0:T(8,128)S(1)}, /*index=5*/bf16[2,160,384]{2,1,0:T(8,128)(2,1)S(1)}) custom-call(s32[1]{0:T(128)} %bitcast.where_ref.refs_0_, f32[3,17,4,128]{3,2,1,0:T(4,128)} %bitcast.14, s32[4,4,128]{2,1,0:T(4,128)} %bitcast.17, ...), custom_call_target="tpu_custom_call" | custom-call | tf_op jit(solution)/shard_map/pallas_call | solution.py:634
  3.0 2.6 %collective-permute-start.1 = (f32[64,128]{1,0:T(8,128)S(1)}, f32[64,128]{1,0:T(8,128)S(1)}, u32[]{:S(2)}, u32[]{:S(2)}) collective-permute-start(f32[64,128]{1,0:T(8,128)S(1)} %get-tuple-element.53), channel_id=1, source_target_pairs={{0,1},{1,0},{2,4},{3,5},{4,2},{5,3},{6,8},{7,9},{8,6},{9,7},{10,12... | collective-permute-start | bytes 98312 | tf_op jit(solution)/shard_map/ppermute | solution.py:657
  5.6 1.7 %shard_map.167 = (f32[320,128]{1,0:T(8,128)S(1)}, f32[320,128]{1,0:T(8,128)S(1)}, f32[16,128]{1,0:T(8,128)S(1)}, bf16[2,640,384]{2,1,0:T(8,128)(2,1)S(1)}, bf16[...) custom-call(s32[1]{0:T(128)} %bitcast.where_ref.refs_0_, ...), custom_call_target="tpu_custom_call" | custom-call | tf_op jit(solution)/shard_map/pallas_call | solution.py:634
  7.9 1.5 %collective-permute-done.2.refs_9_.refs_10_.refs_4_ = f32[48,128]{1,0:T(8,128)S(1)} collective-permute-done((f32[48,128]{1,0:T(8,128)S(1)}, f32[48,128]{1,0:T(8,128)S(1)}, u32[]{:S(2)}, u32[]{:S(2)}) %collective-permute-start.2) | collective-permute-done | bytes 24608 | tf_op jit(solution)/shard_map/ppermute | solution.py:662
  9.4 1.0 %shard_map.169 = (f32[320,128]{1,0:T(8,128)S(1)}, f32[64,128]{1,0:T(8,128)S(1)}, f32[64,128]{1,0:T(8,128)S(1)}, f32[32,128]{1,0:T(8,128)S(1)}) custom-call(s32[1]{0:T(128)} %bitcast.where_ref.refs_0_, f32[320,128]{1,0:T(8,128)S(1)} %get-tuple-element.44.cur_ref.refs_1_.refs_2_, f32[320,128]{1,0:T(8,128)S(1)} %get-tuple-element.45.refs_2_, ...), custom_call_target="tpu_custom_call" | custom-call | tf_op jit(solution)/shard_map/pallas_call | solution.py:634
  10.4 0.6 %collective-permute-start.4 = (f32[64,128]{1,0:T(8,128)S(1)}, f32[64,128]{1,0:T(8,128)S(1)}, u32[]{:S(2)}, u32[]{:S(2)}) collective-permute-start(f32[64,128]{1,0:T(8,128)S(1)} %get-tuple-element.61), channel_id=1, source_target_pairs={{0,1},{1,0},{2,4},{3,5},{4,2},{5,3},{6,8},{7,9},{8,6},{9,7},{10,12... | collective-permute-start | bytes 98312 | tf_op jit(solution)/shard_map/ppermute | solution.py:657
  11.0 1.6 %collective-permute-start.5 = (f32[32,128]{1,0:T(8,128)S(1)}, f32[32,128]{1,0:T(8,128)S(1)}, u32[]{:S(2)}, u32[]{:S(2)}) collective-permute-start(f32[32,128]{1,0:T(8,128)S(1)} %get-tuple-element.62.refs_11_.refs_5_), channel_id=1, source_target_pairs={{1,0},{0,1},{3,2},{2,3},{5,4},{4,5},{7,6},{6,7},{9,8},{8,9},{11,10... | collective-permute-start | bytes 49160 | tf_op jit(solution)/shard_map/ppermute | solution.py:662
  13.0 1.8 %collective-permute-done.5.refs_9_.refs_6_ = f32[32,128]{1,0:T(8,128)S(1)} collective-permute-done((f32[32,128]{1,0:T(8,128)S(1)}, f32[32,128]{1,0:T(8,128)S(1)}, u32[]{:S(2)}, u32[]{:S(2)}) %collective-permute-start.5) | collective-permute-done | bytes 16416 | tf_op jit(solution)/shard_map/ppermute | solution.py:662
  14.8 1.0 %shard_map.171 = (f32[320,128]{1,0:T(8,128)S(1)}, f32[64,128]{1,0:T(8,128)S(1)}, f32[64,128]{1,0:T(8,128)S(1)}, f32[32,128]{1,0:T(8,128)S(1)}) custom-call(s32[1]{0:T(128)} %bitcast.where_ref.refs_0_, f32[320,128]{1,0:T(8,128)S(1)} %get-tuple-element.57.cur_ref.refs_1_.refs_2_, f32[320,128]{1,0:T(8,128)S(1)} %get-tuple-element.44.cur_ref.refs_1_.refs_2_, ...), custom_call_target="tpu_custom_call" | custom-call | tf_op jit(solution)/shard_map/pallas_call | solution.py:634
  15.9 1.5 %collective-permute-start.7 = (f32[64,128]{1,0:T(8,128)S(1)}, f32[64,128]{1,0:T(8,128)S(1)}, u32[]{:S(2)}, u32[]{:S(2)}) collective-permute-start(f32[64,128]{1,0:T(8,128)S(1)} %get-tuple-element.67), channel_id=1, source_target_pairs={{0,1},{1,0},{2,4},{3,5},{4,2},{5,3},{6,8},{7,9},{8,6},{9,7},{10,12... | collective-permute-start | bytes 98312 | tf_op jit(solution)/shard_map/ppermute | solution.py:657
  17.4 0.6 %collective-permute-start.8 = (f32[32,128]{1,0:T(8,128)S(1)}, f32[32,128]{1,0:T(8,128)S(1)}, u32[]{:S(2)}, u32[]{:S(2)}) collective-permute-start(f32[32,128]{1,0:T(8,128)S(1)} %get-tuple-element.68.refs_11_.refs_7_), channel_id=1, source_target_pairs={{1,0},{0,1},{3,2},{2,3},{5,4},{4,5},{7,6},{6,7},{9,8},{8,9},{11,10... | collective-permute-start | bytes 49160 | tf_op jit(solution)/shard_map/ppermute | solution.py:662
  18.5 2.7 %collective-permute-done.8.refs_9_.refs_8_ = f32[32,128]{1,0:T(8,128)S(1)} collective-permute-done((f32[32,128]{1,0:T(8,128)S(1)}, f32[32,128]{1,0:T(8,128)S(1)}, u32[]{:S(2)}, u32[]{:S(2)}) %collective-permute-start.8) | collective-permute-done | bytes 16416 | tf_op jit(solution)/shard_map/ppermute | solution.py:662
  21.1 1.0 %shard_map.173 = (f32[320,128]{1,0:T(8,128)S(1)}, f32[64,128]{1,0:T(8,128)S(1)}, f32[64,128]{1,0:T(8,128)S(1)}, f32[32,128]{1,0:T(8,128)S(1)}) custom-call(s32[1]{0:T(128)} %bitcast.where_ref.refs_0_, f32[320,128]{1,0:T(8,128)S(1)} %get-tuple-element.63.cur_ref.refs_1_.refs_2_, f32[320,128]{1,0:T(8,128)S(1)} %get-tuple-element.57.cur_ref.refs_1_.refs_2_, ...), custom_call_target="tpu_custom_call" | custom-call | tf_op jit(solution)/shard_map/pallas_call | solution.py:634
  22.2 0.7 %collective-permute-start.10 = (f32[64,128]{1,0:T(8,128)S(1)}, f32[64,128]{1,0:T(8,128)S(1)}, u32[]{:S(2)}, u32[]{:S(2)}) collective-permute-start(f32[64,128]{1,0:T(8,128)S(1)} %get-tuple-element.73), channel_id=1, source_target_pairs={{0,1},{1,0},{2,4},{3,5},{4,2},{5,3},{6,8},{7,9},{8,6},{9,7},{10,12... | collective-permute-start | bytes 98312 | tf_op jit(solution)/shard_map/ppermute | solution.py:657
  22.9 1.4 %collective-permute-start.11 = (f32[32,128]{1,0:T(8,128)S(1)}, f32[32,128]{1,0:T(8,128)S(1)}, u32[]{:S(2)}, u32[]{:S(2)}) collective-permute-start(f32[32,128]{1,0:T(8,128)S(1)} %get-tuple-element.74.refs_9_.refs_11_), channel_id=1, source_target_pairs={{1,0},{0,1},{3,2},{2,3},{5,4},{4,5},{7,6},{6,7},{9,8},{8,9},{11,10... | collective-permute-start | bytes 49160 | tf_op jit(solution)/shard_map/ppermute | solution.py:662
  24.8 1.0 %shard_map.175 = (f32[3,17,4,128]{3,2,1,0:T(4,128)}, f32[32,128]{1,0:T(8,128)S(1)}, bf16[128,128]{1,0:T(8,128)(2,1)S(1)}) custom-call(f32[320,128]{1,0:T(8,128)S(1)} %get-tuple-element.69.cur_ref.refs_0_.refs_1_, bf16[512,512]{1,0:T(8,128)(2,1)S(1)} %get-tuple-element.76.refs_1_.refs_16_, f32[16,128]{1,0:T(8,128)S(1)} %get-tuple-element.75.refs_2_, ...), custom_call_target="tpu_custom_call" | custom-call | tf_op jit(solution)/shard_map/pallas_call | solution.py:634
  25.8 0.9 %collective-permute-done.11.refs_8_.refs_9_ = f32[32,128]{1,0:T(8,128)S(1)} collective-permute-done((f32[32,128]{1,0:T(8,128)S(1)}, f32[32,128]{1,0:T(8,128)S(1)}, u32[]{:S(2)}, u32[]{:S(2)}) %collective-permute-start.11) | collective-permute-done | bytes 16416 | tf_op jit(solution)/shard_map/ppermute | solution.py:662
  26.6 0.7 %copy-done = s32[1,4]{1,0:T(1,128)S(1)} copy-done((s32[1,4]{1,0:T(1,128)S(1)}, s32[1,4]{1,0:T(1,128)}, u32[]{:S(2)}) %copy-start) | copy-done | bytes 40
  27.3 0.7 %shard_map.176 = (f32[2,128]{1,0:T(2,128)S(1)}, f32[2,128]{1,0:T(2,128)S(1)}, f32[2,128]{1,0:T(2,128)S(1)}, f32[2,128]{1,0:T(2,128)S(1)}, f32[2,128]{1,0:T(2,128)S(1)}) custom-call(s32[1]{0:T(128)} %bitcast.where_ref.refs_0_, s32[1,4]{1,0:T(1,128)S(1)} %copy-done, f32[16,128]{1,0:T(8,128)S(1)} %get-tuple-element.75.refs_2_, ...), custom_call_target="tpu_custom_call" | custom-call | tf_op jit(solution)/shard_map/pallas_call | solution.py:634
  28.0 1.4 %collective-permute-start.12 = (f32[2,128]{1,0:T(2,128)S(1)}, f32[2,128]{1,0:T(2,128)S(1)}, u32[]{:S(2)}, u32[]{:S(2)}) collective-permute-start(f32[2,128]{1,0:T(2,128)S(1)} %get-tuple-element.81), channel_id=1, source_target_pairs={{0,1},{1,0},{2,4},{3,5},{4,2},{5,3},{6,8},{7,9},{8,6},{9,7},{10,12... | collective-permute-start | bytes 3080 | tf_op jit(solution)/shard_map/ppermute | solution.py:657
  29.4 0.7 %collective-permute-start.13 = (f32[2,128]{1,0:T(2,128)S(1)}, f32[2,128]{1,0:T(2,128)S(1)}, u32[]{:S(2)}, u32[]{:S(2)}) collective-permute-start(f32[2,128]{1,0:T(2,128)S(1)} %get-tuple-element.82), channel_id=1, source_target_pairs={{0,1},{1,0},{2,3},{3,2},{4,8},{5,9},{6,10},{7,11},{8,4},{9,5},{10,... | collective-permute-start | bytes 3080 | tf_op jit(solution)/shard_map/ppermute | solution.py:657
  30.0 2.0 %collective-permute-start.14 = (f32[2,128]{1,0:T(2,128)S(1)}, f32[2,128]{1,0:T(2,128)S(1)}, u32[]{:S(2)}, u32[]{:S(2)}) collective-permute-start(f32[2,128]{1,0:T(2,128)S(1)} %get-tuple-element.83), channel_id=1, source_target_pairs={{0,4},{1,5},{2,6},{3,7},{4,0},{5,1},{6,2},{7,3},{8,12},{9,13},{10,... | collective-permute-start | bytes 3080 | tf_op jit(solution)/shard_map/ppermute | solution.py:657
  32.2 1.6 %shard_map.177 = f32[3,17,4,128]{3,2,1,0:T(4,128)} custom-call(s32[1]{0:T(128)} %bitcast.where_ref.refs_0_, f32[320,128]{1,0:T(8,128)S(1)} %get-tuple-element.69.cur_ref.refs_0_.refs_1_, f32[320,128]{1,0:T(8,128)S(1)} %get-tuple-element.63.cur_ref.refs_1_.refs_2_, f32[320,128]{1,0:T(8,128)S(1)} %get-tuple-element.46.refs_3_, ...), custom_call_target="tpu_custom_call" | custom-call | tf_op jit(solution)/shard_map/pallas_call | solution.py:634
  33.8 0.6 %add_bitcast_fusion = f32[1,2,128]{2,1,0:T(2,128)} fusion(f32[2,128]{1,0:T(2,128)S(1)} %collective-permute-done.15, f32[2,128]{1,0:T(2,128)S(1)} %collective-permute-done.14, f32[2,128]{1,0:T(2,128)S(1)} %collective-permute-done.13, f32[2,128]{1,0:T(2,128)S(1)} %get-tuple-element.79.refs_15_, f32[2,128]{1,0:T(2,128)S(1)} %collective-permute-done.12), kind=kLoop, calls=%fused_computation | loop fusion | flops 1024 | bytes 6144 | tf_op jit(solution)/shard_map/broadcast_in_dim | solution.py:790
  (23 shorter events, 2.9 us)
Async XLA Ops:
  2.4 6.9 %collective-permute-start = (f32[64,128]{1,0:T(8,128)S(1)}, f32[64,128]{1,0:T(8,128)S(1)}, u32[]{:S(2)}, u32[]{:S(2)}) collective-permute-start(f32[64,128]{1,0:T(8,128)S(1)} %get-tuple-element.52), channel_id=1, source_target_pairs={{0,2},{1,3},{2,0},{3,1},{4,6},{5,7},{6,4},{7,5},{8,10},{9,11},{10,... | collective-permute-start | bytes 98312 | tf_op jit(solution)/shard_map/ppermute | solution.py:657
  3.0 6.4 %collective-permute-start.1 = (f32[64,128]{1,0:T(8,128)S(1)}, f32[64,128]{1,0:T(8,128)S(1)}, u32[]{:S(2)}, u32[]{:S(2)}) collective-permute-start(f32[64,128]{1,0:T(8,128)S(1)} %get-tuple-element.53), channel_id=1, source_target_pairs={{0,1},{1,0},{2,4},{3,5},{4,2},{5,3},{6,8},{7,9},{8,6},{9,7},{10,12... | collective-permute-start | bytes 98312 | tf_op jit(solution)/shard_map/ppermute | solution.py:657
  5.5 3.8 %collective-permute-start.2 = (f32[48,128]{1,0:T(8,128)S(1)}, f32[48,128]{1,0:T(8,128)S(1)}, u32[]{:S(2)}, u32[]{:S(2)}) collective-permute-start(f32[48,128]{1,0:T(8,128)S(1)} %get-tuple-element.54.refs_11_.refs_12_.refs_3_), channel_id=1, source_target_pairs={{1,0},{0,1},{3,2},{2,3},{5,4},{4,5},{7,6},{6,7},{9,8},{8,9},{11,10... | collective-permute-start | bytes 73736 | tf_op jit(solution)/shard_map/ppermute | solution.py:662
  10.4 4.4 %collective-permute-start.3 = (f32[64,128]{1,0:T(8,128)S(1)}, f32[64,128]{1,0:T(8,128)S(1)}, u32[]{:S(2)}, u32[]{:S(2)}) collective-permute-start(f32[64,128]{1,0:T(8,128)S(1)} %get-tuple-element.60), channel_id=1, source_target_pairs={{0,2},{1,3},{2,0},{3,1},{4,6},{5,7},{6,4},{7,5},{8,10},{9,11},{10,... | collective-permute-start | bytes 98312 | tf_op jit(solution)/shard_map/ppermute | solution.py:657
  10.4 4.4 %collective-permute-start.4 = (f32[64,128]{1,0:T(8,128)S(1)}, f32[64,128]{1,0:T(8,128)S(1)}, u32[]{:S(2)}, u32[]{:S(2)}) collective-permute-start(f32[64,128]{1,0:T(8,128)S(1)} %get-tuple-element.61), channel_id=1, source_target_pairs={{0,1},{1,0},{2,4},{3,5},{4,2},{5,3},{6,8},{7,9},{8,6},{9,7},{10,12... | collective-permute-start | bytes 98312 | tf_op jit(solution)/shard_map/ppermute | solution.py:657
  11.0 3.8 %collective-permute-start.5 = (f32[32,128]{1,0:T(8,128)S(1)}, f32[32,128]{1,0:T(8,128)S(1)}, u32[]{:S(2)}, u32[]{:S(2)}) collective-permute-start(f32[32,128]{1,0:T(8,128)S(1)} %get-tuple-element.62.refs_11_.refs_5_), channel_id=1, source_target_pairs={{1,0},{0,1},{3,2},{2,3},{5,4},{4,5},{7,6},{6,7},{9,8},{8,9},{11,10... | collective-permute-start | bytes 49160 | tf_op jit(solution)/shard_map/ppermute | solution.py:662
  15.8 5.3 %collective-permute-start.6 = (f32[64,128]{1,0:T(8,128)S(1)}, f32[64,128]{1,0:T(8,128)S(1)}, u32[]{:S(2)}, u32[]{:S(2)}) collective-permute-start(f32[64,128]{1,0:T(8,128)S(1)} %get-tuple-element.66), channel_id=1, source_target_pairs={{0,2},{1,3},{2,0},{3,1},{4,6},{5,7},{6,4},{7,5},{8,10},{9,11},{10,... | collective-permute-start | bytes 98312 | tf_op jit(solution)/shard_map/ppermute | solution.py:657
  15.9 5.3 %collective-permute-start.7 = (f32[64,128]{1,0:T(8,128)S(1)}, f32[64,128]{1,0:T(8,128)S(1)}, u32[]{:S(2)}, u32[]{:S(2)}) collective-permute-start(f32[64,128]{1,0:T(8,128)S(1)} %get-tuple-element.67), channel_id=1, source_target_pairs={{0,1},{1,0},{2,4},{3,5},{4,2},{5,3},{6,8},{7,9},{8,6},{9,7},{10,12... | collective-permute-start | bytes 98312 | tf_op jit(solution)/shard_map/ppermute | solution.py:657
  17.4 3.7 %collective-permute-start.8 = (f32[32,128]{1,0:T(8,128)S(1)}, f32[32,128]{1,0:T(8,128)S(1)}, u32[]{:S(2)}, u32[]{:S(2)}) collective-permute-start(f32[32,128]{1,0:T(8,128)S(1)} %get-tuple-element.68.refs_11_.refs_7_), channel_id=1, source_target_pairs={{1,0},{0,1},{3,2},{2,3},{5,4},{4,5},{7,6},{6,7},{9,8},{8,9},{11,10... | collective-permute-start | bytes 49160 | tf_op jit(solution)/shard_map/ppermute | solution.py:662
  22.2 4.5 %collective-permute-start.9 = (f32[64,128]{1,0:T(8,128)S(1)}, f32[64,128]{1,0:T(8,128)S(1)}, u32[]{:S(2)}, u32[]{:S(2)}) collective-permute-start(f32[64,128]{1,0:T(8,128)S(1)} %get-tuple-element.72), channel_id=1, source_target_pairs={{0,2},{1,3},{2,0},{3,1},{4,6},{5,7},{6,4},{7,5},{8,10},{9,11},{10,... | collective-permute-start | bytes 98312 | tf_op jit(solution)/shard_map/ppermute | solution.py:657
  22.2 4.5 %collective-permute-start.10 = (f32[64,128]{1,0:T(8,128)S(1)}, f32[64,128]{1,0:T(8,128)S(1)}, u32[]{:S(2)}, u32[]{:S(2)}) collective-permute-start(f32[64,128]{1,0:T(8,128)S(1)} %get-tuple-element.73), channel_id=1, source_target_pairs={{0,1},{1,0},{2,4},{3,5},{4,2},{5,3},{6,8},{7,9},{8,6},{9,7},{10,12... | collective-permute-start | bytes 98312 | tf_op jit(solution)/shard_map/ppermute | solution.py:657
  22.9 3.7 %collective-permute-start.11 = (f32[32,128]{1,0:T(8,128)S(1)}, f32[32,128]{1,0:T(8,128)S(1)}, u32[]{:S(2)}, u32[]{:S(2)}) collective-permute-start(f32[32,128]{1,0:T(8,128)S(1)} %get-tuple-element.74.refs_9_.refs_11_), channel_id=1, source_target_pairs={{1,0},{0,1},{3,2},{2,3},{5,4},{4,5},{7,6},{6,7},{9,8},{8,9},{11,10... | collective-permute-start | bytes 49160 | tf_op jit(solution)/shard_map/ppermute | solution.py:662
  26.6 0.7 %copy-start = (s32[1,4]{1,0:T(1,128)S(1)}, s32[1,4]{1,0:T(1,128)}, u32[]{:S(2)}) copy-start(s32[1,4]{1,0:T(1,128)} %refs_1_.1) | copy-start | bytes 52
  28.0 5.8 %collective-permute-start.12 = (f32[2,128]{1,0:T(2,128)S(1)}, f32[2,128]{1,0:T(2,128)S(1)}, u32[]{:S(2)}, u32[]{:S(2)}) collective-permute-start(f32[2,128]{1,0:T(2,128)S(1)} %get-tuple-element.81), channel_id=1, source_target_pairs={{0,1},{1,0},{2,4},{3,5},{4,2},{5,3},{6,8},{7,9},{8,6},{9,7},{10,12... | collective-permute-start | bytes 3080 | tf_op jit(solution)/shard_map/ppermute | solution.py:657
  29.4 4.4 %collective-permute-start.13 = (f32[2,128]{1,0:T(2,128)S(1)}, f32[2,128]{1,0:T(2,128)S(1)}, u32[]{:S(2)}, u32[]{:S(2)}) collective-permute-start(f32[2,128]{1,0:T(2,128)S(1)} %get-tuple-element.82), channel_id=1, source_target_pairs={{0,1},{1,0},{2,3},{3,2},{4,8},{5,9},{6,10},{7,11},{8,4},{9,5},{10,... | collective-permute-start | bytes 3080 | tf_op jit(solution)/shard_map/ppermute | solution.py:657
  30.0 3.8 %collective-permute-start.14 = (f32[2,128]{1,0:T(2,128)S(1)}, f32[2,128]{1,0:T(2,128)S(1)}, u32[]{:S(2)}, u32[]{:S(2)}) collective-permute-start(f32[2,128]{1,0:T(2,128)S(1)} %get-tuple-element.83), channel_id=1, source_target_pairs={{0,4},{1,5},{2,6},{3,7},{4,0},{5,1},{6,2},{7,3},{8,12},{9,13},{10,... | collective-permute-start | bytes 3080 | tf_op jit(solution)/shard_map/ppermute | solution.py:657
  32.0 1.7 %collective-permute-start.15 = (f32[2,128]{1,0:T(2,128)S(1)}, f32[2,128]{1,0:T(2,128)S(1)}, u32[]{:S(2)}, u32[]{:S(2)}) collective-permute-start(f32[2,128]{1,0:T(2,128)S(1)} %get-tuple-element.84), channel_id=1, source_target_pairs={{0,2},{1,3},{2,0},{3,1},{4,6},{5,7},{6,4},{7,5},{8,10},{9,11},{10,... | collective-permute-start | bytes 3080 | tf_op jit(solution)/shard_map/ppermute | solution.py:657

commit v2 on v1

--- a/solution.py
+++ b/solution.py
@@ -12,6 +12,7 @@
 
 PATCH_DEV = 2
 REACH = 2
+PATCH_ROWS = 16
 
 time_step = 0.01
 lock_stiffness = 0.5
@@ -332,7 +333,6 @@
 
 
 def first_kernel(
-    where_ref,
     now_hbm,
     flags_hbm,
     weak_hbm,
@@ -366,7 +366,7 @@
     )
     y_elems, z_elems = lame_ref.shape
     lanes = y_elems * z_elems
-    parity = where_ref[0] % 2
+    parity = lax.axis_index("dom") % 2
     gather = gather_table(lanes, z_elems)
     fault = fault_table(lanes, z_elems)
     copies[1].wait()
@@ -401,7 +401,6 @@
 
 
 def setup_kernel(
-    where_ref,
     next_hbm,
     density_hbm,
     flags_hbm,
@@ -450,7 +449,7 @@
     fol_ref[...] = to_elements(lambda c, y: next_ref[c, y], scratch, gather, y_elems)
     density = to_elements(lambda c, y: density_ref[y], scratch, gather, y_elems)
     table = mass_ref[...]
-    first = where_ref[0] == 0
+    first = lax.axis_index("dom") == 0
     plane = lax.broadcasted_iota(jnp.int32, table.shape, 0) < PLANE
     table = jnp.where(jnp.logical_and(first, plane), 2.0 * table, table)
     minv_ref[...] = jnp.where(table > 0.0, table / jnp.where(table > 0.0, density, 1.0), 0.0)
@@ -544,14 +543,13 @@
 
 def step_kernel(*refs, step, last, last_place, pair, y_elems, z_elems):
     refs = list(refs)
-    where_ref, cur_ref, fol_ref, minv_ref, base_ref, touch_ref, material_ref = refs[:7]
-    even_ref, odd_ref = refs[7:9]
-    refs = refs[9:]
+    cur_ref, fol_ref, minv_ref, base_ref, touch_ref, material_ref, even_ref, odd_ref = refs[:8]
+    refs = refs[8:]
     up_ref = refs.pop(0)
     down_ref = None if pair else refs.pop(0)
     first_up_ref, own_ref, first_own_ref, far_ref, edge_ref = refs[:5]
     refs = refs[5:]
-    place = where_ref[0]
+    place = lax.axis_index("dom")
     cur = cur_ref[...]
     tangents = (first_up_ref[32:], first_own_ref[32:])
     new = advance(
@@ -571,9 +569,9 @@
 
 
 def output_kernel(*refs, pair, steps, y_elems, z_elems):
-    field_ref, back_ref, weight_ref = refs[:3]
-    out_ref, grad_ref, table_ref, scratch = refs[-4:]
-    messages = refs[3:-4]
+    owner_ref, field_ref, back_ref, weight_ref = refs[:4]
+    out_ref, grad_ref, mask_ref, table_ref, scratch = refs[-5:]
+    messages = refs[4:-5]
     count = 2 if pair else 3
     grads = [jnp.zeros((8, weight_ref.shape[1]), jnp.float32) for _ in range(4)]
     for i in range(steps):
@@ -584,24 +582,27 @@
         for x in range(4):
             grads[x] = grads[x] + slip[8 * x : 8 * x + 8] * weight_ref[4 * i + x : 4 * i + x + 1]
     grad_ref[...] = jnp.concatenate(grads, axis=0)
+    shape = (PATCH_ROWS, weight_ref.shape[1])
+    first = (lax.axis_index("dom") - REACH) * PATCH_DEV
+    number = lax.broadcasted_iota(jnp.int32, shape, 0) + first
+    for x in range(4):
+        mask = jnp.where(number == owner_ref[0, x], 1.0, 0.0)
+        mask_ref[PATCH_ROWS * x : PATCH_ROWS * (x + 1)] = mask
     table_ref[...] = fault_table_back(weight_ref.shape[1], z_elems)
     from_elements(field_ref[...], scratch, back_ref, out_ref, y_elems)
 
 
 def patch_kernel(*refs, pair, steps):
-    where_ref, owner_ref, weight_ref, grad_ref, table_ref, _, _, _, up_ref = refs[:9]
-    down_ref = None if pair else refs[9]
+    mask_ref, weight_ref, grad_ref, table_ref, _, _, _, up_ref = refs[:8]
+    down_ref = None if pair else refs[8]
     home_out, out_a, out_b, out_c, out_d = refs[-5:]
-    place = where_ref[0]
-    lanes = weight_ref.shape[1]
+    place = lax.axis_index("dom")
     slip = fault_input(up_ref, down_ref, 32)
-    wide = 16
-    number = lax.broadcasted_iota(jnp.int32, (wide, lanes), 0) + (place - REACH) * PATCH_DEV
-    total = jnp.zeros((wide, lanes), jnp.float32)
+    total = 0.0
     for x in range(4):
         at, k = 8 * x + 4, 4 * (steps - 1) + x
         grad = grad_ref[at : at + 1] + slip[at : at + 1] * weight_ref[k : k + 1]
-        total = total + jnp.where(number == owner_ref[0, x], grad, 0.0)
+        total = total + mask_ref[PATCH_ROWS * x : PATCH_ROWS * (x + 1)] * grad
     total = exact_dot(total, table_ref[...])
     rows = [total[2 * i : 2 * i + 2] for i in range(5)]
     home_out[...] = rows[2]
@@ -619,7 +620,7 @@
 ANY = pl.BlockSpec(memory_space=pl.ANY)
 
 
-def kernel_call(body, outs, args, in_smem, scratch=(), in_hbm=(), kept=(), unread=(), **static):
+def kernel_call(body, outs, args, in_smem=(), scratch=(), in_hbm=(), kept=(), unread=(), **static):
     shapes = []
     for out in outs:
         shape, dtype = out if isinstance(out[0], tuple) else (out, jnp.float32)
@@ -678,7 +679,6 @@
     assert x_elems == 1 and lanes == adjoint_now.shape[3]
     steps = branch_flags.shape[0]
     pair = lax.axis_size("depth") == 2
-    place = lax.axis_index("dom").astype(jnp.int32).reshape(1)
     own_table, far_table, edge_table, touch_table = (jnp.asarray(t) for t in stiffness_tables())
     back = jnp.asarray(back_table(y_elems, z_elems))
     mass = jnp.asarray(mass_table(y_elems, z_elems))
@@ -705,12 +705,12 @@
             (edge_table.shape, edge_table.dtype),
         ],
         (
-            place, now, flags, weak_slope[0], lame_first[0], shear_modulus[0], edge_table,
+            now, flags, weak_slope[0], lame_first[0], shear_modulus[0], edge_table,
         ),
-        (0,),
+        (),
         [native],
-        range(1, 7),
-        (6,),
+        range(6),
+        (5,),
     )
     first_fault = fault_rows
     even_in, odd_in, fault_in = exchange(even, odd, fault_rows)
@@ -719,11 +719,11 @@
     fol, minv, weight, own_table, far_table, touch_table, back = kernel_call(
         setup_kernel,
         [field, field, (4 * steps, lanes)] + [(t.shape, t.dtype) for t in tables],
-        (place, following, rho, flags, normal_stress[0], mass) + tables,
-        (0,),
+        (following, rho, flags, normal_stress[0], mass) + tables,
+        (),
         [native],
-        range(1, 10),
-        range(6, 10),
+        range(9),
+        range(5, 9),
         y_elems=y_elems,
         z_elems=z_elems,
     )
@@ -737,7 +737,7 @@
             [cur, material, own_table, touch_table],
             (),
         )
-        args = [place, cur, fol, minv, base, touch, material, even_in, odd_in] + fault_in
+        args = [cur, fol, minv, base, touch, material, even_in, odd_in] + fault_in
         args += [first_in[0], fault_rows, first_fault, far_table, edge_table]
         static = dict(
             step=step, last=last, last_place=lax.axis_size("dom") - 1, pair=pair, y_elems=y_elems,
@@ -745,18 +745,18 @@
         )
         if not last:
             new, even, odd, new_fault = kernel_call(
-                step_kernel, [field, plane, plane, (32, lanes)], args, (0,), **static
+                step_kernel, [field, plane, plane, (32, lanes)], args, **static
             )
             fol, cur, fault_rows = cur, new, new_fault
             even_in, odd_in, fault_in = exchange(even, odd, fault_rows)
         else:
             whole = (3, 4 * y_elems + 1, 4, lanes)
             known = seen[: len(seen) - len(fault_in)]
-            later, grad, table = kernel_call(
+            later, grad, mask, table = kernel_call(
                 output_kernel,
-                [whole, (32, lanes), ((lanes, lanes), jnp.bfloat16)],
-                [cur, back, weight] + known,
-                (),
+                [whole, (32, lanes), (4 * PATCH_ROWS, lanes), ((lanes, lanes), jnp.bfloat16)],
+                [patch_owner, cur, back, weight] + known,
+                (0,),
                 [native],
                 pair=pair,
                 steps=steps,
@@ -766,9 +766,8 @@
             sums = kernel_call(
                 patch_kernel,
                 [(PATCH_DEV, lanes)] * 5,
-                [place, patch_owner, weight, grad, table, even_in, odd_in, touch] + fault_in,
-                (0, 1),
-                unread=(5, 6, 7),
+                [mask, weight, grad, table, even_in, odd_in, touch] + fault_in,
+                unread=(4, 5, 6),
                 pair=pair,
                 steps=steps,
             )
@@ -779,8 +778,7 @@
                 step_kernel,
                 [whole],
                 args + [sums[0], back],
-                (0,),
-                [native],
+                scratch=[native],
                 unread=(len(args),),
                 **static,
             )[0]

time: 34.5 us -> 33.8 us (0.980)
  waiting for transfers between devices: 6.83 us -> 5.95 us
    ppermute x4, waiting for transfers between devices: 6.79 us -> 5.92 us  [from_behind(): lax.ppermute(block, axis, [((i - distance) % size, i) for i in range(size)])]
  transfers between devices with their start and end apart: 16 -> 16, of which waited for: 4 -> 3; matrix products, arithmetic and copies ran while one was open for 0% -> 0% of each run, Pallas kernels for 18% -> 20%
where the time goes in v2:
time: 33.8 us; the launch traced here: 33.6 us
  starting transfers between devices  13.8 us (41%)
  Pallas kernels  11.9 us (35%)
  waiting for transfers between devices  5.95 us (18%)
  between operations  0.72 us (2%)
  local copies, waits for them, and re-layouts  0.65 us (2%)
  other arithmetic  0.57 us (2%)
    pallas_call x12, Pallas kernels, kernel_call(): pl.pallas_call(functools.partial(body, **static) if static else body, out...  11.9 us
    ppermute x12, starting transfers between devices, swapped(): return lax.ppermute(block, ('dom', 'depth'), route)  10.2 us
    ppermute x4, waiting for transfers between devices, from_behind(): lax.ppermute(block, axis, [((i - distance) % size, i) for i in range(size)])  5.92 us
    ppermute x4, starting transfers between devices, from_behind(): lax.ppermute(block, axis, [((i - distance) % size, i) for i in range(size)])  3.58 us
  transfers between devices with their start and end apart: 16, of which 3 were waited for; matrix products, arithmetic and copies ran while one was open for 0% of the time, Pallas kernels for 20%

profile of v2, /device:TPU:0, one launch (start us, length us, event | category | flops | bytes accessed | tf_op | source)
XLA Modules:
  0.0 33.6 jit_solution(7353188188093446381)
XLA Ops:
  0.6 1.8 %shard_map.166 = (f32[320,128]{1,0:T(8,128)S(1)}, f32[64,128]{1,0:T(8,128)S(1)}, f32[64,128]{1,0:T(8,128)S(1)}, f32[48,128]{1,0:T(8,128)S(1)}, f32[8,128]{1,0:T(8,128)S(1)}, /*index=5*/bf16[2,160,384]{2,1,0:T(8,128)(2,1)S(1)}) custom-call(f32[3,17,4,128]{3,2,1,0:T(4,128)} %bitcast.13, s32[4,4,128]{2,1,0:T(4,128)} %bitcast.16, f32[4,128]{1,0:T(4,128)} %bitcast.18, ...), custom_call_target="tpu_custom_call" | custom-call | tf_op jit(solution)/shard_map/pallas_call | solution.py:635
  2.4 0.5 %collective-permute-start = (f32[64,128]{1,0:T(8,128)S(1)}, f32[64,128]{1,0:T(8,128)S(1)}, u32[]{:S(2)}, u32[]{:S(2)}) collective-permute-start(f32[64,128]{1,0:T(8,128)S(1)} %get-tuple-element.53), channel_id=1, source_target_pairs={{0,2},{1,3},{2,0},{3,1},{4,6},{5,7},{6,4},{7,5},{8,10},{9,11},{10,... | collective-permute-start | bytes 98312 | tf_op jit(solution)/shard_map/ppermute | solution.py:658
  3.0 2.6 %collective-permute-start.1 = (f32[64,128]{1,0:T(8,128)S(1)}, f32[64,128]{1,0:T(8,128)S(1)}, u32[]{:S(2)}, u32[]{:S(2)}) collective-permute-start(f32[64,128]{1,0:T(8,128)S(1)} %get-tuple-element.54), channel_id=1, source_target_pairs={{0,1},{1,0},{2,4},{3,5},{4,2},{5,3},{6,8},{7,9},{8,6},{9,7},{10,12... | collective-permute-start | bytes 98312 | tf_op jit(solution)/shard_map/ppermute | solution.py:658
  5.6 1.7 %shard_map.167 = (f32[320,128]{1,0:T(8,128)S(1)}, f32[320,128]{1,0:T(8,128)S(1)}, f32[16,128]{1,0:T(8,128)S(1)}, bf16[2,640,384]{2,1,0:T(8,128)(2,1)S(1)}, bf16[...) custom-call(f32[3,17,4,128]{3,2,1,0:T(4,128)} %bitcast.12, ...), custom_call_target="tpu_custom_call" | custom-call | tf_op jit(solution)/shard_map/pallas_call | solution.py:635
  7.3 0.5 %shard_map.168 = (f32[320,128]{1,0:T(8,128)S(1)}, f32[160,128]{1,0:T(8,128)S(1)}) custom-call(f32[320,128]{1,0:T(8,128)S(1)} %get-tuple-element.45.cur_ref.refs_0_.refs_1_, f32[8,128]{1,0:T(8,128)S(1)} %get-tuple-element.48.material_ref.refs_5_, bf16[2,640,384]{2,1,0:T(8,128)(2,1)S(1)} %get-tuple-element.49.own_ref, ...), custom_call_target="tpu_custom_call" | custom-call | tf_op jit(solution)/shard_map/pallas_call | solution.py:635
  7.9 1.5 %collective-permute-done.2.refs_8_.refs_9_.refs_5_ = f32[48,128]{1,0:T(8,128)S(1)} collective-permute-done((f32[48,128]{1,0:T(8,128)S(1)}, f32[48,128]{1,0:T(8,128)S(1)}, u32[]{:S(2)}, u32[]{:S(2)}) %collective-permute-start.2) | collective-permute-done | bytes 24608 | tf_op jit(solution)/shard_map/ppermute | solution.py:663
  9.4 1.0 %shard_map.169 = (f32[320,128]{1,0:T(8,128)S(1)}, f32[64,128]{1,0:T(8,128)S(1)}, f32[64,128]{1,0:T(8,128)S(1)}, f32[32,128]{1,0:T(8,128)S(1)}) custom-call(f32[320,128]{1,0:T(8,128)S(1)} %get-tuple-element.45.cur_ref.refs_0_.refs_1_, f32[320,128]{1,0:T(8,128)S(1)} %get-tuple-element.46.refs_1_, f32[320,128]{1,0:T(8,128)S(1)} %get-tuple-element.47.refs_2_, ...), custom_call_target="tpu_custom_call" | custom-call | tf_op jit(solution)/shard_map/pallas_call | solution.py:635
  10.4 0.6 %collective-permute-start.4 = (f32[64,128]{1,0:T(8,128)S(1)}, f32[64,128]{1,0:T(8,128)S(1)}, u32[]{:S(2)}, u32[]{:S(2)}) collective-permute-start(f32[64,128]{1,0:T(8,128)S(1)} %get-tuple-element.62), channel_id=1, source_target_pairs={{0,1},{1,0},{2,4},{3,5},{4,2},{5,3},{6,8},{7,9},{8,6},{9,7},{10,12... | collective-permute-start | bytes 98312 | tf_op jit(solution)/shard_map/ppermute | solution.py:658
  11.0 1.6 %collective-permute-start.5 = (f32[32,128]{1,0:T(8,128)S(1)}, f32[32,128]{1,0:T(8,128)S(1)}, u32[]{:S(2)}, u32[]{:S(2)}) collective-permute-start(f32[32,128]{1,0:T(8,128)S(1)} %get-tuple-element.63.refs_10_.refs_6_), channel_id=1, source_target_pairs={{1,0},{0,1},{3,2},{2,3},{5,4},{4,5},{7,6},{6,7},{9,8},{8,9},{11,10... | collective-permute-start | bytes 49160 | tf_op jit(solution)/shard_map/ppermute | solution.py:663
  13.0 1.8 %collective-permute-done.5.refs_8_.refs_7_ = f32[32,128]{1,0:T(8,128)S(1)} collective-permute-done((f32[32,128]{1,0:T(8,128)S(1)}, f32[32,128]{1,0:T(8,128)S(1)}, u32[]{:S(2)}, u32[]{:S(2)}) %collective-permute-start.5) | collective-permute-done | bytes 16416 | tf_op jit(solution)/shard_map/ppermute | solution.py:663
  14.8 1.0 %shard_map.171 = (f32[320,128]{1,0:T(8,128)S(1)}, f32[64,128]{1,0:T(8,128)S(1)}, f32[64,128]{1,0:T(8,128)S(1)}, f32[32,128]{1,0:T(8,128)S(1)}) custom-call(f32[320,128]{1,0:T(8,128)S(1)} %get-tuple-element.58.cur_ref.refs_0_.refs_1_, f32[320,128]{1,0:T(8,128)S(1)} %get-tuple-element.45.cur_ref.refs_0_.refs_1_, f32[320,128]{1,0:T(8,128)S(1)} %get-tuple-element.47.refs_2_, ...), custom_call_target="tpu_custom_call" | custom-call | tf_op jit(solution)/shard_map/pallas_call | solution.py:635
  15.9 1.5 %collective-permute-start.7 = (f32[64,128]{1,0:T(8,128)S(1)}, f32[64,128]{1,0:T(8,128)S(1)}, u32[]{:S(2)}, u32[]{:S(2)}) collective-permute-start(f32[64,128]{1,0:T(8,128)S(1)} %get-tuple-element.68), channel_id=1, source_target_pairs={{0,1},{1,0},{2,4},{3,5},{4,2},{5,3},{6,8},{7,9},{8,6},{9,7},{10,12... | collective-permute-start | bytes 98312 | tf_op jit(solution)/shard_map/ppermute | solution.py:658
  17.4 0.6 %collective-permute-start.8 = (f32[32,128]{1,0:T(8,128)S(1)}, f32[32,128]{1,0:T(8,128)S(1)}, u32[]{:S(2)}, u32[]{:S(2)}) collective-permute-start(f32[32,128]{1,0:T(8,128)S(1)} %get-tuple-element.69.refs_10_.refs_8_), channel_id=1, source_target_pairs={{1,0},{0,1},{3,2},{2,3},{5,4},{4,5},{7,6},{6,7},{9,8},{8,9},{11,10... | collective-permute-start | bytes 49160 | tf_op jit(solution)/shard_map/ppermute | solution.py:663
  18.5 2.7 %collective-permute-done.8.refs_8_.refs_9_ = f32[32,128]{1,0:T(8,128)S(1)} collective-permute-done((f32[32,128]{1,0:T(8,128)S(1)}, f32[32,128]{1,0:T(8,128)S(1)}, u32[]{:S(2)}, u32[]{:S(2)}) %collective-permute-start.8) | collective-permute-done | bytes 16416 | tf_op jit(solution)/shard_map/ppermute | solution.py:663
  21.1 1.0 %shard_map.173 = (f32[320,128]{1,0:T(8,128)S(1)}, f32[64,128]{1,0:T(8,128)S(1)}, f32[64,128]{1,0:T(8,128)S(1)}, f32[32,128]{1,0:T(8,128)S(1)}) custom-call(f32[320,128]{1,0:T(8,128)S(1)} %get-tuple-element.64.cur_ref.refs_0_.refs_1_, f32[320,128]{1,0:T(8,128)S(1)} %get-tuple-element.58.cur_ref.refs_0_.refs_1_, f32[320,128]{1,0:T(8,128)S(1)} %get-tuple-element.47.refs_2_, ...), custom_call_target="tpu_custom_call" | custom-call | tf_op jit(solution)/shard_map/pallas_call | solution.py:635
  22.2 0.7 %collective-permute-start.10 = (f32[64,128]{1,0:T(8,128)S(1)}, f32[64,128]{1,0:T(8,128)S(1)}, u32[]{:S(2)}, u32[]{:S(2)}) collective-permute-start(f32[64,128]{1,0:T(8,128)S(1)} %get-tuple-element.74), channel_id=1, source_target_pairs={{0,1},{1,0},{2,4},{3,5},{4,2},{5,3},{6,8},{7,9},{8,6},{9,7},{10,12... | collective-permute-start | bytes 98312 | tf_op jit(solution)/shard_map/ppermute | solution.py:658
  22.9 1.4 %collective-permute-start.11 = (f32[32,128]{1,0:T(8,128)S(1)}, f32[32,128]{1,0:T(8,128)S(1)}, u32[]{:S(2)}, u32[]{:S(2)}) collective-permute-start(f32[32,128]{1,0:T(8,128)S(1)} %get-tuple-element.75.refs_10_), channel_id=1, source_target_pairs={{1,0},{0,1},{3,2},{2,3},{5,4},{4,5},{7,6},{6,7},{9,8},{8,9},{11,10... | collective-permute-start | bytes 49160 | tf_op jit(solution)/shard_map/ppermute | solution.py:663
  24.8 0.6 %copy-done = s32[1,4]{1,0:T(1,128)S(1)} copy-done((s32[1,4]{1,0:T(1,128)S(1)}, s32[1,4]{1,0:T(1,128)}, u32[]{:S(2)}) %copy-start) | copy-done | bytes 40
  25.4 1.5 %shard_map.175 = (f32[3,17,4,128]{3,2,1,0:T(4,128)}, f32[32,128]{1,0:T(8,128)S(1)}, f32[64,128]{1,0:T(8,128)S(1)}, bf16[128,128]{1,0:T(8,128)(2,1)S(1)}) custom-call(s32[1,4]{1,0:T(1,128)S(1)} %copy-done, f32[320,128]{1,0:T(8,128)S(1)} %get-tuple-element.70.cur_ref.refs_1_.refs_0_, bf16[512,512]{1,0:T(8,128)(2,1)S(1)} %get-tuple-element.76.refs_2_.refs_15_, ...), custom_call_target="tpu_custom_call" | custom-call | tf_op jit(solution)/shard_map/pallas_call | solution.py:635
  27.1 1.1 %collective-permute-start.12 = (f32[2,128]{1,0:T(2,128)S(1)}, f32[2,128]{1,0:T(2,128)S(1)}, u32[]{:S(2)}, u32[]{:S(2)}) collective-permute-start(f32[2,128]{1,0:T(2,128)S(1)} %get-tuple-element.83), channel_id=1, source_target_pairs={{0,1},{1,0},{2,4},{3,5},{4,2},{5,3},{6,8},{7,9},{8,6},{9,7},{10,12... | collective-permute-start | bytes 3080 | tf_op jit(solution)/shard_map/ppermute | solution.py:658
  28.2 1.0 %collective-permute-start.13 = (f32[2,128]{1,0:T(2,128)S(1)}, f32[2,128]{1,0:T(2,128)S(1)}, u32[]{:S(2)}, u32[]{:S(2)}) collective-permute-start(f32[2,128]{1,0:T(2,128)S(1)} %get-tuple-element.84), channel_id=1, source_target_pairs={{0,1},{1,0},{2,3},{3,2},{4,8},{5,9},{6,10},{7,11},{8,4},{9,5},{10,... | collective-permute-start | bytes 3080 | tf_op jit(solution)/shard_map/ppermute | solution.py:658
  29.1 2.2 %collective-permute-start.14 = (f32[2,128]{1,0:T(2,128)S(1)}, f32[2,128]{1,0:T(2,128)S(1)}, u32[]{:S(2)}, u32[]{:S(2)}) collective-permute-start(f32[2,128]{1,0:T(2,128)S(1)} %get-tuple-element.85), channel_id=1, source_target_pairs={{0,4},{1,5},{2,6},{3,7},{4,0},{5,1},{6,2},{7,3},{8,12},{9,13},{10,... | collective-permute-start | bytes 3080 | tf_op jit(solution)/shard_map/ppermute | solution.py:658
  31.4 1.6 %shard_map.177 = f32[3,17,4,128]{3,2,1,0:T(4,128)} custom-call(f32[320,128]{1,0:T(8,128)S(1)} %get-tuple-element.70.cur_ref.refs_1_.refs_0_, f32[320,128]{1,0:T(8,128)S(1)} %get-tuple-element.64.cur_ref.refs_0_.refs_1_, f32[320,128]{1,0:T(8,128)S(1)} %get-tuple-element.47.refs_2_, f32[320,128]{1,0:T(8,128)S(1)} %get-tuple-element.71.refs_3_, ...), custom_call_target="tpu_custom_call" | custom-call | tf_op jit(solution)/shard_map/pallas_call | solution.py:635
  33.0 0.6 %add_bitcast_fusion = f32[1,2,128]{2,1,0:T(2,128)} fusion(f32[2,128]{1,0:T(2,128)S(1)} %collective-permute-done.15, f32[2,128]{1,0:T(2,128)S(1)} %collective-permute-done.14, f32[2,128]{1,0:T(2,128)S(1)} %collective-permute-done.13, f32[2,128]{1,0:T(2,128)S(1)} %get-tuple-element.81.refs_14_, f32[2,128]{1,0:T(2,128)S(1)} %collective-permute-done.12), kind=kLoop, calls=%fused_computation | loop fusion | flops 1024 | bytes 6144 | tf_op jit(solution)/shard_map/broadcast_in_dim | solution.py:788
  (23 shorter events, 1.9 us)
Async XLA Ops:
  2.4 6.9 %collective-permute-start = (f32[64,128]{1,0:T(8,128)S(1)}, f32[64,128]{1,0:T(8,128)S(1)}, u32[]{:S(2)}, u32[]{:S(2)}) collective-permute-start(f32[64,128]{1,0:T(8,128)S(1)} %get-tuple-element.53), channel_id=1, source_target_pairs={{0,2},{1,3},{2,0},{3,1},{4,6},{5,7},{6,4},{7,5},{8,10},{9,11},{10,... | collective-permute-start | bytes 98312 | tf_op jit(solution)/shard_map/ppermute | solution.py:658
  3.0 6.4 %collective-permute-start.1 = (f32[64,128]{1,0:T(8,128)S(1)}, f32[64,128]{1,0:T(8,128)S(1)}, u32[]{:S(2)}, u32[]{:S(2)}) collective-permute-start(f32[64,128]{1,0:T(8,128)S(1)} %get-tuple-element.54), channel_id=1, source_target_pairs={{0,1},{1,0},{2,4},{3,5},{4,2},{5,3},{6,8},{7,9},{8,6},{9,7},{10,12... | collective-permute-start | bytes 98312 | tf_op jit(solution)/shard_map/ppermute | solution.py:658
  5.5 3.8 %collective-permute-start.2 = (f32[48,128]{1,0:T(8,128)S(1)}, f32[48,128]{1,0:T(8,128)S(1)}, u32[]{:S(2)}, u32[]{:S(2)}) collective-permute-start(f32[48,128]{1,0:T(8,128)S(1)} %get-tuple-element.55.refs_10_.refs_11_.refs_4_), channel_id=1, source_target_pairs={{1,0},{0,1},{3,2},{2,3},{5,4},{4,5},{7,6},{6,7},{9,8},{8,9},{11,10... | collective-permute-start | bytes 73736 | tf_op jit(solution)/shard_map/ppermute | solution.py:663
  10.4 4.4 %collective-permute-start.3 = (f32[64,128]{1,0:T(8,128)S(1)}, f32[64,128]{1,0:T(8,128)S(1)}, u32[]{:S(2)}, u32[]{:S(2)}) collective-permute-start(f32[64,128]{1,0:T(8,128)S(1)} %get-tuple-element.61), channel_id=1, source_target_pairs={{0,2},{1,3},{2,0},{3,1},{4,6},{5,7},{6,4},{7,5},{8,10},{9,11},{10,... | collective-permute-start | bytes 98312 | tf_op jit(solution)/shard_map/ppermute | solution.py:658
  10.4 4.4 %collective-permute-start.4 = (f32[64,128]{1,0:T(8,128)S(1)}, f32[64,128]{1,0:T(8,128)S(1)}, u32[]{:S(2)}, u32[]{:S(2)}) collective-permute-start(f32[64,128]{1,0:T(8,128)S(1)} %get-tuple-element.62), channel_id=1, source_target_pairs={{0,1},{1,0},{2,4},{3,5},{4,2},{5,3},{6,8},{7,9},{8,6},{9,7},{10,12... | collective-permute-start | bytes 98312 | tf_op jit(solution)/shard_map/ppermute | solution.py:658
  11.0 3.8 %collective-permute-start.5 = (f32[32,128]{1,0:T(8,128)S(1)}, f32[32,128]{1,0:T(8,128)S(1)}, u32[]{:S(2)}, u32[]{:S(2)}) collective-permute-start(f32[32,128]{1,0:T(8,128)S(1)} %get-tuple-element.63.refs_10_.refs_6_), channel_id=1, source_target_pairs={{1,0},{0,1},{3,2},{2,3},{5,4},{4,5},{7,6},{6,7},{9,8},{8,9},{11,10... | collective-permute-start | bytes 49160 | tf_op jit(solution)/shard_map/ppermute | solution.py:663
  15.8 5.3 %collective-permute-start.6 = (f32[64,128]{1,0:T(8,128)S(1)}, f32[64,128]{1,0:T(8,128)S(1)}, u32[]{:S(2)}, u32[]{:S(2)}) collective-permute-start(f32[64,128]{1,0:T(8,128)S(1)} %get-tuple-element.67), channel_id=1, source_target_pairs={{0,2},{1,3},{2,0},{3,1},{4,6},{5,7},{6,4},{7,5},{8,10},{9,11},{10,... | collective-permute-start | bytes 98312 | tf_op jit(solution)/shard_map/ppermute | solution.py:658
  15.9 5.2 %collective-permute-start.7 = (f32[64,128]{1,0:T(8,128)S(1)}, f32[64,128]{1,0:T(8,128)S(1)}, u32[]{:S(2)}, u32[]{:S(2)}) collective-permute-start(f32[64,128]{1,0:T(8,128)S(1)} %get-tuple-element.68), channel_id=1, source_target_pairs={{0,1},{1,0},{2,4},{3,5},{4,2},{5,3},{6,8},{7,9},{8,6},{9,7},{10,12... | collective-permute-start | bytes 98312 | tf_op jit(solution)/shard_map/ppermute | solution.py:658
  17.4 3.7 %collective-permute-start.8 = (f32[32,128]{1,0:T(8,128)S(1)}, f32[32,128]{1,0:T(8,128)S(1)}, u32[]{:S(2)}, u32[]{:S(2)}) collective-permute-start(f32[32,128]{1,0:T(8,128)S(1)} %get-tuple-element.69.refs_10_.refs_8_), channel_id=1, source_target_pairs={{1,0},{0,1},{3,2},{2,3},{5,4},{4,5},{7,6},{6,7},{9,8},{8,9},{11,10... | collective-permute-start | bytes 49160 | tf_op jit(solution)/shard_map/ppermute | solution.py:663
  22.2 4.8 %collective-permute-start.9 = (f32[64,128]{1,0:T(8,128)S(1)}, f32[64,128]{1,0:T(8,128)S(1)}, u32[]{:S(2)}, u32[]{:S(2)}) collective-permute-start(f32[64,128]{1,0:T(8,128)S(1)} %get-tuple-element.73), channel_id=1, source_target_pairs={{0,2},{1,3},{2,0},{3,1},{4,6},{5,7},{6,4},{7,5},{8,10},{9,11},{10,... | collective-permute-start | bytes 98312 | tf_op jit(solution)/shard_map/ppermute | solution.py:658
  22.2 4.8 %collective-permute-start.10 = (f32[64,128]{1,0:T(8,128)S(1)}, f32[64,128]{1,0:T(8,128)S(1)}, u32[]{:S(2)}, u32[]{:S(2)}) collective-permute-start(f32[64,128]{1,0:T(8,128)S(1)} %get-tuple-element.74), channel_id=1, source_target_pairs={{0,1},{1,0},{2,4},{3,5},{4,2},{5,3},{6,8},{7,9},{8,6},{9,7},{10,12... | collective-permute-start | bytes 98312 | tf_op jit(solution)/shard_map/ppermute | solution.py:658
  22.9 4.1 %collective-permute-start.11 = (f32[32,128]{1,0:T(8,128)S(1)}, f32[32,128]{1,0:T(8,128)S(1)}, u32[]{:S(2)}, u32[]{:S(2)}) collective-permute-start(f32[32,128]{1,0:T(8,128)S(1)} %get-tuple-element.75.refs_10_), channel_id=1, source_target_pairs={{1,0},{0,1},{3,2},{2,3},{5,4},{4,5},{7,6},{6,7},{9,8},{8,9},{11,10... | collective-permute-start | bytes 49160 | tf_op jit(solution)/shard_map/ppermute | solution.py:663
  24.8 0.7 %copy-start = (s32[1,4]{1,0:T(1,128)S(1)}, s32[1,4]{1,0:T(1,128)}, u32[]{:S(2)}) copy-start(s32[1,4]{1,0:T(1,128)} %refs_0_.1) | copy-start | bytes 52
  27.1 5.9 %collective-permute-start.12 = (f32[2,128]{1,0:T(2,128)S(1)}, f32[2,128]{1,0:T(2,128)S(1)}, u32[]{:S(2)}, u32[]{:S(2)}) collective-permute-start(f32[2,128]{1,0:T(2,128)S(1)} %get-tuple-element.83), channel_id=1, source_target_pairs={{0,1},{1,0},{2,4},{3,5},{4,2},{5,3},{6,8},{7,9},{8,6},{9,7},{10,12... | collective-permute-start | bytes 3080 | tf_op jit(solution)/shard_map/ppermute | solution.py:658
  28.2 4.8 %collective-permute-start.13 = (f32[2,128]{1,0:T(2,128)S(1)}, f32[2,128]{1,0:T(2,128)S(1)}, u32[]{:S(2)}, u32[]{:S(2)}) collective-permute-start(f32[2,128]{1,0:T(2,128)S(1)} %get-tuple-element.84), channel_id=1, source_target_pairs={{0,1},{1,0},{2,3},{3,2},{4,8},{5,9},{6,10},{7,11},{8,4},{9,5},{10,... | collective-permute-start | bytes 3080 | tf_op jit(solution)/shard_map/ppermute | solution.py:658
  29.1 3.8 %collective-permute-start.14 = (f32[2,128]{1,0:T(2,128)S(1)}, f32[2,128]{1,0:T(2,128)S(1)}, u32[]{:S(2)}, u32[]{:S(2)}) collective-permute-start(f32[2,128]{1,0:T(2,128)S(1)} %get-tuple-element.85), channel_id=1, source_target_pairs={{0,4},{1,5},{2,6},{3,7},{4,0},{5,1},{6,2},{7,3},{8,12},{9,13},{10,... | collective-permute-start | bytes 3080 | tf_op jit(solution)/shard_map/ppermute | solution.py:658
  31.4 1.6 %collective-permute-start.15 = (f32[2,128]{1,0:T(2,128)S(1)}, f32[2,128]{1,0:T(2,128)S(1)}, u32[]{:S(2)}, u32[]{:S(2)}) collective-permute-start(f32[2,128]{1,0:T(2,128)S(1)} %get-tuple-element.86), channel_id=1, source_target_pairs={{0,2},{1,3},{2,0},{3,1},{4,6},{5,7},{6,4},{7,5},{8,10},{9,11},{10,... | collective-permute-start | bytes 3080 | tf_op jit(solution)/shard_map/ppermute | solution.py:658

commit v3 on v2

--- a/solution.py
+++ b/solution.py
@@ -18,6 +18,7 @@
 lock_stiffness = 0.5
 
 BLOCK = 16
+ROWS = ((0, 1, 2), (3, 4, 5), (11, 12, 13), (6, 7, 14), (8, 9, 10))
 PLANE = 5 * BLOCK
 
 
@@ -72,7 +73,7 @@
             first[:, c, :, d] += grads[c].T @ (quad[:, None] * grads[d])
             second[:, c, :, d] += grads[d].T @ (quad[:, None] * grads[c])
     where = [
-        node // 5 * BLOCK + node % 5 * 3 + c for node in range(125) for c in range(3)
+        node // 5 * BLOCK + ROWS[node % 5][c] for node in range(125) for c in range(3)
     ]
     wide = []
     for small in (first, second):
@@ -93,18 +94,18 @@
 def stiffness_tables():
     wide = element_stiffness()
     own = 4 * PLANE
-    inner = np.concatenate([w[:own] for w in wide])
-    outer = np.concatenate([w[own:] for w in wide])
-
-    def three(table):
-        high, low = two_parts(table)
+    planes = [slice(x * PLANE, (x + 1) * PLANE) for x in range(5)]
+    inner = np.concatenate([w[:own, :own] for w in wide])
+
+    def three(rows, columns):
+        high, low = two_parts(np.concatenate([w[rows, columns] for w in wide]))
         return padded_table(np.concatenate([high, low, high], axis=1), 256)
 
     return (
-        two_parts(padded_table(inner[:, :own], OWN_COLS)),
-        three(inner[:, own:]),
-        two_parts(padded_table(outer[:, :own], OWN_COLS)),
-        three(outer[:, own:]),
+        two_parts(padded_table(inner, OWN_COLS)),
+        np.stack([three(planes[x], planes[4]) for x in range(4)]),
+        np.stack([three(planes[4], planes[x]) for x in range(4)]),
+        three(planes[4], planes[4]),
     )
 
 
@@ -140,7 +141,7 @@
                     value = time_step * time_step * 8.0 / (mx * my * mz)
                     if zl == 4:
                         value[-1] = 0.0
-                    table[x, zl, 3 * yl : 3 * yl + 3, yel] = value
+                    table[x, zl, list(ROWS[yl]), yel] = value
     return table.reshape(4 * PLANE, y_elems * z_elems).astype(np.float32)
 
 
@@ -191,10 +192,10 @@
     return ones_where(lambda c, z: z == 4 * (c % z_elems) + c // z_elems, (lanes, lanes))
 
 
-def stacked_dot(table, value):
+def stacked(value):
     high, low = pieces(value, 2)
-    gap = jnp.zeros((table.shape[1] - 3 * value.shape[0], value.shape[1]), jnp.bfloat16)
-    return dot(table, jnp.concatenate([high, high, low, gap], axis=0))
+    gap = jnp.zeros((256 - 3 * value.shape[0], value.shape[1]), jnp.bfloat16)
+    return jnp.concatenate([high, high, low, gap], axis=0)
 
 
 def to_elements(native, scratch, table, y_elems):
@@ -204,9 +205,9 @@
         for y in range(4 * y_elems + 1):
             rows = native(c, y)
             if y < 4 * y_elems:
-                scratch[y // 4, pl.ds(y % 4 * 3 + c, 4, stride=BLOCK), :] = rows
+                scratch[y // 4, pl.ds(ROWS[y % 4][c], 4, stride=BLOCK), :] = rows
             if y % 4 == 0 and y > 0:
-                scratch[y // 4 - 1, pl.ds(12 + c, 4, stride=BLOCK), :] = rows
+                scratch[y // 4 - 1, pl.ds(ROWS[4][c], 4, stride=BLOCK), :] = rows
     high, middle, low = pieces(
         jnp.concatenate([scratch[i] for i in range(y_elems)], axis=0), 3
     )
@@ -243,7 +244,12 @@
     for c in range(3):
         for y in range(4 * y_elems + 1):
             yel, yl = (y // 4, y % 4) if y < 4 * y_elems else (y_elems - 1, 4)
-            out_ref[c, y] = scratch[yel, pl.ds(yl * 3 + c, 4, stride=BLOCK), :]
+            out_ref[c, y] = scratch[yel, pl.ds(ROWS[yl][c], 4, stride=BLOCK), :]
+
+
+def shifted(rows, lanes):
+    lanes = lanes % rows.shape[1]
+    return pltpu.roll(rows, lanes, 1) if lanes else rows
 
 
 def block_iotas(lanes):
@@ -253,22 +259,16 @@
     )
 
 
-def fault_message(field, z_elems):
-    lanes = field.shape[1]
+def fault_message(plane, z_elems):
+    lanes = plane.shape[1]
     row, lane = block_iotas(lanes)
-    out = []
-    for x in range(4):
-        total = jnp.zeros((8, lanes), jnp.float32)
-        for zl in range(4):
-            at = x * PLANE + zl * BLOCK
-            first = pltpu.roll(pltpu.roll(field[at : at + 8], 4, 0), zl * z_elems, 1)
-            last = pltpu.roll(
-                pltpu.roll(field[at + 8 : at + 16], 4, 0), (zl + 1) * z_elems % lanes, 1
-            )
-            here = lane // z_elems == zl
-            total = jnp.where(here, jnp.where(row < 4, last, first), total)
-        out.append(total)
-    return jnp.concatenate(out, axis=0)
+    first = last = jnp.zeros((8, lanes), jnp.float32)
+    for zl in range(4):
+        at = zl * BLOCK
+        here = lane // z_elems == zl
+        first = jnp.where(here, shifted(plane[at : at + 8], zl * z_elems), first)
+        last = jnp.where(here, shifted(plane[at + 8 : at + 16], (zl + 1) * z_elems), last)
+    return jnp.where(row < 4, last, pltpu.roll(first, 4, 0))
 
 
 def swap_rows(message):
@@ -299,12 +299,8 @@
     return lax.broadcasted_iota(jnp.int32, (BLOCK, lanes), 1) % z_elems != 0
 
 
-def edge_force(edge_ref, own, lame_row, shear_row, z_elems):
-    lanes = own.shape[1]
-    padded = jnp.concatenate(
-        [own, jnp.zeros((OWN_COLS - own.shape[0], lanes), jnp.float32)], axis=0
-    )
-    result = split_dot(edge_ref[0], edge_ref[1], padded)
+def edge_message(result, lame_row, shear_row, z_elems):
+    lanes = result.shape[1]
     force = lame_row * result[:PLANE] + shear_row * result[PLANE:]
     top = force[:BLOCK] + jnp.where(
         above_lanes(lanes, z_elems), pltpu.roll(force[4 * BLOCK :], 1, 1), 0.0
@@ -388,16 +384,19 @@
     copies[0].wait()
     cur = to_elements(lambda c, y: now_ref[c, y], scratch, gather, y_elems)
     copies[5].wait()
-    right = edge_force(edge_ref, cur, lame_row, shear_row, z_elems)
+    planes = [cur[x * PLANE : (x + 1) * PLANE] for x in range(4)]
+    edge = sum(dot(edge_ref[x], stacked(planes[x])) for x in range(4))
+    right = edge_message(edge, lame_row, shear_row, z_elems)
     even_ref[...], odd_ref[...] = select_messages(parity, cur[: 4 * BLOCK], right)
     cur_ref[...] = cur
-    fault_out_ref[:32] = fault_message(cur, z_elems)
+    for x in range(4):
+        fault_out_ref[8 * x : 8 * x + 8] = fault_message(planes[x], z_elems)
 
 
 def prepare_kernel(cur_ref, material_ref, own_ref, touch_ref, base_ref, edge_part_ref):
     cur = cur_ref[...]
     base_ref[...] = own_force(own_ref, cur, material_ref[0:1], material_ref[1:2])
-    edge_part_ref[...] = stacked_dot(touch_ref[...], cur[:PLANE])
+    edge_part_ref[...] = dot(touch_ref[...], stacked(cur[:PLANE]))
 
 
 def setup_kernel(
@@ -465,74 +464,6 @@
         copy.wait()
 
 
-def advance(
-    step, place, last_place, cur, fol, minv, base, touch, material, even_in, odd_in, fault_in, tangents, far_table, own_fault,
-    y_elems, z_elems,
-):
-    lanes = cur.shape[1]
-    even = place % 2 == 0
-    far = jnp.where(place == last_place, 0.0, jnp.where(even, even_in, odd_in))
-    left = jnp.where(place == 0, 0.0, jnp.where(even, odd_in, even_in))
-    lane_wide = lax.broadcasted_iota(jnp.int32, (BLOCK, lanes), 1)
-    below = jnp.where(
-        lane_wide % z_elems != z_elems - 1, pltpu.roll(far[:BLOCK], lanes - 1, 1), 0.0
-    )
-    far = jnp.concatenate([far, below], axis=0)
-    lame_row, shear_row = material[0:1], material[1:2]
-    result = stacked_dot(far_table, far)
-    force = base + (lame_row * result[: 4 * PLANE] + shear_row * result[4 * PLANE :])
-    left_lame = left[BLOCK - 1 : BLOCK]
-    left_shear = left[2 * BLOCK - 1 : 2 * BLOCK]
-    from_left = left_lame * touch[:PLANE] + left_shear * touch[PLANE:]
-    from_left = jnp.concatenate([from_left[: 4 * BLOCK] + left, from_left[4 * BLOCK :]], axis=0)
-    row, lane = block_iotas(lanes)
-    across = lane // z_elems
-    rows_first = row < 3
-    rows_last = jnp.logical_and(row >= 4, row < 7)
-    add_first = jnp.logical_and(rows_first, across > 0)
-    take_last = jnp.logical_and(rows_last, across < y_elems - 1)
-    pull_first = jnp.logical_and(rows_first, across == 0)
-    pull_last = jnp.logical_and(rows_last, across == y_elems - 1)
-    above = above_lanes(lanes, z_elems)
-    below_t, own_t = tangents
-    planes = []
-    for x in range(4):
-        blocks = []
-        for zl in range(5):
-            at = x * PLANE + zl * BLOCK
-            block = force[at : at + BLOCK]
-            if x == 0:
-                block = block + from_left[zl * BLOCK : (zl + 1) * BLOCK]
-            blocks.append(block)
-        blocks[0] = blocks[0] + jnp.where(above, pltpu.roll(blocks[4], 1, 1), 0.0)
-        stiff = jnp.where(
-            jnp.logical_or(row == 1, row == 5),
-            lock_stiffness,
-            jnp.where(row < 4, below_t[4 * step + x : 4 * step + x + 1], own_t[4 * step + x : 4 * step + x + 1]),
-        )
-        pulled = stiff * (fault_in[8 * x : 8 * x + 8] - own_fault[8 * x : 8 * x + 8])
-        for zl in range(4):
-            low, high = blocks[zl][:8], blocks[zl][8:]
-            low = low + jnp.where(
-                add_first, pltpu.roll(pltpu.roll(high, 4, 0), z_elems, 1), 0.0
-            )
-            high = jnp.where(
-                take_last, pltpu.roll(pltpu.roll(low, 4, 0), lanes - z_elems, 1), high
-            )
-            low = low - jnp.where(
-                pull_first, pltpu.roll(pulled, (lanes - zl * z_elems) % lanes, 1), 0.0
-            )
-            high = high - jnp.where(
-                pull_last,
-                pltpu.roll(pulled, (lanes - (zl + 1) * z_elems) % lanes, 1),
-                0.0,
-            )
-            blocks[zl] = jnp.concatenate([low, high], axis=0)
-        blocks[4] = pltpu.roll(blocks[0], lanes - 1, 1)
-        planes.extend(blocks)
-    return (2.0 * cur - fol) - minv * jnp.concatenate(planes, axis=0)
-
-
 def fault_input(up_ref, down_ref, count):
     if down_ref is None:
         return up_ref[:count]
@@ -541,37 +472,100 @@
     return jnp.where(row % 8 < 4, up, down)
 
 
-def step_kernel(*refs, step, last, last_place, pair, y_elems, z_elems):
-    refs = list(refs)
+def step_kernel(*refs, step, last, extra, last_place, pair, y_elems, z_elems):
     cur_ref, fol_ref, minv_ref, base_ref, touch_ref, material_ref, even_ref, odd_ref = refs[:8]
-    refs = refs[8:]
+    refs = list(refs[8:])
     up_ref = refs.pop(0)
     down_ref = None if pair else refs.pop(0)
     first_up_ref, own_ref, first_own_ref, far_ref, edge_ref = refs[:5]
-    refs = refs[5:]
-    place = lax.axis_index("dom")
-    cur = cur_ref[...]
-    tangents = (first_up_ref[32:], first_own_ref[32:])
-    new = advance(
-        step, place, last_place, cur, fol_ref[...], minv_ref[...], base_ref[...], touch_ref[...],
-        material_ref[...], even_ref[...], odd_ref[...], fault_input(up_ref, down_ref, 32), tangents,
-        far_ref[...], swap_rows(own_ref[:32]), y_elems, z_elems,
-    )
+    refs = refs[5 + extra :]
     if last:
-        _, back_ref, out_ref, scratch = refs
-        from_elements(new, scratch, back_ref, out_ref, y_elems)
+        back_ref, out_ref, scratch = refs
     else:
         new_ref, even_out, odd_out, fault_out = refs
-        new_ref[...] = new
-        fault_out[...] = fault_message(new, z_elems)
-        right = edge_force(edge_ref, new, material_ref[0:1], material_ref[1:2], z_elems)
-        even_out[...], odd_out[...] = select_messages(place % 2, new[: 4 * BLOCK], right)
+    place = lax.axis_index("dom")
+    lanes = cur_ref.shape[1]
+    even = place % 2 == 0
+    far = jnp.where(place == last_place, 0.0, jnp.where(even, even_ref[...], odd_ref[...]))
+    left = jnp.where(place == 0, 0.0, jnp.where(even, odd_ref[...], even_ref[...]))
+    lane_wide = lax.broadcasted_iota(jnp.int32, (BLOCK, lanes), 1)
+    below = jnp.where(
+        lane_wide % z_elems != z_elems - 1, pltpu.roll(far[:BLOCK], lanes - 1, 1), 0.0
+    )
+    far = stacked(jnp.concatenate([far, below], axis=0))
+    lame_row, shear_row = material_ref[0:1], material_ref[1:2]
+    left_lame = left[BLOCK - 1 : BLOCK]
+    left_shear = left[2 * BLOCK - 1 : 2 * BLOCK]
+    from_left = left_lame * touch_ref[:PLANE] + left_shear * touch_ref[PLANE:]
+    row, lane = block_iotas(lanes)
+    across = lane // z_elems
+    shared = row < 3
+    add_first = jnp.logical_and(shared, across > 0)
+    take_last = jnp.logical_and(shared, across < y_elems - 1)
+    pull_first = jnp.logical_and(shared, across == 0)
+    pull_last = jnp.logical_and(shared, across == y_elems - 1)
+    above = above_lanes(lanes, z_elems)
+    fault_in = fault_input(up_ref, down_ref, 32)
+    planes = []
+    edge = 0.0
+    for x in range(4):
+        rows = slice(x * PLANE, (x + 1) * PLANE)
+        result = dot(far_ref[x], far)
+        force = base_ref[rows] + (lame_row * result[:PLANE] + shear_row * result[PLANE:])
+        blocks = [force[zl * BLOCK : (zl + 1) * BLOCK] for zl in range(5)]
+        if x == 0:
+            blocks = [b + from_left[i * BLOCK : (i + 1) * BLOCK] for i, b in enumerate(blocks)]
+            blocks[:4] = [b + left[i * BLOCK : (i + 1) * BLOCK] for i, b in enumerate(blocks[:4])]
+        blocks[0] = blocks[0] + jnp.where(above, pltpu.roll(blocks[4], 1, 1), 0.0)
+        at, k = slice(8 * x, 8 * x + 8), slice(32 + 4 * step + x, 33 + 4 * step + x)
+        stiff = jnp.where(
+            jnp.logical_or(row == 1, row == 5),
+            lock_stiffness,
+            jnp.where(row < 4, first_up_ref[k], first_own_ref[k]),
+        )
+        pulled = stiff * (fault_in[at] - pltpu.roll(own_ref[at], 4, 0))
+        pulled_last = pltpu.roll(pulled, 4, 0)
+        for zl in range(4):
+            low, high = blocks[zl][:8], blocks[zl][8:]
+            low = low + jnp.where(add_first, shifted(high, z_elems), 0.0)
+            high = jnp.where(take_last, shifted(low, -z_elems), high)
+            low = low - jnp.where(pull_first, shifted(pulled, -zl * z_elems), 0.0)
+            high = high - jnp.where(
+                pull_last, shifted(pulled_last, -(zl + 1) * z_elems), 0.0
+            )
+            blocks[zl] = jnp.concatenate([low, high], axis=0)
+        blocks[4] = pltpu.roll(blocks[0], lanes - 1, 1)
+        plane = (2.0 * cur_ref[rows] - fol_ref[rows]) - minv_ref[rows] * jnp.concatenate(
+            blocks, axis=0
+        )
+        if last:
+            planes.append(plane)
+        else:
+            new_ref[rows] = plane
+            fault_out[at] = fault_message(plane, z_elems)
+            edge = edge + dot(edge_ref[x], stacked(plane))
+            if x == 0:
+                first = plane[: 4 * BLOCK]
+    if last:
+        from_elements(jnp.concatenate(planes, axis=0), scratch, back_ref, out_ref, y_elems)
+    else:
+        right = edge_message(edge, lame_row, shear_row, z_elems)
+        even_out[...], odd_out[...] = select_messages(place % 2, first, right)
+
+
+def mask_kernel(owner_ref, _, mask_ref):
+    shape = (PATCH_ROWS, mask_ref.shape[1])
+    first = (lax.axis_index("dom") - REACH) * PATCH_DEV
+    number = lax.broadcasted_iota(jnp.int32, shape, 0) + first
+    for x in range(4):
+        mask = jnp.where(number == owner_ref[0, x], 1.0, 0.0)
+        mask_ref[PATCH_ROWS * x : PATCH_ROWS * (x + 1)] = mask
 
 
 def output_kernel(*refs, pair, steps, y_elems, z_elems):
-    owner_ref, field_ref, back_ref, weight_ref = refs[:4]
-    out_ref, grad_ref, mask_ref, table_ref, scratch = refs[-5:]
-    messages = refs[4:-5]
+    field_ref, back_ref, weight_ref = refs[:3]
+    out_ref, grad_ref, table_ref, scratch = refs[-4:]
+    messages = refs[3:-4]
     count = 2 if pair else 3
     grads = [jnp.zeros((8, weight_ref.shape[1]), jnp.float32) for _ in range(4)]
     for i in range(steps):
@@ -582,12 +576,6 @@
         for x in range(4):
             grads[x] = grads[x] + slip[8 * x : 8 * x + 8] * weight_ref[4 * i + x : 4 * i + x + 1]
     grad_ref[...] = jnp.concatenate(grads, axis=0)
-    shape = (PATCH_ROWS, weight_ref.shape[1])
-    first = (lax.axis_index("dom") - REACH) * PATCH_DEV
-    number = lax.broadcasted_iota(jnp.int32, shape, 0) + first
-    for x in range(4):
-        mask = jnp.where(number == owner_ref[0, x], 1.0, 0.0)
-        mask_ref[PATCH_ROWS * x : PATCH_ROWS * (x + 1)] = mask
     table_ref[...] = fault_table_back(weight_ref.shape[1], z_elems)
     from_elements(field_ref[...], scratch, back_ref, out_ref, y_elems)
 
@@ -740,23 +728,30 @@
         args = [cur, fol, minv, base, touch, material, even_in, odd_in] + fault_in
         args += [first_in[0], fault_rows, first_fault, far_table, edge_table]
         static = dict(
-            step=step, last=last, last_place=lax.axis_size("dom") - 1, pair=pair, y_elems=y_elems,
+            step=step, last=last, extra=1 if last or step == 1 else 0, last_place=lax.axis_size("dom") - 1, pair=pair, y_elems=y_elems,
             z_elems=z_elems,
         )
+        if step == 1:
+            mask = kernel_call(mask_kernel, [(4 * PATCH_ROWS, lanes)], [patch_owner, cur], (0,), unread=(1,))[0]
+            args.append(mask)
         if not last:
             new, even, odd, new_fault = kernel_call(
-                step_kernel, [field, plane, plane, (32, lanes)], args, **static
+                step_kernel,
+                [field, plane, plane, (32, lanes)],
+                args,
+                unread=(len(args) - 1,) if step == 1 else (),
+                **static,
             )
             fol, cur, fault_rows = cur, new, new_fault
             even_in, odd_in, fault_in = exchange(even, odd, fault_rows)
         else:
             whole = (3, 4 * y_elems + 1, 4, lanes)
             known = seen[: len(seen) - len(fault_in)]
-            later, grad, mask, table = kernel_call(
+            later, grad, table = kernel_call(
                 output_kernel,
-                [whole, (32, lanes), (4 * PATCH_ROWS, lanes), ((lanes, lanes), jnp.bfloat16)],
-                [patch_owner, cur, back, weight] + known,
-                (0,),
+                [whole, (32, lanes), ((lanes, lanes), jnp.bfloat16)],
+                [cur, back, weight] + known,
+                (),
                 [native],
                 pair=pair,
                 steps=steps,

time: 33.8 us -> 33.5 us (level)
  local copies, waits for them, and re-layouts: 0.65 us -> 0.14 us
    unnamed x2, local copies, waits for them, and re-layouts: 0.65 us -> 0.14 us
    pallas_call x12 -> x13, Pallas kernels: 11.9 us -> 12 us  [kernel_call(): pl.pallas_call(functools.partial(body, **static) if static else body, out...]
  transfers between devices with their start and end apart: 16 -> 16, of which waited for: 3 -> 4; matrix products, arithmetic and copies ran while one was open for 0% -> 0% of each run, Pallas kernels for 20% -> 20%
where the time goes in v3:
time: 33.5 us; the launch traced here: 33.3 us
  starting transfers between devices  13.7 us (41%)
  Pallas kernels  12 us (36%)
  waiting for transfers between devices  6.13 us (18%)
  between operations  0.71 us (2%)
  other arithmetic  0.57 us (2%)
    pallas_call x13, Pallas kernels, kernel_call(): pl.pallas_call(functools.partial(body, **static) if static else body, out...  12 us
    ppermute x12, starting transfers between devices, swapped(): return lax.ppermute(block, ('dom', 'depth'), route)  10.2 us
    ppermute x4, waiting for transfers between devices, from_behind(): lax.ppermute(block, axis, [((i - distance) % size, i) for i in range(size)])  6.1 us
    ppermute x4, starting transfers between devices, from_behind(): lax.ppermute(block, axis, [((i - distance) % size, i) for i in range(size)])  3.57 us
  transfers between devices with their start and end apart: 16, of which 4 were waited for; matrix products, arithmetic and copies ran while one was open for 0% of the time, Pallas kernels for 20%

profile of v3, /device:TPU:0, one launch (start us, length us, event | category | flops | bytes accessed | tf_op | source)
XLA Modules:
  0.0 33.3 jit_solution(5750877339851983249)
XLA Ops:
  0.6 1.9 %shard_map.166 = (f32[320,128]{1,0:T(8,128)S(1)}, f32[64,128]{1,0:T(8,128)S(1)}, f32[64,128]{1,0:T(8,128)S(1)}, f32[48,128]{1,0:T(8,128)S(1)}, f32[8,128]{1,0:T(8,128)S(1)}, /*index=5*/bf16[4,160,256]{2,1,0:T(8,128)(2,1)S(1)}) custom-call(f32[3,17,4,128]{3,2,1,0:T(4,128)} %bitcast.13, s32[4,4,128]{2,1,0:T(4,128)} %bitcast.16, f32[4,128]{1,0:T(4,128)} %bitcast.18, ...), custom_call_target="tpu_custom_call" | custom-call | tf_op jit(solution)/shard_map/pallas_call | solution.py:623
  2.6 0.5 %collective-permute-start = (f32[64,128]{1,0:T(8,128)S(1)}, f32[64,128]{1,0:T(8,128)S(1)}, u32[]{:S(2)}, u32[]{:S(2)}) collective-permute-start(f32[64,128]{1,0:T(8,128)S(1)} %get-tuple-element.52), channel_id=1, source_target_pairs={{0,2},{1,3},{2,0},{3,1},{4,6},{5,7},{6,4},{7,5},{8,10},{9,11},{10,... | collective-permute-start | bytes 98312 | tf_op jit(solution)/shard_map/ppermute | solution.py:646
  3.1 2.6 %collective-permute-start.1 = (f32[64,128]{1,0:T(8,128)S(1)}, f32[64,128]{1,0:T(8,128)S(1)}, u32[]{:S(2)}, u32[]{:S(2)}) collective-permute-start(f32[64,128]{1,0:T(8,128)S(1)} %get-tuple-element.53), channel_id=1, source_target_pairs={{0,1},{1,0},{2,4},{3,5},{4,2},{5,3},{6,8},{7,9},{8,6},{9,7},{10,12... | collective-permute-start | bytes 98312 | tf_op jit(solution)/shard_map/ppermute | solution.py:646
  5.7 1.7 %shard_map.167 = (f32[320,128]{1,0:T(8,128)S(1)}, f32[320,128]{1,0:T(8,128)S(1)}, f32[16,128]{1,0:T(8,128)S(1)}, bf16[2,640,384]{2,1,0:T(8,128)(2,1)S(1)}, bf16[...) custom-call(f32[3,17,4,128]{3,2,1,0:T(4,128)} %bitcast.12, ...), custom_call_target="tpu_custom_call" | custom-call | tf_op jit(solution)/shard_map/pallas_call | solution.py:623
  8.0 1.5 %collective-permute-done.2.refs_8_.refs_9_.refs_4_ = f32[48,128]{1,0:T(8,128)S(1)} collective-permute-done((f32[48,128]{1,0:T(8,128)S(1)}, f32[48,128]{1,0:T(8,128)S(1)}, u32[]{:S(2)}, u32[]{:S(2)}) %collective-permute-start.2) | collective-permute-done | bytes 24608 | tf_op jit(solution)/shard_map/ppermute | solution.py:651
  9.5 1.1 %shard_map.169 = (f32[320,128]{1,0:T(8,128)S(1)}, f32[64,128]{1,0:T(8,128)S(1)}, f32[64,128]{1,0:T(8,128)S(1)}, f32[32,128]{1,0:T(8,128)S(1)}) custom-call(f32[320,128]{1,0:T(8,128)S(1)} %get-tuple-element.44.cur_ref.refs_0_.refs_1_, f32[320,128]{1,0:T(8,128)S(1)} %get-tuple-element.45.refs_1_, f32[320,128]{1,0:T(8,128)S(1)} %get-tuple-element.46.refs_2_, ...), custom_call_target="tpu_custom_call" | custom-call | tf_op jit(solution)/shard_map/pallas_call | solution.py:623
  10.6 0.6 %collective-permute-start.4 = (f32[64,128]{1,0:T(8,128)S(1)}, f32[64,128]{1,0:T(8,128)S(1)}, u32[]{:S(2)}, u32[]{:S(2)}) collective-permute-start(f32[64,128]{1,0:T(8,128)S(1)} %get-tuple-element.61), channel_id=1, source_target_pairs={{0,1},{1,0},{2,4},{3,5},{4,2},{5,3},{6,8},{7,9},{8,6},{9,7},{10,12... | collective-permute-start | bytes 98312 | tf_op jit(solution)/shard_map/ppermute | solution.py:646
  11.1 1.5 %collective-permute-start.5 = (f32[32,128]{1,0:T(8,128)S(1)}, f32[32,128]{1,0:T(8,128)S(1)}, u32[]{:S(2)}, u32[]{:S(2)}) collective-permute-start(f32[32,128]{1,0:T(8,128)S(1)} %get-tuple-element.62.refs_10_.refs_5_), channel_id=1, source_target_pairs={{1,0},{0,1},{3,2},{2,3},{5,4},{4,5},{7,6},{6,7},{9,8},{8,9},{11,10... | collective-permute-start | bytes 49160 | tf_op jit(solution)/shard_map/ppermute | solution.py:651
  13.3 0.6 %shard_map.171.refs_14_.refs_0_ = f32[64,128]{1,0:T(8,128)S(1)} custom-call(s32[1,4]{1,0:T(1,128)S(1)} %copy-done, f32[320,128]{1,0:T(8,128)S(1)} %get-tuple-element.57.cur_ref._.refs_0_.refs_1_), custom_call_target="tpu_custom_call" | custom-call | tf_op jit(solution)/shard_map/pallas_call | solution.py:623
  13.9 1.1 %collective-permute-done.5.refs_8_.refs_6_ = f32[32,128]{1,0:T(8,128)S(1)} collective-permute-done((f32[32,128]{1,0:T(8,128)S(1)}, f32[32,128]{1,0:T(8,128)S(1)}, u32[]{:S(2)}, u32[]{:S(2)}) %collective-permute-start.5) | collective-permute-done | bytes 16416 | tf_op jit(solution)/shard_map/ppermute | solution.py:651
  15.0 1.1 %shard_map.172 = (f32[320,128]{1,0:T(8,128)S(1)}, f32[64,128]{1,0:T(8,128)S(1)}, f32[64,128]{1,0:T(8,128)S(1)}, f32[32,128]{1,0:T(8,128)S(1)}) custom-call(f32[320,128]{1,0:T(8,128)S(1)} %get-tuple-element.57.cur_ref._.refs_0_.refs_1_, f32[320,128]{1,0:T(8,128)S(1)} %get-tuple-element.44.cur_ref.refs_0_.refs_1_, f32[320,128]{1,0:T(8,128)S(1)} %get-tuple-element.46.refs_2_, ...), custom_call_target="tpu_custom_call" | custom-call | tf_op jit(solution)/shard_map/pallas_call | solution.py:623
  16.1 1.5 %collective-permute-start.7 = (f32[64,128]{1,0:T(8,128)S(1)}, f32[64,128]{1,0:T(8,128)S(1)}, u32[]{:S(2)}, u32[]{:S(2)}) collective-permute-start(f32[64,128]{1,0:T(8,128)S(1)} %get-tuple-element.67), channel_id=1, source_target_pairs={{0,1},{1,0},{2,4},{3,5},{4,2},{5,3},{6,8},{7,9},{8,6},{9,7},{10,12... | collective-permute-start | bytes 98312 | tf_op jit(solution)/shard_map/ppermute | solution.py:646
  17.6 0.6 %collective-permute-start.8 = (f32[32,128]{1,0:T(8,128)S(1)}, f32[32,128]{1,0:T(8,128)S(1)}, u32[]{:S(2)}, u32[]{:S(2)}) collective-permute-start(f32[32,128]{1,0:T(8,128)S(1)} %get-tuple-element.68.refs_10_.refs_7_), channel_id=1, source_target_pairs={{1,0},{0,1},{3,2},{2,3},{5,4},{4,5},{7,6},{6,7},{9,8},{8,9},{11,10... | collective-permute-start | bytes 49160 | tf_op jit(solution)/shard_map/ppermute | solution.py:651
  18.7 2.7 %collective-permute-done.8.refs_8_ = f32[32,128]{1,0:T(8,128)S(1)} collective-permute-done((f32[32,128]{1,0:T(8,128)S(1)}, f32[32,128]{1,0:T(8,128)S(1)}, u32[]{:S(2)}, u32[]{:S(2)}) %collective-permute-start.8) | collective-permute-done | bytes 16416 | tf_op jit(solution)/shard_map/ppermute | solution.py:651
  21.3 1.1 %shard_map.174 = (f32[320,128]{1,0:T(8,128)S(1)}, f32[64,128]{1,0:T(8,128)S(1)}, f32[64,128]{1,0:T(8,128)S(1)}, f32[32,128]{1,0:T(8,128)S(1)}) custom-call(f32[320,128]{1,0:T(8,128)S(1)} %get-tuple-element.63.cur_ref.refs_0_.refs_1_, f32[320,128]{1,0:T(8,128)S(1)} %get-tuple-element.57.cur_ref._.refs_0_.refs_1_, f32[320,128]{1,0:T(8,128)S(1)} %get-tuple-element.46.refs_2_, ...), custom_call_target="tpu_custom_call" | custom-call | tf_op jit(solution)/shard_map/pallas_call | solution.py:623
  22.4 0.7 %collective-permute-start.10 = (f32[64,128]{1,0:T(8,128)S(1)}, f32[64,128]{1,0:T(8,128)S(1)}, u32[]{:S(2)}, u32[]{:S(2)}) collective-permute-start(f32[64,128]{1,0:T(8,128)S(1)} %get-tuple-element.73), channel_id=1, source_target_pairs={{0,1},{1,0},{2,4},{3,5},{4,2},{5,3},{6,8},{7,9},{8,6},{9,7},{10,12... | collective-permute-start | bytes 98312 | tf_op jit(solution)/shard_map/ppermute | solution.py:646
  23.1 1.4 %collective-permute-start.11 = (f32[32,128]{1,0:T(8,128)S(1)}, f32[32,128]{1,0:T(8,128)S(1)}, u32[]{:S(2)}, u32[]{:S(2)}) collective-permute-start(f32[32,128]{1,0:T(8,128)S(1)} %get-tuple-element.74.refs_9_.refs_10_), channel_id=1, source_target_pairs={{1,0},{0,1},{3,2},{2,3},{5,4},{4,5},{7,6},{6,7},{9,8},{8,9},{11,10... | collective-permute-start | bytes 49160 | tf_op jit(solution)/shard_map/ppermute | solution.py:651
  25.0 1.0 %shard_map.176 = (f32[3,17,4,128]{3,2,1,0:T(4,128)}, f32[32,128]{1,0:T(8,128)S(1)}, bf16[128,128]{1,0:T(8,128)(2,1)S(1)}) custom-call(f32[320,128]{1,0:T(8,128)S(1)} %get-tuple-element.69.cur_ref.refs_0_, bf16[512,512]{1,0:T(8,128)(2,1)S(1)} %get-tuple-element.76.refs_1_.refs_15_, f32[16,128]{1,0:T(8,128)S(1)} %get-tuple-element.75.refs_2_.refs_1_, ...), custom_call_target="tpu_custom_call" | custom-call | tf_op jit(solution)/shard_map/pallas_call | solution.py:623
  26.0 0.9 %collective-permute-done.11.refs_7_.refs_8_ = f32[32,128]{1,0:T(8,128)S(1)} collective-permute-done((f32[32,128]{1,0:T(8,128)S(1)}, f32[32,128]{1,0:T(8,128)S(1)}, u32[]{:S(2)}, u32[]{:S(2)}) %collective-permute-start.11) | collective-permute-done | bytes 16416 | tf_op jit(solution)/shard_map/ppermute | solution.py:651
  27.0 1.4 %collective-permute-start.12 = (f32[2,128]{1,0:T(2,128)S(1)}, f32[2,128]{1,0:T(2,128)S(1)}, u32[]{:S(2)}, u32[]{:S(2)}) collective-permute-start(f32[2,128]{1,0:T(2,128)S(1)} %get-tuple-element.81), channel_id=1, source_target_pairs={{0,1},{1,0},{2,4},{3,5},{4,2},{5,3},{6,8},{7,9},{8,6},{9,7},{10,12... | collective-permute-start | bytes 3080 | tf_op jit(solution)/shard_map/ppermute | solution.py:646
  28.4 0.6 %collective-permute-start.13 = (f32[2,128]{1,0:T(2,128)S(1)}, f32[2,128]{1,0:T(2,128)S(1)}, u32[]{:S(2)}, u32[]{:S(2)}) collective-permute-start(f32[2,128]{1,0:T(2,128)S(1)} %get-tuple-element.82), channel_id=1, source_target_pairs={{0,1},{1,0},{2,3},{3,2},{4,8},{5,9},{6,10},{7,11},{8,4},{9,5},{10,... | collective-permute-start | bytes 3080 | tf_op jit(solution)/shard_map/ppermute | solution.py:646
  29.1 2.0 %collective-permute-start.14 = (f32[2,128]{1,0:T(2,128)S(1)}, f32[2,128]{1,0:T(2,128)S(1)}, u32[]{:S(2)}, u32[]{:S(2)}) collective-permute-start(f32[2,128]{1,0:T(2,128)S(1)} %get-tuple-element.83), channel_id=1, source_target_pairs={{0,4},{1,5},{2,6},{3,7},{4,0},{5,1},{6,2},{7,3},{8,12},{9,13},{10,... | collective-permute-start | bytes 3080 | tf_op jit(solution)/shard_map/ppermute | solution.py:646
  31.2 1.5 %shard_map.178 = f32[3,17,4,128]{3,2,1,0:T(4,128)} custom-call(f32[320,128]{1,0:T(8,128)S(1)} %get-tuple-element.69.cur_ref.refs_0_, f32[320,128]{1,0:T(8,128)S(1)} %get-tuple-element.63.cur_ref.refs_0_.refs_1_, f32[320,128]{1,0:T(8,128)S(1)} %get-tuple-element.46.refs_2_, f32[320,128]{1,0:T(8,128)S(1)} %get-tuple-element.70.refs_3_, ...), custom_call_target="tpu_custom_call" | custom-call | tf_op jit(solution)/shard_map/pallas_call | solution.py:623
  32.8 0.6 %add_bitcast_fusion = f32[1,2,128]{2,1,0:T(2,128)} fusion(f32[2,128]{1,0:T(2,128)S(1)} %collective-permute-done.15, f32[2,128]{1,0:T(2,128)S(1)} %collective-permute-done.14, f32[2,128]{1,0:T(2,128)S(1)} %collective-permute-done.13, f32[2,128]{1,0:T(2,128)S(1)} %get-tuple-element.79.refs_14_, f32[2,128]{1,0:T(2,128)S(1)} %collective-permute-done.12), kind=kLoop, calls=%fused_computation | loop fusion | flops 1024 | bytes 6144 | tf_op jit(solution)/shard_map/broadcast_in_dim | solution.py:783
  (24 shorter events, 2.6 us)
Async XLA Ops:
  2.6 6.9 %collective-permute-start = (f32[64,128]{1,0:T(8,128)S(1)}, f32[64,128]{1,0:T(8,128)S(1)}, u32[]{:S(2)}, u32[]{:S(2)}) collective-permute-start(f32[64,128]{1,0:T(8,128)S(1)} %get-tuple-element.52), channel_id=1, source_target_pairs={{0,2},{1,3},{2,0},{3,1},{4,6},{5,7},{6,4},{7,5},{8,10},{9,11},{10,... | collective-permute-start | bytes 98312 | tf_op jit(solution)/shard_map/ppermute | solution.py:646
  3.1 6.4 %collective-permute-start.1 = (f32[64,128]{1,0:T(8,128)S(1)}, f32[64,128]{1,0:T(8,128)S(1)}, u32[]{:S(2)}, u32[]{:S(2)}) collective-permute-start(f32[64,128]{1,0:T(8,128)S(1)} %get-tuple-element.53), channel_id=1, source_target_pairs={{0,1},{1,0},{2,4},{3,5},{4,2},{5,3},{6,8},{7,9},{8,6},{9,7},{10,12... | collective-permute-start | bytes 98312 | tf_op jit(solution)/shard_map/ppermute | solution.py:646
  5.7 3.8 %collective-permute-start.2 = (f32[48,128]{1,0:T(8,128)S(1)}, f32[48,128]{1,0:T(8,128)S(1)}, u32[]{:S(2)}, u32[]{:S(2)}) collective-permute-start(f32[48,128]{1,0:T(8,128)S(1)} %get-tuple-element.54.refs_10_.refs_11_.refs_3_), channel_id=1, source_target_pairs={{1,0},{0,1},{3,2},{2,3},{5,4},{4,5},{7,6},{6,7},{9,8},{8,9},{11,10... | collective-permute-start | bytes 73736 | tf_op jit(solution)/shard_map/ppermute | solution.py:651
  10.6 4.4 %collective-permute-start.3 = (f32[64,128]{1,0:T(8,128)S(1)}, f32[64,128]{1,0:T(8,128)S(1)}, u32[]{:S(2)}, u32[]{:S(2)}) collective-permute-start(f32[64,128]{1,0:T(8,128)S(1)} %get-tuple-element.60), channel_id=1, source_target_pairs={{0,2},{1,3},{2,0},{3,1},{4,6},{5,7},{6,4},{7,5},{8,10},{9,11},{10,... | collective-permute-start | bytes 98312 | tf_op jit(solution)/shard_map/ppermute | solution.py:646
  10.6 4.4 %collective-permute-start.4 = (f32[64,128]{1,0:T(8,128)S(1)}, f32[64,128]{1,0:T(8,128)S(1)}, u32[]{:S(2)}, u32[]{:S(2)}) collective-permute-start(f32[64,128]{1,0:T(8,128)S(1)} %get-tuple-element.61), channel_id=1, source_target_pairs={{0,1},{1,0},{2,4},{3,5},{4,2},{5,3},{6,8},{7,9},{8,6},{9,7},{10,12... | collective-permute-start | bytes 98312 | tf_op jit(solution)/shard_map/ppermute | solution.py:646
  11.1 3.8 %collective-permute-start.5 = (f32[32,128]{1,0:T(8,128)S(1)}, f32[32,128]{1,0:T(8,128)S(1)}, u32[]{:S(2)}, u32[]{:S(2)}) collective-permute-start(f32[32,128]{1,0:T(8,128)S(1)} %get-tuple-element.62.refs_10_.refs_5_), channel_id=1, source_target_pairs={{1,0},{0,1},{3,2},{2,3},{5,4},{4,5},{7,6},{6,7},{9,8},{8,9},{11,10... | collective-permute-start | bytes 49160 | tf_op jit(solution)/shard_map/ppermute | solution.py:651
  12.7 0.7 %copy-start = (s32[1,4]{1,0:T(1,128)S(1)}, s32[1,4]{1,0:T(1,128)}, u32[]{:S(2)}) copy-start(s32[1,4]{1,0:T(1,128)} %owner_ref.1) | copy-start | bytes 52
  16.0 5.3 %collective-permute-start.6 = (f32[64,128]{1,0:T(8,128)S(1)}, f32[64,128]{1,0:T(8,128)S(1)}, u32[]{:S(2)}, u32[]{:S(2)}) collective-permute-start(f32[64,128]{1,0:T(8,128)S(1)} %get-tuple-element.66), channel_id=1, source_target_pairs={{0,2},{1,3},{2,0},{3,1},{4,6},{5,7},{6,4},{7,5},{8,10},{9,11},{10,... | collective-permute-start | bytes 98312 | tf_op jit(solution)/shard_map/ppermute | solution.py:646
  16.1 5.3 %collective-permute-start.7 = (f32[64,128]{1,0:T(8,128)S(1)}, f32[64,128]{1,0:T(8,128)S(1)}, u32[]{:S(2)}, u32[]{:S(2)}) collective-permute-start(f32[64,128]{1,0:T(8,128)S(1)} %get-tuple-element.67), channel_id=1, source_target_pairs={{0,1},{1,0},{2,4},{3,5},{4,2},{5,3},{6,8},{7,9},{8,6},{9,7},{10,12... | collective-permute-start | bytes 98312 | tf_op jit(solution)/shard_map/ppermute | solution.py:646
  17.6 3.7 %collective-permute-start.8 = (f32[32,128]{1,0:T(8,128)S(1)}, f32[32,128]{1,0:T(8,128)S(1)}, u32[]{:S(2)}, u32[]{:S(2)}) collective-permute-start(f32[32,128]{1,0:T(8,128)S(1)} %get-tuple-element.68.refs_10_.refs_7_), channel_id=1, source_target_pairs={{1,0},{0,1},{3,2},{2,3},{5,4},{4,5},{7,6},{6,7},{9,8},{8,9},{11,10... | collective-permute-start | bytes 49160 | tf_op jit(solution)/shard_map/ppermute | solution.py:651
  22.4 4.5 %collective-permute-start.9 = (f32[64,128]{1,0:T(8,128)S(1)}, f32[64,128]{1,0:T(8,128)S(1)}, u32[]{:S(2)}, u32[]{:S(2)}) collective-permute-start(f32[64,128]{1,0:T(8,128)S(1)} %get-tuple-element.72), channel_id=1, source_target_pairs={{0,2},{1,3},{2,0},{3,1},{4,6},{5,7},{6,4},{7,5},{8,10},{9,11},{10,... | collective-permute-start | bytes 98312 | tf_op jit(solution)/shard_map/ppermute | solution.py:646
  22.4 4.5 %collective-permute-start.10 = (f32[64,128]{1,0:T(8,128)S(1)}, f32[64,128]{1,0:T(8,128)S(1)}, u32[]{:S(2)}, u32[]{:S(2)}) collective-permute-start(f32[64,128]{1,0:T(8,128)S(1)} %get-tuple-element.73), channel_id=1, source_target_pairs={{0,1},{1,0},{2,4},{3,5},{4,2},{5,3},{6,8},{7,9},{8,6},{9,7},{10,12... | collective-permute-start | bytes 98312 | tf_op jit(solution)/shard_map/ppermute | solution.py:646
  23.1 3.7 %collective-permute-start.11 = (f32[32,128]{1,0:T(8,128)S(1)}, f32[32,128]{1,0:T(8,128)S(1)}, u32[]{:S(2)}, u32[]{:S(2)}) collective-permute-start(f32[32,128]{1,0:T(8,128)S(1)} %get-tuple-element.74.refs_9_.refs_10_), channel_id=1, source_target_pairs={{1,0},{0,1},{3,2},{2,3},{5,4},{4,5},{7,6},{6,7},{9,8},{8,9},{11,10... | collective-permute-start | bytes 49160 | tf_op jit(solution)/shard_map/ppermute | solution.py:651
  27.0 5.7 %collective-permute-start.12 = (f32[2,128]{1,0:T(2,128)S(1)}, f32[2,128]{1,0:T(2,128)S(1)}, u32[]{:S(2)}, u32[]{:S(2)}) collective-permute-start(f32[2,128]{1,0:T(2,128)S(1)} %get-tuple-element.81), channel_id=1, source_target_pairs={{0,1},{1,0},{2,4},{3,5},{4,2},{5,3},{6,8},{7,9},{8,6},{9,7},{10,12... | collective-permute-start | bytes 3080 | tf_op jit(solution)/shard_map/ppermute | solution.py:646
  28.4 4.3 %collective-permute-start.13 = (f32[2,128]{1,0:T(2,128)S(1)}, f32[2,128]{1,0:T(2,128)S(1)}, u32[]{:S(2)}, u32[]{:S(2)}) collective-permute-start(f32[2,128]{1,0:T(2,128)S(1)} %get-tuple-element.82), channel_id=1, source_target_pairs={{0,1},{1,0},{2,3},{3,2},{4,8},{5,9},{6,10},{7,11},{8,4},{9,5},{10,... | collective-permute-start | bytes 3080 | tf_op jit(solution)/shard_map/ppermute | solution.py:646
  29.1 3.7 %collective-permute-start.14 = (f32[2,128]{1,0:T(2,128)S(1)}, f32[2,128]{1,0:T(2,128)S(1)}, u32[]{:S(2)}, u32[]{:S(2)}) collective-permute-start(f32[2,128]{1,0:T(2,128)S(1)} %get-tuple-element.83), channel_id=1, source_target_pairs={{0,4},{1,5},{2,6},{3,7},{4,0},{5,1},{6,2},{7,3},{8,12},{9,13},{10,... | collective-permute-start | bytes 3080 | tf_op jit(solution)/shard_map/ppermute | solution.py:646
  31.1 1.6 %collective-permute-start.15 = (f32[2,128]{1,0:T(2,128)S(1)}, f32[2,128]{1,0:T(2,128)S(1)}, u32[]{:S(2)}, u32[]{:S(2)}) collective-permute-start(f32[2,128]{1,0:T(2,128)S(1)} %get-tuple-element.84), channel_id=1, source_target_pairs={{0,2},{1,3},{2,0},{3,1},{4,6},{5,7},{6,4},{7,5},{8,10},{9,11},{10,... | collective-permute-start | bytes 3080 | tf_op jit(solution)/shard_map/ppermute | solution.py:646

commit v4 on v3

--- a/solution.py
+++ b/solution.py
@@ -198,7 +198,7 @@
     return jnp.concatenate([high, high, low, gap], axis=0)
 
 
-def to_elements(native, scratch, table, y_elems):
+def to_elements(native, scratch, table, y_elems, parts=3):
     group = 4 * BLOCK
     scratch[...] = jnp.zeros_like(scratch)
     for c in range(3):
@@ -208,12 +208,14 @@
                 scratch[y // 4, pl.ds(ROWS[y % 4][c], 4, stride=BLOCK), :] = rows
             if y % 4 == 0 and y > 0:
                 scratch[y // 4 - 1, pl.ds(ROWS[4][c], 4, stride=BLOCK), :] = rows
-    high, middle, low = pieces(
-        jnp.concatenate([scratch[i] for i in range(y_elems)], axis=0), 3
+    high, middle, *low = pieces(
+        jnp.concatenate([scratch[i] for i in range(y_elems)], axis=0), parts
     )
     result = dot(
         jnp.concatenate([high, middle], axis=1), jnp.concatenate([table, table], axis=0)
-    ) + dot(low, table)
+    )
+    for piece in low:
+        result = result + dot(piece, table)
     lanes = result.shape[1] // 5
     across = lax.broadcasted_iota(jnp.int32, (group, result.shape[1]), 1) % lanes // (
         lanes // y_elems
@@ -335,12 +337,18 @@
     lame_hbm,
     shear_hbm,
     edge_hbm,
+    own_hbm,
+    far_hbm,
+    touch_hbm,
     cur_ref,
     even_ref,
     odd_ref,
     fault_out_ref,
     material_ref,
     edge_ref,
+    own_ref,
+    far_ref,
+    touch_ref,
     scratch,
     now_ref,
     flags_ref,
@@ -357,6 +365,9 @@
             (lame_hbm, lame_ref),
             (shear_hbm, shear_ref),
             (edge_hbm, edge_ref),
+            (own_hbm, own_ref),
+            (far_hbm, far_ref),
+            (touch_hbm, touch_ref),
         ],
         sems,
     )
@@ -391,6 +402,8 @@
     cur_ref[...] = cur
     for x in range(4):
         fault_out_ref[8 * x : 8 * x + 8] = fault_message(planes[x], z_elems)
+    for copy in copies[6:]:
+        copy.wait()
 
 
 def prepare_kernel(cur_ref, material_ref, own_ref, touch_ref, base_ref, edge_part_ref):
@@ -405,17 +418,9 @@
     flags_hbm,
     stress_hbm,
     mass_hbm,
-    own_hbm,
-    far_hbm,
-    touch_hbm,
-    back_hbm,
     fol_ref,
     minv_ref,
     weight_ref,
-    own_ref,
-    far_ref,
-    touch_ref,
-    back_ref,
     scratch,
     next_ref,
     density_ref,
@@ -434,10 +439,6 @@
             (flags_hbm, flags_ref),
             (stress_hbm, stress_ref),
             (mass_hbm, mass_ref),
-            (own_hbm, own_ref),
-            (far_hbm, far_ref),
-            (touch_hbm, touch_ref),
-            (back_hbm, back_ref),
         ],
         sems,
     )
@@ -446,7 +447,7 @@
     for copy in copies[:5]:
         copy.wait()
     fol_ref[...] = to_elements(lambda c, y: next_ref[c, y], scratch, gather, y_elems)
-    density = to_elements(lambda c, y: density_ref[y], scratch, gather, y_elems)
+    density = to_elements(lambda c, y: density_ref[y], scratch, gather, y_elems, 2)
     table = mass_ref[...]
     first = lax.axis_index("dom") == 0
     plane = lax.broadcasted_iota(jnp.int32, table.shape, 0) < PLANE
@@ -460,8 +461,6 @@
             stress * jnp.where(flag == 1, 0.5, jnp.where(flag == 2, 1.0, 0.0))
         )
     weight_ref[...] = exact_dot(jnp.concatenate(weights, axis=0), fault)
-    for copy in copies[5:]:
-        copy.wait()
 
 
 def fault_input(up_ref, down_ref, count):
@@ -473,10 +472,10 @@
 
 
 def step_kernel(*refs, step, last, extra, last_place, pair, y_elems, z_elems):
-    cur_ref, fol_ref, minv_ref, base_ref, touch_ref, material_ref, even_ref, odd_ref = refs[:8]
+    cur_ref, fol_ref, minv_ref, base_ref, touch_ref, material_ref, odd_ref, up_ref = refs[:8]
     refs = list(refs[8:])
-    up_ref = refs.pop(0)
     down_ref = None if pair else refs.pop(0)
+    even_ref = refs.pop(0)
     first_up_ref, own_ref, first_own_ref, far_ref, edge_ref = refs[:5]
     refs = refs[5 + extra :]
     if last:
@@ -516,7 +515,10 @@
         if x == 0:
             blocks = [b + from_left[i * BLOCK : (i + 1) * BLOCK] for i, b in enumerate(blocks)]
             blocks[:4] = [b + left[i * BLOCK : (i + 1) * BLOCK] for i, b in enumerate(blocks[:4])]
-        blocks[0] = blocks[0] + jnp.where(above, pltpu.roll(blocks[4], 1, 1), 0.0)
+        blocks[0], blocks[4] = (
+            blocks[0] + jnp.where(above, pltpu.roll(blocks[4], 1, 1), 0.0),
+            blocks[4] + pltpu.roll(blocks[0], lanes - 1, 1),
+        )
         at, k = slice(8 * x, 8 * x + 8), slice(32 + 4 * step + x, 33 + 4 * step + x)
         stiff = jnp.where(
             jnp.logical_or(row == 1, row == 5),
@@ -525,16 +527,20 @@
         )
         pulled = stiff * (fault_in[at] - pltpu.roll(own_ref[at], 4, 0))
         pulled_last = pltpu.roll(pulled, 4, 0)
-        for zl in range(4):
+        for zl in range(5):
             low, high = blocks[zl][:8], blocks[zl][8:]
-            low = low + jnp.where(add_first, shifted(high, z_elems), 0.0)
-            high = jnp.where(take_last, shifted(low, -z_elems), high)
-            low = low - jnp.where(pull_first, shifted(pulled, -zl * z_elems), 0.0)
-            high = high - jnp.where(
-                pull_last, shifted(pulled_last, -(zl + 1) * z_elems), 0.0
+            move = zl * z_elems if zl < 4 else 1
+            blocks[zl] = jnp.concatenate(
+                [
+                    low
+                    + jnp.where(add_first, shifted(high, z_elems), 0.0)
+                    - jnp.where(pull_first, shifted(pulled, -move), 0.0),
+                    high
+                    + jnp.where(take_last, shifted(low, -z_elems), 0.0)
+                    - jnp.where(pull_last, shifted(pulled_last, -move - z_elems), 0.0),
+                ],
+                axis=0,
             )
-            blocks[zl] = jnp.concatenate([low, high], axis=0)
-        blocks[4] = pltpu.roll(blocks[0], lanes - 1, 1)
         plane = (2.0 * cur_ref[rows] - fol_ref[rows]) - minv_ref[rows] * jnp.concatenate(
             blocks, axis=0
         )
@@ -581,8 +587,8 @@
 
 
 def patch_kernel(*refs, pair, steps):
-    mask_ref, weight_ref, grad_ref, table_ref, _, _, _, up_ref = refs[:8]
-    down_ref = None if pair else refs[8]
+    mask_ref, weight_ref, grad_ref, table_ref, _, up_ref = refs[:6]
+    down_ref = None if pair else refs[6]
     home_out, out_a, out_b, out_c, out_d = refs[-5:]
     place = lax.axis_index("dom")
     slip = fault_input(up_ref, down_ref, 32)
@@ -686,32 +692,25 @@
         odd_in = swapped(odd, 1, 1)
         return swapped(even, 1, 0), odd_in, faults
 
-    cur, even, odd, fault_rows, material, edge_table = kernel_call(
+    tables = (edge_table, own_table, far_table, touch_table)
+    cur, even, odd, fault_rows, material, edge_table, own_table, far_table, touch_table = kernel_call(
         first_kernel,
-        [
-            field, plane, plane, (32 + 4 * steps, lanes), (8, lanes),
-            (edge_table.shape, edge_table.dtype),
-        ],
-        (
-            now, flags, weak_slope[0], lame_first[0], shear_modulus[0], edge_table,
-        ),
-        (),
-        [native],
-        range(6),
-        (5,),
+        [field, plane, plane, (32 + 4 * steps, lanes), (8, lanes)]
+        + [(t.shape, t.dtype) for t in tables],
+        (now, flags, weak_slope[0], lame_first[0], shear_modulus[0]) + tables,
+        scratch=[native],
+        in_hbm=range(9),
+        kept=range(5, 9),
     )
     first_fault = fault_rows
     even_in, odd_in, fault_in = exchange(even, odd, fault_rows)
     first_in = fault_in
-    tables = (own_table, far_table, touch_table, back)
-    fol, minv, weight, own_table, far_table, touch_table, back = kernel_call(
+    fol, minv, weight = kernel_call(
         setup_kernel,
-        [field, field, (4 * steps, lanes)] + [(t.shape, t.dtype) for t in tables],
-        (following, rho, flags, normal_stress[0], mass) + tables,
-        (),
-        [native],
-        range(9),
-        range(5, 9),
+        [field, field, (4 * steps, lanes)],
+        (following, rho, flags, normal_stress[0], mass),
+        scratch=[native],
+        in_hbm=range(5),
         y_elems=y_elems,
         z_elems=z_elems,
     )
@@ -725,8 +724,8 @@
             [cur, material, own_table, touch_table],
             (),
         )
-        args = [cur, fol, minv, base, touch, material, even_in, odd_in] + fault_in
-        args += [first_in[0], fault_rows, first_fault, far_table, edge_table]
+        args = [cur, fol, minv, base, touch, material, odd_in] + fault_in
+        args += [even_in, first_in[0], fault_rows, first_fault, far_table, edge_table]
         static = dict(
             step=step, last=last, extra=1 if last or step == 1 else 0, last_place=lax.axis_size("dom") - 1, pair=pair, y_elems=y_elems,
             z_elems=z_elems,
@@ -761,8 +760,8 @@
             sums = kernel_call(
                 patch_kernel,
                 [(PATCH_DEV, lanes)] * 5,
-                [mask, weight, grad, table, even_in, odd_in, touch] + fault_in,
-                unread=(4, 5, 6),
+                [mask, weight, grad, table, odd_in] + fault_in + [even_in, touch],
+                unread=(4, 5 + len(fault_in), 6 + len(fault_in)),
                 pair=pair,
                 steps=steps,
             )

time: 33.5 us -> 35.2 us (1.051)
  starting transfers between devices: 13.7 us -> 18.1 us
  waiting for transfers between devices: 6.13 us -> 3.41 us
  local copies, waits for them, and re-layouts: 0.14 us -> 0.66 us
  Pallas kernels: 12 us -> 11.5 us
    ppermute x4, waiting for transfers between devices: 6.1 us -> 3.29 us  [from_behind(): lax.ppermute(block, axis, [((i - distance) % size, i) for i in range(size)])]
    ppermute x4, starting transfers between devices: 3.57 us -> 5.97 us  [from_behind(): lax.ppermute(block, axis, [((i - distance) % size, i) for i in range(size)])]
    ppermute x12, starting transfers between devices: 10.2 us -> 12.2 us  [swapped(): return lax.ppermute(block, ('dom', 'depth'), route)]
    pallas_call x13, Pallas kernels: 12 us -> 11.5 us  [kernel_call(): pl.pallas_call(functools.partial(body, **static) if static else body, out...]
    unnamed x2 -> x4, local copies, waits for them, and re-layouts: 0.14 us -> 0.66 us
  transfers between devices with their start and end apart: 16 -> 16, of which waited for: 4 -> 5; matrix products, arithmetic and copies ran while one was open for 0% -> 0% of each run, Pallas kernels for 20% -> 19%
where the time goes in v4:
time: 35.2 us; the launch traced here: 34.9 us
  starting transfers between devices  18.1 us (51%)
  Pallas kernels  11.5 us (33%)
  waiting for transfers between devices  3.41 us (10%)
  between operations  0.69 us (2%)
  local copies, waits for them, and re-layouts  0.66 us (2%)
  other arithmetic  0.57 us (2%)
    ppermute x12, starting transfers between devices, swapped(): return lax.ppermute(block, ('dom', 'depth'), route)  12.2 us
    pallas_call x13, Pallas kernels, kernel_call(): pl.pallas_call(functools.partial(body, **static) if static else body, out...  11.5 us
    ppermute x4, starting transfers between devices, from_behind(): lax.ppermute(block, axis, [((i - distance) % size, i) for i in range(size)])  5.97 us
    ppermute x4, waiting for transfers between devices, from_behind(): lax.ppermute(block, axis, [((i - distance) % size, i) for i in range(size)])  3.29 us
  transfers between devices with their start and end apart: 16, of which 5 were waited for; matrix products, arithmetic and copies ran while one was open for 0% of the time, Pallas kernels for 19%

profile of v4, /device:TPU:0, one launch (start us, length us, event | category | flops | bytes accessed | tf_op | source)
XLA Modules:
  0.0 34.9 jit_solution(11597990752200204111)
XLA Ops:
  0.6 2.0 %shard_map.166 = (f32[320,128]{1,0:T(8,128)S(1)}, f32[64,128]{1,0:T(8,128)S(1)}, f32[64,128]{1,0:T(8,128)S(1)}, f32[48,128]{1,0:T(8,128)S(1)}, f32[8,128]{1,0:T(...) custom-call(f32[3,17,4,128]{3,2,1,0:T(4,128)} %bitcast.12, ...), custom_call_target="tpu_custom_call" | custom-call | tf_op jit(solution)/shard_map/pallas_call | solution.py:629
  2.6 3.0 %collective-permute-start = (f32[64,128]{1,0:T(8,128)S(1)}, f32[64,128]{1,0:T(8,128)S(1)}, u32[]{:S(2)}, u32[]{:S(2)}) collective-permute-start(f32[64,128]{1,0:T(8,128)S(1)} %get-tuple-element.51), channel_id=1, source_target_pairs={{0,1},{1,0},{2,4},{3,5},{4,2},{5,3},{6,8},{7,9},{8,6},{9,7},{10,12... | collective-permute-start | bytes 98312 | tf_op jit(solution)/shard_map/ppermute | solution.py:652
  5.8 1.5 %collective-permute-start.1 = (f32[48,128]{1,0:T(8,128)S(1)}, f32[48,128]{1,0:T(8,128)S(1)}, u32[]{:S(2)}, u32[]{:S(2)}) collective-permute-start(f32[48,128]{1,0:T(8,128)S(1)} %get-tuple-element.52.refs_10_.refs_11_.refs_3_), channel_id=1, source_target_pairs={{1,0},{0,1},{3,2},{2,3},{5,4},{4,5},{7,6},{6,7},{9,8},{8,9},{11,10... | collective-permute-start | bytes 73736 | tf_op jit(solution)/shard_map/ppermute | solution.py:657
  7.3 1.6 %shard_map.167 = (f32[320,128]{1,0:T(8,128)S(1)}, f32[320,128]{1,0:T(8,128)S(1)}, f32[16,128]{1,0:T(8,128)S(1)}) custom-call(f32[3,17,4,128]{3,2,1,0:T(4,128)} %bitcast.13, f32[17,4,128]{2,1,0:T(4,128)} %bitcast.15, s32[4,4,128]{2,1,0:T(4,128)} %bitcast.17, f32[4,128]{1,0:T(4,128)} %bitcast.21, f32[320,128]{1,0:T(8,128)} %constant.17.clone.mass_hbm), custom_call_target="tpu_custom_call" | custom-call | tf_op jit(solution)/shard_map/pallas_call | solution.py:629
  9.6 1.0 %shard_map.169 = (f32[320,128]{1,0:T(8,128)S(1)}, f32[64,128]{1,0:T(8,128)S(1)}, f32[64,128]{1,0:T(8,128)S(1)}, f32[32,128]{1,0:T(8,128)S(1)}) custom-call(f32[320,128]{1,0:T(8,128)S(1)} %get-tuple-element.43.cur_ref.refs_0_.refs_1_, f32[320,128]{1,0:T(8,128)S(1)} %get-tuple-element.44.refs_1_, f32[320,128]{1,0:T(8,128)S(1)} %get-tuple-element.45.refs_2_, ...), custom_call_target="tpu_custom_call" | custom-call | tf_op jit(solution)/shard_map/pallas_call | solution.py:629
  10.6 1.5 %collective-permute-start.3 = (f32[64,128]{1,0:T(8,128)S(1)}, f32[64,128]{1,0:T(8,128)S(1)}, u32[]{:S(2)}, u32[]{:S(2)}) collective-permute-start(f32[64,128]{1,0:T(8,128)S(1)} %get-tuple-element.59), channel_id=1, source_target_pairs={{0,1},{1,0},{2,4},{3,5},{4,2},{5,3},{6,8},{7,9},{8,6},{9,7},{10,12... | collective-permute-start | bytes 98312 | tf_op jit(solution)/shard_map/ppermute | solution.py:652
  12.2 1.5 %collective-permute-start.4 = (f32[32,128]{1,0:T(8,128)S(1)}, f32[32,128]{1,0:T(8,128)S(1)}, u32[]{:S(2)}, u32[]{:S(2)}) collective-permute-start(f32[32,128]{1,0:T(8,128)S(1)} %get-tuple-element.60.refs_10_.refs_5_), channel_id=1, source_target_pairs={{1,0},{0,1},{3,2},{2,3},{5,4},{4,5},{7,6},{6,7},{9,8},{8,9},{11,10... | collective-permute-start | bytes 49160 | tf_op jit(solution)/shard_map/ppermute | solution.py:657
  14.3 0.6 %shard_map.171.refs_14_.refs_0_ = f32[64,128]{1,0:T(8,128)S(1)} custom-call(s32[1,4]{1,0:T(1,128)S(1)} %copy-done.1, f32[320,128]{1,0:T(8,128)S(1)} %get-tuple-element.56.cur_ref._.refs_0_.refs_1_), custom_call_target="tpu_custom_call" | custom-call | tf_op jit(solution)/shard_map/pallas_call | solution.py:629
  14.9 1.0 %collective-permute-done.4.refs_7_.refs_6_ = f32[32,128]{1,0:T(8,128)S(1)} collective-permute-done((f32[32,128]{1,0:T(8,128)S(1)}, f32[32,128]{1,0:T(8,128)S(1)}, u32[]{:S(2)}, u32[]{:S(2)}) %collective-permute-start.4) | collective-permute-done | bytes 16416 | tf_op jit(solution)/shard_map/ppermute | solution.py:657
  15.9 1.0 %shard_map.172 = (f32[320,128]{1,0:T(8,128)S(1)}, f32[64,128]{1,0:T(8,128)S(1)}, f32[64,128]{1,0:T(8,128)S(1)}, f32[32,128]{1,0:T(8,128)S(1)}) custom-call(f32[320,128]{1,0:T(8,128)S(1)} %get-tuple-element.56.cur_ref._.refs_0_.refs_1_, f32[320,128]{1,0:T(8,128)S(1)} %get-tuple-element.43.cur_ref.refs_0_.refs_1_, f32[320,128]{1,0:T(8,128)S(1)} %get-tuple-element.45.refs_2_, ...), custom_call_target="tpu_custom_call" | custom-call | tf_op jit(solution)/shard_map/pallas_call | solution.py:629
  16.9 1.5 %collective-permute-start.6 = (f32[64,128]{1,0:T(8,128)S(1)}, f32[64,128]{1,0:T(8,128)S(1)}, u32[]{:S(2)}, u32[]{:S(2)}) collective-permute-start(f32[64,128]{1,0:T(8,128)S(1)} %get-tuple-element.65), channel_id=1, source_target_pairs={{0,1},{1,0},{2,4},{3,5},{4,2},{5,3},{6,8},{7,9},{8,6},{9,7},{10,12... | collective-permute-start | bytes 98312 | tf_op jit(solution)/shard_map/ppermute | solution.py:652
  18.5 1.5 %collective-permute-start.7 = (f32[32,128]{1,0:T(8,128)S(1)}, f32[32,128]{1,0:T(8,128)S(1)}, u32[]{:S(2)}, u32[]{:S(2)}) collective-permute-start(f32[32,128]{1,0:T(8,128)S(1)} %get-tuple-element.66.refs_10_.refs_7_), channel_id=1, source_target_pairs={{1,0},{0,1},{3,2},{2,3},{5,4},{4,5},{7,6},{6,7},{9,8},{8,9},{11,10... | collective-permute-start | bytes 49160 | tf_op jit(solution)/shard_map/ppermute | solution.py:657
  20.5 1.8 %collective-permute-done.7.refs_7_.refs_8_ = f32[32,128]{1,0:T(8,128)S(1)} collective-permute-done((f32[32,128]{1,0:T(8,128)S(1)}, f32[32,128]{1,0:T(8,128)S(1)}, u32[]{:S(2)}, u32[]{:S(2)}) %collective-permute-start.7) | collective-permute-done | bytes 16416 | tf_op jit(solution)/shard_map/ppermute | solution.py:657
  22.3 0.9 %shard_map.174 = (f32[320,128]{1,0:T(8,128)S(1)}, f32[64,128]{1,0:T(8,128)S(1)}, f32[64,128]{1,0:T(8,128)S(1)}, f32[32,128]{1,0:T(8,128)S(1)}) custom-call(f32[320,128]{1,0:T(8,128)S(1)} %get-tuple-element.62.cur_ref.refs_0_.refs_1_, f32[320,128]{1,0:T(8,128)S(1)} %get-tuple-element.56.cur_ref._.refs_0_.refs_1_, f32[320,128]{1,0:T(8,128)S(1)} %get-tuple-element.45.refs_2_, ...), custom_call_target="tpu_custom_call" | custom-call | tf_op jit(solution)/shard_map/pallas_call | solution.py:629
  23.2 1.5 %collective-permute-start.9 = (f32[64,128]{1,0:T(8,128)S(1)}, f32[64,128]{1,0:T(8,128)S(1)}, u32[]{:S(2)}, u32[]{:S(2)}) collective-permute-start(f32[64,128]{1,0:T(8,128)S(1)} %get-tuple-element.71), channel_id=1, source_target_pairs={{0,1},{1,0},{2,4},{3,5},{4,2},{5,3},{6,8},{7,9},{8,6},{9,7},{10,12... | collective-permute-start | bytes 98312 | tf_op jit(solution)/shard_map/ppermute | solution.py:652
  24.9 1.5 %collective-permute-start.10 = (f32[32,128]{1,0:T(8,128)S(1)}, f32[32,128]{1,0:T(8,128)S(1)}, u32[]{:S(2)}, u32[]{:S(2)}) collective-permute-start(f32[32,128]{1,0:T(8,128)S(1)} %get-tuple-element.72.refs_9_.refs_10_), channel_id=1, source_target_pairs={{1,0},{0,1},{3,2},{2,3},{5,4},{4,5},{7,6},{6,7},{9,8},{8,9},{11,10... | collective-permute-start | bytes 49160 | tf_op jit(solution)/shard_map/ppermute | solution.py:657
  26.9 0.5 %copy-done = bf16[512,512]{1,0:T(8,128)(2,1)S(1)} copy-done((bf16[512,512]{1,0:T(8,128)(2,1)S(1)}, bf16[512,512]{1,0:T(8,128)(2,1)}, u32[]{:S(2)}) %copy-start) | copy-done | bytes 524312
  27.4 1.0 %shard_map.176 = (f32[3,17,4,128]{3,2,1,0:T(4,128)}, f32[32,128]{1,0:T(8,128)S(1)}, bf16[128,128]{1,0:T(8,128)(2,1)S(1)}) custom-call(f32[320,128]{1,0:T(8,128)S(1)} %get-tuple-element.68.cur_ref.refs_0_, bf16[512,512]{1,0:T(8,128)(2,1)S(1)} %copy-done, f32[16,128]{1,0:T(8,128)S(1)} %get-tuple-element.74.refs_2_.refs_1_, ...), custom_call_target="tpu_custom_call" | custom-call | tf_op jit(solution)/shard_map/pallas_call | solution.py:629
  28.8 1.5 %collective-permute-start.12 = (f32[2,128]{1,0:T(2,128)S(1)}, f32[2,128]{1,0:T(2,128)S(1)}, u32[]{:S(2)}, u32[]{:S(2)}) collective-permute-start(f32[2,128]{1,0:T(2,128)S(1)} %get-tuple-element.79), channel_id=1, source_target_pairs={{0,1},{1,0},{2,4},{3,5},{4,2},{5,3},{6,8},{7,9},{8,6},{9,7},{10,12... | collective-permute-start | bytes 3080 | tf_op jit(solution)/shard_map/ppermute | solution.py:652
  30.3 0.5 %collective-permute-start.13 = (f32[2,128]{1,0:T(2,128)S(1)}, f32[2,128]{1,0:T(2,128)S(1)}, u32[]{:S(2)}, u32[]{:S(2)}) collective-permute-start(f32[2,128]{1,0:T(2,128)S(1)} %get-tuple-element.80), channel_id=1, source_target_pairs={{0,1},{1,0},{2,3},{3,2},{4,8},{5,9},{6,10},{7,11},{8,4},{9,5},{10,... | collective-permute-start | bytes 3080 | tf_op jit(solution)/shard_map/ppermute | solution.py:652
  30.8 1.5 %collective-permute-start.14 = (f32[2,128]{1,0:T(2,128)S(1)}, f32[2,128]{1,0:T(2,128)S(1)}, u32[]{:S(2)}, u32[]{:S(2)}) collective-permute-start(f32[2,128]{1,0:T(2,128)S(1)} %get-tuple-element.81), channel_id=1, source_target_pairs={{0,4},{1,5},{2,6},{3,7},{4,0},{5,1},{6,2},{7,3},{8,12},{9,13},{10,... | collective-permute-start | bytes 3080 | tf_op jit(solution)/shard_map/ppermute | solution.py:652
  32.3 0.6 %collective-permute-start.15 = (f32[2,128]{1,0:T(2,128)S(1)}, f32[2,128]{1,0:T(2,128)S(1)}, u32[]{:S(2)}, u32[]{:S(2)}) collective-permute-start(f32[2,128]{1,0:T(2,128)S(1)} %get-tuple-element.82), channel_id=1, source_target_pairs={{0,2},{1,3},{2,0},{3,1},{4,6},{5,7},{6,4},{7,5},{8,10},{9,11},{10,... | collective-permute-start | bytes 3080 | tf_op jit(solution)/shard_map/ppermute | solution.py:652
  32.9 1.4 %shard_map.178 = f32[3,17,4,128]{3,2,1,0:T(4,128)} custom-call(f32[320,128]{1,0:T(8,128)S(1)} %get-tuple-element.68.cur_ref.refs_0_, f32[320,128]{1,0:T(8,128)S(1)} %get-tuple-element.62.cur_ref.refs_0_.refs_1_, f32[320,128]{1,0:T(8,128)S(1)} %get-tuple-element.45.refs_2_, f32[320,128]{1,0:T(8,128)S(1)} %get-tuple-element.69.refs_3_, ...), custom_call_target="tpu_custom_call" | custom-call | tf_op jit(solution)/shard_map/pallas_call | solution.py:629
  34.4 0.6 %add_bitcast_fusion = f32[1,2,128]{2,1,0:T(2,128)} fusion(f32[2,128]{1,0:T(2,128)S(1)} %collective-permute-done.15, f32[2,128]{1,0:T(2,128)S(1)} %collective-permute-done.14, f32[2,128]{1,0:T(2,128)S(1)} %collective-permute-done.13, f32[2,128]{1,0:T(2,128)S(1)} %get-tuple-element.77.refs_14_, f32[2,128]{1,0:T(2,128)S(1)} %collective-permute-done.12), kind=kLoop, calls=%fused_computation | loop fusion | flops 1024 | bytes 6144 | tf_op jit(solution)/shard_map/broadcast_in_dim | solution.py:782
  (26 shorter events, 3.5 us)
Async XLA Ops:
  2.6 7.0 %collective-permute-start = (f32[64,128]{1,0:T(8,128)S(1)}, f32[64,128]{1,0:T(8,128)S(1)}, u32[]{:S(2)}, u32[]{:S(2)}) collective-permute-start(f32[64,128]{1,0:T(8,128)S(1)} %get-tuple-element.51), channel_id=1, source_target_pairs={{0,1},{1,0},{2,4},{3,5},{4,2},{5,3},{6,8},{7,9},{8,6},{9,7},{10,12... | collective-permute-start | bytes 98312 | tf_op jit(solution)/shard_map/ppermute | solution.py:652
  5.6 4.0 %collective-permute-start.2 = (f32[64,128]{1,0:T(8,128)S(1)}, f32[64,128]{1,0:T(8,128)S(1)}, u32[]{:S(2)}, u32[]{:S(2)}) collective-permute-start(f32[64,128]{1,0:T(8,128)S(1)} %get-tuple-element.53), channel_id=1, source_target_pairs={{0,2},{1,3},{2,0},{3,1},{4,6},{5,7},{6,4},{7,5},{8,10},{9,11},{10,... | collective-permute-start | bytes 98312 | tf_op jit(solution)/shard_map/ppermute | solution.py:652
  5.8 3.8 %collective-permute-start.1 = (f32[48,128]{1,0:T(8,128)S(1)}, f32[48,128]{1,0:T(8,128)S(1)}, u32[]{:S(2)}, u32[]{:S(2)}) collective-permute-start(f32[48,128]{1,0:T(8,128)S(1)} %get-tuple-element.52.refs_10_.refs_11_.refs_3_), channel_id=1, source_target_pairs={{1,0},{0,1},{3,2},{2,3},{5,4},{4,5},{7,6},{6,7},{9,8},{8,9},{11,10... | collective-permute-start | bytes 73736 | tf_op jit(solution)/shard_map/ppermute | solution.py:657
  10.6 5.4 %collective-permute-start.3 = (f32[64,128]{1,0:T(8,128)S(1)}, f32[64,128]{1,0:T(8,128)S(1)}, u32[]{:S(2)}, u32[]{:S(2)}) collective-permute-start(f32[64,128]{1,0:T(8,128)S(1)} %get-tuple-element.59), channel_id=1, source_target_pairs={{0,1},{1,0},{2,4},{3,5},{4,2},{5,3},{6,8},{7,9},{8,6},{9,7},{10,12... | collective-permute-start | bytes 98312 | tf_op jit(solution)/shard_map/ppermute | solution.py:652
  12.0 3.9 %collective-permute-start.5 = (f32[64,128]{1,0:T(8,128)S(1)}, f32[64,128]{1,0:T(8,128)S(1)}, u32[]{:S(2)}, u32[]{:S(2)}) collective-permute-start(f32[64,128]{1,0:T(8,128)S(1)} %get-tuple-element.61), channel_id=1, source_target_pairs={{0,2},{1,3},{2,0},{3,1},{4,6},{5,7},{6,4},{7,5},{8,10},{9,11},{10,... | collective-permute-start | bytes 98312 | tf_op jit(solution)/shard_map/ppermute | solution.py:652
  12.2 3.8 %collective-permute-start.4 = (f32[32,128]{1,0:T(8,128)S(1)}, f32[32,128]{1,0:T(8,128)S(1)}, u32[]{:S(2)}, u32[]{:S(2)}) collective-permute-start(f32[32,128]{1,0:T(8,128)S(1)} %get-tuple-element.60.refs_10_.refs_5_), channel_id=1, source_target_pairs={{1,0},{0,1},{3,2},{2,3},{5,4},{4,5},{7,6},{6,7},{9,8},{8,9},{11,10... | collective-permute-start | bytes 49160 | tf_op jit(solution)/shard_map/ppermute | solution.py:657
  13.7 0.7 %copy-start.1 = (s32[1,4]{1,0:T(1,128)S(1)}, s32[1,4]{1,0:T(1,128)}, u32[]{:S(2)}) copy-start(s32[1,4]{1,0:T(1,128)} %owner_ref.1) | copy-start | bytes 52
  16.9 5.4 %collective-permute-start.6 = (f32[64,128]{1,0:T(8,128)S(1)}, f32[64,128]{1,0:T(8,128)S(1)}, u32[]{:S(2)}, u32[]{:S(2)}) collective-permute-start(f32[64,128]{1,0:T(8,128)S(1)} %get-tuple-element.65), channel_id=1, source_target_pairs={{0,1},{1,0},{2,4},{3,5},{4,2},{5,3},{6,8},{7,9},{8,6},{9,7},{10,12... | collective-permute-start | bytes 98312 | tf_op jit(solution)/shard_map/ppermute | solution.py:652
  18.4 3.9 %collective-permute-start.8 = (f32[64,128]{1,0:T(8,128)S(1)}, f32[64,128]{1,0:T(8,128)S(1)}, u32[]{:S(2)}, u32[]{:S(2)}) collective-permute-start(f32[64,128]{1,0:T(8,128)S(1)} %get-tuple-element.67), channel_id=1, source_target_pairs={{0,2},{1,3},{2,0},{3,1},{4,6},{5,7},{6,4},{7,5},{8,10},{9,11},{10,... | collective-permute-start | bytes 98312 | tf_op jit(solution)/shard_map/ppermute | solution.py:652
  18.5 3.8 %collective-permute-start.7 = (f32[32,128]{1,0:T(8,128)S(1)}, f32[32,128]{1,0:T(8,128)S(1)}, u32[]{:S(2)}, u32[]{:S(2)}) collective-permute-start(f32[32,128]{1,0:T(8,128)S(1)} %get-tuple-element.66.refs_10_.refs_7_), channel_id=1, source_target_pairs={{1,0},{0,1},{3,2},{2,3},{5,4},{4,5},{7,6},{6,7},{9,8},{8,9},{11,10... | collective-permute-start | bytes 49160 | tf_op jit(solution)/shard_map/ppermute | solution.py:657
  23.2 5.4 %collective-permute-start.9 = (f32[64,128]{1,0:T(8,128)S(1)}, f32[64,128]{1,0:T(8,128)S(1)}, u32[]{:S(2)}, u32[]{:S(2)}) collective-permute-start(f32[64,128]{1,0:T(8,128)S(1)} %get-tuple-element.71), channel_id=1, source_target_pairs={{0,1},{1,0},{2,4},{3,5},{4,2},{5,3},{6,8},{7,9},{8,6},{9,7},{10,12... | collective-permute-start | bytes 98312 | tf_op jit(solution)/shard_map/ppermute | solution.py:652
  24.7 3.9 %collective-permute-start.11 = (f32[64,128]{1,0:T(8,128)S(1)}, f32[64,128]{1,0:T(8,128)S(1)}, u32[]{:S(2)}, u32[]{:S(2)}) collective-permute-start(f32[64,128]{1,0:T(8,128)S(1)} %get-tuple-element.73), channel_id=1, source_target_pairs={{0,2},{1,3},{2,0},{3,1},{4,6},{5,7},{6,4},{7,5},{8,10},{9,11},{10,... | collective-permute-start | bytes 98312 | tf_op jit(solution)/shard_map/ppermute | solution.py:652
  24.9 3.8 %collective-permute-start.10 = (f32[32,128]{1,0:T(8,128)S(1)}, f32[32,128]{1,0:T(8,128)S(1)}, u32[]{:S(2)}, u32[]{:S(2)}) collective-permute-start(f32[32,128]{1,0:T(8,128)S(1)} %get-tuple-element.72.refs_9_.refs_10_), channel_id=1, source_target_pairs={{1,0},{0,1},{3,2},{2,3},{5,4},{4,5},{7,6},{6,7},{9,8},{8,9},{11,10... | collective-permute-start | bytes 49160 | tf_op jit(solution)/shard_map/ppermute | solution.py:657
  26.4 1.0 %copy-start = (bf16[512,512]{1,0:T(8,128)(2,1)S(1)}, bf16[512,512]{1,0:T(8,128)(2,1)}, u32[]{:S(2)}) copy-start(bf16[512,512]{1,0:T(8,128)(2,1)} %constant.16.clone.refs_1_.refs_15_) | copy-start | bytes 1572868
  28.8 5.5 %collective-permute-start.12 = (f32[2,128]{1,0:T(2,128)S(1)}, f32[2,128]{1,0:T(2,128)S(1)}, u32[]{:S(2)}, u32[]{:S(2)}) collective-permute-start(f32[2,128]{1,0:T(2,128)S(1)} %get-tuple-element.79), channel_id=1, source_target_pairs={{0,1},{1,0},{2,4},{3,5},{4,2},{5,3},{6,8},{7,9},{8,6},{9,7},{10,12... | collective-permute-start | bytes 3080 | tf_op jit(solution)/shard_map/ppermute | solution.py:652
  30.3 4.0 %collective-permute-start.13 = (f32[2,128]{1,0:T(2,128)S(1)}, f32[2,128]{1,0:T(2,128)S(1)}, u32[]{:S(2)}, u32[]{:S(2)}) collective-permute-start(f32[2,128]{1,0:T(2,128)S(1)} %get-tuple-element.80), channel_id=1, source_target_pairs={{0,1},{1,0},{2,3},{3,2},{4,8},{5,9},{6,10},{7,11},{8,4},{9,5},{10,... | collective-permute-start | bytes 3080 | tf_op jit(solution)/shard_map/ppermute | solution.py:652
  30.8 3.6 %collective-permute-start.14 = (f32[2,128]{1,0:T(2,128)S(1)}, f32[2,128]{1,0:T(2,128)S(1)}, u32[]{:S(2)}, u32[]{:S(2)}) collective-permute-start(f32[2,128]{1,0:T(2,128)S(1)} %get-tuple-element.81), channel_id=1, source_target_pairs={{0,4},{1,5},{2,6},{3,7},{4,0},{5,1},{6,2},{7,3},{8,12},{9,13},{10,... | collective-permute-start | bytes 3080 | tf_op jit(solution)/shard_map/ppermute | solution.py:652
  32.3 2.1 %collective-permute-start.15 = (f32[2,128]{1,0:T(2,128)S(1)}, f32[2,128]{1,0:T(2,128)S(1)}, u32[]{:S(2)}, u32[]{:S(2)}) collective-permute-start(f32[2,128]{1,0:T(2,128)S(1)} %get-tuple-element.82), channel_id=1, source_target_pairs={{0,2},{1,3},{2,0},{3,1},{4,6},{5,7},{6,4},{7,5},{8,10},{9,11},{10,... | collective-permute-start | bytes 3080 | tf_op jit(solution)/shard_map/ppermute | solution.py:652

commit v5 on v4

--- a/solution.py
+++ b/solution.py
@@ -472,10 +472,10 @@
 
 
 def step_kernel(*refs, step, last, extra, last_place, pair, y_elems, z_elems):
-    cur_ref, fol_ref, minv_ref, base_ref, touch_ref, material_ref, odd_ref, up_ref = refs[:8]
+    cur_ref, fol_ref, minv_ref, base_ref, touch_ref, material_ref, even_ref, odd_ref = refs[:8]
     refs = list(refs[8:])
+    up_ref = refs.pop(0)
     down_ref = None if pair else refs.pop(0)
-    even_ref = refs.pop(0)
     first_up_ref, own_ref, first_own_ref, far_ref, edge_ref = refs[:5]
     refs = refs[5 + extra :]
     if last:
@@ -587,8 +587,8 @@
 
 
 def patch_kernel(*refs, pair, steps):
-    mask_ref, weight_ref, grad_ref, table_ref, _, up_ref = refs[:6]
-    down_ref = None if pair else refs[6]
+    mask_ref, weight_ref, grad_ref, table_ref, _, _, _, up_ref = refs[:8]
+    down_ref = None if pair else refs[8]
     home_out, out_a, out_b, out_c, out_d = refs[-5:]
     place = lax.axis_index("dom")
     slip = fault_input(up_ref, down_ref, 32)
@@ -689,8 +689,7 @@
             faults = [from_behind(fault_rows, "depth", 1)]
         else:
             faults = [from_behind(fault_rows, "depth", 1), from_behind(fault_rows, "depth", -1)]
-        odd_in = swapped(odd, 1, 1)
-        return swapped(even, 1, 0), odd_in, faults
+        return swapped(even, 1, 0), swapped(odd, 1, 1), faults
 
     tables = (edge_table, own_table, far_table, touch_table)
     cur, even, odd, fault_rows, material, edge_table, own_table, far_table, touch_table = kernel_call(
@@ -724,8 +723,8 @@
             [cur, material, own_table, touch_table],
             (),
         )
-        args = [cur, fol, minv, base, touch, material, odd_in] + fault_in
-        args += [even_in, first_in[0], fault_rows, first_fault, far_table, edge_table]
+        args = [cur, fol, minv, base, touch, material, even_in, odd_in] + fault_in
+        args += [first_in[0], fault_rows, first_fault, far_table, edge_table]
         static = dict(
             step=step, last=last, extra=1 if last or step == 1 else 0, last_place=lax.axis_size("dom") - 1, pair=pair, y_elems=y_elems,
             z_elems=z_elems,
@@ -760,8 +759,8 @@
             sums = kernel_call(
                 patch_kernel,
                 [(PATCH_DEV, lanes)] * 5,
-                [mask, weight, grad, table, odd_in] + fault_in + [even_in, touch],
-                unread=(4, 5 + len(fault_in), 6 + len(fault_in)),
+                [mask, weight, grad, table, even_in, odd_in, touch] + fault_in,
+                unread=(4, 5, 6),
                 pair=pair,
                 steps=steps,
             )

time: 35.2 us -> 33.1 us (0.940)
  starting transfers between devices: 18.1 us -> 13.7 us
  waiting for transfers between devices: 3.41 us -> 5.82 us
    ppermute x4, waiting for transfers between devices: 3.29 us -> 5.73 us  [from_behind(): lax.ppermute(block, axis, [((i - distance) % size, i) for i in range(size)])]
    ppermute x4, starting transfers between devices: 5.97 us -> 3.59 us  [from_behind(): lax.ppermute(block, axis, [((i - distance) % size, i) for i in range(size)])]
    ppermute x12, starting transfers between devices: 12.2 us -> 10.1 us  [swapped(): return lax.ppermute(block, ('dom', 'depth'), route)]
  transfers between devices with their start and end apart: 16 -> 16, of which waited for: 5 -> 5; matrix products, arithmetic and copies ran while one was open for 0% -> 0% of each run, Pallas kernels for 19% -> 20%
where the time goes in v5:
time: 33.1 us; the launch traced here: 32.9 us
  starting transfers between devices  13.7 us (41%)
  Pallas kernels  11.5 us (35%)
  waiting for transfers between devices  5.82 us (18%)
  between operations  0.71 us (2%)
  local copies, waits for them, and re-layouts  0.67 us (2%)
  other arithmetic  0.57 us (2%)
    pallas_call x13, Pallas kernels, kernel_call(): pl.pallas_call(functools.partial(body, **static) if static else body, out...  11.5 us
    ppermute x12, starting transfers between devices, swapped(): return lax.ppermute(block, ('dom', 'depth'), route)  10.1 us
    ppermute x4, waiting for transfers between devices, from_behind(): lax.ppermute(block, axis, [((i - distance) % size, i) for i in range(size)])  5.73 us
    ppermute x4, starting transfers between devices, from_behind(): lax.ppermute(block, axis, [((i - distance) % size, i) for i in range(size)])  3.59 us
    unnamed x4, local copies, waits for them, and re-layouts  0.67 us
  transfers between devices with their start and end apart: 16, of which 5 were waited for; matrix products, arithmetic and copies ran while one was open for 0% of the time, Pallas kernels for 20%

profile of v5, /device:TPU:0, one launch (start us, length us, event | category | flops | bytes accessed | tf_op | source)
XLA Modules:
  0.0 32.9 jit_solution(4957692896766264821)
XLA Ops:
  0.6 2.0 %shard_map.166 = (f32[320,128]{1,0:T(8,128)S(1)}, f32[64,128]{1,0:T(8,128)S(1)}, f32[64,128]{1,0:T(8,128)S(1)}, f32[48,128]{1,0:T(8,128)S(1)}, f32[8,128]{1,0:T(...) custom-call(f32[3,17,4,128]{3,2,1,0:T(4,128)} %bitcast.12, ...), custom_call_target="tpu_custom_call" | custom-call | tf_op jit(solution)/shard_map/pallas_call | solution.py:629
  2.6 0.5 %collective-permute-start = (f32[64,128]{1,0:T(8,128)S(1)}, f32[64,128]{1,0:T(8,128)S(1)}, u32[]{:S(2)}, u32[]{:S(2)}) collective-permute-start(f32[64,128]{1,0:T(8,128)S(1)} %get-tuple-element.51), channel_id=1, source_target_pairs={{0,2},{1,3},{2,0},{3,1},{4,6},{5,7},{6,4},{7,5},{8,10},{9,11},{10,... | collective-permute-start | bytes 98312 | tf_op jit(solution)/shard_map/ppermute | solution.py:652
  3.1 2.6 %collective-permute-start.1 = (f32[64,128]{1,0:T(8,128)S(1)}, f32[64,128]{1,0:T(8,128)S(1)}, u32[]{:S(2)}, u32[]{:S(2)}) collective-permute-start(f32[64,128]{1,0:T(8,128)S(1)} %get-tuple-element.52), channel_id=1, source_target_pairs={{0,1},{1,0},{2,4},{3,5},{4,2},{5,3},{6,8},{7,9},{8,6},{9,7},{10,12... | collective-permute-start | bytes 98312 | tf_op jit(solution)/shard_map/ppermute | solution.py:652
  5.8 1.6 %shard_map.167 = (f32[320,128]{1,0:T(8,128)S(1)}, f32[320,128]{1,0:T(8,128)S(1)}, f32[16,128]{1,0:T(8,128)S(1)}) custom-call(f32[3,17,4,128]{3,2,1,0:T(4,128)} %bitcast.13, f32[17,4,128]{2,1,0:T(4,128)} %bitcast.15, s32[4,4,128]{2,1,0:T(4,128)} %bitcast.17, f32[4,128]{1,0:T(4,128)} %bitcast.21, f32[320,128]{1,0:T(8,128)} %constant.17.clone.mass_hbm), custom_call_target="tpu_custom_call" | custom-call | tf_op jit(solution)/shard_map/pallas_call | solution.py:629
  7.9 1.7 %collective-permute-done.2.refs_8_.refs_9_.refs_4_ = f32[48,128]{1,0:T(8,128)S(1)} collective-permute-done((f32[48,128]{1,0:T(8,128)S(1)}, f32[48,128]{1,0:T(8,128)S(1)}, u32[]{:S(2)}, u32[]{:S(2)}) %collective-permute-start.2) | collective-permute-done | bytes 24608 | tf_op jit(solution)/shard_map/ppermute | solution.py:657
  9.5 0.9 %shard_map.169 = (f32[320,128]{1,0:T(8,128)S(1)}, f32[64,128]{1,0:T(8,128)S(1)}, f32[64,128]{1,0:T(8,128)S(1)}, f32[32,128]{1,0:T(8,128)S(1)}) custom-call(f32[320,128]{1,0:T(8,128)S(1)} %get-tuple-element.43.cur_ref.refs_0_.refs_1_, f32[320,128]{1,0:T(8,128)S(1)} %get-tuple-element.44.refs_1_, f32[320,128]{1,0:T(8,128)S(1)} %get-tuple-element.45.refs_2_, ...), custom_call_target="tpu_custom_call" | custom-call | tf_op jit(solution)/shard_map/pallas_call | solution.py:629
  11.0 1.6 %collective-permute-start.5 = (f32[32,128]{1,0:T(8,128)S(1)}, f32[32,128]{1,0:T(8,128)S(1)}, u32[]{:S(2)}, u32[]{:S(2)}) collective-permute-start(f32[32,128]{1,0:T(8,128)S(1)} %get-tuple-element.61.refs_10_.refs_5_), channel_id=1, source_target_pairs={{1,0},{0,1},{3,2},{2,3},{5,4},{4,5},{7,6},{6,7},{9,8},{8,9},{11,10... | collective-permute-start | bytes 49160 | tf_op jit(solution)/shard_map/ppermute | solution.py:657
  13.3 0.6 %shard_map.171.refs_14_.refs_0_ = f32[64,128]{1,0:T(8,128)S(1)} custom-call(s32[1,4]{1,0:T(1,128)S(1)} %copy-done.1, f32[320,128]{1,0:T(8,128)S(1)} %get-tuple-element.56.cur_ref._.refs_0_.refs_1_), custom_call_target="tpu_custom_call" | custom-call | tf_op jit(solution)/shard_map/pallas_call | solution.py:629
  13.8 1.0 %collective-permute-done.5.refs_8_.refs_6_ = f32[32,128]{1,0:T(8,128)S(1)} collective-permute-done((f32[32,128]{1,0:T(8,128)S(1)}, f32[32,128]{1,0:T(8,128)S(1)}, u32[]{:S(2)}, u32[]{:S(2)}) %collective-permute-start.5) | collective-permute-done | bytes 16416 | tf_op jit(solution)/shard_map/ppermute | solution.py:657
  14.8 1.0 %shard_map.172 = (f32[320,128]{1,0:T(8,128)S(1)}, f32[64,128]{1,0:T(8,128)S(1)}, f32[64,128]{1,0:T(8,128)S(1)}, f32[32,128]{1,0:T(8,128)S(1)}) custom-call(f32[320,128]{1,0:T(8,128)S(1)} %get-tuple-element.56.cur_ref._.refs_0_.refs_1_, f32[320,128]{1,0:T(8,128)S(1)} %get-tuple-element.43.cur_ref.refs_0_.refs_1_, f32[320,128]{1,0:T(8,128)S(1)} %get-tuple-element.45.refs_2_, ...), custom_call_target="tpu_custom_call" | custom-call | tf_op jit(solution)/shard_map/pallas_call | solution.py:629
  15.8 1.6 %collective-permute-start.7 = (f32[64,128]{1,0:T(8,128)S(1)}, f32[64,128]{1,0:T(8,128)S(1)}, u32[]{:S(2)}, u32[]{:S(2)}) collective-permute-start(f32[64,128]{1,0:T(8,128)S(1)} %get-tuple-element.66), channel_id=1, source_target_pairs={{0,1},{1,0},{2,4},{3,5},{4,2},{5,3},{6,8},{7,9},{8,6},{9,7},{10,12... | collective-permute-start | bytes 98312 | tf_op jit(solution)/shard_map/ppermute | solution.py:652
  17.4 0.5 %collective-permute-start.8 = (f32[32,128]{1,0:T(8,128)S(1)}, f32[32,128]{1,0:T(8,128)S(1)}, u32[]{:S(2)}, u32[]{:S(2)}) collective-permute-start(f32[32,128]{1,0:T(8,128)S(1)} %get-tuple-element.67.refs_10_.refs_7_), channel_id=1, source_target_pairs={{1,0},{0,1},{3,2},{2,3},{5,4},{4,5},{7,6},{6,7},{9,8},{8,9},{11,10... | collective-permute-start | bytes 49160 | tf_op jit(solution)/shard_map/ppermute | solution.py:657
  18.4 2.7 %collective-permute-done.8.refs_8_ = f32[32,128]{1,0:T(8,128)S(1)} collective-permute-done((f32[32,128]{1,0:T(8,128)S(1)}, f32[32,128]{1,0:T(8,128)S(1)}, u32[]{:S(2)}, u32[]{:S(2)}) %collective-permute-start.8) | collective-permute-done | bytes 16416 | tf_op jit(solution)/shard_map/ppermute | solution.py:657
  21.1 0.9 %shard_map.174 = (f32[320,128]{1,0:T(8,128)S(1)}, f32[64,128]{1,0:T(8,128)S(1)}, f32[64,128]{1,0:T(8,128)S(1)}, f32[32,128]{1,0:T(8,128)S(1)}) custom-call(f32[320,128]{1,0:T(8,128)S(1)} %get-tuple-element.62.cur_ref.refs_0_.refs_1_, f32[320,128]{1,0:T(8,128)S(1)} %get-tuple-element.56.cur_ref._.refs_0_.refs_1_, f32[320,128]{1,0:T(8,128)S(1)} %get-tuple-element.45.refs_2_, ...), custom_call_target="tpu_custom_call" | custom-call | tf_op jit(solution)/shard_map/pallas_call | solution.py:629
  22.1 0.7 %collective-permute-start.10 = (f32[64,128]{1,0:T(8,128)S(1)}, f32[64,128]{1,0:T(8,128)S(1)}, u32[]{:S(2)}, u32[]{:S(2)}) collective-permute-start(f32[64,128]{1,0:T(8,128)S(1)} %get-tuple-element.72), channel_id=1, source_target_pairs={{0,1},{1,0},{2,4},{3,5},{4,2},{5,3},{6,8},{7,9},{8,6},{9,7},{10,12... | collective-permute-start | bytes 98312 | tf_op jit(solution)/shard_map/ppermute | solution.py:652
  22.8 1.4 %collective-permute-start.11 = (f32[32,128]{1,0:T(8,128)S(1)}, f32[32,128]{1,0:T(8,128)S(1)}, u32[]{:S(2)}, u32[]{:S(2)}) collective-permute-start(f32[32,128]{1,0:T(8,128)S(1)} %get-tuple-element.73.refs_9_.refs_10_), channel_id=1, source_target_pairs={{1,0},{0,1},{3,2},{2,3},{5,4},{4,5},{7,6},{6,7},{9,8},{8,9},{11,10... | collective-permute-start | bytes 49160 | tf_op jit(solution)/shard_map/ppermute | solution.py:657
  24.2 0.5 %shard_map.175 = (f32[320,128]{1,0:T(8,128)S(1)}, f32[160,128]{1,0:T(8,128)S(1)}) custom-call(f32[320,128]{1,0:T(8,128)S(1)} %get-tuple-element.68.cur_ref.refs_0_, f32[8,128]{1,0:T(8,128)S(1)} %get-tuple-element.46.material_ref.refs_5_, bf16[2,640,384]{2,1,0:T(8,128)(2,1)S(1)} %get-tuple-element.47.own_ref, bf16[160,256]{1,0:T(8,128)(2,1)S(1)} %get-tuple-element.48.touch_ref), custom_call_target="tpu_custom_call" | custom-call | tf_op jit(solution)/shard_map/pallas_call | solution.py:629
  24.7 0.5 %copy-done = bf16[512,512]{1,0:T(8,128)(2,1)S(1)} copy-done((bf16[512,512]{1,0:T(8,128)(2,1)S(1)}, bf16[512,512]{1,0:T(8,128)(2,1)}, u32[]{:S(2)}) %copy-start) | copy-done | bytes 524312
  25.2 1.0 %shard_map.176 = (f32[3,17,4,128]{3,2,1,0:T(4,128)}, f32[32,128]{1,0:T(8,128)S(1)}, bf16[128,128]{1,0:T(8,128)(2,1)S(1)}) custom-call(f32[320,128]{1,0:T(8,128)S(1)} %get-tuple-element.68.cur_ref.refs_0_, bf16[512,512]{1,0:T(8,128)(2,1)S(1)} %copy-done, f32[16,128]{1,0:T(8,128)S(1)} %get-tuple-element.74.refs_2_.refs_1_, ...), custom_call_target="tpu_custom_call" | custom-call | tf_op jit(solution)/shard_map/pallas_call | solution.py:629
  26.7 1.4 %collective-permute-start.12 = (f32[2,128]{1,0:T(2,128)S(1)}, f32[2,128]{1,0:T(2,128)S(1)}, u32[]{:S(2)}, u32[]{:S(2)}) collective-permute-start(f32[2,128]{1,0:T(2,128)S(1)} %get-tuple-element.79), channel_id=1, source_target_pairs={{0,1},{1,0},{2,4},{3,5},{4,2},{5,3},{6,8},{7,9},{8,6},{9,7},{10,12... | collective-permute-start | bytes 3080 | tf_op jit(solution)/shard_map/ppermute | solution.py:652
  28.1 0.7 %collective-permute-start.13 = (f32[2,128]{1,0:T(2,128)S(1)}, f32[2,128]{1,0:T(2,128)S(1)}, u32[]{:S(2)}, u32[]{:S(2)}) collective-permute-start(f32[2,128]{1,0:T(2,128)S(1)} %get-tuple-element.80), channel_id=1, source_target_pairs={{0,1},{1,0},{2,3},{3,2},{4,8},{5,9},{6,10},{7,11},{8,4},{9,5},{10,... | collective-permute-start | bytes 3080 | tf_op jit(solution)/shard_map/ppermute | solution.py:652
  28.8 2.1 %collective-permute-start.14 = (f32[2,128]{1,0:T(2,128)S(1)}, f32[2,128]{1,0:T(2,128)S(1)}, u32[]{:S(2)}, u32[]{:S(2)}) collective-permute-start(f32[2,128]{1,0:T(2,128)S(1)} %get-tuple-element.81), channel_id=1, source_target_pairs={{0,4},{1,5},{2,6},{3,7},{4,0},{5,1},{6,2},{7,3},{8,12},{9,13},{10,... | collective-permute-start | bytes 3080 | tf_op jit(solution)/shard_map/ppermute | solution.py:652
  30.9 1.4 %shard_map.178 = f32[3,17,4,128]{3,2,1,0:T(4,128)} custom-call(f32[320,128]{1,0:T(8,128)S(1)} %get-tuple-element.68.cur_ref.refs_0_, f32[320,128]{1,0:T(8,128)S(1)} %get-tuple-element.62.cur_ref.refs_0_.refs_1_, f32[320,128]{1,0:T(8,128)S(1)} %get-tuple-element.45.refs_2_, f32[320,128]{1,0:T(8,128)S(1)} %get-tuple-element.69.refs_3_, ...), custom_call_target="tpu_custom_call" | custom-call | tf_op jit(solution)/shard_map/pallas_call | solution.py:629
  32.3 0.6 %add_bitcast_fusion = f32[1,2,128]{2,1,0:T(2,128)} fusion(f32[2,128]{1,0:T(2,128)S(1)} %collective-permute-done.15, f32[2,128]{1,0:T(2,128)S(1)} %collective-permute-done.14, f32[2,128]{1,0:T(2,128)S(1)} %collective-permute-done.13, f32[2,128]{1,0:T(2,128)S(1)} %get-tuple-element.77.refs_14_, f32[2,128]{1,0:T(2,128)S(1)} %collective-permute-done.12), kind=kLoop, calls=%fused_computation | loop fusion | flops 1024 | bytes 6144 | tf_op jit(solution)/shard_map/broadcast_in_dim | solution.py:781
  (26 shorter events, 2.9 us)
Async XLA Ops:
  2.6 6.9 %collective-permute-start = (f32[64,128]{1,0:T(8,128)S(1)}, f32[64,128]{1,0:T(8,128)S(1)}, u32[]{:S(2)}, u32[]{:S(2)}) collective-permute-start(f32[64,128]{1,0:T(8,128)S(1)} %get-tuple-element.51), channel_id=1, source_target_pairs={{0,2},{1,3},{2,0},{3,1},{4,6},{5,7},{6,4},{7,5},{8,10},{9,11},{10,... | collective-permute-start | bytes 98312 | tf_op jit(solution)/shard_map/ppermute | solution.py:652
  3.1 6.4 %collective-permute-start.1 = (f32[64,128]{1,0:T(8,128)S(1)}, f32[64,128]{1,0:T(8,128)S(1)}, u32[]{:S(2)}, u32[]{:S(2)}) collective-permute-start(f32[64,128]{1,0:T(8,128)S(1)} %get-tuple-element.52), channel_id=1, source_target_pairs={{0,1},{1,0},{2,4},{3,5},{4,2},{5,3},{6,8},{7,9},{8,6},{9,7},{10,12... | collective-permute-start | bytes 98312 | tf_op jit(solution)/shard_map/ppermute | solution.py:652
  5.7 3.8 %collective-permute-start.2 = (f32[48,128]{1,0:T(8,128)S(1)}, f32[48,128]{1,0:T(8,128)S(1)}, u32[]{:S(2)}, u32[]{:S(2)}) collective-permute-start(f32[48,128]{1,0:T(8,128)S(1)} %get-tuple-element.53.refs_10_.refs_11_.refs_3_), channel_id=1, source_target_pairs={{1,0},{0,1},{3,2},{2,3},{5,4},{4,5},{7,6},{6,7},{9,8},{8,9},{11,10... | collective-permute-start | bytes 73736 | tf_op jit(solution)/shard_map/ppermute | solution.py:657
  10.5 4.4 %collective-permute-start.3 = (f32[64,128]{1,0:T(8,128)S(1)}, f32[64,128]{1,0:T(8,128)S(1)}, u32[]{:S(2)}, u32[]{:S(2)}) collective-permute-start(f32[64,128]{1,0:T(8,128)S(1)} %get-tuple-element.59), channel_id=1, source_target_pairs={{0,2},{1,3},{2,0},{3,1},{4,6},{5,7},{6,4},{7,5},{8,10},{9,11},{10,... | collective-permute-start | bytes 98312 | tf_op jit(solution)/shard_map/ppermute | solution.py:652
  10.5 4.3 %collective-permute-start.4 = (f32[64,128]{1,0:T(8,128)S(1)}, f32[64,128]{1,0:T(8,128)S(1)}, u32[]{:S(2)}, u32[]{:S(2)}) collective-permute-start(f32[64,128]{1,0:T(8,128)S(1)} %get-tuple-element.60), channel_id=1, source_target_pairs={{0,1},{1,0},{2,4},{3,5},{4,2},{5,3},{6,8},{7,9},{8,6},{9,7},{10,12... | collective-permute-start | bytes 98312 | tf_op jit(solution)/shard_map/ppermute | solution.py:652
  11.0 3.9 %collective-permute-start.5 = (f32[32,128]{1,0:T(8,128)S(1)}, f32[32,128]{1,0:T(8,128)S(1)}, u32[]{:S(2)}, u32[]{:S(2)}) collective-permute-start(f32[32,128]{1,0:T(8,128)S(1)} %get-tuple-element.61.refs_10_.refs_5_), channel_id=1, source_target_pairs={{1,0},{0,1},{3,2},{2,3},{5,4},{4,5},{7,6},{6,7},{9,8},{8,9},{11,10... | collective-permute-start | bytes 49160 | tf_op jit(solution)/shard_map/ppermute | solution.py:657
  12.6 0.7 %copy-start.1 = (s32[1,4]{1,0:T(1,128)S(1)}, s32[1,4]{1,0:T(1,128)}, u32[]{:S(2)}) copy-start(s32[1,4]{1,0:T(1,128)} %owner_ref.1) | copy-start | bytes 52
  15.8 5.3 %collective-permute-start.6 = (f32[64,128]{1,0:T(8,128)S(1)}, f32[64,128]{1,0:T(8,128)S(1)}, u32[]{:S(2)}, u32[]{:S(2)}) collective-permute-start(f32[64,128]{1,0:T(8,128)S(1)} %get-tuple-element.65), channel_id=1, source_target_pairs={{0,2},{1,3},{2,0},{3,1},{4,6},{5,7},{6,4},{7,5},{8,10},{9,11},{10,... | collective-permute-start | bytes 98312 | tf_op jit(solution)/shard_map/ppermute | solution.py:652
  15.8 5.3 %collective-permute-start.7 = (f32[64,128]{1,0:T(8,128)S(1)}, f32[64,128]{1,0:T(8,128)S(1)}, u32[]{:S(2)}, u32[]{:S(2)}) collective-permute-start(f32[64,128]{1,0:T(8,128)S(1)} %get-tuple-element.66), channel_id=1, source_target_pairs={{0,1},{1,0},{2,4},{3,5},{4,2},{5,3},{6,8},{7,9},{8,6},{9,7},{10,12... | collective-permute-start | bytes 98312 | tf_op jit(solution)/shard_map/ppermute | solution.py:652
  17.4 3.7 %collective-permute-start.8 = (f32[32,128]{1,0:T(8,128)S(1)}, f32[32,128]{1,0:T(8,128)S(1)}, u32[]{:S(2)}, u32[]{:S(2)}) collective-permute-start(f32[32,128]{1,0:T(8,128)S(1)} %get-tuple-element.67.refs_10_.refs_7_), channel_id=1, source_target_pairs={{1,0},{0,1},{3,2},{2,3},{5,4},{4,5},{7,6},{6,7},{9,8},{8,9},{11,10... | collective-permute-start | bytes 49160 | tf_op jit(solution)/shard_map/ppermute | solution.py:657
  22.1 4.5 %collective-permute-start.9 = (f32[64,128]{1,0:T(8,128)S(1)}, f32[64,128]{1,0:T(8,128)S(1)}, u32[]{:S(2)}, u32[]{:S(2)}) collective-permute-start(f32[64,128]{1,0:T(8,128)S(1)} %get-tuple-element.71), channel_id=1, source_target_pairs={{0,2},{1,3},{2,0},{3,1},{4,6},{5,7},{6,4},{7,5},{8,10},{9,11},{10,... | collective-permute-start | bytes 98312 | tf_op jit(solution)/shard_map/ppermute | solution.py:652
  22.1 4.5 %collective-permute-start.10 = (f32[64,128]{1,0:T(8,128)S(1)}, f32[64,128]{1,0:T(8,128)S(1)}, u32[]{:S(2)}, u32[]{:S(2)}) collective-permute-start(f32[64,128]{1,0:T(8,128)S(1)} %get-tuple-element.72), channel_id=1, source_target_pairs={{0,1},{1,0},{2,4},{3,5},{4,2},{5,3},{6,8},{7,9},{8,6},{9,7},{10,12... | collective-permute-start | bytes 98312 | tf_op jit(solution)/shard_map/ppermute | solution.py:652
  22.8 3.7 %collective-permute-start.11 = (f32[32,128]{1,0:T(8,128)S(1)}, f32[32,128]{1,0:T(8,128)S(1)}, u32[]{:S(2)}, u32[]{:S(2)}) collective-permute-start(f32[32,128]{1,0:T(8,128)S(1)} %get-tuple-element.73.refs_9_.refs_10_), channel_id=1, source_target_pairs={{1,0},{0,1},{3,2},{2,3},{5,4},{4,5},{7,6},{6,7},{9,8},{8,9},{11,10... | collective-permute-start | bytes 49160 | tf_op jit(solution)/shard_map/ppermute | solution.py:657
  24.2 1.0 %copy-start = (bf16[512,512]{1,0:T(8,128)(2,1)S(1)}, bf16[512,512]{1,0:T(8,128)(2,1)}, u32[]{:S(2)}) copy-start(bf16[512,512]{1,0:T(8,128)(2,1)} %constant.16.clone.refs_1_.refs_15_) | copy-start | bytes 1572868
  26.7 5.6 %collective-permute-start.12 = (f32[2,128]{1,0:T(2,128)S(1)}, f32[2,128]{1,0:T(2,128)S(1)}, u32[]{:S(2)}, u32[]{:S(2)}) collective-permute-start(f32[2,128]{1,0:T(2,128)S(1)} %get-tuple-element.79), channel_id=1, source_target_pairs={{0,1},{1,0},{2,4},{3,5},{4,2},{5,3},{6,8},{7,9},{8,6},{9,7},{10,12... | collective-permute-start | bytes 3080 | tf_op jit(solution)/shard_map/ppermute | solution.py:652
  28.1 4.2 %collective-permute-start.13 = (f32[2,128]{1,0:T(2,128)S(1)}, f32[2,128]{1,0:T(2,128)S(1)}, u32[]{:S(2)}, u32[]{:S(2)}) collective-permute-start(f32[2,128]{1,0:T(2,128)S(1)} %get-tuple-element.80), channel_id=1, source_target_pairs={{0,1},{1,0},{2,3},{3,2},{4,8},{5,9},{6,10},{7,11},{8,4},{9,5},{10,... | collective-permute-start | bytes 3080 | tf_op jit(solution)/shard_map/ppermute | solution.py:652
  28.8 3.6 %collective-permute-start.14 = (f32[2,128]{1,0:T(2,128)S(1)}, f32[2,128]{1,0:T(2,128)S(1)}, u32[]{:S(2)}, u32[]{:S(2)}) collective-permute-start(f32[2,128]{1,0:T(2,128)S(1)} %get-tuple-element.81), channel_id=1, source_target_pairs={{0,4},{1,5},{2,6},{3,7},{4,0},{5,1},{6,2},{7,3},{8,12},{9,13},{10,... | collective-permute-start | bytes 3080 | tf_op jit(solution)/shard_map/ppermute | solution.py:652
  30.8 1.5 %collective-permute-start.15 = (f32[2,128]{1,0:T(2,128)S(1)}, f32[2,128]{1,0:T(2,128)S(1)}, u32[]{:S(2)}, u32[]{:S(2)}) collective-permute-start(f32[2,128]{1,0:T(2,128)S(1)} %get-tuple-element.82), channel_id=1, source_target_pairs={{0,2},{1,3},{2,0},{3,1},{4,6},{5,7},{6,4},{7,5},{8,10},{9,11},{10,... | collective-permute-start | bytes 3080 | tf_op jit(solution)/shard_map/ppermute | solution.py:652

commit v6 on v4

--- a/solution.py
+++ b/solution.py
@@ -342,6 +342,7 @@
     touch_hbm,
     cur_ref,
     even_ref,
+    even_rest,
     odd_ref,
     fault_out_ref,
     material_ref,
@@ -398,7 +399,8 @@
     planes = [cur[x * PLANE : (x + 1) * PLANE] for x in range(4)]
     edge = sum(dot(edge_ref[x], stacked(planes[x])) for x in range(4))
     right = edge_message(edge, lame_row, shear_row, z_elems)
-    even_ref[...], odd_ref[...] = select_messages(parity, cur[: 4 * BLOCK], right)
+    message, odd_ref[...] = select_messages(parity, cur[: 4 * BLOCK], right)
+    even_ref[...], even_rest[...] = message[: 2 * BLOCK], message[2 * BLOCK :]
     cur_ref[...] = cur
     for x in range(4):
         fault_out_ref[8 * x : 8 * x + 8] = fault_message(planes[x], z_elems)
@@ -475,18 +477,18 @@
     cur_ref, fol_ref, minv_ref, base_ref, touch_ref, material_ref, odd_ref, up_ref = refs[:8]
     refs = list(refs[8:])
     down_ref = None if pair else refs.pop(0)
-    even_ref = refs.pop(0)
+    even_in = jnp.concatenate([refs.pop(0)[...], refs.pop(0)[...]], axis=0)
     first_up_ref, own_ref, first_own_ref, far_ref, edge_ref = refs[:5]
     refs = refs[5 + extra :]
     if last:
         back_ref, out_ref, scratch = refs
     else:
-        new_ref, even_out, odd_out, fault_out = refs
+        new_ref, even_out, even_rest, odd_out, fault_out = refs
     place = lax.axis_index("dom")
     lanes = cur_ref.shape[1]
     even = place % 2 == 0
-    far = jnp.where(place == last_place, 0.0, jnp.where(even, even_ref[...], odd_ref[...]))
-    left = jnp.where(place == 0, 0.0, jnp.where(even, odd_ref[...], even_ref[...]))
+    far = jnp.where(place == last_place, 0.0, jnp.where(even, even_in, odd_ref[...]))
+    left = jnp.where(place == 0, 0.0, jnp.where(even, odd_ref[...], even_in))
     lane_wide = lax.broadcasted_iota(jnp.int32, (BLOCK, lanes), 1)
     below = jnp.where(
         lane_wide % z_elems != z_elems - 1, pltpu.roll(far[:BLOCK], lanes - 1, 1), 0.0
@@ -556,10 +558,11 @@
         from_elements(jnp.concatenate(planes, axis=0), scratch, back_ref, out_ref, y_elems)
     else:
         right = edge_message(edge, lame_row, shear_row, z_elems)
-        even_out[...], odd_out[...] = select_messages(place % 2, first, right)
-
-
-def mask_kernel(owner_ref, _, mask_ref):
+        message, odd_out[...] = select_messages(place % 2, first, right)
+        even_out[...], even_rest[...] = message[: 2 * BLOCK], message[2 * BLOCK :]
+
+
+def mask_kernel(owner_ref, _, back_ref, mask_ref):
     shape = (PATCH_ROWS, mask_ref.shape[1])
     first = (lax.axis_index("dom") - REACH) * PATCH_DEV
     number = lax.broadcasted_iota(jnp.int32, shape, 0) + first
@@ -683,19 +686,19 @@
     native = pltpu.VMEM((y_elems, 4 * BLOCK, lanes), jnp.float32)
     field = (4 * PLANE, lanes)
     plane = (4 * BLOCK, lanes)
+    half = (2 * BLOCK, lanes)
 
     def exchange(even, odd, fault_rows):
         if pair:
             faults = [from_behind(fault_rows, "depth", 1)]
         else:
             faults = [from_behind(fault_rows, "depth", 1), from_behind(fault_rows, "depth", -1)]
-        odd_in = swapped(odd, 1, 1)
-        return swapped(even, 1, 0), odd_in, faults
+        return [swapped(part, 1, 0) for part in even], swapped(odd, 1, 1), faults
 
     tables = (edge_table, own_table, far_table, touch_table)
-    cur, even, odd, fault_rows, material, edge_table, own_table, far_table, touch_table = kernel_call(
+    cur, *even, odd, fault_rows, material, edge_table, own_table, far_table, touch_table = kernel_call(
         first_kernel,
-        [field, plane, plane, (32 + 4 * steps, lanes), (8, lanes)]
+        [field, half, half, plane, (32 + 4 * steps, lanes), (8, lanes)]
         + [(t.shape, t.dtype) for t in tables],
         (now, flags, weak_slope[0], lame_first[0], shear_modulus[0]) + tables,
         scratch=[native],
@@ -724,19 +727,21 @@
             [cur, material, own_table, touch_table],
             (),
         )
-        args = [cur, fol, minv, base, touch, material, odd_in] + fault_in
-        args += [even_in, first_in[0], fault_rows, first_fault, far_table, edge_table]
+        args = [cur, fol, minv, base, touch, material, odd_in] + fault_in + even_in
+        args += [first_in[0], fault_rows, first_fault, far_table, edge_table]
         static = dict(
             step=step, last=last, extra=1 if last or step == 1 else 0, last_place=lax.axis_size("dom") - 1, pair=pair, y_elems=y_elems,
             z_elems=z_elems,
         )
         if step == 1:
-            mask = kernel_call(mask_kernel, [(4 * PATCH_ROWS, lanes)], [patch_owner, cur], (0,), unread=(1,))[0]
+            mask = kernel_call(
+                mask_kernel, [(4 * PATCH_ROWS, lanes)], [patch_owner, cur, back], (0,), unread=(1,)
+            )[0]
             args.append(mask)
         if not last:
-            new, even, odd, new_fault = kernel_call(
+            new, *even, odd, new_fault = kernel_call(
                 step_kernel,
-                [field, plane, plane, (32, lanes)],
+                [field, half, half, plane, (32, lanes)],
                 args,
                 unread=(len(args) - 1,) if step == 1 else (),
                 **static,
@@ -760,8 +765,8 @@
             sums = kernel_call(
                 patch_kernel,
                 [(PATCH_DEV, lanes)] * 5,
-                [mask, weight, grad, table, odd_in] + fault_in + [even_in, touch],
-                unread=(4, 5 + len(fault_in), 6 + len(fault_in)),
+                [mask, weight, grad, table, odd_in] + fault_in + even_in + [touch],
+                unread=(4,) + tuple(range(5 + len(fault_in), 8 + len(fault_in))),
                 pair=pair,
                 steps=steps,
             )

time: 35.2 us -> 35 us (level)
  starting transfers between devices: 18.1 us -> 16 us
  waiting for transfers between devices: 3.41 us -> 5.49 us
    ppermute x4, starting transfers between devices: 5.97 us -> 3.01 us  [from_behind(): lax.ppermute(block, axis, [((i - distance) % size, i) for i in range(size)])]
    ppermute x4, waiting for transfers between devices: 3.29 us -> 4.97 us  [from_behind(): lax.ppermute(block, axis, [((i - distance) % size, i) for i in range(size)])]
    ppermute x12 -> x16, starting transfers between devices: 12.2 us -> 13 us  [swapped(): return lax.ppermute(block, ('dom', 'depth'), route)]
    ppermute x12 -> x16, waiting for transfers between devices: 0.12 us -> 0.52 us  [swapped(): return lax.ppermute(block, ('dom', 'depth'), route)]
  transfers between devices with their start and end apart: 16 -> 20, of which waited for: 5 -> 5; matrix products, arithmetic and copies ran while one was open for 0% -> 0% of each run, Pallas kernels for 19% -> 19%
where the time goes in v6:
time: 35 us; the launch traced here: 34.8 us
  starting transfers between devices  16 us (46%)
  Pallas kernels  11.5 us (33%)
  waiting for transfers between devices  5.49 us (16%)
  between operations  0.74 us (2%)
  other arithmetic  0.57 us (2%)
  local copies, waits for them, and re-layouts  0.53 us (2%)
    ppermute x16, starting transfers between devices, swapped(): return lax.ppermute(block, ('dom', 'depth'), route)  13 us
    pallas_call x13, Pallas kernels, kernel_call(): pl.pallas_call(functools.partial(body, **static) if static else body, out...  11.5 us
    ppermute x4, waiting for transfers between devices, from_behind(): lax.ppermute(block, axis, [((i - distance) % size, i) for i in range(size)])  4.97 us
    ppermute x4, starting transfers between devices, from_behind(): lax.ppermute(block, axis, [((i - distance) % size, i) for i in range(size)])  3.01 us
  transfers between devices with their start and end apart: 20, of which 5 were waited for; matrix products, arithmetic and copies ran while one was open for 0% of the time, Pallas kernels for 19%

profile of v6, /device:TPU:0, one launch (start us, length us, event | category | flops | bytes accessed | tf_op | source)
XLA Modules:
  0.0 34.8 jit_solution(18236792642736993283)
XLA Ops:
  0.6 2.0 %shard_map.166 = (f32[320,128]{1,0:T(8,128)S(1)}, f32[32,128]{1,0:T(8,128)S(1)}, f32[32,128]{1,0:T(8,128)S(1)}, f32[64,128]{1,0:T(8,128)S(1)}, f32[48,128]{1,0:T...) custom-call(f32[3,17,4,128]{3,2,1,0:T(4,128)} %bitcast.12, ...), custom_call_target="tpu_custom_call" | custom-call | tf_op jit(solution)/shard_map/pallas_call | solution.py:632
  2.6 3.0 %collective-permute-start = (f32[64,128]{1,0:T(8,128)S(1)}, f32[64,128]{1,0:T(8,128)S(1)}, u32[]{:S(2)}, u32[]{:S(2)}) collective-permute-start(f32[64,128]{1,0:T(8,128)S(1)} %get-tuple-element.55), channel_id=1, source_target_pairs={{0,1},{1,0},{2,4},{3,5},{4,2},{5,3},{6,8},{7,9},{8,6},{9,7},{10,12... | collective-permute-start | bytes 98312 | tf_op jit(solution)/shard_map/ppermute | solution.py:655
  5.7 1.3 %collective-permute-start.2 = (f32[32,128]{1,0:T(8,128)S(1)}, f32[32,128]{1,0:T(8,128)S(1)}, u32[]{:S(2)}, u32[]{:S(2)}) collective-permute-start(f32[32,128]{1,0:T(8,128)S(1)} %get-tuple-element.57), channel_id=1, source_target_pairs={{0,2},{1,3},{2,0},{3,1},{4,6},{5,7},{6,4},{7,5},{8,10},{9,11},{10,... | collective-permute-start | bytes 49160 | tf_op jit(solution)/shard_map/ppermute | solution.py:655
  7.0 1.6 %shard_map.167 = (f32[320,128]{1,0:T(8,128)S(1)}, f32[320,128]{1,0:T(8,128)S(1)}, f32[16,128]{1,0:T(8,128)S(1)}) custom-call(f32[3,17,4,128]{3,2,1,0:T(4,128)} %bitcast.13, f32[17,4,128]{2,1,0:T(4,128)} %bitcast.15, s32[4,4,128]{2,1,0:T(4,128)} %bitcast.17, f32[4,128]{1,0:T(4,128)} %bitcast.21, f32[320,128]{1,0:T(8,128)} %constant.17.clone.mass_hbm), custom_call_target="tpu_custom_call" | custom-call | tf_op jit(solution)/shard_map/pallas_call | solution.py:632
  9.4 0.9 %shard_map.169 = (f32[320,128]{1,0:T(8,128)S(1)}, f32[32,128]{1,0:T(8,128)S(1)}, f32[32,128]{1,0:T(8,128)S(1)}, f32[64,128]{1,0:T(8,128)S(1)}, f32[32,128]{1,0:T(8,128)S(1)}) custom-call(f32[320,128]{1,0:T(8,128)S(1)} %get-tuple-element.47.cur_ref.refs_0_.refs_1_, f32[320,128]{1,0:T(8,128)S(1)} %get-tuple-element.48.refs_1_, ...), custom_call_target="tpu_custom_call" | custom-call | tf_op jit(solution)/shard_map/pallas_call | solution.py:632
  10.4 0.9 %collective-permute-start.4 = (f32[64,128]{1,0:T(8,128)S(1)}, f32[64,128]{1,0:T(8,128)S(1)}, u32[]{:S(2)}, u32[]{:S(2)}) collective-permute-start(f32[64,128]{1,0:T(8,128)S(1)} %get-tuple-element.64), channel_id=1, source_target_pairs={{0,1},{1,0},{2,4},{3,5},{4,2},{5,3},{6,8},{7,9},{8,6},{9,7},{10,12... | collective-permute-start | bytes 98312 | tf_op jit(solution)/shard_map/ppermute | solution.py:655
  11.8 1.2 %collective-permute-start.5 = (f32[32,128]{1,0:T(8,128)S(1)}, f32[32,128]{1,0:T(8,128)S(1)}, u32[]{:S(2)}, u32[]{:S(2)}) collective-permute-start(f32[32,128]{1,0:T(8,128)S(1)} %get-tuple-element.65.refs_11_.refs_5_), channel_id=1, source_target_pairs={{1,0},{0,1},{3,2},{2,3},{5,4},{4,5},{7,6},{6,7},{9,8},{8,9},{11,10... | collective-permute-start | bytes 49160 | tf_op jit(solution)/shard_map/ppermute | solution.py:660
  14.6 0.9 %collective-permute-done.5.refs_7_.refs_6_ = f32[32,128]{1,0:T(8,128)S(1)} collective-permute-done((f32[32,128]{1,0:T(8,128)S(1)}, f32[32,128]{1,0:T(8,128)S(1)}, u32[]{:S(2)}, u32[]{:S(2)}) %collective-permute-start.5) | collective-permute-done | bytes 16416 | tf_op jit(solution)/shard_map/ppermute | solution.py:660
  15.5 0.9 %shard_map.172 = (f32[320,128]{1,0:T(8,128)S(1)}, f32[32,128]{1,0:T(8,128)S(1)}, f32[32,128]{1,0:T(8,128)S(1)}, f32[64,128]{1,0:T(8,128)S(1)}, f32[32,128]{1,0:T(8,128)S(1)}) custom-call(f32[320,128]{1,0:T(8,128)S(1)} %get-tuple-element.61.cur_ref._.refs_0_.refs_1_, f32[320,128]{1,0:T(8,128)S(1)} %get-tuple-element.47.cur_ref.refs_0_.refs_1_, ...), custom_call_target="tpu_custom_call" | custom-call | tf_op jit(solution)/shard_map/pallas_call | solution.py:632
  16.5 1.2 %collective-permute-start.8 = (f32[64,128]{1,0:T(8,128)S(1)}, f32[64,128]{1,0:T(8,128)S(1)}, u32[]{:S(2)}, u32[]{:S(2)}) collective-permute-start(f32[64,128]{1,0:T(8,128)S(1)} %get-tuple-element.71), channel_id=1, source_target_pairs={{0,1},{1,0},{2,4},{3,5},{4,2},{5,3},{6,8},{7,9},{8,6},{9,7},{10,12... | collective-permute-start | bytes 98312 | tf_op jit(solution)/shard_map/ppermute | solution.py:655
  18.2 1.2 %collective-permute-start.9 = (f32[32,128]{1,0:T(8,128)S(1)}, f32[32,128]{1,0:T(8,128)S(1)}, u32[]{:S(2)}, u32[]{:S(2)}) collective-permute-start(f32[32,128]{1,0:T(8,128)S(1)} %get-tuple-element.72.refs_11_.refs_7_), channel_id=1, source_target_pairs={{1,0},{0,1},{3,2},{2,3},{5,4},{4,5},{7,6},{6,7},{9,8},{8,9},{11,10... | collective-permute-start | bytes 49160 | tf_op jit(solution)/shard_map/ppermute | solution.py:660
  19.8 2.0 %collective-permute-done.9.refs_7_.refs_8_ = f32[32,128]{1,0:T(8,128)S(1)} collective-permute-done((f32[32,128]{1,0:T(8,128)S(1)}, f32[32,128]{1,0:T(8,128)S(1)}, u32[]{:S(2)}, u32[]{:S(2)}) %collective-permute-start.9) | collective-permute-done | bytes 16416 | tf_op jit(solution)/shard_map/ppermute | solution.py:660
  21.9 0.9 %shard_map.174 = (f32[320,128]{1,0:T(8,128)S(1)}, f32[32,128]{1,0:T(8,128)S(1)}, f32[32,128]{1,0:T(8,128)S(1)}, f32[64,128]{1,0:T(8,128)S(1)}, f32[32,128]{1,0:T(8,128)S(1)}) custom-call(f32[320,128]{1,0:T(8,128)S(1)} %get-tuple-element.68.cur_ref.refs_0_.refs_1_, f32[320,128]{1,0:T(8,128)S(1)} %get-tuple-element.61.cur_ref._.refs_0_.refs_1_, ...), custom_call_target="tpu_custom_call" | custom-call | tf_op jit(solution)/shard_map/pallas_call | solution.py:632
  22.8 1.2 %collective-permute-start.12 = (f32[64,128]{1,0:T(8,128)S(1)}, f32[64,128]{1,0:T(8,128)S(1)}, u32[]{:S(2)}, u32[]{:S(2)}) collective-permute-start(f32[64,128]{1,0:T(8,128)S(1)} %get-tuple-element.78), channel_id=1, source_target_pairs={{0,1},{1,0},{2,4},{3,5},{4,2},{5,3},{6,8},{7,9},{8,6},{9,7},{10,12... | collective-permute-start | bytes 98312 | tf_op jit(solution)/shard_map/ppermute | solution.py:655
  24.0 0.8 %collective-permute-start.14 = (f32[32,128]{1,0:T(8,128)S(1)}, f32[32,128]{1,0:T(8,128)S(1)}, u32[]{:S(2)}, u32[]{:S(2)}) collective-permute-start(f32[32,128]{1,0:T(8,128)S(1)} %get-tuple-element.80), channel_id=1, source_target_pairs={{0,2},{1,3},{2,0},{3,1},{4,6},{5,7},{6,4},{7,5},{8,10},{9,11},{10,... | collective-permute-start | bytes 49160 | tf_op jit(solution)/shard_map/ppermute | solution.py:655
  24.8 0.6 %collective-permute-start.13 = (f32[32,128]{1,0:T(8,128)S(1)}, f32[32,128]{1,0:T(8,128)S(1)}, u32[]{:S(2)}, u32[]{:S(2)}) collective-permute-start(f32[32,128]{1,0:T(8,128)S(1)} %get-tuple-element.79.refs_9_.refs_11_), channel_id=1, source_target_pairs={{1,0},{0,1},{3,2},{2,3},{5,4},{4,5},{7,6},{6,7},{9,8},{8,9},{11,10... | collective-permute-start | bytes 49160 | tf_op jit(solution)/shard_map/ppermute | solution.py:660
  25.9 1.0 %shard_map.176 = (f32[3,17,4,128]{3,2,1,0:T(4,128)}, f32[32,128]{1,0:T(8,128)S(1)}, bf16[128,128]{1,0:T(8,128)(2,1)S(1)}) custom-call(f32[320,128]{1,0:T(8,128)S(1)} %get-tuple-element.75.cur_ref.refs_0_, bf16[512,512]{1,0:T(8,128)(2,1)S(1)} %copy-done, f32[16,128]{1,0:T(8,128)S(1)} %get-tuple-element.82.refs_2_.refs_1_, ...), custom_call_target="tpu_custom_call" | custom-call | tf_op jit(solution)/shard_map/pallas_call | solution.py:632
  26.9 1.6 %collective-permute-done.13.refs_5_.refs_7_ = f32[32,128]{1,0:T(8,128)S(1)} collective-permute-done((f32[32,128]{1,0:T(8,128)S(1)}, f32[32,128]{1,0:T(8,128)S(1)}, u32[]{:S(2)}, u32[]{:S(2)}) %collective-permute-start.13) | collective-permute-done | bytes 16416 | tf_op jit(solution)/shard_map/ppermute | solution.py:660
  28.7 0.6 %collective-permute-start.16 = (f32[2,128]{1,0:T(2,128)S(1)}, f32[2,128]{1,0:T(2,128)S(1)}, u32[]{:S(2)}, u32[]{:S(2)}) collective-permute-start(f32[2,128]{1,0:T(2,128)S(1)} %get-tuple-element.87), channel_id=1, source_target_pairs={{0,1},{1,0},{2,4},{3,5},{4,2},{5,3},{6,8},{7,9},{8,6},{9,7},{10,12... | collective-permute-start | bytes 3080 | tf_op jit(solution)/shard_map/ppermute | solution.py:655
  29.3 1.4 %collective-permute-start.17 = (f32[2,128]{1,0:T(2,128)S(1)}, f32[2,128]{1,0:T(2,128)S(1)}, u32[]{:S(2)}, u32[]{:S(2)}) collective-permute-start(f32[2,128]{1,0:T(2,128)S(1)} %get-tuple-element.88), channel_id=1, source_target_pairs={{0,1},{1,0},{2,3},{3,2},{4,8},{5,9},{6,10},{7,11},{8,4},{9,5},{10,... | collective-permute-start | bytes 3080 | tf_op jit(solution)/shard_map/ppermute | solution.py:655
  30.7 1.1 %collective-permute-start.18 = (f32[2,128]{1,0:T(2,128)S(1)}, f32[2,128]{1,0:T(2,128)S(1)}, u32[]{:S(2)}, u32[]{:S(2)}) collective-permute-start(f32[2,128]{1,0:T(2,128)S(1)} %get-tuple-element.89), channel_id=1, source_target_pairs={{0,4},{1,5},{2,6},{3,7},{4,0},{5,1},{6,2},{7,3},{8,12},{9,13},{10,... | collective-permute-start | bytes 3080 | tf_op jit(solution)/shard_map/ppermute | solution.py:655
  31.8 0.6 %collective-permute-start.19 = (f32[2,128]{1,0:T(2,128)S(1)}, f32[2,128]{1,0:T(2,128)S(1)}, u32[]{:S(2)}, u32[]{:S(2)}) collective-permute-start(f32[2,128]{1,0:T(2,128)S(1)} %get-tuple-element.90), channel_id=1, source_target_pairs={{0,2},{1,3},{2,0},{3,1},{4,6},{5,7},{6,4},{7,5},{8,10},{9,11},{10,... | collective-permute-start | bytes 3080 | tf_op jit(solution)/shard_map/ppermute | solution.py:655
  32.4 1.4 %shard_map.178 = f32[3,17,4,128]{3,2,1,0:T(4,128)} custom-call(f32[320,128]{1,0:T(8,128)S(1)} %get-tuple-element.75.cur_ref.refs_0_, f32[320,128]{1,0:T(8,128)S(1)} %get-tuple-element.68.cur_ref.refs_0_.refs_1_, f32[320,128]{1,0:T(8,128)S(1)} %get-tuple-element.49.refs_2_, f32[320,128]{1,0:T(8,128)S(1)} %get-tuple-element.76.refs_3_, ...), custom_call_target="tpu_custom_call" | custom-call | tf_op jit(solution)/shard_map/pallas_call | solution.py:632
  34.3 0.6 %add_bitcast_fusion = f32[1,2,128]{2,1,0:T(2,128)} fusion(f32[2,128]{1,0:T(2,128)S(1)} %collective-permute-done.19, f32[2,128]{1,0:T(2,128)S(1)} %collective-permute-done.18, f32[2,128]{1,0:T(2,128)S(1)} %collective-permute-done.17, f32[2,128]{1,0:T(2,128)S(1)} %get-tuple-element.85.refs_15_, f32[2,128]{1,0:T(2,128)S(1)} %collective-permute-done.16), kind=kLoop, calls=%fused_computation | loop fusion | flops 1024 | bytes 6144 | tf_op jit(solution)/shard_map/broadcast_in_dim | solution.py:787
  (34 shorter events, 5.2 us)
Async XLA Ops:
  2.6 6.8 %collective-permute-start = (f32[64,128]{1,0:T(8,128)S(1)}, f32[64,128]{1,0:T(8,128)S(1)}, u32[]{:S(2)}, u32[]{:S(2)}) collective-permute-start(f32[64,128]{1,0:T(8,128)S(1)} %get-tuple-element.55), channel_id=1, source_target_pairs={{0,1},{1,0},{2,4},{3,5},{4,2},{5,3},{6,8},{7,9},{8,6},{9,7},{10,12... | collective-permute-start | bytes 98312 | tf_op jit(solution)/shard_map/ppermute | solution.py:655
  5.6 3.8 %collective-permute-start.1 = (f32[48,128]{1,0:T(8,128)S(1)}, f32[48,128]{1,0:T(8,128)S(1)}, u32[]{:S(2)}, u32[]{:S(2)}) collective-permute-start(f32[48,128]{1,0:T(8,128)S(1)} %get-tuple-element.56.refs_11_.refs_12_.refs_3_), channel_id=1, source_target_pairs={{1,0},{0,1},{3,2},{2,3},{5,4},{4,5},{7,6},{6,7},{9,8},{8,9},{11,10... | collective-permute-start | bytes 73736 | tf_op jit(solution)/shard_map/ppermute | solution.py:660
  5.7 3.4 %collective-permute-start.2 = (f32[32,128]{1,0:T(8,128)S(1)}, f32[32,128]{1,0:T(8,128)S(1)}, u32[]{:S(2)}, u32[]{:S(2)}) collective-permute-start(f32[32,128]{1,0:T(8,128)S(1)} %get-tuple-element.57), channel_id=1, source_target_pairs={{0,2},{1,3},{2,0},{3,1},{4,6},{5,7},{6,4},{7,5},{8,10},{9,11},{10,... | collective-permute-start | bytes 49160 | tf_op jit(solution)/shard_map/ppermute | solution.py:655
  7.0 2.1 %collective-permute-start.3 = (f32[32,128]{1,0:T(8,128)S(1)}, f32[32,128]{1,0:T(8,128)S(1)}, u32[]{:S(2)}, u32[]{:S(2)}) collective-permute-start(f32[32,128]{1,0:T(8,128)S(1)} %get-tuple-element.58), channel_id=1, source_target_pairs={{0,2},{1,3},{2,0},{3,1},{4,6},{5,7},{6,4},{7,5},{8,10},{9,11},{10,... | collective-permute-start | bytes 49160 | tf_op jit(solution)/shard_map/ppermute | solution.py:655
  10.4 5.1 %collective-permute-start.4 = (f32[64,128]{1,0:T(8,128)S(1)}, f32[64,128]{1,0:T(8,128)S(1)}, u32[]{:S(2)}, u32[]{:S(2)}) collective-permute-start(f32[64,128]{1,0:T(8,128)S(1)} %get-tuple-element.64), channel_id=1, source_target_pairs={{0,1},{1,0},{2,4},{3,5},{4,2},{5,3},{6,8},{7,9},{8,6},{9,7},{10,12... | collective-permute-start | bytes 98312 | tf_op jit(solution)/shard_map/ppermute | solution.py:655
  11.3 3.3 %collective-permute-start.6 = (f32[32,128]{1,0:T(8,128)S(1)}, f32[32,128]{1,0:T(8,128)S(1)}, u32[]{:S(2)}, u32[]{:S(2)}) collective-permute-start(f32[32,128]{1,0:T(8,128)S(1)} %get-tuple-element.66), channel_id=1, source_target_pairs={{0,2},{1,3},{2,0},{3,1},{4,6},{5,7},{6,4},{7,5},{8,10},{9,11},{10,... | collective-permute-start | bytes 49160 | tf_op jit(solution)/shard_map/ppermute | solution.py:655
  11.7 2.8 %collective-permute-start.7 = (f32[32,128]{1,0:T(8,128)S(1)}, f32[32,128]{1,0:T(8,128)S(1)}, u32[]{:S(2)}, u32[]{:S(2)}) collective-permute-start(f32[32,128]{1,0:T(8,128)S(1)} %get-tuple-element.67), channel_id=1, source_target_pairs={{0,2},{1,3},{2,0},{3,1},{4,6},{5,7},{6,4},{7,5},{8,10},{9,11},{10,... | collective-permute-start | bytes 49160 | tf_op jit(solution)/shard_map/ppermute | solution.py:655
  11.8 3.7 %collective-permute-start.5 = (f32[32,128]{1,0:T(8,128)S(1)}, f32[32,128]{1,0:T(8,128)S(1)}, u32[]{:S(2)}, u32[]{:S(2)}) collective-permute-start(f32[32,128]{1,0:T(8,128)S(1)} %get-tuple-element.65.refs_11_.refs_5_), channel_id=1, source_target_pairs={{1,0},{0,1},{3,2},{2,3},{5,4},{4,5},{7,6},{6,7},{9,8},{8,9},{11,10... | collective-permute-start | bytes 49160 | tf_op jit(solution)/shard_map/ppermute | solution.py:660
  12.9 1.0 %copy-start = (bf16[512,512]{1,0:T(8,128)(2,1)S(1)}, bf16[512,512]{1,0:T(8,128)(2,1)}, u32[]{:S(2)}) copy-start(bf16[512,512]{1,0:T(8,128)(2,1)} %constant.16.clone.back_ref.refs_1_.refs_16_) | copy-start | bytes 1572868
  12.9 1.0 %copy-start.1 = (s32[1,4]{1,0:T(1,128)S(1)}, s32[1,4]{1,0:T(1,128)}, u32[]{:S(2)}) copy-start(s32[1,4]{1,0:T(1,128)} %owner_ref.1) | copy-start | bytes 52
  16.5 5.4 %collective-permute-start.8 = (f32[64,128]{1,0:T(8,128)S(1)}, f32[64,128]{1,0:T(8,128)S(1)}, u32[]{:S(2)}, u32[]{:S(2)}) collective-permute-start(f32[64,128]{1,0:T(8,128)S(1)} %get-tuple-element.71), channel_id=1, source_target_pairs={{0,1},{1,0},{2,4},{3,5},{4,2},{5,3},{6,8},{7,9},{8,6},{9,7},{10,12... | collective-permute-start | bytes 98312 | tf_op jit(solution)/shard_map/ppermute | solution.py:655
  17.6 2.2 %collective-permute-start.10 = (f32[32,128]{1,0:T(8,128)S(1)}, f32[32,128]{1,0:T(8,128)S(1)}, u32[]{:S(2)}, u32[]{:S(2)}) collective-permute-start(f32[32,128]{1,0:T(8,128)S(1)} %get-tuple-element.73), channel_id=1, source_target_pairs={{0,2},{1,3},{2,0},{3,1},{4,6},{5,7},{6,4},{7,5},{8,10},{9,11},{10,... | collective-permute-start | bytes 49160 | tf_op jit(solution)/shard_map/ppermute | solution.py:655
  18.1 1.8 %collective-permute-start.11 = (f32[32,128]{1,0:T(8,128)S(1)}, f32[32,128]{1,0:T(8,128)S(1)}, u32[]{:S(2)}, u32[]{:S(2)}) collective-permute-start(f32[32,128]{1,0:T(8,128)S(1)} %get-tuple-element.74), channel_id=1, source_target_pairs={{0,2},{1,3},{2,0},{3,1},{4,6},{5,7},{6,4},{7,5},{8,10},{9,11},{10,... | collective-permute-start | bytes 49160 | tf_op jit(solution)/shard_map/ppermute | solution.py:655
  18.2 3.7 %collective-permute-start.9 = (f32[32,128]{1,0:T(8,128)S(1)}, f32[32,128]{1,0:T(8,128)S(1)}, u32[]{:S(2)}, u32[]{:S(2)}) collective-permute-start(f32[32,128]{1,0:T(8,128)S(1)} %get-tuple-element.72.refs_11_.refs_7_), channel_id=1, source_target_pairs={{1,0},{0,1},{3,2},{2,3},{5,4},{4,5},{7,6},{6,7},{9,8},{8,9},{11,10... | collective-permute-start | bytes 49160 | tf_op jit(solution)/shard_map/ppermute | solution.py:660
  22.8 5.7 %collective-permute-start.12 = (f32[64,128]{1,0:T(8,128)S(1)}, f32[64,128]{1,0:T(8,128)S(1)}, u32[]{:S(2)}, u32[]{:S(2)}) collective-permute-start(f32[64,128]{1,0:T(8,128)S(1)} %get-tuple-element.78), channel_id=1, source_target_pairs={{0,1},{1,0},{2,4},{3,5},{4,2},{5,3},{6,8},{7,9},{8,6},{9,7},{10,12... | collective-permute-start | bytes 98312 | tf_op jit(solution)/shard_map/ppermute | solution.py:655
  24.0 2.9 %collective-permute-start.14 = (f32[32,128]{1,0:T(8,128)S(1)}, f32[32,128]{1,0:T(8,128)S(1)}, u32[]{:S(2)}, u32[]{:S(2)}) collective-permute-start(f32[32,128]{1,0:T(8,128)S(1)} %get-tuple-element.80), channel_id=1, source_target_pairs={{0,2},{1,3},{2,0},{3,1},{4,6},{5,7},{6,4},{7,5},{8,10},{9,11},{10,... | collective-permute-start | bytes 49160 | tf_op jit(solution)/shard_map/ppermute | solution.py:655
  24.8 2.1 %collective-permute-start.15 = (f32[32,128]{1,0:T(8,128)S(1)}, f32[32,128]{1,0:T(8,128)S(1)}, u32[]{:S(2)}, u32[]{:S(2)}) collective-permute-start(f32[32,128]{1,0:T(8,128)S(1)} %get-tuple-element.81), channel_id=1, source_target_pairs={{0,2},{1,3},{2,0},{3,1},{4,6},{5,7},{6,4},{7,5},{8,10},{9,11},{10,... | collective-permute-start | bytes 49160 | tf_op jit(solution)/shard_map/ppermute | solution.py:655
  24.8 3.7 %collective-permute-start.13 = (f32[32,128]{1,0:T(8,128)S(1)}, f32[32,128]{1,0:T(8,128)S(1)}, u32[]{:S(2)}, u32[]{:S(2)}) collective-permute-start(f32[32,128]{1,0:T(8,128)S(1)} %get-tuple-element.79.refs_9_.refs_11_), channel_id=1, source_target_pairs={{1,0},{0,1},{3,2},{2,3},{5,4},{4,5},{7,6},{6,7},{9,8},{8,9},{11,10... | collective-permute-start | bytes 49160 | tf_op jit(solution)/shard_map/ppermute | solution.py:660
  28.7 5.1 %collective-permute-start.16 = (f32[2,128]{1,0:T(2,128)S(1)}, f32[2,128]{1,0:T(2,128)S(1)}, u32[]{:S(2)}, u32[]{:S(2)}) collective-permute-start(f32[2,128]{1,0:T(2,128)S(1)} %get-tuple-element.87), channel_id=1, source_target_pairs={{0,1},{1,0},{2,4},{3,5},{4,2},{5,3},{6,8},{7,9},{8,6},{9,7},{10,12... | collective-permute-start | bytes 3080 | tf_op jit(solution)/shard_map/ppermute | solution.py:655
  29.3 4.5 %collective-permute-start.17 = (f32[2,128]{1,0:T(2,128)S(1)}, f32[2,128]{1,0:T(2,128)S(1)}, u32[]{:S(2)}, u32[]{:S(2)}) collective-permute-start(f32[2,128]{1,0:T(2,128)S(1)} %get-tuple-element.88), channel_id=1, source_target_pairs={{0,1},{1,0},{2,3},{3,2},{4,8},{5,9},{6,10},{7,11},{8,4},{9,5},{10,... | collective-permute-start | bytes 3080 | tf_op jit(solution)/shard_map/ppermute | solution.py:655
  30.7 3.6 %collective-permute-start.18 = (f32[2,128]{1,0:T(2,128)S(1)}, f32[2,128]{1,0:T(2,128)S(1)}, u32[]{:S(2)}, u32[]{:S(2)}) collective-permute-start(f32[2,128]{1,0:T(2,128)S(1)} %get-tuple-element.89), channel_id=1, source_target_pairs={{0,4},{1,5},{2,6},{3,7},{4,0},{5,1},{6,2},{7,3},{8,12},{9,13},{10,... | collective-permute-start | bytes 3080 | tf_op jit(solution)/shard_map/ppermute | solution.py:655
  31.8 2.5 %collective-permute-start.19 = (f32[2,128]{1,0:T(2,128)S(1)}, f32[2,128]{1,0:T(2,128)S(1)}, u32[]{:S(2)}, u32[]{:S(2)}) collective-permute-start(f32[2,128]{1,0:T(2,128)S(1)} %get-tuple-element.90), channel_id=1, source_target_pairs={{0,2},{1,3},{2,0},{3,1},{4,6},{5,7},{6,4},{7,5},{8,10},{9,11},{10,... | collective-permute-start | bytes 3080 | tf_op jit(solution)/shard_map/ppermute | solution.py:655

commit v7 on v6

--- a/solution.py
+++ b/solution.py
@@ -507,6 +507,8 @@
     pull_last = jnp.logical_and(shared, across == y_elems - 1)
     above = above_lanes(lanes, z_elems)
     fault_in = fault_input(up_ref, down_ref, 32)
+    if not last:
+        fault_out[32:] = jnp.zeros_like(fault_out[32:])
     planes = []
     edge = 0.0
     for x in range(4):
@@ -741,7 +743,7 @@
         if not last:
             new, *even, odd, new_fault = kernel_call(
                 step_kernel,
-                [field, half, half, plane, (32, lanes)],
+                [field, half, half, plane, (40, lanes)],
                 args,
                 unread=(len(args) - 1,) if step == 1 else (),
                 **static,

time: 35 us -> 33 us (0.943)
  waiting for transfers between devices: 5.49 us -> 4.24 us
  starting transfers between devices: 16 us -> 15.3 us
    ppermute x4, waiting for transfers between devices: 4.97 us -> 3.02 us  [from_behind(): lax.ppermute(block, axis, [((i - distance) % size, i) for i in range(size)])]
    ppermute x16, starting transfers between devices: 13 us -> 12.1 us  [swapped(): return lax.ppermute(block, ('dom', 'depth'), route)]
    ppermute x16, waiting for transfers between devices: 0.52 us -> 1.22 us  [swapped(): return lax.ppermute(block, ('dom', 'depth'), route)]
  transfers between devices with their start and end apart: 20 -> 20, of which waited for: 5 -> 7; matrix products, arithmetic and copies ran while one was open for 0% -> 0% of each run, Pallas kernels for 19% -> 20%
where the time goes in v7:
time: 33 us; the launch traced here: 32.9 us
  starting transfers between devices  15.3 us (46%)
  Pallas kernels  11.5 us (35%)
  waiting for transfers between devices  4.24 us (13%)
  between operations  0.73 us (2%)
  other arithmetic  0.57 us (2%)
  local copies, waits for them, and re-layouts  0.53 us (2%)
    ppermute x16, starting transfers between devices, swapped(): return lax.ppermute(block, ('dom', 'depth'), route)  12.1 us
    pallas_call x13, Pallas kernels, kernel_call(): pl.pallas_call(functools.partial(body, **static) if static else body, out...  11.5 us
    ppermute x4, starting transfers between devices, from_behind(): lax.ppermute(block, axis, [((i - distance) % size, i) for i in range(size)])  3.28 us
    ppermute x4, waiting for transfers between devices, from_behind(): lax.ppermute(block, axis, [((i - distance) % size, i) for i in range(size)])  3.02 us
    ppermute x16, waiting for transfers between devices, swapped(): return lax.ppermute(block, ('dom', 'depth'), route)  1.22 us
  transfers between devices with their start and end apart: 20, of which 7 were waited for; matrix products, arithmetic and copies ran while one was open for 0% of the time, Pallas kernels for 20%

profile of v7, /device:TPU:0, one launch (start us, length us, event | category | flops | bytes accessed | tf_op | source)
XLA Modules:
  0.0 32.9 jit_solution(3202320574916358069)
XLA Ops:
  0.6 2.0 %shard_map.166 = (f32[320,128]{1,0:T(8,128)S(1)}, f32[32,128]{1,0:T(8,128)S(1)}, f32[32,128]{1,0:T(8,128)S(1)}, f32[64,128]{1,0:T(8,128)S(1)}, f32[48,128]{1,0:T...) custom-call(f32[3,17,4,128]{3,2,1,0:T(4,128)} %bitcast.12, ...), custom_call_target="tpu_custom_call" | custom-call | tf_op jit(solution)/shard_map/pallas_call | solution.py:634
  2.6 3.0 %collective-permute-start = (f32[64,128]{1,0:T(8,128)S(1)}, f32[64,128]{1,0:T(8,128)S(1)}, u32[]{:S(2)}, u32[]{:S(2)}) collective-permute-start(f32[64,128]{1,0:T(8,128)S(1)} %get-tuple-element.55), channel_id=1, source_target_pairs={{0,1},{1,0},{2,4},{3,5},{4,2},{5,3},{6,8},{7,9},{8,6},{9,7},{10,12... | collective-permute-start | bytes 98312 | tf_op jit(solution)/shard_map/ppermute | solution.py:657
  5.7 1.3 %collective-permute-start.2 = (f32[32,128]{1,0:T(8,128)S(1)}, f32[32,128]{1,0:T(8,128)S(1)}, u32[]{:S(2)}, u32[]{:S(2)}) collective-permute-start(f32[32,128]{1,0:T(8,128)S(1)} %get-tuple-element.57), channel_id=1, source_target_pairs={{0,2},{1,3},{2,0},{3,1},{4,6},{5,7},{6,4},{7,5},{8,10},{9,11},{10,... | collective-permute-start | bytes 49160 | tf_op jit(solution)/shard_map/ppermute | solution.py:657
  7.0 1.6 %shard_map.167 = (f32[320,128]{1,0:T(8,128)S(1)}, f32[320,128]{1,0:T(8,128)S(1)}, f32[16,128]{1,0:T(8,128)S(1)}) custom-call(f32[3,17,4,128]{3,2,1,0:T(4,128)} %bitcast.13, f32[17,4,128]{2,1,0:T(4,128)} %bitcast.15, s32[4,4,128]{2,1,0:T(4,128)} %bitcast.17, f32[4,128]{1,0:T(4,128)} %bitcast.21, f32[320,128]{1,0:T(8,128)} %constant.17.clone.mass_hbm), custom_call_target="tpu_custom_call" | custom-call | tf_op jit(solution)/shard_map/pallas_call | solution.py:634
  9.4 0.9 %shard_map.169 = (f32[320,128]{1,0:T(8,128)S(1)}, f32[32,128]{1,0:T(8,128)S(1)}, f32[32,128]{1,0:T(8,128)S(1)}, f32[64,128]{1,0:T(8,128)S(1)}, f32[40,128]{1,0:T(8,128)S(1)}) custom-call(f32[320,128]{1,0:T(8,128)S(1)} %get-tuple-element.47.cur_ref.refs_0_.refs_1_, f32[320,128]{1,0:T(8,128)S(1)} %get-tuple-element.48.refs_1_, ...), custom_call_target="tpu_custom_call" | custom-call | tf_op jit(solution)/shard_map/pallas_call | solution.py:634
  10.4 0.9 %collective-permute-start.4 = (f32[64,128]{1,0:T(8,128)S(1)}, f32[64,128]{1,0:T(8,128)S(1)}, u32[]{:S(2)}, u32[]{:S(2)}) collective-permute-start(f32[64,128]{1,0:T(8,128)S(1)} %get-tuple-element.64), channel_id=1, source_target_pairs={{0,1},{1,0},{2,4},{3,5},{4,2},{5,3},{6,8},{7,9},{8,6},{9,7},{10,12... | collective-permute-start | bytes 98312 | tf_op jit(solution)/shard_map/ppermute | solution.py:657
  11.3 1.2 %collective-permute-start.5 = (f32[40,128]{1,0:T(8,128)S(1)}, f32[40,128]{1,0:T(8,128)S(1)}, u32[]{:S(2)}, u32[]{:S(2)}) collective-permute-start(f32[40,128]{1,0:T(8,128)S(1)} %get-tuple-element.65.refs_11_.refs_5_), channel_id=1, source_target_pairs={{1,0},{0,1},{3,2},{2,3},{5,4},{4,5},{7,6},{6,7},{9,8},{8,9},{11,10... | collective-permute-start | bytes 61448 | tf_op jit(solution)/shard_map/ppermute | solution.py:662
  13.5 0.5 %copy-done = bf16[512,512]{1,0:T(8,128)(2,1)S(1)} copy-done((bf16[512,512]{1,0:T(8,128)(2,1)S(1)}, bf16[512,512]{1,0:T(8,128)(2,1)}, u32[]{:S(2)}) %copy-start) | copy-done | bytes 524312
  14.0 0.6 %shard_map.171.refs_15_.refs_0_ = f32[64,128]{1,0:T(8,128)S(1)} custom-call(s32[1,4]{1,0:T(1,128)S(1)} %copy-done.1, f32[320,128]{1,0:T(8,128)S(1)} %get-tuple-element.61.cur_ref._.refs_0_.refs_1_, bf16[512,512]{1,0:T(8,128)(2,1)S(1)} %copy-done), custom_call_target="tpu_custom_call" | custom-call | tf_op jit(solution)/shard_map/pallas_call | solution.py:634
  15.0 0.9 %shard_map.172 = (f32[320,128]{1,0:T(8,128)S(1)}, f32[32,128]{1,0:T(8,128)S(1)}, f32[32,128]{1,0:T(8,128)S(1)}, f32[64,128]{1,0:T(8,128)S(1)}, f32[40,128]{1,0:T(8,128)S(1)}) custom-call(f32[320,128]{1,0:T(8,128)S(1)} %get-tuple-element.61.cur_ref._.refs_0_.refs_1_, f32[320,128]{1,0:T(8,128)S(1)} %get-tuple-element.47.cur_ref.refs_0_.refs_1_, ...), custom_call_target="tpu_custom_call" | custom-call | tf_op jit(solution)/shard_map/pallas_call | solution.py:634
  16.0 1.2 %collective-permute-start.8 = (f32[64,128]{1,0:T(8,128)S(1)}, f32[64,128]{1,0:T(8,128)S(1)}, u32[]{:S(2)}, u32[]{:S(2)}) collective-permute-start(f32[64,128]{1,0:T(8,128)S(1)} %get-tuple-element.71), channel_id=1, source_target_pairs={{0,1},{1,0},{2,4},{3,5},{4,2},{5,3},{6,8},{7,9},{8,6},{9,7},{10,12... | collective-permute-start | bytes 98312 | tf_op jit(solution)/shard_map/ppermute | solution.py:657
  17.2 0.9 %collective-permute-start.9 = (f32[40,128]{1,0:T(8,128)S(1)}, f32[40,128]{1,0:T(8,128)S(1)}, u32[]{:S(2)}, u32[]{:S(2)}) collective-permute-start(f32[40,128]{1,0:T(8,128)S(1)} %get-tuple-element.72.refs_11_.refs_7_), channel_id=1, source_target_pairs={{1,0},{0,1},{3,2},{2,3},{5,4},{4,5},{7,6},{6,7},{9,8},{8,9},{11,10... | collective-permute-start | bytes 61448 | tf_op jit(solution)/shard_map/ppermute | solution.py:662
  19.4 1.6 %collective-permute-done.9.refs_7_.refs_8_ = f32[40,128]{1,0:T(8,128)S(1)} collective-permute-done((f32[40,128]{1,0:T(8,128)S(1)}, f32[40,128]{1,0:T(8,128)S(1)}, u32[]{:S(2)}, u32[]{:S(2)}) %collective-permute-start.9) | collective-permute-done | bytes 20512 | tf_op jit(solution)/shard_map/ppermute | solution.py:662
  21.0 0.9 %shard_map.174 = (f32[320,128]{1,0:T(8,128)S(1)}, f32[32,128]{1,0:T(8,128)S(1)}, f32[32,128]{1,0:T(8,128)S(1)}, f32[64,128]{1,0:T(8,128)S(1)}, f32[40,128]{1,0:T(8,128)S(1)}) custom-call(f32[320,128]{1,0:T(8,128)S(1)} %get-tuple-element.68.cur_ref.refs_0_.refs_1_, f32[320,128]{1,0:T(8,128)S(1)} %get-tuple-element.61.cur_ref._.refs_0_.refs_1_, ...), custom_call_target="tpu_custom_call" | custom-call | tf_op jit(solution)/shard_map/pallas_call | solution.py:634
  21.9 0.9 %collective-permute-start.12 = (f32[64,128]{1,0:T(8,128)S(1)}, f32[64,128]{1,0:T(8,128)S(1)}, u32[]{:S(2)}, u32[]{:S(2)}) collective-permute-start(f32[64,128]{1,0:T(8,128)S(1)} %get-tuple-element.78), channel_id=1, source_target_pairs={{0,1},{1,0},{2,4},{3,5},{4,2},{5,3},{6,8},{7,9},{8,6},{9,7},{10,12... | collective-permute-start | bytes 98312 | tf_op jit(solution)/shard_map/ppermute | solution.py:657
  22.8 1.2 %collective-permute-start.13 = (f32[40,128]{1,0:T(8,128)S(1)}, f32[40,128]{1,0:T(8,128)S(1)}, u32[]{:S(2)}, u32[]{:S(2)}) collective-permute-start(f32[40,128]{1,0:T(8,128)S(1)} %get-tuple-element.79.refs_9_.refs_11_), channel_id=1, source_target_pairs={{1,0},{0,1},{3,2},{2,3},{5,4},{4,5},{7,6},{6,7},{9,8},{8,9},{11,10... | collective-permute-start | bytes 61448 | tf_op jit(solution)/shard_map/ppermute | solution.py:662
  25.0 1.0 %shard_map.176 = (f32[3,17,4,128]{3,2,1,0:T(4,128)}, f32[32,128]{1,0:T(8,128)S(1)}, bf16[128,128]{1,0:T(8,128)(2,1)S(1)}) custom-call(f32[320,128]{1,0:T(8,128)S(1)} %get-tuple-element.75.cur_ref.refs_0_, bf16[512,512]{1,0:T(8,128)(2,1)S(1)} %copy-done, f32[16,128]{1,0:T(8,128)S(1)} %get-tuple-element.82.refs_2_.refs_1_, ...), custom_call_target="tpu_custom_call" | custom-call | tf_op jit(solution)/shard_map/pallas_call | solution.py:634
  25.9 0.6 %collective-permute-done.13.refs_5_.refs_7_ = f32[40,128]{1,0:T(8,128)S(1)} collective-permute-done((f32[40,128]{1,0:T(8,128)S(1)}, f32[40,128]{1,0:T(8,128)S(1)}, u32[]{:S(2)}, u32[]{:S(2)}) %collective-permute-start.13) | collective-permute-done | bytes 20512 | tf_op jit(solution)/shard_map/ppermute | solution.py:662
  26.7 1.2 %collective-permute-start.16 = (f32[2,128]{1,0:T(2,128)S(1)}, f32[2,128]{1,0:T(2,128)S(1)}, u32[]{:S(2)}, u32[]{:S(2)}) collective-permute-start(f32[2,128]{1,0:T(2,128)S(1)} %get-tuple-element.87), channel_id=1, source_target_pairs={{0,1},{1,0},{2,4},{3,5},{4,2},{5,3},{6,8},{7,9},{8,6},{9,7},{10,12... | collective-permute-start | bytes 3080 | tf_op jit(solution)/shard_map/ppermute | solution.py:657
  27.9 0.8 %collective-permute-start.17 = (f32[2,128]{1,0:T(2,128)S(1)}, f32[2,128]{1,0:T(2,128)S(1)}, u32[]{:S(2)}, u32[]{:S(2)}) collective-permute-start(f32[2,128]{1,0:T(2,128)S(1)} %get-tuple-element.88), channel_id=1, source_target_pairs={{0,1},{1,0},{2,3},{3,2},{4,8},{5,9},{6,10},{7,11},{8,4},{9,5},{10,... | collective-permute-start | bytes 3080 | tf_op jit(solution)/shard_map/ppermute | solution.py:657
  28.7 1.3 %collective-permute-start.18 = (f32[2,128]{1,0:T(2,128)S(1)}, f32[2,128]{1,0:T(2,128)S(1)}, u32[]{:S(2)}, u32[]{:S(2)}) collective-permute-start(f32[2,128]{1,0:T(2,128)S(1)} %get-tuple-element.89), channel_id=1, source_target_pairs={{0,4},{1,5},{2,6},{3,7},{4,0},{5,1},{6,2},{7,3},{8,12},{9,13},{10,... | collective-permute-start | bytes 3080 | tf_op jit(solution)/shard_map/ppermute | solution.py:657
  30.0 1.4 %shard_map.178 = f32[3,17,4,128]{3,2,1,0:T(4,128)} custom-call(f32[320,128]{1,0:T(8,128)S(1)} %get-tuple-element.75.cur_ref.refs_0_, f32[320,128]{1,0:T(8,128)S(1)} %get-tuple-element.68.cur_ref.refs_0_.refs_1_, f32[320,128]{1,0:T(8,128)S(1)} %get-tuple-element.49.refs_2_, f32[320,128]{1,0:T(8,128)S(1)} %get-tuple-element.76.refs_3_, ...), custom_call_target="tpu_custom_call" | custom-call | tf_op jit(solution)/shard_map/pallas_call | solution.py:634
  31.5 0.8 %collective-permute-done.18 = f32[2,128]{1,0:T(2,128)S(1)} collective-permute-done((f32[2,128]{1,0:T(2,128)S(1)}, f32[2,128]{1,0:T(2,128)S(1)}, u32[]{:S(2)}, u32[]{:S(2)}) %collective-permute-start.18) | collective-permute-done | bytes 1056 | tf_op jit(solution)/shard_map/ppermute | solution.py:657
  32.3 0.6 %add_bitcast_fusion = f32[1,2,128]{2,1,0:T(2,128)} fusion(f32[2,128]{1,0:T(2,128)S(1)} %collective-permute-done.19, f32[2,128]{1,0:T(2,128)S(1)} %collective-permute-done.18, f32[2,128]{1,0:T(2,128)S(1)} %collective-permute-done.17, f32[2,128]{1,0:T(2,128)S(1)} %get-tuple-element.85.refs_15_, f32[2,128]{1,0:T(2,128)S(1)} %collective-permute-done.16), kind=kLoop, calls=%fused_computation | loop fusion | flops 1024 | bytes 6144 | tf_op jit(solution)/shard_map/broadcast_in_dim | solution.py:789
  (34 shorter events, 5.0 us)
Async XLA Ops:
  2.6 6.8 %collective-permute-start = (f32[64,128]{1,0:T(8,128)S(1)}, f32[64,128]{1,0:T(8,128)S(1)}, u32[]{:S(2)}, u32[]{:S(2)}) collective-permute-start(f32[64,128]{1,0:T(8,128)S(1)} %get-tuple-element.55), channel_id=1, source_target_pairs={{0,1},{1,0},{2,4},{3,5},{4,2},{5,3},{6,8},{7,9},{8,6},{9,7},{10,12... | collective-permute-start | bytes 98312 | tf_op jit(solution)/shard_map/ppermute | solution.py:657
  5.6 3.8 %collective-permute-start.1 = (f32[48,128]{1,0:T(8,128)S(1)}, f32[48,128]{1,0:T(8,128)S(1)}, u32[]{:S(2)}, u32[]{:S(2)}) collective-permute-start(f32[48,128]{1,0:T(8,128)S(1)} %get-tuple-element.56.refs_11_.refs_12_.refs_3_), channel_id=1, source_target_pairs={{1,0},{0,1},{3,2},{2,3},{5,4},{4,5},{7,6},{6,7},{9,8},{8,9},{11,10... | collective-permute-start | bytes 73736 | tf_op jit(solution)/shard_map/ppermute | solution.py:662
  5.7 3.4 %collective-permute-start.2 = (f32[32,128]{1,0:T(8,128)S(1)}, f32[32,128]{1,0:T(8,128)S(1)}, u32[]{:S(2)}, u32[]{:S(2)}) collective-permute-start(f32[32,128]{1,0:T(8,128)S(1)} %get-tuple-element.57), channel_id=1, source_target_pairs={{0,2},{1,3},{2,0},{3,1},{4,6},{5,7},{6,4},{7,5},{8,10},{9,11},{10,... | collective-permute-start | bytes 49160 | tf_op jit(solution)/shard_map/ppermute | solution.py:657
  7.0 2.1 %collective-permute-start.3 = (f32[32,128]{1,0:T(8,128)S(1)}, f32[32,128]{1,0:T(8,128)S(1)}, u32[]{:S(2)}, u32[]{:S(2)}) collective-permute-start(f32[32,128]{1,0:T(8,128)S(1)} %get-tuple-element.58), channel_id=1, source_target_pairs={{0,2},{1,3},{2,0},{3,1},{4,6},{5,7},{6,4},{7,5},{8,10},{9,11},{10,... | collective-permute-start | bytes 49160 | tf_op jit(solution)/shard_map/ppermute | solution.py:657
  10.4 4.6 %collective-permute-start.4 = (f32[64,128]{1,0:T(8,128)S(1)}, f32[64,128]{1,0:T(8,128)S(1)}, u32[]{:S(2)}, u32[]{:S(2)}) collective-permute-start(f32[64,128]{1,0:T(8,128)S(1)} %get-tuple-element.64), channel_id=1, source_target_pairs={{0,1},{1,0},{2,4},{3,5},{4,2},{5,3},{6,8},{7,9},{8,6},{9,7},{10,12... | collective-permute-start | bytes 98312 | tf_op jit(solution)/shard_map/ppermute | solution.py:657
  11.3 3.8 %collective-permute-start.5 = (f32[40,128]{1,0:T(8,128)S(1)}, f32[40,128]{1,0:T(8,128)S(1)}, u32[]{:S(2)}, u32[]{:S(2)}) collective-permute-start(f32[40,128]{1,0:T(8,128)S(1)} %get-tuple-element.65.refs_11_.refs_5_), channel_id=1, source_target_pairs={{1,0},{0,1},{3,2},{2,3},{5,4},{4,5},{7,6},{6,7},{9,8},{8,9},{11,10... | collective-permute-start | bytes 61448 | tf_op jit(solution)/shard_map/ppermute | solution.py:662
  12.4 2.1 %collective-permute-start.6 = (f32[32,128]{1,0:T(8,128)S(1)}, f32[32,128]{1,0:T(8,128)S(1)}, u32[]{:S(2)}, u32[]{:S(2)}) collective-permute-start(f32[32,128]{1,0:T(8,128)S(1)} %get-tuple-element.66), channel_id=1, source_target_pairs={{0,2},{1,3},{2,0},{3,1},{4,6},{5,7},{6,4},{7,5},{8,10},{9,11},{10,... | collective-permute-start | bytes 49160 | tf_op jit(solution)/shard_map/ppermute | solution.py:657
  12.4 2.1 %collective-permute-start.7 = (f32[32,128]{1,0:T(8,128)S(1)}, f32[32,128]{1,0:T(8,128)S(1)}, u32[]{:S(2)}, u32[]{:S(2)}) collective-permute-start(f32[32,128]{1,0:T(8,128)S(1)} %get-tuple-element.67), channel_id=1, source_target_pairs={{0,2},{1,3},{2,0},{3,1},{4,6},{5,7},{6,4},{7,5},{8,10},{9,11},{10,... | collective-permute-start | bytes 49160 | tf_op jit(solution)/shard_map/ppermute | solution.py:657
  12.9 1.0 %copy-start = (bf16[512,512]{1,0:T(8,128)(2,1)S(1)}, bf16[512,512]{1,0:T(8,128)(2,1)}, u32[]{:S(2)}) copy-start(bf16[512,512]{1,0:T(8,128)(2,1)} %constant.16.clone.back_ref.refs_1_.refs_16_) | copy-start | bytes 1572868
  12.9 1.0 %copy-start.1 = (s32[1,4]{1,0:T(1,128)S(1)}, s32[1,4]{1,0:T(1,128)}, u32[]{:S(2)}) copy-start(s32[1,4]{1,0:T(1,128)} %owner_ref.1) | copy-start | bytes 52
  16.0 5.0 %collective-permute-start.8 = (f32[64,128]{1,0:T(8,128)S(1)}, f32[64,128]{1,0:T(8,128)S(1)}, u32[]{:S(2)}, u32[]{:S(2)}) collective-permute-start(f32[64,128]{1,0:T(8,128)S(1)} %get-tuple-element.71), channel_id=1, source_target_pairs={{0,1},{1,0},{2,4},{3,5},{4,2},{5,3},{6,8},{7,9},{8,6},{9,7},{10,12... | collective-permute-start | bytes 98312 | tf_op jit(solution)/shard_map/ppermute | solution.py:657
  17.2 3.8 %collective-permute-start.9 = (f32[40,128]{1,0:T(8,128)S(1)}, f32[40,128]{1,0:T(8,128)S(1)}, u32[]{:S(2)}, u32[]{:S(2)}) collective-permute-start(f32[40,128]{1,0:T(8,128)S(1)} %get-tuple-element.72.refs_11_.refs_7_), channel_id=1, source_target_pairs={{1,0},{0,1},{3,2},{2,3},{5,4},{4,5},{7,6},{6,7},{9,8},{8,9},{11,10... | collective-permute-start | bytes 61448 | tf_op jit(solution)/shard_map/ppermute | solution.py:662
  18.0 1.2 %collective-permute-start.10 = (f32[32,128]{1,0:T(8,128)S(1)}, f32[32,128]{1,0:T(8,128)S(1)}, u32[]{:S(2)}, u32[]{:S(2)}) collective-permute-start(f32[32,128]{1,0:T(8,128)S(1)} %get-tuple-element.73), channel_id=1, source_target_pairs={{0,2},{1,3},{2,0},{3,1},{4,6},{5,7},{6,4},{7,5},{8,10},{9,11},{10,... | collective-permute-start | bytes 49160 | tf_op jit(solution)/shard_map/ppermute | solution.py:657
  18.0 1.3 %collective-permute-start.11 = (f32[32,128]{1,0:T(8,128)S(1)}, f32[32,128]{1,0:T(8,128)S(1)}, u32[]{:S(2)}, u32[]{:S(2)}) collective-permute-start(f32[32,128]{1,0:T(8,128)S(1)} %get-tuple-element.74), channel_id=1, source_target_pairs={{0,2},{1,3},{2,0},{3,1},{4,6},{5,7},{6,4},{7,5},{8,10},{9,11},{10,... | collective-permute-start | bytes 49160 | tf_op jit(solution)/shard_map/ppermute | solution.py:657
  21.9 4.7 %collective-permute-start.12 = (f32[64,128]{1,0:T(8,128)S(1)}, f32[64,128]{1,0:T(8,128)S(1)}, u32[]{:S(2)}, u32[]{:S(2)}) collective-permute-start(f32[64,128]{1,0:T(8,128)S(1)} %get-tuple-element.78), channel_id=1, source_target_pairs={{0,1},{1,0},{2,4},{3,5},{4,2},{5,3},{6,8},{7,9},{8,6},{9,7},{10,12... | collective-permute-start | bytes 98312 | tf_op jit(solution)/shard_map/ppermute | solution.py:657
  22.8 3.8 %collective-permute-start.13 = (f32[40,128]{1,0:T(8,128)S(1)}, f32[40,128]{1,0:T(8,128)S(1)}, u32[]{:S(2)}, u32[]{:S(2)}) collective-permute-start(f32[40,128]{1,0:T(8,128)S(1)} %get-tuple-element.79.refs_9_.refs_11_), channel_id=1, source_target_pairs={{1,0},{0,1},{3,2},{2,3},{5,4},{4,5},{7,6},{6,7},{9,8},{8,9},{11,10... | collective-permute-start | bytes 61448 | tf_op jit(solution)/shard_map/ppermute | solution.py:662
  23.9 2.0 %collective-permute-start.14 = (f32[32,128]{1,0:T(8,128)S(1)}, f32[32,128]{1,0:T(8,128)S(1)}, u32[]{:S(2)}, u32[]{:S(2)}) collective-permute-start(f32[32,128]{1,0:T(8,128)S(1)} %get-tuple-element.80), channel_id=1, source_target_pairs={{0,2},{1,3},{2,0},{3,1},{4,6},{5,7},{6,4},{7,5},{8,10},{9,11},{10,... | collective-permute-start | bytes 49160 | tf_op jit(solution)/shard_map/ppermute | solution.py:657
  23.9 2.0 %collective-permute-start.15 = (f32[32,128]{1,0:T(8,128)S(1)}, f32[32,128]{1,0:T(8,128)S(1)}, u32[]{:S(2)}, u32[]{:S(2)}) collective-permute-start(f32[32,128]{1,0:T(8,128)S(1)} %get-tuple-element.81), channel_id=1, source_target_pairs={{0,2},{1,3},{2,0},{3,1},{4,6},{5,7},{6,4},{7,5},{8,10},{9,11},{10,... | collective-permute-start | bytes 49160 | tf_op jit(solution)/shard_map/ppermute | solution.py:657
  26.7 4.7 %collective-permute-start.16 = (f32[2,128]{1,0:T(2,128)S(1)}, f32[2,128]{1,0:T(2,128)S(1)}, u32[]{:S(2)}, u32[]{:S(2)}) collective-permute-start(f32[2,128]{1,0:T(2,128)S(1)} %get-tuple-element.87), channel_id=1, source_target_pairs={{0,1},{1,0},{2,4},{3,5},{4,2},{5,3},{6,8},{7,9},{8,6},{9,7},{10,12... | collective-permute-start | bytes 3080 | tf_op jit(solution)/shard_map/ppermute | solution.py:657
  27.9 3.6 %collective-permute-start.17 = (f32[2,128]{1,0:T(2,128)S(1)}, f32[2,128]{1,0:T(2,128)S(1)}, u32[]{:S(2)}, u32[]{:S(2)}) collective-permute-start(f32[2,128]{1,0:T(2,128)S(1)} %get-tuple-element.88), channel_id=1, source_target_pairs={{0,1},{1,0},{2,3},{3,2},{4,8},{5,9},{6,10},{7,11},{8,4},{9,5},{10,... | collective-permute-start | bytes 3080 | tf_op jit(solution)/shard_map/ppermute | solution.py:657
  28.7 3.6 %collective-permute-start.18 = (f32[2,128]{1,0:T(2,128)S(1)}, f32[2,128]{1,0:T(2,128)S(1)}, u32[]{:S(2)}, u32[]{:S(2)}) collective-permute-start(f32[2,128]{1,0:T(2,128)S(1)} %get-tuple-element.89), channel_id=1, source_target_pairs={{0,4},{1,5},{2,6},{3,7},{4,0},{5,1},{6,2},{7,3},{8,12},{9,13},{10,... | collective-permute-start | bytes 3080 | tf_op jit(solution)/shard_map/ppermute | solution.py:657
  30.0 2.3 %collective-permute-start.19 = (f32[2,128]{1,0:T(2,128)S(1)}, f32[2,128]{1,0:T(2,128)S(1)}, u32[]{:S(2)}, u32[]{:S(2)}) collective-permute-start(f32[2,128]{1,0:T(2,128)S(1)} %get-tuple-element.90), channel_id=1, source_target_pairs={{0,2},{1,3},{2,0},{3,1},{4,6},{5,7},{6,4},{7,5},{8,10},{9,11},{10,... | collective-permute-start | bytes 3080 | tf_op jit(solution)/shard_map/ppermute | solution.py:657

commit v8 on v7

--- a/solution.py
+++ b/solution.py
@@ -13,6 +13,7 @@
 PATCH_DEV = 2
 REACH = 2
 PATCH_ROWS = 16
+LATER = 7
 
 time_step = 0.01
 lock_stiffness = 0.5
@@ -200,7 +201,6 @@
 
 def to_elements(native, scratch, table, y_elems, parts=3):
     group = 4 * BLOCK
-    scratch[...] = jnp.zeros_like(scratch)
     for c in range(3):
         for y in range(4 * y_elems + 1):
             rows = native(c, y)
@@ -336,49 +336,43 @@
     weak_hbm,
     lame_hbm,
     shear_hbm,
-    edge_hbm,
-    own_hbm,
-    far_hbm,
-    touch_hbm,
-    cur_ref,
-    even_ref,
-    even_rest,
-    odd_ref,
-    fault_out_ref,
-    material_ref,
-    edge_ref,
-    own_ref,
-    far_ref,
-    touch_ref,
-    scratch,
-    now_ref,
-    flags_ref,
-    weak_ref,
-    lame_ref,
-    shear_ref,
-    sems,
+    *refs,
 ):
+    later_hbm, refs = refs[:LATER], refs[LATER:]
+    cur_ref, even_ref, even_rest, odd_ref, fault_out_ref, material_ref = refs[:6]
+    later_refs, refs = refs[6 : 6 + LATER], refs[6 + LATER :]
+    scratch, now_ref, flags_ref, weak_ref, lame_ref, shear_ref, sems = refs
     copies = start_copies(
         [
-            (now_hbm, now_ref),
             (flags_hbm, flags_ref),
             (weak_hbm, weak_ref),
             (lame_hbm, lame_ref),
             (shear_hbm, shear_ref),
-            (edge_hbm, edge_ref),
-            (own_hbm, own_ref),
-            (far_hbm, far_ref),
-            (touch_hbm, touch_ref),
-        ],
+            (now_hbm, now_ref),
+        ]
+        + list(zip(later_hbm, later_refs)),
         sems,
     )
+    edge_ref = later_refs[0]
     y_elems, z_elems = lame_ref.shape
     lanes = y_elems * z_elems
     parity = lax.axis_index("dom") % 2
     gather = gather_table(lanes, z_elems)
     fault = fault_table(lanes, z_elems)
-    copies[1].wait()
-    copies[2].wait()
+    scratch[...] = jnp.zeros_like(scratch)
+    for copy in copies[:6]:
+        copy.wait()
+    cur = to_elements(lambda c, y: now_ref[c, y], scratch, gather, y_elems)
+    cur_ref[...] = cur
+    lame_row, shear_row = material_rows(lame_ref, shear_ref)
+    material_ref[...] = jnp.concatenate(
+        [lame_row, shear_row, jnp.zeros((6, lanes), jnp.float32)], axis=0
+    )
+    planes = [cur[x * PLANE : (x + 1) * PLANE] for x in range(4)]
+    edge = sum(dot(edge_ref[x], stacked(planes[x])) for x in range(4))
+    right = edge_message(edge, lame_row, shear_row, z_elems)
+    message, odd_ref[...] = select_messages(parity, cur[: 4 * BLOCK], right)
+    even_ref[...], even_rest[...] = message[: 2 * BLOCK], message[2 * BLOCK :]
     weak = weak_ref[...]
     tangent = []
     for i in range(flags_ref.shape[0]):
@@ -386,24 +380,9 @@
         tangent.append(
             jnp.where(flag == 0, lock_stiffness, jnp.where(flag == 1, -weak, 0.0))
         )
-    fault_out_ref[32:] = exact_dot(jnp.concatenate(tangent, axis=0), fault)
-    copies[3].wait()
-    copies[4].wait()
-    lame_row, shear_row = material_rows(lame_ref, shear_ref)
-    material_ref[...] = jnp.concatenate(
-        [lame_row, shear_row, jnp.zeros((6, lanes), jnp.float32)], axis=0
-    )
-    copies[0].wait()
-    cur = to_elements(lambda c, y: now_ref[c, y], scratch, gather, y_elems)
-    copies[5].wait()
-    planes = [cur[x * PLANE : (x + 1) * PLANE] for x in range(4)]
-    edge = sum(dot(edge_ref[x], stacked(planes[x])) for x in range(4))
-    right = edge_message(edge, lame_row, shear_row, z_elems)
-    message, odd_ref[...] = select_messages(parity, cur[: 4 * BLOCK], right)
-    even_ref[...], even_rest[...] = message[: 2 * BLOCK], message[2 * BLOCK :]
-    cur_ref[...] = cur
     for x in range(4):
         fault_out_ref[8 * x : 8 * x + 8] = fault_message(planes[x], z_elems)
+    fault_out_ref[32:] = exact_dot(jnp.concatenate(tangent, axis=0), fault)
     for copy in copies[6:]:
         copy.wait()
 
@@ -414,55 +393,16 @@
     edge_part_ref[...] = dot(touch_ref[...], stacked(cur[:PLANE]))
 
 
-def setup_kernel(
-    next_hbm,
-    density_hbm,
-    flags_hbm,
-    stress_hbm,
-    mass_hbm,
-    fol_ref,
-    minv_ref,
-    weight_ref,
-    scratch,
-    next_ref,
-    density_ref,
-    flags_ref,
-    stress_ref,
-    mass_ref,
-    sems,
-    *,
-    y_elems,
-    z_elems,
-):
-    copies = start_copies(
-        [
-            (next_hbm, next_ref),
-            (density_hbm, density_ref),
-            (flags_hbm, flags_ref),
-            (stress_hbm, stress_ref),
-            (mass_hbm, mass_ref),
-        ],
-        sems,
-    )
+def setup_kernel(next_ref, density_ref, mass_ref, fol_ref, minv_ref, scratch, *, y_elems, z_elems):
     gather = gather_table(y_elems * z_elems, z_elems)
-    fault = fault_table(y_elems * z_elems, z_elems)
-    for copy in copies[:5]:
-        copy.wait()
-    fol_ref[...] = to_elements(lambda c, y: next_ref[c, y], scratch, gather, y_elems)
-    density = to_elements(lambda c, y: density_ref[y], scratch, gather, y_elems, 2)
+    scratch[...] = jnp.zeros_like(scratch)
+    fol_ref[...] = to_elements(lambda c, y: next_ref[c, y], scratch.at[0], gather, y_elems)
+    density = to_elements(lambda c, y: density_ref[y], scratch.at[1], gather, y_elems, 2)
     table = mass_ref[...]
     first = lax.axis_index("dom") == 0
     plane = lax.broadcasted_iota(jnp.int32, table.shape, 0) < PLANE
     table = jnp.where(jnp.logical_and(first, plane), 2.0 * table, table)
     minv_ref[...] = jnp.where(table > 0.0, table / jnp.where(table > 0.0, density, 1.0), 0.0)
-    stress = stress_ref[...]
-    weights = []
-    for i in range(flags_ref.shape[0]):
-        flag = flags_ref[i]
-        weights.append(
-            stress * jnp.where(flag == 1, 0.5, jnp.where(flag == 2, 1.0, 0.0))
-        )
-    weight_ref[...] = exact_dot(jnp.concatenate(weights, axis=0), fault)
 
 
 def fault_input(up_ref, down_ref, count):
@@ -564,13 +504,22 @@
         even_out[...], even_rest[...] = message[: 2 * BLOCK], message[2 * BLOCK :]
 
 
-def mask_kernel(owner_ref, _, back_ref, mask_ref):
+def mask_kernel(owner_ref, _, back_ref, flags_ref, stress_ref, mask_ref, weight_ref, *, z_elems):
     shape = (PATCH_ROWS, mask_ref.shape[1])
     first = (lax.axis_index("dom") - REACH) * PATCH_DEV
     number = lax.broadcasted_iota(jnp.int32, shape, 0) + first
     for x in range(4):
         mask = jnp.where(number == owner_ref[0, x], 1.0, 0.0)
         mask_ref[PATCH_ROWS * x : PATCH_ROWS * (x + 1)] = mask
+    stress = stress_ref[...]
+    weights = []
+    for i in range(flags_ref.shape[0]):
+        flag = flags_ref[i]
+        weights.append(
+            stress * jnp.where(flag == 1, 0.5, jnp.where(flag == 2, 1.0, 0.0))
+        )
+    fault = fault_table(mask_ref.shape[1], z_elems)
+    weight_ref[...] = exact_dot(jnp.concatenate(weights, axis=0), fault)
 
 
 def output_kernel(*refs, pair, steps, y_elems, z_elems):
@@ -697,25 +646,24 @@
             faults = [from_behind(fault_rows, "depth", 1), from_behind(fault_rows, "depth", -1)]
         return [swapped(part, 1, 0) for part in even], swapped(odd, 1, 1), faults
 
-    tables = (edge_table, own_table, far_table, touch_table)
-    cur, *even, odd, fault_rows, material, edge_table, own_table, far_table, touch_table = kernel_call(
+    later_used = (edge_table, following, rho, mass, own_table, far_table, touch_table)
+    assert len(later_used) == LATER
+    cur, *even, odd, fault_rows, material, edge_table, following, rho, mass, own_table, far_table, touch_table = kernel_call(
         first_kernel,
         [field, half, half, plane, (32 + 4 * steps, lanes), (8, lanes)]
-        + [(t.shape, t.dtype) for t in tables],
-        (now, flags, weak_slope[0], lame_first[0], shear_modulus[0]) + tables,
+        + [(t.shape, t.dtype) for t in later_used],
+        (now, flags, weak_slope[0], lame_first[0], shear_modulus[0]) + later_used,
         scratch=[native],
-        in_hbm=range(9),
-        kept=range(5, 9),
-    )
-    first_fault = fault_rows
+        in_hbm=range(5 + LATER),
+        kept=range(5, 5 + LATER),
+    )
     even_in, odd_in, fault_in = exchange(even, odd, fault_rows)
-    first_in = fault_in
-    fol, minv, weight = kernel_call(
+    first_fault, first_in = fault_rows, fault_in
+    fol, minv = kernel_call(
         setup_kernel,
-        [field, field, (4 * steps, lanes)],
-        (following, rho, flags, normal_stress[0], mass),
-        scratch=[native],
-        in_hbm=range(5),
+        [field, field],
+        (following, rho, mass),
+        scratch=[pltpu.VMEM((2, y_elems, 4 * BLOCK, lanes), jnp.float32)],
         y_elems=y_elems,
         z_elems=z_elems,
     )
@@ -736,9 +684,14 @@
             z_elems=z_elems,
         )
         if step == 1:
-            mask = kernel_call(
-                mask_kernel, [(4 * PATCH_ROWS, lanes)], [patch_owner, cur, back], (0,), unread=(1,)
-            )[0]
+            mask, weight = kernel_call(
+                mask_kernel,
+                [(4 * PATCH_ROWS, lanes), (4 * steps, lanes)],
+                [patch_owner, cur, back, flags, normal_stress[0]],
+                (0,),
+                unread=(1,),
+                z_elems=z_elems,
+            )
             args.append(mask)
         if not last:
             new, *even, odd, new_fault = kernel_call(

time: 33 us -> 33 us (level)
  Pallas kernels: 11.5 us -> 10.6 us
  starting transfers between devices: 15.3 us -> 15.8 us
    pallas_call x13, Pallas kernels: 11.5 us -> 10.6 us  [kernel_call(): pl.pallas_call(functools.partial(body, **static) if static else body, out...]
    ppermute x4, starting transfers between devices: 3.28 us -> 3.78 us  [from_behind(): lax.ppermute(block, axis, [((i - distance) % size, i) for i in range(size)])]
    ppermute x4, waiting for transfers between devices: 3.02 us -> 3.48 us  [from_behind(): lax.ppermute(block, axis, [((i - distance) % size, i) for i in range(size)])]
    unnamed x4 -> x8, local copies, waits for them, and re-layouts: 0.53 us -> 0.69 us
  transfers between devices with their start and end apart: 20 -> 20, of which waited for: 7 -> 7; matrix products, arithmetic and copies ran while one was open for 0% -> 0% of each run, Pallas kernels for 20% -> 17%
where the time goes in v8:
time: 33 us; the launch traced here: 32.8 us
  starting transfers between devices  15.8 us (48%)
  Pallas kernels  10.6 us (32%)
  waiting for transfers between devices  4.4 us (13%)
  between operations  0.73 us (2%)
  local copies, waits for them, and re-layouts  0.69 us (2%)
  other arithmetic  0.57 us (2%)
    ppermute x16, starting transfers between devices, swapped(): return lax.ppermute(block, ('dom', 'depth'), route)  12 us
    pallas_call x13, Pallas kernels, kernel_call(): pl.pallas_call(functools.partial(body, **static) if static else body, out...  10.6 us
    ppermute x4, starting transfers between devices, from_behind(): lax.ppermute(block, axis, [((i - distance) % size, i) for i in range(size)])  3.78 us
    ppermute x4, waiting for transfers between devices, from_behind(): lax.ppermute(block, axis, [((i - distance) % size, i) for i in range(size)])  3.48 us
    ppermute x16, waiting for transfers between devices, swapped(): return lax.ppermute(block, ('dom', 'depth'), route)  0.92 us
    unnamed x8, local copies, waits for them, and re-layouts  0.69 us
  transfers between devices with their start and end apart: 20, of which 7 were waited for; matrix products, arithmetic and copies ran while one was open for 0% of the time, Pallas kernels for 17%

profile of v8, /device:TPU:0, one launch (start us, length us, event | category | flops | bytes accessed | tf_op | source)
XLA Modules:
  0.0 32.8 jit_solution(224802083699236904)
XLA Ops:
  0.6 2.0 %shard_map.166 = (f32[320,128]{1,0:T(8,128)S(1)}, f32[32,128]{1,0:T(8,128)S(1)}, f32[32,128]{1,0:T(8,128)S(1)}, f32[64,128]{1,0:T(8,128)S(1)}, f32[48,128]{1,0:T...) custom-call(f32[3,17,4,128]{3,2,1,0:T(4,128)} %bitcast.15, ...), custom_call_target="tpu_custom_call" | custom-call | tf_op jit(solution)/shard_map/pallas_call | solution.py:583
  2.7 3.0 %collective-permute-start = (f32[64,128]{1,0:T(8,128)S(1)}, f32[64,128]{1,0:T(8,128)S(1)}, u32[]{:S(2)}, u32[]{:S(2)}) collective-permute-start(f32[64,128]{1,0:T(8,128)S(1)} %get-tuple-element.62), channel_id=1, source_target_pairs={{0,1},{1,0},{2,4},{3,5},{4,2},{5,3},{6,8},{7,9},{8,6},{9,7},{10,12... | collective-permute-start | bytes 98312 | tf_op jit(solution)/shard_map/ppermute | solution.py:606
  5.8 1.3 %collective-permute-start.2 = (f32[32,128]{1,0:T(8,128)S(1)}, f32[32,128]{1,0:T(8,128)S(1)}, u32[]{:S(2)}, u32[]{:S(2)}) collective-permute-start(f32[32,128]{1,0:T(8,128)S(1)} %get-tuple-element.64), channel_id=1, source_target_pairs={{0,2},{1,3},{2,0},{3,1},{4,6},{5,7},{6,4},{7,5},{8,10},{9,11},{10,... | collective-permute-start | bytes 49160 | tf_op jit(solution)/shard_map/ppermute | solution.py:606
  7.0 0.5 %shard_map.167 = (f32[320,128]{1,0:T(8,128)S(1)}, f32[320,128]{1,0:T(8,128)S(1)}) custom-call(f32[3,17,4,128]{3,2,1,0:T(4,128)S(1)} %get-tuple-element.52.next_ref, f32[17,4,128]{2,1,0:T(4,128)S(1)} %get-tuple-element.53.density_ref, f32[320,128]{1,0:T(8,128)S(1)} %get-tuple-element.54.mass_ref), custom_call_target="tpu_custom_call" | custom-call | tf_op jit(solution)/shard_map/pallas_call | solution.py:583
  7.6 0.5 %shard_map.168 = (f32[320,128]{1,0:T(8,128)S(1)}, f32[160,128]{1,0:T(8,128)S(1)}) custom-call(f32[320,128]{1,0:T(8,128)S(1)} %get-tuple-element.51.cur_ref.refs_0_.refs_1_, f32[8,128]{1,0:T(8,128)S(1)} %get-tuple-element.57.material_ref.refs_5_, bf16[2,640,384]{2,1,0:T(8,128)(2,1)S(1)} %get-tuple-element.58.own_ref, ...), custom_call_target="tpu_custom_call" | custom-call | tf_op jit(solution)/shard_map/pallas_call | solution.py:583
  8.2 1.3 %collective-permute-done.1.refs_7_.refs_10_.refs_4_ = f32[48,128]{1,0:T(8,128)S(1)} collective-permute-done((f32[48,128]{1,0:T(8,128)S(1)}, f32[48,128]{1,0:T(8,128)S(1)}, u32[]{:S(2)}, u32[]{:S(2)}) %collective-permute-start.1) | collective-permute-done | bytes 24608 | tf_op jit(solution)/shard_map/ppermute | solution.py:611
  9.5 0.9 %shard_map.169 = (f32[320,128]{1,0:T(8,128)S(1)}, f32[32,128]{1,0:T(8,128)S(1)}, f32[32,128]{1,0:T(8,128)S(1)}, f32[64,128]{1,0:T(8,128)S(1)}, f32[40,128]{1,0:T(8,128)S(1)}) custom-call(f32[320,128]{1,0:T(8,128)S(1)} %get-tuple-element.51.cur_ref.refs_0_.refs_1_, f32[320,128]{1,0:T(8,128)S(1)} %get-tuple-element.55.refs_1_, ...), custom_call_target="tpu_custom_call" | custom-call | tf_op jit(solution)/shard_map/pallas_call | solution.py:583
  10.8 1.7 %collective-permute-start.5 = (f32[40,128]{1,0:T(8,128)S(1)}, f32[40,128]{1,0:T(8,128)S(1)}, u32[]{:S(2)}, u32[]{:S(2)}) collective-permute-start(f32[40,128]{1,0:T(8,128)S(1)} %get-tuple-element.72.refs_11_.refs_5_), channel_id=1, source_target_pairs={{1,0},{0,1},{3,2},{2,3},{5,4},{4,5},{7,6},{6,7},{9,8},{8,9},{11,10... | collective-permute-start | bytes 61448 | tf_op jit(solution)/shard_map/ppermute | solution.py:611
  13.5 0.5 %copy-done = bf16[512,512]{1,0:T(8,128)(2,1)S(1)} copy-done((bf16[512,512]{1,0:T(8,128)(2,1)S(1)}, bf16[512,512]{1,0:T(8,128)(2,1)}, u32[]{:S(2)}) %copy-start) | copy-done | bytes 524312
  14.2 0.7 %shard_map.171 = (f32[64,128]{1,0:T(8,128)S(1)}, f32[16,128]{1,0:T(8,128)S(1)}) custom-call(s32[1,4]{1,0:T(1,128)S(1)} %copy-done.3, f32[320,128]{1,0:T(8,128)S(1)} %get-tuple-element.68.cur_ref._.refs_0_.refs_1_, bf16[512,512]{1,0:T(8,128)(2,1)S(1)} %copy-done, s32[4,4,128]{2,1,0:T(4,128)S(1)} %bitcast.13, f32[4,128]{1,0:T(4,128)S(1)} %bitcast.14), custom_call_target="tpu_custom_call" | custom-call | tf_op jit(solution)/shard_map/pallas_call | solution.py:583
  14.9 1.0 %shard_map.172 = (f32[320,128]{1,0:T(8,128)S(1)}, f32[32,128]{1,0:T(8,128)S(1)}, f32[32,128]{1,0:T(8,128)S(1)}, f32[64,128]{1,0:T(8,128)S(1)}, f32[40,128]{1,0:T(8,128)S(1)}) custom-call(f32[320,128]{1,0:T(8,128)S(1)} %get-tuple-element.68.cur_ref._.refs_0_.refs_1_, f32[320,128]{1,0:T(8,128)S(1)} %get-tuple-element.51.cur_ref.refs_0_.refs_1_, ...), custom_call_target="tpu_custom_call" | custom-call | tf_op jit(solution)/shard_map/pallas_call | solution.py:583
  15.9 1.3 %collective-permute-start.8 = (f32[64,128]{1,0:T(8,128)S(1)}, f32[64,128]{1,0:T(8,128)S(1)}, u32[]{:S(2)}, u32[]{:S(2)}) collective-permute-start(f32[64,128]{1,0:T(8,128)S(1)} %get-tuple-element.79), channel_id=1, source_target_pairs={{0,1},{1,0},{2,4},{3,5},{4,2},{5,3},{6,8},{7,9},{8,6},{9,7},{10,12... | collective-permute-start | bytes 98312 | tf_op jit(solution)/shard_map/ppermute | solution.py:606
  17.2 0.7 %collective-permute-start.9 = (f32[40,128]{1,0:T(8,128)S(1)}, f32[40,128]{1,0:T(8,128)S(1)}, u32[]{:S(2)}, u32[]{:S(2)}) collective-permute-start(f32[40,128]{1,0:T(8,128)S(1)} %get-tuple-element.80.refs_11_.refs_7_), channel_id=1, source_target_pairs={{1,0},{0,1},{3,2},{2,3},{5,4},{4,5},{7,6},{6,7},{9,8},{8,9},{11,10... | collective-permute-start | bytes 61448 | tf_op jit(solution)/shard_map/ppermute | solution.py:611
  19.3 1.7 %collective-permute-done.9.refs_7_.refs_8_ = f32[40,128]{1,0:T(8,128)S(1)} collective-permute-done((f32[40,128]{1,0:T(8,128)S(1)}, f32[40,128]{1,0:T(8,128)S(1)}, u32[]{:S(2)}, u32[]{:S(2)}) %collective-permute-start.9) | collective-permute-done | bytes 20512 | tf_op jit(solution)/shard_map/ppermute | solution.py:611
  21.0 0.9 %shard_map.174 = (f32[320,128]{1,0:T(8,128)S(1)}, f32[32,128]{1,0:T(8,128)S(1)}, f32[32,128]{1,0:T(8,128)S(1)}, f32[64,128]{1,0:T(8,128)S(1)}, f32[40,128]{1,0:T(8,128)S(1)}) custom-call(f32[320,128]{1,0:T(8,128)S(1)} %get-tuple-element.76.cur_ref.refs_0_.refs_1_, f32[320,128]{1,0:T(8,128)S(1)} %get-tuple-element.68.cur_ref._.refs_0_.refs_1_, ...), custom_call_target="tpu_custom_call" | custom-call | tf_op jit(solution)/shard_map/pallas_call | solution.py:583
  22.0 0.7 %collective-permute-start.12 = (f32[64,128]{1,0:T(8,128)S(1)}, f32[64,128]{1,0:T(8,128)S(1)}, u32[]{:S(2)}, u32[]{:S(2)}) collective-permute-start(f32[64,128]{1,0:T(8,128)S(1)} %get-tuple-element.86), channel_id=1, source_target_pairs={{0,1},{1,0},{2,4},{3,5},{4,2},{5,3},{6,8},{7,9},{8,6},{9,7},{10,12... | collective-permute-start | bytes 98312 | tf_op jit(solution)/shard_map/ppermute | solution.py:606
  22.7 1.3 %collective-permute-start.13 = (f32[40,128]{1,0:T(8,128)S(1)}, f32[40,128]{1,0:T(8,128)S(1)}, u32[]{:S(2)}, u32[]{:S(2)}) collective-permute-start(f32[40,128]{1,0:T(8,128)S(1)} %get-tuple-element.87.refs_9_.refs_11_), channel_id=1, source_target_pairs={{1,0},{0,1},{3,2},{2,3},{5,4},{4,5},{7,6},{6,7},{9,8},{8,9},{11,10... | collective-permute-start | bytes 61448 | tf_op jit(solution)/shard_map/ppermute | solution.py:611
  24.5 0.5 %shard_map.175 = (f32[320,128]{1,0:T(8,128)S(1)}, f32[160,128]{1,0:T(8,128)S(1)}) custom-call(f32[320,128]{1,0:T(8,128)S(1)} %get-tuple-element.83.cur_ref.refs_0_, f32[8,128]{1,0:T(8,128)S(1)} %get-tuple-element.57.material_ref.refs_5_, bf16[2,640,384]{2,1,0:T(8,128)(2,1)S(1)} %get-tuple-element.58.own_ref, bf16[160,256]{1,0:T(8,128)(2,1)S(1)} %get-tuple-element.59.touch_ref), custom_call_target="tpu_custom_call" | custom-call | tf_op jit(solution)/shard_map/pallas_call | solution.py:583
  25.0 1.0 %shard_map.176 = (f32[3,17,4,128]{3,2,1,0:T(4,128)}, f32[32,128]{1,0:T(8,128)S(1)}, bf16[128,128]{1,0:T(8,128)(2,1)S(1)}) custom-call(f32[320,128]{1,0:T(8,128)S(1)} %get-tuple-element.83.cur_ref.refs_0_, bf16[512,512]{1,0:T(8,128)(2,1)S(1)} %copy-done, f32[16,128]{1,0:T(8,128)S(1)} %get-tuple-element.90.refs_2_.refs_1_, ...), custom_call_target="tpu_custom_call" | custom-call | tf_op jit(solution)/shard_map/pallas_call | solution.py:583
  26.6 1.3 %collective-permute-start.16 = (f32[2,128]{1,0:T(2,128)S(1)}, f32[2,128]{1,0:T(2,128)S(1)}, u32[]{:S(2)}, u32[]{:S(2)}) collective-permute-start(f32[2,128]{1,0:T(2,128)S(1)} %get-tuple-element.95), channel_id=1, source_target_pairs={{0,1},{1,0},{2,4},{3,5},{4,2},{5,3},{6,8},{7,9},{8,6},{9,7},{10,12... | collective-permute-start | bytes 3080 | tf_op jit(solution)/shard_map/ppermute | solution.py:606
  27.9 0.7 %collective-permute-start.17 = (f32[2,128]{1,0:T(2,128)S(1)}, f32[2,128]{1,0:T(2,128)S(1)}, u32[]{:S(2)}, u32[]{:S(2)}) collective-permute-start(f32[2,128]{1,0:T(2,128)S(1)} %get-tuple-element.96), channel_id=1, source_target_pairs={{0,1},{1,0},{2,3},{3,2},{4,8},{5,9},{6,10},{7,11},{8,4},{9,5},{10,... | collective-permute-start | bytes 3080 | tf_op jit(solution)/shard_map/ppermute | solution.py:606
  28.6 1.7 %collective-permute-start.18 = (f32[2,128]{1,0:T(2,128)S(1)}, f32[2,128]{1,0:T(2,128)S(1)}, u32[]{:S(2)}, u32[]{:S(2)}) collective-permute-start(f32[2,128]{1,0:T(2,128)S(1)} %get-tuple-element.97), channel_id=1, source_target_pairs={{0,4},{1,5},{2,6},{3,7},{4,0},{5,1},{6,2},{7,3},{8,12},{9,13},{10,... | collective-permute-start | bytes 3080 | tf_op jit(solution)/shard_map/ppermute | solution.py:606
  30.4 1.4 %shard_map.178 = f32[3,17,4,128]{3,2,1,0:T(4,128)} custom-call(f32[320,128]{1,0:T(8,128)S(1)} %get-tuple-element.83.cur_ref.refs_0_, f32[320,128]{1,0:T(8,128)S(1)} %get-tuple-element.76.cur_ref.refs_0_.refs_1_, f32[320,128]{1,0:T(8,128)S(1)} %get-tuple-element.56.refs_2_, f32[320,128]{1,0:T(8,128)S(1)} %get-tuple-element.84.refs_3_, ...), custom_call_target="tpu_custom_call" | custom-call | tf_op jit(solution)/shard_map/pallas_call | solution.py:583
  32.2 0.6 %add_bitcast_fusion = f32[1,2,128]{2,1,0:T(2,128)} fusion(f32[2,128]{1,0:T(2,128)S(1)} %collective-permute-done.19, f32[2,128]{1,0:T(2,128)S(1)} %collective-permute-done.18, f32[2,128]{1,0:T(2,128)S(1)} %collective-permute-done.17, f32[2,128]{1,0:T(2,128)S(1)} %get-tuple-element.93.refs_15_, f32[2,128]{1,0:T(2,128)S(1)} %collective-permute-done.16), kind=kLoop, calls=%fused_computation | loop fusion | flops 1024 | bytes 6144 | tf_op jit(solution)/shard_map/broadcast_in_dim | solution.py:742
  (38 shorter events, 4.7 us)
Async XLA Ops:
  2.7 6.8 %collective-permute-start = (f32[64,128]{1,0:T(8,128)S(1)}, f32[64,128]{1,0:T(8,128)S(1)}, u32[]{:S(2)}, u32[]{:S(2)}) collective-permute-start(f32[64,128]{1,0:T(8,128)S(1)} %get-tuple-element.62), channel_id=1, source_target_pairs={{0,1},{1,0},{2,4},{3,5},{4,2},{5,3},{6,8},{7,9},{8,6},{9,7},{10,12... | collective-permute-start | bytes 98312 | tf_op jit(solution)/shard_map/ppermute | solution.py:606
  5.7 3.8 %collective-permute-start.1 = (f32[48,128]{1,0:T(8,128)S(1)}, f32[48,128]{1,0:T(8,128)S(1)}, u32[]{:S(2)}, u32[]{:S(2)}) collective-permute-start(f32[48,128]{1,0:T(8,128)S(1)} %get-tuple-element.63.refs_11_.refs_12_.refs_3_), channel_id=1, source_target_pairs={{1,0},{0,1},{3,2},{2,3},{5,4},{4,5},{7,6},{6,7},{9,8},{8,9},{11,10... | collective-permute-start | bytes 73736 | tf_op jit(solution)/shard_map/ppermute | solution.py:611
  5.8 2.3 %collective-permute-start.2 = (f32[32,128]{1,0:T(8,128)S(1)}, f32[32,128]{1,0:T(8,128)S(1)}, u32[]{:S(2)}, u32[]{:S(2)}) collective-permute-start(f32[32,128]{1,0:T(8,128)S(1)} %get-tuple-element.64), channel_id=1, source_target_pairs={{0,2},{1,3},{2,0},{3,1},{4,6},{5,7},{6,4},{7,5},{8,10},{9,11},{10,... | collective-permute-start | bytes 49160 | tf_op jit(solution)/shard_map/ppermute | solution.py:606
  7.0 1.2 %collective-permute-start.3 = (f32[32,128]{1,0:T(8,128)S(1)}, f32[32,128]{1,0:T(8,128)S(1)}, u32[]{:S(2)}, u32[]{:S(2)}) collective-permute-start(f32[32,128]{1,0:T(8,128)S(1)} %get-tuple-element.65), channel_id=1, source_target_pairs={{0,2},{1,3},{2,0},{3,1},{4,6},{5,7},{6,4},{7,5},{8,10},{9,11},{10,... | collective-permute-start | bytes 49160 | tf_op jit(solution)/shard_map/ppermute | solution.py:606
  10.5 4.5 %collective-permute-start.4 = (f32[64,128]{1,0:T(8,128)S(1)}, f32[64,128]{1,0:T(8,128)S(1)}, u32[]{:S(2)}, u32[]{:S(2)}) collective-permute-start(f32[64,128]{1,0:T(8,128)S(1)} %get-tuple-element.71), channel_id=1, source_target_pairs={{0,1},{1,0},{2,4},{3,5},{4,2},{5,3},{6,8},{7,9},{8,6},{9,7},{10,12... | collective-permute-start | bytes 98312 | tf_op jit(solution)/shard_map/ppermute | solution.py:606
  10.8 4.1 %collective-permute-start.5 = (f32[40,128]{1,0:T(8,128)S(1)}, f32[40,128]{1,0:T(8,128)S(1)}, u32[]{:S(2)}, u32[]{:S(2)}) collective-permute-start(f32[40,128]{1,0:T(8,128)S(1)} %get-tuple-element.72.refs_11_.refs_5_), channel_id=1, source_target_pairs={{1,0},{0,1},{3,2},{2,3},{5,4},{4,5},{7,6},{6,7},{9,8},{8,9},{11,10... | collective-permute-start | bytes 61448 | tf_op jit(solution)/shard_map/ppermute | solution.py:611
  12.5 2.4 %collective-permute-start.6 = (f32[32,128]{1,0:T(8,128)S(1)}, f32[32,128]{1,0:T(8,128)S(1)}, u32[]{:S(2)}, u32[]{:S(2)}) collective-permute-start(f32[32,128]{1,0:T(8,128)S(1)} %get-tuple-element.73), channel_id=1, source_target_pairs={{0,2},{1,3},{2,0},{3,1},{4,6},{5,7},{6,4},{7,5},{8,10},{9,11},{10,... | collective-permute-start | bytes 49160 | tf_op jit(solution)/shard_map/ppermute | solution.py:606
  12.5 2.4 %collective-permute-start.7 = (f32[32,128]{1,0:T(8,128)S(1)}, f32[32,128]{1,0:T(8,128)S(1)}, u32[]{:S(2)}, u32[]{:S(2)}) collective-permute-start(f32[32,128]{1,0:T(8,128)S(1)} %get-tuple-element.74), channel_id=1, source_target_pairs={{0,2},{1,3},{2,0},{3,1},{4,6},{5,7},{6,4},{7,5},{8,10},{9,11},{10,... | collective-permute-start | bytes 49160 | tf_op jit(solution)/shard_map/ppermute | solution.py:606
  13.0 1.0 %copy-start = (bf16[512,512]{1,0:T(8,128)(2,1)S(1)}, bf16[512,512]{1,0:T(8,128)(2,1)}, u32[]{:S(2)}) copy-start(bf16[512,512]{1,0:T(8,128)(2,1)} %constant.16.clone.back_ref.refs_1_.refs_16_) | copy-start | bytes 1572868
  13.0 1.0 %copy-start.1 = (s32[4,1,4,128]{3,2,1,0:T(4,128)S(1)}, s32[4,1,4,128]{3,2,1,0:T(4,128)}, u32[]{:S(2)}) copy-start(s32[4,1,4,128]{3,2,1,0:T(4,128)} %param.20) | copy-start | bytes 24580
  13.0 1.0 %copy-start.2 = (f32[1,4,128]{2,1,0:T(4,128)S(1)}, f32[1,4,128]{2,1,0:T(4,128)}, u32[]{:S(2)}) copy-start(f32[1,4,128]{2,1,0:T(4,128)} %param.22) | copy-start | bytes 6148
  13.5 0.7 %copy-start.3 = (s32[1,4]{1,0:T(1,128)S(1)}, s32[1,4]{1,0:T(1,128)}, u32[]{:S(2)}) copy-start(s32[1,4]{1,0:T(1,128)} %owner_ref.1) | copy-start | bytes 52
  15.9 5.1 %collective-permute-start.8 = (f32[64,128]{1,0:T(8,128)S(1)}, f32[64,128]{1,0:T(8,128)S(1)}, u32[]{:S(2)}, u32[]{:S(2)}) collective-permute-start(f32[64,128]{1,0:T(8,128)S(1)} %get-tuple-element.79), channel_id=1, source_target_pairs={{0,1},{1,0},{2,4},{3,5},{4,2},{5,3},{6,8},{7,9},{8,6},{9,7},{10,12... | collective-permute-start | bytes 98312 | tf_op jit(solution)/shard_map/ppermute | solution.py:606
  17.2 3.8 %collective-permute-start.9 = (f32[40,128]{1,0:T(8,128)S(1)}, f32[40,128]{1,0:T(8,128)S(1)}, u32[]{:S(2)}, u32[]{:S(2)}) collective-permute-start(f32[40,128]{1,0:T(8,128)S(1)} %get-tuple-element.80.refs_11_.refs_7_), channel_id=1, source_target_pairs={{1,0},{0,1},{3,2},{2,3},{5,4},{4,5},{7,6},{6,7},{9,8},{8,9},{11,10... | collective-permute-start | bytes 61448 | tf_op jit(solution)/shard_map/ppermute | solution.py:611
  17.9 1.2 %collective-permute-start.10 = (f32[32,128]{1,0:T(8,128)S(1)}, f32[32,128]{1,0:T(8,128)S(1)}, u32[]{:S(2)}, u32[]{:S(2)}) collective-permute-start(f32[32,128]{1,0:T(8,128)S(1)} %get-tuple-element.81), channel_id=1, source_target_pairs={{0,2},{1,3},{2,0},{3,1},{4,6},{5,7},{6,4},{7,5},{8,10},{9,11},{10,... | collective-permute-start | bytes 49160 | tf_op jit(solution)/shard_map/ppermute | solution.py:606
  17.9 1.3 %collective-permute-start.11 = (f32[32,128]{1,0:T(8,128)S(1)}, f32[32,128]{1,0:T(8,128)S(1)}, u32[]{:S(2)}, u32[]{:S(2)}) collective-permute-start(f32[32,128]{1,0:T(8,128)S(1)} %get-tuple-element.82), channel_id=1, source_target_pairs={{0,2},{1,3},{2,0},{3,1},{4,6},{5,7},{6,4},{7,5},{8,10},{9,11},{10,... | collective-permute-start | bytes 49160 | tf_op jit(solution)/shard_map/ppermute | solution.py:606
  22.0 4.5 %collective-permute-start.12 = (f32[64,128]{1,0:T(8,128)S(1)}, f32[64,128]{1,0:T(8,128)S(1)}, u32[]{:S(2)}, u32[]{:S(2)}) collective-permute-start(f32[64,128]{1,0:T(8,128)S(1)} %get-tuple-element.86), channel_id=1, source_target_pairs={{0,1},{1,0},{2,4},{3,5},{4,2},{5,3},{6,8},{7,9},{8,6},{9,7},{10,12... | collective-permute-start | bytes 98312 | tf_op jit(solution)/shard_map/ppermute | solution.py:606
  22.7 3.8 %collective-permute-start.13 = (f32[40,128]{1,0:T(8,128)S(1)}, f32[40,128]{1,0:T(8,128)S(1)}, u32[]{:S(2)}, u32[]{:S(2)}) collective-permute-start(f32[40,128]{1,0:T(8,128)S(1)} %get-tuple-element.87.refs_9_.refs_11_), channel_id=1, source_target_pairs={{1,0},{0,1},{3,2},{2,3},{5,4},{4,5},{7,6},{6,7},{9,8},{8,9},{11,10... | collective-permute-start | bytes 61448 | tf_op jit(solution)/shard_map/ppermute | solution.py:611
  24.0 2.0 %collective-permute-start.14 = (f32[32,128]{1,0:T(8,128)S(1)}, f32[32,128]{1,0:T(8,128)S(1)}, u32[]{:S(2)}, u32[]{:S(2)}) collective-permute-start(f32[32,128]{1,0:T(8,128)S(1)} %get-tuple-element.88), channel_id=1, source_target_pairs={{0,2},{1,3},{2,0},{3,1},{4,6},{5,7},{6,4},{7,5},{8,10},{9,11},{10,... | collective-permute-start | bytes 49160 | tf_op jit(solution)/shard_map/ppermute | solution.py:606
  24.0 2.0 %collective-permute-start.15 = (f32[32,128]{1,0:T(8,128)S(1)}, f32[32,128]{1,0:T(8,128)S(1)}, u32[]{:S(2)}, u32[]{:S(2)}) collective-permute-start(f32[32,128]{1,0:T(8,128)S(1)} %get-tuple-element.89), channel_id=1, source_target_pairs={{0,2},{1,3},{2,0},{3,1},{4,6},{5,7},{6,4},{7,5},{8,10},{9,11},{10,... | collective-permute-start | bytes 49160 | tf_op jit(solution)/shard_map/ppermute | solution.py:606
  26.6 5.2 %collective-permute-start.16 = (f32[2,128]{1,0:T(2,128)S(1)}, f32[2,128]{1,0:T(2,128)S(1)}, u32[]{:S(2)}, u32[]{:S(2)}) collective-permute-start(f32[2,128]{1,0:T(2,128)S(1)} %get-tuple-element.95), channel_id=1, source_target_pairs={{0,1},{1,0},{2,4},{3,5},{4,2},{5,3},{6,8},{7,9},{8,6},{9,7},{10,12... | collective-permute-start | bytes 3080 | tf_op jit(solution)/shard_map/ppermute | solution.py:606
  27.9 3.8 %collective-permute-start.17 = (f32[2,128]{1,0:T(2,128)S(1)}, f32[2,128]{1,0:T(2,128)S(1)}, u32[]{:S(2)}, u32[]{:S(2)}) collective-permute-start(f32[2,128]{1,0:T(2,128)S(1)} %get-tuple-element.96), channel_id=1, source_target_pairs={{0,1},{1,0},{2,3},{3,2},{4,8},{5,9},{6,10},{7,11},{8,4},{9,5},{10,... | collective-permute-start | bytes 3080 | tf_op jit(solution)/shard_map/ppermute | solution.py:606
  28.6 3.6 %collective-permute-start.18 = (f32[2,128]{1,0:T(2,128)S(1)}, f32[2,128]{1,0:T(2,128)S(1)}, u32[]{:S(2)}, u32[]{:S(2)}) collective-permute-start(f32[2,128]{1,0:T(2,128)S(1)} %get-tuple-element.97), channel_id=1, source_target_pairs={{0,4},{1,5},{2,6},{3,7},{4,0},{5,1},{6,2},{7,3},{8,12},{9,13},{10,... | collective-permute-start | bytes 3080 | tf_op jit(solution)/shard_map/ppermute | solution.py:606
  30.4 1.8 %collective-permute-start.19 = (f32[2,128]{1,0:T(2,128)S(1)}, f32[2,128]{1,0:T(2,128)S(1)}, u32[]{:S(2)}, u32[]{:S(2)}) collective-permute-start(f32[2,128]{1,0:T(2,128)S(1)} %get-tuple-element.98), channel_id=1, source_target_pairs={{0,2},{1,3},{2,0},{3,1},{4,6},{5,7},{6,4},{7,5},{8,10},{9,11},{10,... | collective-permute-start | bytes 3080 | tf_op jit(solution)/shard_map/ppermute | solution.py:606

commit v9 on v8

--- a/solution.py
+++ b/solution.py
@@ -98,15 +98,18 @@
     planes = [slice(x * PLANE, (x + 1) * PLANE) for x in range(5)]
     inner = np.concatenate([w[:own, :own] for w in wide])
 
-    def three(rows, columns):
-        high, low = two_parts(np.concatenate([w[rows, columns] for w in wide]))
+    def three(table):
+        high, low = two_parts(table)
         return padded_table(np.concatenate([high, low, high], axis=1), 256)
+
+    def both(rows, columns):
+        return three(np.concatenate([w[rows, columns] for w in wide]))
 
     return (
         two_parts(padded_table(inner, OWN_COLS)),
-        np.stack([three(planes[x], planes[4]) for x in range(4)]),
-        np.stack([three(planes[4], planes[x]) for x in range(4)]),
-        three(planes[4], planes[4]),
+        np.concatenate([three(w[:own, planes[4]]) for w in wide], axis=1),
+        np.concatenate([both(planes[4], planes[x]) for x in range(4)], axis=1),
+        both(planes[4], planes[4]),
     )
 
 
@@ -369,7 +372,7 @@
         [lame_row, shear_row, jnp.zeros((6, lanes), jnp.float32)], axis=0
     )
     planes = [cur[x * PLANE : (x + 1) * PLANE] for x in range(4)]
-    edge = sum(dot(edge_ref[x], stacked(planes[x])) for x in range(4))
+    edge = dot(edge_ref[...], jnp.concatenate([stacked(p) for p in planes], axis=0))
     right = edge_message(edge, lame_row, shear_row, z_elems)
     message, odd_ref[...] = select_messages(parity, cur[: 4 * BLOCK], right)
     even_ref[...], even_rest[...] = message[: 2 * BLOCK], message[2 * BLOCK :]
@@ -433,8 +436,9 @@
     below = jnp.where(
         lane_wide % z_elems != z_elems - 1, pltpu.roll(far[:BLOCK], lanes - 1, 1), 0.0
     )
-    far = stacked(jnp.concatenate([far, below], axis=0))
+    far = jnp.concatenate([far, below], axis=0)
     lame_row, shear_row = material_ref[0:1], material_ref[1:2]
+    far = jnp.concatenate([stacked(lame_row * far), stacked(shear_row * far)], axis=0)
     left_lame = left[BLOCK - 1 : BLOCK]
     left_shear = left[2 * BLOCK - 1 : 2 * BLOCK]
     from_left = left_lame * touch_ref[:PLANE] + left_shear * touch_ref[PLANE:]
@@ -450,11 +454,9 @@
     if not last:
         fault_out[32:] = jnp.zeros_like(fault_out[32:])
     planes = []
-    edge = 0.0
     for x in range(4):
         rows = slice(x * PLANE, (x + 1) * PLANE)
-        result = dot(far_ref[x], far)
-        force = base_ref[rows] + (lame_row * result[:PLANE] + shear_row * result[PLANE:])
+        force = base_ref[rows] + dot(far_ref[rows], far)
         blocks = [force[zl * BLOCK : (zl + 1) * BLOCK] for zl in range(5)]
         if x == 0:
             blocks = [b + from_left[i * BLOCK : (i + 1) * BLOCK] for i, b in enumerate(blocks)]
@@ -493,12 +495,13 @@
         else:
             new_ref[rows] = plane
             fault_out[at] = fault_message(plane, z_elems)
-            edge = edge + dot(edge_ref[x], stacked(plane))
+            planes.append(stacked(plane))
             if x == 0:
                 first = plane[: 4 * BLOCK]
     if last:
         from_elements(jnp.concatenate(planes, axis=0), scratch, back_ref, out_ref, y_elems)
     else:
+        edge = dot(edge_ref[...], jnp.concatenate(planes, axis=0))
         right = edge_message(edge, lame_row, shear_row, z_elems)
         message, odd_out[...] = select_messages(place % 2, first, right)
         even_out[...], even_rest[...] = message[: 2 * BLOCK], message[2 * BLOCK :]

time: 33 us -> 32.7 us (level)
  no operation moved by 1% of the time
where the time goes in v9:
time: 32.7 us; the launch traced here: 32.5 us
  starting transfers between devices  15.8 us (48%)
  Pallas kernels  10.3 us (31%)
  waiting for transfers between devices  4.37 us (13%)
  between operations  0.73 us (2%)
  local copies, waits for them, and re-layouts  0.69 us (2%)
  other arithmetic  0.57 us (2%)
    ppermute x16, starting transfers between devices, swapped(): return lax.ppermute(block, ('dom', 'depth'), route)  12 us
    pallas_call x13, Pallas kernels, kernel_call(): pl.pallas_call(functools.partial(body, **static) if static else body, out...  10.3 us
    ppermute x4, starting transfers between devices, from_behind(): lax.ppermute(block, axis, [((i - distance) % size, i) for i in range(size)])  3.78 us
    ppermute x4, waiting for transfers between devices, from_behind(): lax.ppermute(block, axis, [((i - distance) % size, i) for i in range(size)])  3.47 us
    ppermute x16, waiting for transfers between devices, swapped(): return lax.ppermute(block, ('dom', 'depth'), route)  0.89 us
    unnamed x8, local copies, waits for them, and re-layouts  0.69 us
  transfers between devices with their start and end apart: 20, of which 7 were waited for; matrix products, arithmetic and copies ran while one was open for 0% of the time, Pallas kernels for 17%

profile of v9, /device:TPU:0, one launch (start us, length us, event | category | flops | bytes accessed | tf_op | source)
XLA Modules:
  0.0 32.5 jit_solution(13910694997955882004)
XLA Ops:
  0.6 2.0 %shard_map.166 = (f32[320,128]{1,0:T(8,128)S(1)}, f32[32,128]{1,0:T(8,128)S(1)}, f32[32,128]{1,0:T(8,128)S(1)}, f32[64,128]{1,0:T(8,128)S(1)}, f32[48,128]{1,0:T...) custom-call(f32[3,17,4,128]{3,2,1,0:T(4,128)} %bitcast.15, ...), custom_call_target="tpu_custom_call" | custom-call | tf_op jit(solution)/shard_map/pallas_call | solution.py:586
  2.7 3.0 %collective-permute-start = (f32[64,128]{1,0:T(8,128)S(1)}, f32[64,128]{1,0:T(8,128)S(1)}, u32[]{:S(2)}, u32[]{:S(2)}) collective-permute-start(f32[64,128]{1,0:T(8,128)S(1)} %get-tuple-element.62), channel_id=1, source_target_pairs={{0,1},{1,0},{2,4},{3,5},{4,2},{5,3},{6,8},{7,9},{8,6},{9,7},{10,12... | collective-permute-start | bytes 98312 | tf_op jit(solution)/shard_map/ppermute | solution.py:609
  5.8 1.3 %collective-permute-start.2 = (f32[32,128]{1,0:T(8,128)S(1)}, f32[32,128]{1,0:T(8,128)S(1)}, u32[]{:S(2)}, u32[]{:S(2)}) collective-permute-start(f32[32,128]{1,0:T(8,128)S(1)} %get-tuple-element.64), channel_id=1, source_target_pairs={{0,2},{1,3},{2,0},{3,1},{4,6},{5,7},{6,4},{7,5},{8,10},{9,11},{10,... | collective-permute-start | bytes 49160 | tf_op jit(solution)/shard_map/ppermute | solution.py:609
  7.0 0.5 %shard_map.167 = (f32[320,128]{1,0:T(8,128)S(1)}, f32[320,128]{1,0:T(8,128)S(1)}) custom-call(f32[3,17,4,128]{3,2,1,0:T(4,128)S(1)} %get-tuple-element.52.next_ref, f32[17,4,128]{2,1,0:T(4,128)S(1)} %get-tuple-element.53.density_ref, f32[320,128]{1,0:T(8,128)S(1)} %get-tuple-element.54.mass_ref), custom_call_target="tpu_custom_call" | custom-call | tf_op jit(solution)/shard_map/pallas_call | solution.py:586
  7.6 0.5 %shard_map.168 = (f32[320,128]{1,0:T(8,128)S(1)}, f32[160,128]{1,0:T(8,128)S(1)}) custom-call(f32[320,128]{1,0:T(8,128)S(1)} %get-tuple-element.51.cur_ref.refs_0_.refs_1_, f32[8,128]{1,0:T(8,128)S(1)} %get-tuple-element.57.material_ref.refs_5_, bf16[2,640,384]{2,1,0:T(8,128)(2,1)S(1)} %get-tuple-element.58.own_ref, ...), custom_call_target="tpu_custom_call" | custom-call | tf_op jit(solution)/shard_map/pallas_call | solution.py:586
  8.2 1.3 %collective-permute-done.1.refs_7_.refs_10_.refs_4_ = f32[48,128]{1,0:T(8,128)S(1)} collective-permute-done((f32[48,128]{1,0:T(8,128)S(1)}, f32[48,128]{1,0:T(8,128)S(1)}, u32[]{:S(2)}, u32[]{:S(2)}) %collective-permute-start.1) | collective-permute-done | bytes 24608 | tf_op jit(solution)/shard_map/ppermute | solution.py:614
  9.5 0.9 %shard_map.169 = (f32[320,128]{1,0:T(8,128)S(1)}, f32[32,128]{1,0:T(8,128)S(1)}, f32[32,128]{1,0:T(8,128)S(1)}, f32[64,128]{1,0:T(8,128)S(1)}, f32[40,128]{1,0:T(8,128)S(1)}) custom-call(f32[320,128]{1,0:T(8,128)S(1)} %get-tuple-element.51.cur_ref.refs_0_.refs_1_, f32[320,128]{1,0:T(8,128)S(1)} %get-tuple-element.55.refs_1_, ...), custom_call_target="tpu_custom_call" | custom-call | tf_op jit(solution)/shard_map/pallas_call | solution.py:586
  10.7 1.7 %collective-permute-start.5 = (f32[40,128]{1,0:T(8,128)S(1)}, f32[40,128]{1,0:T(8,128)S(1)}, u32[]{:S(2)}, u32[]{:S(2)}) collective-permute-start(f32[40,128]{1,0:T(8,128)S(1)} %get-tuple-element.72.refs_11_.refs_5_), channel_id=1, source_target_pairs={{1,0},{0,1},{3,2},{2,3},{5,4},{4,5},{7,6},{6,7},{9,8},{8,9},{11,10... | collective-permute-start | bytes 61448 | tf_op jit(solution)/shard_map/ppermute | solution.py:614
  12.9 0.5 %shard_map.170 = (f32[320,128]{1,0:T(8,128)S(1)}, f32[160,128]{1,0:T(8,128)S(1)}) custom-call(f32[320,128]{1,0:T(8,128)S(1)} %get-tuple-element.68.cur_ref._.refs_0_.refs_1_, f32[8,128]{1,0:T(8,128)S(1)} %get-tuple-element.57.material_ref.refs_5_, bf16[2,640,384]{2,1,0:T(8,128)(2,1)S(1)} %get-tuple-element.58.own_ref, ...), custom_call_target="tpu_custom_call" | custom-call | tf_op jit(solution)/shard_map/pallas_call | solution.py:586
  14.1 0.7 %shard_map.171 = (f32[64,128]{1,0:T(8,128)S(1)}, f32[16,128]{1,0:T(8,128)S(1)}) custom-call(s32[1,4]{1,0:T(1,128)S(1)} %copy-done.3, f32[320,128]{1,0:T(8,128)S(1)} %get-tuple-element.68.cur_ref._.refs_0_.refs_1_, bf16[512,512]{1,0:T(8,128)(2,1)S(1)} %copy-done, s32[4,4,128]{2,1,0:T(4,128)S(1)} %bitcast.13, f32[4,128]{1,0:T(4,128)S(1)} %bitcast.14), custom_call_target="tpu_custom_call" | custom-call | tf_op jit(solution)/shard_map/pallas_call | solution.py:586
  14.8 0.9 %shard_map.172 = (f32[320,128]{1,0:T(8,128)S(1)}, f32[32,128]{1,0:T(8,128)S(1)}, f32[32,128]{1,0:T(8,128)S(1)}, f32[64,128]{1,0:T(8,128)S(1)}, f32[40,128]{1,0:T(8,128)S(1)}) custom-call(f32[320,128]{1,0:T(8,128)S(1)} %get-tuple-element.68.cur_ref._.refs_0_.refs_1_, f32[320,128]{1,0:T(8,128)S(1)} %get-tuple-element.51.cur_ref.refs_0_.refs_1_, ...), custom_call_target="tpu_custom_call" | custom-call | tf_op jit(solution)/shard_map/pallas_call | solution.py:586
  15.7 1.3 %collective-permute-start.8 = (f32[64,128]{1,0:T(8,128)S(1)}, f32[64,128]{1,0:T(8,128)S(1)}, u32[]{:S(2)}, u32[]{:S(2)}) collective-permute-start(f32[64,128]{1,0:T(8,128)S(1)} %get-tuple-element.79), channel_id=1, source_target_pairs={{0,1},{1,0},{2,4},{3,5},{4,2},{5,3},{6,8},{7,9},{8,6},{9,7},{10,12... | collective-permute-start | bytes 98312 | tf_op jit(solution)/shard_map/ppermute | solution.py:609
  17.1 0.7 %collective-permute-start.9 = (f32[40,128]{1,0:T(8,128)S(1)}, f32[40,128]{1,0:T(8,128)S(1)}, u32[]{:S(2)}, u32[]{:S(2)}) collective-permute-start(f32[40,128]{1,0:T(8,128)S(1)} %get-tuple-element.80.refs_11_.refs_7_), channel_id=1, source_target_pairs={{1,0},{0,1},{3,2},{2,3},{5,4},{4,5},{7,6},{6,7},{9,8},{8,9},{11,10... | collective-permute-start | bytes 61448 | tf_op jit(solution)/shard_map/ppermute | solution.py:614
  18.3 0.5 %shard_map.173 = (f32[320,128]{1,0:T(8,128)S(1)}, f32[160,128]{1,0:T(8,128)S(1)}) custom-call(f32[320,128]{1,0:T(8,128)S(1)} %get-tuple-element.76.cur_ref.refs_0_.refs_1_, f32[8,128]{1,0:T(8,128)S(1)} %get-tuple-element.57.material_ref.refs_5_, bf16[2,640,384]{2,1,0:T(8,128)(2,1)S(1)} %get-tuple-element.58.own_ref, ...), custom_call_target="tpu_custom_call" | custom-call | tf_op jit(solution)/shard_map/pallas_call | solution.py:586
  19.1 1.7 %collective-permute-done.9.refs_7_.refs_8_ = f32[40,128]{1,0:T(8,128)S(1)} collective-permute-done((f32[40,128]{1,0:T(8,128)S(1)}, f32[40,128]{1,0:T(8,128)S(1)}, u32[]{:S(2)}, u32[]{:S(2)}) %collective-permute-start.9) | collective-permute-done | bytes 20512 | tf_op jit(solution)/shard_map/ppermute | solution.py:614
  20.8 0.8 %shard_map.174 = (f32[320,128]{1,0:T(8,128)S(1)}, f32[32,128]{1,0:T(8,128)S(1)}, f32[32,128]{1,0:T(8,128)S(1)}, f32[64,128]{1,0:T(8,128)S(1)}, f32[40,128]{1,0:T(8,128)S(1)}) custom-call(f32[320,128]{1,0:T(8,128)S(1)} %get-tuple-element.76.cur_ref.refs_0_.refs_1_, f32[320,128]{1,0:T(8,128)S(1)} %get-tuple-element.68.cur_ref._.refs_0_.refs_1_, ...), custom_call_target="tpu_custom_call" | custom-call | tf_op jit(solution)/shard_map/pallas_call | solution.py:586
  21.7 0.7 %collective-permute-start.12 = (f32[64,128]{1,0:T(8,128)S(1)}, f32[64,128]{1,0:T(8,128)S(1)}, u32[]{:S(2)}, u32[]{:S(2)}) collective-permute-start(f32[64,128]{1,0:T(8,128)S(1)} %get-tuple-element.86), channel_id=1, source_target_pairs={{0,1},{1,0},{2,4},{3,5},{4,2},{5,3},{6,8},{7,9},{8,6},{9,7},{10,12... | collective-permute-start | bytes 98312 | tf_op jit(solution)/shard_map/ppermute | solution.py:609
  22.4 1.3 %collective-permute-start.13 = (f32[40,128]{1,0:T(8,128)S(1)}, f32[40,128]{1,0:T(8,128)S(1)}, u32[]{:S(2)}, u32[]{:S(2)}) collective-permute-start(f32[40,128]{1,0:T(8,128)S(1)} %get-tuple-element.87.refs_9_.refs_11_), channel_id=1, source_target_pairs={{1,0},{0,1},{3,2},{2,3},{5,4},{4,5},{7,6},{6,7},{9,8},{8,9},{11,10... | collective-permute-start | bytes 61448 | tf_op jit(solution)/shard_map/ppermute | solution.py:614
  24.7 1.0 %shard_map.176 = (f32[3,17,4,128]{3,2,1,0:T(4,128)}, f32[32,128]{1,0:T(8,128)S(1)}, bf16[128,128]{1,0:T(8,128)(2,1)S(1)}) custom-call(f32[320,128]{1,0:T(8,128)S(1)} %get-tuple-element.83.cur_ref.refs_0_, bf16[512,512]{1,0:T(8,128)(2,1)S(1)} %copy-done, f32[16,128]{1,0:T(8,128)S(1)} %get-tuple-element.90.refs_2_.refs_1_, ...), custom_call_target="tpu_custom_call" | custom-call | tf_op jit(solution)/shard_map/pallas_call | solution.py:586
  26.3 1.3 %collective-permute-start.16 = (f32[2,128]{1,0:T(2,128)S(1)}, f32[2,128]{1,0:T(2,128)S(1)}, u32[]{:S(2)}, u32[]{:S(2)}) collective-permute-start(f32[2,128]{1,0:T(2,128)S(1)} %get-tuple-element.95), channel_id=1, source_target_pairs={{0,1},{1,0},{2,4},{3,5},{4,2},{5,3},{6,8},{7,9},{8,6},{9,7},{10,12... | collective-permute-start | bytes 3080 | tf_op jit(solution)/shard_map/ppermute | solution.py:609
  27.7 0.7 %collective-permute-start.17 = (f32[2,128]{1,0:T(2,128)S(1)}, f32[2,128]{1,0:T(2,128)S(1)}, u32[]{:S(2)}, u32[]{:S(2)}) collective-permute-start(f32[2,128]{1,0:T(2,128)S(1)} %get-tuple-element.96), channel_id=1, source_target_pairs={{0,1},{1,0},{2,3},{3,2},{4,8},{5,9},{6,10},{7,11},{8,4},{9,5},{10,... | collective-permute-start | bytes 3080 | tf_op jit(solution)/shard_map/ppermute | solution.py:609
  28.3 1.8 %collective-permute-start.18 = (f32[2,128]{1,0:T(2,128)S(1)}, f32[2,128]{1,0:T(2,128)S(1)}, u32[]{:S(2)}, u32[]{:S(2)}) collective-permute-start(f32[2,128]{1,0:T(2,128)S(1)} %get-tuple-element.97), channel_id=1, source_target_pairs={{0,4},{1,5},{2,6},{3,7},{4,0},{5,1},{6,2},{7,3},{8,12},{9,13},{10,... | collective-permute-start | bytes 3080 | tf_op jit(solution)/shard_map/ppermute | solution.py:609
  30.1 1.4 %shard_map.178 = f32[3,17,4,128]{3,2,1,0:T(4,128)} custom-call(f32[320,128]{1,0:T(8,128)S(1)} %get-tuple-element.83.cur_ref.refs_0_, f32[320,128]{1,0:T(8,128)S(1)} %get-tuple-element.76.cur_ref.refs_0_.refs_1_, f32[320,128]{1,0:T(8,128)S(1)} %get-tuple-element.56.refs_2_, f32[320,128]{1,0:T(8,128)S(1)} %get-tuple-element.84.refs_3_, ...), custom_call_target="tpu_custom_call" | custom-call | tf_op jit(solution)/shard_map/pallas_call | solution.py:586
  31.9 0.6 %add_bitcast_fusion = f32[1,2,128]{2,1,0:T(2,128)} fusion(f32[2,128]{1,0:T(2,128)S(1)} %collective-permute-done.19, f32[2,128]{1,0:T(2,128)S(1)} %collective-permute-done.18, f32[2,128]{1,0:T(2,128)S(1)} %collective-permute-done.17, f32[2,128]{1,0:T(2,128)S(1)} %get-tuple-element.93.refs_15_, f32[2,128]{1,0:T(2,128)S(1)} %collective-permute-done.16), kind=kLoop, calls=%fused_computation | loop fusion | flops 1024 | bytes 6144 | tf_op jit(solution)/shard_map/broadcast_in_dim | solution.py:745
  (38 shorter events, 4.7 us)
Async XLA Ops:
  2.7 6.8 %collective-permute-start = (f32[64,128]{1,0:T(8,128)S(1)}, f32[64,128]{1,0:T(8,128)S(1)}, u32[]{:S(2)}, u32[]{:S(2)}) collective-permute-start(f32[64,128]{1,0:T(8,128)S(1)} %get-tuple-element.62), channel_id=1, source_target_pairs={{0,1},{1,0},{2,4},{3,5},{4,2},{5,3},{6,8},{7,9},{8,6},{9,7},{10,12... | collective-permute-start | bytes 98312 | tf_op jit(solution)/shard_map/ppermute | solution.py:609
  5.7 3.8 %collective-permute-start.1 = (f32[48,128]{1,0:T(8,128)S(1)}, f32[48,128]{1,0:T(8,128)S(1)}, u32[]{:S(2)}, u32[]{:S(2)}) collective-permute-start(f32[48,128]{1,0:T(8,128)S(1)} %get-tuple-element.63.refs_11_.refs_12_.refs_3_), channel_id=1, source_target_pairs={{1,0},{0,1},{3,2},{2,3},{5,4},{4,5},{7,6},{6,7},{9,8},{8,9},{11,10... | collective-permute-start | bytes 73736 | tf_op jit(solution)/shard_map/ppermute | solution.py:614
  5.8 2.3 %collective-permute-start.2 = (f32[32,128]{1,0:T(8,128)S(1)}, f32[32,128]{1,0:T(8,128)S(1)}, u32[]{:S(2)}, u32[]{:S(2)}) collective-permute-start(f32[32,128]{1,0:T(8,128)S(1)} %get-tuple-element.64), channel_id=1, source_target_pairs={{0,2},{1,3},{2,0},{3,1},{4,6},{5,7},{6,4},{7,5},{8,10},{9,11},{10,... | collective-permute-start | bytes 49160 | tf_op jit(solution)/shard_map/ppermute | solution.py:609
  7.0 1.2 %collective-permute-start.3 = (f32[32,128]{1,0:T(8,128)S(1)}, f32[32,128]{1,0:T(8,128)S(1)}, u32[]{:S(2)}, u32[]{:S(2)}) collective-permute-start(f32[32,128]{1,0:T(8,128)S(1)} %get-tuple-element.65), channel_id=1, source_target_pairs={{0,2},{1,3},{2,0},{3,1},{4,6},{5,7},{6,4},{7,5},{8,10},{9,11},{10,... | collective-permute-start | bytes 49160 | tf_op jit(solution)/shard_map/ppermute | solution.py:609
  10.4 4.5 %collective-permute-start.4 = (f32[64,128]{1,0:T(8,128)S(1)}, f32[64,128]{1,0:T(8,128)S(1)}, u32[]{:S(2)}, u32[]{:S(2)}) collective-permute-start(f32[64,128]{1,0:T(8,128)S(1)} %get-tuple-element.71), channel_id=1, source_target_pairs={{0,1},{1,0},{2,4},{3,5},{4,2},{5,3},{6,8},{7,9},{8,6},{9,7},{10,12... | collective-permute-start | bytes 98312 | tf_op jit(solution)/shard_map/ppermute | solution.py:609
  10.7 4.1 %collective-permute-start.5 = (f32[40,128]{1,0:T(8,128)S(1)}, f32[40,128]{1,0:T(8,128)S(1)}, u32[]{:S(2)}, u32[]{:S(2)}) collective-permute-start(f32[40,128]{1,0:T(8,128)S(1)} %get-tuple-element.72.refs_11_.refs_5_), channel_id=1, source_target_pairs={{1,0},{0,1},{3,2},{2,3},{5,4},{4,5},{7,6},{6,7},{9,8},{8,9},{11,10... | collective-permute-start | bytes 61448 | tf_op jit(solution)/shard_map/ppermute | solution.py:614
  12.4 2.4 %collective-permute-start.6 = (f32[32,128]{1,0:T(8,128)S(1)}, f32[32,128]{1,0:T(8,128)S(1)}, u32[]{:S(2)}, u32[]{:S(2)}) collective-permute-start(f32[32,128]{1,0:T(8,128)S(1)} %get-tuple-element.73), channel_id=1, source_target_pairs={{0,2},{1,3},{2,0},{3,1},{4,6},{5,7},{6,4},{7,5},{8,10},{9,11},{10,... | collective-permute-start | bytes 49160 | tf_op jit(solution)/shard_map/ppermute | solution.py:609
  12.4 2.4 %collective-permute-start.7 = (f32[32,128]{1,0:T(8,128)S(1)}, f32[32,128]{1,0:T(8,128)S(1)}, u32[]{:S(2)}, u32[]{:S(2)}) collective-permute-start(f32[32,128]{1,0:T(8,128)S(1)} %get-tuple-element.74), channel_id=1, source_target_pairs={{0,2},{1,3},{2,0},{3,1},{4,6},{5,7},{6,4},{7,5},{8,10},{9,11},{10,... | collective-permute-start | bytes 49160 | tf_op jit(solution)/shard_map/ppermute | solution.py:609
  12.9 1.0 %copy-start = (bf16[512,512]{1,0:T(8,128)(2,1)S(1)}, bf16[512,512]{1,0:T(8,128)(2,1)}, u32[]{:S(2)}) copy-start(bf16[512,512]{1,0:T(8,128)(2,1)} %constant.16.clone.back_ref.refs_1_.refs_16_) | copy-start | bytes 1572868
  12.9 1.0 %copy-start.1 = (s32[4,1,4,128]{3,2,1,0:T(4,128)S(1)}, s32[4,1,4,128]{3,2,1,0:T(4,128)}, u32[]{:S(2)}) copy-start(s32[4,1,4,128]{3,2,1,0:T(4,128)} %param.20) | copy-start | bytes 24580
  12.9 1.0 %copy-start.2 = (f32[1,4,128]{2,1,0:T(4,128)S(1)}, f32[1,4,128]{2,1,0:T(4,128)}, u32[]{:S(2)}) copy-start(f32[1,4,128]{2,1,0:T(4,128)} %param.22) | copy-start | bytes 6148
  13.4 0.7 %copy-start.3 = (s32[1,4]{1,0:T(1,128)S(1)}, s32[1,4]{1,0:T(1,128)}, u32[]{:S(2)}) copy-start(s32[1,4]{1,0:T(1,128)} %owner_ref.1) | copy-start | bytes 52
  15.7 5.1 %collective-permute-start.8 = (f32[64,128]{1,0:T(8,128)S(1)}, f32[64,128]{1,0:T(8,128)S(1)}, u32[]{:S(2)}, u32[]{:S(2)}) collective-permute-start(f32[64,128]{1,0:T(8,128)S(1)} %get-tuple-element.79), channel_id=1, source_target_pairs={{0,1},{1,0},{2,4},{3,5},{4,2},{5,3},{6,8},{7,9},{8,6},{9,7},{10,12... | collective-permute-start | bytes 98312 | tf_op jit(solution)/shard_map/ppermute | solution.py:609
  17.1 3.8 %collective-permute-start.9 = (f32[40,128]{1,0:T(8,128)S(1)}, f32[40,128]{1,0:T(8,128)S(1)}, u32[]{:S(2)}, u32[]{:S(2)}) collective-permute-start(f32[40,128]{1,0:T(8,128)S(1)} %get-tuple-element.80.refs_11_.refs_7_), channel_id=1, source_target_pairs={{1,0},{0,1},{3,2},{2,3},{5,4},{4,5},{7,6},{6,7},{9,8},{8,9},{11,10... | collective-permute-start | bytes 61448 | tf_op jit(solution)/shard_map/ppermute | solution.py:614
  17.7 1.2 %collective-permute-start.10 = (f32[32,128]{1,0:T(8,128)S(1)}, f32[32,128]{1,0:T(8,128)S(1)}, u32[]{:S(2)}, u32[]{:S(2)}) collective-permute-start(f32[32,128]{1,0:T(8,128)S(1)} %get-tuple-element.81), channel_id=1, source_target_pairs={{0,2},{1,3},{2,0},{3,1},{4,6},{5,7},{6,4},{7,5},{8,10},{9,11},{10,... | collective-permute-start | bytes 49160 | tf_op jit(solution)/shard_map/ppermute | solution.py:609
  17.7 1.3 %collective-permute-start.11 = (f32[32,128]{1,0:T(8,128)S(1)}, f32[32,128]{1,0:T(8,128)S(1)}, u32[]{:S(2)}, u32[]{:S(2)}) collective-permute-start(f32[32,128]{1,0:T(8,128)S(1)} %get-tuple-element.82), channel_id=1, source_target_pairs={{0,2},{1,3},{2,0},{3,1},{4,6},{5,7},{6,4},{7,5},{8,10},{9,11},{10,... | collective-permute-start | bytes 49160 | tf_op jit(solution)/shard_map/ppermute | solution.py:609
  21.7 4.5 %collective-permute-start.12 = (f32[64,128]{1,0:T(8,128)S(1)}, f32[64,128]{1,0:T(8,128)S(1)}, u32[]{:S(2)}, u32[]{:S(2)}) collective-permute-start(f32[64,128]{1,0:T(8,128)S(1)} %get-tuple-element.86), channel_id=1, source_target_pairs={{0,1},{1,0},{2,4},{3,5},{4,2},{5,3},{6,8},{7,9},{8,6},{9,7},{10,12... | collective-permute-start | bytes 98312 | tf_op jit(solution)/shard_map/ppermute | solution.py:609
  22.4 3.8 %collective-permute-start.13 = (f32[40,128]{1,0:T(8,128)S(1)}, f32[40,128]{1,0:T(8,128)S(1)}, u32[]{:S(2)}, u32[]{:S(2)}) collective-permute-start(f32[40,128]{1,0:T(8,128)S(1)} %get-tuple-element.87.refs_9_.refs_11_), channel_id=1, source_target_pairs={{1,0},{0,1},{3,2},{2,3},{5,4},{4,5},{7,6},{6,7},{9,8},{8,9},{11,10... | collective-permute-start | bytes 61448 | tf_op jit(solution)/shard_map/ppermute | solution.py:614
  23.7 2.0 %collective-permute-start.14 = (f32[32,128]{1,0:T(8,128)S(1)}, f32[32,128]{1,0:T(8,128)S(1)}, u32[]{:S(2)}, u32[]{:S(2)}) collective-permute-start(f32[32,128]{1,0:T(8,128)S(1)} %get-tuple-element.88), channel_id=1, source_target_pairs={{0,2},{1,3},{2,0},{3,1},{4,6},{5,7},{6,4},{7,5},{8,10},{9,11},{10,... | collective-permute-start | bytes 49160 | tf_op jit(solution)/shard_map/ppermute | solution.py:609
  23.7 2.0 %collective-permute-start.15 = (f32[32,128]{1,0:T(8,128)S(1)}, f32[32,128]{1,0:T(8,128)S(1)}, u32[]{:S(2)}, u32[]{:S(2)}) collective-permute-start(f32[32,128]{1,0:T(8,128)S(1)} %get-tuple-element.89), channel_id=1, source_target_pairs={{0,2},{1,3},{2,0},{3,1},{4,6},{5,7},{6,4},{7,5},{8,10},{9,11},{10,... | collective-permute-start | bytes 49160 | tf_op jit(solution)/shard_map/ppermute | solution.py:609
  26.3 5.2 %collective-permute-start.16 = (f32[2,128]{1,0:T(2,128)S(1)}, f32[2,128]{1,0:T(2,128)S(1)}, u32[]{:S(2)}, u32[]{:S(2)}) collective-permute-start(f32[2,128]{1,0:T(2,128)S(1)} %get-tuple-element.95), channel_id=1, source_target_pairs={{0,1},{1,0},{2,4},{3,5},{4,2},{5,3},{6,8},{7,9},{8,6},{9,7},{10,12... | collective-permute-start | bytes 3080 | tf_op jit(solution)/shard_map/ppermute | solution.py:609
  27.7 3.9 %collective-permute-start.17 = (f32[2,128]{1,0:T(2,128)S(1)}, f32[2,128]{1,0:T(2,128)S(1)}, u32[]{:S(2)}, u32[]{:S(2)}) collective-permute-start(f32[2,128]{1,0:T(2,128)S(1)} %get-tuple-element.96), channel_id=1, source_target_pairs={{0,1},{1,0},{2,3},{3,2},{4,8},{5,9},{6,10},{7,11},{8,4},{9,5},{10,... | collective-permute-start | bytes 3080 | tf_op jit(solution)/shard_map/ppermute | solution.py:609
  28.3 3.6 %collective-permute-start.18 = (f32[2,128]{1,0:T(2,128)S(1)}, f32[2,128]{1,0:T(2,128)S(1)}, u32[]{:S(2)}, u32[]{:S(2)}) collective-permute-start(f32[2,128]{1,0:T(2,128)S(1)} %get-tuple-element.97), channel_id=1, source_target_pairs={{0,4},{1,5},{2,6},{3,7},{4,0},{5,1},{6,2},{7,3},{8,12},{9,13},{10,... | collective-permute-start | bytes 3080 | tf_op jit(solution)/shard_map/ppermute | solution.py:609
  30.1 1.8 %collective-permute-start.19 = (f32[2,128]{1,0:T(2,128)S(1)}, f32[2,128]{1,0:T(2,128)S(1)}, u32[]{:S(2)}, u32[]{:S(2)}) collective-permute-start(f32[2,128]{1,0:T(2,128)S(1)} %get-tuple-element.98), channel_id=1, source_target_pairs={{0,2},{1,3},{2,0},{3,1},{4,6},{5,7},{6,4},{7,5},{8,10},{9,11},{10,... | collective-permute-start | bytes 3080 | tf_op jit(solution)/shard_map/ppermute | solution.py:609

commit v10 on v9

--- a/solution.py
+++ b/solution.py
@@ -14,6 +14,9 @@
 REACH = 2
 PATCH_ROWS = 16
 LATER = 7
+FAULT = 24
+SENT_FAULT = 28
+PARTS = (24, 24, 16)
 
 time_step = 0.01
 lock_stiffness = 0.5
@@ -233,7 +236,7 @@
     return jnp.concatenate(blocks, axis=0)
 
 
-def from_elements(field, scratch, back_ref, out_ref, y_elems):
+def from_elements(field, scratch, back_ref, out_ref, y_elems, stored=None):
     rows = []
     for x in range(4):
         rows.append(
@@ -250,6 +253,8 @@
         for y in range(4 * y_elems + 1):
             yel, yl = (y // 4, y % 4) if y < 4 * y_elems else (y_elems - 1, 4)
             out_ref[c, y] = scratch[yel, pl.ds(ROWS[yl][c], 4, stride=BLOCK), :]
+        if stored is not None:
+            stored(c)
 
 
 def shifted(rows, lanes):
@@ -264,21 +269,17 @@
     )
 
 
-def fault_message(plane, z_elems):
+def store_fault(out_ref, x, plane, z_elems):
     lanes = plane.shape[1]
-    row, lane = block_iotas(lanes)
+    _, lane = block_iotas(lanes)
     first = last = jnp.zeros((8, lanes), jnp.float32)
     for zl in range(4):
         at = zl * BLOCK
         here = lane // z_elems == zl
         first = jnp.where(here, shifted(plane[at : at + 8], zl * z_elems), first)
         last = jnp.where(here, shifted(plane[at + 8 : at + 16], (zl + 1) * z_elems), last)
-    return jnp.where(row < 4, last, pltpu.roll(first, 4, 0))
-
-
-def swap_rows(message):
-    parts = [pltpu.roll(message[i : i + 8], 4, 0) for i in range(0, message.shape[0], 8)]
-    return jnp.concatenate(parts, axis=0)
+    out_ref[pl.ds(x, 3, stride=8), :] = last[:3]
+    out_ref[pl.ds(4 + x, 3, stride=8), :] = first[:3]
 
 
 def select_messages(parity, left, right):
@@ -342,8 +343,8 @@
     *refs,
 ):
     later_hbm, refs = refs[:LATER], refs[LATER:]
-    cur_ref, even_ref, even_rest, odd_ref, fault_out_ref, material_ref = refs[:6]
-    later_refs, refs = refs[6 : 6 + LATER], refs[6 + LATER :]
+    cur_ref, *even_refs, odd_ref, fault_out_ref, material_ref = refs[:7]
+    later_refs, refs = refs[7 : 7 + LATER], refs[7 + LATER :]
     scratch, now_ref, flags_ref, weak_ref, lame_ref, shear_ref, sems = refs
     copies = start_copies(
         [
@@ -375,7 +376,8 @@
     edge = dot(edge_ref[...], jnp.concatenate([stacked(p) for p in planes], axis=0))
     right = edge_message(edge, lame_row, shear_row, z_elems)
     message, odd_ref[...] = select_messages(parity, cur[: 4 * BLOCK], right)
-    even_ref[...], even_rest[...] = message[: 2 * BLOCK], message[2 * BLOCK :]
+    for even_ref, at in zip(even_refs, (0, PARTS[0], PARTS[0] + PARTS[1])):
+        even_ref[...] = message[at : at + even_ref.shape[0]]
     weak = weak_ref[...]
     tangent = []
     for i in range(flags_ref.shape[0]):
@@ -384,8 +386,8 @@
             jnp.where(flag == 0, lock_stiffness, jnp.where(flag == 1, -weak, 0.0))
         )
     for x in range(4):
-        fault_out_ref[8 * x : 8 * x + 8] = fault_message(planes[x], z_elems)
-    fault_out_ref[32:] = exact_dot(jnp.concatenate(tangent, axis=0), fault)
+        store_fault(fault_out_ref, x, planes[x], z_elems)
+    fault_out_ref[FAULT:] = exact_dot(jnp.concatenate(tangent, axis=0), fault)
     for copy in copies[6:]:
         copy.wait()
 
@@ -408,25 +410,19 @@
     minv_ref[...] = jnp.where(table > 0.0, table / jnp.where(table > 0.0, density, 1.0), 0.0)
 
 
-def fault_input(up_ref, down_ref, count):
-    if down_ref is None:
-        return up_ref[:count]
-    up, down = up_ref[:count], down_ref[:count]
-    row = lax.broadcasted_iota(jnp.int32, up.shape, 0)
-    return jnp.where(row % 8 < 4, up, down)
-
-
 def step_kernel(*refs, step, last, extra, last_place, pair, y_elems, z_elems):
     cur_ref, fol_ref, minv_ref, base_ref, touch_ref, material_ref, odd_ref, up_ref = refs[:8]
     refs = list(refs[8:])
     down_ref = None if pair else refs.pop(0)
-    even_in = jnp.concatenate([refs.pop(0)[...], refs.pop(0)[...]], axis=0)
+    even_in = jnp.concatenate([refs.pop(0)[...] for _ in PARTS], axis=0)
+    down_ref = up_ref if pair else down_ref
     first_up_ref, own_ref, first_own_ref, far_ref, edge_ref = refs[:5]
     refs = refs[5 + extra :]
     if last:
-        back_ref, out_ref, scratch = refs
+        later_ref, back_ref, out_hbm, later_hbm, scratch, out_ref, sems = refs
+        copies = start_copies([(later_ref, later_hbm)], sems)
     else:
-        new_ref, even_out, even_rest, odd_out, fault_out = refs
+        new_ref, *even_outs, odd_out, fault_out = refs
     place = lax.axis_index("dom")
     lanes = cur_ref.shape[1]
     even = place % 2 == 0
@@ -450,9 +446,10 @@
     pull_first = jnp.logical_and(shared, across == 0)
     pull_last = jnp.logical_and(shared, across == y_elems - 1)
     above = above_lanes(lanes, z_elems)
-    fault_in = fault_input(up_ref, down_ref, 32)
+    middle = lax.broadcasted_iota(jnp.int32, (3, lanes), 0) == 1
+    gap = jnp.zeros((5, lanes), jnp.float32)
     if not last:
-        fault_out[32:] = jnp.zeros_like(fault_out[32:])
+        fault_out[FAULT:] = jnp.zeros_like(fault_out[FAULT:])
     planes = []
     for x in range(4):
         rows = slice(x * PLANE, (x + 1) * PLANE)
@@ -465,14 +462,16 @@
             blocks[0] + jnp.where(above, pltpu.roll(blocks[4], 1, 1), 0.0),
             blocks[4] + pltpu.roll(blocks[0], lanes - 1, 1),
         )
-        at, k = slice(8 * x, 8 * x + 8), slice(32 + 4 * step + x, 33 + 4 * step + x)
-        stiff = jnp.where(
-            jnp.logical_or(row == 1, row == 5),
-            lock_stiffness,
-            jnp.where(row < 4, first_up_ref[k], first_own_ref[k]),
-        )
-        pulled = stiff * (fault_in[at] - pltpu.roll(own_ref[at], 4, 0))
-        pulled_last = pltpu.roll(pulled, 4, 0)
+        lasts, firsts = pl.ds(x, 3, stride=8), pl.ds(4 + x, 3, stride=8)
+        k = slice(FAULT + 4 * step + x, FAULT + 4 * step + x + 1)
+        below_stiff = jnp.where(middle, lock_stiffness, first_up_ref[k])
+        own_stiff = jnp.where(middle, lock_stiffness, first_own_ref[k])
+        pulled = jnp.concatenate(
+            [below_stiff * (up_ref[lasts, :] - own_ref[firsts, :]), gap], axis=0
+        )
+        pulled_last = jnp.concatenate(
+            [own_stiff * (down_ref[firsts, :] - own_ref[lasts, :]), gap], axis=0
+        )
         for zl in range(5):
             low, high = blocks[zl][:8], blocks[zl][8:]
             move = zl * z_elems if zl < 4 else 1
@@ -494,17 +493,28 @@
             planes.append(plane)
         else:
             new_ref[rows] = plane
-            fault_out[at] = fault_message(plane, z_elems)
+            store_fault(fault_out, x, plane, z_elems)
             planes.append(stacked(plane))
             if x == 0:
                 first = plane[: 4 * BLOCK]
     if last:
-        from_elements(jnp.concatenate(planes, axis=0), scratch, back_ref, out_ref, y_elems)
+
+        def send(c):
+            copy = pltpu.make_async_copy(out_ref.at[c], out_hbm.at[c], sems.at[1 + c])
+            copy.start()
+            copies.append(copy)
+
+        from_elements(
+            jnp.concatenate(planes, axis=0), scratch, back_ref, out_ref, y_elems, send
+        )
+        for copy in copies:
+            copy.wait()
     else:
         edge = dot(edge_ref[...], jnp.concatenate(planes, axis=0))
         right = edge_message(edge, lame_row, shear_row, z_elems)
         message, odd_out[...] = select_messages(place % 2, first, right)
-        even_out[...], even_rest[...] = message[: 2 * BLOCK], message[2 * BLOCK :]
+        for even_out, at in zip(even_outs, (0, PARTS[0], PARTS[0] + PARTS[1])):
+            even_out[...] = message[at : at + even_out.shape[0]]
 
 
 def mask_kernel(owner_ref, _, back_ref, flags_ref, stress_ref, mask_ref, weight_ref, *, z_elems):
@@ -530,30 +540,27 @@
     out_ref, grad_ref, table_ref, scratch = refs[-4:]
     messages = refs[3:-4]
     count = 2 if pair else 3
-    grads = [jnp.zeros((8, weight_ref.shape[1]), jnp.float32) for _ in range(4)]
+    grad = 0.0
     for i in range(steps):
         group = messages[count * i : count * (i + 1)]
-        slip = -swap_rows(group[0][:32])
+        slip = -group[0][:4]
         if i < steps - 1:
-            slip = slip + fault_input(group[1], None if pair else group[2], 32)
-        for x in range(4):
-            grads[x] = grads[x] + slip[8 * x : 8 * x + 8] * weight_ref[4 * i + x : 4 * i + x + 1]
-    grad_ref[...] = jnp.concatenate(grads, axis=0)
+            slip = slip + group[-1][4:8]
+        grad = grad + slip * weight_ref[4 * i : 4 * i + 4]
+    grad_ref[...] = grad
     table_ref[...] = fault_table_back(weight_ref.shape[1], z_elems)
     from_elements(field_ref[...], scratch, back_ref, out_ref, y_elems)
 
 
 def patch_kernel(*refs, pair, steps):
-    mask_ref, weight_ref, grad_ref, table_ref, _, up_ref = refs[:6]
-    down_ref = None if pair else refs[6]
+    mask_ref, weight_ref, grad_ref, table_ref, _ = refs[:5]
+    first_ref = refs[5] if pair else refs[6]
     home_out, out_a, out_b, out_c, out_d = refs[-5:]
     place = lax.axis_index("dom")
-    slip = fault_input(up_ref, down_ref, 32)
+    grad = grad_ref[...] + first_ref[4:8] * weight_ref[4 * (steps - 1) : 4 * steps]
     total = 0.0
     for x in range(4):
-        at, k = 8 * x + 4, 4 * (steps - 1) + x
-        grad = grad_ref[at : at + 1] + slip[at : at + 1] * weight_ref[k : k + 1]
-        total = total + mask_ref[PATCH_ROWS * x : PATCH_ROWS * (x + 1)] * grad
+        total = total + mask_ref[PATCH_ROWS * x : PATCH_ROWS * (x + 1)] * grad[x : x + 1]
     total = exact_dot(total, table_ref[...])
     rows = [total[2 * i : 2 * i + 2] for i in range(5)]
     home_out[...] = rows[2]
@@ -571,11 +578,11 @@
 ANY = pl.BlockSpec(memory_space=pl.ANY)
 
 
-def kernel_call(body, outs, args, in_smem=(), scratch=(), in_hbm=(), kept=(), unread=(), **static):
+def kernel_call(body, outs, args, in_smem=(), scratch=(), in_hbm=(), kept=(), unread=(), stay=False, out_spec=VMEM, **static):
     shapes = []
     for out in outs:
         shape, dtype = out if isinstance(out[0], tuple) else (out, jnp.float32)
-        shapes.append((pltpu.VMEM if in_hbm else jax.ShapeDtypeStruct)(shape, dtype))
+        shapes.append((pltpu.VMEM if in_hbm or stay else jax.ShapeDtypeStruct)(shape, dtype))
     specs = [VMEM] * len(args)
     for places, spec in ((in_smem, SMEM), (in_hbm, HBM), (unread, ANY)):
         for i in places:
@@ -587,7 +594,7 @@
         functools.partial(body, **static) if static else body,
         out_shape=shapes,
         in_specs=specs,
-        out_specs=[VMEM] * len(shapes),
+        out_specs=[out_spec] * len(shapes),
         scratch_shapes=list(scratch) + copied,
         compiler_params=pltpu.CompilerParams(
             vmem_limit_bytes=(56 if in_hbm else 24) * 2**20
@@ -640,7 +647,7 @@
     native = pltpu.VMEM((y_elems, 4 * BLOCK, lanes), jnp.float32)
     field = (4 * PLANE, lanes)
     plane = (4 * BLOCK, lanes)
-    half = (2 * BLOCK, lanes)
+    parts = [(rows, lanes) for rows in PARTS]
 
     def exchange(even, odd, fault_rows):
         if pair:
@@ -653,7 +660,7 @@
     assert len(later_used) == LATER
     cur, *even, odd, fault_rows, material, edge_table, following, rho, mass, own_table, far_table, touch_table = kernel_call(
         first_kernel,
-        [field, half, half, plane, (32 + 4 * steps, lanes), (8, lanes)]
+        [field] + parts + [plane, (FAULT + 4 * steps, lanes), (8, lanes)]
         + [(t.shape, t.dtype) for t in later_used],
         (now, flags, weak_slope[0], lame_first[0], shear_modulus[0]) + later_used,
         scratch=[native],
@@ -699,7 +706,7 @@
         if not last:
             new, *even, odd, new_fault = kernel_call(
                 step_kernel,
-                [field, half, half, plane, (40, lanes)],
+                [field] + parts + [plane, (SENT_FAULT, lanes)],
                 args,
                 unread=(len(args) - 1,) if step == 1 else (),
                 **static,
@@ -711,10 +718,10 @@
             known = seen[: len(seen) - len(fault_in)]
             later, grad, table = kernel_call(
                 output_kernel,
-                [whole, (32, lanes), ((lanes, lanes), jnp.bfloat16)],
+                [whole, (4, lanes), ((lanes, lanes), jnp.bfloat16)],
                 [cur, back, weight] + known,
-                (),
-                [native],
+                scratch=[native],
+                stay=True,
                 pair=pair,
                 steps=steps,
                 y_elems=y_elems,
@@ -724,21 +731,24 @@
                 patch_kernel,
                 [(PATCH_DEV, lanes)] * 5,
                 [mask, weight, grad, table, odd_in] + fault_in + even_in + [touch],
-                unread=(4,) + tuple(range(5 + len(fault_in), 8 + len(fault_in))),
+                unread=(4,) + tuple(range(5 + len(fault_in), 9 + len(fault_in))),
                 pair=pair,
                 steps=steps,
             )
             patch_sums = sums[0]
             for i, distance, group in ((2, 1, 1), (4, 2, 1), (3, 2, 0), (1, 1, 0)):
                 patch_sums = patch_sums + swapped(sums[i], distance, group)
-            earlier = kernel_call(
+            earlier, later = kernel_call(
                 step_kernel,
-                [whole],
-                args + [sums[0], back],
-                scratch=[native],
+                [whole, whole],
+                args + [sums[0], later, back],
+                scratch=[
+                    native, pltpu.VMEM(whole, jnp.float32), pltpu.SemaphoreType.DMA((4,)),
+                ],
                 unread=(len(args),),
+                out_spec=HBM,
                 **static,
-            )[0]
+            )
     return (
         jnp.transpose(earlier, (0, 2, 1, 3)),
         jnp.transpose(later, (0, 2, 1, 3)),

time: 32.7 us -> 32.6 us (level)
  Pallas kernels: 10.3 us -> 9.71 us
  starting transfers between devices: 15.8 us -> 16.3 us
    pallas_call x13, Pallas kernels: 10.3 us -> 9.71 us  [kernel_call(): pl.pallas_call(functools.partial(body, **static) if static else body, out...]
    ppermute x4, waiting for transfers between devices: 3.47 us -> 2.91 us  [from_behind(): lax.ppermute(block, axis, [((i - distance) % size, i) for i in range(size)])]
    ppermute x16 -> x20, starting transfers between devices: 12 us -> 12.5 us  [swapped(): return lax.ppermute(block, ('dom', 'depth'), route)]
    ppermute x16 -> x20, waiting for transfers between devices: 0.89 us -> 1.37 us  [swapped(): return lax.ppermute(block, ('dom', 'depth'), route)]
  transfers between devices with their start and end apart: 20 -> 24, of which waited for: 7 -> 6; matrix products, arithmetic and copies ran while one was open for 0% -> 0% of each run, Pallas kernels for 17% -> 15%
where the time goes in v10:
time: 32.6 us; the launch traced here: 32.4 us
  starting transfers between devices  16.3 us (50%)
  Pallas kernels  9.71 us (30%)
  waiting for transfers between devices  4.29 us (13%)
  between operations  0.79 us (2%)
  local copies, waits for them, and re-layouts  0.69 us (2%)
  other arithmetic  0.57 us (2%)
    ppermute x20, starting transfers between devices, swapped(): return lax.ppermute(block, ('dom', 'depth'), route)  12.5 us
    pallas_call x13, Pallas kernels, kernel_call(): pl.pallas_call(functools.partial(body, **static) if static else body, out...  9.71 us
    ppermute x4, starting transfers between devices, from_behind(): lax.ppermute(block, axis, [((i - distance) % size, i) for i in range(size)])  3.79 us
    ppermute x4, waiting for transfers between devices, from_behind(): lax.ppermute(block, axis, [((i - distance) % size, i) for i in range(size)])  2.91 us
    ppermute x20, waiting for transfers between devices, swapped(): return lax.ppermute(block, ('dom', 'depth'), route)  1.37 us
    unnamed x8, local copies, waits for them, and re-layouts  0.69 us
  transfers between devices with their start and end apart: 24, of which 6 were waited for; matrix products, arithmetic and copies ran while one was open for 0% of the time, Pallas kernels for 15%

profile of v10, /device:TPU:0, one launch (start us, length us, event | category | flops | bytes accessed | tf_op | source)
XLA Modules:
  0.0 32.4 jit_solution(13786571970941987226)
XLA Ops:
  0.6 2.0 %shard_map.166 = (f32[320,128]{1,0:T(8,128)S(1)}, f32[24,128]{1,0:T(8,128)S(1)}, f32[24,128]{1,0:T(8,128)S(1)}, f32[16,128]{1,0:T(8,128)S(1)}, f32[64,128]{1,0:T...) custom-call(f32[3,17,4,128]{3,2,1,0:T(4,128)} %bitcast.15, ...), custom_call_target="tpu_custom_call" | custom-call | tf_op jit(solution)/shard_map/pallas_call | solution.py:593
  2.7 3.0 %collective-permute-start = (f32[64,128]{1,0:T(8,128)S(1)}, f32[64,128]{1,0:T(8,128)S(1)}, u32[]{:S(2)}, u32[]{:S(2)}) collective-permute-start(f32[64,128]{1,0:T(8,128)S(1)} %get-tuple-element.68), channel_id=1, source_target_pairs={{0,1},{1,0},{2,4},{3,5},{4,2},{5,3},{6,8},{7,9},{8,6},{9,7},{10,12... | collective-permute-start | bytes 98312 | tf_op jit(solution)/shard_map/ppermute | solution.py:616
  5.8 1.3 %collective-permute-start.2 = (f32[24,128]{1,0:T(8,128)S(1)}, f32[24,128]{1,0:T(8,128)S(1)}, u32[]{:S(2)}, u32[]{:S(2)}) collective-permute-start(f32[24,128]{1,0:T(8,128)S(1)} %get-tuple-element.70), channel_id=1, source_target_pairs={{0,2},{1,3},{2,0},{3,1},{4,6},{5,7},{6,4},{7,5},{8,10},{9,11},{10,... | collective-permute-start | bytes 36872 | tf_op jit(solution)/shard_map/ppermute | solution.py:616
  7.6 0.5 %shard_map.167 = (f32[320,128]{1,0:T(8,128)S(1)}, f32[320,128]{1,0:T(8,128)S(1)}) custom-call(f32[3,17,4,128]{3,2,1,0:T(4,128)S(1)} %get-tuple-element.58.next_ref, f32[17,4,128]{2,1,0:T(4,128)S(1)} %get-tuple-element.59.density_ref, f32[320,128]{1,0:T(8,128)S(1)} %get-tuple-element.60.mass_ref), custom_call_target="tpu_custom_call" | custom-call | tf_op jit(solution)/shard_map/pallas_call | solution.py:593
  8.1 0.5 %shard_map.168 = (f32[320,128]{1,0:T(8,128)S(1)}, f32[160,128]{1,0:T(8,128)S(1)}) custom-call(f32[320,128]{1,0:T(8,128)S(1)} %get-tuple-element.57.cur_ref.refs_0_.refs_1_, f32[8,128]{1,0:T(8,128)S(1)} %get-tuple-element.63.material_ref.refs_5_, bf16[2,640,384]{2,1,0:T(8,128)(2,1)S(1)} %get-tuple-element.64.own_ref, ...), custom_call_target="tpu_custom_call" | custom-call | tf_op jit(solution)/shard_map/pallas_call | solution.py:593
  8.6 0.8 %collective-permute-done.1.refs_7_.refs_11_.refs_4_ = f32[40,128]{1,0:T(8,128)S(1)} collective-permute-done((f32[40,128]{1,0:T(8,128)S(1)}, f32[40,128]{1,0:T(8,128)S(1)}, u32[]{:S(2)}, u32[]{:S(2)}) %collective-permute-start.1) | collective-permute-done | bytes 20512 | tf_op jit(solution)/shard_map/ppermute | solution.py:621
  9.5 0.8 %shard_map.169 = (f32[320,128]{1,0:T(8,128)S(1)}, f32[24,128]{1,0:T(8,128)S(1)}, f32[24,128]{1,0:T(8,128)S(1)}, f32[16,128]{1,0:T(8,128)S(1)}, f32[64,128]{1,0:T(8,128)S(1)}, /*index=5*/f32[28,128]{1,0:T(8,128)S(1)}) custom-call(f32[320,128]{1,0:T(8,128)S(1)} %get-tuple-element.57.cur_ref.refs_0_.refs_1_, f32[320,128]{1,0:T(8,128)S(1)} %get-tuple-element.61.refs_1_, ...), custom_call_target="tpu_custom_call" | custom-call | tf_op jit(solution)/shard_map/pallas_call | solution.py:593
  10.7 1.7 %collective-permute-start.6 = (f32[28,128]{1,0:T(8,128)S(1)}, f32[28,128]{1,0:T(8,128)S(1)}, u32[]{:S(2)}, u32[]{:S(2)}) collective-permute-start(f32[28,128]{1,0:T(8,128)S(1)} %get-tuple-element.79.refs_12_.refs_5_), channel_id=1, source_target_pairs={{1,0},{0,1},{3,2},{2,3},{5,4},{4,5},{7,6},{6,7},{9,8},{8,9},{11,10... | collective-permute-start | bytes 43016 | tf_op jit(solution)/shard_map/ppermute | solution.py:621
  12.9 0.5 %shard_map.170 = (f32[320,128]{1,0:T(8,128)S(1)}, f32[160,128]{1,0:T(8,128)S(1)}) custom-call(f32[320,128]{1,0:T(8,128)S(1)} %get-tuple-element.75.cur_ref._.refs_0_.refs_1_, f32[8,128]{1,0:T(8,128)S(1)} %get-tuple-element.63.material_ref.refs_5_, bf16[2,640,384]{2,1,0:T(8,128)(2,1)S(1)} %get-tuple-element.64.own_ref, ...), custom_call_target="tpu_custom_call" | custom-call | tf_op jit(solution)/shard_map/pallas_call | solution.py:593
  14.1 0.7 %shard_map.171 = (f32[64,128]{1,0:T(8,128)S(1)}, f32[16,128]{1,0:T(8,128)S(1)}) custom-call(s32[1,4]{1,0:T(1,128)S(1)} %copy-done.3, f32[320,128]{1,0:T(8,128)S(1)} %get-tuple-element.75.cur_ref._.refs_0_.refs_1_, bf16[512,512]{1,0:T(8,128)(2,1)S(1)} %copy-done, s32[4,4,128]{2,1,0:T(4,128)S(1)} %bitcast.13, f32[4,128]{1,0:T(4,128)S(1)} %bitcast.14), custom_call_target="tpu_custom_call" | custom-call | tf_op jit(solution)/shard_map/pallas_call | solution.py:593
  14.8 0.9 %shard_map.172 = (f32[320,128]{1,0:T(8,128)S(1)}, f32[24,128]{1,0:T(8,128)S(1)}, f32[24,128]{1,0:T(8,128)S(1)}, f32[16,128]{1,0:T(8,128)S(1)}, f32[64,128]{1,0:T(8,128)S(1)}, /*index=5*/f32[28,128]{1,0:T(8,128)S(1)}) custom-call(f32[320,128]{1,0:T(8,128)S(1)} %get-tuple-element.75.cur_ref._.refs_0_.refs_1_, ...), custom_call_target="tpu_custom_call" | custom-call | tf_op jit(solution)/shard_map/pallas_call | solution.py:593
  15.7 1.3 %collective-permute-start.10 = (f32[64,128]{1,0:T(8,128)S(1)}, f32[64,128]{1,0:T(8,128)S(1)}, u32[]{:S(2)}, u32[]{:S(2)}) collective-permute-start(f32[64,128]{1,0:T(8,128)S(1)} %get-tuple-element.87), channel_id=1, source_target_pairs={{0,1},{1,0},{2,4},{3,5},{4,2},{5,3},{6,8},{7,9},{8,6},{9,7},{10,12... | collective-permute-start | bytes 98312 | tf_op jit(solution)/shard_map/ppermute | solution.py:616
  17.0 0.8 %collective-permute-start.11 = (f32[28,128]{1,0:T(8,128)S(1)}, f32[28,128]{1,0:T(8,128)S(1)}, u32[]{:S(2)}, u32[]{:S(2)}) collective-permute-start(f32[28,128]{1,0:T(8,128)S(1)} %get-tuple-element.88.refs_12_.refs_7_), channel_id=1, source_target_pairs={{1,0},{0,1},{3,2},{2,3},{5,4},{4,5},{7,6},{6,7},{9,8},{8,9},{11,10... | collective-permute-start | bytes 43016 | tf_op jit(solution)/shard_map/ppermute | solution.py:621
  18.8 0.6 %collective-permute-done.14.refs_10_ = f32[16,128]{1,0:T(8,128)S(1)} collective-permute-done((f32[16,128]{1,0:T(8,128)S(1)}, f32[16,128]{1,0:T(8,128)S(1)}, u32[]{:S(2)}, u32[]{:S(2)}) %collective-permute-start.14) | collective-permute-done | bytes 8224 | tf_op jit(solution)/shard_map/ppermute | solution.py:616
  19.4 1.3 %collective-permute-done.11.refs_7_.refs_8_ = f32[28,128]{1,0:T(8,128)S(1)} collective-permute-done((f32[28,128]{1,0:T(8,128)S(1)}, f32[28,128]{1,0:T(8,128)S(1)}, u32[]{:S(2)}, u32[]{:S(2)}) %collective-permute-start.11) | collective-permute-done | bytes 14368 | tf_op jit(solution)/shard_map/ppermute | solution.py:621
  20.7 0.8 %shard_map.174 = (f32[320,128]{1,0:T(8,128)S(1)}, f32[24,128]{1,0:T(8,128)S(1)}, f32[24,128]{1,0:T(8,128)S(1)}, f32[16,128]{1,0:T(8,128)S(1)}, f32[64,128]{1,0:T(8,128)S(1)}, /*index=5*/f32[28,128]{1,0:T(8,128)S(1)}) custom-call(f32[320,128]{1,0:T(8,128)S(1)} %get-tuple-element.84.cur_ref.refs_0_.refs_1_, ...), custom_call_target="tpu_custom_call" | custom-call | tf_op jit(solution)/shard_map/pallas_call | solution.py:593
  21.5 0.8 %collective-permute-start.15 = (f32[64,128]{1,0:T(8,128)S(1)}, f32[64,128]{1,0:T(8,128)S(1)}, u32[]{:S(2)}, u32[]{:S(2)}) collective-permute-start(f32[64,128]{1,0:T(8,128)S(1)} %get-tuple-element.95), channel_id=1, source_target_pairs={{0,1},{1,0},{2,4},{3,5},{4,2},{5,3},{6,8},{7,9},{8,6},{9,7},{10,12... | collective-permute-start | bytes 98312 | tf_op jit(solution)/shard_map/ppermute | solution.py:616
  22.3 1.3 %collective-permute-start.16 = (f32[28,128]{1,0:T(8,128)S(1)}, f32[28,128]{1,0:T(8,128)S(1)}, u32[]{:S(2)}, u32[]{:S(2)}) collective-permute-start(f32[28,128]{1,0:T(8,128)S(1)} %get-tuple-element.96.refs_9_.refs_12_), channel_id=1, source_target_pairs={{1,0},{0,1},{3,2},{2,3},{5,4},{4,5},{7,6},{6,7},{9,8},{8,9},{11,10... | collective-permute-start | bytes 43016 | tf_op jit(solution)/shard_map/ppermute | solution.py:621
  25.3 0.8 %collective-permute-done.16.refs_5_.refs_7_ = f32[28,128]{1,0:T(8,128)S(1)} collective-permute-done((f32[28,128]{1,0:T(8,128)S(1)}, f32[28,128]{1,0:T(8,128)S(1)}, u32[]{:S(2)}, u32[]{:S(2)}) %collective-permute-start.16) | collective-permute-done | bytes 14368 | tf_op jit(solution)/shard_map/ppermute | solution.py:621
  26.2 1.3 %collective-permute-start.20 = (f32[2,128]{1,0:T(2,128)S(1)}, f32[2,128]{1,0:T(2,128)S(1)}, u32[]{:S(2)}, u32[]{:S(2)}) collective-permute-start(f32[2,128]{1,0:T(2,128)S(1)} %get-tuple-element.107), channel_id=1, source_target_pairs={{0,1},{1,0},{2,4},{3,5},{4,2},{5,3},{6,8},{7,9},{8,6},{9,7},{10,12... | collective-permute-start | bytes 3080 | tf_op jit(solution)/shard_map/ppermute | solution.py:616
  27.5 0.8 %collective-permute-start.21 = (f32[2,128]{1,0:T(2,128)S(1)}, f32[2,128]{1,0:T(2,128)S(1)}, u32[]{:S(2)}, u32[]{:S(2)}) collective-permute-start(f32[2,128]{1,0:T(2,128)S(1)} %get-tuple-element.108), channel_id=1, source_target_pairs={{0,1},{1,0},{2,3},{3,2},{4,8},{5,9},{6,10},{7,11},{8,4},{9,5},{10,... | collective-permute-start | bytes 3080 | tf_op jit(solution)/shard_map/ppermute | solution.py:616
  28.2 1.7 %collective-permute-start.22 = (f32[2,128]{1,0:T(2,128)S(1)}, f32[2,128]{1,0:T(2,128)S(1)}, u32[]{:S(2)}, u32[]{:S(2)}) collective-permute-start(f32[2,128]{1,0:T(2,128)S(1)} %get-tuple-element.109), channel_id=1, source_target_pairs={{0,4},{1,5},{2,6},{3,7},{4,0},{5,1},{6,2},{7,3},{8,12},{9,13},{10,... | collective-permute-start | bytes 3080 | tf_op jit(solution)/shard_map/ppermute | solution.py:616
  29.9 1.4 %shard_map.178 = (f32[3,17,4,128]{3,2,1,0:T(4,128)}, f32[3,17,4,128]{3,2,1,0:T(4,128)}) custom-call(f32[320,128]{1,0:T(8,128)S(1)} %get-tuple-element.92.cur_ref.refs_0_, f32[320,128]{1,0:T(8,128)S(1)} %get-tuple-element.84.cur_ref.refs_0_.refs_1_, f32[320,128]{1,0:T(8,128)S(1)} %get-tuple-element.62.refs_2_, f32[320,128]{1,0:T(8,128)S(1)} %get-tuple-element.93.refs_3_, ...), custom_call_target="tpu_custom_call" | custom-call | tf_op jit(solution)/shard_map/pallas_call | solution.py:593
  31.8 0.6 %add_bitcast_fusion = f32[1,2,128]{2,1,0:T(2,128)} fusion(f32[2,128]{1,0:T(2,128)S(1)} %collective-permute-done.23, f32[2,128]{1,0:T(2,128)S(1)} %collective-permute-done.22, f32[2,128]{1,0:T(2,128)S(1)} %collective-permute-done.21, f32[2,128]{1,0:T(2,128)S(1)} %get-tuple-element.103.refs_16_, f32[2,128]{1,0:T(2,128)S(1)} %collective-permute-done.20), kind=kLoop, calls=%fused_computation | loop fusion | flops 1024 | bytes 6144 | tf_op jit(solution)/shard_map/broadcast_in_dim | solution.py:755
  (46 shorter events, 5.5 us)
Async XLA Ops:
  2.7 6.8 %collective-permute-start = (f32[64,128]{1,0:T(8,128)S(1)}, f32[64,128]{1,0:T(8,128)S(1)}, u32[]{:S(2)}, u32[]{:S(2)}) collective-permute-start(f32[64,128]{1,0:T(8,128)S(1)} %get-tuple-element.68), channel_id=1, source_target_pairs={{0,1},{1,0},{2,4},{3,5},{4,2},{5,3},{6,8},{7,9},{8,6},{9,7},{10,12... | collective-permute-start | bytes 98312 | tf_op jit(solution)/shard_map/ppermute | solution.py:616
  5.7 3.8 %collective-permute-start.1 = (f32[40,128]{1,0:T(8,128)S(1)}, f32[40,128]{1,0:T(8,128)S(1)}, u32[]{:S(2)}, u32[]{:S(2)}) collective-permute-start(f32[40,128]{1,0:T(8,128)S(1)} %get-tuple-element.69.refs_12_.refs_13_.refs_3_), channel_id=1, source_target_pairs={{1,0},{0,1},{3,2},{2,3},{5,4},{4,5},{7,6},{6,7},{9,8},{8,9},{11,10... | collective-permute-start | bytes 61448 | tf_op jit(solution)/shard_map/ppermute | solution.py:621
  5.8 2.8 %collective-permute-start.2 = (f32[24,128]{1,0:T(8,128)S(1)}, f32[24,128]{1,0:T(8,128)S(1)}, u32[]{:S(2)}, u32[]{:S(2)}) collective-permute-start(f32[24,128]{1,0:T(8,128)S(1)} %get-tuple-element.70), channel_id=1, source_target_pairs={{0,2},{1,3},{2,0},{3,1},{4,6},{5,7},{6,4},{7,5},{8,10},{9,11},{10,... | collective-permute-start | bytes 36872 | tf_op jit(solution)/shard_map/ppermute | solution.py:616
  7.0 1.6 %collective-permute-start.3 = (f32[24,128]{1,0:T(8,128)S(1)}, f32[24,128]{1,0:T(8,128)S(1)}, u32[]{:S(2)}, u32[]{:S(2)}) collective-permute-start(f32[24,128]{1,0:T(8,128)S(1)} %get-tuple-element.71), channel_id=1, source_target_pairs={{0,2},{1,3},{2,0},{3,1},{4,6},{5,7},{6,4},{7,5},{8,10},{9,11},{10,... | collective-permute-start | bytes 36872 | tf_op jit(solution)/shard_map/ppermute | solution.py:616
  7.1 1.5 %collective-permute-start.4 = (f32[16,128]{1,0:T(8,128)S(1)}, f32[16,128]{1,0:T(8,128)S(1)}, u32[]{:S(2)}, u32[]{:S(2)}) collective-permute-start(f32[16,128]{1,0:T(8,128)S(1)} %get-tuple-element.72), channel_id=1, source_target_pairs={{0,2},{1,3},{2,0},{3,1},{4,6},{5,7},{6,4},{7,5},{8,10},{9,11},{10,... | collective-permute-start | bytes 24584 | tf_op jit(solution)/shard_map/ppermute | solution.py:616
  10.3 4.5 %collective-permute-start.5 = (f32[64,128]{1,0:T(8,128)S(1)}, f32[64,128]{1,0:T(8,128)S(1)}, u32[]{:S(2)}, u32[]{:S(2)}) collective-permute-start(f32[64,128]{1,0:T(8,128)S(1)} %get-tuple-element.78), channel_id=1, source_target_pairs={{0,1},{1,0},{2,4},{3,5},{4,2},{5,3},{6,8},{7,9},{8,6},{9,7},{10,12... | collective-permute-start | bytes 98312 | tf_op jit(solution)/shard_map/ppermute | solution.py:616
  10.7 4.1 %collective-permute-start.6 = (f32[28,128]{1,0:T(8,128)S(1)}, f32[28,128]{1,0:T(8,128)S(1)}, u32[]{:S(2)}, u32[]{:S(2)}) collective-permute-start(f32[28,128]{1,0:T(8,128)S(1)} %get-tuple-element.79.refs_12_.refs_5_), channel_id=1, source_target_pairs={{1,0},{0,1},{3,2},{2,3},{5,4},{4,5},{7,6},{6,7},{9,8},{8,9},{11,10... | collective-permute-start | bytes 43016 | tf_op jit(solution)/shard_map/ppermute | solution.py:621
  12.4 2.4 %collective-permute-start.7 = (f32[24,128]{1,0:T(8,128)S(1)}, f32[24,128]{1,0:T(8,128)S(1)}, u32[]{:S(2)}, u32[]{:S(2)}) collective-permute-start(f32[24,128]{1,0:T(8,128)S(1)} %get-tuple-element.80), channel_id=1, source_target_pairs={{0,2},{1,3},{2,0},{3,1},{4,6},{5,7},{6,4},{7,5},{8,10},{9,11},{10,... | collective-permute-start | bytes 36872 | tf_op jit(solution)/shard_map/ppermute | solution.py:616
  12.4 2.4 %collective-permute-start.8 = (f32[24,128]{1,0:T(8,128)S(1)}, f32[24,128]{1,0:T(8,128)S(1)}, u32[]{:S(2)}, u32[]{:S(2)}) collective-permute-start(f32[24,128]{1,0:T(8,128)S(1)} %get-tuple-element.81), channel_id=1, source_target_pairs={{0,2},{1,3},{2,0},{3,1},{4,6},{5,7},{6,4},{7,5},{8,10},{9,11},{10,... | collective-permute-start | bytes 36872 | tf_op jit(solution)/shard_map/ppermute | solution.py:616
  12.9 1.9 %collective-permute-start.9 = (f32[16,128]{1,0:T(8,128)S(1)}, f32[16,128]{1,0:T(8,128)S(1)}, u32[]{:S(2)}, u32[]{:S(2)}) collective-permute-start(f32[16,128]{1,0:T(8,128)S(1)} %get-tuple-element.82), channel_id=1, source_target_pairs={{0,2},{1,3},{2,0},{3,1},{4,6},{5,7},{6,4},{7,5},{8,10},{9,11},{10,... | collective-permute-start | bytes 24584 | tf_op jit(solution)/shard_map/ppermute | solution.py:616
  15.7 5.0 %collective-permute-start.10 = (f32[64,128]{1,0:T(8,128)S(1)}, f32[64,128]{1,0:T(8,128)S(1)}, u32[]{:S(2)}, u32[]{:S(2)}) collective-permute-start(f32[64,128]{1,0:T(8,128)S(1)} %get-tuple-element.87), channel_id=1, source_target_pairs={{0,1},{1,0},{2,4},{3,5},{4,2},{5,3},{6,8},{7,9},{8,6},{9,7},{10,12... | collective-permute-start | bytes 98312 | tf_op jit(solution)/shard_map/ppermute | solution.py:616
  17.0 3.7 %collective-permute-start.11 = (f32[28,128]{1,0:T(8,128)S(1)}, f32[28,128]{1,0:T(8,128)S(1)}, u32[]{:S(2)}, u32[]{:S(2)}) collective-permute-start(f32[28,128]{1,0:T(8,128)S(1)} %get-tuple-element.88.refs_12_.refs_7_), channel_id=1, source_target_pairs={{1,0},{0,1},{3,2},{2,3},{5,4},{4,5},{7,6},{6,7},{9,8},{8,9},{11,10... | collective-permute-start | bytes 43016 | tf_op jit(solution)/shard_map/ppermute | solution.py:621
  17.7 1.7 %collective-permute-start.12 = (f32[24,128]{1,0:T(8,128)S(1)}, f32[24,128]{1,0:T(8,128)S(1)}, u32[]{:S(2)}, u32[]{:S(2)}) collective-permute-start(f32[24,128]{1,0:T(8,128)S(1)} %get-tuple-element.89), channel_id=1, source_target_pairs={{0,2},{1,3},{2,0},{3,1},{4,6},{5,7},{6,4},{7,5},{8,10},{9,11},{10,... | collective-permute-start | bytes 36872 | tf_op jit(solution)/shard_map/ppermute | solution.py:616
  17.8 1.6 %collective-permute-start.13 = (f32[24,128]{1,0:T(8,128)S(1)}, f32[24,128]{1,0:T(8,128)S(1)}, u32[]{:S(2)}, u32[]{:S(2)}) collective-permute-start(f32[24,128]{1,0:T(8,128)S(1)} %get-tuple-element.90), channel_id=1, source_target_pairs={{0,2},{1,3},{2,0},{3,1},{4,6},{5,7},{6,4},{7,5},{8,10},{9,11},{10,... | collective-permute-start | bytes 36872 | tf_op jit(solution)/shard_map/ppermute | solution.py:616
  18.2 1.2 %collective-permute-start.14 = (f32[16,128]{1,0:T(8,128)S(1)}, f32[16,128]{1,0:T(8,128)S(1)}, u32[]{:S(2)}, u32[]{:S(2)}) collective-permute-start(f32[16,128]{1,0:T(8,128)S(1)} %get-tuple-element.91), channel_id=1, source_target_pairs={{0,2},{1,3},{2,0},{3,1},{4,6},{5,7},{6,4},{7,5},{8,10},{9,11},{10,... | collective-permute-start | bytes 24584 | tf_op jit(solution)/shard_map/ppermute | solution.py:616
  21.5 4.5 %collective-permute-start.15 = (f32[64,128]{1,0:T(8,128)S(1)}, f32[64,128]{1,0:T(8,128)S(1)}, u32[]{:S(2)}, u32[]{:S(2)}) collective-permute-start(f32[64,128]{1,0:T(8,128)S(1)} %get-tuple-element.95), channel_id=1, source_target_pairs={{0,1},{1,0},{2,4},{3,5},{4,2},{5,3},{6,8},{7,9},{8,6},{9,7},{10,12... | collective-permute-start | bytes 98312 | tf_op jit(solution)/shard_map/ppermute | solution.py:616
  22.3 3.7 %collective-permute-start.16 = (f32[28,128]{1,0:T(8,128)S(1)}, f32[28,128]{1,0:T(8,128)S(1)}, u32[]{:S(2)}, u32[]{:S(2)}) collective-permute-start(f32[28,128]{1,0:T(8,128)S(1)} %get-tuple-element.96.refs_9_.refs_12_), channel_id=1, source_target_pairs={{1,0},{0,1},{3,2},{2,3},{5,4},{4,5},{7,6},{6,7},{9,8},{8,9},{11,10... | collective-permute-start | bytes 43016 | tf_op jit(solution)/shard_map/ppermute | solution.py:621
  23.6 1.7 %collective-permute-start.17 = (f32[24,128]{1,0:T(8,128)S(1)}, f32[24,128]{1,0:T(8,128)S(1)}, u32[]{:S(2)}, u32[]{:S(2)}) collective-permute-start(f32[24,128]{1,0:T(8,128)S(1)} %get-tuple-element.97), channel_id=1, source_target_pairs={{0,2},{1,3},{2,0},{3,1},{4,6},{5,7},{6,4},{7,5},{8,10},{9,11},{10,... | collective-permute-start | bytes 36872 | tf_op jit(solution)/shard_map/ppermute | solution.py:616
  23.6 1.7 %collective-permute-start.18 = (f32[24,128]{1,0:T(8,128)S(1)}, f32[24,128]{1,0:T(8,128)S(1)}, u32[]{:S(2)}, u32[]{:S(2)}) collective-permute-start(f32[24,128]{1,0:T(8,128)S(1)} %get-tuple-element.98), channel_id=1, source_target_pairs={{0,2},{1,3},{2,0},{3,1},{4,6},{5,7},{6,4},{7,5},{8,10},{9,11},{10,... | collective-permute-start | bytes 36872 | tf_op jit(solution)/shard_map/ppermute | solution.py:616
  24.1 1.2 %collective-permute-start.19 = (f32[16,128]{1,0:T(8,128)S(1)}, f32[16,128]{1,0:T(8,128)S(1)}, u32[]{:S(2)}, u32[]{:S(2)}) collective-permute-start(f32[16,128]{1,0:T(8,128)S(1)} %get-tuple-element.99), channel_id=1, source_target_pairs={{0,2},{1,3},{2,0},{3,1},{4,6},{5,7},{6,4},{7,5},{8,10},{9,11},{10,... | collective-permute-start | bytes 24584 | tf_op jit(solution)/shard_map/ppermute | solution.py:616
  26.2 5.2 %collective-permute-start.20 = (f32[2,128]{1,0:T(2,128)S(1)}, f32[2,128]{1,0:T(2,128)S(1)}, u32[]{:S(2)}, u32[]{:S(2)}) collective-permute-start(f32[2,128]{1,0:T(2,128)S(1)} %get-tuple-element.107), channel_id=1, source_target_pairs={{0,1},{1,0},{2,4},{3,5},{4,2},{5,3},{6,8},{7,9},{8,6},{9,7},{10,12... | collective-permute-start | bytes 3080 | tf_op jit(solution)/shard_map/ppermute | solution.py:616
  27.5 3.9 %collective-permute-start.21 = (f32[2,128]{1,0:T(2,128)S(1)}, f32[2,128]{1,0:T(2,128)S(1)}, u32[]{:S(2)}, u32[]{:S(2)}) collective-permute-start(f32[2,128]{1,0:T(2,128)S(1)} %get-tuple-element.108), channel_id=1, source_target_pairs={{0,1},{1,0},{2,3},{3,2},{4,8},{5,9},{6,10},{7,11},{8,4},{9,5},{10,... | collective-permute-start | bytes 3080 | tf_op jit(solution)/shard_map/ppermute | solution.py:616
  28.2 3.6 %collective-permute-start.22 = (f32[2,128]{1,0:T(2,128)S(1)}, f32[2,128]{1,0:T(2,128)S(1)}, u32[]{:S(2)}, u32[]{:S(2)}) collective-permute-start(f32[2,128]{1,0:T(2,128)S(1)} %get-tuple-element.109), channel_id=1, source_target_pairs={{0,4},{1,5},{2,6},{3,7},{4,0},{5,1},{6,2},{7,3},{8,12},{9,13},{10,... | collective-permute-start | bytes 3080 | tf_op jit(solution)/shard_map/ppermute | solution.py:616
  29.9 1.9 %collective-permute-start.23 = (f32[2,128]{1,0:T(2,128)S(1)}, f32[2,128]{1,0:T(2,128)S(1)}, u32[]{:S(2)}, u32[]{:S(2)}) collective-permute-start(f32[2,128]{1,0:T(2,128)S(1)} %get-tuple-element.110), channel_id=1, source_target_pairs={{0,2},{1,3},{2,0},{3,1},{4,6},{5,7},{6,4},{7,5},{8,10},{9,11},{10,... | collective-permute-start | bytes 3080 | tf_op jit(solution)/shard_map/ppermute | solution.py:616
  (4 other events, 3.8 us)

commit v11 on v10

--- a/solution.py
+++ b/solution.py
@@ -13,7 +13,7 @@
 PATCH_DEV = 2
 REACH = 2
 PATCH_ROWS = 16
-LATER = 7
+LATER = 11
 FAULT = 24
 SENT_FAULT = 28
 PARTS = (24, 24, 16)
@@ -517,12 +517,12 @@
             even_out[...] = message[at : at + even_out.shape[0]]
 
 
-def mask_kernel(owner_ref, _, back_ref, flags_ref, stress_ref, mask_ref, weight_ref, *, z_elems):
+def mask_kernel(owner_ref, flags_ref, stress_ref, _, mask_ref, weight_ref, *, z_elems):
     shape = (PATCH_ROWS, mask_ref.shape[1])
     first = (lax.axis_index("dom") - REACH) * PATCH_DEV
     number = lax.broadcasted_iota(jnp.int32, shape, 0) + first
     for x in range(4):
-        mask = jnp.where(number == owner_ref[0, x], 1.0, 0.0)
+        mask = jnp.where(number == owner_ref[:, x : x + 1], 1.0, 0.0)
         mask_ref[PATCH_ROWS * x : PATCH_ROWS * (x + 1)] = mask
     stress = stress_ref[...]
     weights = []
@@ -656,9 +656,12 @@
             faults = [from_behind(fault_rows, "depth", 1), from_behind(fault_rows, "depth", -1)]
         return [swapped(part, 1, 0) for part in even], swapped(odd, 1, 1), faults
 
-    later_used = (edge_table, following, rho, mass, own_table, far_table, touch_table)
+    later_used = (
+        edge_table, following, rho, mass, own_table, far_table, touch_table, back, flags,
+        normal_stress[0], patch_owner,
+    )
     assert len(later_used) == LATER
-    cur, *even, odd, fault_rows, material, edge_table, following, rho, mass, own_table, far_table, touch_table = kernel_call(
+    first_out = kernel_call(
         first_kernel,
         [field] + parts + [plane, (FAULT + 4 * steps, lanes), (8, lanes)]
         + [(t.shape, t.dtype) for t in later_used],
@@ -667,6 +670,9 @@
         in_hbm=range(5 + LATER),
         kept=range(5, 5 + LATER),
     )
+    cur, *even, odd, fault_rows, material = first_out[:-LATER]
+    edge_table, following, rho, mass, own_table, far_table, touch_table, back = first_out[-LATER:-3]
+    flags, stress, owner = first_out[-3:]
     even_in, odd_in, fault_in = exchange(even, odd, fault_rows)
     first_fault, first_in = fault_rows, fault_in
     fol, minv = kernel_call(
@@ -697,9 +703,8 @@
             mask, weight = kernel_call(
                 mask_kernel,
                 [(4 * PATCH_ROWS, lanes), (4 * steps, lanes)],
-                [patch_owner, cur, back, flags, normal_stress[0]],
-                (0,),
-                unread=(1,),
+                [owner, flags, stress, cur],
+                unread=(3,),
                 z_elems=z_elems,
             )
             args.append(mask)

time: 32.6 us -> 32.2 us (0.988)
  waiting for transfers between devices: 4.29 us -> 5.61 us
  local copies, waits for them, and re-layouts: 0.69 us -> 0 us
  Pallas kernels: 9.71 us -> 9.19 us
  starting transfers between devices: 16.3 us -> 15.9 us
    ppermute x20, waiting for transfers between devices: 1.37 us -> 2.3 us  [swapped(): return lax.ppermute(block, ('dom', 'depth'), route)]
    unnamed x8 -> x0, local copies, waits for them, and re-layouts: 0.69 us -> none
    pallas_call x13, Pallas kernels: 9.71 us -> 9.19 us  [kernel_call(): pl.pallas_call(functools.partial(body, **static) if static else body, out...]
    ppermute x20, starting transfers between devices: 12.5 us -> 12.1 us  [swapped(): return lax.ppermute(block, ('dom', 'depth'), route)]
    ppermute x4, waiting for transfers between devices: 2.91 us -> 3.31 us  [from_behind(): lax.ppermute(block, axis, [((i - distance) % size, i) for i in range(size)])]
  transfers between devices with their start and end apart: 24 -> 24, of which waited for: 6 -> 9; matrix products, arithmetic and copies ran while one was open for 0% -> 0% of each run, Pallas kernels for 15% -> 14%
where the time goes in v11:
time: 32.2 us; the launch traced here: 32 us
  starting transfers between devices  15.9 us (49%)
  Pallas kernels  9.19 us (29%)
  waiting for transfers between devices  5.61 us (17%)
  between operations  0.74 us (2%)
  other arithmetic  0.57 us (2%)
    ppermute x20, starting transfers between devices, swapped(): return lax.ppermute(block, ('dom', 'depth'), route)  12.1 us
    pallas_call x13, Pallas kernels, kernel_call(): pl.pallas_call(functools.partial(body, **static) if static else body, out...  9.19 us
    ppermute x4, starting transfers between devices, from_behind(): lax.ppermute(block, axis, [((i - distance) % size, i) for i in range(size)])  3.78 us
    ppermute x4, waiting for transfers between devices, from_behind(): lax.ppermute(block, axis, [((i - distance) % size, i) for i in range(size)])  3.31 us
    ppermute x20, waiting for transfers between devices, swapped(): return lax.ppermute(block, ('dom', 'depth'), route)  2.3 us
  transfers between devices with their start and end apart: 24, of which 9 were waited for; matrix products, arithmetic and copies ran while one was open for 0% of the time, Pallas kernels for 14%

profile of v11, /device:TPU:0, one launch (start us, length us, event | category | flops | bytes accessed | tf_op | source)
XLA Modules:
  0.0 32.0 jit_solution(2262568979112068972)
XLA Ops:
  0.6 2.1 %shard_map.166 = (f32[320,128]{1,0:T(8,128)S(1)}, f32[24,128]{1,0:T(8,128)S(1)}, f32[24,128]{1,0:T(8,128)S(1)}, f32[16,128]{1,0:T(8,128)S(1)}, f32[64,128]{1,0:T...) custom-call(f32[3,17,4,128]{3,2,1,0:T(4,128)} %bitcast.12, ...), custom_call_target="tpu_custom_call" | custom-call | tf_op jit(solution)/shard_map/pallas_call | solution.py:593
  2.7 3.0 %collective-permute-start = (f32[64,128]{1,0:T(8,128)S(1)}, f32[64,128]{1,0:T(8,128)S(1)}, u32[]{:S(2)}, u32[]{:S(2)}) collective-permute-start(f32[64,128]{1,0:T(8,128)S(1)} %get-tuple-element.72), channel_id=1, source_target_pairs={{0,1},{1,0},{2,4},{3,5},{4,2},{5,3},{6,8},{7,9},{8,6},{9,7},{10,12... | collective-permute-start | bytes 98312 | tf_op jit(solution)/shard_map/ppermute | solution.py:616
  5.8 1.3 %collective-permute-start.2 = (f32[24,128]{1,0:T(8,128)S(1)}, f32[24,128]{1,0:T(8,128)S(1)}, u32[]{:S(2)}, u32[]{:S(2)}) collective-permute-start(f32[24,128]{1,0:T(8,128)S(1)} %get-tuple-element.74), channel_id=1, source_target_pairs={{0,2},{1,3},{2,0},{3,1},{4,6},{5,7},{6,4},{7,5},{8,10},{9,11},{10,... | collective-permute-start | bytes 36872 | tf_op jit(solution)/shard_map/ppermute | solution.py:616
  7.1 0.5 %collective-permute-start.4 = (f32[16,128]{1,0:T(8,128)S(1)}, f32[16,128]{1,0:T(8,128)S(1)}, u32[]{:S(2)}, u32[]{:S(2)}) collective-permute-start(f32[16,128]{1,0:T(8,128)S(1)} %get-tuple-element.76), channel_id=1, source_target_pairs={{0,2},{1,3},{2,0},{3,1},{4,6},{5,7},{6,4},{7,5},{8,10},{9,11},{10,... | collective-permute-start | bytes 24584 | tf_op jit(solution)/shard_map/ppermute | solution.py:616
  7.6 0.5 %shard_map.167 = (f32[320,128]{1,0:T(8,128)S(1)}, f32[320,128]{1,0:T(8,128)S(1)}) custom-call(f32[3,17,4,128]{3,2,1,0:T(4,128)S(1)} %get-tuple-element.62.next_ref, f32[17,4,128]{2,1,0:T(4,128)S(1)} %get-tuple-element.63.density_ref, f32[320,128]{1,0:T(8,128)S(1)} %get-tuple-element.64.mass_ref), custom_call_target="tpu_custom_call" | custom-call | tf_op jit(solution)/shard_map/pallas_call | solution.py:593
  8.1 0.5 %shard_map.168 = (f32[320,128]{1,0:T(8,128)S(1)}, f32[160,128]{1,0:T(8,128)S(1)}) custom-call(f32[320,128]{1,0:T(8,128)S(1)} %get-tuple-element.61.cur_ref.refs_0_.refs_1_, f32[8,128]{1,0:T(8,128)S(1)} %get-tuple-element.67.material_ref.refs_5_, bf16[2,640,384]{2,1,0:T(8,128)(2,1)S(1)} %get-tuple-element.68.own_ref, ...), custom_call_target="tpu_custom_call" | custom-call | tf_op jit(solution)/shard_map/pallas_call | solution.py:593
  8.7 0.8 %collective-permute-done.1.refs_7_.refs_11_.refs_4_ = f32[40,128]{1,0:T(8,128)S(1)} collective-permute-done((f32[40,128]{1,0:T(8,128)S(1)}, f32[40,128]{1,0:T(8,128)S(1)}, u32[]{:S(2)}, u32[]{:S(2)}) %collective-permute-start.1) | collective-permute-done | bytes 20512 | tf_op jit(solution)/shard_map/ppermute | solution.py:621
  9.5 0.8 %shard_map.169 = (f32[320,128]{1,0:T(8,128)S(1)}, f32[24,128]{1,0:T(8,128)S(1)}, f32[24,128]{1,0:T(8,128)S(1)}, f32[16,128]{1,0:T(8,128)S(1)}, f32[64,128]{1,0:T(8,128)S(1)}, /*index=5*/f32[28,128]{1,0:T(8,128)S(1)}) custom-call(f32[320,128]{1,0:T(8,128)S(1)} %get-tuple-element.61.cur_ref.refs_0_.refs_1_, f32[320,128]{1,0:T(8,128)S(1)} %get-tuple-element.65.refs_1_, ...), custom_call_target="tpu_custom_call" | custom-call | tf_op jit(solution)/shard_map/pallas_call | solution.py:593
  10.7 1.7 %collective-permute-start.6 = (f32[28,128]{1,0:T(8,128)S(1)}, f32[28,128]{1,0:T(8,128)S(1)}, u32[]{:S(2)}, u32[]{:S(2)}) collective-permute-start(f32[28,128]{1,0:T(8,128)S(1)} %get-tuple-element.83.refs_12_.refs_5_), channel_id=1, source_target_pairs={{1,0},{0,1},{3,2},{2,3},{5,4},{4,5},{7,6},{6,7},{9,8},{8,9},{11,10... | collective-permute-start | bytes 43016 | tf_op jit(solution)/shard_map/ppermute | solution.py:621
  12.4 0.5 %collective-permute-start.8 = (f32[24,128]{1,0:T(8,128)S(1)}, f32[24,128]{1,0:T(8,128)S(1)}, u32[]{:S(2)}, u32[]{:S(2)}) collective-permute-start(f32[24,128]{1,0:T(8,128)S(1)} %get-tuple-element.85), channel_id=1, source_target_pairs={{0,2},{1,3},{2,0},{3,1},{4,6},{5,7},{6,4},{7,5},{8,10},{9,11},{10,... | collective-permute-start | bytes 36872 | tf_op jit(solution)/shard_map/ppermute | solution.py:616
  12.9 0.5 %shard_map.170 = (f32[320,128]{1,0:T(8,128)S(1)}, f32[160,128]{1,0:T(8,128)S(1)}) custom-call(f32[320,128]{1,0:T(8,128)S(1)} %get-tuple-element.79.cur_ref._.refs_0_.refs_1_, f32[8,128]{1,0:T(8,128)S(1)} %get-tuple-element.67.material_ref.refs_5_, bf16[2,640,384]{2,1,0:T(8,128)(2,1)S(1)} %get-tuple-element.68.own_ref, ...), custom_call_target="tpu_custom_call" | custom-call | tf_op jit(solution)/shard_map/pallas_call | solution.py:593
  13.6 0.5 %collective-permute-done.9.refs_10_ = f32[16,128]{1,0:T(8,128)S(1)} collective-permute-done((f32[16,128]{1,0:T(8,128)S(1)}, f32[16,128]{1,0:T(8,128)S(1)}, u32[]{:S(2)}, u32[]{:S(2)}) %collective-permute-start.9) | collective-permute-done | bytes 8224 | tf_op jit(solution)/shard_map/ppermute | solution.py:616
  14.5 0.8 %shard_map.172 = (f32[320,128]{1,0:T(8,128)S(1)}, f32[24,128]{1,0:T(8,128)S(1)}, f32[24,128]{1,0:T(8,128)S(1)}, f32[16,128]{1,0:T(8,128)S(1)}, f32[64,128]{1,0:T(8,128)S(1)}, /*index=5*/f32[28,128]{1,0:T(8,128)S(1)}) custom-call(f32[320,128]{1,0:T(8,128)S(1)} %get-tuple-element.79.cur_ref._.refs_0_.refs_1_, ...), custom_call_target="tpu_custom_call" | custom-call | tf_op jit(solution)/shard_map/pallas_call | solution.py:593
  15.3 1.7 %collective-permute-start.10 = (f32[64,128]{1,0:T(8,128)S(1)}, f32[64,128]{1,0:T(8,128)S(1)}, u32[]{:S(2)}, u32[]{:S(2)}) collective-permute-start(f32[64,128]{1,0:T(8,128)S(1)} %get-tuple-element.94), channel_id=1, source_target_pairs={{0,1},{1,0},{2,4},{3,5},{4,2},{5,3},{6,8},{7,9},{8,6},{9,7},{10,12... | collective-permute-start | bytes 98312 | tf_op jit(solution)/shard_map/ppermute | solution.py:616
  17.9 0.5 %shard_map.173 = (f32[320,128]{1,0:T(8,128)S(1)}, f32[160,128]{1,0:T(8,128)S(1)}) custom-call(f32[320,128]{1,0:T(8,128)S(1)} %get-tuple-element.91.cur_ref.refs_0_.refs_1_, f32[8,128]{1,0:T(8,128)S(1)} %get-tuple-element.67.material_ref.refs_5_, bf16[2,640,384]{2,1,0:T(8,128)(2,1)S(1)} %get-tuple-element.68.own_ref, ...), custom_call_target="tpu_custom_call" | custom-call | tf_op jit(solution)/shard_map/pallas_call | solution.py:593
  18.4 0.7 %collective-permute-done.14.refs_10_ = f32[16,128]{1,0:T(8,128)S(1)} collective-permute-done((f32[16,128]{1,0:T(8,128)S(1)}, f32[16,128]{1,0:T(8,128)S(1)}, u32[]{:S(2)}, u32[]{:S(2)}) %collective-permute-start.14) | collective-permute-done | bytes 8224 | tf_op jit(solution)/shard_map/ppermute | solution.py:616
  19.1 1.7 %collective-permute-done.11.refs_7_.refs_8_ = f32[28,128]{1,0:T(8,128)S(1)} collective-permute-done((f32[28,128]{1,0:T(8,128)S(1)}, f32[28,128]{1,0:T(8,128)S(1)}, u32[]{:S(2)}, u32[]{:S(2)}) %collective-permute-start.11) | collective-permute-done | bytes 14368 | tf_op jit(solution)/shard_map/ppermute | solution.py:621
  20.7 0.8 %shard_map.174 = (f32[320,128]{1,0:T(8,128)S(1)}, f32[24,128]{1,0:T(8,128)S(1)}, f32[24,128]{1,0:T(8,128)S(1)}, f32[16,128]{1,0:T(8,128)S(1)}, f32[64,128]{1,0:T(8,128)S(1)}, /*index=5*/f32[28,128]{1,0:T(8,128)S(1)}) custom-call(f32[320,128]{1,0:T(8,128)S(1)} %get-tuple-element.91.cur_ref.refs_0_.refs_1_, ...), custom_call_target="tpu_custom_call" | custom-call | tf_op jit(solution)/shard_map/pallas_call | solution.py:593
  22.0 1.7 %collective-permute-start.16 = (f32[28,128]{1,0:T(8,128)S(1)}, f32[28,128]{1,0:T(8,128)S(1)}, u32[]{:S(2)}, u32[]{:S(2)}) collective-permute-start(f32[28,128]{1,0:T(8,128)S(1)} %get-tuple-element.103.refs_9_.refs_12_), channel_id=1, source_target_pairs={{1,0},{0,1},{3,2},{2,3},{5,4},{4,5},{7,6},{6,7},{9,8},{8,9},{11,10... | collective-permute-start | bytes 43016 | tf_op jit(solution)/shard_map/ppermute | solution.py:621
  24.1 0.5 %shard_map.175 = (f32[320,128]{1,0:T(8,128)S(1)}, f32[160,128]{1,0:T(8,128)S(1)}) custom-call(f32[320,128]{1,0:T(8,128)S(1)} %get-tuple-element.99.cur_ref.refs_0_, f32[8,128]{1,0:T(8,128)S(1)} %get-tuple-element.67.material_ref.refs_5_, bf16[2,640,384]{2,1,0:T(8,128)(2,1)S(1)} %get-tuple-element.68.own_ref, bf16[160,256]{1,0:T(8,128)(2,1)S(1)} %get-tuple-element.69.touch_ref), custom_call_target="tpu_custom_call" | custom-call | tf_op jit(solution)/shard_map/pallas_call | solution.py:593
  25.8 1.7 %collective-permute-start.20 = (f32[2,128]{1,0:T(2,128)S(1)}, f32[2,128]{1,0:T(2,128)S(1)}, u32[]{:S(2)}, u32[]{:S(2)}) collective-permute-start(f32[2,128]{1,0:T(2,128)S(1)} %get-tuple-element.115), channel_id=1, source_target_pairs={{0,1},{1,0},{2,4},{3,5},{4,2},{5,3},{6,8},{7,9},{8,6},{9,7},{10,12... | collective-permute-start | bytes 3080 | tf_op jit(solution)/shard_map/ppermute | solution.py:616
  27.9 1.3 %collective-permute-start.22 = (f32[2,128]{1,0:T(2,128)S(1)}, f32[2,128]{1,0:T(2,128)S(1)}, u32[]{:S(2)}, u32[]{:S(2)}) collective-permute-start(f32[2,128]{1,0:T(2,128)S(1)} %get-tuple-element.117), channel_id=1, source_target_pairs={{0,4},{1,5},{2,6},{3,7},{4,0},{5,1},{6,2},{7,3},{8,12},{9,13},{10,... | collective-permute-start | bytes 3080 | tf_op jit(solution)/shard_map/ppermute | solution.py:616
  29.2 1.4 %shard_map.178 = (f32[3,17,4,128]{3,2,1,0:T(4,128)}, f32[3,17,4,128]{3,2,1,0:T(4,128)}) custom-call(f32[320,128]{1,0:T(8,128)S(1)} %get-tuple-element.99.cur_ref.refs_0_, f32[320,128]{1,0:T(8,128)S(1)} %get-tuple-element.91.cur_ref.refs_0_.refs_1_, f32[320,128]{1,0:T(8,128)S(1)} %get-tuple-element.66.refs_2_, f32[320,128]{1,0:T(8,128)S(1)} %get-tuple-element.100.refs_3_, ...), custom_call_target="tpu_custom_call" | custom-call | tf_op jit(solution)/shard_map/pallas_call | solution.py:593
  31.4 0.6 %add_bitcast_fusion = f32[1,2,128]{2,1,0:T(2,128)} fusion(f32[2,128]{1,0:T(2,128)S(1)} %collective-permute-done.23, f32[2,128]{1,0:T(2,128)S(1)} %collective-permute-done.22, f32[2,128]{1,0:T(2,128)S(1)} %collective-permute-done.21, f32[2,128]{1,0:T(2,128)S(1)} %get-tuple-element.111.refs_16_, f32[2,128]{1,0:T(2,128)S(1)} %collective-permute-done.20), kind=kLoop, calls=%fused_computation | loop fusion | flops 1024 | bytes 6144 | tf_op jit(solution)/shard_map/broadcast_in_dim | solution.py:760
  (38 shorter events, 5.1 us)
Async XLA Ops:
  2.7 6.8 %collective-permute-start = (f32[64,128]{1,0:T(8,128)S(1)}, f32[64,128]{1,0:T(8,128)S(1)}, u32[]{:S(2)}, u32[]{:S(2)}) collective-permute-start(f32[64,128]{1,0:T(8,128)S(1)} %get-tuple-element.72), channel_id=1, source_target_pairs={{0,1},{1,0},{2,4},{3,5},{4,2},{5,3},{6,8},{7,9},{8,6},{9,7},{10,12... | collective-permute-start | bytes 98312 | tf_op jit(solution)/shard_map/ppermute | solution.py:616
  5.7 3.8 %collective-permute-start.1 = (f32[40,128]{1,0:T(8,128)S(1)}, f32[40,128]{1,0:T(8,128)S(1)}, u32[]{:S(2)}, u32[]{:S(2)}) collective-permute-start(f32[40,128]{1,0:T(8,128)S(1)} %get-tuple-element.73.refs_12_.refs_13_.refs_3_), channel_id=1, source_target_pairs={{1,0},{0,1},{3,2},{2,3},{5,4},{4,5},{7,6},{6,7},{9,8},{8,9},{11,10... | collective-permute-start | bytes 61448 | tf_op jit(solution)/shard_map/ppermute | solution.py:621
  5.8 2.8 %collective-permute-start.2 = (f32[24,128]{1,0:T(8,128)S(1)}, f32[24,128]{1,0:T(8,128)S(1)}, u32[]{:S(2)}, u32[]{:S(2)}) collective-permute-start(f32[24,128]{1,0:T(8,128)S(1)} %get-tuple-element.74), channel_id=1, source_target_pairs={{0,2},{1,3},{2,0},{3,1},{4,6},{5,7},{6,4},{7,5},{8,10},{9,11},{10,... | collective-permute-start | bytes 36872 | tf_op jit(solution)/shard_map/ppermute | solution.py:616
  7.1 1.6 %collective-permute-start.3 = (f32[24,128]{1,0:T(8,128)S(1)}, f32[24,128]{1,0:T(8,128)S(1)}, u32[]{:S(2)}, u32[]{:S(2)}) collective-permute-start(f32[24,128]{1,0:T(8,128)S(1)} %get-tuple-element.75), channel_id=1, source_target_pairs={{0,2},{1,3},{2,0},{3,1},{4,6},{5,7},{6,4},{7,5},{8,10},{9,11},{10,... | collective-permute-start | bytes 36872 | tf_op jit(solution)/shard_map/ppermute | solution.py:616
  7.1 1.5 %collective-permute-start.4 = (f32[16,128]{1,0:T(8,128)S(1)}, f32[16,128]{1,0:T(8,128)S(1)}, u32[]{:S(2)}, u32[]{:S(2)}) collective-permute-start(f32[16,128]{1,0:T(8,128)S(1)} %get-tuple-element.76), channel_id=1, source_target_pairs={{0,2},{1,3},{2,0},{3,1},{4,6},{5,7},{6,4},{7,5},{8,10},{9,11},{10,... | collective-permute-start | bytes 24584 | tf_op jit(solution)/shard_map/ppermute | solution.py:616
  10.4 4.1 %collective-permute-start.5 = (f32[64,128]{1,0:T(8,128)S(1)}, f32[64,128]{1,0:T(8,128)S(1)}, u32[]{:S(2)}, u32[]{:S(2)}) collective-permute-start(f32[64,128]{1,0:T(8,128)S(1)} %get-tuple-element.82), channel_id=1, source_target_pairs={{0,1},{1,0},{2,4},{3,5},{4,2},{5,3},{6,8},{7,9},{8,6},{9,7},{10,12... | collective-permute-start | bytes 98312 | tf_op jit(solution)/shard_map/ppermute | solution.py:616
  10.7 3.8 %collective-permute-start.6 = (f32[28,128]{1,0:T(8,128)S(1)}, f32[28,128]{1,0:T(8,128)S(1)}, u32[]{:S(2)}, u32[]{:S(2)}) collective-permute-start(f32[28,128]{1,0:T(8,128)S(1)} %get-tuple-element.83.refs_12_.refs_5_), channel_id=1, source_target_pairs={{1,0},{0,1},{3,2},{2,3},{5,4},{4,5},{7,6},{6,7},{9,8},{8,9},{11,10... | collective-permute-start | bytes 43016 | tf_op jit(solution)/shard_map/ppermute | solution.py:621
  12.4 1.7 %collective-permute-start.7 = (f32[24,128]{1,0:T(8,128)S(1)}, f32[24,128]{1,0:T(8,128)S(1)}, u32[]{:S(2)}, u32[]{:S(2)}) collective-permute-start(f32[24,128]{1,0:T(8,128)S(1)} %get-tuple-element.84), channel_id=1, source_target_pairs={{0,2},{1,3},{2,0},{3,1},{4,6},{5,7},{6,4},{7,5},{8,10},{9,11},{10,... | collective-permute-start | bytes 36872 | tf_op jit(solution)/shard_map/ppermute | solution.py:616
  12.4 1.7 %collective-permute-start.8 = (f32[24,128]{1,0:T(8,128)S(1)}, f32[24,128]{1,0:T(8,128)S(1)}, u32[]{:S(2)}, u32[]{:S(2)}) collective-permute-start(f32[24,128]{1,0:T(8,128)S(1)} %get-tuple-element.85), channel_id=1, source_target_pairs={{0,2},{1,3},{2,0},{3,1},{4,6},{5,7},{6,4},{7,5},{8,10},{9,11},{10,... | collective-permute-start | bytes 36872 | tf_op jit(solution)/shard_map/ppermute | solution.py:616
  12.9 1.2 %collective-permute-start.9 = (f32[16,128]{1,0:T(8,128)S(1)}, f32[16,128]{1,0:T(8,128)S(1)}, u32[]{:S(2)}, u32[]{:S(2)}) collective-permute-start(f32[16,128]{1,0:T(8,128)S(1)} %get-tuple-element.86), channel_id=1, source_target_pairs={{0,2},{1,3},{2,0},{3,1},{4,6},{5,7},{6,4},{7,5},{8,10},{9,11},{10,... | collective-permute-start | bytes 24584 | tf_op jit(solution)/shard_map/ppermute | solution.py:616
  15.3 5.4 %collective-permute-start.10 = (f32[64,128]{1,0:T(8,128)S(1)}, f32[64,128]{1,0:T(8,128)S(1)}, u32[]{:S(2)}, u32[]{:S(2)}) collective-permute-start(f32[64,128]{1,0:T(8,128)S(1)} %get-tuple-element.94), channel_id=1, source_target_pairs={{0,1},{1,0},{2,4},{3,5},{4,2},{5,3},{6,8},{7,9},{8,6},{9,7},{10,12... | collective-permute-start | bytes 98312 | tf_op jit(solution)/shard_map/ppermute | solution.py:616
  17.0 3.7 %collective-permute-start.11 = (f32[28,128]{1,0:T(8,128)S(1)}, f32[28,128]{1,0:T(8,128)S(1)}, u32[]{:S(2)}, u32[]{:S(2)}) collective-permute-start(f32[28,128]{1,0:T(8,128)S(1)} %get-tuple-element.95.refs_12_.refs_7_), channel_id=1, source_target_pairs={{1,0},{0,1},{3,2},{2,3},{5,4},{4,5},{7,6},{6,7},{9,8},{8,9},{11,10... | collective-permute-start | bytes 43016 | tf_op jit(solution)/shard_map/ppermute | solution.py:621
  17.4 1.7 %collective-permute-start.12 = (f32[24,128]{1,0:T(8,128)S(1)}, f32[24,128]{1,0:T(8,128)S(1)}, u32[]{:S(2)}, u32[]{:S(2)}) collective-permute-start(f32[24,128]{1,0:T(8,128)S(1)} %get-tuple-element.96), channel_id=1, source_target_pairs={{0,2},{1,3},{2,0},{3,1},{4,6},{5,7},{6,4},{7,5},{8,10},{9,11},{10,... | collective-permute-start | bytes 36872 | tf_op jit(solution)/shard_map/ppermute | solution.py:616
  17.4 1.7 %collective-permute-start.13 = (f32[24,128]{1,0:T(8,128)S(1)}, f32[24,128]{1,0:T(8,128)S(1)}, u32[]{:S(2)}, u32[]{:S(2)}) collective-permute-start(f32[24,128]{1,0:T(8,128)S(1)} %get-tuple-element.97), channel_id=1, source_target_pairs={{0,2},{1,3},{2,0},{3,1},{4,6},{5,7},{6,4},{7,5},{8,10},{9,11},{10,... | collective-permute-start | bytes 36872 | tf_op jit(solution)/shard_map/ppermute | solution.py:616
  17.9 1.2 %collective-permute-start.14 = (f32[16,128]{1,0:T(8,128)S(1)}, f32[16,128]{1,0:T(8,128)S(1)}, u32[]{:S(2)}, u32[]{:S(2)}) collective-permute-start(f32[16,128]{1,0:T(8,128)S(1)} %get-tuple-element.98), channel_id=1, source_target_pairs={{0,2},{1,3},{2,0},{3,1},{4,6},{5,7},{6,4},{7,5},{8,10},{9,11},{10,... | collective-permute-start | bytes 24584 | tf_op jit(solution)/shard_map/ppermute | solution.py:616
  21.6 4.1 %collective-permute-start.15 = (f32[64,128]{1,0:T(8,128)S(1)}, f32[64,128]{1,0:T(8,128)S(1)}, u32[]{:S(2)}, u32[]{:S(2)}) collective-permute-start(f32[64,128]{1,0:T(8,128)S(1)} %get-tuple-element.102), channel_id=1, source_target_pairs={{0,1},{1,0},{2,4},{3,5},{4,2},{5,3},{6,8},{7,9},{8,6},{9,7},{10,12... | collective-permute-start | bytes 98312 | tf_op jit(solution)/shard_map/ppermute | solution.py:616
  22.0 3.7 %collective-permute-start.16 = (f32[28,128]{1,0:T(8,128)S(1)}, f32[28,128]{1,0:T(8,128)S(1)}, u32[]{:S(2)}, u32[]{:S(2)}) collective-permute-start(f32[28,128]{1,0:T(8,128)S(1)} %get-tuple-element.103.refs_9_.refs_12_), channel_id=1, source_target_pairs={{1,0},{0,1},{3,2},{2,3},{5,4},{4,5},{7,6},{6,7},{9,8},{8,9},{11,10... | collective-permute-start | bytes 43016 | tf_op jit(solution)/shard_map/ppermute | solution.py:621
  23.6 1.7 %collective-permute-start.17 = (f32[24,128]{1,0:T(8,128)S(1)}, f32[24,128]{1,0:T(8,128)S(1)}, u32[]{:S(2)}, u32[]{:S(2)}) collective-permute-start(f32[24,128]{1,0:T(8,128)S(1)} %get-tuple-element.104), channel_id=1, source_target_pairs={{0,2},{1,3},{2,0},{3,1},{4,6},{5,7},{6,4},{7,5},{8,10},{9,11},{10,... | collective-permute-start | bytes 36872 | tf_op jit(solution)/shard_map/ppermute | solution.py:616
  23.6 1.7 %collective-permute-start.18 = (f32[24,128]{1,0:T(8,128)S(1)}, f32[24,128]{1,0:T(8,128)S(1)}, u32[]{:S(2)}, u32[]{:S(2)}) collective-permute-start(f32[24,128]{1,0:T(8,128)S(1)} %get-tuple-element.105), channel_id=1, source_target_pairs={{0,2},{1,3},{2,0},{3,1},{4,6},{5,7},{6,4},{7,5},{8,10},{9,11},{10,... | collective-permute-start | bytes 36872 | tf_op jit(solution)/shard_map/ppermute | solution.py:616
  24.1 1.2 %collective-permute-start.19 = (f32[16,128]{1,0:T(8,128)S(1)}, f32[16,128]{1,0:T(8,128)S(1)}, u32[]{:S(2)}, u32[]{:S(2)}) collective-permute-start(f32[16,128]{1,0:T(8,128)S(1)} %get-tuple-element.106), channel_id=1, source_target_pairs={{0,2},{1,3},{2,0},{3,1},{4,6},{5,7},{6,4},{7,5},{8,10},{9,11},{10,... | collective-permute-start | bytes 24584 | tf_op jit(solution)/shard_map/ppermute | solution.py:616
  25.8 4.8 %collective-permute-start.20 = (f32[2,128]{1,0:T(2,128)S(1)}, f32[2,128]{1,0:T(2,128)S(1)}, u32[]{:S(2)}, u32[]{:S(2)}) collective-permute-start(f32[2,128]{1,0:T(2,128)S(1)} %get-tuple-element.115), channel_id=1, source_target_pairs={{0,1},{1,0},{2,4},{3,5},{4,2},{5,3},{6,8},{7,9},{8,6},{9,7},{10,12... | collective-permute-start | bytes 3080 | tf_op jit(solution)/shard_map/ppermute | solution.py:616
  27.5 3.6 %collective-permute-start.21 = (f32[2,128]{1,0:T(2,128)S(1)}, f32[2,128]{1,0:T(2,128)S(1)}, u32[]{:S(2)}, u32[]{:S(2)}) collective-permute-start(f32[2,128]{1,0:T(2,128)S(1)} %get-tuple-element.116), channel_id=1, source_target_pairs={{0,1},{1,0},{2,3},{3,2},{4,8},{5,9},{6,10},{7,11},{8,4},{9,5},{10,... | collective-permute-start | bytes 3080 | tf_op jit(solution)/shard_map/ppermute | solution.py:616
  27.9 3.6 %collective-permute-start.22 = (f32[2,128]{1,0:T(2,128)S(1)}, f32[2,128]{1,0:T(2,128)S(1)}, u32[]{:S(2)}, u32[]{:S(2)}) collective-permute-start(f32[2,128]{1,0:T(2,128)S(1)} %get-tuple-element.117), channel_id=1, source_target_pairs={{0,4},{1,5},{2,6},{3,7},{4,0},{5,1},{6,2},{7,3},{8,12},{9,13},{10,... | collective-permute-start | bytes 3080 | tf_op jit(solution)/shard_map/ppermute | solution.py:616
  29.2 2.2 %collective-permute-start.23 = (f32[2,128]{1,0:T(2,128)S(1)}, f32[2,128]{1,0:T(2,128)S(1)}, u32[]{:S(2)}, u32[]{:S(2)}) collective-permute-start(f32[2,128]{1,0:T(2,128)S(1)} %get-tuple-element.118), channel_id=1, source_target_pairs={{0,2},{1,3},{2,0},{3,1},{4,6},{5,7},{6,4},{7,5},{8,10},{9,11},{10,... | collective-permute-start | bytes 3080 | tf_op jit(solution)/shard_map/ppermute | solution.py:616

commit v12 on v11

--- a/solution.py
+++ b/solution.py
@@ -348,13 +348,14 @@
     scratch, now_ref, flags_ref, weak_ref, lame_ref, shear_ref, sems = refs
     copies = start_copies(
         [
+            (now_hbm, now_ref),
+            (later_hbm[0], later_refs[0]),
+            (lame_hbm, lame_ref),
+            (shear_hbm, shear_ref),
             (flags_hbm, flags_ref),
             (weak_hbm, weak_ref),
-            (lame_hbm, lame_ref),
-            (shear_hbm, shear_ref),
-            (now_hbm, now_ref),
         ]
-        + list(zip(later_hbm, later_refs)),
+        + list(zip(later_hbm[1:], later_refs[1:])),
         sems,
     )
     edge_ref = later_refs[0]
@@ -741,7 +742,7 @@
                 steps=steps,
             )
             patch_sums = sums[0]
-            for i, distance, group in ((2, 1, 1), (4, 2, 1), (3, 2, 0), (1, 1, 0)):
+            for i, distance, group in ((4, 2, 1), (2, 1, 1), (3, 2, 0), (1, 1, 0)):
                 patch_sums = patch_sums + swapped(sums[i], distance, group)
             earlier, later = kernel_call(
                 step_kernel,

time: 32.2 us -> 32.1 us (level)
  no operation moved by 1% of the time
where the time goes in v12:
time: 32.1 us; the launch traced here: 32 us
  starting transfers between devices  15.8 us (49%)
  Pallas kernels  9.14 us (28%)
  waiting for transfers between devices  5.71 us (18%)
  between operations  0.74 us (2%)
  other arithmetic  0.57 us (2%)
    ppermute x20, starting transfers between devices, swapped(): return lax.ppermute(block, ('dom', 'depth'), route)  12 us
    pallas_call x13, Pallas kernels, kernel_call(): pl.pallas_call(functools.partial(body, **static) if static else body, out...  9.14 us
    ppermute x4, starting transfers between devices, from_behind(): lax.ppermute(block, axis, [((i - distance) % size, i) for i in range(size)])  3.78 us
    ppermute x4, waiting for transfers between devices, from_behind(): lax.ppermute(block, axis, [((i - distance) % size, i) for i in range(size)])  3.3 us
    ppermute x20, waiting for transfers between devices, swapped(): return lax.ppermute(block, ('dom', 'depth'), route)  2.4 us
  transfers between devices with their start and end apart: 24, of which 9 were waited for; matrix products, arithmetic and copies ran while one was open for 0% of the time, Pallas kernels for 14%

profile of v12, /device:TPU:0, one launch (start us, length us, event | category | flops | bytes accessed | tf_op | source)
XLA Modules:
  0.0 32.0 jit_solution(936130449577595366)
XLA Ops:
  0.6 2.0 %shard_map.166 = (f32[320,128]{1,0:T(8,128)S(1)}, f32[24,128]{1,0:T(8,128)S(1)}, f32[24,128]{1,0:T(8,128)S(1)}, f32[16,128]{1,0:T(8,128)S(1)}, f32[64,128]{1,0:T...) custom-call(f32[3,17,4,128]{3,2,1,0:T(4,128)} %bitcast.12, ...), custom_call_target="tpu_custom_call" | custom-call | tf_op jit(solution)/shard_map/pallas_call | solution.py:594
  2.7 3.0 %collective-permute-start = (f32[64,128]{1,0:T(8,128)S(1)}, f32[64,128]{1,0:T(8,128)S(1)}, u32[]{:S(2)}, u32[]{:S(2)}) collective-permute-start(f32[64,128]{1,0:T(8,128)S(1)} %get-tuple-element.72), channel_id=1, source_target_pairs={{0,1},{1,0},{2,4},{3,5},{4,2},{5,3},{6,8},{7,9},{8,6},{9,7},{10,12... | collective-permute-start | bytes 98312 | tf_op jit(solution)/shard_map/ppermute | solution.py:617
  5.8 1.3 %collective-permute-start.2 = (f32[24,128]{1,0:T(8,128)S(1)}, f32[24,128]{1,0:T(8,128)S(1)}, u32[]{:S(2)}, u32[]{:S(2)}) collective-permute-start(f32[24,128]{1,0:T(8,128)S(1)} %get-tuple-element.74), channel_id=1, source_target_pairs={{0,2},{1,3},{2,0},{3,1},{4,6},{5,7},{6,4},{7,5},{8,10},{9,11},{10,... | collective-permute-start | bytes 36872 | tf_op jit(solution)/shard_map/ppermute | solution.py:617
  7.1 0.5 %collective-permute-start.4 = (f32[16,128]{1,0:T(8,128)S(1)}, f32[16,128]{1,0:T(8,128)S(1)}, u32[]{:S(2)}, u32[]{:S(2)}) collective-permute-start(f32[16,128]{1,0:T(8,128)S(1)} %get-tuple-element.76), channel_id=1, source_target_pairs={{0,2},{1,3},{2,0},{3,1},{4,6},{5,7},{6,4},{7,5},{8,10},{9,11},{10,... | collective-permute-start | bytes 24584 | tf_op jit(solution)/shard_map/ppermute | solution.py:617
  7.6 0.5 %shard_map.167 = (f32[320,128]{1,0:T(8,128)S(1)}, f32[320,128]{1,0:T(8,128)S(1)}) custom-call(f32[3,17,4,128]{3,2,1,0:T(4,128)S(1)} %get-tuple-element.62.next_ref, f32[17,4,128]{2,1,0:T(4,128)S(1)} %get-tuple-element.63.density_ref, f32[320,128]{1,0:T(8,128)S(1)} %get-tuple-element.64.mass_ref), custom_call_target="tpu_custom_call" | custom-call | tf_op jit(solution)/shard_map/pallas_call | solution.py:594
  8.1 0.5 %shard_map.168 = (f32[320,128]{1,0:T(8,128)S(1)}, f32[160,128]{1,0:T(8,128)S(1)}) custom-call(f32[320,128]{1,0:T(8,128)S(1)} %get-tuple-element.61.cur_ref.refs_0_.refs_1_, f32[8,128]{1,0:T(8,128)S(1)} %get-tuple-element.67.material_ref.refs_5_, bf16[2,640,384]{2,1,0:T(8,128)(2,1)S(1)} %get-tuple-element.68.own_ref, ...), custom_call_target="tpu_custom_call" | custom-call | tf_op jit(solution)/shard_map/pallas_call | solution.py:594
  8.6 0.8 %collective-permute-done.1.refs_7_.refs_11_.refs_4_ = f32[40,128]{1,0:T(8,128)S(1)} collective-permute-done((f32[40,128]{1,0:T(8,128)S(1)}, f32[40,128]{1,0:T(8,128)S(1)}, u32[]{:S(2)}, u32[]{:S(2)}) %collective-permute-start.1) | collective-permute-done | bytes 20512 | tf_op jit(solution)/shard_map/ppermute | solution.py:622
  9.5 0.8 %shard_map.169 = (f32[320,128]{1,0:T(8,128)S(1)}, f32[24,128]{1,0:T(8,128)S(1)}, f32[24,128]{1,0:T(8,128)S(1)}, f32[16,128]{1,0:T(8,128)S(1)}, f32[64,128]{1,0:T(8,128)S(1)}, /*index=5*/f32[28,128]{1,0:T(8,128)S(1)}) custom-call(f32[320,128]{1,0:T(8,128)S(1)} %get-tuple-element.61.cur_ref.refs_0_.refs_1_, f32[320,128]{1,0:T(8,128)S(1)} %get-tuple-element.65.refs_1_, ...), custom_call_target="tpu_custom_call" | custom-call | tf_op jit(solution)/shard_map/pallas_call | solution.py:594
  10.7 1.7 %collective-permute-start.6 = (f32[28,128]{1,0:T(8,128)S(1)}, f32[28,128]{1,0:T(8,128)S(1)}, u32[]{:S(2)}, u32[]{:S(2)}) collective-permute-start(f32[28,128]{1,0:T(8,128)S(1)} %get-tuple-element.83.refs_12_.refs_5_), channel_id=1, source_target_pairs={{1,0},{0,1},{3,2},{2,3},{5,4},{4,5},{7,6},{6,7},{9,8},{8,9},{11,10... | collective-permute-start | bytes 43016 | tf_op jit(solution)/shard_map/ppermute | solution.py:622
  12.9 0.5 %shard_map.170 = (f32[320,128]{1,0:T(8,128)S(1)}, f32[160,128]{1,0:T(8,128)S(1)}) custom-call(f32[320,128]{1,0:T(8,128)S(1)} %get-tuple-element.79.cur_ref._.refs_0_.refs_1_, f32[8,128]{1,0:T(8,128)S(1)} %get-tuple-element.67.material_ref.refs_5_, bf16[2,640,384]{2,1,0:T(8,128)(2,1)S(1)} %get-tuple-element.68.own_ref, ...), custom_call_target="tpu_custom_call" | custom-call | tf_op jit(solution)/shard_map/pallas_call | solution.py:594
  13.5 0.5 %collective-permute-done.9.refs_10_ = f32[16,128]{1,0:T(8,128)S(1)} collective-permute-done((f32[16,128]{1,0:T(8,128)S(1)}, f32[16,128]{1,0:T(8,128)S(1)}, u32[]{:S(2)}, u32[]{:S(2)}) %collective-permute-start.9) | collective-permute-done | bytes 8224 | tf_op jit(solution)/shard_map/ppermute | solution.py:617
  14.4 0.8 %shard_map.172 = (f32[320,128]{1,0:T(8,128)S(1)}, f32[24,128]{1,0:T(8,128)S(1)}, f32[24,128]{1,0:T(8,128)S(1)}, f32[16,128]{1,0:T(8,128)S(1)}, f32[64,128]{1,0:T(8,128)S(1)}, /*index=5*/f32[28,128]{1,0:T(8,128)S(1)}) custom-call(f32[320,128]{1,0:T(8,128)S(1)} %get-tuple-element.79.cur_ref._.refs_0_.refs_1_, ...), custom_call_target="tpu_custom_call" | custom-call | tf_op jit(solution)/shard_map/pallas_call | solution.py:594
  15.3 1.7 %collective-permute-start.10 = (f32[64,128]{1,0:T(8,128)S(1)}, f32[64,128]{1,0:T(8,128)S(1)}, u32[]{:S(2)}, u32[]{:S(2)}) collective-permute-start(f32[64,128]{1,0:T(8,128)S(1)} %get-tuple-element.94), channel_id=1, source_target_pairs={{0,1},{1,0},{2,4},{3,5},{4,2},{5,3},{6,8},{7,9},{8,6},{9,7},{10,12... | collective-permute-start | bytes 98312 | tf_op jit(solution)/shard_map/ppermute | solution.py:617
  17.3 0.5 %collective-permute-start.13 = (f32[24,128]{1,0:T(8,128)S(1)}, f32[24,128]{1,0:T(8,128)S(1)}, u32[]{:S(2)}, u32[]{:S(2)}) collective-permute-start(f32[24,128]{1,0:T(8,128)S(1)} %get-tuple-element.97), channel_id=1, source_target_pairs={{0,2},{1,3},{2,0},{3,1},{4,6},{5,7},{6,4},{7,5},{8,10},{9,11},{10,... | collective-permute-start | bytes 36872 | tf_op jit(solution)/shard_map/ppermute | solution.py:617
  17.8 0.5 %shard_map.173 = (f32[320,128]{1,0:T(8,128)S(1)}, f32[160,128]{1,0:T(8,128)S(1)}) custom-call(f32[320,128]{1,0:T(8,128)S(1)} %get-tuple-element.91.cur_ref.refs_0_.refs_1_, f32[8,128]{1,0:T(8,128)S(1)} %get-tuple-element.67.material_ref.refs_5_, bf16[2,640,384]{2,1,0:T(8,128)(2,1)S(1)} %get-tuple-element.68.own_ref, ...), custom_call_target="tpu_custom_call" | custom-call | tf_op jit(solution)/shard_map/pallas_call | solution.py:594
  18.4 0.7 %collective-permute-done.14.refs_10_ = f32[16,128]{1,0:T(8,128)S(1)} collective-permute-done((f32[16,128]{1,0:T(8,128)S(1)}, f32[16,128]{1,0:T(8,128)S(1)}, u32[]{:S(2)}, u32[]{:S(2)}) %collective-permute-start.14) | collective-permute-done | bytes 8224 | tf_op jit(solution)/shard_map/ppermute | solution.py:617
  19.0 1.7 %collective-permute-done.11.refs_7_.refs_8_ = f32[28,128]{1,0:T(8,128)S(1)} collective-permute-done((f32[28,128]{1,0:T(8,128)S(1)}, f32[28,128]{1,0:T(8,128)S(1)}, u32[]{:S(2)}, u32[]{:S(2)}) %collective-permute-start.11) | collective-permute-done | bytes 14368 | tf_op jit(solution)/shard_map/ppermute | solution.py:622
  20.7 0.8 %shard_map.174 = (f32[320,128]{1,0:T(8,128)S(1)}, f32[24,128]{1,0:T(8,128)S(1)}, f32[24,128]{1,0:T(8,128)S(1)}, f32[16,128]{1,0:T(8,128)S(1)}, f32[64,128]{1,0:T(8,128)S(1)}, /*index=5*/f32[28,128]{1,0:T(8,128)S(1)}) custom-call(f32[320,128]{1,0:T(8,128)S(1)} %get-tuple-element.91.cur_ref.refs_0_.refs_1_, ...), custom_call_target="tpu_custom_call" | custom-call | tf_op jit(solution)/shard_map/pallas_call | solution.py:594
  21.9 1.7 %collective-permute-start.16 = (f32[28,128]{1,0:T(8,128)S(1)}, f32[28,128]{1,0:T(8,128)S(1)}, u32[]{:S(2)}, u32[]{:S(2)}) collective-permute-start(f32[28,128]{1,0:T(8,128)S(1)} %get-tuple-element.103.refs_9_.refs_12_), channel_id=1, source_target_pairs={{1,0},{0,1},{3,2},{2,3},{5,4},{4,5},{7,6},{6,7},{9,8},{8,9},{11,10... | collective-permute-start | bytes 43016 | tf_op jit(solution)/shard_map/ppermute | solution.py:622
  24.1 0.5 %shard_map.175 = (f32[320,128]{1,0:T(8,128)S(1)}, f32[160,128]{1,0:T(8,128)S(1)}) custom-call(f32[320,128]{1,0:T(8,128)S(1)} %get-tuple-element.99.cur_ref.refs_0_, f32[8,128]{1,0:T(8,128)S(1)} %get-tuple-element.67.material_ref.refs_5_, bf16[2,640,384]{2,1,0:T(8,128)(2,1)S(1)} %get-tuple-element.68.own_ref, bf16[160,256]{1,0:T(8,128)(2,1)S(1)} %get-tuple-element.69.touch_ref), custom_call_target="tpu_custom_call" | custom-call | tf_op jit(solution)/shard_map/pallas_call | solution.py:594
  25.8 1.7 %collective-permute-start.20 = (f32[2,128]{1,0:T(2,128)S(1)}, f32[2,128]{1,0:T(2,128)S(1)}, u32[]{:S(2)}, u32[]{:S(2)}) collective-permute-start(f32[2,128]{1,0:T(2,128)S(1)} %get-tuple-element.115), channel_id=1, source_target_pairs={{0,1},{1,0},{2,3},{3,2},{4,8},{5,9},{6,10},{7,11},{8,4},{9,5},{10,... | collective-permute-start | bytes 3080 | tf_op jit(solution)/shard_map/ppermute | solution.py:617
  28.3 0.8 %collective-permute-start.23 = (f32[2,128]{1,0:T(2,128)S(1)}, f32[2,128]{1,0:T(2,128)S(1)}, u32[]{:S(2)}, u32[]{:S(2)}) collective-permute-start(f32[2,128]{1,0:T(2,128)S(1)} %get-tuple-element.118), channel_id=1, source_target_pairs={{0,2},{1,3},{2,0},{3,1},{4,6},{5,7},{6,4},{7,5},{8,10},{9,11},{10,... | collective-permute-start | bytes 3080 | tf_op jit(solution)/shard_map/ppermute | solution.py:617
  29.1 1.4 %shard_map.178 = (f32[3,17,4,128]{3,2,1,0:T(4,128)}, f32[3,17,4,128]{3,2,1,0:T(4,128)}) custom-call(f32[320,128]{1,0:T(8,128)S(1)} %get-tuple-element.99.cur_ref.refs_0_, f32[320,128]{1,0:T(8,128)S(1)} %get-tuple-element.91.cur_ref.refs_0_.refs_1_, f32[320,128]{1,0:T(8,128)S(1)} %get-tuple-element.66.refs_2_, f32[320,128]{1,0:T(8,128)S(1)} %get-tuple-element.100.refs_3_, ...), custom_call_target="tpu_custom_call" | custom-call | tf_op jit(solution)/shard_map/pallas_call | solution.py:594
  31.4 0.6 %add_bitcast_fusion = f32[1,2,128]{2,1,0:T(2,128)} fusion(f32[2,128]{1,0:T(2,128)S(1)} %collective-permute-done.23, f32[2,128]{1,0:T(2,128)S(1)} %collective-permute-done.22, f32[2,128]{1,0:T(2,128)S(1)} %collective-permute-done.21, f32[2,128]{1,0:T(2,128)S(1)} %get-tuple-element.111.refs_16_, f32[2,128]{1,0:T(2,128)S(1)} %collective-permute-done.20), kind=kLoop, calls=%fused_computation | loop fusion | flops 1024 | bytes 6144 | tf_op jit(solution)/shard_map/broadcast_in_dim | solution.py:761
  (38 shorter events, 5.6 us)
Async XLA Ops:
  2.7 6.8 %collective-permute-start = (f32[64,128]{1,0:T(8,128)S(1)}, f32[64,128]{1,0:T(8,128)S(1)}, u32[]{:S(2)}, u32[]{:S(2)}) collective-permute-start(f32[64,128]{1,0:T(8,128)S(1)} %get-tuple-element.72), channel_id=1, source_target_pairs={{0,1},{1,0},{2,4},{3,5},{4,2},{5,3},{6,8},{7,9},{8,6},{9,7},{10,12... | collective-permute-start | bytes 98312 | tf_op jit(solution)/shard_map/ppermute | solution.py:617
  5.7 3.8 %collective-permute-start.1 = (f32[40,128]{1,0:T(8,128)S(1)}, f32[40,128]{1,0:T(8,128)S(1)}, u32[]{:S(2)}, u32[]{:S(2)}) collective-permute-start(f32[40,128]{1,0:T(8,128)S(1)} %get-tuple-element.73.refs_12_.refs_13_.refs_3_), channel_id=1, source_target_pairs={{1,0},{0,1},{3,2},{2,3},{5,4},{4,5},{7,6},{6,7},{9,8},{8,9},{11,10... | collective-permute-start | bytes 61448 | tf_op jit(solution)/shard_map/ppermute | solution.py:622
  5.8 2.8 %collective-permute-start.2 = (f32[24,128]{1,0:T(8,128)S(1)}, f32[24,128]{1,0:T(8,128)S(1)}, u32[]{:S(2)}, u32[]{:S(2)}) collective-permute-start(f32[24,128]{1,0:T(8,128)S(1)} %get-tuple-element.74), channel_id=1, source_target_pairs={{0,2},{1,3},{2,0},{3,1},{4,6},{5,7},{6,4},{7,5},{8,10},{9,11},{10,... | collective-permute-start | bytes 36872 | tf_op jit(solution)/shard_map/ppermute | solution.py:617
  7.1 1.6 %collective-permute-start.3 = (f32[24,128]{1,0:T(8,128)S(1)}, f32[24,128]{1,0:T(8,128)S(1)}, u32[]{:S(2)}, u32[]{:S(2)}) collective-permute-start(f32[24,128]{1,0:T(8,128)S(1)} %get-tuple-element.75), channel_id=1, source_target_pairs={{0,2},{1,3},{2,0},{3,1},{4,6},{5,7},{6,4},{7,5},{8,10},{9,11},{10,... | collective-permute-start | bytes 36872 | tf_op jit(solution)/shard_map/ppermute | solution.py:617
  7.1 1.5 %collective-permute-start.4 = (f32[16,128]{1,0:T(8,128)S(1)}, f32[16,128]{1,0:T(8,128)S(1)}, u32[]{:S(2)}, u32[]{:S(2)}) collective-permute-start(f32[16,128]{1,0:T(8,128)S(1)} %get-tuple-element.76), channel_id=1, source_target_pairs={{0,2},{1,3},{2,0},{3,1},{4,6},{5,7},{6,4},{7,5},{8,10},{9,11},{10,... | collective-permute-start | bytes 24584 | tf_op jit(solution)/shard_map/ppermute | solution.py:617
  10.3 4.1 %collective-permute-start.5 = (f32[64,128]{1,0:T(8,128)S(1)}, f32[64,128]{1,0:T(8,128)S(1)}, u32[]{:S(2)}, u32[]{:S(2)}) collective-permute-start(f32[64,128]{1,0:T(8,128)S(1)} %get-tuple-element.82), channel_id=1, source_target_pairs={{0,1},{1,0},{2,4},{3,5},{4,2},{5,3},{6,8},{7,9},{8,6},{9,7},{10,12... | collective-permute-start | bytes 98312 | tf_op jit(solution)/shard_map/ppermute | solution.py:617
  10.7 3.8 %collective-permute-start.6 = (f32[28,128]{1,0:T(8,128)S(1)}, f32[28,128]{1,0:T(8,128)S(1)}, u32[]{:S(2)}, u32[]{:S(2)}) collective-permute-start(f32[28,128]{1,0:T(8,128)S(1)} %get-tuple-element.83.refs_12_.refs_5_), channel_id=1, source_target_pairs={{1,0},{0,1},{3,2},{2,3},{5,4},{4,5},{7,6},{6,7},{9,8},{8,9},{11,10... | collective-permute-start | bytes 43016 | tf_op jit(solution)/shard_map/ppermute | solution.py:622
  12.4 1.7 %collective-permute-start.7 = (f32[24,128]{1,0:T(8,128)S(1)}, f32[24,128]{1,0:T(8,128)S(1)}, u32[]{:S(2)}, u32[]{:S(2)}) collective-permute-start(f32[24,128]{1,0:T(8,128)S(1)} %get-tuple-element.84), channel_id=1, source_target_pairs={{0,2},{1,3},{2,0},{3,1},{4,6},{5,7},{6,4},{7,5},{8,10},{9,11},{10,... | collective-permute-start | bytes 36872 | tf_op jit(solution)/shard_map/ppermute | solution.py:617
  12.4 1.7 %collective-permute-start.8 = (f32[24,128]{1,0:T(8,128)S(1)}, f32[24,128]{1,0:T(8,128)S(1)}, u32[]{:S(2)}, u32[]{:S(2)}) collective-permute-start(f32[24,128]{1,0:T(8,128)S(1)} %get-tuple-element.85), channel_id=1, source_target_pairs={{0,2},{1,3},{2,0},{3,1},{4,6},{5,7},{6,4},{7,5},{8,10},{9,11},{10,... | collective-permute-start | bytes 36872 | tf_op jit(solution)/shard_map/ppermute | solution.py:617
  12.9 1.2 %collective-permute-start.9 = (f32[16,128]{1,0:T(8,128)S(1)}, f32[16,128]{1,0:T(8,128)S(1)}, u32[]{:S(2)}, u32[]{:S(2)}) collective-permute-start(f32[16,128]{1,0:T(8,128)S(1)} %get-tuple-element.86), channel_id=1, source_target_pairs={{0,2},{1,3},{2,0},{3,1},{4,6},{5,7},{6,4},{7,5},{8,10},{9,11},{10,... | collective-permute-start | bytes 24584 | tf_op jit(solution)/shard_map/ppermute | solution.py:617
  15.3 5.4 %collective-permute-start.10 = (f32[64,128]{1,0:T(8,128)S(1)}, f32[64,128]{1,0:T(8,128)S(1)}, u32[]{:S(2)}, u32[]{:S(2)}) collective-permute-start(f32[64,128]{1,0:T(8,128)S(1)} %get-tuple-element.94), channel_id=1, source_target_pairs={{0,1},{1,0},{2,4},{3,5},{4,2},{5,3},{6,8},{7,9},{8,6},{9,7},{10,12... | collective-permute-start | bytes 98312 | tf_op jit(solution)/shard_map/ppermute | solution.py:617
  17.0 3.7 %collective-permute-start.11 = (f32[28,128]{1,0:T(8,128)S(1)}, f32[28,128]{1,0:T(8,128)S(1)}, u32[]{:S(2)}, u32[]{:S(2)}) collective-permute-start(f32[28,128]{1,0:T(8,128)S(1)} %get-tuple-element.95.refs_12_.refs_7_), channel_id=1, source_target_pairs={{1,0},{0,1},{3,2},{2,3},{5,4},{4,5},{7,6},{6,7},{9,8},{8,9},{11,10... | collective-permute-start | bytes 43016 | tf_op jit(solution)/shard_map/ppermute | solution.py:622
  17.3 1.7 %collective-permute-start.12 = (f32[24,128]{1,0:T(8,128)S(1)}, f32[24,128]{1,0:T(8,128)S(1)}, u32[]{:S(2)}, u32[]{:S(2)}) collective-permute-start(f32[24,128]{1,0:T(8,128)S(1)} %get-tuple-element.96), channel_id=1, source_target_pairs={{0,2},{1,3},{2,0},{3,1},{4,6},{5,7},{6,4},{7,5},{8,10},{9,11},{10,... | collective-permute-start | bytes 36872 | tf_op jit(solution)/shard_map/ppermute | solution.py:617
  17.3 1.7 %collective-permute-start.13 = (f32[24,128]{1,0:T(8,128)S(1)}, f32[24,128]{1,0:T(8,128)S(1)}, u32[]{:S(2)}, u32[]{:S(2)}) collective-permute-start(f32[24,128]{1,0:T(8,128)S(1)} %get-tuple-element.97), channel_id=1, source_target_pairs={{0,2},{1,3},{2,0},{3,1},{4,6},{5,7},{6,4},{7,5},{8,10},{9,11},{10,... | collective-permute-start | bytes 36872 | tf_op jit(solution)/shard_map/ppermute | solution.py:617
  17.8 1.2 %collective-permute-start.14 = (f32[16,128]{1,0:T(8,128)S(1)}, f32[16,128]{1,0:T(8,128)S(1)}, u32[]{:S(2)}, u32[]{:S(2)}) collective-permute-start(f32[16,128]{1,0:T(8,128)S(1)} %get-tuple-element.98), channel_id=1, source_target_pairs={{0,2},{1,3},{2,0},{3,1},{4,6},{5,7},{6,4},{7,5},{8,10},{9,11},{10,... | collective-permute-start | bytes 24584 | tf_op jit(solution)/shard_map/ppermute | solution.py:617
  21.5 4.1 %collective-permute-start.15 = (f32[64,128]{1,0:T(8,128)S(1)}, f32[64,128]{1,0:T(8,128)S(1)}, u32[]{:S(2)}, u32[]{:S(2)}) collective-permute-start(f32[64,128]{1,0:T(8,128)S(1)} %get-tuple-element.102), channel_id=1, source_target_pairs={{0,1},{1,0},{2,4},{3,5},{4,2},{5,3},{6,8},{7,9},{8,6},{9,7},{10,12... | collective-permute-start | bytes 98312 | tf_op jit(solution)/shard_map/ppermute | solution.py:617
  21.9 3.7 %collective-permute-start.16 = (f32[28,128]{1,0:T(8,128)S(1)}, f32[28,128]{1,0:T(8,128)S(1)}, u32[]{:S(2)}, u32[]{:S(2)}) collective-permute-start(f32[28,128]{1,0:T(8,128)S(1)} %get-tuple-element.103.refs_9_.refs_12_), channel_id=1, source_target_pairs={{1,0},{0,1},{3,2},{2,3},{5,4},{4,5},{7,6},{6,7},{9,8},{8,9},{11,10... | collective-permute-start | bytes 43016 | tf_op jit(solution)/shard_map/ppermute | solution.py:622
  23.6 1.7 %collective-permute-start.17 = (f32[24,128]{1,0:T(8,128)S(1)}, f32[24,128]{1,0:T(8,128)S(1)}, u32[]{:S(2)}, u32[]{:S(2)}) collective-permute-start(f32[24,128]{1,0:T(8,128)S(1)} %get-tuple-element.104), channel_id=1, source_target_pairs={{0,2},{1,3},{2,0},{3,1},{4,6},{5,7},{6,4},{7,5},{8,10},{9,11},{10,... | collective-permute-start | bytes 36872 | tf_op jit(solution)/shard_map/ppermute | solution.py:617
  23.6 1.7 %collective-permute-start.18 = (f32[24,128]{1,0:T(8,128)S(1)}, f32[24,128]{1,0:T(8,128)S(1)}, u32[]{:S(2)}, u32[]{:S(2)}) collective-permute-start(f32[24,128]{1,0:T(8,128)S(1)} %get-tuple-element.105), channel_id=1, source_target_pairs={{0,2},{1,3},{2,0},{3,1},{4,6},{5,7},{6,4},{7,5},{8,10},{9,11},{10,... | collective-permute-start | bytes 36872 | tf_op jit(solution)/shard_map/ppermute | solution.py:617
  24.1 1.2 %collective-permute-start.19 = (f32[16,128]{1,0:T(8,128)S(1)}, f32[16,128]{1,0:T(8,128)S(1)}, u32[]{:S(2)}, u32[]{:S(2)}) collective-permute-start(f32[16,128]{1,0:T(8,128)S(1)} %get-tuple-element.106), channel_id=1, source_target_pairs={{0,2},{1,3},{2,0},{3,1},{4,6},{5,7},{6,4},{7,5},{8,10},{9,11},{10,... | collective-permute-start | bytes 24584 | tf_op jit(solution)/shard_map/ppermute | solution.py:617
  25.8 4.7 %collective-permute-start.20 = (f32[2,128]{1,0:T(2,128)S(1)}, f32[2,128]{1,0:T(2,128)S(1)}, u32[]{:S(2)}, u32[]{:S(2)}) collective-permute-start(f32[2,128]{1,0:T(2,128)S(1)} %get-tuple-element.115), channel_id=1, source_target_pairs={{0,1},{1,0},{2,3},{3,2},{4,8},{5,9},{6,10},{7,11},{8,4},{9,5},{10,... | collective-permute-start | bytes 3080 | tf_op jit(solution)/shard_map/ppermute | solution.py:617
  27.5 3.6 %collective-permute-start.21 = (f32[2,128]{1,0:T(2,128)S(1)}, f32[2,128]{1,0:T(2,128)S(1)}, u32[]{:S(2)}, u32[]{:S(2)}) collective-permute-start(f32[2,128]{1,0:T(2,128)S(1)} %get-tuple-element.116), channel_id=1, source_target_pairs={{0,1},{1,0},{2,4},{3,5},{4,2},{5,3},{6,8},{7,9},{8,6},{9,7},{10,12... | collective-permute-start | bytes 3080 | tf_op jit(solution)/shard_map/ppermute | solution.py:617
  27.8 3.6 %collective-permute-start.22 = (f32[2,128]{1,0:T(2,128)S(1)}, f32[2,128]{1,0:T(2,128)S(1)}, u32[]{:S(2)}, u32[]{:S(2)}) collective-permute-start(f32[2,128]{1,0:T(2,128)S(1)} %get-tuple-element.117), channel_id=1, source_target_pairs={{0,4},{1,5},{2,6},{3,7},{4,0},{5,1},{6,2},{7,3},{8,12},{9,13},{10,... | collective-permute-start | bytes 3080 | tf_op jit(solution)/shard_map/ppermute | solution.py:617
  28.3 3.1 %collective-permute-start.23 = (f32[2,128]{1,0:T(2,128)S(1)}, f32[2,128]{1,0:T(2,128)S(1)}, u32[]{:S(2)}, u32[]{:S(2)}) collective-permute-start(f32[2,128]{1,0:T(2,128)S(1)} %get-tuple-element.118), channel_id=1, source_target_pairs={{0,2},{1,3},{2,0},{3,1},{4,6},{5,7},{6,4},{7,5},{8,10},{9,11},{10,... | collective-permute-start | bytes 3080 | tf_op jit(solution)/shard_map/ppermute | solution.py:617

commit v13 on v12

--- a/solution.py
+++ b/solution.py
@@ -181,22 +181,35 @@
     return wide[:, :lanes] + (wide[:, lanes:] + dot(table_low, high))
 
 
-def ones_where(rule, shape):
-    row = lax.broadcasted_iota(jnp.int32, shape, 0)
-    column = lax.broadcasted_iota(jnp.int32, shape, 1)
-    return jnp.where(rule(row, column), 1.0, 0.0).astype(jnp.bfloat16)
+def over(value, size):
+    if size & (size - 1) == 0:
+        return lax.shift_right_logical(value, np.int32(size.bit_length() - 1))
+    return lax.div(value, np.int32(size))
+
+
+def within(value, size):
+    return value & (size - 1) if size & (size - 1) == 0 else lax.rem(value, np.int32(size))
+
+
+def ones_where(shape, axis, wanted):
+    line = (shape[0], 1) if axis == 0 else (1, shape[1])
+    target = wanted(lax.broadcasted_iota(jnp.int32, line, axis))
+    number = lax.broadcasted_iota(jnp.int32, shape, 1 - axis)
+    return jnp.where(number == target, 1.0, 0.0).astype(jnp.bfloat16)
 
 
 def gather_table(lanes, z_elems):
-    return ones_where(lambda z, c: z == 4 * (c % z_elems) + c // lanes, (lanes, 5 * lanes))
+    return ones_where(
+        (lanes, 5 * lanes), 1, lambda c: 4 * within(c, z_elems) + over(c, lanes)
+    )
 
 
 def fault_table(lanes, z_elems):
-    return ones_where(lambda z, c: z == 4 * (c % z_elems) + c // z_elems, (lanes, lanes))
+    return ones_where((lanes, lanes), 1, lambda c: 4 * within(c, z_elems) + over(c, z_elems))
 
 
 def fault_table_back(lanes, z_elems):
-    return ones_where(lambda c, z: z == 4 * (c % z_elems) + c // z_elems, (lanes, lanes))
+    return ones_where((lanes, lanes), 0, lambda c: 4 * within(c, z_elems) + over(c, z_elems))
 
 
 def stacked(value):
@@ -223,9 +236,8 @@
     for piece in low:
         result = result + dot(piece, table)
     lanes = result.shape[1] // 5
-    across = lax.broadcasted_iota(jnp.int32, (group, result.shape[1]), 1) % lanes // (
-        lanes // y_elems
-    )
+    across = lax.broadcasted_iota(jnp.int32, (1, result.shape[1]), 1)
+    across = over(within(across, lanes), lanes // y_elems)
     total = result[:group]
     for yel in range(1, y_elems):
         total = jnp.where(across == yel, result[yel * group : (yel + 1) * group], total)
@@ -275,7 +287,7 @@
     first = last = jnp.zeros((8, lanes), jnp.float32)
     for zl in range(4):
         at = zl * BLOCK
-        here = lane // z_elems == zl
+        here = over(lane, z_elems) == zl
         first = jnp.where(here, shifted(plane[at : at + 8], zl * z_elems), first)
         last = jnp.where(here, shifted(plane[at + 8 : at + 16], (zl + 1) * z_elems), last)
     out_ref[pl.ds(x, 3, stride=8), :] = last[:3]
@@ -290,11 +302,11 @@
 def material_rows(lame_ref, shear_ref):
     y_elems, z_elems = lame_ref.shape
     both = jnp.concatenate([lame_ref[...], shear_ref[...]], axis=0)
-    spread = ones_where(lambda k, c: c % z_elems == k, (z_elems, y_elems * z_elems))
+    spread = ones_where((z_elems, y_elems * z_elems), 1, lambda c: within(c, z_elems))
     tiled = exact_dot(both, spread)
     row = lax.broadcasted_iota(jnp.int32, tiled.shape, 0)
     lane = lax.broadcasted_iota(jnp.int32, tiled.shape, 1)
-    kept = jnp.where(row % y_elems == lane // z_elems, tiled, 0.0)
+    kept = jnp.where(within(row, y_elems) == over(lane, z_elems), tiled, 0.0)
     return (
         jnp.sum(kept[:y_elems], axis=0, keepdims=True),
         jnp.sum(kept[y_elems:], axis=0, keepdims=True),
@@ -302,7 +314,7 @@
 
 
 def above_lanes(lanes, z_elems):
-    return lax.broadcasted_iota(jnp.int32, (BLOCK, lanes), 1) % z_elems != 0
+    return within(lax.broadcasted_iota(jnp.int32, (BLOCK, lanes), 1), z_elems) != 0
 
 
 def edge_message(result, lame_row, shear_row, z_elems):
@@ -431,7 +443,7 @@
     left = jnp.where(place == 0, 0.0, jnp.where(even, odd_ref[...], even_in))
     lane_wide = lax.broadcasted_iota(jnp.int32, (BLOCK, lanes), 1)
     below = jnp.where(
-        lane_wide % z_elems != z_elems - 1, pltpu.roll(far[:BLOCK], lanes - 1, 1), 0.0
+        within(lane_wide, z_elems) != z_elems - 1, pltpu.roll(far[:BLOCK], lanes - 1, 1), 0.0
     )
     far = jnp.concatenate([far, below], axis=0)
     lame_row, shear_row = material_ref[0:1], material_ref[1:2]
@@ -440,7 +452,7 @@
     left_shear = left[2 * BLOCK - 1 : 2 * BLOCK]
     from_left = left_lame * touch_ref[:PLANE] + left_shear * touch_ref[PLANE:]
     row, lane = block_iotas(lanes)
-    across = lane // z_elems
+    across = over(lane, z_elems)
     shared = row < 3
     add_first = jnp.logical_and(shared, across > 0)
     take_last = jnp.logical_and(shared, across < y_elems - 1)

time: 32.1 us -> 32.1 us (level)
  no operation moved by 1% of the time
where the time goes in v13:
time: 32.1 us; the launch traced here: 32 us
  starting transfers between devices  15.8 us (49%)
  Pallas kernels  9.15 us (29%)
  waiting for transfers between devices  5.71 us (18%)
  between operations  0.74 us (2%)
  other arithmetic  0.57 us (2%)
    ppermute x20, starting transfers between devices, swapped(): return lax.ppermute(block, ('dom', 'depth'), route)  12 us
    pallas_call x13, Pallas kernels, kernel_call(): pl.pallas_call(functools.partial(body, **static) if static else body, out...  9.15 us
    ppermute x4, starting transfers between devices, from_behind(): lax.ppermute(block, axis, [((i - distance) % size, i) for i in range(size)])  3.79 us
    ppermute x4, waiting for transfers between devices, from_behind(): lax.ppermute(block, axis, [((i - distance) % size, i) for i in range(size)])  3.31 us
    ppermute x20, waiting for transfers between devices, swapped(): return lax.ppermute(block, ('dom', 'depth'), route)  2.4 us
  transfers between devices with their start and end apart: 24, of which 9 were waited for; matrix products, arithmetic and copies ran while one was open for 0% of the time, Pallas kernels for 14%

profile of v13, /device:TPU:0, one launch (start us, length us, event | category | flops | bytes accessed | tf_op | source)
XLA Modules:
  0.0 32.0 jit_solution(7312692356807736166)
XLA Ops:
  0.6 2.0 %shard_map.166 = (f32[320,128]{1,0:T(8,128)S(1)}, f32[24,128]{1,0:T(8,128)S(1)}, f32[24,128]{1,0:T(8,128)S(1)}, f32[16,128]{1,0:T(8,128)S(1)}, f32[64,128]{1,0:T...) custom-call(f32[3,17,4,128]{3,2,1,0:T(4,128)} %bitcast.12, ...), custom_call_target="tpu_custom_call" | custom-call | tf_op jit(solution)/shard_map/pallas_call | solution.py:606
  2.7 3.0 %collective-permute-start = (f32[64,128]{1,0:T(8,128)S(1)}, f32[64,128]{1,0:T(8,128)S(1)}, u32[]{:S(2)}, u32[]{:S(2)}) collective-permute-start(f32[64,128]{1,0:T(8,128)S(1)} %get-tuple-element.72), channel_id=1, source_target_pairs={{0,1},{1,0},{2,4},{3,5},{4,2},{5,3},{6,8},{7,9},{8,6},{9,7},{10,12... | collective-permute-start | bytes 98312 | tf_op jit(solution)/shard_map/ppermute | solution.py:629
  5.8 1.3 %collective-permute-start.2 = (f32[24,128]{1,0:T(8,128)S(1)}, f32[24,128]{1,0:T(8,128)S(1)}, u32[]{:S(2)}, u32[]{:S(2)}) collective-permute-start(f32[24,128]{1,0:T(8,128)S(1)} %get-tuple-element.74), channel_id=1, source_target_pairs={{0,2},{1,3},{2,0},{3,1},{4,6},{5,7},{6,4},{7,5},{8,10},{9,11},{10,... | collective-permute-start | bytes 36872 | tf_op jit(solution)/shard_map/ppermute | solution.py:629
  7.0 0.5 %collective-permute-start.4 = (f32[16,128]{1,0:T(8,128)S(1)}, f32[16,128]{1,0:T(8,128)S(1)}, u32[]{:S(2)}, u32[]{:S(2)}) collective-permute-start(f32[16,128]{1,0:T(8,128)S(1)} %get-tuple-element.76), channel_id=1, source_target_pairs={{0,2},{1,3},{2,0},{3,1},{4,6},{5,7},{6,4},{7,5},{8,10},{9,11},{10,... | collective-permute-start | bytes 24584 | tf_op jit(solution)/shard_map/ppermute | solution.py:629
  7.6 0.5 %shard_map.167 = (f32[320,128]{1,0:T(8,128)S(1)}, f32[320,128]{1,0:T(8,128)S(1)}) custom-call(f32[3,17,4,128]{3,2,1,0:T(4,128)S(1)} %get-tuple-element.62.next_ref, f32[17,4,128]{2,1,0:T(4,128)S(1)} %get-tuple-element.63.density_ref, f32[320,128]{1,0:T(8,128)S(1)} %get-tuple-element.64.mass_ref), custom_call_target="tpu_custom_call" | custom-call | tf_op jit(solution)/shard_map/pallas_call | solution.py:606
  8.1 0.5 %shard_map.168 = (f32[320,128]{1,0:T(8,128)S(1)}, f32[160,128]{1,0:T(8,128)S(1)}) custom-call(f32[320,128]{1,0:T(8,128)S(1)} %get-tuple-element.61.cur_ref.refs_0_.refs_1_, f32[8,128]{1,0:T(8,128)S(1)} %get-tuple-element.67.material_ref.refs_5_, bf16[2,640,384]{2,1,0:T(8,128)(2,1)S(1)} %get-tuple-element.68.own_ref, ...), custom_call_target="tpu_custom_call" | custom-call | tf_op jit(solution)/shard_map/pallas_call | solution.py:606
  8.6 0.8 %collective-permute-done.1.refs_7_.refs_11_.refs_4_ = f32[40,128]{1,0:T(8,128)S(1)} collective-permute-done((f32[40,128]{1,0:T(8,128)S(1)}, f32[40,128]{1,0:T(8,128)S(1)}, u32[]{:S(2)}, u32[]{:S(2)}) %collective-permute-start.1) | collective-permute-done | bytes 20512 | tf_op jit(solution)/shard_map/ppermute | solution.py:634
  9.5 0.8 %shard_map.169 = (f32[320,128]{1,0:T(8,128)S(1)}, f32[24,128]{1,0:T(8,128)S(1)}, f32[24,128]{1,0:T(8,128)S(1)}, f32[16,128]{1,0:T(8,128)S(1)}, f32[64,128]{1,0:T(8,128)S(1)}, /*index=5*/f32[28,128]{1,0:T(8,128)S(1)}) custom-call(f32[320,128]{1,0:T(8,128)S(1)} %get-tuple-element.61.cur_ref.refs_0_.refs_1_, f32[320,128]{1,0:T(8,128)S(1)} %get-tuple-element.65.refs_1_, ...), custom_call_target="tpu_custom_call" | custom-call | tf_op jit(solution)/shard_map/pallas_call | solution.py:606
  10.7 1.7 %collective-permute-start.6 = (f32[28,128]{1,0:T(8,128)S(1)}, f32[28,128]{1,0:T(8,128)S(1)}, u32[]{:S(2)}, u32[]{:S(2)}) collective-permute-start(f32[28,128]{1,0:T(8,128)S(1)} %get-tuple-element.83.refs_12_.refs_5_), channel_id=1, source_target_pairs={{1,0},{0,1},{3,2},{2,3},{5,4},{4,5},{7,6},{6,7},{9,8},{8,9},{11,10... | collective-permute-start | bytes 43016 | tf_op jit(solution)/shard_map/ppermute | solution.py:634
  12.9 0.5 %shard_map.170 = (f32[320,128]{1,0:T(8,128)S(1)}, f32[160,128]{1,0:T(8,128)S(1)}) custom-call(f32[320,128]{1,0:T(8,128)S(1)} %get-tuple-element.79.cur_ref._.refs_0_.refs_1_, f32[8,128]{1,0:T(8,128)S(1)} %get-tuple-element.67.material_ref.refs_5_, bf16[2,640,384]{2,1,0:T(8,128)(2,1)S(1)} %get-tuple-element.68.own_ref, ...), custom_call_target="tpu_custom_call" | custom-call | tf_op jit(solution)/shard_map/pallas_call | solution.py:606
  13.5 0.5 %collective-permute-done.9.refs_10_ = f32[16,128]{1,0:T(8,128)S(1)} collective-permute-done((f32[16,128]{1,0:T(8,128)S(1)}, f32[16,128]{1,0:T(8,128)S(1)}, u32[]{:S(2)}, u32[]{:S(2)}) %collective-permute-start.9) | collective-permute-done | bytes 8224 | tf_op jit(solution)/shard_map/ppermute | solution.py:629
  14.4 0.8 %shard_map.172 = (f32[320,128]{1,0:T(8,128)S(1)}, f32[24,128]{1,0:T(8,128)S(1)}, f32[24,128]{1,0:T(8,128)S(1)}, f32[16,128]{1,0:T(8,128)S(1)}, f32[64,128]{1,0:T(8,128)S(1)}, /*index=5*/f32[28,128]{1,0:T(8,128)S(1)}) custom-call(f32[320,128]{1,0:T(8,128)S(1)} %get-tuple-element.79.cur_ref._.refs_0_.refs_1_, ...), custom_call_target="tpu_custom_call" | custom-call | tf_op jit(solution)/shard_map/pallas_call | solution.py:606
  15.3 1.7 %collective-permute-start.10 = (f32[64,128]{1,0:T(8,128)S(1)}, f32[64,128]{1,0:T(8,128)S(1)}, u32[]{:S(2)}, u32[]{:S(2)}) collective-permute-start(f32[64,128]{1,0:T(8,128)S(1)} %get-tuple-element.94), channel_id=1, source_target_pairs={{0,1},{1,0},{2,4},{3,5},{4,2},{5,3},{6,8},{7,9},{8,6},{9,7},{10,12... | collective-permute-start | bytes 98312 | tf_op jit(solution)/shard_map/ppermute | solution.py:629
  17.3 0.5 %collective-permute-start.13 = (f32[24,128]{1,0:T(8,128)S(1)}, f32[24,128]{1,0:T(8,128)S(1)}, u32[]{:S(2)}, u32[]{:S(2)}) collective-permute-start(f32[24,128]{1,0:T(8,128)S(1)} %get-tuple-element.97), channel_id=1, source_target_pairs={{0,2},{1,3},{2,0},{3,1},{4,6},{5,7},{6,4},{7,5},{8,10},{9,11},{10,... | collective-permute-start | bytes 36872 | tf_op jit(solution)/shard_map/ppermute | solution.py:629
  17.8 0.5 %shard_map.173 = (f32[320,128]{1,0:T(8,128)S(1)}, f32[160,128]{1,0:T(8,128)S(1)}) custom-call(f32[320,128]{1,0:T(8,128)S(1)} %get-tuple-element.91.cur_ref.refs_0_.refs_1_, f32[8,128]{1,0:T(8,128)S(1)} %get-tuple-element.67.material_ref.refs_5_, bf16[2,640,384]{2,1,0:T(8,128)(2,1)S(1)} %get-tuple-element.68.own_ref, ...), custom_call_target="tpu_custom_call" | custom-call | tf_op jit(solution)/shard_map/pallas_call | solution.py:606
  18.4 0.7 %collective-permute-done.14.refs_10_ = f32[16,128]{1,0:T(8,128)S(1)} collective-permute-done((f32[16,128]{1,0:T(8,128)S(1)}, f32[16,128]{1,0:T(8,128)S(1)}, u32[]{:S(2)}, u32[]{:S(2)}) %collective-permute-start.14) | collective-permute-done | bytes 8224 | tf_op jit(solution)/shard_map/ppermute | solution.py:629
  19.0 1.7 %collective-permute-done.11.refs_7_.refs_8_ = f32[28,128]{1,0:T(8,128)S(1)} collective-permute-done((f32[28,128]{1,0:T(8,128)S(1)}, f32[28,128]{1,0:T(8,128)S(1)}, u32[]{:S(2)}, u32[]{:S(2)}) %collective-permute-start.11) | collective-permute-done | bytes 14368 | tf_op jit(solution)/shard_map/ppermute | solution.py:634
  20.7 0.8 %shard_map.174 = (f32[320,128]{1,0:T(8,128)S(1)}, f32[24,128]{1,0:T(8,128)S(1)}, f32[24,128]{1,0:T(8,128)S(1)}, f32[16,128]{1,0:T(8,128)S(1)}, f32[64,128]{1,0:T(8,128)S(1)}, /*index=5*/f32[28,128]{1,0:T(8,128)S(1)}) custom-call(f32[320,128]{1,0:T(8,128)S(1)} %get-tuple-element.91.cur_ref.refs_0_.refs_1_, ...), custom_call_target="tpu_custom_call" | custom-call | tf_op jit(solution)/shard_map/pallas_call | solution.py:606
  21.9 1.7 %collective-permute-start.16 = (f32[28,128]{1,0:T(8,128)S(1)}, f32[28,128]{1,0:T(8,128)S(1)}, u32[]{:S(2)}, u32[]{:S(2)}) collective-permute-start(f32[28,128]{1,0:T(8,128)S(1)} %get-tuple-element.103.refs_9_.refs_12_), channel_id=1, source_target_pairs={{1,0},{0,1},{3,2},{2,3},{5,4},{4,5},{7,6},{6,7},{9,8},{8,9},{11,10... | collective-permute-start | bytes 43016 | tf_op jit(solution)/shard_map/ppermute | solution.py:634
  24.1 0.5 %shard_map.175 = (f32[320,128]{1,0:T(8,128)S(1)}, f32[160,128]{1,0:T(8,128)S(1)}) custom-call(f32[320,128]{1,0:T(8,128)S(1)} %get-tuple-element.99.cur_ref.refs_0_, f32[8,128]{1,0:T(8,128)S(1)} %get-tuple-element.67.material_ref.refs_5_, bf16[2,640,384]{2,1,0:T(8,128)(2,1)S(1)} %get-tuple-element.68.own_ref, bf16[160,256]{1,0:T(8,128)(2,1)S(1)} %get-tuple-element.69.touch_ref), custom_call_target="tpu_custom_call" | custom-call | tf_op jit(solution)/shard_map/pallas_call | solution.py:606
  25.8 1.7 %collective-permute-start.20 = (f32[2,128]{1,0:T(2,128)S(1)}, f32[2,128]{1,0:T(2,128)S(1)}, u32[]{:S(2)}, u32[]{:S(2)}) collective-permute-start(f32[2,128]{1,0:T(2,128)S(1)} %get-tuple-element.115), channel_id=1, source_target_pairs={{0,1},{1,0},{2,3},{3,2},{4,8},{5,9},{6,10},{7,11},{8,4},{9,5},{10,... | collective-permute-start | bytes 3080 | tf_op jit(solution)/shard_map/ppermute | solution.py:629
  28.3 0.8 %collective-permute-start.23 = (f32[2,128]{1,0:T(2,128)S(1)}, f32[2,128]{1,0:T(2,128)S(1)}, u32[]{:S(2)}, u32[]{:S(2)}) collective-permute-start(f32[2,128]{1,0:T(2,128)S(1)} %get-tuple-element.118), channel_id=1, source_target_pairs={{0,2},{1,3},{2,0},{3,1},{4,6},{5,7},{6,4},{7,5},{8,10},{9,11},{10,... | collective-permute-start | bytes 3080 | tf_op jit(solution)/shard_map/ppermute | solution.py:629
  29.1 1.4 %shard_map.178 = (f32[3,17,4,128]{3,2,1,0:T(4,128)}, f32[3,17,4,128]{3,2,1,0:T(4,128)}) custom-call(f32[320,128]{1,0:T(8,128)S(1)} %get-tuple-element.99.cur_ref.refs_0_, f32[320,128]{1,0:T(8,128)S(1)} %get-tuple-element.91.cur_ref.refs_0_.refs_1_, f32[320,128]{1,0:T(8,128)S(1)} %get-tuple-element.66.refs_2_, f32[320,128]{1,0:T(8,128)S(1)} %get-tuple-element.100.refs_3_, ...), custom_call_target="tpu_custom_call" | custom-call | tf_op jit(solution)/shard_map/pallas_call | solution.py:606
  31.4 0.6 %add_bitcast_fusion = f32[1,2,128]{2,1,0:T(2,128)} fusion(f32[2,128]{1,0:T(2,128)S(1)} %collective-permute-done.23, f32[2,128]{1,0:T(2,128)S(1)} %collective-permute-done.22, f32[2,128]{1,0:T(2,128)S(1)} %collective-permute-done.21, f32[2,128]{1,0:T(2,128)S(1)} %get-tuple-element.111.refs_16_, f32[2,128]{1,0:T(2,128)S(1)} %collective-permute-done.20), kind=kLoop, calls=%fused_computation | loop fusion | flops 1024 | bytes 6144 | tf_op jit(solution)/shard_map/broadcast_in_dim | solution.py:773
  (38 shorter events, 5.6 us)
Async XLA Ops:
  2.7 6.8 %collective-permute-start = (f32[64,128]{1,0:T(8,128)S(1)}, f32[64,128]{1,0:T(8,128)S(1)}, u32[]{:S(2)}, u32[]{:S(2)}) collective-permute-start(f32[64,128]{1,0:T(8,128)S(1)} %get-tuple-element.72), channel_id=1, source_target_pairs={{0,1},{1,0},{2,4},{3,5},{4,2},{5,3},{6,8},{7,9},{8,6},{9,7},{10,12... | collective-permute-start | bytes 98312 | tf_op jit(solution)/shard_map/ppermute | solution.py:629
  5.7 3.8 %collective-permute-start.1 = (f32[40,128]{1,0:T(8,128)S(1)}, f32[40,128]{1,0:T(8,128)S(1)}, u32[]{:S(2)}, u32[]{:S(2)}) collective-permute-start(f32[40,128]{1,0:T(8,128)S(1)} %get-tuple-element.73.refs_12_.refs_13_.refs_3_), channel_id=1, source_target_pairs={{1,0},{0,1},{3,2},{2,3},{5,4},{4,5},{7,6},{6,7},{9,8},{8,9},{11,10... | collective-permute-start | bytes 61448 | tf_op jit(solution)/shard_map/ppermute | solution.py:634
  5.8 2.8 %collective-permute-start.2 = (f32[24,128]{1,0:T(8,128)S(1)}, f32[24,128]{1,0:T(8,128)S(1)}, u32[]{:S(2)}, u32[]{:S(2)}) collective-permute-start(f32[24,128]{1,0:T(8,128)S(1)} %get-tuple-element.74), channel_id=1, source_target_pairs={{0,2},{1,3},{2,0},{3,1},{4,6},{5,7},{6,4},{7,5},{8,10},{9,11},{10,... | collective-permute-start | bytes 36872 | tf_op jit(solution)/shard_map/ppermute | solution.py:629
  7.0 1.6 %collective-permute-start.3 = (f32[24,128]{1,0:T(8,128)S(1)}, f32[24,128]{1,0:T(8,128)S(1)}, u32[]{:S(2)}, u32[]{:S(2)}) collective-permute-start(f32[24,128]{1,0:T(8,128)S(1)} %get-tuple-element.75), channel_id=1, source_target_pairs={{0,2},{1,3},{2,0},{3,1},{4,6},{5,7},{6,4},{7,5},{8,10},{9,11},{10,... | collective-permute-start | bytes 36872 | tf_op jit(solution)/shard_map/ppermute | solution.py:629
  7.0 1.5 %collective-permute-start.4 = (f32[16,128]{1,0:T(8,128)S(1)}, f32[16,128]{1,0:T(8,128)S(1)}, u32[]{:S(2)}, u32[]{:S(2)}) collective-permute-start(f32[16,128]{1,0:T(8,128)S(1)} %get-tuple-element.76), channel_id=1, source_target_pairs={{0,2},{1,3},{2,0},{3,1},{4,6},{5,7},{6,4},{7,5},{8,10},{9,11},{10,... | collective-permute-start | bytes 24584 | tf_op jit(solution)/shard_map/ppermute | solution.py:629
  10.3 4.1 %collective-permute-start.5 = (f32[64,128]{1,0:T(8,128)S(1)}, f32[64,128]{1,0:T(8,128)S(1)}, u32[]{:S(2)}, u32[]{:S(2)}) collective-permute-start(f32[64,128]{1,0:T(8,128)S(1)} %get-tuple-element.82), channel_id=1, source_target_pairs={{0,1},{1,0},{2,4},{3,5},{4,2},{5,3},{6,8},{7,9},{8,6},{9,7},{10,12... | collective-permute-start | bytes 98312 | tf_op jit(solution)/shard_map/ppermute | solution.py:629
  10.7 3.8 %collective-permute-start.6 = (f32[28,128]{1,0:T(8,128)S(1)}, f32[28,128]{1,0:T(8,128)S(1)}, u32[]{:S(2)}, u32[]{:S(2)}) collective-permute-start(f32[28,128]{1,0:T(8,128)S(1)} %get-tuple-element.83.refs_12_.refs_5_), channel_id=1, source_target_pairs={{1,0},{0,1},{3,2},{2,3},{5,4},{4,5},{7,6},{6,7},{9,8},{8,9},{11,10... | collective-permute-start | bytes 43016 | tf_op jit(solution)/shard_map/ppermute | solution.py:634
  12.4 1.7 %collective-permute-start.7 = (f32[24,128]{1,0:T(8,128)S(1)}, f32[24,128]{1,0:T(8,128)S(1)}, u32[]{:S(2)}, u32[]{:S(2)}) collective-permute-start(f32[24,128]{1,0:T(8,128)S(1)} %get-tuple-element.84), channel_id=1, source_target_pairs={{0,2},{1,3},{2,0},{3,1},{4,6},{5,7},{6,4},{7,5},{8,10},{9,11},{10,... | collective-permute-start | bytes 36872 | tf_op jit(solution)/shard_map/ppermute | solution.py:629
  12.4 1.7 %collective-permute-start.8 = (f32[24,128]{1,0:T(8,128)S(1)}, f32[24,128]{1,0:T(8,128)S(1)}, u32[]{:S(2)}, u32[]{:S(2)}) collective-permute-start(f32[24,128]{1,0:T(8,128)S(1)} %get-tuple-element.85), channel_id=1, source_target_pairs={{0,2},{1,3},{2,0},{3,1},{4,6},{5,7},{6,4},{7,5},{8,10},{9,11},{10,... | collective-permute-start | bytes 36872 | tf_op jit(solution)/shard_map/ppermute | solution.py:629
  12.9 1.2 %collective-permute-start.9 = (f32[16,128]{1,0:T(8,128)S(1)}, f32[16,128]{1,0:T(8,128)S(1)}, u32[]{:S(2)}, u32[]{:S(2)}) collective-permute-start(f32[16,128]{1,0:T(8,128)S(1)} %get-tuple-element.86), channel_id=1, source_target_pairs={{0,2},{1,3},{2,0},{3,1},{4,6},{5,7},{6,4},{7,5},{8,10},{9,11},{10,... | collective-permute-start | bytes 24584 | tf_op jit(solution)/shard_map/ppermute | solution.py:629
  15.3 5.4 %collective-permute-start.10 = (f32[64,128]{1,0:T(8,128)S(1)}, f32[64,128]{1,0:T(8,128)S(1)}, u32[]{:S(2)}, u32[]{:S(2)}) collective-permute-start(f32[64,128]{1,0:T(8,128)S(1)} %get-tuple-element.94), channel_id=1, source_target_pairs={{0,1},{1,0},{2,4},{3,5},{4,2},{5,3},{6,8},{7,9},{8,6},{9,7},{10,12... | collective-permute-start | bytes 98312 | tf_op jit(solution)/shard_map/ppermute | solution.py:629
  17.0 3.7 %collective-permute-start.11 = (f32[28,128]{1,0:T(8,128)S(1)}, f32[28,128]{1,0:T(8,128)S(1)}, u32[]{:S(2)}, u32[]{:S(2)}) collective-permute-start(f32[28,128]{1,0:T(8,128)S(1)} %get-tuple-element.95.refs_12_.refs_7_), channel_id=1, source_target_pairs={{1,0},{0,1},{3,2},{2,3},{5,4},{4,5},{7,6},{6,7},{9,8},{8,9},{11,10... | collective-permute-start | bytes 43016 | tf_op jit(solution)/shard_map/ppermute | solution.py:634
  17.3 1.7 %collective-permute-start.12 = (f32[24,128]{1,0:T(8,128)S(1)}, f32[24,128]{1,0:T(8,128)S(1)}, u32[]{:S(2)}, u32[]{:S(2)}) collective-permute-start(f32[24,128]{1,0:T(8,128)S(1)} %get-tuple-element.96), channel_id=1, source_target_pairs={{0,2},{1,3},{2,0},{3,1},{4,6},{5,7},{6,4},{7,5},{8,10},{9,11},{10,... | collective-permute-start | bytes 36872 | tf_op jit(solution)/shard_map/ppermute | solution.py:629
  17.3 1.7 %collective-permute-start.13 = (f32[24,128]{1,0:T(8,128)S(1)}, f32[24,128]{1,0:T(8,128)S(1)}, u32[]{:S(2)}, u32[]{:S(2)}) collective-permute-start(f32[24,128]{1,0:T(8,128)S(1)} %get-tuple-element.97), channel_id=1, source_target_pairs={{0,2},{1,3},{2,0},{3,1},{4,6},{5,7},{6,4},{7,5},{8,10},{9,11},{10,... | collective-permute-start | bytes 36872 | tf_op jit(solution)/shard_map/ppermute | solution.py:629
  17.8 1.2 %collective-permute-start.14 = (f32[16,128]{1,0:T(8,128)S(1)}, f32[16,128]{1,0:T(8,128)S(1)}, u32[]{:S(2)}, u32[]{:S(2)}) collective-permute-start(f32[16,128]{1,0:T(8,128)S(1)} %get-tuple-element.98), channel_id=1, source_target_pairs={{0,2},{1,3},{2,0},{3,1},{4,6},{5,7},{6,4},{7,5},{8,10},{9,11},{10,... | collective-permute-start | bytes 24584 | tf_op jit(solution)/shard_map/ppermute | solution.py:629
  21.5 4.1 %collective-permute-start.15 = (f32[64,128]{1,0:T(8,128)S(1)}, f32[64,128]{1,0:T(8,128)S(1)}, u32[]{:S(2)}, u32[]{:S(2)}) collective-permute-start(f32[64,128]{1,0:T(8,128)S(1)} %get-tuple-element.102), channel_id=1, source_target_pairs={{0,1},{1,0},{2,4},{3,5},{4,2},{5,3},{6,8},{7,9},{8,6},{9,7},{10,12... | collective-permute-start | bytes 98312 | tf_op jit(solution)/shard_map/ppermute | solution.py:629
  21.9 3.7 %collective-permute-start.16 = (f32[28,128]{1,0:T(8,128)S(1)}, f32[28,128]{1,0:T(8,128)S(1)}, u32[]{:S(2)}, u32[]{:S(2)}) collective-permute-start(f32[28,128]{1,0:T(8,128)S(1)} %get-tuple-element.103.refs_9_.refs_12_), channel_id=1, source_target_pairs={{1,0},{0,1},{3,2},{2,3},{5,4},{4,5},{7,6},{6,7},{9,8},{8,9},{11,10... | collective-permute-start | bytes 43016 | tf_op jit(solution)/shard_map/ppermute | solution.py:634
  23.6 1.7 %collective-permute-start.17 = (f32[24,128]{1,0:T(8,128)S(1)}, f32[24,128]{1,0:T(8,128)S(1)}, u32[]{:S(2)}, u32[]{:S(2)}) collective-permute-start(f32[24,128]{1,0:T(8,128)S(1)} %get-tuple-element.104), channel_id=1, source_target_pairs={{0,2},{1,3},{2,0},{3,1},{4,6},{5,7},{6,4},{7,5},{8,10},{9,11},{10,... | collective-permute-start | bytes 36872 | tf_op jit(solution)/shard_map/ppermute | solution.py:629
  23.6 1.7 %collective-permute-start.18 = (f32[24,128]{1,0:T(8,128)S(1)}, f32[24,128]{1,0:T(8,128)S(1)}, u32[]{:S(2)}, u32[]{:S(2)}) collective-permute-start(f32[24,128]{1,0:T(8,128)S(1)} %get-tuple-element.105), channel_id=1, source_target_pairs={{0,2},{1,3},{2,0},{3,1},{4,6},{5,7},{6,4},{7,5},{8,10},{9,11},{10,... | collective-permute-start | bytes 36872 | tf_op jit(solution)/shard_map/ppermute | solution.py:629
  24.1 1.2 %collective-permute-start.19 = (f32[16,128]{1,0:T(8,128)S(1)}, f32[16,128]{1,0:T(8,128)S(1)}, u32[]{:S(2)}, u32[]{:S(2)}) collective-permute-start(f32[16,128]{1,0:T(8,128)S(1)} %get-tuple-element.106), channel_id=1, source_target_pairs={{0,2},{1,3},{2,0},{3,1},{4,6},{5,7},{6,4},{7,5},{8,10},{9,11},{10,... | collective-permute-start | bytes 24584 | tf_op jit(solution)/shard_map/ppermute | solution.py:629
  25.8 4.7 %collective-permute-start.20 = (f32[2,128]{1,0:T(2,128)S(1)}, f32[2,128]{1,0:T(2,128)S(1)}, u32[]{:S(2)}, u32[]{:S(2)}) collective-permute-start(f32[2,128]{1,0:T(2,128)S(1)} %get-tuple-element.115), channel_id=1, source_target_pairs={{0,1},{1,0},{2,3},{3,2},{4,8},{5,9},{6,10},{7,11},{8,4},{9,5},{10,... | collective-permute-start | bytes 3080 | tf_op jit(solution)/shard_map/ppermute | solution.py:629
  27.5 3.6 %collective-permute-start.21 = (f32[2,128]{1,0:T(2,128)S(1)}, f32[2,128]{1,0:T(2,128)S(1)}, u32[]{:S(2)}, u32[]{:S(2)}) collective-permute-start(f32[2,128]{1,0:T(2,128)S(1)} %get-tuple-element.116), channel_id=1, source_target_pairs={{0,1},{1,0},{2,4},{3,5},{4,2},{5,3},{6,8},{7,9},{8,6},{9,7},{10,12... | collective-permute-start | bytes 3080 | tf_op jit(solution)/shard_map/ppermute | solution.py:629
  27.8 3.6 %collective-permute-start.22 = (f32[2,128]{1,0:T(2,128)S(1)}, f32[2,128]{1,0:T(2,128)S(1)}, u32[]{:S(2)}, u32[]{:S(2)}) collective-permute-start(f32[2,128]{1,0:T(2,128)S(1)} %get-tuple-element.117), channel_id=1, source_target_pairs={{0,4},{1,5},{2,6},{3,7},{4,0},{5,1},{6,2},{7,3},{8,12},{9,13},{10,... | collective-permute-start | bytes 3080 | tf_op jit(solution)/shard_map/ppermute | solution.py:629
  28.3 3.1 %collective-permute-start.23 = (f32[2,128]{1,0:T(2,128)S(1)}, f32[2,128]{1,0:T(2,128)S(1)}, u32[]{:S(2)}, u32[]{:S(2)}) collective-permute-start(f32[2,128]{1,0:T(2,128)S(1)} %get-tuple-element.118), channel_id=1, source_target_pairs={{0,2},{1,3},{2,0},{3,1},{4,6},{5,7},{6,4},{7,5},{8,10},{9,11},{10,... | collective-permute-start | bytes 3080 | tf_op jit(solution)/shard_map/ppermute | solution.py:629

commit v14 on v13

--- a/solution.py
+++ b/solution.py
@@ -16,13 +16,14 @@
 LATER = 11
 FAULT = 24
 SENT_FAULT = 28
-PARTS = (24, 24, 16)
+SENT = 56
+PARTS = (24, 16, 16)
 
 time_step = 0.01
 lock_stiffness = 0.5
 
 BLOCK = 16
-ROWS = ((0, 1, 2), (3, 4, 5), (11, 12, 13), (6, 7, 14), (8, 9, 10))
+ROWS = ((4, 5, 6), (0, 1, 2), (8, 9, 10), (3, 7, 11), (12, 13, 14))
 PLANE = 5 * BLOCK
 
 
@@ -290,8 +291,17 @@
         here = over(lane, z_elems) == zl
         first = jnp.where(here, shifted(plane[at : at + 8], zl * z_elems), first)
         last = jnp.where(here, shifted(plane[at + 8 : at + 16], (zl + 1) * z_elems), last)
-    out_ref[pl.ds(x, 3, stride=8), :] = last[:3]
-    out_ref[pl.ds(4 + x, 3, stride=8), :] = first[:3]
+    out_ref[pl.ds(x, 3, stride=8), :] = last[4:7]
+    out_ref[pl.ds(4 + x, 3, stride=8), :] = first[4:7]
+    return last
+
+
+def sent_plane(plane, last):
+    return packed(
+        [plane[i * BLOCK : i * BLOCK + 8] for i in range(4)],
+        [plane[i * BLOCK + 8 : (i + 1) * BLOCK] for i in range(4)],
+        last,
+    )
 
 
 def select_messages(parity, left, right):
@@ -317,16 +327,77 @@
     return within(lax.broadcasted_iota(jnp.int32, (BLOCK, lanes), 1), z_elems) != 0
 
 
+def shared_rows(row):
+    return jnp.logical_and(row >= 4, row < 7)
+
+
+def packed(lows, highs, last):
+    row, _ = block_iotas(last.shape[1])
+    pairs = [
+        jnp.where(row < 4, highs[i], pltpu.roll(highs[i + 1], 4, 0)) for i in (0, 2)
+    ]
+    return jnp.concatenate(list(lows) + pairs + [last], axis=0)
+
+
+def unpacked(sent):
+    parts = [sent[i : i + 8] for i in range(0, SENT, 8)]
+    highs = [parts[4], pltpu.roll(parts[4], 4, 0), parts[5], pltpu.roll(parts[5], 4, 0)]
+    return parts[:4], highs, parts[6]
+
+
+def far_plane(sent, z_elems):
+    lanes = sent.shape[1]
+    lows, highs, last = unpacked(sent)
+    row, lane = block_iotas(lanes)
+    inner = lane < lanes - z_elems
+    below = within(lane, z_elems) != z_elems - 1
+    rows = []
+    for zl in range(4):
+        node = jnp.where(
+            inner, shifted(lows[zl], -z_elems), shifted(last, -(zl + 1) * z_elems)
+        )
+        rows += [lows[zl], jnp.where(row < 4, highs[zl], node)]
+    node = jnp.where(inner, shifted(lows[0], -z_elems - 1), shifted(last, -z_elems - 1))
+    rows.append(jnp.where(below, shifted(lows[0], -1), 0.0))
+    rows.append(jnp.where(below, jnp.where(row < 4, shifted(highs[0], -1), node), 0.0))
+    return jnp.concatenate(rows, axis=0)
+
+
+def left_blocks(sent, z_elems):
+    lanes = sent.shape[1]
+    lows, highs, last = unpacked(sent)
+    row, lane = block_iotas(lanes)
+    outer = jnp.logical_and(lane >= lanes - z_elems, shared_rows(row))
+    blocks = []
+    for zl in range(4):
+        node = jnp.where(outer, shifted(last, -(zl + 1) * z_elems), 0.0)
+        blocks.append(jnp.concatenate([lows[zl], jnp.where(row < 4, highs[zl], node)], axis=0))
+    return blocks, last[0:1], last[1:2]
+
+
 def edge_message(result, lame_row, shear_row, z_elems):
     lanes = result.shape[1]
     force = lame_row * result[:PLANE] + shear_row * result[PLANE:]
-    top = force[:BLOCK] + jnp.where(
-        above_lanes(lanes, z_elems), pltpu.roll(force[4 * BLOCK :], 1, 1), 0.0
-    )
-    row = lax.broadcasted_iota(jnp.int32, top.shape, 0)
-    top = jnp.where(row == BLOCK - 1, lame_row, top)
-    second = jnp.where(row == BLOCK - 1, shear_row, force[BLOCK : 2 * BLOCK])
-    return jnp.concatenate([top, second, force[2 * BLOCK : 4 * BLOCK]], axis=0)
+    lows = [force[i * BLOCK : i * BLOCK + 8] for i in range(5)]
+    highs = [force[i * BLOCK + 8 : (i + 1) * BLOCK] for i in range(5)]
+    row, lane = block_iotas(lanes)
+    take = jnp.logical_and(shared_rows(row), over(lane, z_elems) > 0)
+    above = within(lane, z_elems) != 0
+    corner = jnp.where(above, shifted(highs[4], z_elems + 1), 0.0)
+    ends = [shifted(highs[zl], (zl + 1) * z_elems) for zl in range(4)]
+    ends[0] = ends[0] + corner
+    new_lows = [lows[zl] + jnp.where(take, shifted(highs[zl], z_elems), 0.0) for zl in range(4)]
+    new_lows[0] = (
+        new_lows[0]
+        + jnp.where(above, shifted(lows[4], 1), 0.0)
+        + jnp.where(take, corner, 0.0)
+    )
+    highs[0] = highs[0] + jnp.where(above, shifted(highs[4], 1), 0.0)
+    last = ends[3]
+    for zl in range(3):
+        last = jnp.where(over(lane, z_elems) == zl, ends[zl], last)
+    last = jnp.where(row == 0, lame_row, jnp.where(row == 1, shear_row, last))
+    return packed(new_lows, highs, last)
 
 
 def own_force(own_ref, cur, lame_row, shear_row):
@@ -388,7 +459,8 @@
     planes = [cur[x * PLANE : (x + 1) * PLANE] for x in range(4)]
     edge = dot(edge_ref[...], jnp.concatenate([stacked(p) for p in planes], axis=0))
     right = edge_message(edge, lame_row, shear_row, z_elems)
-    message, odd_ref[...] = select_messages(parity, cur[: 4 * BLOCK], right)
+    lasts = [store_fault(fault_out_ref, x, planes[x], z_elems) for x in range(4)]
+    message, odd_ref[...] = select_messages(parity, sent_plane(planes[0], lasts[0]), right)
     for even_ref, at in zip(even_refs, (0, PARTS[0], PARTS[0] + PARTS[1])):
         even_ref[...] = message[at : at + even_ref.shape[0]]
     weak = weak_ref[...]
@@ -398,8 +470,6 @@
         tangent.append(
             jnp.where(flag == 0, lock_stiffness, jnp.where(flag == 1, -weak, 0.0))
         )
-    for x in range(4):
-        store_fault(fault_out_ref, x, planes[x], z_elems)
     fault_out_ref[FAULT:] = exact_dot(jnp.concatenate(tangent, axis=0), fault)
     for copy in copies[6:]:
         copy.wait()
@@ -441,26 +511,21 @@
     even = place % 2 == 0
     far = jnp.where(place == last_place, 0.0, jnp.where(even, even_in, odd_ref[...]))
     left = jnp.where(place == 0, 0.0, jnp.where(even, odd_ref[...], even_in))
-    lane_wide = lax.broadcasted_iota(jnp.int32, (BLOCK, lanes), 1)
-    below = jnp.where(
-        within(lane_wide, z_elems) != z_elems - 1, pltpu.roll(far[:BLOCK], lanes - 1, 1), 0.0
-    )
-    far = jnp.concatenate([far, below], axis=0)
+    far = far_plane(far, z_elems)
+    left, left_lame, left_shear = left_blocks(left, z_elems)
     lame_row, shear_row = material_ref[0:1], material_ref[1:2]
     far = jnp.concatenate([stacked(lame_row * far), stacked(shear_row * far)], axis=0)
-    left_lame = left[BLOCK - 1 : BLOCK]
-    left_shear = left[2 * BLOCK - 1 : 2 * BLOCK]
     from_left = left_lame * touch_ref[:PLANE] + left_shear * touch_ref[PLANE:]
     row, lane = block_iotas(lanes)
     across = over(lane, z_elems)
-    shared = row < 3
+    shared = shared_rows(row)
     add_first = jnp.logical_and(shared, across > 0)
     take_last = jnp.logical_and(shared, across < y_elems - 1)
     pull_first = jnp.logical_and(shared, across == 0)
     pull_last = jnp.logical_and(shared, across == y_elems - 1)
     above = above_lanes(lanes, z_elems)
     middle = lax.broadcasted_iota(jnp.int32, (3, lanes), 0) == 1
-    gap = jnp.zeros((5, lanes), jnp.float32)
+    gap = jnp.zeros((4, lanes), jnp.float32)
     if not last:
         fault_out[FAULT:] = jnp.zeros_like(fault_out[FAULT:])
     planes = []
@@ -470,7 +535,7 @@
         blocks = [force[zl * BLOCK : (zl + 1) * BLOCK] for zl in range(5)]
         if x == 0:
             blocks = [b + from_left[i * BLOCK : (i + 1) * BLOCK] for i, b in enumerate(blocks)]
-            blocks[:4] = [b + left[i * BLOCK : (i + 1) * BLOCK] for i, b in enumerate(blocks[:4])]
+            blocks[:4] = [b + left[i] for i, b in enumerate(blocks[:4])]
         blocks[0], blocks[4] = (
             blocks[0] + jnp.where(above, pltpu.roll(blocks[4], 1, 1), 0.0),
             blocks[4] + pltpu.roll(blocks[0], lanes - 1, 1),
@@ -480,10 +545,10 @@
         below_stiff = jnp.where(middle, lock_stiffness, first_up_ref[k])
         own_stiff = jnp.where(middle, lock_stiffness, first_own_ref[k])
         pulled = jnp.concatenate(
-            [below_stiff * (up_ref[lasts, :] - own_ref[firsts, :]), gap], axis=0
+            [gap, below_stiff * (up_ref[lasts, :] - own_ref[firsts, :]), gap[:1]], axis=0
         )
         pulled_last = jnp.concatenate(
-            [own_stiff * (down_ref[firsts, :] - own_ref[lasts, :]), gap], axis=0
+            [gap, own_stiff * (down_ref[firsts, :] - own_ref[lasts, :]), gap[:1]], axis=0
         )
         for zl in range(5):
             low, high = blocks[zl][:8], blocks[zl][8:]
@@ -506,10 +571,10 @@
             planes.append(plane)
         else:
             new_ref[rows] = plane
-            store_fault(fault_out, x, plane, z_elems)
+            end = store_fault(fault_out, x, plane, z_elems)
             planes.append(stacked(plane))
             if x == 0:
-                first = plane[: 4 * BLOCK]
+                first = sent_plane(plane, end)
     if last:
 
         def send(c):
@@ -659,7 +724,7 @@
     flags = branch_flags[:, 0]
     native = pltpu.VMEM((y_elems, 4 * BLOCK, lanes), jnp.float32)
     field = (4 * PLANE, lanes)
-    plane = (4 * BLOCK, lanes)
+    plane = (SENT, lanes)
     parts = [(rows, lanes) for rows in PARTS]
 
     def exchange(even, odd, fault_rows):

time: 32.1 us -> 32.3 us (level)
  transfers between devices with their start and end apart: 24 -> 24, of which waited for: 9 -> 11; matrix products, arithmetic and copies ran while one was open for 0% -> 0% of each run, Pallas kernels for 14% -> 14%
where the time goes in v14:
time: 32.3 us; the launch traced here: 32.2 us
  starting transfers between devices  16 us (50%)
  Pallas kernels  9.24 us (29%)
  waiting for transfers between devices  5.59 us (17%)
  between operations  0.77 us (2%)
  other arithmetic  0.57 us (2%)
    ppermute x20, starting transfers between devices, swapped(): return lax.ppermute(block, ('dom', 'depth'), route)  12.2 us
    pallas_call x13, Pallas kernels, kernel_call(): pl.pallas_call(functools.partial(body, **static) if static else body, out...  9.24 us
    ppermute x4, starting transfers between devices, from_behind(): lax.ppermute(block, axis, [((i - distance) % size, i) for i in range(size)])  3.82 us
    ppermute x4, waiting for transfers between devices, from_behind(): lax.ppermute(block, axis, [((i - distance) % size, i) for i in range(size)])  3.28 us
    ppermute x20, waiting for transfers between devices, swapped(): return lax.ppermute(block, ('dom', 'depth'), route)  2.31 us
  transfers between devices with their start and end apart: 24, of which 11 were waited for; matrix products, arithmetic and copies ran while one was open for 0% of the time, Pallas kernels for 14%

profile of v14, /device:TPU:0, one launch (start us, length us, event | category | flops | bytes accessed | tf_op | source)
XLA Modules:
  0.0 32.2 jit_solution(1688631292267955679)
XLA Ops:
  0.6 2.0 %shard_map.166 = (f32[320,128]{1,0:T(8,128)S(1)}, f32[24,128]{1,0:T(8,128)S(1)}, f32[16,128]{1,0:T(8,128)S(1)}, f32[16,128]{1,0:T(8,128)S(1)}, f32[56,128]{1,0:T...) custom-call(f32[3,17,4,128]{3,2,1,0:T(4,128)} %bitcast.12, ...), custom_call_target="tpu_custom_call" | custom-call | tf_op jit(solution)/shard_map/pallas_call | solution.py:671
  2.7 3.0 %collective-permute-start = (f32[56,128]{1,0:T(8,128)S(1)}, f32[56,128]{1,0:T(8,128)S(1)}, u32[]{:S(2)}, u32[]{:S(2)}) collective-permute-start(f32[56,128]{1,0:T(8,128)S(1)} %get-tuple-element.72), channel_id=1, source_target_pairs={{0,1},{1,0},{2,4},{3,5},{4,2},{5,3},{6,8},{7,9},{8,6},{9,7},{10,12... | collective-permute-start | bytes 86024 | tf_op jit(solution)/shard_map/ppermute | solution.py:694
  5.8 1.3 %collective-permute-start.2 = (f32[24,128]{1,0:T(8,128)S(1)}, f32[24,128]{1,0:T(8,128)S(1)}, u32[]{:S(2)}, u32[]{:S(2)}) collective-permute-start(f32[24,128]{1,0:T(8,128)S(1)} %get-tuple-element.74), channel_id=1, source_target_pairs={{0,2},{1,3},{2,0},{3,1},{4,6},{5,7},{6,4},{7,5},{8,10},{9,11},{10,... | collective-permute-start | bytes 36872 | tf_op jit(solution)/shard_map/ppermute | solution.py:694
  7.0 0.5 %collective-permute-start.4 = (f32[16,128]{1,0:T(8,128)S(1)}, f32[16,128]{1,0:T(8,128)S(1)}, u32[]{:S(2)}, u32[]{:S(2)}) collective-permute-start(f32[16,128]{1,0:T(8,128)S(1)} %get-tuple-element.76), channel_id=1, source_target_pairs={{0,2},{1,3},{2,0},{3,1},{4,6},{5,7},{6,4},{7,5},{8,10},{9,11},{10,... | collective-permute-start | bytes 24584 | tf_op jit(solution)/shard_map/ppermute | solution.py:694
  7.6 0.5 %shard_map.167 = (f32[320,128]{1,0:T(8,128)S(1)}, f32[320,128]{1,0:T(8,128)S(1)}) custom-call(f32[3,17,4,128]{3,2,1,0:T(4,128)S(1)} %get-tuple-element.62.next_ref, f32[17,4,128]{2,1,0:T(4,128)S(1)} %get-tuple-element.63.density_ref, f32[320,128]{1,0:T(8,128)S(1)} %get-tuple-element.64.mass_ref), custom_call_target="tpu_custom_call" | custom-call | tf_op jit(solution)/shard_map/pallas_call | solution.py:671
  8.1 0.5 %shard_map.168 = (f32[320,128]{1,0:T(8,128)S(1)}, f32[160,128]{1,0:T(8,128)S(1)}) custom-call(f32[320,128]{1,0:T(8,128)S(1)} %get-tuple-element.61.cur_ref.refs_0_.refs_1_, f32[8,128]{1,0:T(8,128)S(1)} %get-tuple-element.67.material_ref.refs_5_, bf16[2,640,384]{2,1,0:T(8,128)(2,1)S(1)} %get-tuple-element.68.own_ref, ...), custom_call_target="tpu_custom_call" | custom-call | tf_op jit(solution)/shard_map/pallas_call | solution.py:671
  8.6 0.8 %collective-permute-done.1.refs_7_.refs_11_.refs_4_ = f32[40,128]{1,0:T(8,128)S(1)} collective-permute-done((f32[40,128]{1,0:T(8,128)S(1)}, f32[40,128]{1,0:T(8,128)S(1)}, u32[]{:S(2)}, u32[]{:S(2)}) %collective-permute-start.1) | collective-permute-done | bytes 20512 | tf_op jit(solution)/shard_map/ppermute | solution.py:699
  9.5 0.9 %shard_map.169 = (f32[320,128]{1,0:T(8,128)S(1)}, f32[24,128]{1,0:T(8,128)S(1)}, f32[16,128]{1,0:T(8,128)S(1)}, f32[16,128]{1,0:T(8,128)S(1)}, f32[56,128]{1,0:T(8,128)S(1)}, /*index=5*/f32[28,128]{1,0:T(8,128)S(1)}) custom-call(f32[320,128]{1,0:T(8,128)S(1)} %get-tuple-element.61.cur_ref.refs_0_.refs_1_, f32[320,128]{1,0:T(8,128)S(1)} %get-tuple-element.65.refs_1_, ...), custom_call_target="tpu_custom_call" | custom-call | tf_op jit(solution)/shard_map/pallas_call | solution.py:671
  10.7 1.7 %collective-permute-start.6 = (f32[28,128]{1,0:T(8,128)S(1)}, f32[28,128]{1,0:T(8,128)S(1)}, u32[]{:S(2)}, u32[]{:S(2)}) collective-permute-start(f32[28,128]{1,0:T(8,128)S(1)} %get-tuple-element.83.refs_12_.refs_5_), channel_id=1, source_target_pairs={{1,0},{0,1},{3,2},{2,3},{5,4},{4,5},{7,6},{6,7},{9,8},{8,9},{11,10... | collective-permute-start | bytes 43016 | tf_op jit(solution)/shard_map/ppermute | solution.py:699
  12.4 0.5 %collective-permute-start.8 = (f32[16,128]{1,0:T(8,128)S(1)}, f32[16,128]{1,0:T(8,128)S(1)}, u32[]{:S(2)}, u32[]{:S(2)}) collective-permute-start(f32[16,128]{1,0:T(8,128)S(1)} %get-tuple-element.85), channel_id=1, source_target_pairs={{0,2},{1,3},{2,0},{3,1},{4,6},{5,7},{6,4},{7,5},{8,10},{9,11},{10,... | collective-permute-start | bytes 24584 | tf_op jit(solution)/shard_map/ppermute | solution.py:694
  12.9 0.5 %shard_map.170 = (f32[320,128]{1,0:T(8,128)S(1)}, f32[160,128]{1,0:T(8,128)S(1)}) custom-call(f32[320,128]{1,0:T(8,128)S(1)} %get-tuple-element.79.cur_ref._.refs_0_.refs_1_, f32[8,128]{1,0:T(8,128)S(1)} %get-tuple-element.67.material_ref.refs_5_, bf16[2,640,384]{2,1,0:T(8,128)(2,1)S(1)} %get-tuple-element.68.own_ref, ...), custom_call_target="tpu_custom_call" | custom-call | tf_op jit(solution)/shard_map/pallas_call | solution.py:671
  14.5 0.9 %shard_map.172 = (f32[320,128]{1,0:T(8,128)S(1)}, f32[24,128]{1,0:T(8,128)S(1)}, f32[16,128]{1,0:T(8,128)S(1)}, f32[16,128]{1,0:T(8,128)S(1)}, f32[56,128]{1,0:T(8,128)S(1)}, /*index=5*/f32[28,128]{1,0:T(8,128)S(1)}) custom-call(f32[320,128]{1,0:T(8,128)S(1)} %get-tuple-element.79.cur_ref._.refs_0_.refs_1_, ...), custom_call_target="tpu_custom_call" | custom-call | tf_op jit(solution)/shard_map/pallas_call | solution.py:671
  15.3 1.8 %collective-permute-start.10 = (f32[56,128]{1,0:T(8,128)S(1)}, f32[56,128]{1,0:T(8,128)S(1)}, u32[]{:S(2)}, u32[]{:S(2)}) collective-permute-start(f32[56,128]{1,0:T(8,128)S(1)} %get-tuple-element.94), channel_id=1, source_target_pairs={{0,1},{1,0},{2,4},{3,5},{4,2},{5,3},{6,8},{7,9},{8,6},{9,7},{10,12... | collective-permute-start | bytes 86024 | tf_op jit(solution)/shard_map/ppermute | solution.py:694
  17.4 0.5 %collective-permute-start.13 = (f32[16,128]{1,0:T(8,128)S(1)}, f32[16,128]{1,0:T(8,128)S(1)}, u32[]{:S(2)}, u32[]{:S(2)}) collective-permute-start(f32[16,128]{1,0:T(8,128)S(1)} %get-tuple-element.97), channel_id=1, source_target_pairs={{0,2},{1,3},{2,0},{3,1},{4,6},{5,7},{6,4},{7,5},{8,10},{9,11},{10,... | collective-permute-start | bytes 24584 | tf_op jit(solution)/shard_map/ppermute | solution.py:694
  17.9 0.5 %shard_map.173 = (f32[320,128]{1,0:T(8,128)S(1)}, f32[160,128]{1,0:T(8,128)S(1)}) custom-call(f32[320,128]{1,0:T(8,128)S(1)} %get-tuple-element.91.cur_ref.refs_0_.refs_1_, f32[8,128]{1,0:T(8,128)S(1)} %get-tuple-element.67.material_ref.refs_5_, bf16[2,640,384]{2,1,0:T(8,128)(2,1)S(1)} %get-tuple-element.68.own_ref, ...), custom_call_target="tpu_custom_call" | custom-call | tf_op jit(solution)/shard_map/pallas_call | solution.py:671
  19.1 1.7 %collective-permute-done.11.refs_7_.refs_8_ = f32[28,128]{1,0:T(8,128)S(1)} collective-permute-done((f32[28,128]{1,0:T(8,128)S(1)}, f32[28,128]{1,0:T(8,128)S(1)}, u32[]{:S(2)}, u32[]{:S(2)}) %collective-permute-start.11) | collective-permute-done | bytes 14368 | tf_op jit(solution)/shard_map/ppermute | solution.py:699
  20.9 0.9 %shard_map.174 = (f32[320,128]{1,0:T(8,128)S(1)}, f32[24,128]{1,0:T(8,128)S(1)}, f32[16,128]{1,0:T(8,128)S(1)}, f32[16,128]{1,0:T(8,128)S(1)}, f32[56,128]{1,0:T(8,128)S(1)}, /*index=5*/f32[28,128]{1,0:T(8,128)S(1)}) custom-call(f32[320,128]{1,0:T(8,128)S(1)} %get-tuple-element.91.cur_ref.refs_0_.refs_1_, ...), custom_call_target="tpu_custom_call" | custom-call | tf_op jit(solution)/shard_map/pallas_call | solution.py:671
  22.1 1.7 %collective-permute-start.16 = (f32[28,128]{1,0:T(8,128)S(1)}, f32[28,128]{1,0:T(8,128)S(1)}, u32[]{:S(2)}, u32[]{:S(2)}) collective-permute-start(f32[28,128]{1,0:T(8,128)S(1)} %get-tuple-element.103.refs_9_.refs_12_), channel_id=1, source_target_pairs={{1,0},{0,1},{3,2},{2,3},{5,4},{4,5},{7,6},{6,7},{9,8},{8,9},{11,10... | collective-permute-start | bytes 43016 | tf_op jit(solution)/shard_map/ppermute | solution.py:699
  24.3 0.5 %shard_map.175 = (f32[320,128]{1,0:T(8,128)S(1)}, f32[160,128]{1,0:T(8,128)S(1)}) custom-call(f32[320,128]{1,0:T(8,128)S(1)} %get-tuple-element.99.cur_ref.refs_0_, f32[8,128]{1,0:T(8,128)S(1)} %get-tuple-element.67.material_ref.refs_5_, bf16[2,640,384]{2,1,0:T(8,128)(2,1)S(1)} %get-tuple-element.68.own_ref, bf16[160,256]{1,0:T(8,128)(2,1)S(1)} %get-tuple-element.69.touch_ref), custom_call_target="tpu_custom_call" | custom-call | tf_op jit(solution)/shard_map/pallas_call | solution.py:671
  26.0 1.7 %collective-permute-start.20 = (f32[2,128]{1,0:T(2,128)S(1)}, f32[2,128]{1,0:T(2,128)S(1)}, u32[]{:S(2)}, u32[]{:S(2)}) collective-permute-start(f32[2,128]{1,0:T(2,128)S(1)} %get-tuple-element.115), channel_id=1, source_target_pairs={{0,1},{1,0},{2,3},{3,2},{4,8},{5,9},{6,10},{7,11},{8,4},{9,5},{10,... | collective-permute-start | bytes 3080 | tf_op jit(solution)/shard_map/ppermute | solution.py:694
  28.0 0.5 %collective-permute-start.22 = (f32[2,128]{1,0:T(2,128)S(1)}, f32[2,128]{1,0:T(2,128)S(1)}, u32[]{:S(2)}, u32[]{:S(2)}) collective-permute-start(f32[2,128]{1,0:T(2,128)S(1)} %get-tuple-element.117), channel_id=1, source_target_pairs={{0,4},{1,5},{2,6},{3,7},{4,0},{5,1},{6,2},{7,3},{8,12},{9,13},{10,... | collective-permute-start | bytes 3080 | tf_op jit(solution)/shard_map/ppermute | solution.py:694
  28.5 0.8 %collective-permute-start.23 = (f32[2,128]{1,0:T(2,128)S(1)}, f32[2,128]{1,0:T(2,128)S(1)}, u32[]{:S(2)}, u32[]{:S(2)}) collective-permute-start(f32[2,128]{1,0:T(2,128)S(1)} %get-tuple-element.118), channel_id=1, source_target_pairs={{0,2},{1,3},{2,0},{3,1},{4,6},{5,7},{6,4},{7,5},{8,10},{9,11},{10,... | collective-permute-start | bytes 3080 | tf_op jit(solution)/shard_map/ppermute | solution.py:694
  29.3 1.5 %shard_map.178 = (f32[3,17,4,128]{3,2,1,0:T(4,128)}, f32[3,17,4,128]{3,2,1,0:T(4,128)}) custom-call(f32[320,128]{1,0:T(8,128)S(1)} %get-tuple-element.99.cur_ref.refs_0_, f32[320,128]{1,0:T(8,128)S(1)} %get-tuple-element.91.cur_ref.refs_0_.refs_1_, f32[320,128]{1,0:T(8,128)S(1)} %get-tuple-element.66.refs_2_, f32[320,128]{1,0:T(8,128)S(1)} %get-tuple-element.100.refs_3_, ...), custom_call_target="tpu_custom_call" | custom-call | tf_op jit(solution)/shard_map/pallas_call | solution.py:671
  31.6 0.6 %add_bitcast_fusion = f32[1,2,128]{2,1,0:T(2,128)} fusion(f32[2,128]{1,0:T(2,128)S(1)} %collective-permute-done.23, f32[2,128]{1,0:T(2,128)S(1)} %collective-permute-done.22, f32[2,128]{1,0:T(2,128)S(1)} %collective-permute-done.21, f32[2,128]{1,0:T(2,128)S(1)} %get-tuple-element.111.refs_16_, f32[2,128]{1,0:T(2,128)S(1)} %collective-permute-done.20), kind=kLoop, calls=%fused_computation | loop fusion | flops 1024 | bytes 6144 | tf_op jit(solution)/shard_map/broadcast_in_dim | solution.py:838
  (38 shorter events, 5.6 us)
Async XLA Ops:
  2.7 6.8 %collective-permute-start = (f32[56,128]{1,0:T(8,128)S(1)}, f32[56,128]{1,0:T(8,128)S(1)}, u32[]{:S(2)}, u32[]{:S(2)}) collective-permute-start(f32[56,128]{1,0:T(8,128)S(1)} %get-tuple-element.72), channel_id=1, source_target_pairs={{0,1},{1,0},{2,4},{3,5},{4,2},{5,3},{6,8},{7,9},{8,6},{9,7},{10,12... | collective-permute-start | bytes 86024 | tf_op jit(solution)/shard_map/ppermute | solution.py:694
  5.7 3.8 %collective-permute-start.1 = (f32[40,128]{1,0:T(8,128)S(1)}, f32[40,128]{1,0:T(8,128)S(1)}, u32[]{:S(2)}, u32[]{:S(2)}) collective-permute-start(f32[40,128]{1,0:T(8,128)S(1)} %get-tuple-element.73.refs_12_.refs_13_.refs_3_), channel_id=1, source_target_pairs={{1,0},{0,1},{3,2},{2,3},{5,4},{4,5},{7,6},{6,7},{9,8},{8,9},{11,10... | collective-permute-start | bytes 61448 | tf_op jit(solution)/shard_map/ppermute | solution.py:699
  5.8 2.8 %collective-permute-start.2 = (f32[24,128]{1,0:T(8,128)S(1)}, f32[24,128]{1,0:T(8,128)S(1)}, u32[]{:S(2)}, u32[]{:S(2)}) collective-permute-start(f32[24,128]{1,0:T(8,128)S(1)} %get-tuple-element.74), channel_id=1, source_target_pairs={{0,2},{1,3},{2,0},{3,1},{4,6},{5,7},{6,4},{7,5},{8,10},{9,11},{10,... | collective-permute-start | bytes 36872 | tf_op jit(solution)/shard_map/ppermute | solution.py:694
  7.0 1.6 %collective-permute-start.3 = (f32[16,128]{1,0:T(8,128)S(1)}, f32[16,128]{1,0:T(8,128)S(1)}, u32[]{:S(2)}, u32[]{:S(2)}) collective-permute-start(f32[16,128]{1,0:T(8,128)S(1)} %get-tuple-element.75), channel_id=1, source_target_pairs={{0,2},{1,3},{2,0},{3,1},{4,6},{5,7},{6,4},{7,5},{8,10},{9,11},{10,... | collective-permute-start | bytes 24584 | tf_op jit(solution)/shard_map/ppermute | solution.py:694
  7.0 1.6 %collective-permute-start.4 = (f32[16,128]{1,0:T(8,128)S(1)}, f32[16,128]{1,0:T(8,128)S(1)}, u32[]{:S(2)}, u32[]{:S(2)}) collective-permute-start(f32[16,128]{1,0:T(8,128)S(1)} %get-tuple-element.76), channel_id=1, source_target_pairs={{0,2},{1,3},{2,0},{3,1},{4,6},{5,7},{6,4},{7,5},{8,10},{9,11},{10,... | collective-permute-start | bytes 24584 | tf_op jit(solution)/shard_map/ppermute | solution.py:694
  10.3 4.1 %collective-permute-start.5 = (f32[56,128]{1,0:T(8,128)S(1)}, f32[56,128]{1,0:T(8,128)S(1)}, u32[]{:S(2)}, u32[]{:S(2)}) collective-permute-start(f32[56,128]{1,0:T(8,128)S(1)} %get-tuple-element.82), channel_id=1, source_target_pairs={{0,1},{1,0},{2,4},{3,5},{4,2},{5,3},{6,8},{7,9},{8,6},{9,7},{10,12... | collective-permute-start | bytes 86024 | tf_op jit(solution)/shard_map/ppermute | solution.py:694
  10.7 3.8 %collective-permute-start.6 = (f32[28,128]{1,0:T(8,128)S(1)}, f32[28,128]{1,0:T(8,128)S(1)}, u32[]{:S(2)}, u32[]{:S(2)}) collective-permute-start(f32[28,128]{1,0:T(8,128)S(1)} %get-tuple-element.83.refs_12_.refs_5_), channel_id=1, source_target_pairs={{1,0},{0,1},{3,2},{2,3},{5,4},{4,5},{7,6},{6,7},{9,8},{8,9},{11,10... | collective-permute-start | bytes 43016 | tf_op jit(solution)/shard_map/ppermute | solution.py:699
  12.4 1.7 %collective-permute-start.7 = (f32[24,128]{1,0:T(8,128)S(1)}, f32[24,128]{1,0:T(8,128)S(1)}, u32[]{:S(2)}, u32[]{:S(2)}) collective-permute-start(f32[24,128]{1,0:T(8,128)S(1)} %get-tuple-element.84), channel_id=1, source_target_pairs={{0,2},{1,3},{2,0},{3,1},{4,6},{5,7},{6,4},{7,5},{8,10},{9,11},{10,... | collective-permute-start | bytes 36872 | tf_op jit(solution)/shard_map/ppermute | solution.py:694
  12.4 1.3 %collective-permute-start.8 = (f32[16,128]{1,0:T(8,128)S(1)}, f32[16,128]{1,0:T(8,128)S(1)}, u32[]{:S(2)}, u32[]{:S(2)}) collective-permute-start(f32[16,128]{1,0:T(8,128)S(1)} %get-tuple-element.85), channel_id=1, source_target_pairs={{0,2},{1,3},{2,0},{3,1},{4,6},{5,7},{6,4},{7,5},{8,10},{9,11},{10,... | collective-permute-start | bytes 24584 | tf_op jit(solution)/shard_map/ppermute | solution.py:694
  12.9 1.2 %collective-permute-start.9 = (f32[16,128]{1,0:T(8,128)S(1)}, f32[16,128]{1,0:T(8,128)S(1)}, u32[]{:S(2)}, u32[]{:S(2)}) collective-permute-start(f32[16,128]{1,0:T(8,128)S(1)} %get-tuple-element.86), channel_id=1, source_target_pairs={{0,2},{1,3},{2,0},{3,1},{4,6},{5,7},{6,4},{7,5},{8,10},{9,11},{10,... | collective-permute-start | bytes 24584 | tf_op jit(solution)/shard_map/ppermute | solution.py:694
  15.3 5.5 %collective-permute-start.10 = (f32[56,128]{1,0:T(8,128)S(1)}, f32[56,128]{1,0:T(8,128)S(1)}, u32[]{:S(2)}, u32[]{:S(2)}) collective-permute-start(f32[56,128]{1,0:T(8,128)S(1)} %get-tuple-element.94), channel_id=1, source_target_pairs={{0,1},{1,0},{2,4},{3,5},{4,2},{5,3},{6,8},{7,9},{8,6},{9,7},{10,12... | collective-permute-start | bytes 86024 | tf_op jit(solution)/shard_map/ppermute | solution.py:694
  17.1 3.7 %collective-permute-start.11 = (f32[28,128]{1,0:T(8,128)S(1)}, f32[28,128]{1,0:T(8,128)S(1)}, u32[]{:S(2)}, u32[]{:S(2)}) collective-permute-start(f32[28,128]{1,0:T(8,128)S(1)} %get-tuple-element.95.refs_12_.refs_7_), channel_id=1, source_target_pairs={{1,0},{0,1},{3,2},{2,3},{5,4},{4,5},{7,6},{6,7},{9,8},{8,9},{11,10... | collective-permute-start | bytes 43016 | tf_op jit(solution)/shard_map/ppermute | solution.py:699
  17.4 1.7 %collective-permute-start.12 = (f32[24,128]{1,0:T(8,128)S(1)}, f32[24,128]{1,0:T(8,128)S(1)}, u32[]{:S(2)}, u32[]{:S(2)}) collective-permute-start(f32[24,128]{1,0:T(8,128)S(1)} %get-tuple-element.96), channel_id=1, source_target_pairs={{0,2},{1,3},{2,0},{3,1},{4,6},{5,7},{6,4},{7,5},{8,10},{9,11},{10,... | collective-permute-start | bytes 36872 | tf_op jit(solution)/shard_map/ppermute | solution.py:694
  17.4 1.3 %collective-permute-start.13 = (f32[16,128]{1,0:T(8,128)S(1)}, f32[16,128]{1,0:T(8,128)S(1)}, u32[]{:S(2)}, u32[]{:S(2)}) collective-permute-start(f32[16,128]{1,0:T(8,128)S(1)} %get-tuple-element.97), channel_id=1, source_target_pairs={{0,2},{1,3},{2,0},{3,1},{4,6},{5,7},{6,4},{7,5},{8,10},{9,11},{10,... | collective-permute-start | bytes 24584 | tf_op jit(solution)/shard_map/ppermute | solution.py:694
  17.9 1.2 %collective-permute-start.14 = (f32[16,128]{1,0:T(8,128)S(1)}, f32[16,128]{1,0:T(8,128)S(1)}, u32[]{:S(2)}, u32[]{:S(2)}) collective-permute-start(f32[16,128]{1,0:T(8,128)S(1)} %get-tuple-element.98), channel_id=1, source_target_pairs={{0,2},{1,3},{2,0},{3,1},{4,6},{5,7},{6,4},{7,5},{8,10},{9,11},{10,... | collective-permute-start | bytes 24584 | tf_op jit(solution)/shard_map/ppermute | solution.py:694
  21.7 4.1 %collective-permute-start.15 = (f32[56,128]{1,0:T(8,128)S(1)}, f32[56,128]{1,0:T(8,128)S(1)}, u32[]{:S(2)}, u32[]{:S(2)}) collective-permute-start(f32[56,128]{1,0:T(8,128)S(1)} %get-tuple-element.102), channel_id=1, source_target_pairs={{0,1},{1,0},{2,4},{3,5},{4,2},{5,3},{6,8},{7,9},{8,6},{9,7},{10,12... | collective-permute-start | bytes 86024 | tf_op jit(solution)/shard_map/ppermute | solution.py:694
  22.1 3.7 %collective-permute-start.16 = (f32[28,128]{1,0:T(8,128)S(1)}, f32[28,128]{1,0:T(8,128)S(1)}, u32[]{:S(2)}, u32[]{:S(2)}) collective-permute-start(f32[28,128]{1,0:T(8,128)S(1)} %get-tuple-element.103.refs_9_.refs_12_), channel_id=1, source_target_pairs={{1,0},{0,1},{3,2},{2,3},{5,4},{4,5},{7,6},{6,7},{9,8},{8,9},{11,10... | collective-permute-start | bytes 43016 | tf_op jit(solution)/shard_map/ppermute | solution.py:699
  23.8 1.7 %collective-permute-start.17 = (f32[24,128]{1,0:T(8,128)S(1)}, f32[24,128]{1,0:T(8,128)S(1)}, u32[]{:S(2)}, u32[]{:S(2)}) collective-permute-start(f32[24,128]{1,0:T(8,128)S(1)} %get-tuple-element.104), channel_id=1, source_target_pairs={{0,2},{1,3},{2,0},{3,1},{4,6},{5,7},{6,4},{7,5},{8,10},{9,11},{10,... | collective-permute-start | bytes 36872 | tf_op jit(solution)/shard_map/ppermute | solution.py:694
  23.8 1.4 %collective-permute-start.18 = (f32[16,128]{1,0:T(8,128)S(1)}, f32[16,128]{1,0:T(8,128)S(1)}, u32[]{:S(2)}, u32[]{:S(2)}) collective-permute-start(f32[16,128]{1,0:T(8,128)S(1)} %get-tuple-element.105), channel_id=1, source_target_pairs={{0,2},{1,3},{2,0},{3,1},{4,6},{5,7},{6,4},{7,5},{8,10},{9,11},{10,... | collective-permute-start | bytes 24584 | tf_op jit(solution)/shard_map/ppermute | solution.py:694
  24.3 1.2 %collective-permute-start.19 = (f32[16,128]{1,0:T(8,128)S(1)}, f32[16,128]{1,0:T(8,128)S(1)}, u32[]{:S(2)}, u32[]{:S(2)}) collective-permute-start(f32[16,128]{1,0:T(8,128)S(1)} %get-tuple-element.106), channel_id=1, source_target_pairs={{0,2},{1,3},{2,0},{3,1},{4,6},{5,7},{6,4},{7,5},{8,10},{9,11},{10,... | collective-permute-start | bytes 24584 | tf_op jit(solution)/shard_map/ppermute | solution.py:694
  26.0 4.8 %collective-permute-start.20 = (f32[2,128]{1,0:T(2,128)S(1)}, f32[2,128]{1,0:T(2,128)S(1)}, u32[]{:S(2)}, u32[]{:S(2)}) collective-permute-start(f32[2,128]{1,0:T(2,128)S(1)} %get-tuple-element.115), channel_id=1, source_target_pairs={{0,1},{1,0},{2,3},{3,2},{4,8},{5,9},{6,10},{7,11},{8,4},{9,5},{10,... | collective-permute-start | bytes 3080 | tf_op jit(solution)/shard_map/ppermute | solution.py:694
  27.7 3.6 %collective-permute-start.21 = (f32[2,128]{1,0:T(2,128)S(1)}, f32[2,128]{1,0:T(2,128)S(1)}, u32[]{:S(2)}, u32[]{:S(2)}) collective-permute-start(f32[2,128]{1,0:T(2,128)S(1)} %get-tuple-element.116), channel_id=1, source_target_pairs={{0,1},{1,0},{2,4},{3,5},{4,2},{5,3},{6,8},{7,9},{8,6},{9,7},{10,12... | collective-permute-start | bytes 3080 | tf_op jit(solution)/shard_map/ppermute | solution.py:694
  28.0 3.6 %collective-permute-start.22 = (f32[2,128]{1,0:T(2,128)S(1)}, f32[2,128]{1,0:T(2,128)S(1)}, u32[]{:S(2)}, u32[]{:S(2)}) collective-permute-start(f32[2,128]{1,0:T(2,128)S(1)} %get-tuple-element.117), channel_id=1, source_target_pairs={{0,4},{1,5},{2,6},{3,7},{4,0},{5,1},{6,2},{7,3},{8,12},{9,13},{10,... | collective-permute-start | bytes 3080 | tf_op jit(solution)/shard_map/ppermute | solution.py:694
  28.5 3.1 %collective-permute-start.23 = (f32[2,128]{1,0:T(2,128)S(1)}, f32[2,128]{1,0:T(2,128)S(1)}, u32[]{:S(2)}, u32[]{:S(2)}) collective-permute-start(f32[2,128]{1,0:T(2,128)S(1)} %get-tuple-element.118), channel_id=1, source_target_pairs={{0,2},{1,3},{2,0},{3,1},{4,6},{5,7},{6,4},{7,5},{8,10},{9,11},{10,... | collective-permute-start | bytes 3080 | tf_op jit(solution)/shard_map/ppermute | solution.py:694

commit v15 on v14

--- a/solution.py
+++ b/solution.py
@@ -15,9 +15,9 @@
 PATCH_ROWS = 16
 LATER = 11
 FAULT = 24
-SENT_FAULT = 28
+SENT_FAULT = 24
 SENT = 56
-PARTS = (24, 16, 16)
+PARTS = (56,)
 
 time_step = 0.01
 lock_stiffness = 0.5
@@ -426,8 +426,8 @@
     *refs,
 ):
     later_hbm, refs = refs[:LATER], refs[LATER:]
-    cur_ref, *even_refs, odd_ref, fault_out_ref, material_ref = refs[:7]
-    later_refs, refs = refs[7 : 7 + LATER], refs[7 + LATER :]
+    cur_ref, *even_refs, odd_ref, fault_out_ref, material_ref = refs[:5]
+    later_refs, refs = refs[5 : 5 + LATER], refs[5 + LATER :]
     scratch, now_ref, flags_ref, weak_ref, lame_ref, shear_ref, sems = refs
     copies = start_copies(
         [
@@ -461,8 +461,7 @@
     right = edge_message(edge, lame_row, shear_row, z_elems)
     lasts = [store_fault(fault_out_ref, x, planes[x], z_elems) for x in range(4)]
     message, odd_ref[...] = select_messages(parity, sent_plane(planes[0], lasts[0]), right)
-    for even_ref, at in zip(even_refs, (0, PARTS[0], PARTS[0] + PARTS[1])):
-        even_ref[...] = message[at : at + even_ref.shape[0]]
+    even_refs[0][...] = message
     weak = weak_ref[...]
     tangent = []
     for i in range(flags_ref.shape[0]):
@@ -494,10 +493,10 @@
 
 
 def step_kernel(*refs, step, last, extra, last_place, pair, y_elems, z_elems):
-    cur_ref, fol_ref, minv_ref, base_ref, touch_ref, material_ref, odd_ref, up_ref = refs[:8]
-    refs = list(refs[8:])
+    cur_ref, fol_ref, minv_ref, base_ref, touch_ref, material_ref, even_ref, odd_ref, up_ref = refs[:9]
+    refs = list(refs[9:])
     down_ref = None if pair else refs.pop(0)
-    even_in = jnp.concatenate([refs.pop(0)[...] for _ in PARTS], axis=0)
+    even_in = even_ref[...]
     down_ref = up_ref if pair else down_ref
     first_up_ref, own_ref, first_own_ref, far_ref, edge_ref = refs[:5]
     refs = refs[5 + extra :]
@@ -526,8 +525,6 @@
     above = above_lanes(lanes, z_elems)
     middle = lax.broadcasted_iota(jnp.int32, (3, lanes), 0) == 1
     gap = jnp.zeros((4, lanes), jnp.float32)
-    if not last:
-        fault_out[FAULT:] = jnp.zeros_like(fault_out[FAULT:])
     planes = []
     for x in range(4):
         rows = slice(x * PLANE, (x + 1) * PLANE)
@@ -591,8 +588,7 @@
         edge = dot(edge_ref[...], jnp.concatenate(planes, axis=0))
         right = edge_message(edge, lame_row, shear_row, z_elems)
         message, odd_out[...] = select_messages(place % 2, first, right)
-        for even_out, at in zip(even_outs, (0, PARTS[0], PARTS[0] + PARTS[1])):
-            even_out[...] = message[at : at + even_out.shape[0]]
+        even_outs[0][...] = message
 
 
 def mask_kernel(owner_ref, flags_ref, stress_ref, _, mask_ref, weight_ref, *, z_elems):
@@ -631,8 +627,8 @@
 
 
 def patch_kernel(*refs, pair, steps):
-    mask_ref, weight_ref, grad_ref, table_ref, _ = refs[:5]
-    first_ref = refs[5] if pair else refs[6]
+    mask_ref, weight_ref, grad_ref, table_ref = refs[:4]
+    first_ref = refs[6] if pair else refs[7]
     home_out, out_a, out_b, out_c, out_d = refs[-5:]
     place = lax.axis_index("dom")
     grad = grad_ref[...] + first_ref[4:8] * weight_ref[4 * (steps - 1) : 4 * steps]
@@ -771,7 +767,7 @@
             [cur, material, own_table, touch_table],
             (),
         )
-        args = [cur, fol, minv, base, touch, material, odd_in] + fault_in + even_in
+        args = [cur, fol, minv, base, touch, material] + even_in + [odd_in] + fault_in
         args += [first_in[0], fault_rows, first_fault, far_table, edge_table]
         static = dict(
             step=step, last=last, extra=1 if last or step == 1 else 0, last_place=lax.axis_size("dom") - 1, pair=pair, y_elems=y_elems,
@@ -813,8 +809,8 @@
             sums = kernel_call(
                 patch_kernel,
                 [(PATCH_DEV, lanes)] * 5,
-                [mask, weight, grad, table, odd_in] + fault_in + even_in + [touch],
-                unread=(4,) + tuple(range(5 + len(fault_in), 9 + len(fault_in))),
+                [mask, weight, grad, table] + even_in + [odd_in] + fault_in + [touch],
+                unread=(4, 5, 6 + len(fault_in)),
                 pair=pair,
                 steps=steps,
             )

time: 32.3 us -> 33 us (1.022)
  waiting for transfers between devices: 5.59 us -> 8.21 us
  starting transfers between devices: 16 us -> 14 us
    ppermute x4, waiting for transfers between devices: 3.28 us -> 8.17 us  [from_behind(): lax.ppermute(block, axis, [((i - distance) % size, i) for i in range(size)])]
    ppermute x20 -> x12, waiting for transfers between devices: 2.31 us -> 0.03 us  [swapped(): return lax.ppermute(block, ('dom', 'depth'), route)]
    ppermute x20 -> x12, starting transfers between devices: 12.2 us -> 10.4 us  [swapped(): return lax.ppermute(block, ('dom', 'depth'), route)]
  transfers between devices with their start and end apart: 24 -> 16, of which waited for: 11 -> 4; matrix products, arithmetic and copies ran while one was open for 0% -> 0% of each run, Pallas kernels for 14% -> 14%
where the time goes in v15:
time: 33 us; the launch traced here: 32.8 us
  starting transfers between devices  14 us (42%)
  Pallas kernels  9.25 us (28%)
  waiting for transfers between devices  8.21 us (25%)
  between operations  0.77 us (2%)
  other arithmetic  0.57 us (2%)
    ppermute x12, starting transfers between devices, swapped(): return lax.ppermute(block, ('dom', 'depth'), route)  10.4 us
    pallas_call x13, Pallas kernels, kernel_call(): pl.pallas_call(functools.partial(body, **static) if static else body, out...  9.25 us
    ppermute x4, waiting for transfers between devices, from_behind(): lax.ppermute(block, axis, [((i - distance) % size, i) for i in range(size)])  8.17 us
    ppermute x4, starting transfers between devices, from_behind(): lax.ppermute(block, axis, [((i - distance) % size, i) for i in range(size)])  3.66 us
  transfers between devices with their start and end apart: 16, of which 4 were waited for; matrix products, arithmetic and copies ran while one was open for 0% of the time, Pallas kernels for 14%

profile of v15, /device:TPU:0, one launch (start us, length us, event | category | flops | bytes accessed | tf_op | source)
XLA Modules:
  0.0 32.8 jit_solution(581692237930597083)
XLA Ops:
  0.6 2.0 %shard_map.166 = (f32[320,128]{1,0:T(8,128)S(1)}, f32[56,128]{1,0:T(8,128)S(1)}, f32[56,128]{1,0:T(8,128)S(1)}, f32[40,128]{1,0:T(8,128)S(1)}, f32[8,128]{1,0:T(...) custom-call(f32[3,17,4,128]{3,2,1,0:T(4,128)} %bitcast.12, ...), custom_call_target="tpu_custom_call" | custom-call | tf_op jit(solution)/shard_map/pallas_call | solution.py:667
  2.7 0.5 %collective-permute-start = (f32[56,128]{1,0:T(8,128)S(1)}, f32[56,128]{1,0:T(8,128)S(1)}, u32[]{:S(2)}, u32[]{:S(2)}) collective-permute-start(f32[56,128]{1,0:T(8,128)S(1)} %get-tuple-element.64), channel_id=1, source_target_pairs={{0,2},{1,3},{2,0},{3,1},{4,6},{5,7},{6,4},{7,5},{8,10},{9,11},{10,... | collective-permute-start | bytes 86024 | tf_op jit(solution)/shard_map/ppermute | solution.py:690
  3.2 2.6 %collective-permute-start.1 = (f32[56,128]{1,0:T(8,128)S(1)}, f32[56,128]{1,0:T(8,128)S(1)}, u32[]{:S(2)}, u32[]{:S(2)}) collective-permute-start(f32[56,128]{1,0:T(8,128)S(1)} %get-tuple-element.65), channel_id=1, source_target_pairs={{0,1},{1,0},{2,4},{3,5},{4,2},{5,3},{6,8},{7,9},{8,6},{9,7},{10,12... | collective-permute-start | bytes 86024 | tf_op jit(solution)/shard_map/ppermute | solution.py:690
  5.8 0.5 %shard_map.167 = (f32[320,128]{1,0:T(8,128)S(1)}, f32[320,128]{1,0:T(8,128)S(1)}) custom-call(f32[3,17,4,128]{3,2,1,0:T(4,128)S(1)} %get-tuple-element.54.next_ref, f32[17,4,128]{2,1,0:T(4,128)S(1)} %get-tuple-element.55.density_ref, f32[320,128]{1,0:T(8,128)S(1)} %get-tuple-element.56.mass_ref), custom_call_target="tpu_custom_call" | custom-call | tf_op jit(solution)/shard_map/pallas_call | solution.py:667
  6.4 0.5 %shard_map.168 = (f32[320,128]{1,0:T(8,128)S(1)}, f32[160,128]{1,0:T(8,128)S(1)}) custom-call(f32[320,128]{1,0:T(8,128)S(1)} %get-tuple-element.53.cur_ref.refs_0_.refs_1_, f32[8,128]{1,0:T(8,128)S(1)} %get-tuple-element.59.material_ref.refs_5_, bf16[2,640,384]{2,1,0:T(8,128)(2,1)S(1)} %get-tuple-element.60.own_ref, ...), custom_call_target="tpu_custom_call" | custom-call | tf_op jit(solution)/shard_map/pallas_call | solution.py:667
  6.9 2.7 %collective-permute-done.2.refs_8_.refs_9_.refs_4_ = f32[40,128]{1,0:T(8,128)S(1)} collective-permute-done((f32[40,128]{1,0:T(8,128)S(1)}, f32[40,128]{1,0:T(8,128)S(1)}, u32[]{:S(2)}, u32[]{:S(2)}) %collective-permute-start.2) | collective-permute-done | bytes 20512 | tf_op jit(solution)/shard_map/ppermute | solution.py:695
  9.6 0.9 %shard_map.169 = (f32[320,128]{1,0:T(8,128)S(1)}, f32[56,128]{1,0:T(8,128)S(1)}, f32[56,128]{1,0:T(8,128)S(1)}, f32[24,128]{1,0:T(8,128)S(1)}) custom-call(f32[320,128]{1,0:T(8,128)S(1)} %get-tuple-element.53.cur_ref.refs_0_.refs_1_, f32[320,128]{1,0:T(8,128)S(1)} %get-tuple-element.57.refs_1_, f32[320,128]{1,0:T(8,128)S(1)} %get-tuple-element.58.refs_2_, ...), custom_call_target="tpu_custom_call" | custom-call | tf_op jit(solution)/shard_map/pallas_call | solution.py:667
  11.0 1.6 %collective-permute-start.5 = (f32[24,128]{1,0:T(8,128)S(1)}, f32[24,128]{1,0:T(8,128)S(1)}, u32[]{:S(2)}, u32[]{:S(2)}) collective-permute-start(f32[24,128]{1,0:T(8,128)S(1)} %get-tuple-element.74.refs_10_.refs_5_), channel_id=1, source_target_pairs={{1,0},{0,1},{3,2},{2,3},{5,4},{4,5},{7,6},{6,7},{9,8},{8,9},{11,10... | collective-permute-start | bytes 36872 | tf_op jit(solution)/shard_map/ppermute | solution.py:695
  12.6 0.5 %shard_map.170 = (f32[320,128]{1,0:T(8,128)S(1)}, f32[160,128]{1,0:T(8,128)S(1)}) custom-call(f32[320,128]{1,0:T(8,128)S(1)} %get-tuple-element.69.cur_ref._.refs_0_.refs_1_, f32[8,128]{1,0:T(8,128)S(1)} %get-tuple-element.59.material_ref.refs_5_, bf16[2,640,384]{2,1,0:T(8,128)(2,1)S(1)} %get-tuple-element.60.own_ref, ...), custom_call_target="tpu_custom_call" | custom-call | tf_op jit(solution)/shard_map/pallas_call | solution.py:667
  13.3 1.4 %collective-permute-done.5.refs_8_.refs_6_ = f32[24,128]{1,0:T(8,128)S(1)} collective-permute-done((f32[24,128]{1,0:T(8,128)S(1)}, f32[24,128]{1,0:T(8,128)S(1)}, u32[]{:S(2)}, u32[]{:S(2)}) %collective-permute-start.5) | collective-permute-done | bytes 12320 | tf_op jit(solution)/shard_map/ppermute | solution.py:695
  14.7 0.9 %shard_map.172 = (f32[320,128]{1,0:T(8,128)S(1)}, f32[56,128]{1,0:T(8,128)S(1)}, f32[56,128]{1,0:T(8,128)S(1)}, f32[24,128]{1,0:T(8,128)S(1)}) custom-call(f32[320,128]{1,0:T(8,128)S(1)} %get-tuple-element.69.cur_ref._.refs_0_.refs_1_, f32[320,128]{1,0:T(8,128)S(1)} %get-tuple-element.53.cur_ref.refs_0_.refs_1_, f32[320,128]{1,0:T(8,128)S(1)} %get-tuple-element.58.refs_2_, ...), custom_call_target="tpu_custom_call" | custom-call | tf_op jit(solution)/shard_map/pallas_call | solution.py:667
  15.6 1.7 %collective-permute-start.7 = (f32[56,128]{1,0:T(8,128)S(1)}, f32[56,128]{1,0:T(8,128)S(1)}, u32[]{:S(2)}, u32[]{:S(2)}) collective-permute-start(f32[56,128]{1,0:T(8,128)S(1)} %get-tuple-element.83), channel_id=1, source_target_pairs={{0,1},{1,0},{2,4},{3,5},{4,2},{5,3},{6,8},{7,9},{8,6},{9,7},{10,12... | collective-permute-start | bytes 86024 | tf_op jit(solution)/shard_map/ppermute | solution.py:690
  17.7 0.5 %shard_map.173 = (f32[320,128]{1,0:T(8,128)S(1)}, f32[160,128]{1,0:T(8,128)S(1)}) custom-call(f32[320,128]{1,0:T(8,128)S(1)} %get-tuple-element.79.cur_ref.refs_0_.refs_1_, f32[8,128]{1,0:T(8,128)S(1)} %get-tuple-element.59.material_ref.refs_5_, bf16[2,640,384]{2,1,0:T(8,128)(2,1)S(1)} %get-tuple-element.60.own_ref, ...), custom_call_target="tpu_custom_call" | custom-call | tf_op jit(solution)/shard_map/pallas_call | solution.py:667
  18.2 2.8 %collective-permute-done.8.refs_8_ = f32[24,128]{1,0:T(8,128)S(1)} collective-permute-done((f32[24,128]{1,0:T(8,128)S(1)}, f32[24,128]{1,0:T(8,128)S(1)}, u32[]{:S(2)}, u32[]{:S(2)}) %collective-permute-start.8) | collective-permute-done | bytes 12320 | tf_op jit(solution)/shard_map/ppermute | solution.py:695
  21.0 0.9 %shard_map.174 = (f32[320,128]{1,0:T(8,128)S(1)}, f32[56,128]{1,0:T(8,128)S(1)}, f32[56,128]{1,0:T(8,128)S(1)}, f32[24,128]{1,0:T(8,128)S(1)}) custom-call(f32[320,128]{1,0:T(8,128)S(1)} %get-tuple-element.79.cur_ref.refs_0_.refs_1_, f32[320,128]{1,0:T(8,128)S(1)} %get-tuple-element.69.cur_ref._.refs_0_.refs_1_, f32[320,128]{1,0:T(8,128)S(1)} %get-tuple-element.58.refs_2_, ...), custom_call_target="tpu_custom_call" | custom-call | tf_op jit(solution)/shard_map/pallas_call | solution.py:667
  22.0 0.5 %collective-permute-start.10 = (f32[56,128]{1,0:T(8,128)S(1)}, f32[56,128]{1,0:T(8,128)S(1)}, u32[]{:S(2)}, u32[]{:S(2)}) collective-permute-start(f32[56,128]{1,0:T(8,128)S(1)} %get-tuple-element.89), channel_id=1, source_target_pairs={{0,1},{1,0},{2,4},{3,5},{4,2},{5,3},{6,8},{7,9},{8,6},{9,7},{10,12... | collective-permute-start | bytes 86024 | tf_op jit(solution)/shard_map/ppermute | solution.py:690
  22.5 1.6 %collective-permute-start.11 = (f32[24,128]{1,0:T(8,128)S(1)}, f32[24,128]{1,0:T(8,128)S(1)}, u32[]{:S(2)}, u32[]{:S(2)}) collective-permute-start(f32[24,128]{1,0:T(8,128)S(1)} %get-tuple-element.90.refs_9_.refs_10_), channel_id=1, source_target_pairs={{1,0},{0,1},{3,2},{2,3},{5,4},{4,5},{7,6},{6,7},{9,8},{8,9},{11,10... | collective-permute-start | bytes 36872 | tf_op jit(solution)/shard_map/ppermute | solution.py:695
  24.1 0.5 %shard_map.175 = (f32[320,128]{1,0:T(8,128)S(1)}, f32[160,128]{1,0:T(8,128)S(1)}) custom-call(f32[320,128]{1,0:T(8,128)S(1)} %get-tuple-element.85.cur_ref.refs_0_, f32[8,128]{1,0:T(8,128)S(1)} %get-tuple-element.59.material_ref.refs_5_, bf16[2,640,384]{2,1,0:T(8,128)(2,1)S(1)} %get-tuple-element.60.own_ref, bf16[160,256]{1,0:T(8,128)(2,1)S(1)} %get-tuple-element.61.touch_ref), custom_call_target="tpu_custom_call" | custom-call | tf_op jit(solution)/shard_map/pallas_call | solution.py:667
  24.9 1.3 %collective-permute-done.11.refs_6_.refs_8_ = f32[24,128]{1,0:T(8,128)S(1)} collective-permute-done((f32[24,128]{1,0:T(8,128)S(1)}, f32[24,128]{1,0:T(8,128)S(1)}, u32[]{:S(2)}, u32[]{:S(2)}) %collective-permute-start.11) | collective-permute-done | bytes 12320 | tf_op jit(solution)/shard_map/ppermute | solution.py:695
  26.3 1.6 %collective-permute-start.12 = (f32[2,128]{1,0:T(2,128)S(1)}, f32[2,128]{1,0:T(2,128)S(1)}, u32[]{:S(2)}, u32[]{:S(2)}) collective-permute-start(f32[2,128]{1,0:T(2,128)S(1)} %get-tuple-element.99), channel_id=1, source_target_pairs={{0,1},{1,0},{2,3},{3,2},{4,8},{5,9},{6,10},{7,11},{8,4},{9,5},{10,... | collective-permute-start | bytes 3080 | tf_op jit(solution)/shard_map/ppermute | solution.py:690
  28.4 1.1 %collective-permute-start.14 = (f32[2,128]{1,0:T(2,128)S(1)}, f32[2,128]{1,0:T(2,128)S(1)}, u32[]{:S(2)}, u32[]{:S(2)}) collective-permute-start(f32[2,128]{1,0:T(2,128)S(1)} %get-tuple-element.101), channel_id=1, source_target_pairs={{0,4},{1,5},{2,6},{3,7},{4,0},{5,1},{6,2},{7,3},{8,12},{9,13},{10,... | collective-permute-start | bytes 3080 | tf_op jit(solution)/shard_map/ppermute | solution.py:690
  29.5 1.2 %collective-permute-start.15 = (f32[2,128]{1,0:T(2,128)S(1)}, f32[2,128]{1,0:T(2,128)S(1)}, u32[]{:S(2)}, u32[]{:S(2)}) collective-permute-start(f32[2,128]{1,0:T(2,128)S(1)} %get-tuple-element.102), channel_id=1, source_target_pairs={{0,2},{1,3},{2,0},{3,1},{4,6},{5,7},{6,4},{7,5},{8,10},{9,11},{10,... | collective-permute-start | bytes 3080 | tf_op jit(solution)/shard_map/ppermute | solution.py:690
  30.7 1.5 %shard_map.178 = (f32[3,17,4,128]{3,2,1,0:T(4,128)}, f32[3,17,4,128]{3,2,1,0:T(4,128)}) custom-call(f32[320,128]{1,0:T(8,128)S(1)} %get-tuple-element.85.cur_ref.refs_0_, f32[320,128]{1,0:T(8,128)S(1)} %get-tuple-element.79.cur_ref.refs_0_.refs_1_, f32[320,128]{1,0:T(8,128)S(1)} %get-tuple-element.58.refs_2_, f32[320,128]{1,0:T(8,128)S(1)} %get-tuple-element.86.refs_3_, ...), custom_call_target="tpu_custom_call" | custom-call | tf_op jit(solution)/shard_map/pallas_call | solution.py:667
  32.3 0.6 %add_bitcast_fusion = f32[1,2,128]{2,1,0:T(2,128)} fusion(f32[2,128]{1,0:T(2,128)S(1)} %collective-permute-done.15, f32[2,128]{1,0:T(2,128)S(1)} %collective-permute-done.14, f32[2,128]{1,0:T(2,128)S(1)} %collective-permute-done.13, f32[2,128]{1,0:T(2,128)S(1)} %get-tuple-element.95.refs_14_, f32[2,128]{1,0:T(2,128)S(1)} %collective-permute-done.12), kind=kLoop, calls=%fused_computation | loop fusion | flops 1024 | bytes 6144 | tf_op jit(solution)/shard_map/broadcast_in_dim | solution.py:834
  (22 shorter events, 2.2 us)
Async XLA Ops:
  2.7 6.9 %collective-permute-start = (f32[56,128]{1,0:T(8,128)S(1)}, f32[56,128]{1,0:T(8,128)S(1)}, u32[]{:S(2)}, u32[]{:S(2)}) collective-permute-start(f32[56,128]{1,0:T(8,128)S(1)} %get-tuple-element.64), channel_id=1, source_target_pairs={{0,2},{1,3},{2,0},{3,1},{4,6},{5,7},{6,4},{7,5},{8,10},{9,11},{10,... | collective-permute-start | bytes 86024 | tf_op jit(solution)/shard_map/ppermute | solution.py:690
  3.2 6.4 %collective-permute-start.1 = (f32[56,128]{1,0:T(8,128)S(1)}, f32[56,128]{1,0:T(8,128)S(1)}, u32[]{:S(2)}, u32[]{:S(2)}) collective-permute-start(f32[56,128]{1,0:T(8,128)S(1)} %get-tuple-element.65), channel_id=1, source_target_pairs={{0,1},{1,0},{2,4},{3,5},{4,2},{5,3},{6,8},{7,9},{8,6},{9,7},{10,12... | collective-permute-start | bytes 86024 | tf_op jit(solution)/shard_map/ppermute | solution.py:690
  5.8 3.8 %collective-permute-start.2 = (f32[40,128]{1,0:T(8,128)S(1)}, f32[40,128]{1,0:T(8,128)S(1)}, u32[]{:S(2)}, u32[]{:S(2)}) collective-permute-start(f32[40,128]{1,0:T(8,128)S(1)} %get-tuple-element.66.refs_10_.refs_11_.refs_3_), channel_id=1, source_target_pairs={{1,0},{0,1},{3,2},{2,3},{5,4},{4,5},{7,6},{6,7},{9,8},{8,9},{11,10... | collective-permute-start | bytes 61448 | tf_op jit(solution)/shard_map/ppermute | solution.py:695
  10.4 4.2 %collective-permute-start.3 = (f32[56,128]{1,0:T(8,128)S(1)}, f32[56,128]{1,0:T(8,128)S(1)}, u32[]{:S(2)}, u32[]{:S(2)}) collective-permute-start(f32[56,128]{1,0:T(8,128)S(1)} %get-tuple-element.72), channel_id=1, source_target_pairs={{0,2},{1,3},{2,0},{3,1},{4,6},{5,7},{6,4},{7,5},{8,10},{9,11},{10,... | collective-permute-start | bytes 86024 | tf_op jit(solution)/shard_map/ppermute | solution.py:690
  10.5 4.2 %collective-permute-start.4 = (f32[56,128]{1,0:T(8,128)S(1)}, f32[56,128]{1,0:T(8,128)S(1)}, u32[]{:S(2)}, u32[]{:S(2)}) collective-permute-start(f32[56,128]{1,0:T(8,128)S(1)} %get-tuple-element.73), channel_id=1, source_target_pairs={{0,1},{1,0},{2,4},{3,5},{4,2},{5,3},{6,8},{7,9},{8,6},{9,7},{10,12... | collective-permute-start | bytes 86024 | tf_op jit(solution)/shard_map/ppermute | solution.py:690
  11.0 3.7 %collective-permute-start.5 = (f32[24,128]{1,0:T(8,128)S(1)}, f32[24,128]{1,0:T(8,128)S(1)}, u32[]{:S(2)}, u32[]{:S(2)}) collective-permute-start(f32[24,128]{1,0:T(8,128)S(1)} %get-tuple-element.74.refs_10_.refs_5_), channel_id=1, source_target_pairs={{1,0},{0,1},{3,2},{2,3},{5,4},{4,5},{7,6},{6,7},{9,8},{8,9},{11,10... | collective-permute-start | bytes 36872 | tf_op jit(solution)/shard_map/ppermute | solution.py:695
  15.5 5.5 %collective-permute-start.6 = (f32[56,128]{1,0:T(8,128)S(1)}, f32[56,128]{1,0:T(8,128)S(1)}, u32[]{:S(2)}, u32[]{:S(2)}) collective-permute-start(f32[56,128]{1,0:T(8,128)S(1)} %get-tuple-element.82), channel_id=1, source_target_pairs={{0,2},{1,3},{2,0},{3,1},{4,6},{5,7},{6,4},{7,5},{8,10},{9,11},{10,... | collective-permute-start | bytes 86024 | tf_op jit(solution)/shard_map/ppermute | solution.py:690
  15.6 5.4 %collective-permute-start.7 = (f32[56,128]{1,0:T(8,128)S(1)}, f32[56,128]{1,0:T(8,128)S(1)}, u32[]{:S(2)}, u32[]{:S(2)}) collective-permute-start(f32[56,128]{1,0:T(8,128)S(1)} %get-tuple-element.83), channel_id=1, source_target_pairs={{0,1},{1,0},{2,4},{3,5},{4,2},{5,3},{6,8},{7,9},{8,6},{9,7},{10,12... | collective-permute-start | bytes 86024 | tf_op jit(solution)/shard_map/ppermute | solution.py:690
  17.3 3.7 %collective-permute-start.8 = (f32[24,128]{1,0:T(8,128)S(1)}, f32[24,128]{1,0:T(8,128)S(1)}, u32[]{:S(2)}, u32[]{:S(2)}) collective-permute-start(f32[24,128]{1,0:T(8,128)S(1)} %get-tuple-element.84.refs_10_.refs_7_), channel_id=1, source_target_pairs={{1,0},{0,1},{3,2},{2,3},{5,4},{4,5},{7,6},{6,7},{9,8},{8,9},{11,10... | collective-permute-start | bytes 36872 | tf_op jit(solution)/shard_map/ppermute | solution.py:695
  21.9 4.3 %collective-permute-start.9 = (f32[56,128]{1,0:T(8,128)S(1)}, f32[56,128]{1,0:T(8,128)S(1)}, u32[]{:S(2)}, u32[]{:S(2)}) collective-permute-start(f32[56,128]{1,0:T(8,128)S(1)} %get-tuple-element.88), channel_id=1, source_target_pairs={{0,2},{1,3},{2,0},{3,1},{4,6},{5,7},{6,4},{7,5},{8,10},{9,11},{10,... | collective-permute-start | bytes 86024 | tf_op jit(solution)/shard_map/ppermute | solution.py:690
  22.0 4.2 %collective-permute-start.10 = (f32[56,128]{1,0:T(8,128)S(1)}, f32[56,128]{1,0:T(8,128)S(1)}, u32[]{:S(2)}, u32[]{:S(2)}) collective-permute-start(f32[56,128]{1,0:T(8,128)S(1)} %get-tuple-element.89), channel_id=1, source_target_pairs={{0,1},{1,0},{2,4},{3,5},{4,2},{5,3},{6,8},{7,9},{8,6},{9,7},{10,12... | collective-permute-start | bytes 86024 | tf_op jit(solution)/shard_map/ppermute | solution.py:690
  22.5 3.7 %collective-permute-start.11 = (f32[24,128]{1,0:T(8,128)S(1)}, f32[24,128]{1,0:T(8,128)S(1)}, u32[]{:S(2)}, u32[]{:S(2)}) collective-permute-start(f32[24,128]{1,0:T(8,128)S(1)} %get-tuple-element.90.refs_9_.refs_10_), channel_id=1, source_target_pairs={{1,0},{0,1},{3,2},{2,3},{5,4},{4,5},{7,6},{6,7},{9,8},{8,9},{11,10... | collective-permute-start | bytes 36872 | tf_op jit(solution)/shard_map/ppermute | solution.py:695
  26.3 5.9 %collective-permute-start.12 = (f32[2,128]{1,0:T(2,128)S(1)}, f32[2,128]{1,0:T(2,128)S(1)}, u32[]{:S(2)}, u32[]{:S(2)}) collective-permute-start(f32[2,128]{1,0:T(2,128)S(1)} %get-tuple-element.99), channel_id=1, source_target_pairs={{0,1},{1,0},{2,3},{3,2},{4,8},{5,9},{6,10},{7,11},{8,4},{9,5},{10,... | collective-permute-start | bytes 3080 | tf_op jit(solution)/shard_map/ppermute | solution.py:690
  27.9 4.3 %collective-permute-start.13 = (f32[2,128]{1,0:T(2,128)S(1)}, f32[2,128]{1,0:T(2,128)S(1)}, u32[]{:S(2)}, u32[]{:S(2)}) collective-permute-start(f32[2,128]{1,0:T(2,128)S(1)} %get-tuple-element.100), channel_id=1, source_target_pairs={{0,1},{1,0},{2,4},{3,5},{4,2},{5,3},{6,8},{7,9},{8,6},{9,7},{10,12... | collective-permute-start | bytes 3080 | tf_op jit(solution)/shard_map/ppermute | solution.py:690
  28.4 3.8 %collective-permute-start.14 = (f32[2,128]{1,0:T(2,128)S(1)}, f32[2,128]{1,0:T(2,128)S(1)}, u32[]{:S(2)}, u32[]{:S(2)}) collective-permute-start(f32[2,128]{1,0:T(2,128)S(1)} %get-tuple-element.101), channel_id=1, source_target_pairs={{0,4},{1,5},{2,6},{3,7},{4,0},{5,1},{6,2},{7,3},{8,12},{9,13},{10,... | collective-permute-start | bytes 3080 | tf_op jit(solution)/shard_map/ppermute | solution.py:690
  29.5 2.8 %collective-permute-start.15 = (f32[2,128]{1,0:T(2,128)S(1)}, f32[2,128]{1,0:T(2,128)S(1)}, u32[]{:S(2)}, u32[]{:S(2)}) collective-permute-start(f32[2,128]{1,0:T(2,128)S(1)} %get-tuple-element.102), channel_id=1, source_target_pairs={{0,2},{1,3},{2,0},{3,1},{4,6},{5,7},{6,4},{7,5},{8,10},{9,11},{10,... | collective-permute-start | bytes 3080 | tf_op jit(solution)/shard_map/ppermute | solution.py:690

commit v16 on v13

--- a/solution.py
+++ b/solution.py
@@ -361,11 +361,11 @@
     copies = start_copies(
         [
             (now_hbm, now_ref),
-            (later_hbm[0], later_refs[0]),
             (lame_hbm, lame_ref),
             (shear_hbm, shear_ref),
             (flags_hbm, flags_ref),
             (weak_hbm, weak_ref),
+            (later_hbm[0], later_refs[0]),
         ]
         + list(zip(later_hbm[1:], later_refs[1:])),
         sems,
@@ -377,20 +377,12 @@
     gather = gather_table(lanes, z_elems)
     fault = fault_table(lanes, z_elems)
     scratch[...] = jnp.zeros_like(scratch)
-    for copy in copies[:6]:
+    for copy in copies[1:5]:
         copy.wait()
-    cur = to_elements(lambda c, y: now_ref[c, y], scratch, gather, y_elems)
-    cur_ref[...] = cur
     lame_row, shear_row = material_rows(lame_ref, shear_ref)
     material_ref[...] = jnp.concatenate(
         [lame_row, shear_row, jnp.zeros((6, lanes), jnp.float32)], axis=0
     )
-    planes = [cur[x * PLANE : (x + 1) * PLANE] for x in range(4)]
-    edge = dot(edge_ref[...], jnp.concatenate([stacked(p) for p in planes], axis=0))
-    right = edge_message(edge, lame_row, shear_row, z_elems)
-    message, odd_ref[...] = select_messages(parity, cur[: 4 * BLOCK], right)
-    for even_ref, at in zip(even_refs, (0, PARTS[0], PARTS[0] + PARTS[1])):
-        even_ref[...] = message[at : at + even_ref.shape[0]]
     weak = weak_ref[...]
     tangent = []
     for i in range(flags_ref.shape[0]):
@@ -398,9 +390,19 @@
         tangent.append(
             jnp.where(flag == 0, lock_stiffness, jnp.where(flag == 1, -weak, 0.0))
         )
+    fault_out_ref[FAULT:] = exact_dot(jnp.concatenate(tangent, axis=0), fault)
+    copies[0].wait()
+    cur = to_elements(lambda c, y: now_ref[c, y], scratch, gather, y_elems)
+    cur_ref[...] = cur
+    planes = [cur[x * PLANE : (x + 1) * PLANE] for x in range(4)]
     for x in range(4):
         store_fault(fault_out_ref, x, planes[x], z_elems)
-    fault_out_ref[FAULT:] = exact_dot(jnp.concatenate(tangent, axis=0), fault)
+    copies[5].wait()
+    edge = dot(edge_ref[...], jnp.concatenate([stacked(p) for p in planes], axis=0))
+    right = edge_message(edge, lame_row, shear_row, z_elems)
+    message, odd_ref[...] = select_messages(parity, cur[: 4 * BLOCK], right)
+    for even_ref, at in zip(even_refs, (0, PARTS[0], PARTS[0] + PARTS[1])):
+        even_ref[...] = message[at : at + even_ref.shape[0]]
     for copy in copies[6:]:
         copy.wait()
 
@@ -583,6 +585,10 @@
     low = place % 4 < 2
     out_c[...] = jnp.where(low, rows[4], rows[0])
     out_d[...] = jnp.where(low, rows[0], rows[4])
+
+
+def sum_kernel(*refs):
+    refs[-1][...] = sum(ref[...] for ref in refs[:-1])
 
 
 VMEM = pl.BlockSpec(memory_space=pltpu.VMEM)
@@ -753,9 +759,10 @@
                 pair=pair,
                 steps=steps,
             )
-            patch_sums = sums[0]
+            shares = [sums[0]]
             for i, distance, group in ((4, 2, 1), (2, 1, 1), (3, 2, 0), (1, 1, 0)):
-                patch_sums = patch_sums + swapped(sums[i], distance, group)
+                shares.append(swapped(sums[i], distance, group))
+            patch_sums = kernel_call(sum_kernel, [(PATCH_DEV, lanes)], shares)[0]
             earlier, later = kernel_call(
                 step_kernel,
                 [whole, whole],

time: 32.1 us -> 32.1 us (level)
  other arithmetic: 0.57 us -> 0 us
  Pallas kernels: 9.15 us -> 9.63 us
    broadcast_in_dim x1 -> x0, other arithmetic: 0.57 us -> none  [on_device(): patch_sums[None]]
    pallas_call x13 -> x14, Pallas kernels: 9.15 us -> 9.63 us  [kernel_call(): pl.pallas_call(functools.partial(body, **static) if static else body, out...]
where the time goes in v16:
time: 32.1 us; the launch traced here: 31.9 us
  starting transfers between devices  15.8 us (49%)
  Pallas kernels  9.63 us (30%)
  waiting for transfers between devices  5.72 us (18%)
  between operations  0.74 us (2%)
    ppermute x20, starting transfers between devices, swapped(): return lax.ppermute(block, ('dom', 'depth'), route)  12 us
    pallas_call x14, Pallas kernels, kernel_call(): pl.pallas_call(functools.partial(body, **static) if static else body, out...  9.63 us
    ppermute x4, starting transfers between devices, from_behind(): lax.ppermute(block, axis, [((i - distance) % size, i) for i in range(size)])  3.78 us
    ppermute x4, waiting for transfers between devices, from_behind(): lax.ppermute(block, axis, [((i - distance) % size, i) for i in range(size)])  3.31 us
    ppermute x20, waiting for transfers between devices, swapped(): return lax.ppermute(block, ('dom', 'depth'), route)  2.4 us
  transfers between devices with their start and end apart: 24, of which 9 were waited for; matrix products, arithmetic and copies ran while one was open for 0% of the time, Pallas kernels for 14%

profile of v16, /device:TPU:0, one launch (start us, length us, event | category | flops | bytes accessed | tf_op | source)
XLA Modules:
  0.0 31.9 jit_solution(17404283167084077959)
XLA Ops:
  0.6 2.0 %shard_map.166 = (f32[320,128]{1,0:T(8,128)S(1)}, f32[24,128]{1,0:T(8,128)S(1)}, f32[24,128]{1,0:T(8,128)S(1)}, f32[16,128]{1,0:T(8,128)S(1)}, f32[64,128]{1,0:T...) custom-call(f32[3,17,4,128]{3,2,1,0:T(4,128)} %bitcast.11, ...), custom_call_target="tpu_custom_call" | custom-call | tf_op jit(solution)/shard_map/pallas_call | solution.py:612
  2.6 3.0 %collective-permute-start = (f32[64,128]{1,0:T(8,128)S(1)}, f32[64,128]{1,0:T(8,128)S(1)}, u32[]{:S(2)}, u32[]{:S(2)}) collective-permute-start(f32[64,128]{1,0:T(8,128)S(1)} %get-tuple-element.72), channel_id=1, source_target_pairs={{0,1},{1,0},{2,4},{3,5},{4,2},{5,3},{6,8},{7,9},{8,6},{9,7},{10,12... | collective-permute-start | bytes 98312 | tf_op jit(solution)/shard_map/ppermute | solution.py:635
  5.7 1.3 %collective-permute-start.2 = (f32[24,128]{1,0:T(8,128)S(1)}, f32[24,128]{1,0:T(8,128)S(1)}, u32[]{:S(2)}, u32[]{:S(2)}) collective-permute-start(f32[24,128]{1,0:T(8,128)S(1)} %get-tuple-element.74), channel_id=1, source_target_pairs={{0,2},{1,3},{2,0},{3,1},{4,6},{5,7},{6,4},{7,5},{8,10},{9,11},{10,... | collective-permute-start | bytes 36872 | tf_op jit(solution)/shard_map/ppermute | solution.py:635
  7.5 0.5 %shard_map.167 = (f32[320,128]{1,0:T(8,128)S(1)}, f32[320,128]{1,0:T(8,128)S(1)}) custom-call(f32[3,17,4,128]{3,2,1,0:T(4,128)S(1)} %get-tuple-element.62.next_ref, f32[17,4,128]{2,1,0:T(4,128)S(1)} %get-tuple-element.63.density_ref, f32[320,128]{1,0:T(8,128)S(1)} %get-tuple-element.64.mass_ref), custom_call_target="tpu_custom_call" | custom-call | tf_op jit(solution)/shard_map/pallas_call | solution.py:612
  8.0 0.5 %shard_map.168 = (f32[320,128]{1,0:T(8,128)S(1)}, f32[160,128]{1,0:T(8,128)S(1)}) custom-call(f32[320,128]{1,0:T(8,128)S(1)} %get-tuple-element.61.cur_ref.refs_0_.refs_1_, f32[8,128]{1,0:T(8,128)S(1)} %get-tuple-element.67.material_ref.refs_5_, bf16[2,640,384]{2,1,0:T(8,128)(2,1)S(1)} %get-tuple-element.68.own_ref, ...), custom_call_target="tpu_custom_call" | custom-call | tf_op jit(solution)/shard_map/pallas_call | solution.py:612
  8.5 0.8 %collective-permute-done.1.refs_7_.refs_11_.refs_4_ = f32[40,128]{1,0:T(8,128)S(1)} collective-permute-done((f32[40,128]{1,0:T(8,128)S(1)}, f32[40,128]{1,0:T(8,128)S(1)}, u32[]{:S(2)}, u32[]{:S(2)}) %collective-permute-start.1) | collective-permute-done | bytes 20512 | tf_op jit(solution)/shard_map/ppermute | solution.py:640
  9.4 0.8 %shard_map.169 = (f32[320,128]{1,0:T(8,128)S(1)}, f32[24,128]{1,0:T(8,128)S(1)}, f32[24,128]{1,0:T(8,128)S(1)}, f32[16,128]{1,0:T(8,128)S(1)}, f32[64,128]{1,0:T(8,128)S(1)}, /*index=5*/f32[28,128]{1,0:T(8,128)S(1)}) custom-call(f32[320,128]{1,0:T(8,128)S(1)} %get-tuple-element.61.cur_ref.refs_0_.refs_1_, f32[320,128]{1,0:T(8,128)S(1)} %get-tuple-element.65.refs_1_, ...), custom_call_target="tpu_custom_call" | custom-call | tf_op jit(solution)/shard_map/pallas_call | solution.py:612
  10.6 1.7 %collective-permute-start.6 = (f32[28,128]{1,0:T(8,128)S(1)}, f32[28,128]{1,0:T(8,128)S(1)}, u32[]{:S(2)}, u32[]{:S(2)}) collective-permute-start(f32[28,128]{1,0:T(8,128)S(1)} %get-tuple-element.83.refs_12_.refs_5_), channel_id=1, source_target_pairs={{1,0},{0,1},{3,2},{2,3},{5,4},{4,5},{7,6},{6,7},{9,8},{8,9},{11,10... | collective-permute-start | bytes 43016 | tf_op jit(solution)/shard_map/ppermute | solution.py:640
  12.3 0.5 %collective-permute-start.8 = (f32[24,128]{1,0:T(8,128)S(1)}, f32[24,128]{1,0:T(8,128)S(1)}, u32[]{:S(2)}, u32[]{:S(2)}) collective-permute-start(f32[24,128]{1,0:T(8,128)S(1)} %get-tuple-element.85), channel_id=1, source_target_pairs={{0,2},{1,3},{2,0},{3,1},{4,6},{5,7},{6,4},{7,5},{8,10},{9,11},{10,... | collective-permute-start | bytes 36872 | tf_op jit(solution)/shard_map/ppermute | solution.py:635
  12.8 0.5 %shard_map.170 = (f32[320,128]{1,0:T(8,128)S(1)}, f32[160,128]{1,0:T(8,128)S(1)}) custom-call(f32[320,128]{1,0:T(8,128)S(1)} %get-tuple-element.79.cur_ref._.refs_0_.refs_1_, f32[8,128]{1,0:T(8,128)S(1)} %get-tuple-element.67.material_ref.refs_5_, bf16[2,640,384]{2,1,0:T(8,128)(2,1)S(1)} %get-tuple-element.68.own_ref, ...), custom_call_target="tpu_custom_call" | custom-call | tf_op jit(solution)/shard_map/pallas_call | solution.py:612
  13.4 0.5 %collective-permute-done.9.refs_10_ = f32[16,128]{1,0:T(8,128)S(1)} collective-permute-done((f32[16,128]{1,0:T(8,128)S(1)}, f32[16,128]{1,0:T(8,128)S(1)}, u32[]{:S(2)}, u32[]{:S(2)}) %collective-permute-start.9) | collective-permute-done | bytes 8224 | tf_op jit(solution)/shard_map/ppermute | solution.py:635
  14.4 0.8 %shard_map.172 = (f32[320,128]{1,0:T(8,128)S(1)}, f32[24,128]{1,0:T(8,128)S(1)}, f32[24,128]{1,0:T(8,128)S(1)}, f32[16,128]{1,0:T(8,128)S(1)}, f32[64,128]{1,0:T(8,128)S(1)}, /*index=5*/f32[28,128]{1,0:T(8,128)S(1)}) custom-call(f32[320,128]{1,0:T(8,128)S(1)} %get-tuple-element.79.cur_ref._.refs_0_.refs_1_, ...), custom_call_target="tpu_custom_call" | custom-call | tf_op jit(solution)/shard_map/pallas_call | solution.py:612
  15.2 1.7 %collective-permute-start.10 = (f32[64,128]{1,0:T(8,128)S(1)}, f32[64,128]{1,0:T(8,128)S(1)}, u32[]{:S(2)}, u32[]{:S(2)}) collective-permute-start(f32[64,128]{1,0:T(8,128)S(1)} %get-tuple-element.94), channel_id=1, source_target_pairs={{0,1},{1,0},{2,4},{3,5},{4,2},{5,3},{6,8},{7,9},{8,6},{9,7},{10,12... | collective-permute-start | bytes 98312 | tf_op jit(solution)/shard_map/ppermute | solution.py:635
  17.8 0.5 %shard_map.173 = (f32[320,128]{1,0:T(8,128)S(1)}, f32[160,128]{1,0:T(8,128)S(1)}) custom-call(f32[320,128]{1,0:T(8,128)S(1)} %get-tuple-element.91.cur_ref.refs_0_.refs_1_, f32[8,128]{1,0:T(8,128)S(1)} %get-tuple-element.67.material_ref.refs_5_, bf16[2,640,384]{2,1,0:T(8,128)(2,1)S(1)} %get-tuple-element.68.own_ref, ...), custom_call_target="tpu_custom_call" | custom-call | tf_op jit(solution)/shard_map/pallas_call | solution.py:612
  18.3 0.7 %collective-permute-done.14.refs_10_ = f32[16,128]{1,0:T(8,128)S(1)} collective-permute-done((f32[16,128]{1,0:T(8,128)S(1)}, f32[16,128]{1,0:T(8,128)S(1)}, u32[]{:S(2)}, u32[]{:S(2)}) %collective-permute-start.14) | collective-permute-done | bytes 8224 | tf_op jit(solution)/shard_map/ppermute | solution.py:635
  18.9 1.7 %collective-permute-done.11.refs_7_.refs_8_ = f32[28,128]{1,0:T(8,128)S(1)} collective-permute-done((f32[28,128]{1,0:T(8,128)S(1)}, f32[28,128]{1,0:T(8,128)S(1)}, u32[]{:S(2)}, u32[]{:S(2)}) %collective-permute-start.11) | collective-permute-done | bytes 14368 | tf_op jit(solution)/shard_map/ppermute | solution.py:640
  20.6 0.8 %shard_map.174 = (f32[320,128]{1,0:T(8,128)S(1)}, f32[24,128]{1,0:T(8,128)S(1)}, f32[24,128]{1,0:T(8,128)S(1)}, f32[16,128]{1,0:T(8,128)S(1)}, f32[64,128]{1,0:T(8,128)S(1)}, /*index=5*/f32[28,128]{1,0:T(8,128)S(1)}) custom-call(f32[320,128]{1,0:T(8,128)S(1)} %get-tuple-element.91.cur_ref.refs_0_.refs_1_, ...), custom_call_target="tpu_custom_call" | custom-call | tf_op jit(solution)/shard_map/pallas_call | solution.py:612
  21.8 1.7 %collective-permute-start.16 = (f32[28,128]{1,0:T(8,128)S(1)}, f32[28,128]{1,0:T(8,128)S(1)}, u32[]{:S(2)}, u32[]{:S(2)}) collective-permute-start(f32[28,128]{1,0:T(8,128)S(1)} %get-tuple-element.103.refs_9_.refs_12_), channel_id=1, source_target_pairs={{1,0},{0,1},{3,2},{2,3},{5,4},{4,5},{7,6},{6,7},{9,8},{8,9},{11,10... | collective-permute-start | bytes 43016 | tf_op jit(solution)/shard_map/ppermute | solution.py:640
  23.5 0.5 %collective-permute-start.18 = (f32[24,128]{1,0:T(8,128)S(1)}, f32[24,128]{1,0:T(8,128)S(1)}, u32[]{:S(2)}, u32[]{:S(2)}) collective-permute-start(f32[24,128]{1,0:T(8,128)S(1)} %get-tuple-element.105), channel_id=1, source_target_pairs={{0,2},{1,3},{2,0},{3,1},{4,6},{5,7},{6,4},{7,5},{8,10},{9,11},{10,... | collective-permute-start | bytes 36872 | tf_op jit(solution)/shard_map/ppermute | solution.py:635
  24.0 0.5 %shard_map.175 = (f32[320,128]{1,0:T(8,128)S(1)}, f32[160,128]{1,0:T(8,128)S(1)}) custom-call(f32[320,128]{1,0:T(8,128)S(1)} %get-tuple-element.99.cur_ref.refs_0_, f32[8,128]{1,0:T(8,128)S(1)} %get-tuple-element.67.material_ref.refs_5_, bf16[2,640,384]{2,1,0:T(8,128)(2,1)S(1)} %get-tuple-element.68.own_ref, bf16[160,256]{1,0:T(8,128)(2,1)S(1)} %get-tuple-element.69.touch_ref), custom_call_target="tpu_custom_call" | custom-call | tf_op jit(solution)/shard_map/pallas_call | solution.py:612
  25.7 1.7 %collective-permute-start.20 = (f32[2,128]{1,0:T(2,128)S(1)}, f32[2,128]{1,0:T(2,128)S(1)}, u32[]{:S(2)}, u32[]{:S(2)}) collective-permute-start(f32[2,128]{1,0:T(2,128)S(1)} %get-tuple-element.115), channel_id=1, source_target_pairs={{0,1},{1,0},{2,3},{3,2},{4,8},{5,9},{6,10},{7,11},{8,4},{9,5},{10,... | collective-permute-start | bytes 3080 | tf_op jit(solution)/shard_map/ppermute | solution.py:635
  28.2 0.8 %collective-permute-start.23 = (f32[2,128]{1,0:T(2,128)S(1)}, f32[2,128]{1,0:T(2,128)S(1)}, u32[]{:S(2)}, u32[]{:S(2)}) collective-permute-start(f32[2,128]{1,0:T(2,128)S(1)} %get-tuple-element.118), channel_id=1, source_target_pairs={{0,2},{1,3},{2,0},{3,1},{4,6},{5,7},{6,4},{7,5},{8,10},{9,11},{10,... | collective-permute-start | bytes 3080 | tf_op jit(solution)/shard_map/ppermute | solution.py:635
  29.0 1.4 %shard_map.178 = (f32[3,17,4,128]{3,2,1,0:T(4,128)}, f32[3,17,4,128]{3,2,1,0:T(4,128)}) custom-call(f32[320,128]{1,0:T(8,128)S(1)} %get-tuple-element.99.cur_ref.refs_0_, f32[320,128]{1,0:T(8,128)S(1)} %get-tuple-element.91.cur_ref.refs_0_.refs_1_, f32[320,128]{1,0:T(8,128)S(1)} %get-tuple-element.66.refs_2_, f32[320,128]{1,0:T(8,128)S(1)} %get-tuple-element.100.refs_3_, ...), custom_call_target="tpu_custom_call" | custom-call | tf_op jit(solution)/shard_map/pallas_call | solution.py:612
  31.3 0.6 %shard_map.179 = f32[2,128]{1,0:T(2,128)} custom-call(f32[2,128]{1,0:T(2,128)S(1)} %get-tuple-element.111.refs_16_.refs_0_, f32[2,128]{1,0:T(2,128)S(1)} %collective-permute-done.20.refs_1_, f32[2,128]{1,0:T(2,128)S(1)} %collective-permute-done.21.refs_2_, f32[2,128]{1,0:T(2,128)S(1)} %collective-permute-done.22.refs_3_, ...), custom_call_target="tpu_custom_call" | custom-call | tf_op jit(solution)/shard_map/pallas_call | solution.py:612
  (38 shorter events, 5.7 us)
Async XLA Ops:
  2.6 6.8 %collective-permute-start = (f32[64,128]{1,0:T(8,128)S(1)}, f32[64,128]{1,0:T(8,128)S(1)}, u32[]{:S(2)}, u32[]{:S(2)}) collective-permute-start(f32[64,128]{1,0:T(8,128)S(1)} %get-tuple-element.72), channel_id=1, source_target_pairs={{0,1},{1,0},{2,4},{3,5},{4,2},{5,3},{6,8},{7,9},{8,6},{9,7},{10,12... | collective-permute-start | bytes 98312 | tf_op jit(solution)/shard_map/ppermute | solution.py:635
  5.6 3.8 %collective-permute-start.1 = (f32[40,128]{1,0:T(8,128)S(1)}, f32[40,128]{1,0:T(8,128)S(1)}, u32[]{:S(2)}, u32[]{:S(2)}) collective-permute-start(f32[40,128]{1,0:T(8,128)S(1)} %get-tuple-element.73.refs_12_.refs_13_.refs_3_), channel_id=1, source_target_pairs={{1,0},{0,1},{3,2},{2,3},{5,4},{4,5},{7,6},{6,7},{9,8},{8,9},{11,10... | collective-permute-start | bytes 61448 | tf_op jit(solution)/shard_map/ppermute | solution.py:640
  5.7 2.8 %collective-permute-start.2 = (f32[24,128]{1,0:T(8,128)S(1)}, f32[24,128]{1,0:T(8,128)S(1)}, u32[]{:S(2)}, u32[]{:S(2)}) collective-permute-start(f32[24,128]{1,0:T(8,128)S(1)} %get-tuple-element.74), channel_id=1, source_target_pairs={{0,2},{1,3},{2,0},{3,1},{4,6},{5,7},{6,4},{7,5},{8,10},{9,11},{10,... | collective-permute-start | bytes 36872 | tf_op jit(solution)/shard_map/ppermute | solution.py:635
  7.0 1.6 %collective-permute-start.3 = (f32[24,128]{1,0:T(8,128)S(1)}, f32[24,128]{1,0:T(8,128)S(1)}, u32[]{:S(2)}, u32[]{:S(2)}) collective-permute-start(f32[24,128]{1,0:T(8,128)S(1)} %get-tuple-element.75), channel_id=1, source_target_pairs={{0,2},{1,3},{2,0},{3,1},{4,6},{5,7},{6,4},{7,5},{8,10},{9,11},{10,... | collective-permute-start | bytes 36872 | tf_op jit(solution)/shard_map/ppermute | solution.py:635
  7.0 1.5 %collective-permute-start.4 = (f32[16,128]{1,0:T(8,128)S(1)}, f32[16,128]{1,0:T(8,128)S(1)}, u32[]{:S(2)}, u32[]{:S(2)}) collective-permute-start(f32[16,128]{1,0:T(8,128)S(1)} %get-tuple-element.76), channel_id=1, source_target_pairs={{0,2},{1,3},{2,0},{3,1},{4,6},{5,7},{6,4},{7,5},{8,10},{9,11},{10,... | collective-permute-start | bytes 24584 | tf_op jit(solution)/shard_map/ppermute | solution.py:635
  10.2 4.1 %collective-permute-start.5 = (f32[64,128]{1,0:T(8,128)S(1)}, f32[64,128]{1,0:T(8,128)S(1)}, u32[]{:S(2)}, u32[]{:S(2)}) collective-permute-start(f32[64,128]{1,0:T(8,128)S(1)} %get-tuple-element.82), channel_id=1, source_target_pairs={{0,1},{1,0},{2,4},{3,5},{4,2},{5,3},{6,8},{7,9},{8,6},{9,7},{10,12... | collective-permute-start | bytes 98312 | tf_op jit(solution)/shard_map/ppermute | solution.py:635
  10.6 3.8 %collective-permute-start.6 = (f32[28,128]{1,0:T(8,128)S(1)}, f32[28,128]{1,0:T(8,128)S(1)}, u32[]{:S(2)}, u32[]{:S(2)}) collective-permute-start(f32[28,128]{1,0:T(8,128)S(1)} %get-tuple-element.83.refs_12_.refs_5_), channel_id=1, source_target_pairs={{1,0},{0,1},{3,2},{2,3},{5,4},{4,5},{7,6},{6,7},{9,8},{8,9},{11,10... | collective-permute-start | bytes 43016 | tf_op jit(solution)/shard_map/ppermute | solution.py:640
  12.3 1.7 %collective-permute-start.7 = (f32[24,128]{1,0:T(8,128)S(1)}, f32[24,128]{1,0:T(8,128)S(1)}, u32[]{:S(2)}, u32[]{:S(2)}) collective-permute-start(f32[24,128]{1,0:T(8,128)S(1)} %get-tuple-element.84), channel_id=1, source_target_pairs={{0,2},{1,3},{2,0},{3,1},{4,6},{5,7},{6,4},{7,5},{8,10},{9,11},{10,... | collective-permute-start | bytes 36872 | tf_op jit(solution)/shard_map/ppermute | solution.py:635
  12.3 1.7 %collective-permute-start.8 = (f32[24,128]{1,0:T(8,128)S(1)}, f32[24,128]{1,0:T(8,128)S(1)}, u32[]{:S(2)}, u32[]{:S(2)}) collective-permute-start(f32[24,128]{1,0:T(8,128)S(1)} %get-tuple-element.85), channel_id=1, source_target_pairs={{0,2},{1,3},{2,0},{3,1},{4,6},{5,7},{6,4},{7,5},{8,10},{9,11},{10,... | collective-permute-start | bytes 36872 | tf_op jit(solution)/shard_map/ppermute | solution.py:635
  12.8 1.2 %collective-permute-start.9 = (f32[16,128]{1,0:T(8,128)S(1)}, f32[16,128]{1,0:T(8,128)S(1)}, u32[]{:S(2)}, u32[]{:S(2)}) collective-permute-start(f32[16,128]{1,0:T(8,128)S(1)} %get-tuple-element.86), channel_id=1, source_target_pairs={{0,2},{1,3},{2,0},{3,1},{4,6},{5,7},{6,4},{7,5},{8,10},{9,11},{10,... | collective-permute-start | bytes 24584 | tf_op jit(solution)/shard_map/ppermute | solution.py:635
  15.2 5.4 %collective-permute-start.10 = (f32[64,128]{1,0:T(8,128)S(1)}, f32[64,128]{1,0:T(8,128)S(1)}, u32[]{:S(2)}, u32[]{:S(2)}) collective-permute-start(f32[64,128]{1,0:T(8,128)S(1)} %get-tuple-element.94), channel_id=1, source_target_pairs={{0,1},{1,0},{2,4},{3,5},{4,2},{5,3},{6,8},{7,9},{8,6},{9,7},{10,12... | collective-permute-start | bytes 98312 | tf_op jit(solution)/shard_map/ppermute | solution.py:635
  16.9 3.7 %collective-permute-start.11 = (f32[28,128]{1,0:T(8,128)S(1)}, f32[28,128]{1,0:T(8,128)S(1)}, u32[]{:S(2)}, u32[]{:S(2)}) collective-permute-start(f32[28,128]{1,0:T(8,128)S(1)} %get-tuple-element.95.refs_12_.refs_7_), channel_id=1, source_target_pairs={{1,0},{0,1},{3,2},{2,3},{5,4},{4,5},{7,6},{6,7},{9,8},{8,9},{11,10... | collective-permute-start | bytes 43016 | tf_op jit(solution)/shard_map/ppermute | solution.py:640
  17.3 1.7 %collective-permute-start.12 = (f32[24,128]{1,0:T(8,128)S(1)}, f32[24,128]{1,0:T(8,128)S(1)}, u32[]{:S(2)}, u32[]{:S(2)}) collective-permute-start(f32[24,128]{1,0:T(8,128)S(1)} %get-tuple-element.96), channel_id=1, source_target_pairs={{0,2},{1,3},{2,0},{3,1},{4,6},{5,7},{6,4},{7,5},{8,10},{9,11},{10,... | collective-permute-start | bytes 36872 | tf_op jit(solution)/shard_map/ppermute | solution.py:635
  17.3 1.7 %collective-permute-start.13 = (f32[24,128]{1,0:T(8,128)S(1)}, f32[24,128]{1,0:T(8,128)S(1)}, u32[]{:S(2)}, u32[]{:S(2)}) collective-permute-start(f32[24,128]{1,0:T(8,128)S(1)} %get-tuple-element.97), channel_id=1, source_target_pairs={{0,2},{1,3},{2,0},{3,1},{4,6},{5,7},{6,4},{7,5},{8,10},{9,11},{10,... | collective-permute-start | bytes 36872 | tf_op jit(solution)/shard_map/ppermute | solution.py:635
  17.8 1.2 %collective-permute-start.14 = (f32[16,128]{1,0:T(8,128)S(1)}, f32[16,128]{1,0:T(8,128)S(1)}, u32[]{:S(2)}, u32[]{:S(2)}) collective-permute-start(f32[16,128]{1,0:T(8,128)S(1)} %get-tuple-element.98), channel_id=1, source_target_pairs={{0,2},{1,3},{2,0},{3,1},{4,6},{5,7},{6,4},{7,5},{8,10},{9,11},{10,... | collective-permute-start | bytes 24584 | tf_op jit(solution)/shard_map/ppermute | solution.py:635
  21.5 4.1 %collective-permute-start.15 = (f32[64,128]{1,0:T(8,128)S(1)}, f32[64,128]{1,0:T(8,128)S(1)}, u32[]{:S(2)}, u32[]{:S(2)}) collective-permute-start(f32[64,128]{1,0:T(8,128)S(1)} %get-tuple-element.102), channel_id=1, source_target_pairs={{0,1},{1,0},{2,4},{3,5},{4,2},{5,3},{6,8},{7,9},{8,6},{9,7},{10,12... | collective-permute-start | bytes 98312 | tf_op jit(solution)/shard_map/ppermute | solution.py:635
  21.8 3.7 %collective-permute-start.16 = (f32[28,128]{1,0:T(8,128)S(1)}, f32[28,128]{1,0:T(8,128)S(1)}, u32[]{:S(2)}, u32[]{:S(2)}) collective-permute-start(f32[28,128]{1,0:T(8,128)S(1)} %get-tuple-element.103.refs_9_.refs_12_), channel_id=1, source_target_pairs={{1,0},{0,1},{3,2},{2,3},{5,4},{4,5},{7,6},{6,7},{9,8},{8,9},{11,10... | collective-permute-start | bytes 43016 | tf_op jit(solution)/shard_map/ppermute | solution.py:640
  23.5 1.7 %collective-permute-start.17 = (f32[24,128]{1,0:T(8,128)S(1)}, f32[24,128]{1,0:T(8,128)S(1)}, u32[]{:S(2)}, u32[]{:S(2)}) collective-permute-start(f32[24,128]{1,0:T(8,128)S(1)} %get-tuple-element.104), channel_id=1, source_target_pairs={{0,2},{1,3},{2,0},{3,1},{4,6},{5,7},{6,4},{7,5},{8,10},{9,11},{10,... | collective-permute-start | bytes 36872 | tf_op jit(solution)/shard_map/ppermute | solution.py:635
  23.5 1.7 %collective-permute-start.18 = (f32[24,128]{1,0:T(8,128)S(1)}, f32[24,128]{1,0:T(8,128)S(1)}, u32[]{:S(2)}, u32[]{:S(2)}) collective-permute-start(f32[24,128]{1,0:T(8,128)S(1)} %get-tuple-element.105), channel_id=1, source_target_pairs={{0,2},{1,3},{2,0},{3,1},{4,6},{5,7},{6,4},{7,5},{8,10},{9,11},{10,... | collective-permute-start | bytes 36872 | tf_op jit(solution)/shard_map/ppermute | solution.py:635
  24.0 1.2 %collective-permute-start.19 = (f32[16,128]{1,0:T(8,128)S(1)}, f32[16,128]{1,0:T(8,128)S(1)}, u32[]{:S(2)}, u32[]{:S(2)}) collective-permute-start(f32[16,128]{1,0:T(8,128)S(1)} %get-tuple-element.106), channel_id=1, source_target_pairs={{0,2},{1,3},{2,0},{3,1},{4,6},{5,7},{6,4},{7,5},{8,10},{9,11},{10,... | collective-permute-start | bytes 24584 | tf_op jit(solution)/shard_map/ppermute | solution.py:635
  25.7 4.7 %collective-permute-start.20 = (f32[2,128]{1,0:T(2,128)S(1)}, f32[2,128]{1,0:T(2,128)S(1)}, u32[]{:S(2)}, u32[]{:S(2)}) collective-permute-start(f32[2,128]{1,0:T(2,128)S(1)} %get-tuple-element.115), channel_id=1, source_target_pairs={{0,1},{1,0},{2,3},{3,2},{4,8},{5,9},{6,10},{7,11},{8,4},{9,5},{10,... | collective-permute-start | bytes 3080 | tf_op jit(solution)/shard_map/ppermute | solution.py:635
  27.4 3.6 %collective-permute-start.21 = (f32[2,128]{1,0:T(2,128)S(1)}, f32[2,128]{1,0:T(2,128)S(1)}, u32[]{:S(2)}, u32[]{:S(2)}) collective-permute-start(f32[2,128]{1,0:T(2,128)S(1)} %get-tuple-element.116), channel_id=1, source_target_pairs={{0,1},{1,0},{2,4},{3,5},{4,2},{5,3},{6,8},{7,9},{8,6},{9,7},{10,12... | collective-permute-start | bytes 3080 | tf_op jit(solution)/shard_map/ppermute | solution.py:635
  27.8 3.6 %collective-permute-start.22 = (f32[2,128]{1,0:T(2,128)S(1)}, f32[2,128]{1,0:T(2,128)S(1)}, u32[]{:S(2)}, u32[]{:S(2)}) collective-permute-start(f32[2,128]{1,0:T(2,128)S(1)} %get-tuple-element.117), channel_id=1, source_target_pairs={{0,4},{1,5},{2,6},{3,7},{4,0},{5,1},{6,2},{7,3},{8,12},{9,13},{10,... | collective-permute-start | bytes 3080 | tf_op jit(solution)/shard_map/ppermute | solution.py:635
  28.2 3.1 %collective-permute-start.23 = (f32[2,128]{1,0:T(2,128)S(1)}, f32[2,128]{1,0:T(2,128)S(1)}, u32[]{:S(2)}, u32[]{:S(2)}) collective-permute-start(f32[2,128]{1,0:T(2,128)S(1)} %get-tuple-element.118), channel_id=1, source_target_pairs={{0,2},{1,3},{2,0},{3,1},{4,6},{5,7},{6,4},{7,5},{8,10},{9,11},{10,... | collective-permute-start | bytes 3080 | tf_op jit(solution)/shard_map/ppermute | solution.py:635

commit v17 on v16

--- a/solution.py
+++ b/solution.py
@@ -630,8 +630,12 @@
     route = []
     for i in range(size):
         for j in range(across):
-            side = j if i in partner else min(j ^ 1, across - 1)
-            route.append((i * across + j, partner.get(i, i) * across + side))
+            other, side = partner.get(i, i), j
+            if i not in partner and i ^ 1 < size and i ^ 1 not in partner:
+                other = i ^ 1
+            elif i not in partner:
+                side = min(j ^ 1, across - 1)
+            route.append((i * across + j, other * across + side))
     return lax.ppermute(block, ("dom", "depth"), route)
 
 
@@ -760,7 +764,7 @@
                 steps=steps,
             )
             shares = [sums[0]]
-            for i, distance, group in ((4, 2, 1), (2, 1, 1), (3, 2, 0), (1, 1, 0)):
+            for i, distance, group in ((3, 2, 0), (2, 1, 1), (4, 2, 1), (1, 1, 0)):
                 shares.append(swapped(sums[i], distance, group))
             patch_sums = kernel_call(sum_kernel, [(PATCH_DEV, lanes)], shares)[0]
             earlier, later = kernel_call(

time: 32.1 us -> 30.6 us (0.953)
  starting transfers between devices: 15.8 us -> 14.7 us
  waiting for transfers between devices: 5.72 us -> 5.28 us
    ppermute x20, starting transfers between devices: 12 us -> 11 us  [swapped(): return lax.ppermute(block, ('dom', 'depth'), route)]
    ppermute x20, waiting for transfers between devices: 2.4 us -> 1.96 us  [swapped(): return lax.ppermute(block, ('dom', 'depth'), route)]
  transfers between devices with their start and end apart: 24 -> 24, of which waited for: 9 -> 8; matrix products, arithmetic and copies ran while one was open for 0% -> 0% of each run, Pallas kernels for 14% -> 15%
where the time goes in v17:
time: 30.6 us; the launch traced here: 30.4 us
  starting transfers between devices  14.7 us (48%)
  Pallas kernels  9.64 us (32%)
  waiting for transfers between devices  5.28 us (17%)
  between operations  0.74 us (2%)
    ppermute x20, starting transfers between devices, swapped(): return lax.ppermute(block, ('dom', 'depth'), route)  11 us
    pallas_call x14, Pallas kernels, kernel_call(): pl.pallas_call(functools.partial(body, **static) if static else body, out...  9.64 us
    ppermute x4, starting transfers between devices, from_behind(): lax.ppermute(block, axis, [((i - distance) % size, i) for i in range(size)])  3.78 us
    ppermute x4, waiting for transfers between devices, from_behind(): lax.ppermute(block, axis, [((i - distance) % size, i) for i in range(size)])  3.31 us
    ppermute x20, waiting for transfers between devices, swapped(): return lax.ppermute(block, ('dom', 'depth'), route)  1.96 us
  transfers between devices with their start and end apart: 24, of which 8 were waited for; matrix products, arithmetic and copies ran while one was open for 0% of the time, Pallas kernels for 15%

profile of v17, /device:TPU:0, one launch (start us, length us, event | category | flops | bytes accessed | tf_op | source)
XLA Modules:
  0.0 30.4 jit_solution(13777102634379957628)
XLA Ops:
  0.6 2.0 %shard_map.166 = (f32[320,128]{1,0:T(8,128)S(1)}, f32[24,128]{1,0:T(8,128)S(1)}, f32[24,128]{1,0:T(8,128)S(1)}, f32[16,128]{1,0:T(8,128)S(1)}, f32[64,128]{1,0:T...) custom-call(f32[3,17,4,128]{3,2,1,0:T(4,128)} %bitcast.11, ...), custom_call_target="tpu_custom_call" | custom-call | tf_op jit(solution)/shard_map/pallas_call | solution.py:612
  2.6 3.0 %collective-permute-start = (f32[64,128]{1,0:T(8,128)S(1)}, f32[64,128]{1,0:T(8,128)S(1)}, u32[]{:S(2)}, u32[]{:S(2)}) collective-permute-start(f32[64,128]{1,0:T(8,128)S(1)} %get-tuple-element.72), channel_id=1, source_target_pairs={{0,1},{1,0},{2,4},{3,5},{4,2},{5,3},{6,8},{7,9},{8,6},{9,7},{10,12... | collective-permute-start | bytes 98312 | tf_op jit(solution)/shard_map/ppermute | solution.py:639
  5.7 1.3 %collective-permute-start.2 = (f32[24,128]{1,0:T(8,128)S(1)}, f32[24,128]{1,0:T(8,128)S(1)}, u32[]{:S(2)}, u32[]{:S(2)}) collective-permute-start(f32[24,128]{1,0:T(8,128)S(1)} %get-tuple-element.74), channel_id=1, source_target_pairs={{0,2},{1,3},{2,0},{3,1},{4,6},{5,7},{6,4},{7,5},{8,10},{9,11},{10,... | collective-permute-start | bytes 36872 | tf_op jit(solution)/shard_map/ppermute | solution.py:639
  7.0 0.5 %collective-permute-start.4 = (f32[16,128]{1,0:T(8,128)S(1)}, f32[16,128]{1,0:T(8,128)S(1)}, u32[]{:S(2)}, u32[]{:S(2)}) collective-permute-start(f32[16,128]{1,0:T(8,128)S(1)} %get-tuple-element.76), channel_id=1, source_target_pairs={{0,2},{1,3},{2,0},{3,1},{4,6},{5,7},{6,4},{7,5},{8,10},{9,11},{10,... | collective-permute-start | bytes 24584 | tf_op jit(solution)/shard_map/ppermute | solution.py:639
  7.5 0.5 %shard_map.167 = (f32[320,128]{1,0:T(8,128)S(1)}, f32[320,128]{1,0:T(8,128)S(1)}) custom-call(f32[3,17,4,128]{3,2,1,0:T(4,128)S(1)} %get-tuple-element.62.next_ref, f32[17,4,128]{2,1,0:T(4,128)S(1)} %get-tuple-element.63.density_ref, f32[320,128]{1,0:T(8,128)S(1)} %get-tuple-element.64.mass_ref), custom_call_target="tpu_custom_call" | custom-call | tf_op jit(solution)/shard_map/pallas_call | solution.py:612
  8.0 0.5 %shard_map.168 = (f32[320,128]{1,0:T(8,128)S(1)}, f32[160,128]{1,0:T(8,128)S(1)}) custom-call(f32[320,128]{1,0:T(8,128)S(1)} %get-tuple-element.61.cur_ref.refs_0_.refs_1_, f32[8,128]{1,0:T(8,128)S(1)} %get-tuple-element.67.material_ref.refs_5_, bf16[2,640,384]{2,1,0:T(8,128)(2,1)S(1)} %get-tuple-element.68.own_ref, ...), custom_call_target="tpu_custom_call" | custom-call | tf_op jit(solution)/shard_map/pallas_call | solution.py:612
  8.5 0.8 %collective-permute-done.1.refs_7_.refs_11_.refs_4_ = f32[40,128]{1,0:T(8,128)S(1)} collective-permute-done((f32[40,128]{1,0:T(8,128)S(1)}, f32[40,128]{1,0:T(8,128)S(1)}, u32[]{:S(2)}, u32[]{:S(2)}) %collective-permute-start.1) | collective-permute-done | bytes 20512 | tf_op jit(solution)/shard_map/ppermute | solution.py:644
  9.4 0.8 %shard_map.169 = (f32[320,128]{1,0:T(8,128)S(1)}, f32[24,128]{1,0:T(8,128)S(1)}, f32[24,128]{1,0:T(8,128)S(1)}, f32[16,128]{1,0:T(8,128)S(1)}, f32[64,128]{1,0:T(8,128)S(1)}, /*index=5*/f32[28,128]{1,0:T(8,128)S(1)}) custom-call(f32[320,128]{1,0:T(8,128)S(1)} %get-tuple-element.61.cur_ref.refs_0_.refs_1_, f32[320,128]{1,0:T(8,128)S(1)} %get-tuple-element.65.refs_1_, ...), custom_call_target="tpu_custom_call" | custom-call | tf_op jit(solution)/shard_map/pallas_call | solution.py:612
  10.6 1.7 %collective-permute-start.6 = (f32[28,128]{1,0:T(8,128)S(1)}, f32[28,128]{1,0:T(8,128)S(1)}, u32[]{:S(2)}, u32[]{:S(2)}) collective-permute-start(f32[28,128]{1,0:T(8,128)S(1)} %get-tuple-element.83.refs_12_.refs_5_), channel_id=1, source_target_pairs={{1,0},{0,1},{3,2},{2,3},{5,4},{4,5},{7,6},{6,7},{9,8},{8,9},{11,10... | collective-permute-start | bytes 43016 | tf_op jit(solution)/shard_map/ppermute | solution.py:644
  12.8 0.5 %shard_map.170 = (f32[320,128]{1,0:T(8,128)S(1)}, f32[160,128]{1,0:T(8,128)S(1)}) custom-call(f32[320,128]{1,0:T(8,128)S(1)} %get-tuple-element.79.cur_ref._.refs_0_.refs_1_, f32[8,128]{1,0:T(8,128)S(1)} %get-tuple-element.67.material_ref.refs_5_, bf16[2,640,384]{2,1,0:T(8,128)(2,1)S(1)} %get-tuple-element.68.own_ref, ...), custom_call_target="tpu_custom_call" | custom-call | tf_op jit(solution)/shard_map/pallas_call | solution.py:612
  13.4 0.5 %collective-permute-done.9.refs_10_ = f32[16,128]{1,0:T(8,128)S(1)} collective-permute-done((f32[16,128]{1,0:T(8,128)S(1)}, f32[16,128]{1,0:T(8,128)S(1)}, u32[]{:S(2)}, u32[]{:S(2)}) %collective-permute-start.9) | collective-permute-done | bytes 8224 | tf_op jit(solution)/shard_map/ppermute | solution.py:639
  14.4 0.8 %shard_map.172 = (f32[320,128]{1,0:T(8,128)S(1)}, f32[24,128]{1,0:T(8,128)S(1)}, f32[24,128]{1,0:T(8,128)S(1)}, f32[16,128]{1,0:T(8,128)S(1)}, f32[64,128]{1,0:T(8,128)S(1)}, /*index=5*/f32[28,128]{1,0:T(8,128)S(1)}) custom-call(f32[320,128]{1,0:T(8,128)S(1)} %get-tuple-element.79.cur_ref._.refs_0_.refs_1_, ...), custom_call_target="tpu_custom_call" | custom-call | tf_op jit(solution)/shard_map/pallas_call | solution.py:612
  15.2 1.7 %collective-permute-start.10 = (f32[64,128]{1,0:T(8,128)S(1)}, f32[64,128]{1,0:T(8,128)S(1)}, u32[]{:S(2)}, u32[]{:S(2)}) collective-permute-start(f32[64,128]{1,0:T(8,128)S(1)} %get-tuple-element.94), channel_id=1, source_target_pairs={{0,1},{1,0},{2,4},{3,5},{4,2},{5,3},{6,8},{7,9},{8,6},{9,7},{10,12... | collective-permute-start | bytes 98312 | tf_op jit(solution)/shard_map/ppermute | solution.py:639
  17.3 0.5 %collective-permute-start.13 = (f32[24,128]{1,0:T(8,128)S(1)}, f32[24,128]{1,0:T(8,128)S(1)}, u32[]{:S(2)}, u32[]{:S(2)}) collective-permute-start(f32[24,128]{1,0:T(8,128)S(1)} %get-tuple-element.97), channel_id=1, source_target_pairs={{0,2},{1,3},{2,0},{3,1},{4,6},{5,7},{6,4},{7,5},{8,10},{9,11},{10,... | collective-permute-start | bytes 36872 | tf_op jit(solution)/shard_map/ppermute | solution.py:639
  17.8 0.5 %shard_map.173 = (f32[320,128]{1,0:T(8,128)S(1)}, f32[160,128]{1,0:T(8,128)S(1)}) custom-call(f32[320,128]{1,0:T(8,128)S(1)} %get-tuple-element.91.cur_ref.refs_0_.refs_1_, f32[8,128]{1,0:T(8,128)S(1)} %get-tuple-element.67.material_ref.refs_5_, bf16[2,640,384]{2,1,0:T(8,128)(2,1)S(1)} %get-tuple-element.68.own_ref, ...), custom_call_target="tpu_custom_call" | custom-call | tf_op jit(solution)/shard_map/pallas_call | solution.py:612
  18.3 0.7 %collective-permute-done.14.refs_10_ = f32[16,128]{1,0:T(8,128)S(1)} collective-permute-done((f32[16,128]{1,0:T(8,128)S(1)}, f32[16,128]{1,0:T(8,128)S(1)}, u32[]{:S(2)}, u32[]{:S(2)}) %collective-permute-start.14) | collective-permute-done | bytes 8224 | tf_op jit(solution)/shard_map/ppermute | solution.py:639
  18.9 1.7 %collective-permute-done.11.refs_7_.refs_8_ = f32[28,128]{1,0:T(8,128)S(1)} collective-permute-done((f32[28,128]{1,0:T(8,128)S(1)}, f32[28,128]{1,0:T(8,128)S(1)}, u32[]{:S(2)}, u32[]{:S(2)}) %collective-permute-start.11) | collective-permute-done | bytes 14368 | tf_op jit(solution)/shard_map/ppermute | solution.py:644
  20.6 0.8 %shard_map.174 = (f32[320,128]{1,0:T(8,128)S(1)}, f32[24,128]{1,0:T(8,128)S(1)}, f32[24,128]{1,0:T(8,128)S(1)}, f32[16,128]{1,0:T(8,128)S(1)}, f32[64,128]{1,0:T(8,128)S(1)}, /*index=5*/f32[28,128]{1,0:T(8,128)S(1)}) custom-call(f32[320,128]{1,0:T(8,128)S(1)} %get-tuple-element.91.cur_ref.refs_0_.refs_1_, ...), custom_call_target="tpu_custom_call" | custom-call | tf_op jit(solution)/shard_map/pallas_call | solution.py:612
  21.8 1.7 %collective-permute-start.16 = (f32[28,128]{1,0:T(8,128)S(1)}, f32[28,128]{1,0:T(8,128)S(1)}, u32[]{:S(2)}, u32[]{:S(2)}) collective-permute-start(f32[28,128]{1,0:T(8,128)S(1)} %get-tuple-element.103.refs_9_.refs_12_), channel_id=1, source_target_pairs={{1,0},{0,1},{3,2},{2,3},{5,4},{4,5},{7,6},{6,7},{9,8},{8,9},{11,10... | collective-permute-start | bytes 43016 | tf_op jit(solution)/shard_map/ppermute | solution.py:644
  24.0 0.5 %shard_map.175 = (f32[320,128]{1,0:T(8,128)S(1)}, f32[160,128]{1,0:T(8,128)S(1)}) custom-call(f32[320,128]{1,0:T(8,128)S(1)} %get-tuple-element.99.cur_ref.refs_0_, f32[8,128]{1,0:T(8,128)S(1)} %get-tuple-element.67.material_ref.refs_5_, bf16[2,640,384]{2,1,0:T(8,128)(2,1)S(1)} %get-tuple-element.68.own_ref, bf16[160,256]{1,0:T(8,128)(2,1)S(1)} %get-tuple-element.69.touch_ref), custom_call_target="tpu_custom_call" | custom-call | tf_op jit(solution)/shard_map/pallas_call | solution.py:612
  25.7 0.5 %collective-permute-start.20 = (f32[2,128]{1,0:T(2,128)S(1)}, f32[2,128]{1,0:T(2,128)S(1)}, u32[]{:S(2)}, u32[]{:S(2)}) collective-permute-start(f32[2,128]{1,0:T(2,128)S(1)} %get-tuple-element.115), channel_id=1, source_target_pairs={{0,4},{1,5},{2,6},{3,7},{4,0},{5,1},{6,2},{7,3},{8,12},{9,13},{10,... | collective-permute-start | bytes 3080 | tf_op jit(solution)/shard_map/ppermute | solution.py:639
  26.3 1.2 %collective-permute-start.21 = (f32[2,128]{1,0:T(2,128)S(1)}, f32[2,128]{1,0:T(2,128)S(1)}, u32[]{:S(2)}, u32[]{:S(2)}) collective-permute-start(f32[2,128]{1,0:T(2,128)S(1)} %get-tuple-element.116), channel_id=1, source_target_pairs={{0,1},{1,0},{2,4},{3,5},{4,2},{5,3},{6,8},{7,9},{8,6},{9,7},{10,12... | collective-permute-start | bytes 3080 | tf_op jit(solution)/shard_map/ppermute | solution.py:639
  27.9 1.4 %shard_map.178 = (f32[3,17,4,128]{3,2,1,0:T(4,128)}, f32[3,17,4,128]{3,2,1,0:T(4,128)}) custom-call(f32[320,128]{1,0:T(8,128)S(1)} %get-tuple-element.99.cur_ref.refs_0_, f32[320,128]{1,0:T(8,128)S(1)} %get-tuple-element.91.cur_ref.refs_0_.refs_1_, f32[320,128]{1,0:T(8,128)S(1)} %get-tuple-element.66.refs_2_, f32[320,128]{1,0:T(8,128)S(1)} %get-tuple-element.100.refs_3_, ...), custom_call_target="tpu_custom_call" | custom-call | tf_op jit(solution)/shard_map/pallas_call | solution.py:612
  29.8 0.6 %shard_map.179 = f32[2,128]{1,0:T(2,128)} custom-call(f32[2,128]{1,0:T(2,128)S(1)} %get-tuple-element.111.refs_16_.refs_0_, f32[2,128]{1,0:T(2,128)S(1)} %collective-permute-done.20.refs_1_, f32[2,128]{1,0:T(2,128)S(1)} %collective-permute-done.21.refs_2_, f32[2,128]{1,0:T(2,128)S(1)} %collective-permute-done.22.refs_3_, ...), custom_call_target="tpu_custom_call" | custom-call | tf_op jit(solution)/shard_map/pallas_call | solution.py:612
  (38 shorter events, 4.9 us)
Async XLA Ops:
  2.6 6.8 %collective-permute-start = (f32[64,128]{1,0:T(8,128)S(1)}, f32[64,128]{1,0:T(8,128)S(1)}, u32[]{:S(2)}, u32[]{:S(2)}) collective-permute-start(f32[64,128]{1,0:T(8,128)S(1)} %get-tuple-element.72), channel_id=1, source_target_pairs={{0,1},{1,0},{2,4},{3,5},{4,2},{5,3},{6,8},{7,9},{8,6},{9,7},{10,12... | collective-permute-start | bytes 98312 | tf_op jit(solution)/shard_map/ppermute | solution.py:639
  5.6 3.8 %collective-permute-start.1 = (f32[40,128]{1,0:T(8,128)S(1)}, f32[40,128]{1,0:T(8,128)S(1)}, u32[]{:S(2)}, u32[]{:S(2)}) collective-permute-start(f32[40,128]{1,0:T(8,128)S(1)} %get-tuple-element.73.refs_12_.refs_13_.refs_3_), channel_id=1, source_target_pairs={{1,0},{0,1},{3,2},{2,3},{5,4},{4,5},{7,6},{6,7},{9,8},{8,9},{11,10... | collective-permute-start | bytes 61448 | tf_op jit(solution)/shard_map/ppermute | solution.py:644
  5.7 2.8 %collective-permute-start.2 = (f32[24,128]{1,0:T(8,128)S(1)}, f32[24,128]{1,0:T(8,128)S(1)}, u32[]{:S(2)}, u32[]{:S(2)}) collective-permute-start(f32[24,128]{1,0:T(8,128)S(1)} %get-tuple-element.74), channel_id=1, source_target_pairs={{0,2},{1,3},{2,0},{3,1},{4,6},{5,7},{6,4},{7,5},{8,10},{9,11},{10,... | collective-permute-start | bytes 36872 | tf_op jit(solution)/shard_map/ppermute | solution.py:639
  7.0 1.6 %collective-permute-start.3 = (f32[24,128]{1,0:T(8,128)S(1)}, f32[24,128]{1,0:T(8,128)S(1)}, u32[]{:S(2)}, u32[]{:S(2)}) collective-permute-start(f32[24,128]{1,0:T(8,128)S(1)} %get-tuple-element.75), channel_id=1, source_target_pairs={{0,2},{1,3},{2,0},{3,1},{4,6},{5,7},{6,4},{7,5},{8,10},{9,11},{10,... | collective-permute-start | bytes 36872 | tf_op jit(solution)/shard_map/ppermute | solution.py:639
  7.0 1.5 %collective-permute-start.4 = (f32[16,128]{1,0:T(8,128)S(1)}, f32[16,128]{1,0:T(8,128)S(1)}, u32[]{:S(2)}, u32[]{:S(2)}) collective-permute-start(f32[16,128]{1,0:T(8,128)S(1)} %get-tuple-element.76), channel_id=1, source_target_pairs={{0,2},{1,3},{2,0},{3,1},{4,6},{5,7},{6,4},{7,5},{8,10},{9,11},{10,... | collective-permute-start | bytes 24584 | tf_op jit(solution)/shard_map/ppermute | solution.py:639
  10.2 4.1 %collective-permute-start.5 = (f32[64,128]{1,0:T(8,128)S(1)}, f32[64,128]{1,0:T(8,128)S(1)}, u32[]{:S(2)}, u32[]{:S(2)}) collective-permute-start(f32[64,128]{1,0:T(8,128)S(1)} %get-tuple-element.82), channel_id=1, source_target_pairs={{0,1},{1,0},{2,4},{3,5},{4,2},{5,3},{6,8},{7,9},{8,6},{9,7},{10,12... | collective-permute-start | bytes 98312 | tf_op jit(solution)/shard_map/ppermute | solution.py:639
  10.6 3.8 %collective-permute-start.6 = (f32[28,128]{1,0:T(8,128)S(1)}, f32[28,128]{1,0:T(8,128)S(1)}, u32[]{:S(2)}, u32[]{:S(2)}) collective-permute-start(f32[28,128]{1,0:T(8,128)S(1)} %get-tuple-element.83.refs_12_.refs_5_), channel_id=1, source_target_pairs={{1,0},{0,1},{3,2},{2,3},{5,4},{4,5},{7,6},{6,7},{9,8},{8,9},{11,10... | collective-permute-start | bytes 43016 | tf_op jit(solution)/shard_map/ppermute | solution.py:644
  12.3 1.7 %collective-permute-start.7 = (f32[24,128]{1,0:T(8,128)S(1)}, f32[24,128]{1,0:T(8,128)S(1)}, u32[]{:S(2)}, u32[]{:S(2)}) collective-permute-start(f32[24,128]{1,0:T(8,128)S(1)} %get-tuple-element.84), channel_id=1, source_target_pairs={{0,2},{1,3},{2,0},{3,1},{4,6},{5,7},{6,4},{7,5},{8,10},{9,11},{10,... | collective-permute-start | bytes 36872 | tf_op jit(solution)/shard_map/ppermute | solution.py:639
  12.3 1.7 %collective-permute-start.8 = (f32[24,128]{1,0:T(8,128)S(1)}, f32[24,128]{1,0:T(8,128)S(1)}, u32[]{:S(2)}, u32[]{:S(2)}) collective-permute-start(f32[24,128]{1,0:T(8,128)S(1)} %get-tuple-element.85), channel_id=1, source_target_pairs={{0,2},{1,3},{2,0},{3,1},{4,6},{5,7},{6,4},{7,5},{8,10},{9,11},{10,... | collective-permute-start | bytes 36872 | tf_op jit(solution)/shard_map/ppermute | solution.py:639
  12.8 1.2 %collective-permute-start.9 = (f32[16,128]{1,0:T(8,128)S(1)}, f32[16,128]{1,0:T(8,128)S(1)}, u32[]{:S(2)}, u32[]{:S(2)}) collective-permute-start(f32[16,128]{1,0:T(8,128)S(1)} %get-tuple-element.86), channel_id=1, source_target_pairs={{0,2},{1,3},{2,0},{3,1},{4,6},{5,7},{6,4},{7,5},{8,10},{9,11},{10,... | collective-permute-start | bytes 24584 | tf_op jit(solution)/shard_map/ppermute | solution.py:639
  15.2 5.4 %collective-permute-start.10 = (f32[64,128]{1,0:T(8,128)S(1)}, f32[64,128]{1,0:T(8,128)S(1)}, u32[]{:S(2)}, u32[]{:S(2)}) collective-permute-start(f32[64,128]{1,0:T(8,128)S(1)} %get-tuple-element.94), channel_id=1, source_target_pairs={{0,1},{1,0},{2,4},{3,5},{4,2},{5,3},{6,8},{7,9},{8,6},{9,7},{10,12... | collective-permute-start | bytes 98312 | tf_op jit(solution)/shard_map/ppermute | solution.py:639
  16.9 3.7 %collective-permute-start.11 = (f32[28,128]{1,0:T(8,128)S(1)}, f32[28,128]{1,0:T(8,128)S(1)}, u32[]{:S(2)}, u32[]{:S(2)}) collective-permute-start(f32[28,128]{1,0:T(8,128)S(1)} %get-tuple-element.95.refs_12_.refs_7_), channel_id=1, source_target_pairs={{1,0},{0,1},{3,2},{2,3},{5,4},{4,5},{7,6},{6,7},{9,8},{8,9},{11,10... | collective-permute-start | bytes 43016 | tf_op jit(solution)/shard_map/ppermute | solution.py:644
  17.3 1.7 %collective-permute-start.12 = (f32[24,128]{1,0:T(8,128)S(1)}, f32[24,128]{1,0:T(8,128)S(1)}, u32[]{:S(2)}, u32[]{:S(2)}) collective-permute-start(f32[24,128]{1,0:T(8,128)S(1)} %get-tuple-element.96), channel_id=1, source_target_pairs={{0,2},{1,3},{2,0},{3,1},{4,6},{5,7},{6,4},{7,5},{8,10},{9,11},{10,... | collective-permute-start | bytes 36872 | tf_op jit(solution)/shard_map/ppermute | solution.py:639
  17.3 1.7 %collective-permute-start.13 = (f32[24,128]{1,0:T(8,128)S(1)}, f32[24,128]{1,0:T(8,128)S(1)}, u32[]{:S(2)}, u32[]{:S(2)}) collective-permute-start(f32[24,128]{1,0:T(8,128)S(1)} %get-tuple-element.97), channel_id=1, source_target_pairs={{0,2},{1,3},{2,0},{3,1},{4,6},{5,7},{6,4},{7,5},{8,10},{9,11},{10,... | collective-permute-start | bytes 36872 | tf_op jit(solution)/shard_map/ppermute | solution.py:639
  17.8 1.2 %collective-permute-start.14 = (f32[16,128]{1,0:T(8,128)S(1)}, f32[16,128]{1,0:T(8,128)S(1)}, u32[]{:S(2)}, u32[]{:S(2)}) collective-permute-start(f32[16,128]{1,0:T(8,128)S(1)} %get-tuple-element.98), channel_id=1, source_target_pairs={{0,2},{1,3},{2,0},{3,1},{4,6},{5,7},{6,4},{7,5},{8,10},{9,11},{10,... | collective-permute-start | bytes 24584 | tf_op jit(solution)/shard_map/ppermute | solution.py:639
  21.5 4.1 %collective-permute-start.15 = (f32[64,128]{1,0:T(8,128)S(1)}, f32[64,128]{1,0:T(8,128)S(1)}, u32[]{:S(2)}, u32[]{:S(2)}) collective-permute-start(f32[64,128]{1,0:T(8,128)S(1)} %get-tuple-element.102), channel_id=1, source_target_pairs={{0,1},{1,0},{2,4},{3,5},{4,2},{5,3},{6,8},{7,9},{8,6},{9,7},{10,12... | collective-permute-start | bytes 98312 | tf_op jit(solution)/shard_map/ppermute | solution.py:639
  21.8 3.7 %collective-permute-start.16 = (f32[28,128]{1,0:T(8,128)S(1)}, f32[28,128]{1,0:T(8,128)S(1)}, u32[]{:S(2)}, u32[]{:S(2)}) collective-permute-start(f32[28,128]{1,0:T(8,128)S(1)} %get-tuple-element.103.refs_9_.refs_12_), channel_id=1, source_target_pairs={{1,0},{0,1},{3,2},{2,3},{5,4},{4,5},{7,6},{6,7},{9,8},{8,9},{11,10... | collective-permute-start | bytes 43016 | tf_op jit(solution)/shard_map/ppermute | solution.py:644
  23.5 1.7 %collective-permute-start.17 = (f32[24,128]{1,0:T(8,128)S(1)}, f32[24,128]{1,0:T(8,128)S(1)}, u32[]{:S(2)}, u32[]{:S(2)}) collective-permute-start(f32[24,128]{1,0:T(8,128)S(1)} %get-tuple-element.104), channel_id=1, source_target_pairs={{0,2},{1,3},{2,0},{3,1},{4,6},{5,7},{6,4},{7,5},{8,10},{9,11},{10,... | collective-permute-start | bytes 36872 | tf_op jit(solution)/shard_map/ppermute | solution.py:639
  23.5 1.7 %collective-permute-start.18 = (f32[24,128]{1,0:T(8,128)S(1)}, f32[24,128]{1,0:T(8,128)S(1)}, u32[]{:S(2)}, u32[]{:S(2)}) collective-permute-start(f32[24,128]{1,0:T(8,128)S(1)} %get-tuple-element.105), channel_id=1, source_target_pairs={{0,2},{1,3},{2,0},{3,1},{4,6},{5,7},{6,4},{7,5},{8,10},{9,11},{10,... | collective-permute-start | bytes 36872 | tf_op jit(solution)/shard_map/ppermute | solution.py:639
  24.0 1.2 %collective-permute-start.19 = (f32[16,128]{1,0:T(8,128)S(1)}, f32[16,128]{1,0:T(8,128)S(1)}, u32[]{:S(2)}, u32[]{:S(2)}) collective-permute-start(f32[16,128]{1,0:T(8,128)S(1)} %get-tuple-element.106), channel_id=1, source_target_pairs={{0,2},{1,3},{2,0},{3,1},{4,6},{5,7},{6,4},{7,5},{8,10},{9,11},{10,... | collective-permute-start | bytes 24584 | tf_op jit(solution)/shard_map/ppermute | solution.py:639
  25.7 3.7 %collective-permute-start.20 = (f32[2,128]{1,0:T(2,128)S(1)}, f32[2,128]{1,0:T(2,128)S(1)}, u32[]{:S(2)}, u32[]{:S(2)}) collective-permute-start(f32[2,128]{1,0:T(2,128)S(1)} %get-tuple-element.115), channel_id=1, source_target_pairs={{0,4},{1,5},{2,6},{3,7},{4,0},{5,1},{6,2},{7,3},{8,12},{9,13},{10,... | collective-permute-start | bytes 3080 | tf_op jit(solution)/shard_map/ppermute | solution.py:639
  26.3 3.6 %collective-permute-start.21 = (f32[2,128]{1,0:T(2,128)S(1)}, f32[2,128]{1,0:T(2,128)S(1)}, u32[]{:S(2)}, u32[]{:S(2)}) collective-permute-start(f32[2,128]{1,0:T(2,128)S(1)} %get-tuple-element.116), channel_id=1, source_target_pairs={{0,1},{1,0},{2,4},{3,5},{4,2},{5,3},{6,8},{7,9},{8,6},{9,7},{10,12... | collective-permute-start | bytes 3080 | tf_op jit(solution)/shard_map/ppermute | solution.py:639
  27.4 2.4 %collective-permute-start.22 = (f32[2,128]{1,0:T(2,128)S(1)}, f32[2,128]{1,0:T(2,128)S(1)}, u32[]{:S(2)}, u32[]{:S(2)}) collective-permute-start(f32[2,128]{1,0:T(2,128)S(1)} %get-tuple-element.117), channel_id=1, source_target_pairs={{0,2},{1,3},{2,0},{3,1},{4,8},{5,9},{6,10},{7,11},{8,4},{9,5},{10,... | collective-permute-start | bytes 3080 | tf_op jit(solution)/shard_map/ppermute | solution.py:639
  27.9 2.0 %collective-permute-start.23 = (f32[2,128]{1,0:T(2,128)S(1)}, f32[2,128]{1,0:T(2,128)S(1)}, u32[]{:S(2)}, u32[]{:S(2)}) collective-permute-start(f32[2,128]{1,0:T(2,128)S(1)} %get-tuple-element.118), channel_id=1, source_target_pairs={{0,2},{1,3},{2,0},{3,1},{4,6},{5,7},{6,4},{7,5},{8,10},{9,11},{10,... | collective-permute-start | bytes 3080 | tf_op jit(solution)/shard_map/ppermute | solution.py:639

commit v18 on v14

--- a/solution.py
+++ b/solution.py
@@ -432,11 +432,11 @@
     copies = start_copies(
         [
             (now_hbm, now_ref),
-            (later_hbm[0], later_refs[0]),
             (lame_hbm, lame_ref),
             (shear_hbm, shear_ref),
             (flags_hbm, flags_ref),
             (weak_hbm, weak_ref),
+            (later_hbm[0], later_refs[0]),
         ]
         + list(zip(later_hbm[1:], later_refs[1:])),
         sems,
@@ -448,21 +448,12 @@
     gather = gather_table(lanes, z_elems)
     fault = fault_table(lanes, z_elems)
     scratch[...] = jnp.zeros_like(scratch)
-    for copy in copies[:6]:
+    for copy in copies[1:5]:
         copy.wait()
-    cur = to_elements(lambda c, y: now_ref[c, y], scratch, gather, y_elems)
-    cur_ref[...] = cur
     lame_row, shear_row = material_rows(lame_ref, shear_ref)
     material_ref[...] = jnp.concatenate(
         [lame_row, shear_row, jnp.zeros((6, lanes), jnp.float32)], axis=0
     )
-    planes = [cur[x * PLANE : (x + 1) * PLANE] for x in range(4)]
-    edge = dot(edge_ref[...], jnp.concatenate([stacked(p) for p in planes], axis=0))
-    right = edge_message(edge, lame_row, shear_row, z_elems)
-    lasts = [store_fault(fault_out_ref, x, planes[x], z_elems) for x in range(4)]
-    message, odd_ref[...] = select_messages(parity, sent_plane(planes[0], lasts[0]), right)
-    for even_ref, at in zip(even_refs, (0, PARTS[0], PARTS[0] + PARTS[1])):
-        even_ref[...] = message[at : at + even_ref.shape[0]]
     weak = weak_ref[...]
     tangent = []
     for i in range(flags_ref.shape[0]):
@@ -471,6 +462,17 @@
             jnp.where(flag == 0, lock_stiffness, jnp.where(flag == 1, -weak, 0.0))
         )
     fault_out_ref[FAULT:] = exact_dot(jnp.concatenate(tangent, axis=0), fault)
+    copies[0].wait()
+    cur = to_elements(lambda c, y: now_ref[c, y], scratch, gather, y_elems)
+    cur_ref[...] = cur
+    planes = [cur[x * PLANE : (x + 1) * PLANE] for x in range(4)]
+    lasts = [store_fault(fault_out_ref, x, planes[x], z_elems) for x in range(4)]
+    copies[5].wait()
+    edge = dot(edge_ref[...], jnp.concatenate([stacked(p) for p in planes], axis=0))
+    right = edge_message(edge, lame_row, shear_row, z_elems)
+    message, odd_ref[...] = select_messages(parity, sent_plane(planes[0], lasts[0]), right)
+    for even_ref, at in zip(even_refs, (0, PARTS[0], PARTS[0] + PARTS[1])):
+        even_ref[...] = message[at : at + even_ref.shape[0]]
     for copy in copies[6:]:
         copy.wait()
 
@@ -650,6 +652,10 @@
     out_d[...] = jnp.where(low, rows[0], rows[4])
 
 
+def sum_kernel(*refs):
+    refs[-1][...] = sum(ref[...] for ref in refs[:-1])
+
+
 VMEM = pl.BlockSpec(memory_space=pltpu.VMEM)
 HBM = pl.BlockSpec(memory_space=pltpu.HBM)
 SMEM = pl.BlockSpec(memory_space=pltpu.SMEM)
@@ -689,8 +695,12 @@
     route = []
     for i in range(size):
         for j in range(across):
-            side = j if i in partner else min(j ^ 1, across - 1)
-            route.append((i * across + j, partner.get(i, i) * across + side))
+            other, side = partner.get(i, i), j
+            if i not in partner and i ^ 1 < size and i ^ 1 not in partner:
+                other = i ^ 1
+            elif i not in partner:
+                side = min(j ^ 1, across - 1)
+            route.append((i * across + j, other * across + side))
     return lax.ppermute(block, ("dom", "depth"), route)
 
 
@@ -818,9 +828,10 @@
                 pair=pair,
                 steps=steps,
             )
-            patch_sums = sums[0]
-            for i, distance, group in ((4, 2, 1), (2, 1, 1), (3, 2, 0), (1, 1, 0)):
-                patch_sums = patch_sums + swapped(sums[i], distance, group)
+            shares = [sums[0]]
+            for i, distance, group in ((3, 2, 0), (2, 1, 1), (4, 2, 1), (1, 1, 0)):
+                shares.append(swapped(sums[i], distance, group))
+            patch_sums = kernel_call(sum_kernel, [(PATCH_DEV, lanes)], shares)[0]
             earlier, later = kernel_call(
                 step_kernel,
                 [whole, whole],

time: 32.3 us -> 30.9 us (0.957)
  starting transfers between devices: 16 us -> 14.9 us
  other arithmetic: 0.57 us -> 0 us
  Pallas kernels: 9.24 us -> 9.73 us
  waiting for transfers between devices: 5.59 us -> 5.18 us
    ppermute x20, starting transfers between devices: 12.2 us -> 11.1 us  [swapped(): return lax.ppermute(block, ('dom', 'depth'), route)]
    broadcast_in_dim x1 -> x0, other arithmetic: 0.57 us -> none  [on_device(): patch_sums[None]]
    pallas_call x13 -> x14, Pallas kernels: 9.24 us -> 9.73 us  [kernel_call(): pl.pallas_call(functools.partial(body, **static) if static else body, out...]
    ppermute x20, waiting for transfers between devices: 2.31 us -> 1.9 us  [swapped(): return lax.ppermute(block, ('dom', 'depth'), route)]
  transfers between devices with their start and end apart: 24 -> 24, of which waited for: 11 -> 10; matrix products, arithmetic and copies ran while one was open for 0% -> 0% of each run, Pallas kernels for 14% -> 15%
where the time goes in v18:
time: 30.9 us; the launch traced here: 30.6 us
  starting transfers between devices  14.9 us (48%)
  Pallas kernels  9.73 us (31%)
  waiting for transfers between devices  5.18 us (17%)
  between operations  0.77 us (2%)
    ppermute x20, starting transfers between devices, swapped(): return lax.ppermute(block, ('dom', 'depth'), route)  11.1 us
    pallas_call x14, Pallas kernels, kernel_call(): pl.pallas_call(functools.partial(body, **static) if static else body, out...  9.73 us
    ppermute x4, starting transfers between devices, from_behind(): lax.ppermute(block, axis, [((i - distance) % size, i) for i in range(size)])  3.82 us
    ppermute x4, waiting for transfers between devices, from_behind(): lax.ppermute(block, axis, [((i - distance) % size, i) for i in range(size)])  3.28 us
    ppermute x20, waiting for transfers between devices, swapped(): return lax.ppermute(block, ('dom', 'depth'), route)  1.9 us
  transfers between devices with their start and end apart: 24, of which 10 were waited for; matrix products, arithmetic and copies ran while one was open for 0% of the time, Pallas kernels for 15%

profile of v18, /device:TPU:0, one launch (start us, length us, event | category | flops | bytes accessed | tf_op | source)
XLA Modules:
  0.0 30.6 jit_solution(10705756483791598820)
XLA Ops:
  0.6 2.0 %shard_map.166 = (f32[320,128]{1,0:T(8,128)S(1)}, f32[24,128]{1,0:T(8,128)S(1)}, f32[16,128]{1,0:T(8,128)S(1)}, f32[16,128]{1,0:T(8,128)S(1)}, f32[56,128]{1,0:T...) custom-call(f32[3,17,4,128]{3,2,1,0:T(4,128)} %bitcast.11, ...), custom_call_target="tpu_custom_call" | custom-call | tf_op jit(solution)/shard_map/pallas_call | solution.py:677
  2.6 3.0 %collective-permute-start = (f32[56,128]{1,0:T(8,128)S(1)}, f32[56,128]{1,0:T(8,128)S(1)}, u32[]{:S(2)}, u32[]{:S(2)}) collective-permute-start(f32[56,128]{1,0:T(8,128)S(1)} %get-tuple-element.72), channel_id=1, source_target_pairs={{0,1},{1,0},{2,4},{3,5},{4,2},{5,3},{6,8},{7,9},{8,6},{9,7},{10,12... | collective-permute-start | bytes 86024 | tf_op jit(solution)/shard_map/ppermute | solution.py:704
  5.7 1.3 %collective-permute-start.2 = (f32[24,128]{1,0:T(8,128)S(1)}, f32[24,128]{1,0:T(8,128)S(1)}, u32[]{:S(2)}, u32[]{:S(2)}) collective-permute-start(f32[24,128]{1,0:T(8,128)S(1)} %get-tuple-element.74), channel_id=1, source_target_pairs={{0,2},{1,3},{2,0},{3,1},{4,6},{5,7},{6,4},{7,5},{8,10},{9,11},{10,... | collective-permute-start | bytes 36872 | tf_op jit(solution)/shard_map/ppermute | solution.py:704
  7.0 0.5 %collective-permute-start.4 = (f32[16,128]{1,0:T(8,128)S(1)}, f32[16,128]{1,0:T(8,128)S(1)}, u32[]{:S(2)}, u32[]{:S(2)}) collective-permute-start(f32[16,128]{1,0:T(8,128)S(1)} %get-tuple-element.76), channel_id=1, source_target_pairs={{0,2},{1,3},{2,0},{3,1},{4,6},{5,7},{6,4},{7,5},{8,10},{9,11},{10,... | collective-permute-start | bytes 24584 | tf_op jit(solution)/shard_map/ppermute | solution.py:704
  7.5 0.5 %shard_map.167 = (f32[320,128]{1,0:T(8,128)S(1)}, f32[320,128]{1,0:T(8,128)S(1)}) custom-call(f32[3,17,4,128]{3,2,1,0:T(4,128)S(1)} %get-tuple-element.62.next_ref, f32[17,4,128]{2,1,0:T(4,128)S(1)} %get-tuple-element.63.density_ref, f32[320,128]{1,0:T(8,128)S(1)} %get-tuple-element.64.mass_ref), custom_call_target="tpu_custom_call" | custom-call | tf_op jit(solution)/shard_map/pallas_call | solution.py:677
  8.0 0.5 %shard_map.168 = (f32[320,128]{1,0:T(8,128)S(1)}, f32[160,128]{1,0:T(8,128)S(1)}) custom-call(f32[320,128]{1,0:T(8,128)S(1)} %get-tuple-element.61.cur_ref.refs_0_.refs_1_, f32[8,128]{1,0:T(8,128)S(1)} %get-tuple-element.67.material_ref.refs_5_, bf16[2,640,384]{2,1,0:T(8,128)(2,1)S(1)} %get-tuple-element.68.own_ref, ...), custom_call_target="tpu_custom_call" | custom-call | tf_op jit(solution)/shard_map/pallas_call | solution.py:677
  8.6 0.8 %collective-permute-done.1.refs_7_.refs_11_.refs_4_ = f32[40,128]{1,0:T(8,128)S(1)} collective-permute-done((f32[40,128]{1,0:T(8,128)S(1)}, f32[40,128]{1,0:T(8,128)S(1)}, u32[]{:S(2)}, u32[]{:S(2)}) %collective-permute-start.1) | collective-permute-done | bytes 20512 | tf_op jit(solution)/shard_map/ppermute | solution.py:709
  9.4 0.9 %shard_map.169 = (f32[320,128]{1,0:T(8,128)S(1)}, f32[24,128]{1,0:T(8,128)S(1)}, f32[16,128]{1,0:T(8,128)S(1)}, f32[16,128]{1,0:T(8,128)S(1)}, f32[56,128]{1,0:T(8,128)S(1)}, /*index=5*/f32[28,128]{1,0:T(8,128)S(1)}) custom-call(f32[320,128]{1,0:T(8,128)S(1)} %get-tuple-element.61.cur_ref.refs_0_.refs_1_, f32[320,128]{1,0:T(8,128)S(1)} %get-tuple-element.65.refs_1_, ...), custom_call_target="tpu_custom_call" | custom-call | tf_op jit(solution)/shard_map/pallas_call | solution.py:677
  10.6 1.7 %collective-permute-start.6 = (f32[28,128]{1,0:T(8,128)S(1)}, f32[28,128]{1,0:T(8,128)S(1)}, u32[]{:S(2)}, u32[]{:S(2)}) collective-permute-start(f32[28,128]{1,0:T(8,128)S(1)} %get-tuple-element.83.refs_12_.refs_5_), channel_id=1, source_target_pairs={{1,0},{0,1},{3,2},{2,3},{5,4},{4,5},{7,6},{6,7},{9,8},{8,9},{11,10... | collective-permute-start | bytes 43016 | tf_op jit(solution)/shard_map/ppermute | solution.py:709
  12.4 0.5 %collective-permute-start.8 = (f32[16,128]{1,0:T(8,128)S(1)}, f32[16,128]{1,0:T(8,128)S(1)}, u32[]{:S(2)}, u32[]{:S(2)}) collective-permute-start(f32[16,128]{1,0:T(8,128)S(1)} %get-tuple-element.85), channel_id=1, source_target_pairs={{0,2},{1,3},{2,0},{3,1},{4,6},{5,7},{6,4},{7,5},{8,10},{9,11},{10,... | collective-permute-start | bytes 24584 | tf_op jit(solution)/shard_map/ppermute | solution.py:704
  12.9 0.5 %shard_map.170 = (f32[320,128]{1,0:T(8,128)S(1)}, f32[160,128]{1,0:T(8,128)S(1)}) custom-call(f32[320,128]{1,0:T(8,128)S(1)} %get-tuple-element.79.cur_ref._.refs_0_.refs_1_, f32[8,128]{1,0:T(8,128)S(1)} %get-tuple-element.67.material_ref.refs_5_, bf16[2,640,384]{2,1,0:T(8,128)(2,1)S(1)} %get-tuple-element.68.own_ref, ...), custom_call_target="tpu_custom_call" | custom-call | tf_op jit(solution)/shard_map/pallas_call | solution.py:677
  14.4 0.9 %shard_map.172 = (f32[320,128]{1,0:T(8,128)S(1)}, f32[24,128]{1,0:T(8,128)S(1)}, f32[16,128]{1,0:T(8,128)S(1)}, f32[16,128]{1,0:T(8,128)S(1)}, f32[56,128]{1,0:T(8,128)S(1)}, /*index=5*/f32[28,128]{1,0:T(8,128)S(1)}) custom-call(f32[320,128]{1,0:T(8,128)S(1)} %get-tuple-element.79.cur_ref._.refs_0_.refs_1_, ...), custom_call_target="tpu_custom_call" | custom-call | tf_op jit(solution)/shard_map/pallas_call | solution.py:677
  15.3 1.8 %collective-permute-start.10 = (f32[56,128]{1,0:T(8,128)S(1)}, f32[56,128]{1,0:T(8,128)S(1)}, u32[]{:S(2)}, u32[]{:S(2)}) collective-permute-start(f32[56,128]{1,0:T(8,128)S(1)} %get-tuple-element.94), channel_id=1, source_target_pairs={{0,1},{1,0},{2,4},{3,5},{4,2},{5,3},{6,8},{7,9},{8,6},{9,7},{10,12... | collective-permute-start | bytes 86024 | tf_op jit(solution)/shard_map/ppermute | solution.py:704
  17.4 0.5 %collective-permute-start.13 = (f32[16,128]{1,0:T(8,128)S(1)}, f32[16,128]{1,0:T(8,128)S(1)}, u32[]{:S(2)}, u32[]{:S(2)}) collective-permute-start(f32[16,128]{1,0:T(8,128)S(1)} %get-tuple-element.97), channel_id=1, source_target_pairs={{0,2},{1,3},{2,0},{3,1},{4,6},{5,7},{6,4},{7,5},{8,10},{9,11},{10,... | collective-permute-start | bytes 24584 | tf_op jit(solution)/shard_map/ppermute | solution.py:704
  17.9 0.5 %shard_map.173 = (f32[320,128]{1,0:T(8,128)S(1)}, f32[160,128]{1,0:T(8,128)S(1)}) custom-call(f32[320,128]{1,0:T(8,128)S(1)} %get-tuple-element.91.cur_ref.refs_0_.refs_1_, f32[8,128]{1,0:T(8,128)S(1)} %get-tuple-element.67.material_ref.refs_5_, bf16[2,640,384]{2,1,0:T(8,128)(2,1)S(1)} %get-tuple-element.68.own_ref, ...), custom_call_target="tpu_custom_call" | custom-call | tf_op jit(solution)/shard_map/pallas_call | solution.py:677
  19.0 1.7 %collective-permute-done.11.refs_7_.refs_8_ = f32[28,128]{1,0:T(8,128)S(1)} collective-permute-done((f32[28,128]{1,0:T(8,128)S(1)}, f32[28,128]{1,0:T(8,128)S(1)}, u32[]{:S(2)}, u32[]{:S(2)}) %collective-permute-start.11) | collective-permute-done | bytes 14368 | tf_op jit(solution)/shard_map/ppermute | solution.py:709
  20.8 0.9 %shard_map.174 = (f32[320,128]{1,0:T(8,128)S(1)}, f32[24,128]{1,0:T(8,128)S(1)}, f32[16,128]{1,0:T(8,128)S(1)}, f32[16,128]{1,0:T(8,128)S(1)}, f32[56,128]{1,0:T(8,128)S(1)}, /*index=5*/f32[28,128]{1,0:T(8,128)S(1)}) custom-call(f32[320,128]{1,0:T(8,128)S(1)} %get-tuple-element.91.cur_ref.refs_0_.refs_1_, ...), custom_call_target="tpu_custom_call" | custom-call | tf_op jit(solution)/shard_map/pallas_call | solution.py:677
  22.0 1.7 %collective-permute-start.16 = (f32[28,128]{1,0:T(8,128)S(1)}, f32[28,128]{1,0:T(8,128)S(1)}, u32[]{:S(2)}, u32[]{:S(2)}) collective-permute-start(f32[28,128]{1,0:T(8,128)S(1)} %get-tuple-element.103.refs_9_.refs_12_), channel_id=1, source_target_pairs={{1,0},{0,1},{3,2},{2,3},{5,4},{4,5},{7,6},{6,7},{9,8},{8,9},{11,10... | collective-permute-start | bytes 43016 | tf_op jit(solution)/shard_map/ppermute | solution.py:709
  23.7 0.5 %collective-permute-start.18 = (f32[16,128]{1,0:T(8,128)S(1)}, f32[16,128]{1,0:T(8,128)S(1)}, u32[]{:S(2)}, u32[]{:S(2)}) collective-permute-start(f32[16,128]{1,0:T(8,128)S(1)} %get-tuple-element.105), channel_id=1, source_target_pairs={{0,2},{1,3},{2,0},{3,1},{4,6},{5,7},{6,4},{7,5},{8,10},{9,11},{10,... | collective-permute-start | bytes 24584 | tf_op jit(solution)/shard_map/ppermute | solution.py:704
  24.2 0.5 %shard_map.175 = (f32[320,128]{1,0:T(8,128)S(1)}, f32[160,128]{1,0:T(8,128)S(1)}) custom-call(f32[320,128]{1,0:T(8,128)S(1)} %get-tuple-element.99.cur_ref.refs_0_, f32[8,128]{1,0:T(8,128)S(1)} %get-tuple-element.67.material_ref.refs_5_, bf16[2,640,384]{2,1,0:T(8,128)(2,1)S(1)} %get-tuple-element.68.own_ref, bf16[160,256]{1,0:T(8,128)(2,1)S(1)} %get-tuple-element.69.touch_ref), custom_call_target="tpu_custom_call" | custom-call | tf_op jit(solution)/shard_map/pallas_call | solution.py:677
  25.9 0.6 %collective-permute-start.20 = (f32[2,128]{1,0:T(2,128)S(1)}, f32[2,128]{1,0:T(2,128)S(1)}, u32[]{:S(2)}, u32[]{:S(2)}) collective-permute-start(f32[2,128]{1,0:T(2,128)S(1)} %get-tuple-element.115), channel_id=1, source_target_pairs={{0,4},{1,5},{2,6},{3,7},{4,0},{5,1},{6,2},{7,3},{8,12},{9,13},{10,... | collective-permute-start | bytes 3080 | tf_op jit(solution)/shard_map/ppermute | solution.py:704
  26.5 1.2 %collective-permute-start.21 = (f32[2,128]{1,0:T(2,128)S(1)}, f32[2,128]{1,0:T(2,128)S(1)}, u32[]{:S(2)}, u32[]{:S(2)}) collective-permute-start(f32[2,128]{1,0:T(2,128)S(1)} %get-tuple-element.116), channel_id=1, source_target_pairs={{0,1},{1,0},{2,4},{3,5},{4,2},{5,3},{6,8},{7,9},{8,6},{9,7},{10,12... | collective-permute-start | bytes 3080 | tf_op jit(solution)/shard_map/ppermute | solution.py:704
  28.2 1.5 %shard_map.178 = (f32[3,17,4,128]{3,2,1,0:T(4,128)}, f32[3,17,4,128]{3,2,1,0:T(4,128)}) custom-call(f32[320,128]{1,0:T(8,128)S(1)} %get-tuple-element.99.cur_ref.refs_0_, f32[320,128]{1,0:T(8,128)S(1)} %get-tuple-element.91.cur_ref.refs_0_.refs_1_, f32[320,128]{1,0:T(8,128)S(1)} %get-tuple-element.66.refs_2_, f32[320,128]{1,0:T(8,128)S(1)} %get-tuple-element.100.refs_3_, ...), custom_call_target="tpu_custom_call" | custom-call | tf_op jit(solution)/shard_map/pallas_call | solution.py:677
  30.1 0.6 %shard_map.179 = f32[2,128]{1,0:T(2,128)} custom-call(f32[2,128]{1,0:T(2,128)S(1)} %get-tuple-element.111.refs_16_.refs_0_, f32[2,128]{1,0:T(2,128)S(1)} %collective-permute-done.20.refs_1_, f32[2,128]{1,0:T(2,128)S(1)} %collective-permute-done.21.refs_2_, f32[2,128]{1,0:T(2,128)S(1)} %collective-permute-done.22.refs_3_, ...), custom_call_target="tpu_custom_call" | custom-call | tf_op jit(solution)/shard_map/pallas_call | solution.py:677
  (38 shorter events, 4.9 us)
Async XLA Ops:
  2.6 6.8 %collective-permute-start = (f32[56,128]{1,0:T(8,128)S(1)}, f32[56,128]{1,0:T(8,128)S(1)}, u32[]{:S(2)}, u32[]{:S(2)}) collective-permute-start(f32[56,128]{1,0:T(8,128)S(1)} %get-tuple-element.72), channel_id=1, source_target_pairs={{0,1},{1,0},{2,4},{3,5},{4,2},{5,3},{6,8},{7,9},{8,6},{9,7},{10,12... | collective-permute-start | bytes 86024 | tf_op jit(solution)/shard_map/ppermute | solution.py:704
  5.6 3.8 %collective-permute-start.1 = (f32[40,128]{1,0:T(8,128)S(1)}, f32[40,128]{1,0:T(8,128)S(1)}, u32[]{:S(2)}, u32[]{:S(2)}) collective-permute-start(f32[40,128]{1,0:T(8,128)S(1)} %get-tuple-element.73.refs_12_.refs_13_.refs_3_), channel_id=1, source_target_pairs={{1,0},{0,1},{3,2},{2,3},{5,4},{4,5},{7,6},{6,7},{9,8},{8,9},{11,10... | collective-permute-start | bytes 61448 | tf_op jit(solution)/shard_map/ppermute | solution.py:709
  5.7 2.8 %collective-permute-start.2 = (f32[24,128]{1,0:T(8,128)S(1)}, f32[24,128]{1,0:T(8,128)S(1)}, u32[]{:S(2)}, u32[]{:S(2)}) collective-permute-start(f32[24,128]{1,0:T(8,128)S(1)} %get-tuple-element.74), channel_id=1, source_target_pairs={{0,2},{1,3},{2,0},{3,1},{4,6},{5,7},{6,4},{7,5},{8,10},{9,11},{10,... | collective-permute-start | bytes 36872 | tf_op jit(solution)/shard_map/ppermute | solution.py:704
  7.0 1.6 %collective-permute-start.3 = (f32[16,128]{1,0:T(8,128)S(1)}, f32[16,128]{1,0:T(8,128)S(1)}, u32[]{:S(2)}, u32[]{:S(2)}) collective-permute-start(f32[16,128]{1,0:T(8,128)S(1)} %get-tuple-element.75), channel_id=1, source_target_pairs={{0,2},{1,3},{2,0},{3,1},{4,6},{5,7},{6,4},{7,5},{8,10},{9,11},{10,... | collective-permute-start | bytes 24584 | tf_op jit(solution)/shard_map/ppermute | solution.py:704
  7.0 1.6 %collective-permute-start.4 = (f32[16,128]{1,0:T(8,128)S(1)}, f32[16,128]{1,0:T(8,128)S(1)}, u32[]{:S(2)}, u32[]{:S(2)}) collective-permute-start(f32[16,128]{1,0:T(8,128)S(1)} %get-tuple-element.76), channel_id=1, source_target_pairs={{0,2},{1,3},{2,0},{3,1},{4,6},{5,7},{6,4},{7,5},{8,10},{9,11},{10,... | collective-permute-start | bytes 24584 | tf_op jit(solution)/shard_map/ppermute | solution.py:704
  10.3 4.1 %collective-permute-start.5 = (f32[56,128]{1,0:T(8,128)S(1)}, f32[56,128]{1,0:T(8,128)S(1)}, u32[]{:S(2)}, u32[]{:S(2)}) collective-permute-start(f32[56,128]{1,0:T(8,128)S(1)} %get-tuple-element.82), channel_id=1, source_target_pairs={{0,1},{1,0},{2,4},{3,5},{4,2},{5,3},{6,8},{7,9},{8,6},{9,7},{10,12... | collective-permute-start | bytes 86024 | tf_op jit(solution)/shard_map/ppermute | solution.py:704
  10.6 3.8 %collective-permute-start.6 = (f32[28,128]{1,0:T(8,128)S(1)}, f32[28,128]{1,0:T(8,128)S(1)}, u32[]{:S(2)}, u32[]{:S(2)}) collective-permute-start(f32[28,128]{1,0:T(8,128)S(1)} %get-tuple-element.83.refs_12_.refs_5_), channel_id=1, source_target_pairs={{1,0},{0,1},{3,2},{2,3},{5,4},{4,5},{7,6},{6,7},{9,8},{8,9},{11,10... | collective-permute-start | bytes 43016 | tf_op jit(solution)/shard_map/ppermute | solution.py:709
  12.4 1.7 %collective-permute-start.7 = (f32[24,128]{1,0:T(8,128)S(1)}, f32[24,128]{1,0:T(8,128)S(1)}, u32[]{:S(2)}, u32[]{:S(2)}) collective-permute-start(f32[24,128]{1,0:T(8,128)S(1)} %get-tuple-element.84), channel_id=1, source_target_pairs={{0,2},{1,3},{2,0},{3,1},{4,6},{5,7},{6,4},{7,5},{8,10},{9,11},{10,... | collective-permute-start | bytes 36872 | tf_op jit(solution)/shard_map/ppermute | solution.py:704
  12.4 1.3 %collective-permute-start.8 = (f32[16,128]{1,0:T(8,128)S(1)}, f32[16,128]{1,0:T(8,128)S(1)}, u32[]{:S(2)}, u32[]{:S(2)}) collective-permute-start(f32[16,128]{1,0:T(8,128)S(1)} %get-tuple-element.85), channel_id=1, source_target_pairs={{0,2},{1,3},{2,0},{3,1},{4,6},{5,7},{6,4},{7,5},{8,10},{9,11},{10,... | collective-permute-start | bytes 24584 | tf_op jit(solution)/shard_map/ppermute | solution.py:704
  12.9 1.2 %collective-permute-start.9 = (f32[16,128]{1,0:T(8,128)S(1)}, f32[16,128]{1,0:T(8,128)S(1)}, u32[]{:S(2)}, u32[]{:S(2)}) collective-permute-start(f32[16,128]{1,0:T(8,128)S(1)} %get-tuple-element.86), channel_id=1, source_target_pairs={{0,2},{1,3},{2,0},{3,1},{4,6},{5,7},{6,4},{7,5},{8,10},{9,11},{10,... | collective-permute-start | bytes 24584 | tf_op jit(solution)/shard_map/ppermute | solution.py:704
  15.3 5.5 %collective-permute-start.10 = (f32[56,128]{1,0:T(8,128)S(1)}, f32[56,128]{1,0:T(8,128)S(1)}, u32[]{:S(2)}, u32[]{:S(2)}) collective-permute-start(f32[56,128]{1,0:T(8,128)S(1)} %get-tuple-element.94), channel_id=1, source_target_pairs={{0,1},{1,0},{2,4},{3,5},{4,2},{5,3},{6,8},{7,9},{8,6},{9,7},{10,12... | collective-permute-start | bytes 86024 | tf_op jit(solution)/shard_map/ppermute | solution.py:704
  17.0 3.7 %collective-permute-start.11 = (f32[28,128]{1,0:T(8,128)S(1)}, f32[28,128]{1,0:T(8,128)S(1)}, u32[]{:S(2)}, u32[]{:S(2)}) collective-permute-start(f32[28,128]{1,0:T(8,128)S(1)} %get-tuple-element.95.refs_12_.refs_7_), channel_id=1, source_target_pairs={{1,0},{0,1},{3,2},{2,3},{5,4},{4,5},{7,6},{6,7},{9,8},{8,9},{11,10... | collective-permute-start | bytes 43016 | tf_op jit(solution)/shard_map/ppermute | solution.py:709
  17.4 1.7 %collective-permute-start.12 = (f32[24,128]{1,0:T(8,128)S(1)}, f32[24,128]{1,0:T(8,128)S(1)}, u32[]{:S(2)}, u32[]{:S(2)}) collective-permute-start(f32[24,128]{1,0:T(8,128)S(1)} %get-tuple-element.96), channel_id=1, source_target_pairs={{0,2},{1,3},{2,0},{3,1},{4,6},{5,7},{6,4},{7,5},{8,10},{9,11},{10,... | collective-permute-start | bytes 36872 | tf_op jit(solution)/shard_map/ppermute | solution.py:704
  17.4 1.3 %collective-permute-start.13 = (f32[16,128]{1,0:T(8,128)S(1)}, f32[16,128]{1,0:T(8,128)S(1)}, u32[]{:S(2)}, u32[]{:S(2)}) collective-permute-start(f32[16,128]{1,0:T(8,128)S(1)} %get-tuple-element.97), channel_id=1, source_target_pairs={{0,2},{1,3},{2,0},{3,1},{4,6},{5,7},{6,4},{7,5},{8,10},{9,11},{10,... | collective-permute-start | bytes 24584 | tf_op jit(solution)/shard_map/ppermute | solution.py:704
  17.9 1.2 %collective-permute-start.14 = (f32[16,128]{1,0:T(8,128)S(1)}, f32[16,128]{1,0:T(8,128)S(1)}, u32[]{:S(2)}, u32[]{:S(2)}) collective-permute-start(f32[16,128]{1,0:T(8,128)S(1)} %get-tuple-element.98), channel_id=1, source_target_pairs={{0,2},{1,3},{2,0},{3,1},{4,6},{5,7},{6,4},{7,5},{8,10},{9,11},{10,... | collective-permute-start | bytes 24584 | tf_op jit(solution)/shard_map/ppermute | solution.py:704
  21.6 4.1 %collective-permute-start.15 = (f32[56,128]{1,0:T(8,128)S(1)}, f32[56,128]{1,0:T(8,128)S(1)}, u32[]{:S(2)}, u32[]{:S(2)}) collective-permute-start(f32[56,128]{1,0:T(8,128)S(1)} %get-tuple-element.102), channel_id=1, source_target_pairs={{0,1},{1,0},{2,4},{3,5},{4,2},{5,3},{6,8},{7,9},{8,6},{9,7},{10,12... | collective-permute-start | bytes 86024 | tf_op jit(solution)/shard_map/ppermute | solution.py:704
  22.0 3.7 %collective-permute-start.16 = (f32[28,128]{1,0:T(8,128)S(1)}, f32[28,128]{1,0:T(8,128)S(1)}, u32[]{:S(2)}, u32[]{:S(2)}) collective-permute-start(f32[28,128]{1,0:T(8,128)S(1)} %get-tuple-element.103.refs_9_.refs_12_), channel_id=1, source_target_pairs={{1,0},{0,1},{3,2},{2,3},{5,4},{4,5},{7,6},{6,7},{9,8},{8,9},{11,10... | collective-permute-start | bytes 43016 | tf_op jit(solution)/shard_map/ppermute | solution.py:709
  23.7 1.7 %collective-permute-start.17 = (f32[24,128]{1,0:T(8,128)S(1)}, f32[24,128]{1,0:T(8,128)S(1)}, u32[]{:S(2)}, u32[]{:S(2)}) collective-permute-start(f32[24,128]{1,0:T(8,128)S(1)} %get-tuple-element.104), channel_id=1, source_target_pairs={{0,2},{1,3},{2,0},{3,1},{4,6},{5,7},{6,4},{7,5},{8,10},{9,11},{10,... | collective-permute-start | bytes 36872 | tf_op jit(solution)/shard_map/ppermute | solution.py:704
  23.7 1.4 %collective-permute-start.18 = (f32[16,128]{1,0:T(8,128)S(1)}, f32[16,128]{1,0:T(8,128)S(1)}, u32[]{:S(2)}, u32[]{:S(2)}) collective-permute-start(f32[16,128]{1,0:T(8,128)S(1)} %get-tuple-element.105), channel_id=1, source_target_pairs={{0,2},{1,3},{2,0},{3,1},{4,6},{5,7},{6,4},{7,5},{8,10},{9,11},{10,... | collective-permute-start | bytes 24584 | tf_op jit(solution)/shard_map/ppermute | solution.py:704
  24.2 1.2 %collective-permute-start.19 = (f32[16,128]{1,0:T(8,128)S(1)}, f32[16,128]{1,0:T(8,128)S(1)}, u32[]{:S(2)}, u32[]{:S(2)}) collective-permute-start(f32[16,128]{1,0:T(8,128)S(1)} %get-tuple-element.106), channel_id=1, source_target_pairs={{0,2},{1,3},{2,0},{3,1},{4,6},{5,7},{6,4},{7,5},{8,10},{9,11},{10,... | collective-permute-start | bytes 24584 | tf_op jit(solution)/shard_map/ppermute | solution.py:704
  25.9 3.8 %collective-permute-start.20 = (f32[2,128]{1,0:T(2,128)S(1)}, f32[2,128]{1,0:T(2,128)S(1)}, u32[]{:S(2)}, u32[]{:S(2)}) collective-permute-start(f32[2,128]{1,0:T(2,128)S(1)} %get-tuple-element.115), channel_id=1, source_target_pairs={{0,4},{1,5},{2,6},{3,7},{4,0},{5,1},{6,2},{7,3},{8,12},{9,13},{10,... | collective-permute-start | bytes 3080 | tf_op jit(solution)/shard_map/ppermute | solution.py:704
  26.5 3.6 %collective-permute-start.21 = (f32[2,128]{1,0:T(2,128)S(1)}, f32[2,128]{1,0:T(2,128)S(1)}, u32[]{:S(2)}, u32[]{:S(2)}) collective-permute-start(f32[2,128]{1,0:T(2,128)S(1)} %get-tuple-element.116), channel_id=1, source_target_pairs={{0,1},{1,0},{2,4},{3,5},{4,2},{5,3},{6,8},{7,9},{8,6},{9,7},{10,12... | collective-permute-start | bytes 3080 | tf_op jit(solution)/shard_map/ppermute | solution.py:704
  27.7 2.4 %collective-permute-start.22 = (f32[2,128]{1,0:T(2,128)S(1)}, f32[2,128]{1,0:T(2,128)S(1)}, u32[]{:S(2)}, u32[]{:S(2)}) collective-permute-start(f32[2,128]{1,0:T(2,128)S(1)} %get-tuple-element.117), channel_id=1, source_target_pairs={{0,2},{1,3},{2,0},{3,1},{4,8},{5,9},{6,10},{7,11},{8,4},{9,5},{10,... | collective-permute-start | bytes 3080 | tf_op jit(solution)/shard_map/ppermute | solution.py:704
  28.1 2.0 %collective-permute-start.23 = (f32[2,128]{1,0:T(2,128)S(1)}, f32[2,128]{1,0:T(2,128)S(1)}, u32[]{:S(2)}, u32[]{:S(2)}) collective-permute-start(f32[2,128]{1,0:T(2,128)S(1)} %get-tuple-element.118), channel_id=1, source_target_pairs={{0,2},{1,3},{2,0},{3,1},{4,6},{5,7},{6,4},{7,5},{8,10},{9,11},{10,... | collective-permute-start | bytes 3080 | tf_op jit(solution)/shard_map/ppermute | solution.py:704

commit v19 on v17

--- a/solution.py
+++ b/solution.py
@@ -329,6 +329,12 @@
     return jnp.concatenate([top, second, force[2 * BLOCK : 4 * BLOCK]], axis=0)
 
 
+def edge_of(field_ref, edge_ref, material_ref, z_elems):
+    planes = [stacked(field_ref[x * PLANE : (x + 1) * PLANE]) for x in range(4)]
+    edge = dot(edge_ref[...], jnp.concatenate(planes, axis=0))
+    return edge_message(edge, material_ref[0:1], material_ref[1:2], z_elems)
+
+
 def own_force(own_ref, cur, lame_row, shear_row):
     rows, lanes = cur.shape
     padded = jnp.concatenate([cur, jnp.zeros((OWN_COLS - rows, lanes), jnp.float32)], axis=0)
@@ -437,7 +443,7 @@
         later_ref, back_ref, out_hbm, later_hbm, scratch, out_ref, sems = refs
         copies = start_copies([(later_ref, later_hbm)], sems)
     else:
-        new_ref, *even_outs, odd_out, fault_out = refs
+        new_ref, odd_out, fault_out = refs
     place = lax.axis_index("dom")
     lanes = cur_ref.shape[1]
     even = place % 2 == 0
@@ -509,7 +515,6 @@
         else:
             new_ref[rows] = plane
             store_fault(fault_out, x, plane, z_elems)
-            planes.append(stacked(plane))
             if x == 0:
                 first = plane[: 4 * BLOCK]
     if last:
@@ -525,11 +530,24 @@
         for copy in copies:
             copy.wait()
     else:
-        edge = dot(edge_ref[...], jnp.concatenate(planes, axis=0))
-        right = edge_message(edge, lame_row, shear_row, z_elems)
-        message, odd_out[...] = select_messages(place % 2, first, right)
-        for even_out, at in zip(even_outs, (0, PARTS[0], PARTS[0] + PARTS[1])):
-            even_out[...] = message[at : at + even_out.shape[0]]
+        odd_out[...] = first
+
+        @pl.when(jnp.logical_not(even))
+        def _():
+            odd_out[...] = edge_of(new_ref, edge_ref, material_ref, z_elems)
+
+
+def on_chip_kernel(cur_ref, material_ref, edge_ref, *even_outs, z_elems):
+    message = even_outs[-1]
+    even_outs = even_outs[:-1]
+    message[...] = cur_ref[: 4 * BLOCK]
+
+    @pl.when(lax.axis_index("dom") % 2 == 0)
+    def _():
+        message[...] = edge_of(cur_ref, edge_ref, material_ref, z_elems)
+
+    for even_out, at in zip(even_outs, (0, PARTS[0], PARTS[0] + PARTS[1])):
+        even_out[...] = message[at : at + even_out.shape[0]]
 
 
 def mask_kernel(owner_ref, flags_ref, stress_ref, _, mask_ref, weight_ref, *, z_elems):
@@ -732,14 +750,21 @@
             )
             args.append(mask)
         if not last:
-            new, *even, odd, new_fault = kernel_call(
+            new, odd, new_fault = kernel_call(
                 step_kernel,
-                [field] + parts + [plane, (SENT_FAULT, lanes)],
+                [field, plane, (SENT_FAULT, lanes)],
                 args,
                 unread=(len(args) - 1,) if step == 1 else (),
                 **static,
             )
             fol, cur, fault_rows = cur, new, new_fault
+            even = kernel_call(
+                on_chip_kernel,
+                parts,
+                [cur, material, edge_table],
+                scratch=[pltpu.VMEM(plane, jnp.float32)],
+                z_elems=z_elems,
+            )
             even_in, odd_in, fault_in = exchange(even, odd, fault_rows)
         else:
             whole = (3, 4 * y_elems + 1, 4, lanes)

time: 30.6 us -> 30.3 us (level)
  waiting for transfers between devices: 5.28 us -> 4.02 us
  starting transfers between devices: 14.7 us -> 15.4 us
    ppermute x4, waiting for transfers between devices: 3.31 us -> 2.32 us  [from_behind(): lax.ppermute(block, axis, [((i - distance) % size, i) for i in range(size)])]
    ppermute x20, starting transfers between devices: 11 us -> 11.6 us  [swapped(): return lax.ppermute(block, ('dom', 'depth'), route)]
    pallas_call x14 -> x17, Pallas kernels: 9.64 us -> 9.8 us  [kernel_call(): pl.pallas_call(functools.partial(body, **static) if static else body, out...]
  transfers between devices with their start and end apart: 24 -> 24, of which waited for: 8 -> 8; matrix products, arithmetic and copies ran while one was open for 0% -> 0% of each run, Pallas kernels for 15% -> 18%
where the time goes in v19:
time: 30.3 us; the launch traced here: 30 us
  starting transfers between devices  15.4 us (51%)
  Pallas kernels  9.8 us (32%)
  waiting for transfers between devices  4.02 us (13%)
  between operations  0.76 us (3%)
    ppermute x20, starting transfers between devices, swapped(): return lax.ppermute(block, ('dom', 'depth'), route)  11.6 us
    pallas_call x17, Pallas kernels, kernel_call(): pl.pallas_call(functools.partial(body, **static) if static else body, out...  9.8 us
    ppermute x4, starting transfers between devices, from_behind(): lax.ppermute(block, axis, [((i - distance) % size, i) for i in range(size)])  3.78 us
    ppermute x4, waiting for transfers between devices, from_behind(): lax.ppermute(block, axis, [((i - distance) % size, i) for i in range(size)])  2.32 us
    ppermute x20, waiting for transfers between devices, swapped(): return lax.ppermute(block, ('dom', 'depth'), route)  1.7 us
  transfers between devices with their start and end apart: 24, of which 8 were waited for; matrix products, arithmetic and copies ran while one was open for 0% of the time, Pallas kernels for 18%

profile of v19, /device:TPU:0, one launch (start us, length us, event | category | flops | bytes accessed | tf_op | source)
XLA Modules:
  0.0 30.0 jit_solution(11588788076226527532)
XLA Ops:
  0.6 2.0 %shard_map.166 = (f32[320,128]{1,0:T(8,128)S(1)}, f32[24,128]{1,0:T(8,128)S(1)}, f32[24,128]{1,0:T(8,128)S(1)}, f32[16,128]{1,0:T(8,128)S(1)}, f32[64,128]{1,0:T...) custom-call(f32[3,17,4,128]{3,2,1,0:T(4,128)} %bitcast.11, ...), custom_call_target="tpu_custom_call" | custom-call | tf_op jit(solution)/shard_map/pallas_call | solution.py:630
  2.6 3.0 %collective-permute-start = (f32[64,128]{1,0:T(8,128)S(1)}, f32[64,128]{1,0:T(8,128)S(1)}, u32[]{:S(2)}, u32[]{:S(2)}) collective-permute-start(f32[64,128]{1,0:T(8,128)S(1)} %get-tuple-element.72), channel_id=1, source_target_pairs={{0,1},{1,0},{2,4},{3,5},{4,2},{5,3},{6,8},{7,9},{8,6},{9,7},{10,12... | collective-permute-start | bytes 98312 | tf_op jit(solution)/shard_map/ppermute | solution.py:657
  5.7 1.3 %collective-permute-start.2 = (f32[24,128]{1,0:T(8,128)S(1)}, f32[24,128]{1,0:T(8,128)S(1)}, u32[]{:S(2)}, u32[]{:S(2)}) collective-permute-start(f32[24,128]{1,0:T(8,128)S(1)} %get-tuple-element.74), channel_id=1, source_target_pairs={{0,2},{1,3},{2,0},{3,1},{4,6},{5,7},{6,4},{7,5},{8,10},{9,11},{10,... | collective-permute-start | bytes 36872 | tf_op jit(solution)/shard_map/ppermute | solution.py:657
  7.0 0.5 %collective-permute-start.4 = (f32[16,128]{1,0:T(8,128)S(1)}, f32[16,128]{1,0:T(8,128)S(1)}, u32[]{:S(2)}, u32[]{:S(2)}) collective-permute-start(f32[16,128]{1,0:T(8,128)S(1)} %get-tuple-element.76), channel_id=1, source_target_pairs={{0,2},{1,3},{2,0},{3,1},{4,6},{5,7},{6,4},{7,5},{8,10},{9,11},{10,... | collective-permute-start | bytes 24584 | tf_op jit(solution)/shard_map/ppermute | solution.py:657
  7.5 0.5 %shard_map.167 = (f32[320,128]{1,0:T(8,128)S(1)}, f32[320,128]{1,0:T(8,128)S(1)}) custom-call(f32[3,17,4,128]{3,2,1,0:T(4,128)S(1)} %get-tuple-element.62.next_ref, f32[17,4,128]{2,1,0:T(4,128)S(1)} %get-tuple-element.63.density_ref, f32[320,128]{1,0:T(8,128)S(1)} %get-tuple-element.64.mass_ref), custom_call_target="tpu_custom_call" | custom-call | tf_op jit(solution)/shard_map/pallas_call | solution.py:630
  8.0 0.5 %shard_map.168 = (f32[320,128]{1,0:T(8,128)S(1)}, f32[160,128]{1,0:T(8,128)S(1)}) custom-call(f32[320,128]{1,0:T(8,128)S(1)} %get-tuple-element.61.cur_ref.refs_0_.refs_1_, f32[8,128]{1,0:T(8,128)S(1)} %get-tuple-element.67.material_ref.refs_5_, bf16[2,640,384]{2,1,0:T(8,128)(2,1)S(1)} %get-tuple-element.68.own_ref, ...), custom_call_target="tpu_custom_call" | custom-call | tf_op jit(solution)/shard_map/pallas_call | solution.py:630
  8.5 0.8 %collective-permute-done.1.refs_7_.refs_11_.refs_4_ = f32[40,128]{1,0:T(8,128)S(1)} collective-permute-done((f32[40,128]{1,0:T(8,128)S(1)}, f32[40,128]{1,0:T(8,128)S(1)}, u32[]{:S(2)}, u32[]{:S(2)}) %collective-permute-start.1) | collective-permute-done | bytes 20512 | tf_op jit(solution)/shard_map/ppermute | solution.py:662
  9.4 0.6 %shard_map.169 = (f32[320,128]{1,0:T(8,128)S(1)}, f32[64,128]{1,0:T(8,128)S(1)}, f32[28,128]{1,0:T(8,128)S(1)}) custom-call(f32[320,128]{1,0:T(8,128)S(1)} %get-tuple-element.61.cur_ref.refs_0_.refs_1_, f32[320,128]{1,0:T(8,128)S(1)} %get-tuple-element.65.refs_1_, f32[320,128]{1,0:T(8,128)S(1)} %get-tuple-element.66.refs_2_, ...), custom_call_target="tpu_custom_call" | custom-call | tf_op jit(solution)/shard_map/pallas_call | solution.py:630
  10.4 1.7 %collective-permute-start.6 = (f32[28,128]{1,0:T(8,128)S(1)}, f32[28,128]{1,0:T(8,128)S(1)}, u32[]{:S(2)}, u32[]{:S(2)}) collective-permute-start(f32[28,128]{1,0:T(8,128)S(1)} %get-tuple-element.83.refs_12_.refs_5_), channel_id=1, source_target_pairs={{1,0},{0,1},{3,2},{2,3},{5,4},{4,5},{7,6},{6,7},{9,8},{8,9},{11,10... | collective-permute-start | bytes 43016 | tf_op jit(solution)/shard_map/ppermute | solution.py:662
  12.4 0.5 %collective-permute-start.8 = (f32[24,128]{1,0:T(8,128)S(1)}, f32[24,128]{1,0:T(8,128)S(1)}, u32[]{:S(2)}, u32[]{:S(2)}) collective-permute-start(f32[24,128]{1,0:T(8,128)S(1)} %get-tuple-element.85), channel_id=1, source_target_pairs={{0,2},{1,3},{2,0},{3,1},{4,6},{5,7},{6,4},{7,5},{8,10},{9,11},{10,... | collective-permute-start | bytes 36872 | tf_op jit(solution)/shard_map/ppermute | solution.py:657
  13.0 0.5 %shard_map.170 = (f32[320,128]{1,0:T(8,128)S(1)}, f32[160,128]{1,0:T(8,128)S(1)}) custom-call(f32[320,128]{1,0:T(8,128)S(1)} %get-tuple-element.79.cur_ref._.refs_0_.refs_1_, f32[8,128]{1,0:T(8,128)S(1)} %get-tuple-element.67.material_ref.refs_5_, bf16[2,640,384]{2,1,0:T(8,128)(2,1)S(1)} %get-tuple-element.68.own_ref, ...), custom_call_target="tpu_custom_call" | custom-call | tf_op jit(solution)/shard_map/pallas_call | solution.py:630
  14.1 0.6 %shard_map.173 = (f32[320,128]{1,0:T(8,128)S(1)}, f32[64,128]{1,0:T(8,128)S(1)}, f32[28,128]{1,0:T(8,128)S(1)}) custom-call(f32[320,128]{1,0:T(8,128)S(1)} %get-tuple-element.79.cur_ref._.refs_0_.refs_1_, f32[320,128]{1,0:T(8,128)S(1)} %get-tuple-element.61.cur_ref.refs_0_.refs_1_, f32[320,128]{1,0:T(8,128)S(1)} %get-tuple-element.66.refs_2_, ...), custom_call_target="tpu_custom_call" | custom-call | tf_op jit(solution)/shard_map/pallas_call | solution.py:630
  14.7 1.7 %collective-permute-start.10 = (f32[64,128]{1,0:T(8,128)S(1)}, f32[64,128]{1,0:T(8,128)S(1)}, u32[]{:S(2)}, u32[]{:S(2)}) collective-permute-start(f32[64,128]{1,0:T(8,128)S(1)} %get-tuple-element.94), channel_id=1, source_target_pairs={{0,1},{1,0},{2,4},{3,5},{4,2},{5,3},{6,8},{7,9},{8,6},{9,7},{10,12... | collective-permute-start | bytes 98312 | tf_op jit(solution)/shard_map/ppermute | solution.py:657
  17.7 0.5 %shard_map.174 = (f32[320,128]{1,0:T(8,128)S(1)}, f32[160,128]{1,0:T(8,128)S(1)}) custom-call(f32[320,128]{1,0:T(8,128)S(1)} %get-tuple-element.91.cur_ref.refs_0_.refs_1_, f32[8,128]{1,0:T(8,128)S(1)} %get-tuple-element.67.material_ref.refs_5_, bf16[2,640,384]{2,1,0:T(8,128)(2,1)S(1)} %get-tuple-element.68.own_ref, ...), custom_call_target="tpu_custom_call" | custom-call | tf_op jit(solution)/shard_map/pallas_call | solution.py:630
  18.2 0.6 %collective-permute-done.14.refs_10_ = f32[16,128]{1,0:T(8,128)S(1)} collective-permute-done((f32[16,128]{1,0:T(8,128)S(1)}, f32[16,128]{1,0:T(8,128)S(1)}, u32[]{:S(2)}, u32[]{:S(2)}) %collective-permute-start.14) | collective-permute-done | bytes 8224 | tf_op jit(solution)/shard_map/ppermute | solution.py:657
  18.8 1.3 %collective-permute-done.11.refs_7_.refs_8_ = f32[28,128]{1,0:T(8,128)S(1)} collective-permute-done((f32[28,128]{1,0:T(8,128)S(1)}, f32[28,128]{1,0:T(8,128)S(1)}, u32[]{:S(2)}, u32[]{:S(2)}) %collective-permute-start.11) | collective-permute-done | bytes 14368 | tf_op jit(solution)/shard_map/ppermute | solution.py:662
  20.2 0.6 %shard_map.176 = (f32[320,128]{1,0:T(8,128)S(1)}, f32[64,128]{1,0:T(8,128)S(1)}, f32[28,128]{1,0:T(8,128)S(1)}) custom-call(f32[320,128]{1,0:T(8,128)S(1)} %get-tuple-element.91.cur_ref.refs_0_.refs_1_, f32[320,128]{1,0:T(8,128)S(1)} %get-tuple-element.79.cur_ref._.refs_0_.refs_1_, f32[320,128]{1,0:T(8,128)S(1)} %get-tuple-element.66.refs_2_, ...), custom_call_target="tpu_custom_call" | custom-call | tf_op jit(solution)/shard_map/pallas_call | solution.py:630
  21.2 1.6 %collective-permute-start.16 = (f32[28,128]{1,0:T(8,128)S(1)}, f32[28,128]{1,0:T(8,128)S(1)}, u32[]{:S(2)}, u32[]{:S(2)}) collective-permute-start(f32[28,128]{1,0:T(8,128)S(1)} %get-tuple-element.103.refs_9_.refs_12_), channel_id=1, source_target_pairs={{1,0},{0,1},{3,2},{2,3},{5,4},{4,5},{7,6},{6,7},{9,8},{8,9},{11,10... | collective-permute-start | bytes 43016 | tf_op jit(solution)/shard_map/ppermute | solution.py:662
  23.2 0.5 %collective-permute-start.18 = (f32[24,128]{1,0:T(8,128)S(1)}, f32[24,128]{1,0:T(8,128)S(1)}, u32[]{:S(2)}, u32[]{:S(2)}) collective-permute-start(f32[24,128]{1,0:T(8,128)S(1)} %get-tuple-element.105), channel_id=1, source_target_pairs={{0,2},{1,3},{2,0},{3,1},{4,6},{5,7},{6,4},{7,5},{8,10},{9,11},{10,... | collective-permute-start | bytes 36872 | tf_op jit(solution)/shard_map/ppermute | solution.py:657
  23.7 0.5 %shard_map.177 = (f32[320,128]{1,0:T(8,128)S(1)}, f32[160,128]{1,0:T(8,128)S(1)}) custom-call(f32[320,128]{1,0:T(8,128)S(1)} %get-tuple-element.99.cur_ref.refs_0_, f32[8,128]{1,0:T(8,128)S(1)} %get-tuple-element.67.material_ref.refs_5_, bf16[2,640,384]{2,1,0:T(8,128)(2,1)S(1)} %get-tuple-element.68.own_ref, bf16[160,256]{1,0:T(8,128)(2,1)S(1)} %get-tuple-element.69.touch_ref), custom_call_target="tpu_custom_call" | custom-call | tf_op jit(solution)/shard_map/pallas_call | solution.py:630
  25.0 0.8 %collective-permute-start.20 = (f32[2,128]{1,0:T(2,128)S(1)}, f32[2,128]{1,0:T(2,128)S(1)}, u32[]{:S(2)}, u32[]{:S(2)}) collective-permute-start(f32[2,128]{1,0:T(2,128)S(1)} %get-tuple-element.115), channel_id=1, source_target_pairs={{0,4},{1,5},{2,6},{3,7},{4,0},{5,1},{6,2},{7,3},{8,12},{9,13},{10,... | collective-permute-start | bytes 3080 | tf_op jit(solution)/shard_map/ppermute | solution.py:657
  25.9 1.2 %collective-permute-start.21 = (f32[2,128]{1,0:T(2,128)S(1)}, f32[2,128]{1,0:T(2,128)S(1)}, u32[]{:S(2)}, u32[]{:S(2)}) collective-permute-start(f32[2,128]{1,0:T(2,128)S(1)} %get-tuple-element.116), channel_id=1, source_target_pairs={{0,1},{1,0},{2,4},{3,5},{4,2},{5,3},{6,8},{7,9},{8,6},{9,7},{10,12... | collective-permute-start | bytes 3080 | tf_op jit(solution)/shard_map/ppermute | solution.py:657
  27.6 1.4 %shard_map.181 = (f32[3,17,4,128]{3,2,1,0:T(4,128)}, f32[3,17,4,128]{3,2,1,0:T(4,128)}) custom-call(f32[320,128]{1,0:T(8,128)S(1)} %get-tuple-element.99.cur_ref.refs_0_, f32[320,128]{1,0:T(8,128)S(1)} %get-tuple-element.91.cur_ref.refs_0_.refs_1_, f32[320,128]{1,0:T(8,128)S(1)} %get-tuple-element.66.refs_2_, f32[320,128]{1,0:T(8,128)S(1)} %get-tuple-element.100.refs_3_, ...), custom_call_target="tpu_custom_call" | custom-call | tf_op jit(solution)/shard_map/pallas_call | solution.py:630
  29.4 0.6 %shard_map.182 = f32[2,128]{1,0:T(2,128)} custom-call(f32[2,128]{1,0:T(2,128)S(1)} %get-tuple-element.111.refs_16_.refs_0_, f32[2,128]{1,0:T(2,128)S(1)} %collective-permute-done.20.refs_1_, f32[2,128]{1,0:T(2,128)S(1)} %collective-permute-done.21.refs_2_, f32[2,128]{1,0:T(2,128)S(1)} %collective-permute-done.22.refs_3_, ...), custom_call_target="tpu_custom_call" | custom-call | tf_op jit(solution)/shard_map/pallas_call | solution.py:630
  (41 shorter events, 5.3 us)
Async XLA Ops:
  2.6 6.8 %collective-permute-start = (f32[64,128]{1,0:T(8,128)S(1)}, f32[64,128]{1,0:T(8,128)S(1)}, u32[]{:S(2)}, u32[]{:S(2)}) collective-permute-start(f32[64,128]{1,0:T(8,128)S(1)} %get-tuple-element.72), channel_id=1, source_target_pairs={{0,1},{1,0},{2,4},{3,5},{4,2},{5,3},{6,8},{7,9},{8,6},{9,7},{10,12... | collective-permute-start | bytes 98312 | tf_op jit(solution)/shard_map/ppermute | solution.py:657
  5.6 3.8 %collective-permute-start.1 = (f32[40,128]{1,0:T(8,128)S(1)}, f32[40,128]{1,0:T(8,128)S(1)}, u32[]{:S(2)}, u32[]{:S(2)}) collective-permute-start(f32[40,128]{1,0:T(8,128)S(1)} %get-tuple-element.73.refs_12_.refs_13_.refs_3_), channel_id=1, source_target_pairs={{1,0},{0,1},{3,2},{2,3},{5,4},{4,5},{7,6},{6,7},{9,8},{8,9},{11,10... | collective-permute-start | bytes 61448 | tf_op jit(solution)/shard_map/ppermute | solution.py:662
  5.7 2.8 %collective-permute-start.2 = (f32[24,128]{1,0:T(8,128)S(1)}, f32[24,128]{1,0:T(8,128)S(1)}, u32[]{:S(2)}, u32[]{:S(2)}) collective-permute-start(f32[24,128]{1,0:T(8,128)S(1)} %get-tuple-element.74), channel_id=1, source_target_pairs={{0,2},{1,3},{2,0},{3,1},{4,6},{5,7},{6,4},{7,5},{8,10},{9,11},{10,... | collective-permute-start | bytes 36872 | tf_op jit(solution)/shard_map/ppermute | solution.py:657
  7.0 1.6 %collective-permute-start.3 = (f32[24,128]{1,0:T(8,128)S(1)}, f32[24,128]{1,0:T(8,128)S(1)}, u32[]{:S(2)}, u32[]{:S(2)}) collective-permute-start(f32[24,128]{1,0:T(8,128)S(1)} %get-tuple-element.75), channel_id=1, source_target_pairs={{0,2},{1,3},{2,0},{3,1},{4,6},{5,7},{6,4},{7,5},{8,10},{9,11},{10,... | collective-permute-start | bytes 36872 | tf_op jit(solution)/shard_map/ppermute | solution.py:657
  7.0 1.5 %collective-permute-start.4 = (f32[16,128]{1,0:T(8,128)S(1)}, f32[16,128]{1,0:T(8,128)S(1)}, u32[]{:S(2)}, u32[]{:S(2)}) collective-permute-start(f32[16,128]{1,0:T(8,128)S(1)} %get-tuple-element.76), channel_id=1, source_target_pairs={{0,2},{1,3},{2,0},{3,1},{4,6},{5,7},{6,4},{7,5},{8,10},{9,11},{10,... | collective-permute-start | bytes 24584 | tf_op jit(solution)/shard_map/ppermute | solution.py:657
  10.0 4.2 %collective-permute-start.5 = (f32[64,128]{1,0:T(8,128)S(1)}, f32[64,128]{1,0:T(8,128)S(1)}, u32[]{:S(2)}, u32[]{:S(2)}) collective-permute-start(f32[64,128]{1,0:T(8,128)S(1)} %get-tuple-element.82), channel_id=1, source_target_pairs={{0,1},{1,0},{2,4},{3,5},{4,2},{5,3},{6,8},{7,9},{8,6},{9,7},{10,12... | collective-permute-start | bytes 98312 | tf_op jit(solution)/shard_map/ppermute | solution.py:657
  10.4 3.8 %collective-permute-start.6 = (f32[28,128]{1,0:T(8,128)S(1)}, f32[28,128]{1,0:T(8,128)S(1)}, u32[]{:S(2)}, u32[]{:S(2)}) collective-permute-start(f32[28,128]{1,0:T(8,128)S(1)} %get-tuple-element.83.refs_12_.refs_5_), channel_id=1, source_target_pairs={{1,0},{0,1},{3,2},{2,3},{5,4},{4,5},{7,6},{6,7},{9,8},{8,9},{11,10... | collective-permute-start | bytes 43016 | tf_op jit(solution)/shard_map/ppermute | solution.py:662
  12.4 1.7 %collective-permute-start.7 = (f32[24,128]{1,0:T(8,128)S(1)}, f32[24,128]{1,0:T(8,128)S(1)}, u32[]{:S(2)}, u32[]{:S(2)}) collective-permute-start(f32[24,128]{1,0:T(8,128)S(1)} %get-tuple-element.84), channel_id=1, source_target_pairs={{0,2},{1,3},{2,0},{3,1},{4,6},{5,7},{6,4},{7,5},{8,10},{9,11},{10,... | collective-permute-start | bytes 36872 | tf_op jit(solution)/shard_map/ppermute | solution.py:657
  12.4 1.7 %collective-permute-start.8 = (f32[24,128]{1,0:T(8,128)S(1)}, f32[24,128]{1,0:T(8,128)S(1)}, u32[]{:S(2)}, u32[]{:S(2)}) collective-permute-start(f32[24,128]{1,0:T(8,128)S(1)} %get-tuple-element.85), channel_id=1, source_target_pairs={{0,2},{1,3},{2,0},{3,1},{4,6},{5,7},{6,4},{7,5},{8,10},{9,11},{10,... | collective-permute-start | bytes 36872 | tf_op jit(solution)/shard_map/ppermute | solution.py:657
  12.9 1.2 %collective-permute-start.9 = (f32[16,128]{1,0:T(8,128)S(1)}, f32[16,128]{1,0:T(8,128)S(1)}, u32[]{:S(2)}, u32[]{:S(2)}) collective-permute-start(f32[16,128]{1,0:T(8,128)S(1)} %get-tuple-element.86), channel_id=1, source_target_pairs={{0,2},{1,3},{2,0},{3,1},{4,6},{5,7},{6,4},{7,5},{8,10},{9,11},{10,... | collective-permute-start | bytes 24584 | tf_op jit(solution)/shard_map/ppermute | solution.py:657
  14.7 5.4 %collective-permute-start.10 = (f32[64,128]{1,0:T(8,128)S(1)}, f32[64,128]{1,0:T(8,128)S(1)}, u32[]{:S(2)}, u32[]{:S(2)}) collective-permute-start(f32[64,128]{1,0:T(8,128)S(1)} %get-tuple-element.94), channel_id=1, source_target_pairs={{0,1},{1,0},{2,4},{3,5},{4,2},{5,3},{6,8},{7,9},{8,6},{9,7},{10,12... | collective-permute-start | bytes 98312 | tf_op jit(solution)/shard_map/ppermute | solution.py:657
  16.4 3.7 %collective-permute-start.11 = (f32[28,128]{1,0:T(8,128)S(1)}, f32[28,128]{1,0:T(8,128)S(1)}, u32[]{:S(2)}, u32[]{:S(2)}) collective-permute-start(f32[28,128]{1,0:T(8,128)S(1)} %get-tuple-element.95.refs_12_.refs_7_), channel_id=1, source_target_pairs={{1,0},{0,1},{3,2},{2,3},{5,4},{4,5},{7,6},{6,7},{9,8},{8,9},{11,10... | collective-permute-start | bytes 43016 | tf_op jit(solution)/shard_map/ppermute | solution.py:662
  17.1 1.7 %collective-permute-start.12 = (f32[24,128]{1,0:T(8,128)S(1)}, f32[24,128]{1,0:T(8,128)S(1)}, u32[]{:S(2)}, u32[]{:S(2)}) collective-permute-start(f32[24,128]{1,0:T(8,128)S(1)} %get-tuple-element.96), channel_id=1, source_target_pairs={{0,2},{1,3},{2,0},{3,1},{4,6},{5,7},{6,4},{7,5},{8,10},{9,11},{10,... | collective-permute-start | bytes 36872 | tf_op jit(solution)/shard_map/ppermute | solution.py:657
  17.1 1.7 %collective-permute-start.13 = (f32[24,128]{1,0:T(8,128)S(1)}, f32[24,128]{1,0:T(8,128)S(1)}, u32[]{:S(2)}, u32[]{:S(2)}) collective-permute-start(f32[24,128]{1,0:T(8,128)S(1)} %get-tuple-element.97), channel_id=1, source_target_pairs={{0,2},{1,3},{2,0},{3,1},{4,6},{5,7},{6,4},{7,5},{8,10},{9,11},{10,... | collective-permute-start | bytes 36872 | tf_op jit(solution)/shard_map/ppermute | solution.py:657
  17.6 1.2 %collective-permute-start.14 = (f32[16,128]{1,0:T(8,128)S(1)}, f32[16,128]{1,0:T(8,128)S(1)}, u32[]{:S(2)}, u32[]{:S(2)}) collective-permute-start(f32[16,128]{1,0:T(8,128)S(1)} %get-tuple-element.98), channel_id=1, source_target_pairs={{0,2},{1,3},{2,0},{3,1},{4,6},{5,7},{6,4},{7,5},{8,10},{9,11},{10,... | collective-permute-start | bytes 24584 | tf_op jit(solution)/shard_map/ppermute | solution.py:657
  20.7 4.2 %collective-permute-start.15 = (f32[64,128]{1,0:T(8,128)S(1)}, f32[64,128]{1,0:T(8,128)S(1)}, u32[]{:S(2)}, u32[]{:S(2)}) collective-permute-start(f32[64,128]{1,0:T(8,128)S(1)} %get-tuple-element.102), channel_id=1, source_target_pairs={{0,1},{1,0},{2,4},{3,5},{4,2},{5,3},{6,8},{7,9},{8,6},{9,7},{10,12... | collective-permute-start | bytes 98312 | tf_op jit(solution)/shard_map/ppermute | solution.py:657
  21.2 3.7 %collective-permute-start.16 = (f32[28,128]{1,0:T(8,128)S(1)}, f32[28,128]{1,0:T(8,128)S(1)}, u32[]{:S(2)}, u32[]{:S(2)}) collective-permute-start(f32[28,128]{1,0:T(8,128)S(1)} %get-tuple-element.103.refs_9_.refs_12_), channel_id=1, source_target_pairs={{1,0},{0,1},{3,2},{2,3},{5,4},{4,5},{7,6},{6,7},{9,8},{8,9},{11,10... | collective-permute-start | bytes 43016 | tf_op jit(solution)/shard_map/ppermute | solution.py:662
  23.1 1.7 %collective-permute-start.17 = (f32[24,128]{1,0:T(8,128)S(1)}, f32[24,128]{1,0:T(8,128)S(1)}, u32[]{:S(2)}, u32[]{:S(2)}) collective-permute-start(f32[24,128]{1,0:T(8,128)S(1)} %get-tuple-element.104), channel_id=1, source_target_pairs={{0,2},{1,3},{2,0},{3,1},{4,6},{5,7},{6,4},{7,5},{8,10},{9,11},{10,... | collective-permute-start | bytes 36872 | tf_op jit(solution)/shard_map/ppermute | solution.py:657
  23.2 1.7 %collective-permute-start.18 = (f32[24,128]{1,0:T(8,128)S(1)}, f32[24,128]{1,0:T(8,128)S(1)}, u32[]{:S(2)}, u32[]{:S(2)}) collective-permute-start(f32[24,128]{1,0:T(8,128)S(1)} %get-tuple-element.105), channel_id=1, source_target_pairs={{0,2},{1,3},{2,0},{3,1},{4,6},{5,7},{6,4},{7,5},{8,10},{9,11},{10,... | collective-permute-start | bytes 36872 | tf_op jit(solution)/shard_map/ppermute | solution.py:657
  23.7 1.2 %collective-permute-start.19 = (f32[16,128]{1,0:T(8,128)S(1)}, f32[16,128]{1,0:T(8,128)S(1)}, u32[]{:S(2)}, u32[]{:S(2)}) collective-permute-start(f32[16,128]{1,0:T(8,128)S(1)} %get-tuple-element.106), channel_id=1, source_target_pairs={{0,2},{1,3},{2,0},{3,1},{4,6},{5,7},{6,4},{7,5},{8,10},{9,11},{10,... | collective-permute-start | bytes 24584 | tf_op jit(solution)/shard_map/ppermute | solution.py:657
  25.0 4.0 %collective-permute-start.20 = (f32[2,128]{1,0:T(2,128)S(1)}, f32[2,128]{1,0:T(2,128)S(1)}, u32[]{:S(2)}, u32[]{:S(2)}) collective-permute-start(f32[2,128]{1,0:T(2,128)S(1)} %get-tuple-element.115), channel_id=1, source_target_pairs={{0,4},{1,5},{2,6},{3,7},{4,0},{5,1},{6,2},{7,3},{8,12},{9,13},{10,... | collective-permute-start | bytes 3080 | tf_op jit(solution)/shard_map/ppermute | solution.py:657
  25.9 3.6 %collective-permute-start.21 = (f32[2,128]{1,0:T(2,128)S(1)}, f32[2,128]{1,0:T(2,128)S(1)}, u32[]{:S(2)}, u32[]{:S(2)}) collective-permute-start(f32[2,128]{1,0:T(2,128)S(1)} %get-tuple-element.116), channel_id=1, source_target_pairs={{0,1},{1,0},{2,4},{3,5},{4,2},{5,3},{6,8},{7,9},{8,6},{9,7},{10,12... | collective-permute-start | bytes 3080 | tf_op jit(solution)/shard_map/ppermute | solution.py:657
  27.1 2.3 %collective-permute-start.22 = (f32[2,128]{1,0:T(2,128)S(1)}, f32[2,128]{1,0:T(2,128)S(1)}, u32[]{:S(2)}, u32[]{:S(2)}) collective-permute-start(f32[2,128]{1,0:T(2,128)S(1)} %get-tuple-element.117), channel_id=1, source_target_pairs={{0,2},{1,3},{2,0},{3,1},{4,8},{5,9},{6,10},{7,11},{8,4},{9,5},{10,... | collective-permute-start | bytes 3080 | tf_op jit(solution)/shard_map/ppermute | solution.py:657
  27.2 2.2 %collective-permute-start.23 = (f32[2,128]{1,0:T(2,128)S(1)}, f32[2,128]{1,0:T(2,128)S(1)}, u32[]{:S(2)}, u32[]{:S(2)}) collective-permute-start(f32[2,128]{1,0:T(2,128)S(1)} %get-tuple-element.118), channel_id=1, source_target_pairs={{0,2},{1,3},{2,0},{3,1},{4,6},{5,7},{6,4},{7,5},{8,10},{9,11},{10,... | collective-permute-start | bytes 3080 | tf_op jit(solution)/shard_map/ppermute | solution.py:657

commit v20 on v19

--- a/solution.py
+++ b/solution.py
@@ -294,11 +294,6 @@
     out_ref[pl.ds(4 + x, 3, stride=8), :] = first[:3]
 
 
-def select_messages(parity, left, right):
-    even = parity == 0
-    return jnp.where(even, right, left), jnp.where(even, left, right)
-
-
 def material_rows(lame_ref, shear_ref):
     y_elems, z_elems = lame_ref.shape
     both = jnp.concatenate([lame_ref[...], shear_ref[...]], axis=0)
@@ -361,8 +356,8 @@
     *refs,
 ):
     later_hbm, refs = refs[:LATER], refs[LATER:]
-    cur_ref, *even_refs, odd_ref, fault_out_ref, material_ref = refs[:7]
-    later_refs, refs = refs[7 : 7 + LATER], refs[7 + LATER :]
+    cur_ref, odd_ref, fault_out_ref, material_ref = refs[:4]
+    later_refs, refs = refs[4 : 4 + LATER], refs[4 + LATER :]
     scratch, now_ref, flags_ref, weak_ref, lame_ref, shear_ref, sems = refs
     copies = start_copies(
         [
@@ -379,7 +374,6 @@
     edge_ref = later_refs[0]
     y_elems, z_elems = lame_ref.shape
     lanes = y_elems * z_elems
-    parity = lax.axis_index("dom") % 2
     gather = gather_table(lanes, z_elems)
     fault = fault_table(lanes, z_elems)
     scratch[...] = jnp.zeros_like(scratch)
@@ -403,12 +397,13 @@
     planes = [cur[x * PLANE : (x + 1) * PLANE] for x in range(4)]
     for x in range(4):
         store_fault(fault_out_ref, x, planes[x], z_elems)
+    odd_ref[...] = cur[: 4 * BLOCK]
     copies[5].wait()
-    edge = dot(edge_ref[...], jnp.concatenate([stacked(p) for p in planes], axis=0))
-    right = edge_message(edge, lame_row, shear_row, z_elems)
-    message, odd_ref[...] = select_messages(parity, cur[: 4 * BLOCK], right)
-    for even_ref, at in zip(even_refs, (0, PARTS[0], PARTS[0] + PARTS[1])):
-        even_ref[...] = message[at : at + even_ref.shape[0]]
+
+    @pl.when(lax.axis_index("dom") % 2 == 1)
+    def _():
+        odd_ref[...] = edge_of(cur_ref, edge_ref, material_ref, z_elems)
+
     for copy in copies[6:]:
         copy.wait()
 
@@ -704,17 +699,27 @@
     assert len(later_used) == LATER
     first_out = kernel_call(
         first_kernel,
-        [field] + parts + [plane, (FAULT + 4 * steps, lanes), (8, lanes)]
+        [field, plane, (FAULT + 4 * steps, lanes), (8, lanes)]
         + [(t.shape, t.dtype) for t in later_used],
         (now, flags, weak_slope[0], lame_first[0], shear_modulus[0]) + later_used,
         scratch=[native],
         in_hbm=range(5 + LATER),
         kept=range(5, 5 + LATER),
     )
-    cur, *even, odd, fault_rows, material = first_out[:-LATER]
+    cur, odd, fault_rows, material = first_out[:-LATER]
     edge_table, following, rho, mass, own_table, far_table, touch_table, back = first_out[-LATER:-3]
     flags, stress, owner = first_out[-3:]
-    even_in, odd_in, fault_in = exchange(even, odd, fault_rows)
+
+    def on_chip(field):
+        return kernel_call(
+            on_chip_kernel,
+            parts,
+            [field, material, edge_table],
+            scratch=[pltpu.VMEM(plane, jnp.float32)],
+            z_elems=z_elems,
+        )
+
+    even_in, odd_in, fault_in = exchange(on_chip(cur), odd, fault_rows)
     first_fault, first_in = fault_rows, fault_in
     fol, minv = kernel_call(
         setup_kernel,
@@ -758,14 +763,7 @@
                 **static,
             )
             fol, cur, fault_rows = cur, new, new_fault
-            even = kernel_call(
-                on_chip_kernel,
-                parts,
-                [cur, material, edge_table],
-                scratch=[pltpu.VMEM(plane, jnp.float32)],
-                z_elems=z_elems,
-            )
-            even_in, odd_in, fault_in = exchange(even, odd, fault_rows)
+            even_in, odd_in, fault_in = exchange(on_chip(cur), odd, fault_rows)
         else:
             whole = (3, 4 * y_elems + 1, 4, lanes)
             known = seen[: len(seen) - len(fault_in)]

time: 30.3 us -> 30.2 us (level)
    ppermute x20, starting transfers between devices: 11.6 us -> 11.3 us  [swapped(): return lax.ppermute(block, ('dom', 'depth'), route)]
    pallas_call x17 -> x18, Pallas kernels: 9.8 us -> 10.1 us  [kernel_call(): pl.pallas_call(functools.partial(body, **static) if static else body, out...]
  transfers between devices with their start and end apart: 24 -> 24, of which waited for: 8 -> 8; matrix products, arithmetic and copies ran while one was open for 0% -> 0% of each run, Pallas kernels for 18% -> 19%
where the time goes in v20:
time: 30.2 us; the launch traced here: 30 us
  starting transfers between devices  15.1 us (50%)
  Pallas kernels  10.1 us (33%)
  waiting for transfers between devices  4.03 us (13%)
  between operations  0.76 us (3%)
    ppermute x20, starting transfers between devices, swapped(): return lax.ppermute(block, ('dom', 'depth'), route)  11.3 us
    pallas_call x18, Pallas kernels, kernel_call(): pl.pallas_call(functools.partial(body, **static) if static else body, out...  10.1 us
    ppermute x4, starting transfers between devices, from_behind(): lax.ppermute(block, axis, [((i - distance) % size, i) for i in range(size)])  3.78 us
    ppermute x4, waiting for transfers between devices, from_behind(): lax.ppermute(block, axis, [((i - distance) % size, i) for i in range(size)])  2.32 us
    ppermute x20, waiting for transfers between devices, swapped(): return lax.ppermute(block, ('dom', 'depth'), route)  1.7 us
  transfers between devices with their start and end apart: 24, of which 8 were waited for; matrix products, arithmetic and copies ran while one was open for 0% of the time, Pallas kernels for 19%

profile of v20, /device:TPU:0, one launch (start us, length us, event | category | flops | bytes accessed | tf_op | source)
XLA Modules:
  0.0 30.0 jit_solution(10514557412427321803)
XLA Ops:
  0.6 2.0 %shard_map.166 = (f32[320,128]{1,0:T(8,128)S(1)}, f32[64,128]{1,0:T(8,128)S(1)}, f32[40,128]{1,0:T(8,128)S(1)}, f32[8,128]{1,0:T(8,128)S(1)}, bf16[160,1024]{1,0...) custom-call(f32[3,17,4,128]{3,2,1,0:T(4,128)} %bitcast.11, ...), custom_call_target="tpu_custom_call" | custom-call | tf_op jit(solution)/shard_map/pallas_call | solution.py:625
  2.6 3.0 %collective-permute-start = (f32[64,128]{1,0:T(8,128)S(1)}, f32[64,128]{1,0:T(8,128)S(1)}, u32[]{:S(2)}, u32[]{:S(2)}) collective-permute-start(f32[64,128]{1,0:T(8,128)S(1)} %get-tuple-element.72), channel_id=1, source_target_pairs={{0,1},{1,0},{2,4},{3,5},{4,2},{5,3},{6,8},{7,9},{8,6},{9,7},{10,12... | collective-permute-start | bytes 98312 | tf_op jit(solution)/shard_map/ppermute | solution.py:652
  6.0 1.0 %collective-permute-start.2 = (f32[24,128]{1,0:T(8,128)S(1)}, f32[24,128]{1,0:T(8,128)S(1)}, u32[]{:S(2)}, u32[]{:S(2)}) collective-permute-start(f32[24,128]{1,0:T(8,128)S(1)} %get-tuple-element.75), channel_id=1, source_target_pairs={{0,2},{1,3},{2,0},{3,1},{4,6},{5,7},{6,4},{7,5},{8,10},{9,11},{10,... | collective-permute-start | bytes 36872 | tf_op jit(solution)/shard_map/ppermute | solution.py:652
  7.5 0.5 %shard_map.168 = (f32[320,128]{1,0:T(8,128)S(1)}, f32[160,128]{1,0:T(8,128)S(1)}) custom-call(f32[320,128]{1,0:T(8,128)S(1)} %get-tuple-element.61.cur_ref.refs_0_.refs_1_, f32[8,128]{1,0:T(8,128)S(1)} %get-tuple-element.67.material_ref.refs_5_, bf16[2,640,384]{2,1,0:T(8,128)(2,1)S(1)} %get-tuple-element.68.own_ref, ...), custom_call_target="tpu_custom_call" | custom-call | tf_op jit(solution)/shard_map/pallas_call | solution.py:625
  8.0 0.5 %shard_map.167 = (f32[320,128]{1,0:T(8,128)S(1)}, f32[320,128]{1,0:T(8,128)S(1)}) custom-call(f32[3,17,4,128]{3,2,1,0:T(4,128)S(1)} %get-tuple-element.62.next_ref, f32[17,4,128]{2,1,0:T(4,128)S(1)} %get-tuple-element.63.density_ref, f32[320,128]{1,0:T(8,128)S(1)} %get-tuple-element.64.mass_ref), custom_call_target="tpu_custom_call" | custom-call | tf_op jit(solution)/shard_map/pallas_call | solution.py:625
  8.6 0.8 %collective-permute-done.1.refs_7_.refs_11_.refs_4_ = f32[40,128]{1,0:T(8,128)S(1)} collective-permute-done((f32[40,128]{1,0:T(8,128)S(1)}, f32[40,128]{1,0:T(8,128)S(1)}, u32[]{:S(2)}, u32[]{:S(2)}) %collective-permute-start.1) | collective-permute-done | bytes 20512 | tf_op jit(solution)/shard_map/ppermute | solution.py:657
  9.4 0.6 %shard_map.170 = (f32[320,128]{1,0:T(8,128)S(1)}, f32[64,128]{1,0:T(8,128)S(1)}, f32[28,128]{1,0:T(8,128)S(1)}) custom-call(f32[320,128]{1,0:T(8,128)S(1)} %get-tuple-element.61.cur_ref.refs_0_.refs_1_, f32[320,128]{1,0:T(8,128)S(1)} %get-tuple-element.65.refs_1_, f32[320,128]{1,0:T(8,128)S(1)} %get-tuple-element.66.refs_2_, ...), custom_call_target="tpu_custom_call" | custom-call | tf_op jit(solution)/shard_map/pallas_call | solution.py:625
  10.4 1.7 %collective-permute-start.6 = (f32[28,128]{1,0:T(8,128)S(1)}, f32[28,128]{1,0:T(8,128)S(1)}, u32[]{:S(2)}, u32[]{:S(2)}) collective-permute-start(f32[28,128]{1,0:T(8,128)S(1)} %get-tuple-element.83.refs_12_.refs_5_), channel_id=1, source_target_pairs={{1,0},{0,1},{3,2},{2,3},{5,4},{4,5},{7,6},{6,7},{9,8},{8,9},{11,10... | collective-permute-start | bytes 43016 | tf_op jit(solution)/shard_map/ppermute | solution.py:657
  12.4 0.5 %collective-permute-start.8 = (f32[24,128]{1,0:T(8,128)S(1)}, f32[24,128]{1,0:T(8,128)S(1)}, u32[]{:S(2)}, u32[]{:S(2)}) collective-permute-start(f32[24,128]{1,0:T(8,128)S(1)} %get-tuple-element.85), channel_id=1, source_target_pairs={{0,2},{1,3},{2,0},{3,1},{4,6},{5,7},{6,4},{7,5},{8,10},{9,11},{10,... | collective-permute-start | bytes 36872 | tf_op jit(solution)/shard_map/ppermute | solution.py:652
  13.0 0.5 %shard_map.171 = (f32[320,128]{1,0:T(8,128)S(1)}, f32[160,128]{1,0:T(8,128)S(1)}) custom-call(f32[320,128]{1,0:T(8,128)S(1)} %get-tuple-element.79.cur_ref._.refs_0_.refs_1_, f32[8,128]{1,0:T(8,128)S(1)} %get-tuple-element.67.material_ref.refs_5_, bf16[2,640,384]{2,1,0:T(8,128)(2,1)S(1)} %get-tuple-element.68.own_ref, ...), custom_call_target="tpu_custom_call" | custom-call | tf_op jit(solution)/shard_map/pallas_call | solution.py:625
  14.1 0.6 %shard_map.174 = (f32[320,128]{1,0:T(8,128)S(1)}, f32[64,128]{1,0:T(8,128)S(1)}, f32[28,128]{1,0:T(8,128)S(1)}) custom-call(f32[320,128]{1,0:T(8,128)S(1)} %get-tuple-element.79.cur_ref._.refs_0_.refs_1_, f32[320,128]{1,0:T(8,128)S(1)} %get-tuple-element.61.cur_ref.refs_0_.refs_1_, f32[320,128]{1,0:T(8,128)S(1)} %get-tuple-element.66.refs_2_, ...), custom_call_target="tpu_custom_call" | custom-call | tf_op jit(solution)/shard_map/pallas_call | solution.py:625
  14.7 1.7 %collective-permute-start.10 = (f32[64,128]{1,0:T(8,128)S(1)}, f32[64,128]{1,0:T(8,128)S(1)}, u32[]{:S(2)}, u32[]{:S(2)}) collective-permute-start(f32[64,128]{1,0:T(8,128)S(1)} %get-tuple-element.94), channel_id=1, source_target_pairs={{0,1},{1,0},{2,4},{3,5},{4,2},{5,3},{6,8},{7,9},{8,6},{9,7},{10,12... | collective-permute-start | bytes 98312 | tf_op jit(solution)/shard_map/ppermute | solution.py:652
  17.1 0.5 %collective-permute-start.13 = (f32[24,128]{1,0:T(8,128)S(1)}, f32[24,128]{1,0:T(8,128)S(1)}, u32[]{:S(2)}, u32[]{:S(2)}) collective-permute-start(f32[24,128]{1,0:T(8,128)S(1)} %get-tuple-element.97), channel_id=1, source_target_pairs={{0,2},{1,3},{2,0},{3,1},{4,6},{5,7},{6,4},{7,5},{8,10},{9,11},{10,... | collective-permute-start | bytes 36872 | tf_op jit(solution)/shard_map/ppermute | solution.py:652
  17.7 0.5 %shard_map.175 = (f32[320,128]{1,0:T(8,128)S(1)}, f32[160,128]{1,0:T(8,128)S(1)}) custom-call(f32[320,128]{1,0:T(8,128)S(1)} %get-tuple-element.91.cur_ref.refs_0_.refs_1_, f32[8,128]{1,0:T(8,128)S(1)} %get-tuple-element.67.material_ref.refs_5_, bf16[2,640,384]{2,1,0:T(8,128)(2,1)S(1)} %get-tuple-element.68.own_ref, ...), custom_call_target="tpu_custom_call" | custom-call | tf_op jit(solution)/shard_map/pallas_call | solution.py:625
  18.2 0.6 %collective-permute-done.14.refs_10_ = f32[16,128]{1,0:T(8,128)S(1)} collective-permute-done((f32[16,128]{1,0:T(8,128)S(1)}, f32[16,128]{1,0:T(8,128)S(1)}, u32[]{:S(2)}, u32[]{:S(2)}) %collective-permute-start.14) | collective-permute-done | bytes 8224 | tf_op jit(solution)/shard_map/ppermute | solution.py:652
  18.8 1.3 %collective-permute-done.11.refs_7_.refs_8_ = f32[28,128]{1,0:T(8,128)S(1)} collective-permute-done((f32[28,128]{1,0:T(8,128)S(1)}, f32[28,128]{1,0:T(8,128)S(1)}, u32[]{:S(2)}, u32[]{:S(2)}) %collective-permute-start.11) | collective-permute-done | bytes 14368 | tf_op jit(solution)/shard_map/ppermute | solution.py:657
  20.2 0.6 %shard_map.177 = (f32[320,128]{1,0:T(8,128)S(1)}, f32[64,128]{1,0:T(8,128)S(1)}, f32[28,128]{1,0:T(8,128)S(1)}) custom-call(f32[320,128]{1,0:T(8,128)S(1)} %get-tuple-element.91.cur_ref.refs_0_.refs_1_, f32[320,128]{1,0:T(8,128)S(1)} %get-tuple-element.79.cur_ref._.refs_0_.refs_1_, f32[320,128]{1,0:T(8,128)S(1)} %get-tuple-element.66.refs_2_, ...), custom_call_target="tpu_custom_call" | custom-call | tf_op jit(solution)/shard_map/pallas_call | solution.py:625
  21.2 1.6 %collective-permute-start.16 = (f32[28,128]{1,0:T(8,128)S(1)}, f32[28,128]{1,0:T(8,128)S(1)}, u32[]{:S(2)}, u32[]{:S(2)}) collective-permute-start(f32[28,128]{1,0:T(8,128)S(1)} %get-tuple-element.103.refs_9_.refs_12_), channel_id=1, source_target_pairs={{1,0},{0,1},{3,2},{2,3},{5,4},{4,5},{7,6},{6,7},{9,8},{8,9},{11,10... | collective-permute-start | bytes 43016 | tf_op jit(solution)/shard_map/ppermute | solution.py:657
  23.2 0.5 %collective-permute-start.18 = (f32[24,128]{1,0:T(8,128)S(1)}, f32[24,128]{1,0:T(8,128)S(1)}, u32[]{:S(2)}, u32[]{:S(2)}) collective-permute-start(f32[24,128]{1,0:T(8,128)S(1)} %get-tuple-element.105), channel_id=1, source_target_pairs={{0,2},{1,3},{2,0},{3,1},{4,6},{5,7},{6,4},{7,5},{8,10},{9,11},{10,... | collective-permute-start | bytes 36872 | tf_op jit(solution)/shard_map/ppermute | solution.py:652
  23.7 0.5 %shard_map.178 = (f32[320,128]{1,0:T(8,128)S(1)}, f32[160,128]{1,0:T(8,128)S(1)}) custom-call(f32[320,128]{1,0:T(8,128)S(1)} %get-tuple-element.99.cur_ref.refs_0_, f32[8,128]{1,0:T(8,128)S(1)} %get-tuple-element.67.material_ref.refs_5_, bf16[2,640,384]{2,1,0:T(8,128)(2,1)S(1)} %get-tuple-element.68.own_ref, bf16[160,256]{1,0:T(8,128)(2,1)S(1)} %get-tuple-element.69.touch_ref), custom_call_target="tpu_custom_call" | custom-call | tf_op jit(solution)/shard_map/pallas_call | solution.py:625
  25.0 0.8 %collective-permute-start.20 = (f32[2,128]{1,0:T(2,128)S(1)}, f32[2,128]{1,0:T(2,128)S(1)}, u32[]{:S(2)}, u32[]{:S(2)}) collective-permute-start(f32[2,128]{1,0:T(2,128)S(1)} %get-tuple-element.115), channel_id=1, source_target_pairs={{0,4},{1,5},{2,6},{3,7},{4,0},{5,1},{6,2},{7,3},{8,12},{9,13},{10,... | collective-permute-start | bytes 3080 | tf_op jit(solution)/shard_map/ppermute | solution.py:652
  25.8 1.2 %collective-permute-start.21 = (f32[2,128]{1,0:T(2,128)S(1)}, f32[2,128]{1,0:T(2,128)S(1)}, u32[]{:S(2)}, u32[]{:S(2)}) collective-permute-start(f32[2,128]{1,0:T(2,128)S(1)} %get-tuple-element.116), channel_id=1, source_target_pairs={{0,1},{1,0},{2,4},{3,5},{4,2},{5,3},{6,8},{7,9},{8,6},{9,7},{10,12... | collective-permute-start | bytes 3080 | tf_op jit(solution)/shard_map/ppermute | solution.py:652
  27.6 1.4 %shard_map.182 = (f32[3,17,4,128]{3,2,1,0:T(4,128)}, f32[3,17,4,128]{3,2,1,0:T(4,128)}) custom-call(f32[320,128]{1,0:T(8,128)S(1)} %get-tuple-element.99.cur_ref.refs_0_, f32[320,128]{1,0:T(8,128)S(1)} %get-tuple-element.91.cur_ref.refs_0_.refs_1_, f32[320,128]{1,0:T(8,128)S(1)} %get-tuple-element.66.refs_2_, f32[320,128]{1,0:T(8,128)S(1)} %get-tuple-element.100.refs_3_, ...), custom_call_target="tpu_custom_call" | custom-call | tf_op jit(solution)/shard_map/pallas_call | solution.py:625
  29.4 0.6 %shard_map.183 = f32[2,128]{1,0:T(2,128)} custom-call(f32[2,128]{1,0:T(2,128)S(1)} %get-tuple-element.111.refs_16_.refs_0_, f32[2,128]{1,0:T(2,128)S(1)} %collective-permute-done.20.refs_1_, f32[2,128]{1,0:T(2,128)S(1)} %collective-permute-done.21.refs_2_, f32[2,128]{1,0:T(2,128)S(1)} %collective-permute-done.22.refs_3_, ...), custom_call_target="tpu_custom_call" | custom-call | tf_op jit(solution)/shard_map/pallas_call | solution.py:625
  (42 shorter events, 5.7 us)
Async XLA Ops:
  2.6 6.8 %collective-permute-start = (f32[64,128]{1,0:T(8,128)S(1)}, f32[64,128]{1,0:T(8,128)S(1)}, u32[]{:S(2)}, u32[]{:S(2)}) collective-permute-start(f32[64,128]{1,0:T(8,128)S(1)} %get-tuple-element.72), channel_id=1, source_target_pairs={{0,1},{1,0},{2,4},{3,5},{4,2},{5,3},{6,8},{7,9},{8,6},{9,7},{10,12... | collective-permute-start | bytes 98312 | tf_op jit(solution)/shard_map/ppermute | solution.py:652
  5.6 3.8 %collective-permute-start.1 = (f32[40,128]{1,0:T(8,128)S(1)}, f32[40,128]{1,0:T(8,128)S(1)}, u32[]{:S(2)}, u32[]{:S(2)}) collective-permute-start(f32[40,128]{1,0:T(8,128)S(1)} %get-tuple-element.73.refs_12_.refs_13_.refs_3_), channel_id=1, source_target_pairs={{1,0},{0,1},{3,2},{2,3},{5,4},{4,5},{7,6},{6,7},{9,8},{8,9},{11,10... | collective-permute-start | bytes 61448 | tf_op jit(solution)/shard_map/ppermute | solution.py:657
  6.0 2.5 %collective-permute-start.2 = (f32[24,128]{1,0:T(8,128)S(1)}, f32[24,128]{1,0:T(8,128)S(1)}, u32[]{:S(2)}, u32[]{:S(2)}) collective-permute-start(f32[24,128]{1,0:T(8,128)S(1)} %get-tuple-element.75), channel_id=1, source_target_pairs={{0,2},{1,3},{2,0},{3,1},{4,6},{5,7},{6,4},{7,5},{8,10},{9,11},{10,... | collective-permute-start | bytes 36872 | tf_op jit(solution)/shard_map/ppermute | solution.py:652
  7.0 1.6 %collective-permute-start.3 = (f32[24,128]{1,0:T(8,128)S(1)}, f32[24,128]{1,0:T(8,128)S(1)}, u32[]{:S(2)}, u32[]{:S(2)}) collective-permute-start(f32[24,128]{1,0:T(8,128)S(1)} %get-tuple-element.76), channel_id=1, source_target_pairs={{0,2},{1,3},{2,0},{3,1},{4,6},{5,7},{6,4},{7,5},{8,10},{9,11},{10,... | collective-permute-start | bytes 36872 | tf_op jit(solution)/shard_map/ppermute | solution.py:652
  7.0 1.5 %collective-permute-start.4 = (f32[16,128]{1,0:T(8,128)S(1)}, f32[16,128]{1,0:T(8,128)S(1)}, u32[]{:S(2)}, u32[]{:S(2)}) collective-permute-start(f32[16,128]{1,0:T(8,128)S(1)} %get-tuple-element.77), channel_id=1, source_target_pairs={{0,2},{1,3},{2,0},{3,1},{4,6},{5,7},{6,4},{7,5},{8,10},{9,11},{10,... | collective-permute-start | bytes 24584 | tf_op jit(solution)/shard_map/ppermute | solution.py:652
  10.0 4.2 %collective-permute-start.5 = (f32[64,128]{1,0:T(8,128)S(1)}, f32[64,128]{1,0:T(8,128)S(1)}, u32[]{:S(2)}, u32[]{:S(2)}) collective-permute-start(f32[64,128]{1,0:T(8,128)S(1)} %get-tuple-element.82), channel_id=1, source_target_pairs={{0,1},{1,0},{2,4},{3,5},{4,2},{5,3},{6,8},{7,9},{8,6},{9,7},{10,12... | collective-permute-start | bytes 98312 | tf_op jit(solution)/shard_map/ppermute | solution.py:652
  10.4 3.8 %collective-permute-start.6 = (f32[28,128]{1,0:T(8,128)S(1)}, f32[28,128]{1,0:T(8,128)S(1)}, u32[]{:S(2)}, u32[]{:S(2)}) collective-permute-start(f32[28,128]{1,0:T(8,128)S(1)} %get-tuple-element.83.refs_12_.refs_5_), channel_id=1, source_target_pairs={{1,0},{0,1},{3,2},{2,3},{5,4},{4,5},{7,6},{6,7},{9,8},{8,9},{11,10... | collective-permute-start | bytes 43016 | tf_op jit(solution)/shard_map/ppermute | solution.py:657
  12.4 1.7 %collective-permute-start.7 = (f32[24,128]{1,0:T(8,128)S(1)}, f32[24,128]{1,0:T(8,128)S(1)}, u32[]{:S(2)}, u32[]{:S(2)}) collective-permute-start(f32[24,128]{1,0:T(8,128)S(1)} %get-tuple-element.84), channel_id=1, source_target_pairs={{0,2},{1,3},{2,0},{3,1},{4,6},{5,7},{6,4},{7,5},{8,10},{9,11},{10,... | collective-permute-start | bytes 36872 | tf_op jit(solution)/shard_map/ppermute | solution.py:652
  12.4 1.7 %collective-permute-start.8 = (f32[24,128]{1,0:T(8,128)S(1)}, f32[24,128]{1,0:T(8,128)S(1)}, u32[]{:S(2)}, u32[]{:S(2)}) collective-permute-start(f32[24,128]{1,0:T(8,128)S(1)} %get-tuple-element.85), channel_id=1, source_target_pairs={{0,2},{1,3},{2,0},{3,1},{4,6},{5,7},{6,4},{7,5},{8,10},{9,11},{10,... | collective-permute-start | bytes 36872 | tf_op jit(solution)/shard_map/ppermute | solution.py:652
  12.9 1.2 %collective-permute-start.9 = (f32[16,128]{1,0:T(8,128)S(1)}, f32[16,128]{1,0:T(8,128)S(1)}, u32[]{:S(2)}, u32[]{:S(2)}) collective-permute-start(f32[16,128]{1,0:T(8,128)S(1)} %get-tuple-element.86), channel_id=1, source_target_pairs={{0,2},{1,3},{2,0},{3,1},{4,6},{5,7},{6,4},{7,5},{8,10},{9,11},{10,... | collective-permute-start | bytes 24584 | tf_op jit(solution)/shard_map/ppermute | solution.py:652
  14.7 5.4 %collective-permute-start.10 = (f32[64,128]{1,0:T(8,128)S(1)}, f32[64,128]{1,0:T(8,128)S(1)}, u32[]{:S(2)}, u32[]{:S(2)}) collective-permute-start(f32[64,128]{1,0:T(8,128)S(1)} %get-tuple-element.94), channel_id=1, source_target_pairs={{0,1},{1,0},{2,4},{3,5},{4,2},{5,3},{6,8},{7,9},{8,6},{9,7},{10,12... | collective-permute-start | bytes 98312 | tf_op jit(solution)/shard_map/ppermute | solution.py:652
  16.4 3.7 %collective-permute-start.11 = (f32[28,128]{1,0:T(8,128)S(1)}, f32[28,128]{1,0:T(8,128)S(1)}, u32[]{:S(2)}, u32[]{:S(2)}) collective-permute-start(f32[28,128]{1,0:T(8,128)S(1)} %get-tuple-element.95.refs_12_.refs_7_), channel_id=1, source_target_pairs={{1,0},{0,1},{3,2},{2,3},{5,4},{4,5},{7,6},{6,7},{9,8},{8,9},{11,10... | collective-permute-start | bytes 43016 | tf_op jit(solution)/shard_map/ppermute | solution.py:657
  17.1 1.7 %collective-permute-start.12 = (f32[24,128]{1,0:T(8,128)S(1)}, f32[24,128]{1,0:T(8,128)S(1)}, u32[]{:S(2)}, u32[]{:S(2)}) collective-permute-start(f32[24,128]{1,0:T(8,128)S(1)} %get-tuple-element.96), channel_id=1, source_target_pairs={{0,2},{1,3},{2,0},{3,1},{4,6},{5,7},{6,4},{7,5},{8,10},{9,11},{10,... | collective-permute-start | bytes 36872 | tf_op jit(solution)/shard_map/ppermute | solution.py:652
  17.1 1.7 %collective-permute-start.13 = (f32[24,128]{1,0:T(8,128)S(1)}, f32[24,128]{1,0:T(8,128)S(1)}, u32[]{:S(2)}, u32[]{:S(2)}) collective-permute-start(f32[24,128]{1,0:T(8,128)S(1)} %get-tuple-element.97), channel_id=1, source_target_pairs={{0,2},{1,3},{2,0},{3,1},{4,6},{5,7},{6,4},{7,5},{8,10},{9,11},{10,... | collective-permute-start | bytes 36872 | tf_op jit(solution)/shard_map/ppermute | solution.py:652
  17.6 1.2 %collective-permute-start.14 = (f32[16,128]{1,0:T(8,128)S(1)}, f32[16,128]{1,0:T(8,128)S(1)}, u32[]{:S(2)}, u32[]{:S(2)}) collective-permute-start(f32[16,128]{1,0:T(8,128)S(1)} %get-tuple-element.98), channel_id=1, source_target_pairs={{0,2},{1,3},{2,0},{3,1},{4,6},{5,7},{6,4},{7,5},{8,10},{9,11},{10,... | collective-permute-start | bytes 24584 | tf_op jit(solution)/shard_map/ppermute | solution.py:652
  20.7 4.2 %collective-permute-start.15 = (f32[64,128]{1,0:T(8,128)S(1)}, f32[64,128]{1,0:T(8,128)S(1)}, u32[]{:S(2)}, u32[]{:S(2)}) collective-permute-start(f32[64,128]{1,0:T(8,128)S(1)} %get-tuple-element.102), channel_id=1, source_target_pairs={{0,1},{1,0},{2,4},{3,5},{4,2},{5,3},{6,8},{7,9},{8,6},{9,7},{10,12... | collective-permute-start | bytes 98312 | tf_op jit(solution)/shard_map/ppermute | solution.py:652
  21.2 3.7 %collective-permute-start.16 = (f32[28,128]{1,0:T(8,128)S(1)}, f32[28,128]{1,0:T(8,128)S(1)}, u32[]{:S(2)}, u32[]{:S(2)}) collective-permute-start(f32[28,128]{1,0:T(8,128)S(1)} %get-tuple-element.103.refs_9_.refs_12_), channel_id=1, source_target_pairs={{1,0},{0,1},{3,2},{2,3},{5,4},{4,5},{7,6},{6,7},{9,8},{8,9},{11,10... | collective-permute-start | bytes 43016 | tf_op jit(solution)/shard_map/ppermute | solution.py:657
  23.1 1.7 %collective-permute-start.17 = (f32[24,128]{1,0:T(8,128)S(1)}, f32[24,128]{1,0:T(8,128)S(1)}, u32[]{:S(2)}, u32[]{:S(2)}) collective-permute-start(f32[24,128]{1,0:T(8,128)S(1)} %get-tuple-element.104), channel_id=1, source_target_pairs={{0,2},{1,3},{2,0},{3,1},{4,6},{5,7},{6,4},{7,5},{8,10},{9,11},{10,... | collective-permute-start | bytes 36872 | tf_op jit(solution)/shard_map/ppermute | solution.py:652
  23.2 1.7 %collective-permute-start.18 = (f32[24,128]{1,0:T(8,128)S(1)}, f32[24,128]{1,0:T(8,128)S(1)}, u32[]{:S(2)}, u32[]{:S(2)}) collective-permute-start(f32[24,128]{1,0:T(8,128)S(1)} %get-tuple-element.105), channel_id=1, source_target_pairs={{0,2},{1,3},{2,0},{3,1},{4,6},{5,7},{6,4},{7,5},{8,10},{9,11},{10,... | collective-permute-start | bytes 36872 | tf_op jit(solution)/shard_map/ppermute | solution.py:652
  23.6 1.2 %collective-permute-start.19 = (f32[16,128]{1,0:T(8,128)S(1)}, f32[16,128]{1,0:T(8,128)S(1)}, u32[]{:S(2)}, u32[]{:S(2)}) collective-permute-start(f32[16,128]{1,0:T(8,128)S(1)} %get-tuple-element.106), channel_id=1, source_target_pairs={{0,2},{1,3},{2,0},{3,1},{4,6},{5,7},{6,4},{7,5},{8,10},{9,11},{10,... | collective-permute-start | bytes 24584 | tf_op jit(solution)/shard_map/ppermute | solution.py:652
  25.0 4.0 %collective-permute-start.20 = (f32[2,128]{1,0:T(2,128)S(1)}, f32[2,128]{1,0:T(2,128)S(1)}, u32[]{:S(2)}, u32[]{:S(2)}) collective-permute-start(f32[2,128]{1,0:T(2,128)S(1)} %get-tuple-element.115), channel_id=1, source_target_pairs={{0,4},{1,5},{2,6},{3,7},{4,0},{5,1},{6,2},{7,3},{8,12},{9,13},{10,... | collective-permute-start | bytes 3080 | tf_op jit(solution)/shard_map/ppermute | solution.py:652
  25.8 3.6 %collective-permute-start.21 = (f32[2,128]{1,0:T(2,128)S(1)}, f32[2,128]{1,0:T(2,128)S(1)}, u32[]{:S(2)}, u32[]{:S(2)}) collective-permute-start(f32[2,128]{1,0:T(2,128)S(1)} %get-tuple-element.116), channel_id=1, source_target_pairs={{0,1},{1,0},{2,4},{3,5},{4,2},{5,3},{6,8},{7,9},{8,6},{9,7},{10,12... | collective-permute-start | bytes 3080 | tf_op jit(solution)/shard_map/ppermute | solution.py:652
  27.1 2.3 %collective-permute-start.22 = (f32[2,128]{1,0:T(2,128)S(1)}, f32[2,128]{1,0:T(2,128)S(1)}, u32[]{:S(2)}, u32[]{:S(2)}) collective-permute-start(f32[2,128]{1,0:T(2,128)S(1)} %get-tuple-element.117), channel_id=1, source_target_pairs={{0,2},{1,3},{2,0},{3,1},{4,8},{5,9},{6,10},{7,11},{8,4},{9,5},{10,... | collective-permute-start | bytes 3080 | tf_op jit(solution)/shard_map/ppermute | solution.py:652
  27.2 2.2 %collective-permute-start.23 = (f32[2,128]{1,0:T(2,128)S(1)}, f32[2,128]{1,0:T(2,128)S(1)}, u32[]{:S(2)}, u32[]{:S(2)}) collective-permute-start(f32[2,128]{1,0:T(2,128)S(1)} %get-tuple-element.118), channel_id=1, source_target_pairs={{0,2},{1,3},{2,0},{3,1},{4,6},{5,7},{6,4},{7,5},{8,10},{9,11},{10,... | collective-permute-start | bytes 3080 | tf_op jit(solution)/shard_map/ppermute | solution.py:652

commit v21 on v20

--- a/solution.py
+++ b/solution.py
@@ -13,7 +13,7 @@
 PATCH_DEV = 2
 REACH = 2
 PATCH_ROWS = 16
-LATER = 11
+LATER = 10
 FAULT = 24
 SENT_FAULT = 28
 PARTS = (24, 24, 16)
@@ -693,7 +693,7 @@
         return [swapped(part, 1, 0) for part in even], swapped(odd, 1, 1), faults
 
     later_used = (
-        edge_table, following, rho, mass, own_table, far_table, touch_table, back, flags,
+        edge_table, following, rho, mass, own_table, far_table, touch_table, flags,
         normal_stress[0], patch_owner,
     )
     assert len(later_used) == LATER
@@ -707,7 +707,7 @@
         kept=range(5, 5 + LATER),
     )
     cur, odd, fault_rows, material = first_out[:-LATER]
-    edge_table, following, rho, mass, own_table, far_table, touch_table, back = first_out[-LATER:-3]
+    edge_table, following, rho, mass, own_table, far_table, touch_table = first_out[-LATER:-3]
     flags, stress, owner = first_out[-3:]
 
     def on_chip(field):

time: 30.2 us -> 30.2 us (level)
  local copies, waits for them, and re-layouts: 0 us -> 0.45 us
    unnamed x0 -> x2, local copies, waits for them, and re-layouts: none -> 0.45 us
  transfers between devices with their start and end apart: 24 -> 24, of which waited for: 8 -> 6; matrix products, arithmetic and copies ran while one was open for 0% -> 0% of each run, Pallas kernels for 19% -> 19%
where the time goes in v21:
time: 30.2 us; the launch traced here: 29.9 us
  starting transfers between devices  14.9 us (49%)
  Pallas kernels  9.92 us (33%)
  waiting for transfers between devices  3.83 us (13%)
  between operations  0.8 us (3%)
  local copies, waits for them, and re-layouts  0.45 us (1%)
    ppermute x20, starting transfers between devices, swapped(): return lax.ppermute(block, ('dom', 'depth'), route)  11.2 us
    pallas_call x18, Pallas kernels, kernel_call(): pl.pallas_call(functools.partial(body, **static) if static else body, out...  9.92 us
    ppermute x4, starting transfers between devices, from_behind(): lax.ppermute(block, axis, [((i - distance) % size, i) for i in range(size)])  3.78 us
    ppermute x4, waiting for transfers between devices, from_behind(): lax.ppermute(block, axis, [((i - distance) % size, i) for i in range(size)])  2.25 us
    ppermute x20, waiting for transfers between devices, swapped(): return lax.ppermute(block, ('dom', 'depth'), route)  1.58 us
  transfers between devices with their start and end apart: 24, of which 6 were waited for; matrix products, arithmetic and copies ran while one was open for 0% of the time, Pallas kernels for 19%

profile of v21, /device:TPU:0, one launch (start us, length us, event | category | flops | bytes accessed | tf_op | source)
XLA Modules:
  0.0 29.9 jit_solution(12387214009337663670)
XLA Ops:
  0.6 1.8 %shard_map.166 = (f32[320,128]{1,0:T(8,128)S(1)}, f32[64,128]{1,0:T(8,128)S(1)}, f32[40,128]{1,0:T(8,128)S(1)}, f32[8,128]{1,0:T(8,128)S(1)}, bf16[160,1024]{1,0...) custom-call(f32[3,17,4,128]{3,2,1,0:T(4,128)} %bitcast.11, ...), custom_call_target="tpu_custom_call" | custom-call | tf_op jit(solution)/shard_map/pallas_call | solution.py:625
  2.4 3.0 %collective-permute-start = (f32[64,128]{1,0:T(8,128)S(1)}, f32[64,128]{1,0:T(8,128)S(1)}, u32[]{:S(2)}, u32[]{:S(2)}) collective-permute-start(f32[64,128]{1,0:T(8,128)S(1)} %get-tuple-element.71), channel_id=1, source_target_pairs={{0,1},{1,0},{2,4},{3,5},{4,2},{5,3},{6,8},{7,9},{8,6},{9,7},{10,12... | collective-permute-start | bytes 98312 | tf_op jit(solution)/shard_map/ppermute | solution.py:652
  5.8 1.0 %collective-permute-start.2 = (f32[24,128]{1,0:T(8,128)S(1)}, f32[24,128]{1,0:T(8,128)S(1)}, u32[]{:S(2)}, u32[]{:S(2)}) collective-permute-start(f32[24,128]{1,0:T(8,128)S(1)} %get-tuple-element.74), channel_id=1, source_target_pairs={{0,2},{1,3},{2,0},{3,1},{4,6},{5,7},{6,4},{7,5},{8,10},{9,11},{10,... | collective-permute-start | bytes 36872 | tf_op jit(solution)/shard_map/ppermute | solution.py:652
  7.3 0.5 %shard_map.168 = (f32[320,128]{1,0:T(8,128)S(1)}, f32[160,128]{1,0:T(8,128)S(1)}) custom-call(f32[320,128]{1,0:T(8,128)S(1)} %get-tuple-element.60.cur_ref.refs_0_.refs_1_, f32[8,128]{1,0:T(8,128)S(1)} %get-tuple-element.66.material_ref.refs_5_, bf16[2,640,384]{2,1,0:T(8,128)(2,1)S(1)} %get-tuple-element.67.own_ref, ...), custom_call_target="tpu_custom_call" | custom-call | tf_op jit(solution)/shard_map/pallas_call | solution.py:625
  7.8 0.5 %shard_map.167 = (f32[320,128]{1,0:T(8,128)S(1)}, f32[320,128]{1,0:T(8,128)S(1)}) custom-call(f32[3,17,4,128]{3,2,1,0:T(4,128)S(1)} %get-tuple-element.61.next_ref, f32[17,4,128]{2,1,0:T(4,128)S(1)} %get-tuple-element.62.density_ref, f32[320,128]{1,0:T(8,128)S(1)} %get-tuple-element.63.mass_ref), custom_call_target="tpu_custom_call" | custom-call | tf_op jit(solution)/shard_map/pallas_call | solution.py:625
  8.3 0.8 %collective-permute-done.1.refs_7_.refs_11_.refs_4_ = f32[40,128]{1,0:T(8,128)S(1)} collective-permute-done((f32[40,128]{1,0:T(8,128)S(1)}, f32[40,128]{1,0:T(8,128)S(1)}, u32[]{:S(2)}, u32[]{:S(2)}) %collective-permute-start.1) | collective-permute-done | bytes 20512 | tf_op jit(solution)/shard_map/ppermute | solution.py:657
  9.2 0.6 %shard_map.170 = (f32[320,128]{1,0:T(8,128)S(1)}, f32[64,128]{1,0:T(8,128)S(1)}, f32[28,128]{1,0:T(8,128)S(1)}) custom-call(f32[320,128]{1,0:T(8,128)S(1)} %get-tuple-element.60.cur_ref.refs_0_.refs_1_, f32[320,128]{1,0:T(8,128)S(1)} %get-tuple-element.64.refs_1_, f32[320,128]{1,0:T(8,128)S(1)} %get-tuple-element.65.refs_2_, ...), custom_call_target="tpu_custom_call" | custom-call | tf_op jit(solution)/shard_map/pallas_call | solution.py:625
  10.2 1.7 %collective-permute-start.6 = (f32[28,128]{1,0:T(8,128)S(1)}, f32[28,128]{1,0:T(8,128)S(1)}, u32[]{:S(2)}, u32[]{:S(2)}) collective-permute-start(f32[28,128]{1,0:T(8,128)S(1)} %get-tuple-element.82.refs_12_.refs_5_), channel_id=1, source_target_pairs={{1,0},{0,1},{3,2},{2,3},{5,4},{4,5},{7,6},{6,7},{9,8},{8,9},{11,10... | collective-permute-start | bytes 43016 | tf_op jit(solution)/shard_map/ppermute | solution.py:657
  12.2 0.5 %collective-permute-start.8 = (f32[24,128]{1,0:T(8,128)S(1)}, f32[24,128]{1,0:T(8,128)S(1)}, u32[]{:S(2)}, u32[]{:S(2)}) collective-permute-start(f32[24,128]{1,0:T(8,128)S(1)} %get-tuple-element.84), channel_id=1, source_target_pairs={{0,2},{1,3},{2,0},{3,1},{4,6},{5,7},{6,4},{7,5},{8,10},{9,11},{10,... | collective-permute-start | bytes 36872 | tf_op jit(solution)/shard_map/ppermute | solution.py:652
  12.8 0.5 %shard_map.171 = (f32[320,128]{1,0:T(8,128)S(1)}, f32[160,128]{1,0:T(8,128)S(1)}) custom-call(f32[320,128]{1,0:T(8,128)S(1)} %get-tuple-element.78.cur_ref._.refs_0_.refs_1_, f32[8,128]{1,0:T(8,128)S(1)} %get-tuple-element.66.material_ref.refs_5_, bf16[2,640,384]{2,1,0:T(8,128)(2,1)S(1)} %get-tuple-element.67.own_ref, ...), custom_call_target="tpu_custom_call" | custom-call | tf_op jit(solution)/shard_map/pallas_call | solution.py:625
  13.9 0.6 %shard_map.174 = (f32[320,128]{1,0:T(8,128)S(1)}, f32[64,128]{1,0:T(8,128)S(1)}, f32[28,128]{1,0:T(8,128)S(1)}) custom-call(f32[320,128]{1,0:T(8,128)S(1)} %get-tuple-element.78.cur_ref._.refs_0_.refs_1_, f32[320,128]{1,0:T(8,128)S(1)} %get-tuple-element.60.cur_ref.refs_0_.refs_1_, f32[320,128]{1,0:T(8,128)S(1)} %get-tuple-element.65.refs_2_, ...), custom_call_target="tpu_custom_call" | custom-call | tf_op jit(solution)/shard_map/pallas_call | solution.py:625
  14.5 1.7 %collective-permute-start.10 = (f32[64,128]{1,0:T(8,128)S(1)}, f32[64,128]{1,0:T(8,128)S(1)}, u32[]{:S(2)}, u32[]{:S(2)}) collective-permute-start(f32[64,128]{1,0:T(8,128)S(1)} %get-tuple-element.93), channel_id=1, source_target_pairs={{0,1},{1,0},{2,4},{3,5},{4,2},{5,3},{6,8},{7,9},{8,6},{9,7},{10,12... | collective-permute-start | bytes 98312 | tf_op jit(solution)/shard_map/ppermute | solution.py:652
  16.9 0.5 %collective-permute-start.13 = (f32[24,128]{1,0:T(8,128)S(1)}, f32[24,128]{1,0:T(8,128)S(1)}, u32[]{:S(2)}, u32[]{:S(2)}) collective-permute-start(f32[24,128]{1,0:T(8,128)S(1)} %get-tuple-element.96), channel_id=1, source_target_pairs={{0,2},{1,3},{2,0},{3,1},{4,6},{5,7},{6,4},{7,5},{8,10},{9,11},{10,... | collective-permute-start | bytes 36872 | tf_op jit(solution)/shard_map/ppermute | solution.py:652
  17.5 0.5 %shard_map.175 = (f32[320,128]{1,0:T(8,128)S(1)}, f32[160,128]{1,0:T(8,128)S(1)}) custom-call(f32[320,128]{1,0:T(8,128)S(1)} %get-tuple-element.90.cur_ref.refs_0_.refs_1_, f32[8,128]{1,0:T(8,128)S(1)} %get-tuple-element.66.material_ref.refs_5_, bf16[2,640,384]{2,1,0:T(8,128)(2,1)S(1)} %get-tuple-element.67.own_ref, ...), custom_call_target="tpu_custom_call" | custom-call | tf_op jit(solution)/shard_map/pallas_call | solution.py:625
  18.0 0.6 %collective-permute-done.14.refs_10_ = f32[16,128]{1,0:T(8,128)S(1)} collective-permute-done((f32[16,128]{1,0:T(8,128)S(1)}, f32[16,128]{1,0:T(8,128)S(1)}, u32[]{:S(2)}, u32[]{:S(2)}) %collective-permute-start.14) | collective-permute-done | bytes 8224 | tf_op jit(solution)/shard_map/ppermute | solution.py:652
  18.6 1.3 %collective-permute-done.11.refs_7_.refs_8_ = f32[28,128]{1,0:T(8,128)S(1)} collective-permute-done((f32[28,128]{1,0:T(8,128)S(1)}, f32[28,128]{1,0:T(8,128)S(1)}, u32[]{:S(2)}, u32[]{:S(2)}) %collective-permute-start.11) | collective-permute-done | bytes 14368 | tf_op jit(solution)/shard_map/ppermute | solution.py:657
  20.0 0.6 %shard_map.177 = (f32[320,128]{1,0:T(8,128)S(1)}, f32[64,128]{1,0:T(8,128)S(1)}, f32[28,128]{1,0:T(8,128)S(1)}) custom-call(f32[320,128]{1,0:T(8,128)S(1)} %get-tuple-element.90.cur_ref.refs_0_.refs_1_, f32[320,128]{1,0:T(8,128)S(1)} %get-tuple-element.78.cur_ref._.refs_0_.refs_1_, f32[320,128]{1,0:T(8,128)S(1)} %get-tuple-element.65.refs_2_, ...), custom_call_target="tpu_custom_call" | custom-call | tf_op jit(solution)/shard_map/pallas_call | solution.py:625
  21.0 1.6 %collective-permute-start.16 = (f32[28,128]{1,0:T(8,128)S(1)}, f32[28,128]{1,0:T(8,128)S(1)}, u32[]{:S(2)}, u32[]{:S(2)}) collective-permute-start(f32[28,128]{1,0:T(8,128)S(1)} %get-tuple-element.102.refs_9_.refs_12_), channel_id=1, source_target_pairs={{1,0},{0,1},{3,2},{2,3},{5,4},{4,5},{7,6},{6,7},{9,8},{8,9},{11,10... | collective-permute-start | bytes 43016 | tf_op jit(solution)/shard_map/ppermute | solution.py:657
  23.5 0.5 %shard_map.178 = (f32[320,128]{1,0:T(8,128)S(1)}, f32[160,128]{1,0:T(8,128)S(1)}) custom-call(f32[320,128]{1,0:T(8,128)S(1)} %get-tuple-element.98.cur_ref.refs_0_, f32[8,128]{1,0:T(8,128)S(1)} %get-tuple-element.66.material_ref.refs_5_, bf16[2,640,384]{2,1,0:T(8,128)(2,1)S(1)} %get-tuple-element.67.own_ref, bf16[160,256]{1,0:T(8,128)(2,1)S(1)} %get-tuple-element.68.touch_ref), custom_call_target="tpu_custom_call" | custom-call | tf_op jit(solution)/shard_map/pallas_call | solution.py:625
  25.0 0.8 %collective-permute-start.20 = (f32[2,128]{1,0:T(2,128)S(1)}, f32[2,128]{1,0:T(2,128)S(1)}, u32[]{:S(2)}, u32[]{:S(2)}) collective-permute-start(f32[2,128]{1,0:T(2,128)S(1)} %get-tuple-element.113), channel_id=1, source_target_pairs={{0,4},{1,5},{2,6},{3,7},{4,0},{5,1},{6,2},{7,3},{8,12},{9,13},{10,... | collective-permute-start | bytes 3080 | tf_op jit(solution)/shard_map/ppermute | solution.py:652
  25.8 1.1 %collective-permute-start.21 = (f32[2,128]{1,0:T(2,128)S(1)}, f32[2,128]{1,0:T(2,128)S(1)}, u32[]{:S(2)}, u32[]{:S(2)}) collective-permute-start(f32[2,128]{1,0:T(2,128)S(1)} %get-tuple-element.114), channel_id=1, source_target_pairs={{0,1},{1,0},{2,4},{3,5},{4,2},{5,3},{6,8},{7,9},{8,6},{9,7},{10,12... | collective-permute-start | bytes 3080 | tf_op jit(solution)/shard_map/ppermute | solution.py:652
  27.4 1.4 %shard_map.182 = (f32[3,17,4,128]{3,2,1,0:T(4,128)}, f32[3,17,4,128]{3,2,1,0:T(4,128)}) custom-call(f32[320,128]{1,0:T(8,128)S(1)} %get-tuple-element.98.cur_ref.refs_0_, f32[320,128]{1,0:T(8,128)S(1)} %get-tuple-element.90.cur_ref.refs_0_.refs_1_, f32[320,128]{1,0:T(8,128)S(1)} %get-tuple-element.65.refs_2_, f32[320,128]{1,0:T(8,128)S(1)} %get-tuple-element.99.refs_3_, ...), custom_call_target="tpu_custom_call" | custom-call | tf_op jit(solution)/shard_map/pallas_call | solution.py:625
  28.9 0.5 %collective-permute-done.21.refs_2_ = f32[2,128]{1,0:T(2,128)S(1)} collective-permute-done((f32[2,128]{1,0:T(2,128)S(1)}, f32[2,128]{1,0:T(2,128)S(1)}, u32[]{:S(2)}, u32[]{:S(2)}) %collective-permute-start.21) | collective-permute-done | bytes 1056 | tf_op jit(solution)/shard_map/ppermute | solution.py:652
  29.4 0.6 %shard_map.183 = f32[2,128]{1,0:T(2,128)} custom-call(f32[2,128]{1,0:T(2,128)S(1)} %get-tuple-element.109.refs_16_.refs_0_, f32[2,128]{1,0:T(2,128)S(1)} %collective-permute-done.20.refs_1_, f32[2,128]{1,0:T(2,128)S(1)} %collective-permute-done.21.refs_2_, f32[2,128]{1,0:T(2,128)S(1)} %collective-permute-done.22.refs_3_, ...), custom_call_target="tpu_custom_call" | custom-call | tf_op jit(solution)/shard_map/pallas_call | solution.py:625
  (44 shorter events, 6.0 us)
Async XLA Ops:
  2.4 6.8 %collective-permute-start = (f32[64,128]{1,0:T(8,128)S(1)}, f32[64,128]{1,0:T(8,128)S(1)}, u32[]{:S(2)}, u32[]{:S(2)}) collective-permute-start(f32[64,128]{1,0:T(8,128)S(1)} %get-tuple-element.71), channel_id=1, source_target_pairs={{0,1},{1,0},{2,4},{3,5},{4,2},{5,3},{6,8},{7,9},{8,6},{9,7},{10,12... | collective-permute-start | bytes 98312 | tf_op jit(solution)/shard_map/ppermute | solution.py:652
  5.4 3.8 %collective-permute-start.1 = (f32[40,128]{1,0:T(8,128)S(1)}, f32[40,128]{1,0:T(8,128)S(1)}, u32[]{:S(2)}, u32[]{:S(2)}) collective-permute-start(f32[40,128]{1,0:T(8,128)S(1)} %get-tuple-element.72.refs_12_.refs_13_.refs_3_), channel_id=1, source_target_pairs={{1,0},{0,1},{3,2},{2,3},{5,4},{4,5},{7,6},{6,7},{9,8},{8,9},{11,10... | collective-permute-start | bytes 61448 | tf_op jit(solution)/shard_map/ppermute | solution.py:657
  5.8 2.5 %collective-permute-start.2 = (f32[24,128]{1,0:T(8,128)S(1)}, f32[24,128]{1,0:T(8,128)S(1)}, u32[]{:S(2)}, u32[]{:S(2)}) collective-permute-start(f32[24,128]{1,0:T(8,128)S(1)} %get-tuple-element.74), channel_id=1, source_target_pairs={{0,2},{1,3},{2,0},{3,1},{4,6},{5,7},{6,4},{7,5},{8,10},{9,11},{10,... | collective-permute-start | bytes 36872 | tf_op jit(solution)/shard_map/ppermute | solution.py:652
  6.8 1.6 %collective-permute-start.3 = (f32[24,128]{1,0:T(8,128)S(1)}, f32[24,128]{1,0:T(8,128)S(1)}, u32[]{:S(2)}, u32[]{:S(2)}) collective-permute-start(f32[24,128]{1,0:T(8,128)S(1)} %get-tuple-element.75), channel_id=1, source_target_pairs={{0,2},{1,3},{2,0},{3,1},{4,6},{5,7},{6,4},{7,5},{8,10},{9,11},{10,... | collective-permute-start | bytes 36872 | tf_op jit(solution)/shard_map/ppermute | solution.py:652
  6.8 1.5 %collective-permute-start.4 = (f32[16,128]{1,0:T(8,128)S(1)}, f32[16,128]{1,0:T(8,128)S(1)}, u32[]{:S(2)}, u32[]{:S(2)}) collective-permute-start(f32[16,128]{1,0:T(8,128)S(1)} %get-tuple-element.76), channel_id=1, source_target_pairs={{0,2},{1,3},{2,0},{3,1},{4,6},{5,7},{6,4},{7,5},{8,10},{9,11},{10,... | collective-permute-start | bytes 24584 | tf_op jit(solution)/shard_map/ppermute | solution.py:652
  9.8 4.2 %collective-permute-start.5 = (f32[64,128]{1,0:T(8,128)S(1)}, f32[64,128]{1,0:T(8,128)S(1)}, u32[]{:S(2)}, u32[]{:S(2)}) collective-permute-start(f32[64,128]{1,0:T(8,128)S(1)} %get-tuple-element.81), channel_id=1, source_target_pairs={{0,1},{1,0},{2,4},{3,5},{4,2},{5,3},{6,8},{7,9},{8,6},{9,7},{10,12... | collective-permute-start | bytes 98312 | tf_op jit(solution)/shard_map/ppermute | solution.py:652
  10.2 3.8 %collective-permute-start.6 = (f32[28,128]{1,0:T(8,128)S(1)}, f32[28,128]{1,0:T(8,128)S(1)}, u32[]{:S(2)}, u32[]{:S(2)}) collective-permute-start(f32[28,128]{1,0:T(8,128)S(1)} %get-tuple-element.82.refs_12_.refs_5_), channel_id=1, source_target_pairs={{1,0},{0,1},{3,2},{2,3},{5,4},{4,5},{7,6},{6,7},{9,8},{8,9},{11,10... | collective-permute-start | bytes 43016 | tf_op jit(solution)/shard_map/ppermute | solution.py:657
  12.2 1.7 %collective-permute-start.7 = (f32[24,128]{1,0:T(8,128)S(1)}, f32[24,128]{1,0:T(8,128)S(1)}, u32[]{:S(2)}, u32[]{:S(2)}) collective-permute-start(f32[24,128]{1,0:T(8,128)S(1)} %get-tuple-element.83), channel_id=1, source_target_pairs={{0,2},{1,3},{2,0},{3,1},{4,6},{5,7},{6,4},{7,5},{8,10},{9,11},{10,... | collective-permute-start | bytes 36872 | tf_op jit(solution)/shard_map/ppermute | solution.py:652
  12.2 1.7 %collective-permute-start.8 = (f32[24,128]{1,0:T(8,128)S(1)}, f32[24,128]{1,0:T(8,128)S(1)}, u32[]{:S(2)}, u32[]{:S(2)}) collective-permute-start(f32[24,128]{1,0:T(8,128)S(1)} %get-tuple-element.84), channel_id=1, source_target_pairs={{0,2},{1,3},{2,0},{3,1},{4,6},{5,7},{6,4},{7,5},{8,10},{9,11},{10,... | collective-permute-start | bytes 36872 | tf_op jit(solution)/shard_map/ppermute | solution.py:652
  12.7 1.2 %collective-permute-start.9 = (f32[16,128]{1,0:T(8,128)S(1)}, f32[16,128]{1,0:T(8,128)S(1)}, u32[]{:S(2)}, u32[]{:S(2)}) collective-permute-start(f32[16,128]{1,0:T(8,128)S(1)} %get-tuple-element.85), channel_id=1, source_target_pairs={{0,2},{1,3},{2,0},{3,1},{4,6},{5,7},{6,4},{7,5},{8,10},{9,11},{10,... | collective-permute-start | bytes 24584 | tf_op jit(solution)/shard_map/ppermute | solution.py:652
  14.5 5.4 %collective-permute-start.10 = (f32[64,128]{1,0:T(8,128)S(1)}, f32[64,128]{1,0:T(8,128)S(1)}, u32[]{:S(2)}, u32[]{:S(2)}) collective-permute-start(f32[64,128]{1,0:T(8,128)S(1)} %get-tuple-element.93), channel_id=1, source_target_pairs={{0,1},{1,0},{2,4},{3,5},{4,2},{5,3},{6,8},{7,9},{8,6},{9,7},{10,12... | collective-permute-start | bytes 98312 | tf_op jit(solution)/shard_map/ppermute | solution.py:652
  16.2 3.7 %collective-permute-start.11 = (f32[28,128]{1,0:T(8,128)S(1)}, f32[28,128]{1,0:T(8,128)S(1)}, u32[]{:S(2)}, u32[]{:S(2)}) collective-permute-start(f32[28,128]{1,0:T(8,128)S(1)} %get-tuple-element.94.refs_12_.refs_7_), channel_id=1, source_target_pairs={{1,0},{0,1},{3,2},{2,3},{5,4},{4,5},{7,6},{6,7},{9,8},{8,9},{11,10... | collective-permute-start | bytes 43016 | tf_op jit(solution)/shard_map/ppermute | solution.py:657
  16.9 1.7 %collective-permute-start.12 = (f32[24,128]{1,0:T(8,128)S(1)}, f32[24,128]{1,0:T(8,128)S(1)}, u32[]{:S(2)}, u32[]{:S(2)}) collective-permute-start(f32[24,128]{1,0:T(8,128)S(1)} %get-tuple-element.95), channel_id=1, source_target_pairs={{0,2},{1,3},{2,0},{3,1},{4,6},{5,7},{6,4},{7,5},{8,10},{9,11},{10,... | collective-permute-start | bytes 36872 | tf_op jit(solution)/shard_map/ppermute | solution.py:652
  16.9 1.7 %collective-permute-start.13 = (f32[24,128]{1,0:T(8,128)S(1)}, f32[24,128]{1,0:T(8,128)S(1)}, u32[]{:S(2)}, u32[]{:S(2)}) collective-permute-start(f32[24,128]{1,0:T(8,128)S(1)} %get-tuple-element.96), channel_id=1, source_target_pairs={{0,2},{1,3},{2,0},{3,1},{4,6},{5,7},{6,4},{7,5},{8,10},{9,11},{10,... | collective-permute-start | bytes 36872 | tf_op jit(solution)/shard_map/ppermute | solution.py:652
  17.4 1.2 %collective-permute-start.14 = (f32[16,128]{1,0:T(8,128)S(1)}, f32[16,128]{1,0:T(8,128)S(1)}, u32[]{:S(2)}, u32[]{:S(2)}) collective-permute-start(f32[16,128]{1,0:T(8,128)S(1)} %get-tuple-element.97), channel_id=1, source_target_pairs={{0,2},{1,3},{2,0},{3,1},{4,6},{5,7},{6,4},{7,5},{8,10},{9,11},{10,... | collective-permute-start | bytes 24584 | tf_op jit(solution)/shard_map/ppermute | solution.py:652
  20.5 4.3 %collective-permute-start.15 = (f32[64,128]{1,0:T(8,128)S(1)}, f32[64,128]{1,0:T(8,128)S(1)}, u32[]{:S(2)}, u32[]{:S(2)}) collective-permute-start(f32[64,128]{1,0:T(8,128)S(1)} %get-tuple-element.101), channel_id=1, source_target_pairs={{0,1},{1,0},{2,4},{3,5},{4,2},{5,3},{6,8},{7,9},{8,6},{9,7},{10,12... | collective-permute-start | bytes 98312 | tf_op jit(solution)/shard_map/ppermute | solution.py:652
  21.0 3.9 %collective-permute-start.16 = (f32[28,128]{1,0:T(8,128)S(1)}, f32[28,128]{1,0:T(8,128)S(1)}, u32[]{:S(2)}, u32[]{:S(2)}) collective-permute-start(f32[28,128]{1,0:T(8,128)S(1)} %get-tuple-element.102.refs_9_.refs_12_), channel_id=1, source_target_pairs={{1,0},{0,1},{3,2},{2,3},{5,4},{4,5},{7,6},{6,7},{9,8},{8,9},{11,10... | collective-permute-start | bytes 43016 | tf_op jit(solution)/shard_map/ppermute | solution.py:657
  22.9 1.9 %collective-permute-start.17 = (f32[24,128]{1,0:T(8,128)S(1)}, f32[24,128]{1,0:T(8,128)S(1)}, u32[]{:S(2)}, u32[]{:S(2)}) collective-permute-start(f32[24,128]{1,0:T(8,128)S(1)} %get-tuple-element.103), channel_id=1, source_target_pairs={{0,2},{1,3},{2,0},{3,1},{4,6},{5,7},{6,4},{7,5},{8,10},{9,11},{10,... | collective-permute-start | bytes 36872 | tf_op jit(solution)/shard_map/ppermute | solution.py:652
  23.0 1.9 %collective-permute-start.18 = (f32[24,128]{1,0:T(8,128)S(1)}, f32[24,128]{1,0:T(8,128)S(1)}, u32[]{:S(2)}, u32[]{:S(2)}) collective-permute-start(f32[24,128]{1,0:T(8,128)S(1)} %get-tuple-element.104), channel_id=1, source_target_pairs={{0,2},{1,3},{2,0},{3,1},{4,6},{5,7},{6,4},{7,5},{8,10},{9,11},{10,... | collective-permute-start | bytes 36872 | tf_op jit(solution)/shard_map/ppermute | solution.py:652
  23.5 1.4 %collective-permute-start.19 = (f32[16,128]{1,0:T(8,128)S(1)}, f32[16,128]{1,0:T(8,128)S(1)}, u32[]{:S(2)}, u32[]{:S(2)}) collective-permute-start(f32[16,128]{1,0:T(8,128)S(1)} %get-tuple-element.105), channel_id=1, source_target_pairs={{0,2},{1,3},{2,0},{3,1},{4,6},{5,7},{6,4},{7,5},{8,10},{9,11},{10,... | collective-permute-start | bytes 24584 | tf_op jit(solution)/shard_map/ppermute | solution.py:652
  25.0 3.8 %collective-permute-start.20 = (f32[2,128]{1,0:T(2,128)S(1)}, f32[2,128]{1,0:T(2,128)S(1)}, u32[]{:S(2)}, u32[]{:S(2)}) collective-permute-start(f32[2,128]{1,0:T(2,128)S(1)} %get-tuple-element.113), channel_id=1, source_target_pairs={{0,4},{1,5},{2,6},{3,7},{4,0},{5,1},{6,2},{7,3},{8,12},{9,13},{10,... | collective-permute-start | bytes 3080 | tf_op jit(solution)/shard_map/ppermute | solution.py:652
  25.8 3.6 %collective-permute-start.21 = (f32[2,128]{1,0:T(2,128)S(1)}, f32[2,128]{1,0:T(2,128)S(1)}, u32[]{:S(2)}, u32[]{:S(2)}) collective-permute-start(f32[2,128]{1,0:T(2,128)S(1)} %get-tuple-element.114), channel_id=1, source_target_pairs={{0,1},{1,0},{2,4},{3,5},{4,2},{5,3},{6,8},{7,9},{8,6},{9,7},{10,12... | collective-permute-start | bytes 3080 | tf_op jit(solution)/shard_map/ppermute | solution.py:652
  26.9 2.5 %collective-permute-start.22 = (f32[2,128]{1,0:T(2,128)S(1)}, f32[2,128]{1,0:T(2,128)S(1)}, u32[]{:S(2)}, u32[]{:S(2)}) collective-permute-start(f32[2,128]{1,0:T(2,128)S(1)} %get-tuple-element.115), channel_id=1, source_target_pairs={{0,2},{1,3},{2,0},{3,1},{4,8},{5,9},{6,10},{7,11},{8,4},{9,5},{10,... | collective-permute-start | bytes 3080 | tf_op jit(solution)/shard_map/ppermute | solution.py:652
  27.2 2.2 %collective-permute-start.23 = (f32[2,128]{1,0:T(2,128)S(1)}, f32[2,128]{1,0:T(2,128)S(1)}, u32[]{:S(2)}, u32[]{:S(2)}) collective-permute-start(f32[2,128]{1,0:T(2,128)S(1)} %get-tuple-element.116), channel_id=1, source_target_pairs={{0,2},{1,3},{2,0},{3,1},{4,6},{5,7},{6,4},{7,5},{8,10},{9,11},{10,... | collective-permute-start | bytes 3080 | tf_op jit(solution)/shard_map/ppermute | solution.py:652
  (1 other events, 1.0 us)

commit v22 on v21

--- a/solution.py
+++ b/solution.py
@@ -545,7 +545,7 @@
         even_out[...] = message[at : at + even_out.shape[0]]
 
 
-def mask_kernel(owner_ref, flags_ref, stress_ref, _, mask_ref, weight_ref, *, z_elems):
+def mask_kernel(owner_ref, flags_ref, stress_ref, _, back_ref, mask_ref, weight_ref, *, z_elems):
     shape = (PATCH_ROWS, mask_ref.shape[1])
     first = (lax.axis_index("dom") - REACH) * PATCH_DEV
     number = lax.broadcasted_iota(jnp.int32, shape, 0) + first
@@ -749,7 +749,7 @@
             mask, weight = kernel_call(
                 mask_kernel,
                 [(4 * PATCH_ROWS, lanes), (4 * steps, lanes)],
-                [owner, flags, stress, cur],
+                [owner, flags, stress, cur, back],
                 unread=(3,),
                 z_elems=z_elems,
             )

time: 30.2 us -> 30.1 us (level)
  no operation moved by 1% of the time
where the time goes in v22:
time: 30.1 us; the launch traced here: 29.8 us
  starting transfers between devices  15.1 us (50%)
  Pallas kernels  9.9 us (33%)
  waiting for transfers between devices  3.62 us (12%)
  between operations  0.78 us (3%)
  local copies, waits for them, and re-layouts  0.45 us (1%)
    ppermute x20, starting transfers between devices, swapped(): return lax.ppermute(block, ('dom', 'depth'), route)  11.3 us
    pallas_call x18, Pallas kernels, kernel_call(): pl.pallas_call(functools.partial(body, **static) if static else body, out...  9.9 us
    ppermute x4, starting transfers between devices, from_behind(): lax.ppermute(block, axis, [((i - distance) % size, i) for i in range(size)])  3.78 us
    ppermute x4, waiting for transfers between devices, from_behind(): lax.ppermute(block, axis, [((i - distance) % size, i) for i in range(size)])  2.3 us
    ppermute x20, waiting for transfers between devices, swapped(): return lax.ppermute(block, ('dom', 'depth'), route)  1.32 us
  transfers between devices with their start and end apart: 24, of which 6 were waited for; matrix products, arithmetic and copies ran while one was open for 0% of the time, Pallas kernels for 19%

profile of v22, /device:TPU:0, one launch (start us, length us, event | category | flops | bytes accessed | tf_op | source)
XLA Modules:
  0.0 29.8 jit_solution(10078633786805283006)
XLA Ops:
  0.6 1.8 %shard_map.166 = (f32[320,128]{1,0:T(8,128)S(1)}, f32[64,128]{1,0:T(8,128)S(1)}, f32[40,128]{1,0:T(8,128)S(1)}, f32[8,128]{1,0:T(8,128)S(1)}, bf16[160,1024]{1,0...) custom-call(f32[3,17,4,128]{3,2,1,0:T(4,128)} %bitcast.11, ...), custom_call_target="tpu_custom_call" | custom-call | tf_op jit(solution)/shard_map/pallas_call | solution.py:625
  2.4 3.0 %collective-permute-start = (f32[64,128]{1,0:T(8,128)S(1)}, f32[64,128]{1,0:T(8,128)S(1)}, u32[]{:S(2)}, u32[]{:S(2)}) collective-permute-start(f32[64,128]{1,0:T(8,128)S(1)} %get-tuple-element.71), channel_id=1, source_target_pairs={{0,1},{1,0},{2,4},{3,5},{4,2},{5,3},{6,8},{7,9},{8,6},{9,7},{10,12... | collective-permute-start | bytes 98312 | tf_op jit(solution)/shard_map/ppermute | solution.py:652
  5.8 1.0 %collective-permute-start.2 = (f32[24,128]{1,0:T(8,128)S(1)}, f32[24,128]{1,0:T(8,128)S(1)}, u32[]{:S(2)}, u32[]{:S(2)}) collective-permute-start(f32[24,128]{1,0:T(8,128)S(1)} %get-tuple-element.74), channel_id=1, source_target_pairs={{0,2},{1,3},{2,0},{3,1},{4,6},{5,7},{6,4},{7,5},{8,10},{9,11},{10,... | collective-permute-start | bytes 36872 | tf_op jit(solution)/shard_map/ppermute | solution.py:652
  7.3 0.5 %shard_map.168 = (f32[320,128]{1,0:T(8,128)S(1)}, f32[160,128]{1,0:T(8,128)S(1)}) custom-call(f32[320,128]{1,0:T(8,128)S(1)} %get-tuple-element.60.cur_ref.refs_0_.refs_1_, f32[8,128]{1,0:T(8,128)S(1)} %get-tuple-element.66.material_ref.refs_5_, bf16[2,640,384]{2,1,0:T(8,128)(2,1)S(1)} %get-tuple-element.67.own_ref, ...), custom_call_target="tpu_custom_call" | custom-call | tf_op jit(solution)/shard_map/pallas_call | solution.py:625
  7.8 0.5 %shard_map.167 = (f32[320,128]{1,0:T(8,128)S(1)}, f32[320,128]{1,0:T(8,128)S(1)}) custom-call(f32[3,17,4,128]{3,2,1,0:T(4,128)S(1)} %get-tuple-element.61.next_ref, f32[17,4,128]{2,1,0:T(4,128)S(1)} %get-tuple-element.62.density_ref, f32[320,128]{1,0:T(8,128)S(1)} %get-tuple-element.63.mass_ref), custom_call_target="tpu_custom_call" | custom-call | tf_op jit(solution)/shard_map/pallas_call | solution.py:625
  8.3 0.8 %collective-permute-done.1.refs_7_.refs_11_.refs_4_ = f32[40,128]{1,0:T(8,128)S(1)} collective-permute-done((f32[40,128]{1,0:T(8,128)S(1)}, f32[40,128]{1,0:T(8,128)S(1)}, u32[]{:S(2)}, u32[]{:S(2)}) %collective-permute-start.1) | collective-permute-done | bytes 20512 | tf_op jit(solution)/shard_map/ppermute | solution.py:657
  9.2 0.6 %shard_map.170 = (f32[320,128]{1,0:T(8,128)S(1)}, f32[64,128]{1,0:T(8,128)S(1)}, f32[28,128]{1,0:T(8,128)S(1)}) custom-call(f32[320,128]{1,0:T(8,128)S(1)} %get-tuple-element.60.cur_ref.refs_0_.refs_1_, f32[320,128]{1,0:T(8,128)S(1)} %get-tuple-element.64.refs_1_, f32[320,128]{1,0:T(8,128)S(1)} %get-tuple-element.65.refs_2_, ...), custom_call_target="tpu_custom_call" | custom-call | tf_op jit(solution)/shard_map/pallas_call | solution.py:625
  10.2 1.7 %collective-permute-start.6 = (f32[28,128]{1,0:T(8,128)S(1)}, f32[28,128]{1,0:T(8,128)S(1)}, u32[]{:S(2)}, u32[]{:S(2)}) collective-permute-start(f32[28,128]{1,0:T(8,128)S(1)} %get-tuple-element.82.refs_12_.refs_5_), channel_id=1, source_target_pairs={{1,0},{0,1},{3,2},{2,3},{5,4},{4,5},{7,6},{6,7},{9,8},{8,9},{11,10... | collective-permute-start | bytes 43016 | tf_op jit(solution)/shard_map/ppermute | solution.py:657
  12.2 0.5 %collective-permute-start.8 = (f32[24,128]{1,0:T(8,128)S(1)}, f32[24,128]{1,0:T(8,128)S(1)}, u32[]{:S(2)}, u32[]{:S(2)}) collective-permute-start(f32[24,128]{1,0:T(8,128)S(1)} %get-tuple-element.84), channel_id=1, source_target_pairs={{0,2},{1,3},{2,0},{3,1},{4,6},{5,7},{6,4},{7,5},{8,10},{9,11},{10,... | collective-permute-start | bytes 36872 | tf_op jit(solution)/shard_map/ppermute | solution.py:652
  12.8 0.5 %shard_map.171 = (f32[320,128]{1,0:T(8,128)S(1)}, f32[160,128]{1,0:T(8,128)S(1)}) custom-call(f32[320,128]{1,0:T(8,128)S(1)} %get-tuple-element.78.cur_ref._.refs_0_.refs_1_, f32[8,128]{1,0:T(8,128)S(1)} %get-tuple-element.66.material_ref.refs_5_, bf16[2,640,384]{2,1,0:T(8,128)(2,1)S(1)} %get-tuple-element.67.own_ref, ...), custom_call_target="tpu_custom_call" | custom-call | tf_op jit(solution)/shard_map/pallas_call | solution.py:625
  13.9 0.6 %shard_map.174 = (f32[320,128]{1,0:T(8,128)S(1)}, f32[64,128]{1,0:T(8,128)S(1)}, f32[28,128]{1,0:T(8,128)S(1)}) custom-call(f32[320,128]{1,0:T(8,128)S(1)} %get-tuple-element.78.cur_ref._.refs_0_.refs_1_, f32[320,128]{1,0:T(8,128)S(1)} %get-tuple-element.60.cur_ref.refs_0_.refs_1_, f32[320,128]{1,0:T(8,128)S(1)} %get-tuple-element.65.refs_2_, ...), custom_call_target="tpu_custom_call" | custom-call | tf_op jit(solution)/shard_map/pallas_call | solution.py:625
  14.5 1.7 %collective-permute-start.10 = (f32[64,128]{1,0:T(8,128)S(1)}, f32[64,128]{1,0:T(8,128)S(1)}, u32[]{:S(2)}, u32[]{:S(2)}) collective-permute-start(f32[64,128]{1,0:T(8,128)S(1)} %get-tuple-element.93), channel_id=1, source_target_pairs={{0,1},{1,0},{2,4},{3,5},{4,2},{5,3},{6,8},{7,9},{8,6},{9,7},{10,12... | collective-permute-start | bytes 98312 | tf_op jit(solution)/shard_map/ppermute | solution.py:652
  16.9 0.5 %collective-permute-start.13 = (f32[24,128]{1,0:T(8,128)S(1)}, f32[24,128]{1,0:T(8,128)S(1)}, u32[]{:S(2)}, u32[]{:S(2)}) collective-permute-start(f32[24,128]{1,0:T(8,128)S(1)} %get-tuple-element.96), channel_id=1, source_target_pairs={{0,2},{1,3},{2,0},{3,1},{4,6},{5,7},{6,4},{7,5},{8,10},{9,11},{10,... | collective-permute-start | bytes 36872 | tf_op jit(solution)/shard_map/ppermute | solution.py:652
  17.5 0.5 %shard_map.175 = (f32[320,128]{1,0:T(8,128)S(1)}, f32[160,128]{1,0:T(8,128)S(1)}) custom-call(f32[320,128]{1,0:T(8,128)S(1)} %get-tuple-element.90.cur_ref.refs_0_.refs_1_, f32[8,128]{1,0:T(8,128)S(1)} %get-tuple-element.66.material_ref.refs_5_, bf16[2,640,384]{2,1,0:T(8,128)(2,1)S(1)} %get-tuple-element.67.own_ref, ...), custom_call_target="tpu_custom_call" | custom-call | tf_op jit(solution)/shard_map/pallas_call | solution.py:625
  18.0 0.6 %collective-permute-done.14.refs_10_ = f32[16,128]{1,0:T(8,128)S(1)} collective-permute-done((f32[16,128]{1,0:T(8,128)S(1)}, f32[16,128]{1,0:T(8,128)S(1)}, u32[]{:S(2)}, u32[]{:S(2)}) %collective-permute-start.14) | collective-permute-done | bytes 8224 | tf_op jit(solution)/shard_map/ppermute | solution.py:652
  18.6 1.3 %collective-permute-done.11.refs_7_.refs_8_ = f32[28,128]{1,0:T(8,128)S(1)} collective-permute-done((f32[28,128]{1,0:T(8,128)S(1)}, f32[28,128]{1,0:T(8,128)S(1)}, u32[]{:S(2)}, u32[]{:S(2)}) %collective-permute-start.11) | collective-permute-done | bytes 14368 | tf_op jit(solution)/shard_map/ppermute | solution.py:657
  20.0 0.6 %shard_map.177 = (f32[320,128]{1,0:T(8,128)S(1)}, f32[64,128]{1,0:T(8,128)S(1)}, f32[28,128]{1,0:T(8,128)S(1)}) custom-call(f32[320,128]{1,0:T(8,128)S(1)} %get-tuple-element.90.cur_ref.refs_0_.refs_1_, f32[320,128]{1,0:T(8,128)S(1)} %get-tuple-element.78.cur_ref._.refs_0_.refs_1_, f32[320,128]{1,0:T(8,128)S(1)} %get-tuple-element.65.refs_2_, ...), custom_call_target="tpu_custom_call" | custom-call | tf_op jit(solution)/shard_map/pallas_call | solution.py:625
  21.0 1.6 %collective-permute-start.16 = (f32[28,128]{1,0:T(8,128)S(1)}, f32[28,128]{1,0:T(8,128)S(1)}, u32[]{:S(2)}, u32[]{:S(2)}) collective-permute-start(f32[28,128]{1,0:T(8,128)S(1)} %get-tuple-element.102.refs_9_.refs_12_), channel_id=1, source_target_pairs={{1,0},{0,1},{3,2},{2,3},{5,4},{4,5},{7,6},{6,7},{9,8},{8,9},{11,10... | collective-permute-start | bytes 43016 | tf_op jit(solution)/shard_map/ppermute | solution.py:657
  23.0 0.5 %collective-permute-start.18 = (f32[24,128]{1,0:T(8,128)S(1)}, f32[24,128]{1,0:T(8,128)S(1)}, u32[]{:S(2)}, u32[]{:S(2)}) collective-permute-start(f32[24,128]{1,0:T(8,128)S(1)} %get-tuple-element.104), channel_id=1, source_target_pairs={{0,2},{1,3},{2,0},{3,1},{4,6},{5,7},{6,4},{7,5},{8,10},{9,11},{10,... | collective-permute-start | bytes 36872 | tf_op jit(solution)/shard_map/ppermute | solution.py:652
  23.5 0.5 %shard_map.178 = (f32[320,128]{1,0:T(8,128)S(1)}, f32[160,128]{1,0:T(8,128)S(1)}) custom-call(f32[320,128]{1,0:T(8,128)S(1)} %get-tuple-element.98.cur_ref.refs_0_, f32[8,128]{1,0:T(8,128)S(1)} %get-tuple-element.66.material_ref.refs_5_, bf16[2,640,384]{2,1,0:T(8,128)(2,1)S(1)} %get-tuple-element.67.own_ref, bf16[160,256]{1,0:T(8,128)(2,1)S(1)} %get-tuple-element.68.touch_ref), custom_call_target="tpu_custom_call" | custom-call | tf_op jit(solution)/shard_map/pallas_call | solution.py:625
  24.8 0.9 %collective-permute-start.20 = (f32[2,128]{1,0:T(2,128)S(1)}, f32[2,128]{1,0:T(2,128)S(1)}, u32[]{:S(2)}, u32[]{:S(2)}) collective-permute-start(f32[2,128]{1,0:T(2,128)S(1)} %get-tuple-element.113), channel_id=1, source_target_pairs={{0,4},{1,5},{2,6},{3,7},{4,0},{5,1},{6,2},{7,3},{8,12},{9,13},{10,... | collective-permute-start | bytes 3080 | tf_op jit(solution)/shard_map/ppermute | solution.py:652
  25.7 1.2 %collective-permute-start.21 = (f32[2,128]{1,0:T(2,128)S(1)}, f32[2,128]{1,0:T(2,128)S(1)}, u32[]{:S(2)}, u32[]{:S(2)}) collective-permute-start(f32[2,128]{1,0:T(2,128)S(1)} %get-tuple-element.114), channel_id=1, source_target_pairs={{0,1},{1,0},{2,4},{3,5},{4,2},{5,3},{6,8},{7,9},{8,6},{9,7},{10,12... | collective-permute-start | bytes 3080 | tf_op jit(solution)/shard_map/ppermute | solution.py:652
  27.4 1.4 %shard_map.182 = (f32[3,17,4,128]{3,2,1,0:T(4,128)}, f32[3,17,4,128]{3,2,1,0:T(4,128)}) custom-call(f32[320,128]{1,0:T(8,128)S(1)} %get-tuple-element.98.cur_ref.refs_0_, f32[320,128]{1,0:T(8,128)S(1)} %get-tuple-element.90.cur_ref.refs_0_.refs_1_, f32[320,128]{1,0:T(8,128)S(1)} %get-tuple-element.65.refs_2_, f32[320,128]{1,0:T(8,128)S(1)} %get-tuple-element.99.refs_3_, ...), custom_call_target="tpu_custom_call" | custom-call | tf_op jit(solution)/shard_map/pallas_call | solution.py:625
  29.3 0.6 %shard_map.183 = f32[2,128]{1,0:T(2,128)} custom-call(f32[2,128]{1,0:T(2,128)S(1)} %get-tuple-element.109.refs_16_.refs_0_, f32[2,128]{1,0:T(2,128)S(1)} %collective-permute-done.20.refs_1_, f32[2,128]{1,0:T(2,128)S(1)} %collective-permute-done.21.refs_2_, f32[2,128]{1,0:T(2,128)S(1)} %collective-permute-done.22.refs_3_, ...), custom_call_target="tpu_custom_call" | custom-call | tf_op jit(solution)/shard_map/pallas_call | solution.py:625
  (44 shorter events, 5.7 us)
Async XLA Ops:
  2.4 6.8 %collective-permute-start = (f32[64,128]{1,0:T(8,128)S(1)}, f32[64,128]{1,0:T(8,128)S(1)}, u32[]{:S(2)}, u32[]{:S(2)}) collective-permute-start(f32[64,128]{1,0:T(8,128)S(1)} %get-tuple-element.71), channel_id=1, source_target_pairs={{0,1},{1,0},{2,4},{3,5},{4,2},{5,3},{6,8},{7,9},{8,6},{9,7},{10,12... | collective-permute-start | bytes 98312 | tf_op jit(solution)/shard_map/ppermute | solution.py:652
  5.4 3.8 %collective-permute-start.1 = (f32[40,128]{1,0:T(8,128)S(1)}, f32[40,128]{1,0:T(8,128)S(1)}, u32[]{:S(2)}, u32[]{:S(2)}) collective-permute-start(f32[40,128]{1,0:T(8,128)S(1)} %get-tuple-element.72.refs_12_.refs_13_.refs_3_), channel_id=1, source_target_pairs={{1,0},{0,1},{3,2},{2,3},{5,4},{4,5},{7,6},{6,7},{9,8},{8,9},{11,10... | collective-permute-start | bytes 61448 | tf_op jit(solution)/shard_map/ppermute | solution.py:657
  5.8 2.5 %collective-permute-start.2 = (f32[24,128]{1,0:T(8,128)S(1)}, f32[24,128]{1,0:T(8,128)S(1)}, u32[]{:S(2)}, u32[]{:S(2)}) collective-permute-start(f32[24,128]{1,0:T(8,128)S(1)} %get-tuple-element.74), channel_id=1, source_target_pairs={{0,2},{1,3},{2,0},{3,1},{4,6},{5,7},{6,4},{7,5},{8,10},{9,11},{10,... | collective-permute-start | bytes 36872 | tf_op jit(solution)/shard_map/ppermute | solution.py:652
  6.8 1.6 %collective-permute-start.3 = (f32[24,128]{1,0:T(8,128)S(1)}, f32[24,128]{1,0:T(8,128)S(1)}, u32[]{:S(2)}, u32[]{:S(2)}) collective-permute-start(f32[24,128]{1,0:T(8,128)S(1)} %get-tuple-element.75), channel_id=1, source_target_pairs={{0,2},{1,3},{2,0},{3,1},{4,6},{5,7},{6,4},{7,5},{8,10},{9,11},{10,... | collective-permute-start | bytes 36872 | tf_op jit(solution)/shard_map/ppermute | solution.py:652
  6.8 1.5 %collective-permute-start.4 = (f32[16,128]{1,0:T(8,128)S(1)}, f32[16,128]{1,0:T(8,128)S(1)}, u32[]{:S(2)}, u32[]{:S(2)}) collective-permute-start(f32[16,128]{1,0:T(8,128)S(1)} %get-tuple-element.76), channel_id=1, source_target_pairs={{0,2},{1,3},{2,0},{3,1},{4,6},{5,7},{6,4},{7,5},{8,10},{9,11},{10,... | collective-permute-start | bytes 24584 | tf_op jit(solution)/shard_map/ppermute | solution.py:652
  9.8 4.2 %collective-permute-start.5 = (f32[64,128]{1,0:T(8,128)S(1)}, f32[64,128]{1,0:T(8,128)S(1)}, u32[]{:S(2)}, u32[]{:S(2)}) collective-permute-start(f32[64,128]{1,0:T(8,128)S(1)} %get-tuple-element.81), channel_id=1, source_target_pairs={{0,1},{1,0},{2,4},{3,5},{4,2},{5,3},{6,8},{7,9},{8,6},{9,7},{10,12... | collective-permute-start | bytes 98312 | tf_op jit(solution)/shard_map/ppermute | solution.py:652
  10.2 3.8 %collective-permute-start.6 = (f32[28,128]{1,0:T(8,128)S(1)}, f32[28,128]{1,0:T(8,128)S(1)}, u32[]{:S(2)}, u32[]{:S(2)}) collective-permute-start(f32[28,128]{1,0:T(8,128)S(1)} %get-tuple-element.82.refs_12_.refs_5_), channel_id=1, source_target_pairs={{1,0},{0,1},{3,2},{2,3},{5,4},{4,5},{7,6},{6,7},{9,8},{8,9},{11,10... | collective-permute-start | bytes 43016 | tf_op jit(solution)/shard_map/ppermute | solution.py:657
  12.2 1.7 %collective-permute-start.7 = (f32[24,128]{1,0:T(8,128)S(1)}, f32[24,128]{1,0:T(8,128)S(1)}, u32[]{:S(2)}, u32[]{:S(2)}) collective-permute-start(f32[24,128]{1,0:T(8,128)S(1)} %get-tuple-element.83), channel_id=1, source_target_pairs={{0,2},{1,3},{2,0},{3,1},{4,6},{5,7},{6,4},{7,5},{8,10},{9,11},{10,... | collective-permute-start | bytes 36872 | tf_op jit(solution)/shard_map/ppermute | solution.py:652
  12.2 1.7 %collective-permute-start.8 = (f32[24,128]{1,0:T(8,128)S(1)}, f32[24,128]{1,0:T(8,128)S(1)}, u32[]{:S(2)}, u32[]{:S(2)}) collective-permute-start(f32[24,128]{1,0:T(8,128)S(1)} %get-tuple-element.84), channel_id=1, source_target_pairs={{0,2},{1,3},{2,0},{3,1},{4,6},{5,7},{6,4},{7,5},{8,10},{9,11},{10,... | collective-permute-start | bytes 36872 | tf_op jit(solution)/shard_map/ppermute | solution.py:652
  12.7 1.2 %collective-permute-start.9 = (f32[16,128]{1,0:T(8,128)S(1)}, f32[16,128]{1,0:T(8,128)S(1)}, u32[]{:S(2)}, u32[]{:S(2)}) collective-permute-start(f32[16,128]{1,0:T(8,128)S(1)} %get-tuple-element.85), channel_id=1, source_target_pairs={{0,2},{1,3},{2,0},{3,1},{4,6},{5,7},{6,4},{7,5},{8,10},{9,11},{10,... | collective-permute-start | bytes 24584 | tf_op jit(solution)/shard_map/ppermute | solution.py:652
  14.5 5.4 %collective-permute-start.10 = (f32[64,128]{1,0:T(8,128)S(1)}, f32[64,128]{1,0:T(8,128)S(1)}, u32[]{:S(2)}, u32[]{:S(2)}) collective-permute-start(f32[64,128]{1,0:T(8,128)S(1)} %get-tuple-element.93), channel_id=1, source_target_pairs={{0,1},{1,0},{2,4},{3,5},{4,2},{5,3},{6,8},{7,9},{8,6},{9,7},{10,12... | collective-permute-start | bytes 98312 | tf_op jit(solution)/shard_map/ppermute | solution.py:652
  16.2 3.7 %collective-permute-start.11 = (f32[28,128]{1,0:T(8,128)S(1)}, f32[28,128]{1,0:T(8,128)S(1)}, u32[]{:S(2)}, u32[]{:S(2)}) collective-permute-start(f32[28,128]{1,0:T(8,128)S(1)} %get-tuple-element.94.refs_12_.refs_7_), channel_id=1, source_target_pairs={{1,0},{0,1},{3,2},{2,3},{5,4},{4,5},{7,6},{6,7},{9,8},{8,9},{11,10... | collective-permute-start | bytes 43016 | tf_op jit(solution)/shard_map/ppermute | solution.py:657
  16.9 1.7 %collective-permute-start.12 = (f32[24,128]{1,0:T(8,128)S(1)}, f32[24,128]{1,0:T(8,128)S(1)}, u32[]{:S(2)}, u32[]{:S(2)}) collective-permute-start(f32[24,128]{1,0:T(8,128)S(1)} %get-tuple-element.95), channel_id=1, source_target_pairs={{0,2},{1,3},{2,0},{3,1},{4,6},{5,7},{6,4},{7,5},{8,10},{9,11},{10,... | collective-permute-start | bytes 36872 | tf_op jit(solution)/shard_map/ppermute | solution.py:652
  16.9 1.7 %collective-permute-start.13 = (f32[24,128]{1,0:T(8,128)S(1)}, f32[24,128]{1,0:T(8,128)S(1)}, u32[]{:S(2)}, u32[]{:S(2)}) collective-permute-start(f32[24,128]{1,0:T(8,128)S(1)} %get-tuple-element.96), channel_id=1, source_target_pairs={{0,2},{1,3},{2,0},{3,1},{4,6},{5,7},{6,4},{7,5},{8,10},{9,11},{10,... | collective-permute-start | bytes 36872 | tf_op jit(solution)/shard_map/ppermute | solution.py:652
  17.4 1.2 %collective-permute-start.14 = (f32[16,128]{1,0:T(8,128)S(1)}, f32[16,128]{1,0:T(8,128)S(1)}, u32[]{:S(2)}, u32[]{:S(2)}) collective-permute-start(f32[16,128]{1,0:T(8,128)S(1)} %get-tuple-element.97), channel_id=1, source_target_pairs={{0,2},{1,3},{2,0},{3,1},{4,6},{5,7},{6,4},{7,5},{8,10},{9,11},{10,... | collective-permute-start | bytes 24584 | tf_op jit(solution)/shard_map/ppermute | solution.py:652
  20.5 4.2 %collective-permute-start.15 = (f32[64,128]{1,0:T(8,128)S(1)}, f32[64,128]{1,0:T(8,128)S(1)}, u32[]{:S(2)}, u32[]{:S(2)}) collective-permute-start(f32[64,128]{1,0:T(8,128)S(1)} %get-tuple-element.101), channel_id=1, source_target_pairs={{0,1},{1,0},{2,4},{3,5},{4,2},{5,3},{6,8},{7,9},{8,6},{9,7},{10,12... | collective-permute-start | bytes 98312 | tf_op jit(solution)/shard_map/ppermute | solution.py:652
  21.0 3.7 %collective-permute-start.16 = (f32[28,128]{1,0:T(8,128)S(1)}, f32[28,128]{1,0:T(8,128)S(1)}, u32[]{:S(2)}, u32[]{:S(2)}) collective-permute-start(f32[28,128]{1,0:T(8,128)S(1)} %get-tuple-element.102.refs_9_.refs_12_), channel_id=1, source_target_pairs={{1,0},{0,1},{3,2},{2,3},{5,4},{4,5},{7,6},{6,7},{9,8},{8,9},{11,10... | collective-permute-start | bytes 43016 | tf_op jit(solution)/shard_map/ppermute | solution.py:657
  22.9 1.7 %collective-permute-start.17 = (f32[24,128]{1,0:T(8,128)S(1)}, f32[24,128]{1,0:T(8,128)S(1)}, u32[]{:S(2)}, u32[]{:S(2)}) collective-permute-start(f32[24,128]{1,0:T(8,128)S(1)} %get-tuple-element.103), channel_id=1, source_target_pairs={{0,2},{1,3},{2,0},{3,1},{4,6},{5,7},{6,4},{7,5},{8,10},{9,11},{10,... | collective-permute-start | bytes 36872 | tf_op jit(solution)/shard_map/ppermute | solution.py:652
  23.0 1.7 %collective-permute-start.18 = (f32[24,128]{1,0:T(8,128)S(1)}, f32[24,128]{1,0:T(8,128)S(1)}, u32[]{:S(2)}, u32[]{:S(2)}) collective-permute-start(f32[24,128]{1,0:T(8,128)S(1)} %get-tuple-element.104), channel_id=1, source_target_pairs={{0,2},{1,3},{2,0},{3,1},{4,6},{5,7},{6,4},{7,5},{8,10},{9,11},{10,... | collective-permute-start | bytes 36872 | tf_op jit(solution)/shard_map/ppermute | solution.py:652
  23.5 1.2 %collective-permute-start.19 = (f32[16,128]{1,0:T(8,128)S(1)}, f32[16,128]{1,0:T(8,128)S(1)}, u32[]{:S(2)}, u32[]{:S(2)}) collective-permute-start(f32[16,128]{1,0:T(8,128)S(1)} %get-tuple-element.105), channel_id=1, source_target_pairs={{0,2},{1,3},{2,0},{3,1},{4,6},{5,7},{6,4},{7,5},{8,10},{9,11},{10,... | collective-permute-start | bytes 24584 | tf_op jit(solution)/shard_map/ppermute | solution.py:652
  24.8 4.0 %collective-permute-start.20 = (f32[2,128]{1,0:T(2,128)S(1)}, f32[2,128]{1,0:T(2,128)S(1)}, u32[]{:S(2)}, u32[]{:S(2)}) collective-permute-start(f32[2,128]{1,0:T(2,128)S(1)} %get-tuple-element.113), channel_id=1, source_target_pairs={{0,4},{1,5},{2,6},{3,7},{4,0},{5,1},{6,2},{7,3},{8,12},{9,13},{10,... | collective-permute-start | bytes 3080 | tf_op jit(solution)/shard_map/ppermute | solution.py:652
  25.7 3.6 %collective-permute-start.21 = (f32[2,128]{1,0:T(2,128)S(1)}, f32[2,128]{1,0:T(2,128)S(1)}, u32[]{:S(2)}, u32[]{:S(2)}) collective-permute-start(f32[2,128]{1,0:T(2,128)S(1)} %get-tuple-element.114), channel_id=1, source_target_pairs={{0,1},{1,0},{2,4},{3,5},{4,2},{5,3},{6,8},{7,9},{8,6},{9,7},{10,12... | collective-permute-start | bytes 3080 | tf_op jit(solution)/shard_map/ppermute | solution.py:652
  26.9 2.4 %collective-permute-start.22 = (f32[2,128]{1,0:T(2,128)S(1)}, f32[2,128]{1,0:T(2,128)S(1)}, u32[]{:S(2)}, u32[]{:S(2)}) collective-permute-start(f32[2,128]{1,0:T(2,128)S(1)} %get-tuple-element.115), channel_id=1, source_target_pairs={{0,2},{1,3},{2,0},{3,1},{4,8},{5,9},{6,10},{7,11},{8,4},{9,5},{10,... | collective-permute-start | bytes 3080 | tf_op jit(solution)/shard_map/ppermute | solution.py:652
  27.0 2.3 %collective-permute-start.23 = (f32[2,128]{1,0:T(2,128)S(1)}, f32[2,128]{1,0:T(2,128)S(1)}, u32[]{:S(2)}, u32[]{:S(2)}) collective-permute-start(f32[2,128]{1,0:T(2,128)S(1)} %get-tuple-element.116), channel_id=1, source_target_pairs={{0,2},{1,3},{2,0},{3,1},{4,6},{5,7},{6,4},{7,5},{8,10},{9,11},{10,... | collective-permute-start | bytes 3080 | tf_op jit(solution)/shard_map/ppermute | solution.py:652
  (1 other events, 1.0 us)

commit v23 on v22

--- a/solution.py
+++ b/solution.py
@@ -13,7 +13,7 @@
 PATCH_DEV = 2
 REACH = 2
 PATCH_ROWS = 16
-LATER = 10
+LATER = 9
 FAULT = 24
 SENT_FAULT = 28
 PARTS = (24, 24, 16)
@@ -693,7 +693,7 @@
         return [swapped(part, 1, 0) for part in even], swapped(odd, 1, 1), faults
 
     later_used = (
-        edge_table, following, rho, mass, own_table, far_table, touch_table, flags,
+        edge_table, following, rho, mass, own_table, touch_table, flags,
         normal_stress[0], patch_owner,
     )
     assert len(later_used) == LATER
@@ -707,7 +707,7 @@
         kept=range(5, 5 + LATER),
     )
     cur, odd, fault_rows, material = first_out[:-LATER]
-    edge_table, following, rho, mass, own_table, far_table, touch_table = first_out[-LATER:-3]
+    edge_table, following, rho, mass, own_table, touch_table = first_out[-LATER:-3]
     flags, stress, owner = first_out[-3:]
 
     def on_chip(field):

time: 30.1 us -> 30.1 us (level)
  transfers between devices with their start and end apart: 24 -> 24, of which waited for: 6 -> 7; matrix products, arithmetic and copies ran while one was open for 0% -> 0% of each run, Pallas kernels for 19% -> 19%
where the time goes in v23:
time: 30.1 us; the launch traced here: 29.8 us
  starting transfers between devices  15.1 us (50%)
  Pallas kernels  9.83 us (33%)
  waiting for transfers between devices  3.68 us (12%)
  between operations  0.78 us (3%)
  local copies, waits for them, and re-layouts  0.45 us (1%)
    ppermute x20, starting transfers between devices, swapped(): return lax.ppermute(block, ('dom', 'depth'), route)  11.3 us
    pallas_call x18, Pallas kernels, kernel_call(): pl.pallas_call(functools.partial(body, **static) if static else body, out...  9.83 us
    ppermute x4, starting transfers between devices, from_behind(): lax.ppermute(block, axis, [((i - distance) % size, i) for i in range(size)])  3.78 us
    ppermute x4, waiting for transfers between devices, from_behind(): lax.ppermute(block, axis, [((i - distance) % size, i) for i in range(size)])  2.3 us
    ppermute x20, waiting for transfers between devices, swapped(): return lax.ppermute(block, ('dom', 'depth'), route)  1.39 us
  transfers between devices with their start and end apart: 24, of which 7 were waited for; matrix products, arithmetic and copies ran while one was open for 0% of the time, Pallas kernels for 19%

profile of v23, /device:TPU:0, one launch (start us, length us, event | category | flops | bytes accessed | tf_op | source)
XLA Modules:
  0.0 29.8 jit_solution(8931775583945723444)
XLA Ops:
  0.6 1.7 %shard_map.166 = (f32[320,128]{1,0:T(8,128)S(1)}, f32[64,128]{1,0:T(8,128)S(1)}, f32[40,128]{1,0:T(8,128)S(1)}, f32[8,128]{1,0:T(8,128)S(1)}, bf16[160,1024]{1,0...) custom-call(f32[3,17,4,128]{3,2,1,0:T(4,128)} %bitcast.11, ...), custom_call_target="tpu_custom_call" | custom-call | tf_op jit(solution)/shard_map/pallas_call | solution.py:625
  2.3 3.0 %collective-permute-start = (f32[64,128]{1,0:T(8,128)S(1)}, f32[64,128]{1,0:T(8,128)S(1)}, u32[]{:S(2)}, u32[]{:S(2)}) collective-permute-start(f32[64,128]{1,0:T(8,128)S(1)} %get-tuple-element.70), channel_id=1, source_target_pairs={{0,1},{1,0},{2,4},{3,5},{4,2},{5,3},{6,8},{7,9},{8,6},{9,7},{10,12... | collective-permute-start | bytes 98312 | tf_op jit(solution)/shard_map/ppermute | solution.py:652
  5.7 1.0 %collective-permute-start.2 = (f32[24,128]{1,0:T(8,128)S(1)}, f32[24,128]{1,0:T(8,128)S(1)}, u32[]{:S(2)}, u32[]{:S(2)}) collective-permute-start(f32[24,128]{1,0:T(8,128)S(1)} %get-tuple-element.73), channel_id=1, source_target_pairs={{0,2},{1,3},{2,0},{3,1},{4,6},{5,7},{6,4},{7,5},{8,10},{9,11},{10,... | collective-permute-start | bytes 36872 | tf_op jit(solution)/shard_map/ppermute | solution.py:652
  7.2 0.5 %shard_map.168 = (f32[320,128]{1,0:T(8,128)S(1)}, f32[160,128]{1,0:T(8,128)S(1)}) custom-call(f32[320,128]{1,0:T(8,128)S(1)} %get-tuple-element.59.cur_ref.refs_0_.refs_1_, f32[8,128]{1,0:T(8,128)S(1)} %get-tuple-element.65.material_ref.refs_5_, bf16[2,640,384]{2,1,0:T(8,128)(2,1)S(1)} %get-tuple-element.66.own_ref, ...), custom_call_target="tpu_custom_call" | custom-call | tf_op jit(solution)/shard_map/pallas_call | solution.py:625
  7.7 0.5 %shard_map.167 = (f32[320,128]{1,0:T(8,128)S(1)}, f32[320,128]{1,0:T(8,128)S(1)}) custom-call(f32[3,17,4,128]{3,2,1,0:T(4,128)S(1)} %get-tuple-element.60.next_ref, f32[17,4,128]{2,1,0:T(4,128)S(1)} %get-tuple-element.61.density_ref, f32[320,128]{1,0:T(8,128)S(1)} %get-tuple-element.62.mass_ref), custom_call_target="tpu_custom_call" | custom-call | tf_op jit(solution)/shard_map/pallas_call | solution.py:625
  8.3 0.8 %collective-permute-done.1.refs_7_.refs_11_.refs_4_ = f32[40,128]{1,0:T(8,128)S(1)} collective-permute-done((f32[40,128]{1,0:T(8,128)S(1)}, f32[40,128]{1,0:T(8,128)S(1)}, u32[]{:S(2)}, u32[]{:S(2)}) %collective-permute-start.1) | collective-permute-done | bytes 20512 | tf_op jit(solution)/shard_map/ppermute | solution.py:657
  9.1 0.6 %shard_map.170 = (f32[320,128]{1,0:T(8,128)S(1)}, f32[64,128]{1,0:T(8,128)S(1)}, f32[28,128]{1,0:T(8,128)S(1)}) custom-call(f32[320,128]{1,0:T(8,128)S(1)} %get-tuple-element.59.cur_ref.refs_0_.refs_1_, f32[320,128]{1,0:T(8,128)S(1)} %get-tuple-element.63.refs_1_, f32[320,128]{1,0:T(8,128)S(1)} %get-tuple-element.64.refs_2_, ...), custom_call_target="tpu_custom_call" | custom-call | tf_op jit(solution)/shard_map/pallas_call | solution.py:625
  10.1 1.7 %collective-permute-start.6 = (f32[28,128]{1,0:T(8,128)S(1)}, f32[28,128]{1,0:T(8,128)S(1)}, u32[]{:S(2)}, u32[]{:S(2)}) collective-permute-start(f32[28,128]{1,0:T(8,128)S(1)} %get-tuple-element.80.refs_12_.refs_5_), channel_id=1, source_target_pairs={{1,0},{0,1},{3,2},{2,3},{5,4},{4,5},{7,6},{6,7},{9,8},{8,9},{11,10... | collective-permute-start | bytes 43016 | tf_op jit(solution)/shard_map/ppermute | solution.py:657
  12.1 0.5 %collective-permute-start.8 = (f32[24,128]{1,0:T(8,128)S(1)}, f32[24,128]{1,0:T(8,128)S(1)}, u32[]{:S(2)}, u32[]{:S(2)}) collective-permute-start(f32[24,128]{1,0:T(8,128)S(1)} %get-tuple-element.82), channel_id=1, source_target_pairs={{0,2},{1,3},{2,0},{3,1},{4,6},{5,7},{6,4},{7,5},{8,10},{9,11},{10,... | collective-permute-start | bytes 36872 | tf_op jit(solution)/shard_map/ppermute | solution.py:652
  12.7 0.5 %shard_map.171 = (f32[320,128]{1,0:T(8,128)S(1)}, f32[160,128]{1,0:T(8,128)S(1)}) custom-call(f32[320,128]{1,0:T(8,128)S(1)} %get-tuple-element.76.cur_ref._.refs_0_.refs_1_, f32[8,128]{1,0:T(8,128)S(1)} %get-tuple-element.65.material_ref.refs_5_, bf16[2,640,384]{2,1,0:T(8,128)(2,1)S(1)} %get-tuple-element.66.own_ref, ...), custom_call_target="tpu_custom_call" | custom-call | tf_op jit(solution)/shard_map/pallas_call | solution.py:625
  13.9 0.6 %shard_map.174 = (f32[320,128]{1,0:T(8,128)S(1)}, f32[64,128]{1,0:T(8,128)S(1)}, f32[28,128]{1,0:T(8,128)S(1)}) custom-call(f32[320,128]{1,0:T(8,128)S(1)} %get-tuple-element.76.cur_ref._.refs_0_.refs_1_, f32[320,128]{1,0:T(8,128)S(1)} %get-tuple-element.59.cur_ref.refs_0_.refs_1_, f32[320,128]{1,0:T(8,128)S(1)} %get-tuple-element.64.refs_2_, ...), custom_call_target="tpu_custom_call" | custom-call | tf_op jit(solution)/shard_map/pallas_call | solution.py:625
  14.5 1.7 %collective-permute-start.10 = (f32[64,128]{1,0:T(8,128)S(1)}, f32[64,128]{1,0:T(8,128)S(1)}, u32[]{:S(2)}, u32[]{:S(2)}) collective-permute-start(f32[64,128]{1,0:T(8,128)S(1)} %get-tuple-element.91), channel_id=1, source_target_pairs={{0,1},{1,0},{2,4},{3,5},{4,2},{5,3},{6,8},{7,9},{8,6},{9,7},{10,12... | collective-permute-start | bytes 98312 | tf_op jit(solution)/shard_map/ppermute | solution.py:652
  16.9 0.5 %collective-permute-start.13 = (f32[24,128]{1,0:T(8,128)S(1)}, f32[24,128]{1,0:T(8,128)S(1)}, u32[]{:S(2)}, u32[]{:S(2)}) collective-permute-start(f32[24,128]{1,0:T(8,128)S(1)} %get-tuple-element.94), channel_id=1, source_target_pairs={{0,2},{1,3},{2,0},{3,1},{4,6},{5,7},{6,4},{7,5},{8,10},{9,11},{10,... | collective-permute-start | bytes 36872 | tf_op jit(solution)/shard_map/ppermute | solution.py:652
  17.4 0.5 %shard_map.175 = (f32[320,128]{1,0:T(8,128)S(1)}, f32[160,128]{1,0:T(8,128)S(1)}) custom-call(f32[320,128]{1,0:T(8,128)S(1)} %get-tuple-element.88.cur_ref.refs_0_.refs_1_, f32[8,128]{1,0:T(8,128)S(1)} %get-tuple-element.65.material_ref.refs_5_, bf16[2,640,384]{2,1,0:T(8,128)(2,1)S(1)} %get-tuple-element.66.own_ref, ...), custom_call_target="tpu_custom_call" | custom-call | tf_op jit(solution)/shard_map/pallas_call | solution.py:625
  18.0 0.6 %collective-permute-done.14.refs_10_ = f32[16,128]{1,0:T(8,128)S(1)} collective-permute-done((f32[16,128]{1,0:T(8,128)S(1)}, f32[16,128]{1,0:T(8,128)S(1)}, u32[]{:S(2)}, u32[]{:S(2)}) %collective-permute-start.14) | collective-permute-done | bytes 8224 | tf_op jit(solution)/shard_map/ppermute | solution.py:652
  18.5 1.3 %collective-permute-done.11.refs_7_.refs_8_ = f32[28,128]{1,0:T(8,128)S(1)} collective-permute-done((f32[28,128]{1,0:T(8,128)S(1)}, f32[28,128]{1,0:T(8,128)S(1)}, u32[]{:S(2)}, u32[]{:S(2)}) %collective-permute-start.11) | collective-permute-done | bytes 14368 | tf_op jit(solution)/shard_map/ppermute | solution.py:657
  19.9 0.6 %shard_map.177 = (f32[320,128]{1,0:T(8,128)S(1)}, f32[64,128]{1,0:T(8,128)S(1)}, f32[28,128]{1,0:T(8,128)S(1)}) custom-call(f32[320,128]{1,0:T(8,128)S(1)} %get-tuple-element.88.cur_ref.refs_0_.refs_1_, f32[320,128]{1,0:T(8,128)S(1)} %get-tuple-element.76.cur_ref._.refs_0_.refs_1_, f32[320,128]{1,0:T(8,128)S(1)} %get-tuple-element.64.refs_2_, ...), custom_call_target="tpu_custom_call" | custom-call | tf_op jit(solution)/shard_map/pallas_call | solution.py:625
  20.9 1.6 %collective-permute-start.16 = (f32[28,128]{1,0:T(8,128)S(1)}, f32[28,128]{1,0:T(8,128)S(1)}, u32[]{:S(2)}, u32[]{:S(2)}) collective-permute-start(f32[28,128]{1,0:T(8,128)S(1)} %get-tuple-element.100.refs_9_.refs_12_), channel_id=1, source_target_pairs={{1,0},{0,1},{3,2},{2,3},{5,4},{4,5},{7,6},{6,7},{9,8},{8,9},{11,10... | collective-permute-start | bytes 43016 | tf_op jit(solution)/shard_map/ppermute | solution.py:657
  22.9 0.5 %collective-permute-start.18 = (f32[24,128]{1,0:T(8,128)S(1)}, f32[24,128]{1,0:T(8,128)S(1)}, u32[]{:S(2)}, u32[]{:S(2)}) collective-permute-start(f32[24,128]{1,0:T(8,128)S(1)} %get-tuple-element.102), channel_id=1, source_target_pairs={{0,2},{1,3},{2,0},{3,1},{4,6},{5,7},{6,4},{7,5},{8,10},{9,11},{10,... | collective-permute-start | bytes 36872 | tf_op jit(solution)/shard_map/ppermute | solution.py:652
  23.4 0.5 %shard_map.178 = (f32[320,128]{1,0:T(8,128)S(1)}, f32[160,128]{1,0:T(8,128)S(1)}) custom-call(f32[320,128]{1,0:T(8,128)S(1)} %get-tuple-element.96.cur_ref.refs_0_, f32[8,128]{1,0:T(8,128)S(1)} %get-tuple-element.65.material_ref.refs_5_, bf16[2,640,384]{2,1,0:T(8,128)(2,1)S(1)} %get-tuple-element.66.own_ref, bf16[160,256]{1,0:T(8,128)(2,1)S(1)} %get-tuple-element.67.touch_ref), custom_call_target="tpu_custom_call" | custom-call | tf_op jit(solution)/shard_map/pallas_call | solution.py:625
  24.8 0.9 %collective-permute-start.20 = (f32[2,128]{1,0:T(2,128)S(1)}, f32[2,128]{1,0:T(2,128)S(1)}, u32[]{:S(2)}, u32[]{:S(2)}) collective-permute-start(f32[2,128]{1,0:T(2,128)S(1)} %get-tuple-element.111), channel_id=1, source_target_pairs={{0,4},{1,5},{2,6},{3,7},{4,0},{5,1},{6,2},{7,3},{8,12},{9,13},{10,... | collective-permute-start | bytes 3080 | tf_op jit(solution)/shard_map/ppermute | solution.py:652
  25.7 1.1 %collective-permute-start.21 = (f32[2,128]{1,0:T(2,128)S(1)}, f32[2,128]{1,0:T(2,128)S(1)}, u32[]{:S(2)}, u32[]{:S(2)}) collective-permute-start(f32[2,128]{1,0:T(2,128)S(1)} %get-tuple-element.112), channel_id=1, source_target_pairs={{0,1},{1,0},{2,4},{3,5},{4,2},{5,3},{6,8},{7,9},{8,6},{9,7},{10,12... | collective-permute-start | bytes 3080 | tf_op jit(solution)/shard_map/ppermute | solution.py:652
  27.3 1.4 %shard_map.182 = (f32[3,17,4,128]{3,2,1,0:T(4,128)}, f32[3,17,4,128]{3,2,1,0:T(4,128)}) custom-call(f32[320,128]{1,0:T(8,128)S(1)} %get-tuple-element.96.cur_ref.refs_0_, f32[320,128]{1,0:T(8,128)S(1)} %get-tuple-element.88.cur_ref.refs_0_.refs_1_, f32[320,128]{1,0:T(8,128)S(1)} %get-tuple-element.64.refs_2_, f32[320,128]{1,0:T(8,128)S(1)} %get-tuple-element.97.refs_3_, ...), custom_call_target="tpu_custom_call" | custom-call | tf_op jit(solution)/shard_map/pallas_call | solution.py:625
  29.3 0.6 %shard_map.183 = f32[2,128]{1,0:T(2,128)} custom-call(f32[2,128]{1,0:T(2,128)S(1)} %get-tuple-element.107.refs_16_.refs_0_, f32[2,128]{1,0:T(2,128)S(1)} %collective-permute-done.20.refs_1_, f32[2,128]{1,0:T(2,128)S(1)} %collective-permute-done.21.refs_2_, f32[2,128]{1,0:T(2,128)S(1)} %collective-permute-done.22.refs_3_, ...), custom_call_target="tpu_custom_call" | custom-call | tf_op jit(solution)/shard_map/pallas_call | solution.py:625
  (46 shorter events, 5.8 us)
Async XLA Ops:
  2.3 6.8 %collective-permute-start = (f32[64,128]{1,0:T(8,128)S(1)}, f32[64,128]{1,0:T(8,128)S(1)}, u32[]{:S(2)}, u32[]{:S(2)}) collective-permute-start(f32[64,128]{1,0:T(8,128)S(1)} %get-tuple-element.70), channel_id=1, source_target_pairs={{0,1},{1,0},{2,4},{3,5},{4,2},{5,3},{6,8},{7,9},{8,6},{9,7},{10,12... | collective-permute-start | bytes 98312 | tf_op jit(solution)/shard_map/ppermute | solution.py:652
  5.3 3.8 %collective-permute-start.1 = (f32[40,128]{1,0:T(8,128)S(1)}, f32[40,128]{1,0:T(8,128)S(1)}, u32[]{:S(2)}, u32[]{:S(2)}) collective-permute-start(f32[40,128]{1,0:T(8,128)S(1)} %get-tuple-element.71.refs_12_.refs_13_.refs_3_), channel_id=1, source_target_pairs={{1,0},{0,1},{3,2},{2,3},{5,4},{4,5},{7,6},{6,7},{9,8},{8,9},{11,10... | collective-permute-start | bytes 61448 | tf_op jit(solution)/shard_map/ppermute | solution.py:657
  5.7 2.5 %collective-permute-start.2 = (f32[24,128]{1,0:T(8,128)S(1)}, f32[24,128]{1,0:T(8,128)S(1)}, u32[]{:S(2)}, u32[]{:S(2)}) collective-permute-start(f32[24,128]{1,0:T(8,128)S(1)} %get-tuple-element.73), channel_id=1, source_target_pairs={{0,2},{1,3},{2,0},{3,1},{4,6},{5,7},{6,4},{7,5},{8,10},{9,11},{10,... | collective-permute-start | bytes 36872 | tf_op jit(solution)/shard_map/ppermute | solution.py:652
  6.7 1.6 %collective-permute-start.3 = (f32[24,128]{1,0:T(8,128)S(1)}, f32[24,128]{1,0:T(8,128)S(1)}, u32[]{:S(2)}, u32[]{:S(2)}) collective-permute-start(f32[24,128]{1,0:T(8,128)S(1)} %get-tuple-element.74), channel_id=1, source_target_pairs={{0,2},{1,3},{2,0},{3,1},{4,6},{5,7},{6,4},{7,5},{8,10},{9,11},{10,... | collective-permute-start | bytes 36872 | tf_op jit(solution)/shard_map/ppermute | solution.py:652
  6.8 1.5 %collective-permute-start.4 = (f32[16,128]{1,0:T(8,128)S(1)}, f32[16,128]{1,0:T(8,128)S(1)}, u32[]{:S(2)}, u32[]{:S(2)}) collective-permute-start(f32[16,128]{1,0:T(8,128)S(1)} %get-tuple-element.75), channel_id=1, source_target_pairs={{0,2},{1,3},{2,0},{3,1},{4,6},{5,7},{6,4},{7,5},{8,10},{9,11},{10,... | collective-permute-start | bytes 24584 | tf_op jit(solution)/shard_map/ppermute | solution.py:652
  9.7 4.2 %collective-permute-start.5 = (f32[64,128]{1,0:T(8,128)S(1)}, f32[64,128]{1,0:T(8,128)S(1)}, u32[]{:S(2)}, u32[]{:S(2)}) collective-permute-start(f32[64,128]{1,0:T(8,128)S(1)} %get-tuple-element.79), channel_id=1, source_target_pairs={{0,1},{1,0},{2,4},{3,5},{4,2},{5,3},{6,8},{7,9},{8,6},{9,7},{10,12... | collective-permute-start | bytes 98312 | tf_op jit(solution)/shard_map/ppermute | solution.py:652
  10.1 3.8 %collective-permute-start.6 = (f32[28,128]{1,0:T(8,128)S(1)}, f32[28,128]{1,0:T(8,128)S(1)}, u32[]{:S(2)}, u32[]{:S(2)}) collective-permute-start(f32[28,128]{1,0:T(8,128)S(1)} %get-tuple-element.80.refs_12_.refs_5_), channel_id=1, source_target_pairs={{1,0},{0,1},{3,2},{2,3},{5,4},{4,5},{7,6},{6,7},{9,8},{8,9},{11,10... | collective-permute-start | bytes 43016 | tf_op jit(solution)/shard_map/ppermute | solution.py:657
  12.1 1.7 %collective-permute-start.7 = (f32[24,128]{1,0:T(8,128)S(1)}, f32[24,128]{1,0:T(8,128)S(1)}, u32[]{:S(2)}, u32[]{:S(2)}) collective-permute-start(f32[24,128]{1,0:T(8,128)S(1)} %get-tuple-element.81), channel_id=1, source_target_pairs={{0,2},{1,3},{2,0},{3,1},{4,6},{5,7},{6,4},{7,5},{8,10},{9,11},{10,... | collective-permute-start | bytes 36872 | tf_op jit(solution)/shard_map/ppermute | solution.py:652
  12.1 1.7 %collective-permute-start.8 = (f32[24,128]{1,0:T(8,128)S(1)}, f32[24,128]{1,0:T(8,128)S(1)}, u32[]{:S(2)}, u32[]{:S(2)}) collective-permute-start(f32[24,128]{1,0:T(8,128)S(1)} %get-tuple-element.82), channel_id=1, source_target_pairs={{0,2},{1,3},{2,0},{3,1},{4,6},{5,7},{6,4},{7,5},{8,10},{9,11},{10,... | collective-permute-start | bytes 36872 | tf_op jit(solution)/shard_map/ppermute | solution.py:652
  12.6 1.2 %collective-permute-start.9 = (f32[16,128]{1,0:T(8,128)S(1)}, f32[16,128]{1,0:T(8,128)S(1)}, u32[]{:S(2)}, u32[]{:S(2)}) collective-permute-start(f32[16,128]{1,0:T(8,128)S(1)} %get-tuple-element.83), channel_id=1, source_target_pairs={{0,2},{1,3},{2,0},{3,1},{4,6},{5,7},{6,4},{7,5},{8,10},{9,11},{10,... | collective-permute-start | bytes 24584 | tf_op jit(solution)/shard_map/ppermute | solution.py:652
  14.5 5.4 %collective-permute-start.10 = (f32[64,128]{1,0:T(8,128)S(1)}, f32[64,128]{1,0:T(8,128)S(1)}, u32[]{:S(2)}, u32[]{:S(2)}) collective-permute-start(f32[64,128]{1,0:T(8,128)S(1)} %get-tuple-element.91), channel_id=1, source_target_pairs={{0,1},{1,0},{2,4},{3,5},{4,2},{5,3},{6,8},{7,9},{8,6},{9,7},{10,12... | collective-permute-start | bytes 98312 | tf_op jit(solution)/shard_map/ppermute | solution.py:652
  16.1 3.7 %collective-permute-start.11 = (f32[28,128]{1,0:T(8,128)S(1)}, f32[28,128]{1,0:T(8,128)S(1)}, u32[]{:S(2)}, u32[]{:S(2)}) collective-permute-start(f32[28,128]{1,0:T(8,128)S(1)} %get-tuple-element.92.refs_12_.refs_7_), channel_id=1, source_target_pairs={{1,0},{0,1},{3,2},{2,3},{5,4},{4,5},{7,6},{6,7},{9,8},{8,9},{11,10... | collective-permute-start | bytes 43016 | tf_op jit(solution)/shard_map/ppermute | solution.py:657
  16.8 1.7 %collective-permute-start.12 = (f32[24,128]{1,0:T(8,128)S(1)}, f32[24,128]{1,0:T(8,128)S(1)}, u32[]{:S(2)}, u32[]{:S(2)}) collective-permute-start(f32[24,128]{1,0:T(8,128)S(1)} %get-tuple-element.93), channel_id=1, source_target_pairs={{0,2},{1,3},{2,0},{3,1},{4,6},{5,7},{6,4},{7,5},{8,10},{9,11},{10,... | collective-permute-start | bytes 36872 | tf_op jit(solution)/shard_map/ppermute | solution.py:652
  16.9 1.7 %collective-permute-start.13 = (f32[24,128]{1,0:T(8,128)S(1)}, f32[24,128]{1,0:T(8,128)S(1)}, u32[]{:S(2)}, u32[]{:S(2)}) collective-permute-start(f32[24,128]{1,0:T(8,128)S(1)} %get-tuple-element.94), channel_id=1, source_target_pairs={{0,2},{1,3},{2,0},{3,1},{4,6},{5,7},{6,4},{7,5},{8,10},{9,11},{10,... | collective-permute-start | bytes 36872 | tf_op jit(solution)/shard_map/ppermute | solution.py:652
  17.4 1.2 %collective-permute-start.14 = (f32[16,128]{1,0:T(8,128)S(1)}, f32[16,128]{1,0:T(8,128)S(1)}, u32[]{:S(2)}, u32[]{:S(2)}) collective-permute-start(f32[16,128]{1,0:T(8,128)S(1)} %get-tuple-element.95), channel_id=1, source_target_pairs={{0,2},{1,3},{2,0},{3,1},{4,6},{5,7},{6,4},{7,5},{8,10},{9,11},{10,... | collective-permute-start | bytes 24584 | tf_op jit(solution)/shard_map/ppermute | solution.py:652
  20.5 4.2 %collective-permute-start.15 = (f32[64,128]{1,0:T(8,128)S(1)}, f32[64,128]{1,0:T(8,128)S(1)}, u32[]{:S(2)}, u32[]{:S(2)}) collective-permute-start(f32[64,128]{1,0:T(8,128)S(1)} %get-tuple-element.99), channel_id=1, source_target_pairs={{0,1},{1,0},{2,4},{3,5},{4,2},{5,3},{6,8},{7,9},{8,6},{9,7},{10,12... | collective-permute-start | bytes 98312 | tf_op jit(solution)/shard_map/ppermute | solution.py:652
  20.9 3.7 %collective-permute-start.16 = (f32[28,128]{1,0:T(8,128)S(1)}, f32[28,128]{1,0:T(8,128)S(1)}, u32[]{:S(2)}, u32[]{:S(2)}) collective-permute-start(f32[28,128]{1,0:T(8,128)S(1)} %get-tuple-element.100.refs_9_.refs_12_), channel_id=1, source_target_pairs={{1,0},{0,1},{3,2},{2,3},{5,4},{4,5},{7,6},{6,7},{9,8},{8,9},{11,10... | collective-permute-start | bytes 43016 | tf_op jit(solution)/shard_map/ppermute | solution.py:657
  22.9 1.7 %collective-permute-start.17 = (f32[24,128]{1,0:T(8,128)S(1)}, f32[24,128]{1,0:T(8,128)S(1)}, u32[]{:S(2)}, u32[]{:S(2)}) collective-permute-start(f32[24,128]{1,0:T(8,128)S(1)} %get-tuple-element.101), channel_id=1, source_target_pairs={{0,2},{1,3},{2,0},{3,1},{4,6},{5,7},{6,4},{7,5},{8,10},{9,11},{10,... | collective-permute-start | bytes 36872 | tf_op jit(solution)/shard_map/ppermute | solution.py:652
  22.9 1.7 %collective-permute-start.18 = (f32[24,128]{1,0:T(8,128)S(1)}, f32[24,128]{1,0:T(8,128)S(1)}, u32[]{:S(2)}, u32[]{:S(2)}) collective-permute-start(f32[24,128]{1,0:T(8,128)S(1)} %get-tuple-element.102), channel_id=1, source_target_pairs={{0,2},{1,3},{2,0},{3,1},{4,6},{5,7},{6,4},{7,5},{8,10},{9,11},{10,... | collective-permute-start | bytes 36872 | tf_op jit(solution)/shard_map/ppermute | solution.py:652
  23.4 1.2 %collective-permute-start.19 = (f32[16,128]{1,0:T(8,128)S(1)}, f32[16,128]{1,0:T(8,128)S(1)}, u32[]{:S(2)}, u32[]{:S(2)}) collective-permute-start(f32[16,128]{1,0:T(8,128)S(1)} %get-tuple-element.103), channel_id=1, source_target_pairs={{0,2},{1,3},{2,0},{3,1},{4,6},{5,7},{6,4},{7,5},{8,10},{9,11},{10,... | collective-permute-start | bytes 24584 | tf_op jit(solution)/shard_map/ppermute | solution.py:652
  24.8 4.0 %collective-permute-start.20 = (f32[2,128]{1,0:T(2,128)S(1)}, f32[2,128]{1,0:T(2,128)S(1)}, u32[]{:S(2)}, u32[]{:S(2)}) collective-permute-start(f32[2,128]{1,0:T(2,128)S(1)} %get-tuple-element.111), channel_id=1, source_target_pairs={{0,4},{1,5},{2,6},{3,7},{4,0},{5,1},{6,2},{7,3},{8,12},{9,13},{10,... | collective-permute-start | bytes 3080 | tf_op jit(solution)/shard_map/ppermute | solution.py:652
  25.7 3.6 %collective-permute-start.21 = (f32[2,128]{1,0:T(2,128)S(1)}, f32[2,128]{1,0:T(2,128)S(1)}, u32[]{:S(2)}, u32[]{:S(2)}) collective-permute-start(f32[2,128]{1,0:T(2,128)S(1)} %get-tuple-element.112), channel_id=1, source_target_pairs={{0,1},{1,0},{2,4},{3,5},{4,2},{5,3},{6,8},{7,9},{8,6},{9,7},{10,12... | collective-permute-start | bytes 3080 | tf_op jit(solution)/shard_map/ppermute | solution.py:652
  26.8 2.5 %collective-permute-start.22 = (f32[2,128]{1,0:T(2,128)S(1)}, f32[2,128]{1,0:T(2,128)S(1)}, u32[]{:S(2)}, u32[]{:S(2)}) collective-permute-start(f32[2,128]{1,0:T(2,128)S(1)} %get-tuple-element.113), channel_id=1, source_target_pairs={{0,2},{1,3},{2,0},{3,1},{4,8},{5,9},{6,10},{7,11},{8,4},{9,5},{10,... | collective-permute-start | bytes 3080 | tf_op jit(solution)/shard_map/ppermute | solution.py:652
  26.9 2.4 %collective-permute-start.23 = (f32[2,128]{1,0:T(2,128)S(1)}, f32[2,128]{1,0:T(2,128)S(1)}, u32[]{:S(2)}, u32[]{:S(2)}) collective-permute-start(f32[2,128]{1,0:T(2,128)S(1)} %get-tuple-element.114), channel_id=1, source_target_pairs={{0,2},{1,3},{2,0},{3,1},{4,6},{5,7},{6,4},{7,5},{8,10},{9,11},{10,... | collective-permute-start | bytes 3080 | tf_op jit(solution)/shard_map/ppermute | solution.py:652
  (2 other events, 3.0 us)
